TPU v7x, 32 devices: a whole 2x2x4 slice. The times are simulated.
32 devices in a mesh: section: 4 (over y, core), rows: 8 (over z, x).
Axes of the slice: x: 2, y: 2, z: 4, core: 2. Of those that a mesh axis runs over, the one named last changes fastest.
Arguments:
- grad_in: bfloat16 [4, 2048, 256], P('section', 'rows'), may hold values from -6 to 6
- grad_last: bfloat16 [2048, 256], P('rows'), may hold values from -6 to 6
- support: bfloat16 [4, 2, 2, 2048, 256], P('section', None, None, 'rows'), may hold values from -6 to 6
- preact: bfloat16 [4, 2, 2, 2048, 256], P('section', None, None, 'rows'), may hold values from -6 to 6
- weights: bfloat16 [4, 2, 256, 256], P('section'), may hold values from -0.375 to 0.375
- tile_vals: bfloat16 [4, 2, 768, 128, 128], P('section', None, 'rows'), may hold values from -0.078125 to 0.078125
- tile_row: int32 [4, 2, 768], P('section', None, 'rows'), may hold values from 0 to 1
- tile_col: int32 [4, 2, 768], P('section', None, 'rows'), may hold values from 0 to 15, as said below
- tile_count: int32 [4, 2, 8], P('section', None, 'rows'), may hold values from 48 to 96, as said below
Outputs:
- handoff: bfloat16 [2, 4, 2048, 256], P(None, 'section', 'rows')
- init_grad: float32 [4, 2, 2048, 256], P('section', None, 'rows')
- weight_grad: float32 [4, 2, 256, 256], P('section')
Inputs may be any that keep to these rules, and one draw needn't show every extreme that they name: tile_count[s, t, d] is the number of live entries in device d's list; in every section and micro-batch some device has all 96 live. `tile_col`: for every section, micro-batch and pair of devices d and o with o != d, all entries of device d's list (live or padding) whose column tile lies in device o's rows name one and the same of o's 2 row tiles.
All inputs are finite; a program needn't handle non-finite values.
Results may differ from a plain program's by a relative error of at most 0.0066.
Values may be sent and summed in bfloat16 or wider, within the bound.
No kernel may reach another device: no remote copies, remote signals or barrier semaphores. Data moves between devices by JAX's collectives and lax.ppermute only.
A program may use at most 128 MiB of HBM per device.

v0:
```python
import jax
import jax.numpy as jnp
from jax import lax
from jax.sharding import PartitionSpec as P

ALPHA = 0.1
BETA_SCALE = 0.5


def passed_along(block, axis, distance):
    devices = range(lax.axis_size(axis))
    route = [(i - distance, i) for i in devices if i - distance in devices]
    return lax.ppermute(block, axis, route)


def tile_product(gathered, values, row_local, index, count, row_tiles):
    tile = values.shape[-1]
    width = gathered.shape[-1]
    blocks = gathered.reshape(-1, tile, width)[index]
    products = jnp.einsum("kab,kbf->kaf", values, blocks, preferred_element_type=jnp.float32)
    live = jnp.arange(index.shape[0]) < count
    select = ((row_local[None, :] == jnp.arange(row_tiles)[:, None]) & live[None, :]).astype(
        jnp.float32
    )
    summed = jnp.einsum("ik,kaf->iaf", select, products, precision=lax.Precision.HIGHEST)
    return summed.reshape(row_tiles * tile, width)


def shards(grad_in, grad_last, support, preact, weights, tile_vals, tile_row, tile_col, tile_count):
    section = lax.axis_index("section")
    sections = lax.axis_size("section")
    ticks = support.shape[1]
    layers = support.shape[2]
    rows_dev, width = grad_last.shape
    tile = tile_vals.shape[-1]
    row_tiles = rows_dev // tile
    weight_acc = [jnp.zeros((width, width), jnp.float32) for layer in range(layers)]
    handed = []
    initial = []
    for tick in range(ticks):
        if tick == 0:
            grad = grad_in[0]
        else:
            passed = passed_along(handed[-1], "section", -1)
            grad = jnp.where(section == sections - 1, grad_last, passed)
        columns = tile_col[0, tick]
        count = tile_count[0, tick, 0]
        toward = jnp.zeros((rows_dev, width), jnp.float32)
        for layer in reversed(range(layers)):
            beta = jnp.log(BETA_SCALE / (layers * section + layer + 1).astype(jnp.float32) + 1.0)
            weight = weights[0, layer]
            masked = jnp.where(preact[0, tick, layer] > 0, grad, jnp.zeros_like(grad))
            term = beta * jnp.dot(
                support[0, tick, layer].T, masked, preferred_element_type=jnp.float32
            )
            weight_acc[layer] = weight_acc[layer] + lax.psum(term, "rows")
            image = (
                (1.0 - beta) * masked.astype(jnp.float32)
                + beta * jnp.dot(masked, weight.T, preferred_element_type=jnp.float32)
            ).astype(jnp.bfloat16)
            toward = toward + ALPHA * image.astype(jnp.float32)
            gathered = lax.all_gather(image, "rows", axis=0, tiled=True)
            spread = tile_product(
                gathered, tile_vals[0, tick], tile_row[0, tick], columns, count, row_tiles
            )
            grad = ((1.0 - ALPHA) * spread).astype(jnp.bfloat16)
        handed.append(grad)
        initial.append(toward)
    return (jnp.stack(handed)[:, None], jnp.stack(initial)[None], jnp.stack(weight_acc)[None])


def solution(mesh):
    return jax.shard_map(
        shards,
        mesh=mesh,
        in_specs=(
            P("section", "rows", None),
            P("rows", None),
            P("section", None, None, "rows", None),
            P("section", None, None, "rows", None),
            P("section", None, None, None),
            P("section", None, "rows", None, None),
            P("section", None, "rows"),
            P("section", None, "rows"),
            P("section", None, "rows"),
        ),
        out_specs=(
            P(None, "section", "rows", None),
            P("section", None, "rows", None),
            P("section", None, None, None),
        ),
        check_vma=False,
    )
```

profile of v0, /device:TPU:0, one launch (start us, length us, event | category | flops | bytes accessed | tf_op | source)
XLA Modules:
  0.0 407.9 jit_solution(1422922073714444054)
XLA Ops:
  7.3 2.0 fusion.15
  9.5 1.3 fusion.83
  13.0 40.6 %all-gather.5.cloned.1.call-done = bf16[2048,256]{1,0:T(8,128)(2,1)} async-done(((bf16[256,256]{1,0:T(8,128)(2,1)}), bf16[2048,256]{1,0:T(8,128)(2,1)}) %all-gather.5.cloned.1.call-update) | async-done | bytes 1048592 | tf_op jit(solution)/shard_map/all_gather | solution.py:62
  53.6 7.1 %gather_fusion = bf16[96,128,256]{2,1,0:T(8,128)(2,1)} fusion(bf16[16,128,256]{2,1,0:T(8,128)(2,1)} %bitcast.141, s32[1024]{0:T(1024)S(1)} %pad_clamp_fusion.1), kind=kCustom, calls=%fused_computation | custom fusion | bytes 12583296 | tf_op jit(solution)/shard_map/gather | solution.py:19
  60.7 10.1 %convolution_bitcast_fusion.3 = f32[96,128,256]{1,2,0:T(8,128)} fusion(bf16[96,128,256]{2,1,0:T(8,128)(2,1)} %gather_fusion, bf16[1,2,96,128,128]{4,3,2,1,0:T(8,128)(2,1)} %param.14), kind=kOutput, calls=%fused_computation.7 | convolution fusion | flops 805306368 | bytes 22020096 | tf_op jit(solution)/shard_map/kab,kbf->kaf/dot_general | solution.py:20
  70.8 12.8 %copy.38 = f32[96,128,256]{2,0,1:T(8,128)} copy(f32[96,128,256]{1,2,0:T(8,128)} %convolution_bitcast_fusion.3) | data formatting | bytes 25165824 | tf_op jit(solution)/shard_map/kab,kbf->kaf/dot_general | solution.py:20
  83.6 7.1 %fusion.65 = f32[2,128,256]{2,0,1:T(2,128)S(1)} fusion(f32[96,128,256]{2,0,1:T(8,128)} %copy.38, pred[96]{0:T(512)(128)(4,1)S(1)} %iota_compare_fusion.1, s32[96]{0:T(128)S(1)} %get-tuple-element.18), kind=kOutput, calls=%fused_computation.97 | convolution fusion | flops 75497856 | bytes 12845536 | tf_op jit(solution)/shard_map/ik,kaf->iaf/dot_general | solution.py:25
  91.8 38.8 %all-gather.7.cloned.1.call-done = bf16[2048,256]{1,0:T(8,128)(2,1)} async-done(((bf16[256,256]{1,0:T(8,128)(2,1)}), bf16[2048,256]{1,0:T(8,128)(2,1)}) %all-gather.7.cloned.1.call-update) | async-done | bytes 1048592 | tf_op jit(solution)/shard_map/all_gather | solution.py:62
  130.7 7.1 %gather_fusion.1 = bf16[96,128,256]{2,1,0:T(8,128)(2,1)} fusion(bf16[16,128,256]{2,1,0:T(8,128)(2,1)} %bitcast.144, s32[1024]{0:T(1024)S(1)} %pad_clamp_fusion.1), kind=kCustom, calls=%fused_computation.1 | custom fusion | bytes 12583296 | tf_op jit(solution)/shard_map/gather | solution.py:19
  137.8 10.1 %convolution_bitcast_fusion.2 = f32[96,128,256]{1,2,0:T(8,128)} fusion(bf16[96,128,256]{2,1,0:T(8,128)(2,1)} %gather_fusion.1, bf16[1,2,96,128,128]{4,3,2,1,0:T(8,128)(2,1)} %param.14), kind=kOutput, calls=%fused_computation.6 | convolution fusion | flops 805306368 | bytes 22020096 | tf_op jit(solution)/shard_map/kab,kbf->kaf/dot_general | solution.py:20
  147.9 12.8 %copy.41 = f32[96,128,256]{2,0,1:T(8,128)} copy(f32[96,128,256]{1,2,0:T(8,128)} %convolution_bitcast_fusion.2) | data formatting | bytes 25165824 | tf_op jit(solution)/shard_map/kab,kbf->kaf/dot_general | solution.py:20
  160.6 7.1 %fusion.63 = f32[2,128,256]{2,0,1:T(2,128)S(1)} fusion(f32[96,128,256]{2,0,1:T(8,128)} %copy.41, pred[96]{0:T(512)(128)(4,1)S(1)} %iota_compare_fusion.1, s32[96]{0:T(128)S(1)} %get-tuple-element.18), kind=kOutput, calls=%fused_computation.95 | convolution fusion | flops 75497856 | bytes 12845536 | tf_op jit(solution)/shard_map/ik,kaf->iaf/dot_general | solution.py:25
  169.0 1.9 collective-permute-done
  174.3 38.3 %all-gather.9.cloned.1.call-done = bf16[2048,256]{1,0:T(8,128)(2,1)} async-done(((bf16[256,256]{1,0:T(8,128)(2,1)}), bf16[2048,256]{1,0:T(8,128)(2,1)}) %all-gather.9.cloned.1.call-update) | async-done | bytes 1048592 | tf_op jit(solution)/shard_map/all_gather | solution.py:62
  212.6 7.1 %gather_fusion.2 = bf16[96,128,256]{2,1,0:T(8,128)(2,1)} fusion(bf16[16,128,256]{2,1,0:T(8,128)(2,1)} %bitcast.143, s32[1024]{0:T(1024)S(1)} %pad_clamp_fusion), kind=kCustom, calls=%fused_computation.2 | custom fusion | bytes 12583296 | tf_op jit(solution)/shard_map/gather | solution.py:19
  219.7 10.1 %convolution_bitcast_fusion.1 = f32[96,128,256]{1,2,0:T(8,128)} fusion(bf16[96,128,256]{2,1,0:T(8,128)(2,1)} %gather_fusion.2, bf16[1,2,96,128,128]{4,3,2,1,0:T(8,128)(2,1)} %param.14), kind=kOutput, calls=%fused_computation.5 | convolution fusion | flops 805306368 | bytes 22020096 | tf_op jit(solution)/shard_map/kab,kbf->kaf/dot_general | solution.py:20
  229.8 12.8 %copy.44 = f32[96,128,256]{2,0,1:T(8,128)} copy(f32[96,128,256]{1,2,0:T(8,128)} %convolution_bitcast_fusion.1) | data formatting | bytes 25165824 | tf_op jit(solution)/shard_map/kab,kbf->kaf/dot_general | solution.py:20
  242.5 7.0 %fusion.61 = f32[2,128,256]{2,0,1:T(2,128)S(1)} fusion(f32[96,128,256]{2,0,1:T(8,128)} %copy.44, pred[96]{0:T(512)(128)(4,1)S(1)} %iota_compare_fusion, s32[96]{0:T(128)S(1)} %get-tuple-element.17), kind=kOutput, calls=%fused_computation.93 | convolution fusion | flops 75497856 | bytes 12845536 | tf_op jit(solution)/shard_map/ik,kaf->iaf/dot_general | solution.py:25
  253.6 68.5 %all-reduce.3.cloned.1.call-done = (f32[256,256]{0,1:T(8,128)}, f32[256,256]{0,1:T(8,128)}) async-done(((f32[256,256]{0,1:T(8,128)}, f32[256,256]{0,1:T(8,128)}), (f32[256,256]{0,1:T(8,128)}, f32[256,256]{0,1:T(8,128)})) %all-reduce.3.cloned.1.call-update) | async-done | bytes 524304 | tf_op jit(solution)/shard_map/psum | solution.py:56
  324.2 39.5 %all-gather.11.cloned.1.call-done = bf16[2048,256]{1,0:T(8,128)(2,1)} async-done(((bf16[256,256]{1,0:T(8,128)(2,1)}), bf16[2048,256]{1,0:T(8,128)(2,1)}) %all-gather.11.cloned.1.call-update) | async-done | bytes 1048592 | tf_op jit(solution)/shard_map/all_gather | solution.py:62
  363.7 7.1 %gather_fusion.3 = bf16[96,128,256]{2,1,0:T(8,128)(2,1)} fusion(bf16[16,128,256]{2,1,0:T(8,128)(2,1)} %bitcast.142, s32[1024]{0:T(1024)S(1)} %pad_clamp_fusion), kind=kCustom, calls=%fused_computation.3 | custom fusion | bytes 12583296 | tf_op jit(solution)/shard_map/gather | solution.py:19
  370.7 10.1 %convolution_bitcast_fusion = f32[96,128,256]{1,2,0:T(8,128)} fusion(bf16[96,128,256]{2,1,0:T(8,128)(2,1)} %gather_fusion.3, bf16[1,2,96,128,128]{4,3,2,1,0:T(8,128)(2,1)} %param.14), kind=kOutput, calls=%fused_computation.4 | convolution fusion | flops 805306368 | bytes 22020096 | tf_op jit(solution)/shard_map/kab,kbf->kaf/dot_general | solution.py:20
  380.8 12.8 %copy.47 = f32[96,128,256]{2,0,1:T(8,128)} copy(f32[96,128,256]{1,2,0:T(8,128)} %convolution_bitcast_fusion) | data formatting | bytes 25165824 | tf_op jit(solution)/shard_map/kab,kbf->kaf/dot_general | solution.py:20
  393.6 7.0 %fusion.59 = f32[2,128,256]{2,0,1:T(2,128)S(1)} fusion(f32[96,128,256]{2,0,1:T(8,128)} %copy.47, pred[96]{0:T(512)(128)(4,1)S(1)} %iota_compare_fusion, s32[96]{0:T(128)S(1)} %get-tuple-element.17), kind=kOutput, calls=%fused_computation.91 | convolution fusion | flops 75497856 | bytes 12845536 | tf_op jit(solution)/shard_map/ik,kaf->iaf/dot_general | solution.py:25
  (51 shorter events, 14.8 us)
Async XLA Ops:
  7.2 46.4 %all-gather.5.cloned.1.call-start = ((), (), s32[]{:S(2)}) async-start(), calls=%async_computation | async-start | bytes 1179648 | tf_op jit(solution)/shard_map/all_gather | solution.py:62
  9.4 121.3 %all-gather.7.cloned.1.call-start = ((), (), s32[]{:S(2)}) async-start(), calls=%async_computation.1 | async-start | bytes 1179648 | tf_op jit(solution)/shard_map/all_gather | solution.py:62
  83.5 7.1 %copy-start = (bf16[1,2,2,256,256]{4,3,2,1,0:T(8,128)(2,1)S(1)}, bf16[1,2,2,256,256]{4,3,2,1,0:T(8,128)(2,1)}, u32[]{:S(2)}) copy-start(bf16[1,2,2,256,256]{4,3,2,1,0:T(8,128)(2,1)} %param.12) | copy-start | bytes 1572868
  83.5 7.1 %copy-start.7 = (bf16[1,2,256,256]{3,2,1,0:T(8,128)(2,1)S(1)}, bf16[1,2,256,256]{3,2,1,0:T(8,128)(2,1)}, u32[]{:S(2)}) copy-start(bf16[1,2,256,256]{3,2,1,0:T(8,128)(2,1)} %param.13) | copy-start | bytes 786436
  91.6 121.0 %all-gather.9.cloned.1.call-start = ((), (), s32[]{:S(2)}) async-start(), calls=%async_computation.2 | async-start | bytes 1179648 | tf_op jit(solution)/shard_map/all_gather | solution.py:62
  160.6 10.4 %copy-start.5 = (bf16[256,256]{1,0:T(8,128)(2,1)S(1)}, bf16[256,256]{1,0:T(8,128)(2,1)}, u32[]{:S(2)}) copy-start(bf16[256,256]{1,0:T(8,128)(2,1)} %param.10) | copy-start | bytes 393220
  160.6 12.2 %copy-start.1 = (bf16[1,2,2,256,256]{4,3,2,1,0:T(8,128)(2,1)S(1)}, bf16[1,2,2,256,256]{4,3,2,1,0:T(8,128)(2,1)}, u32[]{:S(2)}) copy-start(bf16[1,2,2,256,256]{4,3,2,1,0:T(8,128)(2,1)} %param.11) | copy-start | bytes 1572868
  160.6 12.2 %copy-start.6 = (bf16[1,256,256]{2,1,0:T(8,128)(2,1)S(1)}, bf16[1,256,256]{2,1,0:T(8,128)(2,1)}, u32[]{:S(2)}) copy-start(bf16[1,256,256]{2,1,0:T(8,128)(2,1)} %param.9) | copy-start | bytes 393220
  167.7 3.2 collective-permute-start
  171.9 150.2 %all-reduce.3.cloned.1.call-start = ((), (), s32[]{:S(2)}) async-start(), calls=%async_computation.4 | async-start | bytes 1048576 | tf_op jit(solution)/shard_map/psum | solution.py:56
  242.5 9.3 %copy-start.2 = (bf16[256,256]{1,0:T(8,128)(2,1)S(1)}, bf16[256,256]{1,0:T(8,128)(2,1)}, u32[]{:S(2)}) copy-start(bf16[256,256]{1,0:T(8,128)(2,1)} %fusion.15) | copy-start | bytes 393220
  242.5 9.3 %copy-start.3 = (bf16[256,256]{1,0:T(8,128)(2,1)S(1)}, bf16[256,256]{1,0:T(8,128)(2,1)}, u32[]{:S(2)}) copy-start(bf16[256,256]{1,0:T(8,128)(2,1)} %fusion.16) | copy-start | bytes 393220
  242.5 9.3 %copy-start.4 = (bf16[256,256]{1,0:T(8,128)(2,1)S(1)}, bf16[256,256]{1,0:T(8,128)(2,1)}, u32[]{:S(2)}) copy-start(bf16[256,256]{1,0:T(8,128)(2,1)} %add_convert_fusion) | copy-start | bytes 393220
  250.6 113.1 %all-gather.11.cloned.1.call-start = ((), (), s32[]{:S(2)}) async-start(), calls=%async_computation.3 | async-start | bytes 1179648 | tf_op jit(solution)/shard_map/all_gather | solution.py:62
Sparse Core Ops, SparseCore 0:
  10.7 42.8 all-gather.4
  91.7 38.8 all-gather.6
  172.0 40.5 all-gather.8
  250.7 71.3 all-reduce.2
  324.3 39.3 all-gather.10
where the time goes:
time: 409 us; the launch traced here: 408 us
  waiting for transfers between devices  228 us (56%)
  local copies, waits for them, and re-layouts  82.6 us (20%)
  matrix products  75.5 us (18%)
  between operations  14.2 us (3%)
  other arithmetic  5.81 us (1%)
    all_gather x4, waiting for transfers between devices, shards(): gathered = lax.all_gather(image, 'rows', axis=0, tiled=True)  157 us
    psum x1, waiting for transfers between devices, shards(): weight_acc[layer] = weight_acc[layer] + lax.psum(term, 'rows')  68.5 us
    dot_general x4, local copies, waits for them, and re-layouts, tile_product(): jnp.einsum('kab,kbf->kaf', values, blocks, preferred_element_type=jnp.flo...  51 us
    dot_general x4, matrix products, tile_product(): jnp.einsum('kab,kbf->kaf', values, blocks, preferred_element_type=jnp.flo...  40.3 us
    gather x4, local copies, waits for them, and re-layouts, tile_product(): blocks = gathered.reshape(-1, tile, width)[index]  28.4 us
    dot_general x4, matrix products, tile_product(): jnp.einsum('ik,kaf->iaf', select, products, precision=lax.Precision.HIGHEST)  28.2 us
  transfers between devices with their start and end apart: 6, of which 6 were waited for; matrix products, arithmetic and copies ran while one was open for 3% of the time, Pallas kernels for 0%

commit v1 on v0

v1 whole, which is shorter than its diff:
```python
import functools

import jax
import jax.numpy as jnp
import numpy as np
from jax import lax
from jax.experimental import pallas as pl
from jax.experimental.pallas import tpu as pltpu
from jax.sharding import PartitionSpec as P

ALPHA = 0.1
BETA_SCALE = 0.5
VMEM = pl.BlockSpec(memory_space=pltpu.VMEM)
SMEM = pl.BlockSpec(memory_space=pltpu.SMEM)


def cost(flops, nbytes):
    return pl.CostEstimate(flops=flops, bytes_accessed=nbytes, transcendentals=0)


def passed_along(block, axis, distance):
    devices = range(lax.axis_size(axis))
    route = [(i - distance, i) for i in devices if i - distance in devices]
    return lax.ppermute(block, axis, route)


def exchange(blocks):
    return lax.all_to_all(blocks, "rows", 0, 0, tiled=True)


def densify_kernel(row_tiles, n, tile, me_ref, rows_ref, cols_ref, count_ref, vals_ref, out_ref, acc):
    step = pl.program_id(0)
    chunk = vals_ref.shape[0]
    me = me_ref[0]

    @pl.when(step == 0)
    def _():
        acc[...] = jnp.zeros_like(acc)

    base = step * chunk

    def add(i, carry):
        entry = base + i
        row = rows_ref[entry]
        col = cols_ref[entry]
        owner = lax.div(col, row_tiles)
        block = lax.rem(col, row_tiles)
        slot = jnp.where((owner == me) & (block > 0), n - 1 + block, owner)
        rows = pl.ds(pl.multiple_of(row * tile, tile), tile)
        cols = pl.ds(pl.multiple_of(slot * tile, tile), tile)
        acc[rows, cols] += vals_ref[i].astype(jnp.float32)
        return carry

    lax.fori_loop(0, jnp.clip(count_ref[0] - base, 0, chunk), add, 0)

    @pl.when(step == pl.num_programs(0) - 1)
    def _():
        out_ref[...] = acc[...].astype(jnp.bfloat16)


def densify(me, rows, cols, count, vals, row_tiles, n):
    entries, tile, _ = vals.shape
    steps = 4 if entries % 4 == 0 else 1
    chunk = entries // steps
    wide = (n + row_tiles - 1) * tile
    return pl.pallas_call(
        functools.partial(densify_kernel, row_tiles, n, tile),
        grid=(steps,),
        out_shape=jax.ShapeDtypeStruct((row_tiles * tile, wide), jnp.bfloat16),
        in_specs=[SMEM, SMEM, SMEM, SMEM, pl.BlockSpec((chunk, tile, tile), lambda i: (i, 0, 0))],
        out_specs=pl.BlockSpec((row_tiles * tile, wide), lambda i: (0, 0)),
        scratch_shapes=[pltpu.VMEM((row_tiles * tile, wide), jnp.float32)],
        compiler_params=pltpu.CompilerParams(vmem_limit_bytes=24 * 2**20),
        cost_estimate=cost(entries * tile * tile * 20, vals.size * 2),
        name="densify",
    )(me, rows, cols, count, vals)


def spread_of(adj_ref, recv_ref, own_ref):
    n, tile, width = recv_ref.shape
    total = jnp.dot(
        adj_ref[:, : n * tile],
        recv_ref[...].reshape(n * tile, width),
        preferred_element_type=jnp.float32,
    )
    rest = own_ref.shape[0] - tile
    if rest:
        total = total + jnp.dot(
            adj_ref[:, n * tile :], own_ref[tile:, :], preferred_element_type=jnp.float32
        )
    return ((1.0 - ALPHA) * total).astype(jnp.bfloat16)


def emit_image(grad, beta, preact_ref, weight_ref, want_ref, image_ref, masked_ref, send_ref):
    tile = send_ref.shape[1]
    masked = jnp.where(preact_ref[...] > 0, grad, jnp.zeros_like(grad))
    masked_ref[...] = masked
    product = lax.dot_general(
        masked, weight_ref[...], (((1,), (1,)), ((), ())), preferred_element_type=jnp.float32
    )
    image = ((1.0 - beta) * masked.astype(jnp.float32) + beta * product).astype(jnp.bfloat16)
    image_ref[...] = image
    for d in range(send_ref.shape[0]):
        send_ref[d] = image_ref[pl.ds(pl.multiple_of(want_ref[d] * tile, tile), tile), :]
    return image


def entry_kernel(beta_ref, want_ref, grad_ref, preact_ref, weight_ref, image_ref, masked_ref, send_ref):
    emit_image(
        grad_ref[...], beta_ref[0], preact_ref, weight_ref, want_ref, image_ref, masked_ref, send_ref
    )


def middle_kernel(
    beta_ref, want_ref, adj_ref, recv_ref, own_ref, before_ref, preact_ref, weight_ref,
    image_ref, masked_ref, send_ref, toward_ref,
):
    grad = spread_of(adj_ref, recv_ref, own_ref)
    image = emit_image(
        grad, beta_ref[0], preact_ref, weight_ref, want_ref, image_ref, masked_ref, send_ref
    )
    toward_ref[...] = before_ref[...].astype(jnp.float32) + ALPHA * image.astype(jnp.float32)


def middle_first_kernel(
    beta_ref, want_ref, adj_ref, recv_ref, own_ref, preact_ref, weight_ref,
    image_ref, masked_ref, send_ref, toward_ref,
):
    grad = spread_of(adj_ref, recv_ref, own_ref)
    image = emit_image(
        grad, beta_ref[0], preact_ref, weight_ref, want_ref, image_ref, masked_ref, send_ref
    )
    toward_ref[...] = ALPHA * own_ref[...].astype(jnp.float32) + ALPHA * image.astype(jnp.float32)


def exit_kernel(adj_ref, recv_ref, own_ref, grad_ref):
    grad_ref[...] = spread_of(adj_ref, recv_ref, own_ref)


def shards(grad_in, grad_last, support, preact, weights, tile_vals, tile_row, tile_col, tile_count):
    section = lax.axis_index("section")
    me = lax.axis_index("rows")
    n = lax.axis_size("rows")
    sections = lax.axis_size("section")
    ticks = support.shape[1]
    layers = support.shape[2]
    rows_dev, width = grad_last.shape
    tile = tile_vals.shape[-1]
    row_tiles = rows_dev // tile
    me_arr = jnp.full((1,), me, jnp.int32)

    owner = tile_col[0] // row_tiles
    named = jnp.where(
        owner[:, :, None] == jnp.arange(n)[None, None, :], (tile_col[0] % row_tiles)[:, :, None], 0
    )
    pick = jnp.max(named, axis=1)
    pick = jnp.where(jnp.arange(n)[None, :] == me, 0, pick).astype(jnp.int32)
    want = exchange(pick.T)

    image_shapes = [
        jax.ShapeDtypeStruct((rows_dev, width), jnp.bfloat16),
        jax.ShapeDtypeStruct((rows_dev, width), jnp.bfloat16),
        jax.ShapeDtypeStruct((n, tile, width), jnp.bfloat16),
    ]
    toward_shape = jax.ShapeDtypeStruct((rows_dev, width), jnp.float32)
    small = cost(2 * rows_dev * width * width, (3 + n) * rows_dev * width)
    large = cost(
        2 * rows_dev * width * (width + (n + 1) * tile), (6 + 2 * n) * rows_dev * width
    )
    params = pltpu.CompilerParams(vmem_limit_bytes=24 * 2**20)
    weight_acc = [jnp.zeros((width, width), jnp.float32) for layer in range(layers)]
    handed = []
    initial = []
    for tick in range(ticks):
        if tick == 0:
            grad = grad_in[0]
        else:
            passed = passed_along(handed[-1], "section", -1)
            grad = jnp.where(section == sections - 1, grad_last, passed)
        adj = densify(
            me_arr, tile_row[0, tick], tile_col[0, tick], tile_count[0, tick], tile_vals[0, tick],
            row_tiles, n,
        )
        image = recv = toward = None
        for layer in reversed(range(layers)):
            beta = jnp.log(BETA_SCALE / (layers * section + layer + 1).astype(jnp.float32) + 1.0)
            beta_arr = jnp.full((1,), beta, jnp.float32)
            head = (beta_arr, want[:, tick])
            tail = (preact[0, tick, layer], weights[0, layer])
            if layer == layers - 1:
                image, masked, send = pl.pallas_call(
                    entry_kernel,
                    out_shape=image_shapes,
                    in_specs=[SMEM] * 2 + [VMEM] * 3,
                    out_specs=[VMEM] * 3,
                    compiler_params=params,
                    cost_estimate=small,
                    name="entry",
                )(*head, grad, *tail)
            else:
                first = layer == layers - 2
                before = () if first else (toward,)
                image, masked, send, toward = pl.pallas_call(
                    middle_first_kernel if first else middle_kernel,
                    out_shape=image_shapes + [toward_shape],
                    in_specs=[SMEM] * 2 + [VMEM] * (5 + len(before)),
                    out_specs=[VMEM] * 4,
                    compiler_params=params,
                    cost_estimate=large,
                    name="middle",
                )(*head, adj, recv, image, *before, *tail)
            term = beta * jnp.dot(
                support[0, tick, layer].T, masked, preferred_element_type=jnp.float32
            )
            weight_acc[layer] = weight_acc[layer] + term
            recv = exchange(send)
        handed.append(
            pl.pallas_call(
                exit_kernel,
                out_shape=image_shapes[0],
                in_specs=[VMEM] * 3,
                out_specs=VMEM,
                compiler_params=params,
                cost_estimate=large,
                name="exit",
            )(adj, recv, image)
        )
        initial.append(toward)
    parts = jnp.stack(weight_acc).reshape(layers, n, width // n, width).swapaxes(0, 1)
    summed = jnp.sum(exchange(parts.astype(jnp.bfloat16)).astype(jnp.float32), axis=0)
    whole = exchange(jnp.broadcast_to(summed[None].astype(jnp.bfloat16), parts.shape))
    weight_grad = whole.astype(jnp.float32).swapaxes(0, 1).reshape(layers, width, width)
    return (jnp.stack(handed)[:, None], jnp.stack(initial)[None], weight_grad[None])


def solution(mesh):
    return jax.shard_map(
        shards,
        mesh=mesh,
        in_specs=(
            P("section", "rows", None),
            P("rows", None),
            P("section", None, None, "rows", None),
            P("section", None, None, "rows", None),
            P("section", None, None, None),
            P("section", None, "rows", None, None),
            P("section", None, "rows"),
            P("section", None, "rows"),
            P("section", None, "rows"),
        ),
        out_specs=(
            P(None, "section", "rows", None),
            P("section", None, "rows", None),
            P("section", None, None, None),
        ),
        check_vma=False,
    )
```

time: 409 us -> 140 us (0.34)
  waiting for transfers between devices: 228 us -> 39.6 us
  matrix products: 75.5 us -> 1.81 us
  local copies, waits for them, and re-layouts: 82.6 us -> 22.3 us
  blocking collectives: 0 us -> 31.4 us
  starting transfers between devices: 2.16 us -> 24.1 us
  Pallas kernels: 0 us -> 13.5 us
  between operations: 14.2 us -> 1.06 us
    all_gather x4 -> x0, waiting for transfers between devices: 157 us -> none  [shards(): gathered = lax.all_gather(image, 'rows', axis=0, tiled=True)]
    dot_general x12 -> x0, matrix products: 73.1 us -> none  [the longest x4 40.3 us: tile_product(): jnp.einsum('kab,kbf->kaf', values, blocks, preferred_element_type=jnp.flo...]
    psum x1 -> x0, waiting for transfers between devices: 68.5 us -> none  [shards(): weight_acc[layer] = weight_acc[layer] + lax.psum(term, 'rows')]
    dot_general x4 -> x0, local copies, waits for them, and re-layouts: 51 us -> none  [tile_product(): jnp.einsum('kab,kbf->kaf', values, blocks, preferred_element_type=jnp.flo...]
    all_to_all x0 -> x5, waiting for transfers between devices: none -> 37.3 us  [exchange(): return lax.all_to_all(blocks, 'rows', 0, 0, tiled=True)]
    all_to_all x0 -> x2, blocking collectives: none -> 31.4 us  [exchange(): return lax.all_to_all(blocks, 'rows', 0, 0, tiled=True)]
    gather x4 -> x0, local copies, waits for them, and re-layouts: 28.4 us -> none  [tile_product(): blocks = gathered.reshape(-1, tile, width)[index]]
    all_to_all x0 -> x5, starting transfers between devices: none -> 22.8 us  [exchange(): return lax.all_to_all(blocks, 'rows', 0, 0, tiled=True)]
  transfers between devices with their start and end apart: 6 -> 6, of which waited for: 6 -> 6; matrix products, arithmetic and copies ran while one was open for 3% -> 9% of each run, Pallas kernels for 0% -> 4%
where the time goes in v1:
time: 140 us; the launch traced here: 139 us
  waiting for transfers between devices  39.6 us (28%)
  blocking collectives  31.4 us (22%)
  starting transfers between devices  24.1 us (17%)
  local copies, waits for them, and re-layouts  22.3 us (16%)
  Pallas kernels  13.5 us (10%)
  other arithmetic  5.1 us (4%)
  matrix products  1.81 us (1%)
    all_to_all x5, waiting for transfers between devices, exchange(): return lax.all_to_all(blocks, 'rows', 0, 0, tiled=True)  37.3 us
    all_to_all x2, blocking collectives, exchange(): return lax.all_to_all(blocks, 'rows', 0, 0, tiled=True)  31.4 us
    all_to_all x5, starting transfers between devices, exchange(): return lax.all_to_all(blocks, 'rows', 0, 0, tiled=True)  22.8 us
    unnamed x44, local copies, waits for them, and re-layouts  11.7 us
    pallas_call x2, Pallas kernels, densify(): pl.pallas_call(functools.partial(densify_kernel, row_tiles, n, tile), gri...  5.8 us
    squeeze x1, local copies, waits for them, and re-layouts, shards(): tile_vals[0, tick]  4.2 us
    pallas_call x2, Pallas kernels, shards(): pl.pallas_call(middle_first_kernel if first else middle_kernel, out_shape...  4 us
    squeeze x2, local copies, waits for them, and re-layouts, shards(): tail = (preact[0, tick, layer], weights[0, layer])  2.81 us
  transfers between devices with their start and end apart: 6, of which 6 were waited for; matrix products, arithmetic and copies ran while one was open for 9% of the time, Pallas kernels for 4%

profile of v1, /device:TPU:0, one launch (start us, length us, event | category | flops | bytes accessed | tf_op | source)
XLA Modules:
  0.0 138.8 jit_solution(8763709559548278985)
XLA Ops:
  2.1 7.3 %all-to-all-start = ((s32[8,1,2]{2,1,0:T(1,128)}), s32[8,1,2]{2,1,0:T(1,128)S(1)}, u32[]{:S(2)}, u32[]{:S(2)}) async-start(s32[8,1,2]{2,1,0:T(1,128)} %copy.24), calls=%async_computation | async-start | bytes 8192 | tf_op jit(solution)/shard_map/all_to_all | solution.py:28
  9.4 1.8 %slice_bitcast_fusion.2 = (bf16[256,256]{1,0:T(8,128)(2,1)S(1)}, bf16[256,256]{1,0:T(8,128)(2,1)}, bf16[256,256]{1,0:T(8,128)(2,1)S(1)}, bf16[256,256]{1,0:T(8,128)(2,1)}) fusion(bf16[1,2,2,256,256]{4,3,2,1,0:T(8,128)(2,1)} %param.12), kind=kLoop, calls=%fused_computation.22 | loop fusion | bytes 1048576 | tf_op jit(solution)/shard_map/squeeze | solution.py:189
  12.3 3.5 %all-to-all-done = s32[8,1,2]{2,1,0:T(1,128)S(1)} async-done(((s32[8,1,2]{2,1,0:T(1,128)}), s32[8,1,2]{2,1,0:T(1,128)S(1)}, u32[]{:S(2)}, u32[]{:S(2)}) %all-to-all-start) | async-done | bytes 96 | tf_op jit(solution)/shard_map/all_to_all | solution.py:28
  16.8 1.6 %entry.2 = (bf16[256,256]{1,0:T(8,128)(2,1)S(1)}, bf16[256,256]{1,0:T(8,128)(2,1)S(1)}, bf16[8,128,256]{2,1,0:T(8,128)(2,1)}) custom-call(f32[1]{0:T(128)} %bitcast.11.beta_ref, s32[8]{0:T(128)S(1)} %get-tuple-element.51.want_ref, bf16[256,256]{1,0:T(8,128)(2,1)S(1)} %bitcast.103, bf16[256,256]{1,0:T(8,128)(2,1)S(1)} %get-tuple-element.47.preact_ref, ...), custom_call_target="tpu_custom_call" | custom-call | flops 33554432 | bytes 720896 | tf_op jit(solution)/shard_map/entry/pallas_call | solution.py:191
  19.7 4.2 %all-to-all-start.1 = ((bf16[8,128,256]{2,1,0:T(8,128)(2,1)}), bf16[8,128,256]{2,1,0:T(8,128)(2,1)}, u32[]{:S(2)}, u32[]{:S(2)}) async-start(bf16[8,128,256]{2,1,0:T(8,128)(2,1)} %get-tuple-element.17), calls=%async_computation.1 | async-start | bytes 1048576 | tf_op jit(solution)/shard_map/all_to_all | solution.py:28
  23.9 1.3 fusion.14
  26.0 4.2 %slice_bitcast_fusion.1 = (bf16[96,128,128]{2,1,0:T(8,128)(2,1)S(1)}, bf16[96,128,128]{2,1,0:T(8,128)(2,1)S(1)}) fusion(bf16[1,2,96,128,128]{4,3,2,1,0:T(8,128)(2,1)} %param.14), kind=kLoop, calls=%fused_computation.1 | loop fusion | bytes 12582912 | tf_op jit(solution)/shard_map/squeeze | solution.py:181
  30.2 2.8 %densify.2.adj_ref = bf16[256,1152]{1,0:T(8,128)(2,1)S(1)} custom-call(s32[1]{0:T(128)} %bitcast.me_ref, s32[96]{0:T(128)S(1)} %get-tuple-element.62.rows_ref, s32[96]{0:T(128)S(1)} %get-tuple-element.53.cols_ref, s32[1]{0:T(128)} %bitcast.3.count_ref, bf16[96,128,128]{2,1,0:T(8,128)(2,1)S(1)} %get-tuple-element.43.vals_ref), custom_call_target="tpu_custom_call" | custom-call | flops 31457280 | bytes 3145728 | tf_op jit(solution)/shard_map/densify/pallas_call | solution.py:66
  33.8 3.4 %all-to-all-done.1.recv_ref = bf16[8,128,256]{2,1,0:T(8,128)(2,1)} async-done(((bf16[8,128,256]{2,1,0:T(8,128)(2,1)}), bf16[8,128,256]{2,1,0:T(8,128)(2,1)}, u32[]{:S(2)}, u32[]{:S(2)}) %all-to-all-start.1) | async-done | bytes 524320 | tf_op jit(solution)/shard_map/all_to_all | solution.py:28
  40.0 1.6 %middle.2 = (bf16[256,256]{1,0:T(8,128)(2,1)S(1)}, bf16[256,256]{1,0:T(8,128)(2,1)S(1)}, bf16[8,128,256]{2,1,0:T(8,128)(2,1)S(1)}, f32[256,256]{1,0:T(8,128)S(1)}) custom-call(f32[1]{0:T(128)} %bitcast.5.beta_ref, s32[8]{0:T(128)S(1)} %get-tuple-element.51.want_ref, bf16[256,1152]{1,0:T(8,128)(2,1)S(1)} %copy-done.4, ...), custom_call_target="tpu_custom_call" | custom-call | flops 184549376 | bytes 1441792 | tf_op jit(solution)/shard_map/middle/pallas_call | solution.py:203
  41.6 17.3 %all_to_all.42.recv_ref = bf16[8,128,256]{2,1,0:T(8,128)(2,1)S(1)} all-to-all(bf16[8,128,256]{2,1,0:T(8,128)(2,1)S(1)} %get-tuple-element.19), channel_id=1, replica_groups=mesh['section'=4,'rows'=8] {'rows'}, dimensions={0} | all-to-all | bytes 1048576 | tf_op jit(solution)/shard_map/all_to_all | solution.py:28
  59.9 1.3 collective-permute-start
  61.2 2.3 %collective-permute-done = bf16[256,256]{1,0:T(8,128)(2,1)} collective-permute-done((bf16[256,256]{1,0:T(8,128)(2,1)}, bf16[256,256]{1,0:T(8,128)(2,1)}, u32[]{:S(2)}, u32[]{:S(2)}) %collective-permute-start) | collective-permute-done | bytes 131104 | tf_op jit(solution)/shard_map/ppermute | solution.py:24
  68.2 4.2 %all-to-all-start.3 = ((bf16[8,128,256]{2,1,0:T(8,128)(2,1)}), bf16[8,128,256]{2,1,0:T(8,128)(2,1)}, u32[]{:S(2)}, u32[]{:S(2)}) async-start(bf16[8,128,256]{2,1,0:T(8,128)(2,1)} %copy-done.5), calls=%async_computation.3 | async-start | bytes 1048576 | tf_op jit(solution)/shard_map/all_to_all | solution.py:28
  72.4 3.0 %densify.3.adj_ref = bf16[256,1152]{1,0:T(8,128)(2,1)S(1)} custom-call(s32[1]{0:T(128)} %bitcast.me_ref, s32[96]{0:T(128)S(1)} %get-tuple-element.61.rows_ref, s32[96]{0:T(128)S(1)} %get-tuple-element.54.cols_ref, s32[1]{0:T(128)} %bitcast.20.count_ref, bf16[96,128,128]{2,1,0:T(8,128)(2,1)S(1)} %get-tuple-element.44.vals_ref), custom_call_target="tpu_custom_call" | custom-call | flops 31457280 | bytes 3145728 | tf_op jit(solution)/shard_map/densify/pallas_call | solution.py:66
  77.0 9.5 %all-to-all-done.3.recv_ref = bf16[8,128,256]{2,1,0:T(8,128)(2,1)} async-done(((bf16[8,128,256]{2,1,0:T(8,128)(2,1)}), bf16[8,128,256]{2,1,0:T(8,128)(2,1)}, u32[]{:S(2)}, u32[]{:S(2)}) %all-to-all-start.3) | async-done | bytes 524320 | tf_op jit(solution)/shard_map/all_to_all | solution.py:28
  88.5 2.4 %middle.3 = (bf16[256,256]{1,0:T(8,128)(2,1)S(1)}, bf16[256,256]{1,0:T(8,128)(2,1)S(1)}, bf16[8,128,256]{2,1,0:T(8,128)(2,1)}, f32[256,256]{1,0:T(8,128)S(1)}) custom-call(f32[1]{0:T(128)} %bitcast.5.beta_ref, s32[8]{0:T(128)S(1)} %get-tuple-element.52.want_ref, bf16[256,1152]{1,0:T(8,128)(2,1)S(1)} %copy-done.1, ...), custom_call_target="tpu_custom_call" | custom-call | flops 184549376 | bytes 1441792 | tf_op jit(solution)/shard_map/middle/pallas_call | solution.py:203
  91.0 1.1 fusion.2
  92.1 14.1 %all_to_all.43 = bf16[8,2,32,256]{3,2,1,0:T(8,128)(2,1)S(1)} all-to-all(bf16[8,2,32,256]{3,2,1,0:T(8,128)(2,1)S(1)} %maximum_bitcast_fusion.2), channel_id=1, replica_groups=mesh['section'=4,'rows'=8] {'rows'}, dimensions={0} | all-to-all | bytes 524288 | tf_op jit(solution)/shard_map/all_to_all | solution.py:28
  106.3 3.6 %all-to-all-start.4 = ((bf16[8,128,256]{2,1,0:T(8,128)(2,1)}), bf16[8,128,256]{2,1,0:T(8,128)(2,1)S(1)}, u32[]{:S(2)}, u32[]{:S(2)}) async-start(bf16[8,128,256]{2,1,0:T(8,128)(2,1)} %get-tuple-element.23), calls=%async_computation.4 | async-start | bytes 1048576 | tf_op jit(solution)/shard_map/all_to_all | solution.py:28
  109.9 14.6 %all-to-all-done.4.recv_ref = bf16[8,128,256]{2,1,0:T(8,128)(2,1)S(1)} async-done(((bf16[8,128,256]{2,1,0:T(8,128)(2,1)}), bf16[8,128,256]{2,1,0:T(8,128)(2,1)S(1)}, u32[]{:S(2)}, u32[]{:S(2)}) %all-to-all-start.4) | async-done | bytes 524320 | tf_op jit(solution)/shard_map/all_to_all | solution.py:28
  125.2 3.6 %all-to-all-start.6 = ((bf16[8,2,32,256]{3,2,1,0:T(8,128)(2,1)}), bf16[8,2,32,256]{3,2,1,0:T(8,128)(2,1)S(1)}, u32[]{:S(2)}, u32[]{:S(2)}) async-start(bf16[8,2,32,256]{3,2,1,0:T(8,128)(2,1)} %broadcast_in_dim.60), calls=%async_computation.6 | async-start | bytes 524288 | tf_op jit(solution)/shard_map/all_to_all | solution.py:28
  130.0 1.6 %maximum_bitcast_fusion.1 = bf16[2,1,256,256]{3,2,1,0:T(8,128)(2,1)} fusion(bf16[1,256,256]{2,1,0:T(8,128)(2,1)S(1)} %bitcast.100, bf16[1,256,256]{2,1,0:T(8,128)(2,1)} %bitcast.17), kind=kLoop, calls=%fused_computation.9 | loop fusion | flops 131072 | bytes 524288
  131.7 6.3 %all-to-all-done.6 = bf16[8,2,32,256]{3,2,1,0:T(8,128)(2,1)S(1)} async-done(((bf16[8,2,32,256]{3,2,1,0:T(8,128)(2,1)}), bf16[8,2,32,256]{3,2,1,0:T(8,128)(2,1)S(1)}, u32[]{:S(2)}, u32[]{:S(2)}) %all-to-all-start.6) | async-done | bytes 262176 | tf_op jit(solution)/shard_map/all_to_all | solution.py:28
  (65 shorter events, 21.2 us)
Async XLA Ops:
  2.1 13.6 %all-to-all-start = ((s32[8,1,2]{2,1,0:T(1,128)}), s32[8,1,2]{2,1,0:T(1,128)S(1)}, u32[]{:S(2)}, u32[]{:S(2)}) async-start(s32[8,1,2]{2,1,0:T(1,128)} %copy.24), calls=%async_computation | async-start | bytes 8192 | tf_op jit(solution)/shard_map/all_to_all | solution.py:28
  15.9 0.9 copy-start.10
  19.7 17.5 %all-to-all-start.1 = ((bf16[8,128,256]{2,1,0:T(8,128)(2,1)}), bf16[8,128,256]{2,1,0:T(8,128)(2,1)}, u32[]{:S(2)}, u32[]{:S(2)}) async-start(bf16[8,128,256]{2,1,0:T(8,128)(2,1)} %get-tuple-element.17), calls=%async_computation.1 | async-start | bytes 1048576 | tf_op jit(solution)/shard_map/all_to_all | solution.py:28
  33.0 0.8 copy-start.3
  37.2 1.1 copy-start.4
  38.2 0.9 copy-start.7
  39.1 0.9 copy-start.12
  41.6 18.3 %copy-start.8 = (f32[256,256]{1,0:T(8,128)}, f32[256,256]{1,0:T(8,128)S(1)}, u32[]{:S(2)}) copy-start(f32[256,256]{1,0:T(8,128)S(1)} %get-tuple-element.25) | copy-start | bytes 786436
  41.6 18.2 %copy-start.17 = (bf16[256,256]{1,0:T(8,128)(2,1)}, bf16[256,256]{1,0:T(8,128)(2,1)S(1)}, u32[]{:S(2)}) copy-start(bf16[256,256]{1,0:T(8,128)(2,1)S(1)} %get-tuple-element.27) | copy-start | bytes 393220
  59.9 3.6 %collective-permute-start = (bf16[256,256]{1,0:T(8,128)(2,1)}, bf16[256,256]{1,0:T(8,128)(2,1)}, u32[]{:S(2)}, u32[]{:S(2)}) collective-permute-start(bf16[256,256]{1,0:T(8,128)(2,1)} %exit.2), channel_id=1, source_target_pairs={{8,0},{16,8},{24,16},{9,1},{17,9},{25,17},{10,2},{18,10},{26,18},{... | collective-permute-start | bytes 393224 | tf_op jit(solution)/shard_map/ppermute | solution.py:24
  64.4 0.9 copy-start.6
  66.1 0.8 copy-start.5
  68.2 18.3 %all-to-all-start.3 = ((bf16[8,128,256]{2,1,0:T(8,128)(2,1)}), bf16[8,128,256]{2,1,0:T(8,128)(2,1)}, u32[]{:S(2)}, u32[]{:S(2)}) async-start(bf16[8,128,256]{2,1,0:T(8,128)(2,1)} %copy-done.5), calls=%async_computation.3 | async-start | bytes 1048576 | tf_op jit(solution)/shard_map/all_to_all | solution.py:28
  72.4 3.9 %copy-start.16 = (bf16[256,256]{1,0:T(8,128)(2,1)S(1)}, bf16[256,256]{1,0:T(8,128)(2,1)}, u32[]{:S(2)}) copy-start(bf16[256,256]{1,0:T(8,128)(2,1)} %copy-done.15) | copy-start | bytes 393220
  72.4 3.9 %copy-start.21 = (bf16[1,2,2,256,256]{4,3,2,1,0:T(8,128)(2,1)S(1)}, bf16[1,2,2,256,256]{4,3,2,1,0:T(8,128)(2,1)}, u32[]{:S(2)}) copy-start(bf16[1,2,2,256,256]{4,3,2,1,0:T(8,128)(2,1)} %param.11) | copy-start | bytes 1572868
  72.4 4.1 %copy-start.18 = (bf16[256,256]{1,0:T(8,128)(2,1)S(1)}, bf16[256,256]{1,0:T(8,128)(2,1)}, u32[]{:S(2)}) copy-start(bf16[256,256]{1,0:T(8,128)(2,1)} %copy-done.17) | copy-start | bytes 393220
  72.4 4.3 %copy-start.20 = (bf16[256,256]{1,0:T(8,128)(2,1)S(1)}, bf16[256,256]{1,0:T(8,128)(2,1)}, u32[]{:S(2)}) copy-start(bf16[256,256]{1,0:T(8,128)(2,1)} %copy-done.19) | copy-start | bytes 393220
  75.5 0.8 copy-start
  76.8 52.1 %copy-start.9 = (f32[256,256]{1,0:T(8,128)S(1)}, f32[256,256]{1,0:T(8,128)}, u32[]{:S(2)}) copy-start(f32[256,256]{1,0:T(8,128)} %copy-done.8) | copy-start | bytes 786436
  86.5 1.1 copy-start.1
  87.6 0.9 copy-start.14
  88.5 41.2 %copy-start.2 = (bf16[256,1152]{1,0:T(8,128)(2,1)S(1)}, bf16[256,1152]{1,0:T(8,128)(2,1)}, u32[]{:S(2)}) copy-start(bf16[256,1152]{1,0:T(8,128)(2,1)} %copy-done) | copy-start | bytes 1769476
  106.3 18.2 %all-to-all-start.4 = ((bf16[8,128,256]{2,1,0:T(8,128)(2,1)}), bf16[8,128,256]{2,1,0:T(8,128)(2,1)S(1)}, u32[]{:S(2)}, u32[]{:S(2)}) async-start(bf16[8,128,256]{2,1,0:T(8,128)(2,1)} %get-tuple-element.23), calls=%async_computation.4 | async-start | bytes 1048576 | tf_op jit(solution)/shard_map/all_to_all | solution.py:28
  125.2 12.7 %all-to-all-start.6 = ((bf16[8,2,32,256]{3,2,1,0:T(8,128)(2,1)}), bf16[8,2,32,256]{3,2,1,0:T(8,128)(2,1)S(1)}, u32[]{:S(2)}, u32[]{:S(2)}) async-start(bf16[8,2,32,256]{3,2,1,0:T(8,128)(2,1)} %broadcast_in_dim.60), calls=%async_computation.6 | async-start | bytes 524288 | tf_op jit(solution)/shard_map/all_to_all | solution.py:28
  (4 other events, 2.6 us)

commit v2 on v0

v2 whole, which is shorter than its diff:
```python
import functools

import jax
import jax.numpy as jnp
from jax import lax
from jax.experimental import pallas as pl
from jax.experimental.pallas import tpu as pltpu
from jax.sharding import PartitionSpec as P

ALPHA = 0.1
BETA_SCALE = 0.5
VMEM = pl.BlockSpec(memory_space=pltpu.VMEM)
SMEM = pl.BlockSpec(memory_space=pltpu.SMEM)
ANY = pl.BlockSpec(memory_space=pl.ANY)
PARAMS = pltpu.CompilerParams(vmem_limit_bytes=24 * 2**20)
F32 = jnp.float32
BF16 = jnp.bfloat16


def cost(flops, nbytes):
    return pl.CostEstimate(flops=flops, bytes_accessed=nbytes, transcendentals=0)


def passed_along(block, axis, distance):
    devices = range(lax.axis_size(axis))
    route = [(i - distance, i) for i in devices if i - distance in devices]
    return lax.ppermute(block, axis, route)


def power_of_two(n):
    return n & (n - 1) == 0


def target(me, k, n):
    return me ^ k if power_of_two(n) else (me + k) % n


def source(me, k, n):
    return me ^ k if power_of_two(n) else (me - k) % n


def dynamic_target(me, k, n):
    return jnp.bitwise_xor(me, k) if power_of_two(n) else lax.rem(me + k, n)


def dynamic_source(me, k, n):
    return jnp.bitwise_xor(me, k) if power_of_two(n) else lax.rem(me - k + n, n)


def exchange(messages):
    n = len(messages) + 1
    got = [None] * (n - 1)
    for k in reversed(range(1, n)):
        route = [(i, target(i, k, n)) for i in range(n)]
        got[k - 1] = lax.ppermute(messages[k - 1], "rows", route)
    return got


def densify_kernel(tick, row_tiles, n, me_ref, rows_ref, cols_ref, count_ref, vals_ref, out_ref, acc):
    step = pl.program_id(0)
    chunk, tile, _ = vals_ref.shape
    me = me_ref[0]

    @pl.when(step == 0)
    def _():
        acc[...] = jnp.zeros_like(acc)

    base = step * chunk

    def add(i, carry):
        row = rows_ref[0, tick, base + i]
        col = cols_ref[0, tick, base + i]
        owner = lax.div(col, row_tiles)
        block = lax.rem(col, row_tiles)
        if power_of_two(n):
            slot = jnp.bitwise_xor(owner, me)
        else:
            slot = lax.rem(me - owner + n, n)
        slot = jnp.where((owner == me) & (block > 0), n - 1 + block, slot)
        rows = pl.ds(pl.multiple_of(row * tile, tile), tile)
        cols = pl.ds(pl.multiple_of(slot * tile, tile), tile)
        acc[rows, cols] += vals_ref[i].astype(F32)
        return carry

    lax.fori_loop(0, jnp.clip(count_ref[0, tick, 0] - base, 0, chunk), add, 0)

    @pl.when(step == pl.num_programs(0) - 1)
    def _():
        out_ref[...] = acc[...].astype(BF16)


def densify(tick, me, rows, cols, count, vals, row_tiles, n):
    _, _, entries, tile, _ = vals.shape
    steps = 4 if entries % 4 == 0 else 1
    chunk = entries // steps
    shape = (row_tiles * tile, (n + row_tiles - 1) * tile)
    return pl.pallas_call(
        functools.partial(densify_kernel, tick, row_tiles, n),
        grid=(steps,),
        out_shape=jax.ShapeDtypeStruct(shape, BF16),
        in_specs=[SMEM] * 4
        + [pl.BlockSpec((None, None, chunk, tile, tile), lambda i: (0, tick, i, 0, 0))],
        out_specs=pl.BlockSpec(shape, lambda i: (0, 0)),
        scratch_shapes=[pltpu.VMEM(shape, F32)],
        compiler_params=PARAMS,
        cost_estimate=cost(entries * tile * tile * 20, entries * tile * tile * 2),
        name="densify",
    )(me, rows, cols, count, vals)


def spread_of(adj_ref, got, own_ref, tile):
    blocks = jnp.concatenate(
        [own_ref[:tile, :]] + [ref[:tile, :] for ref in got] + [own_ref[tile:, :]], axis=0
    )
    total = jnp.dot(adj_ref[...], blocks, preferred_element_type=F32)
    return ((1.0 - ALPHA) * total).astype(BF16)


def layer_kernel(c, *refs):
    refs = list(refs)

    def take(count):
        taken, refs[:count] = refs[:count], []
        return taken

    n, tile = c["n"], c["tile"]
    me_ref, section_ref, picks_ref, preact_all, weight_all = take(5)
    me = me_ref[0]
    section = section_ref[0]
    step = (c["layers"] * section + c["layer"] + 1).astype(F32)
    beta = jnp.log(BETA_SCALE / jnp.full((1, c["width"]), step, F32) + 1.0)
    got = []
    if c["entry"]:
        if c["tick"] == 0:
            (grad_all,) = take(1)
        else:
            last_ref, passed_ref = take(2)
    else:
        adj_ref, own_ref = take(2)
        got = take(n - 1)
        before_ref = take(1)[0] if c["before"] else None
        if c["toward"] and c["tick"] > 0:
            take(1)
    if c["final"]:
        support_all, acc_ref = take(2)
        if c["sum_above"]:
            (above_ref,) = take(1)
    image_ref, masked_ref = take(2)
    sends = take(n - 1)
    toward_ref = take(1)[0] if not c["entry"] else None
    own_sum_ref = take(1)[0] if c["sum_above"] else None
    term_ref = take(1)[0] if c["final"] else None
    if c["toward"]:
        hold_ref, sem = take(2)
    preact_ref, weight_ref, load_sems = take(3)
    loads = [
        (preact_all.at[0, c["tick"], c["layer"]], preact_ref),
        (weight_all.at[0, c["layer"]], weight_ref),
    ]
    if c["entry"] and c["tick"] == 0:
        (grad_ref,) = take(1)
        loads.append((grad_all.at[0], grad_ref))
    if c["final"]:
        (support_ref,) = take(1)
        loads.append((support_all.at[0, c["tick"], c["layer"]], support_ref))
    loads = [pltpu.make_async_copy(a, b, load_sems.at[i]) for i, (a, b) in enumerate(loads)]
    for load in loads:
        load.start()
    if not c["entry"]:
        grad = spread_of(adj_ref, got, own_ref, tile)
    for load in loads:
        load.wait()
    if c["entry"]:
        if c["tick"] == 0:
            grad = grad_ref[...]
        else:
            is_last = section == c["sections"] - 1
            grad = jnp.where(is_last, last_ref[...], passed_ref[...])

    masked = jnp.where(preact_ref[...] > 0, grad, jnp.zeros_like(grad))
    masked_ref[...] = masked
    product = lax.dot_general(
        masked, weight_ref[...], (((1,), (1,)), ((), ())), preferred_element_type=F32
    )
    image = ((1.0 - beta) * masked.astype(F32) + beta * product).astype(BF16)
    image_ref[...] = image
    for k in range(1, n):
        want = picks_ref[dynamic_target(me, k, n), c["tick"] * n + me]
        sends[k - 1][:tile, :] = image_ref[pl.ds(pl.multiple_of(want * tile, tile), tile), :]
    copy = None
    if not c["entry"]:
        before = before_ref[...] if c["before"] else ALPHA * own_ref[...].astype(F32)
        total = before + ALPHA * image.astype(F32)
        if c["toward"]:
            hold_ref[...] = total
            copy = pltpu.make_async_copy(hold_ref, toward_ref.at[0, c["tick"]], sem)
            copy.start()
        else:
            toward_ref[...] = total
    if c["final"]:
        part, room = c["part"], c["room"]
        term = lax.dot_general(
            support_ref[...], masked, (((0,), (0,)), ((), ())), preferred_element_type=F32
        )
        term_ref[...] = acc_ref[...] + beta * term
        at = tile
        if c["sum_above"]:
            total = above_ref[pl.ds(pl.multiple_of(me * part, 8), part), :]
            for ref in got:
                total = total + ref[tile + c["above_at"] : tile + c["above_at"] + part, :].astype(F32)
            own_sum_ref[...] = total.astype(BF16)
            for send in sends:
                send[at : at + part, :] = own_sum_ref[...]
            at += room
        for k in range(1, n):
            start = pl.multiple_of(dynamic_target(me, k, n) * part, 8)
            sends[k - 1][at : at + part, :] = term_ref[pl.ds(start, part), :].astype(BF16)
    if copy is not None:
        copy.wait()


def exit_kernel(c, *refs):
    refs = list(refs)

    def take(count):
        taken, refs[:count] = refs[:count], []
        return taken

    n, tile, part, room = c["n"], c["tile"], c["part"], c["room"]
    me_ref, adj_ref, own_ref = take(3)
    me = me_ref[0]
    got = take(n - 1)
    if c["tick"] > 0:
        take(1)
    if c["final"]:
        (acc_ref,) = take(1)
        own_sum_ref = take(1)[0] if c["above"] else None
    (out_ref,) = take(1)
    grad_ref = None if c["final"] else take(1)[0]
    if c["final"]:
        last_sum_ref, weight_ref = take(2)
    hold_ref, sem = take(2)
    if c["final"] and c["above"]:
        hold_weight_ref, weight_sem = take(2)
    grad = spread_of(adj_ref, got, own_ref, tile)
    hold_ref[...] = grad
    copy = pltpu.make_async_copy(hold_ref, out_ref.at[c["tick"], 0], sem)
    copy.start()
    if c["final"]:
        at = tile + (room if c["above"] else 0)
        total = acc_ref[pl.ds(pl.multiple_of(me * part, 8), part), :]
        for ref in got:
            total = total + ref[at : at + part, :].astype(F32)
        last_sum_ref[...] = total.astype(BF16)
        if c["above"]:
            place(hold_weight_ref, me, n, part, own_sum_ref, [ref.at[tile : tile + part, :] for ref in got])
            weight_copy = pltpu.make_async_copy(hold_weight_ref, weight_ref.at[0, 1], weight_sem)
            weight_copy.start()
            weight_copy.wait()
    else:
        grad_ref[...] = grad
    copy.wait()


def place(whole_ref, me, n, part, own_ref, others):
    whole_ref[pl.ds(pl.multiple_of(me * part, 8), part), :] = own_ref[...].astype(F32)
    for k in range(1, n):
        start = pl.multiple_of(dynamic_source(me, k, n) * part, 8)
        whole_ref[pl.ds(start, part), :] = others[k - 1][...].astype(F32)


def finish_kernel(n, part, *refs):
    me_ref, own_ref = refs[:2]
    others = refs[2 : n + 1]
    weight_ref, hold_ref, sem = refs[n + 2 :]
    place(hold_ref, me_ref[0], n, part, own_ref, others)
    copy = pltpu.make_async_copy(hold_ref, weight_ref.at[0, 0], sem)
    copy.start()
    copy.wait()


def shards(grad_in, grad_last, support, preact, weights, tile_vals, tile_row, tile_col, tile_count):
    section = lax.axis_index("section")
    me = lax.axis_index("rows")
    n = lax.axis_size("rows")
    sections = lax.axis_size("section")
    ticks = support.shape[1]
    layers = support.shape[2]
    rows_dev, width = grad_last.shape
    tile = tile_vals.shape[-1]
    row_tiles = rows_dev // tile
    part = width // n
    room = max(part, 16)
    me_arr = me.astype(jnp.int32).reshape(1)
    section_arr = section.astype(jnp.int32).reshape(1)

    owner = tile_col[0] // row_tiles
    named = jnp.where(
        owner[:, :, None] == jnp.arange(n)[None, None, :], (tile_col[0] % row_tiles)[:, :, None], 0
    )
    pick = jnp.max(named, axis=1).reshape(1, ticks * n).astype(jnp.int32)
    picks = jnp.where(jnp.arange(n)[:, None] == me, pick, 0)
    if power_of_two(n):
        k = 1
        while k < n:
            picks = picks + lax.ppermute(picks, "rows", [(i, i ^ k) for i in range(n)])
            k *= 2
    else:
        picks = lax.psum(picks, "rows")

    def shape(rows, dtype):
        return jax.ShapeDtypeStruct((rows, width), dtype)

    handoff = initial = passed = None
    above_sum = None
    weight_acc = [None] * layers
    for tick in range(ticks):
        final = tick == ticks - 1
        if tick > 0:
            passed = passed_along(passed, "section", -1)
        adj = densify(
            tick, me_arr, tile_row, tile_col, tile_count, tile_vals, row_tiles, n
        )
        image = got = toward = None
        for layer in reversed(range(layers)):
            entry = layer == layers - 1
            c = dict(
                n=n, tile=tile, width=width, layers=layers, layer=layer, tick=tick, sections=sections,
                entry=entry, final=final, part=part, room=room,
                before=not entry and layer < layers - 2,
                toward=layer == 0 and not entry,
                sum_above=final and not entry,
                above_at=0 if layer >= layers - 2 else room,
            )
            message = tile + (room * (1 if entry else 2) if final else 0)
            operands = [me_arr, section_arr, picks, preact, weights]
            specs = [SMEM, SMEM, SMEM, ANY, ANY]
            aliases = {}
            if entry:
                if tick == 0:
                    operands.append(grad_in)
                    specs.append(ANY)
                else:
                    operands += [grad_last, passed]
                    specs += [VMEM, VMEM]
            else:
                operands += [adj, image] + got
                specs += [VMEM] * (n + 1)
                if c["before"]:
                    operands.append(toward)
                    specs.append(VMEM)
                if c["toward"] and tick > 0:
                    aliases[len(operands)] = n + 1
                    operands.append(initial)
                    specs.append(ANY)
            if final:
                operands += [support, weight_acc[layer]]
                specs += [ANY, VMEM]
                if c["sum_above"]:
                    operands.append(above_sum)
                    specs.append(VMEM)
            outs = [shape(rows_dev, BF16)] * 2 + [shape(message, BF16)] * (n - 1)
            out_specs = [VMEM] * (n + 1)
            scratch = []
            if not entry:
                if c["toward"]:
                    outs.append(jax.ShapeDtypeStruct((1, ticks, rows_dev, width), F32))
                    out_specs.append(ANY)
                    scratch = [pltpu.VMEM((rows_dev, width), F32), pltpu.SemaphoreType.DMA]
                else:
                    outs.append(shape(rows_dev, F32))
                    out_specs.append(VMEM)
            if c["sum_above"]:
                outs.append(shape(part, BF16))
                out_specs.append(VMEM)
            if final:
                outs.append(shape(width, F32))
                out_specs.append(VMEM)
            scratch += [
                pltpu.VMEM((rows_dev, width), BF16),
                pltpu.VMEM((width, width), BF16),
                pltpu.SemaphoreType.DMA((4,)),
            ]
            if entry and tick == 0:
                scratch.append(pltpu.VMEM((rows_dev, width), BF16))
            if final:
                scratch.append(pltpu.VMEM((rows_dev, width), BF16))
            results = pl.pallas_call(
                functools.partial(layer_kernel, c),
                out_shape=outs,
                in_specs=specs,
                out_specs=out_specs,
                scratch_shapes=scratch,
                input_output_aliases=aliases,
                compiler_params=PARAMS,
                cost_estimate=cost(
                    2 * rows_dev * width * (width + (n + 1) * tile), (6 + 2 * n) * rows_dev * width
                ),
                name="entry" if entry else "middle",
            )(*operands)
            results = list(results)
            image, masked = results[:2]
            sends = results[2 : n + 1]
            rest = results[n + 1 :]
            if not entry:
                toward = rest.pop(0)
                if c["toward"]:
                    initial = toward
            if c["sum_above"]:
                own_sum = rest.pop(0)
            if final:
                above_sum = rest.pop(0)
            else:
                beta = jnp.log(
                    BETA_SCALE / (layers * section + layer + 1).astype(F32) + 1.0
                )
                term = beta * jnp.dot(
                    support[0, tick, layer].T, masked, preferred_element_type=F32
                )
                old = weight_acc[layer]
                weight_acc[layer] = term if old is None else old + term
            got = exchange(sends)
        c = dict(n=n, tile=tile, tick=tick, final=final, part=part, room=room, above=layers > 1)
        operands = [me_arr, adj, image] + got
        specs = [SMEM] + [VMEM] * (n + 1)
        aliases = {}
        if tick > 0:
            aliases[len(operands)] = 0
            operands.append(handoff)
            specs.append(ANY)
        outs = [jax.ShapeDtypeStruct((ticks, 1, rows_dev, width), BF16)]
        out_specs = [ANY]
        scratch = [pltpu.VMEM((rows_dev, width), BF16), pltpu.SemaphoreType.DMA]
        if final:
            operands += [above_sum, own_sum]
            specs += [VMEM, VMEM]
            outs += [shape(part, BF16), jax.ShapeDtypeStruct((1, layers, width, width), F32)]
            out_specs += [VMEM, ANY]
            scratch += [pltpu.VMEM((width, width), F32), pltpu.SemaphoreType.DMA]
        else:
            outs.append(shape(rows_dev, BF16))
            out_specs.append(VMEM)
        results = pl.pallas_call(
            functools.partial(exit_kernel, c),
            out_shape=outs,
            in_specs=specs,
            out_specs=out_specs,
            scratch_shapes=scratch,
            input_output_aliases=aliases,
            compiler_params=PARAMS,
            cost_estimate=cost(
                2 * rows_dev * width * (n + 1) * tile, (6 + 2 * n) * rows_dev * width
            ),
            name="exit",
        )(*operands)
        handoff = results[0]
        if final:
            last_sum, weight_grad = results[1:]
        else:
            passed = results[1]
    others = exchange([last_sum] * (n - 1))
    weight_grad = pl.pallas_call(
        functools.partial(finish_kernel, n, part),
        out_shape=jax.ShapeDtypeStruct((1, layers, width, width), F32),
        in_specs=[SMEM] + [VMEM] * n + [ANY],
        out_specs=ANY,
        scratch_shapes=[pltpu.VMEM((width, width), F32), pltpu.SemaphoreType.DMA],
        input_output_aliases={n + 1: 0},
        compiler_params=PARAMS,
        name="finish",
    )(me_arr, last_sum, *others, weight_grad)
    return handoff, initial, weight_grad


def solution(mesh):
    return jax.shard_map(
        shards,
        mesh=mesh,
        in_specs=(
            P("section", "rows", None),
            P("rows", None),
            P("section", None, None, "rows", None),
            P("section", None, None, "rows", None),
            P("section", None, None, None),
            P("section", None, "rows", None, None),
            P("section", None, "rows"),
            P("section", None, "rows"),
            P("section", None, "rows"),
        ),
        out_specs=(
            P(None, "section", "rows", None),
            P("section", None, "rows", None),
            P("section", None, None, None),
        ),
        check_vma=False,
    )
```

time: 409 us -> 130 us (0.32)
  waiting for transfers between devices: 228 us -> 32 us
  matrix products: 75.5 us -> 0.45 us
  local copies, waits for them, and re-layouts: 82.6 us -> 10.7 us
  starting transfers between devices: 2.16 us -> 68.8 us
  Pallas kernels: 0 us -> 16 us
  between operations: 14.2 us -> 1.09 us
  other arithmetic: 5.81 us -> 1.03 us
    all_gather x4 -> x0, waiting for transfers between devices: 157 us -> none  [shards(): gathered = lax.all_gather(image, 'rows', axis=0, tiled=True)]
    dot_general x16 -> x2, matrix products: 75.5 us -> 0.45 us  [shards(): jnp.dot(support[0, tick, layer].T, masked, preferred_element_type=F32)]
    psum x1 -> x0, waiting for transfers between devices: 68.5 us -> none  [shards(): weight_acc[layer] = weight_acc[layer] + lax.psum(term, 'rows')]
    ppermute x0 -> x38, starting transfers between devices: none -> 67.6 us  [the longest x35 59.5 us: exchange(): got[k - 1] = lax.ppermute(messages[k - 1], 'rows', route)]
    dot_general x4 -> x0, local copies, waits for them, and re-layouts: 51 us -> none  [tile_product(): jnp.einsum('kab,kbf->kaf', values, blocks, preferred_element_type=jnp.flo...]
    ppermute x0 -> x38, waiting for transfers between devices: none -> 30.3 us  [the longest x35 25.5 us: exchange(): got[k - 1] = lax.ppermute(messages[k - 1], 'rows', route)]
    gather x4 -> x0, local copies, waits for them, and re-layouts: 28.4 us -> none  [tile_product(): blocks = gathered.reshape(-1, tile, width)[index]]
    pallas_call x0 -> x9, Pallas kernels: none -> 16 us  [the longest x4 8.89 us: shards(): pl.pallas_call(functools.partial(layer_kernel, c), out_shape=outs, in_spe...]
  transfers between devices with their start and end apart: 6 -> 39, of which waited for: 6 -> 15; matrix products, arithmetic and copies ran while one was open for 3% -> 1% of each run, Pallas kernels for 0% -> 3%
where the time goes in v2:
time: 130 us
  starting transfers between devices  68.8 us (53%)
  waiting for transfers between devices  32 us (25%)
  Pallas kernels  16 us (12%)
  local copies, waits for them, and re-layouts  10.7 us (8%)
    ppermute x35, starting transfers between devices, exchange(): got[k - 1] = lax.ppermute(messages[k - 1], 'rows', route)  59.5 us
    ppermute x35, waiting for transfers between devices, exchange(): got[k - 1] = lax.ppermute(messages[k - 1], 'rows', route)  25.5 us
    unnamed x27, local copies, waits for them, and re-layouts  10.6 us
    pallas_call x4, Pallas kernels, shards(): pl.pallas_call(functools.partial(layer_kernel, c), out_shape=outs, in_spe...  8.89 us
    ppermute x3, starting transfers between devices, shards(): picks = picks + lax.ppermute(picks, 'rows', [(i, i ^ k) for i in range(n)])  8.09 us
    ppermute x3, waiting for transfers between devices, shards(): picks = picks + lax.ppermute(picks, 'rows', [(i, i ^ k) for i in range(n)])  4.75 us
    pallas_call x2, Pallas kernels, densify(): pl.pallas_call(functools.partial(densify_kernel, tick, row_tiles, n), gri...  4.37 us
  transfers between devices with their start and end apart: 39, of which 15 were waited for; matrix products, arithmetic and copies ran while one was open for 1% of the time, Pallas kernels for 3%

profile of v2, /device:TPU:0, one launch (start us, length us, event | category | flops | bytes accessed | tf_op | source)
XLA Modules:
  0.0 130.1 jit_solution(17086285647723589753)
XLA Ops:
  1.6 2.9 %collective-permute-start = (s32[8,16]{1,0:T(8,128)S(1)}, s32[8,16]{1,0:T(8,128)S(1)}, u32[]{:S(2)}, u32[]{:S(2)}) collective-permute-start(s32[8,16]{1,0:T(8,128)S(1)} %broadcast_select_fusion), channel_id=1, source_target_pairs={{0,1},{1,0},{2,3},{3,2},{4,5},{5,4},{6,7},{7,6},{8,9},{9,8},{10,11... | collective-permute-start | bytes 1544 | tf_op jit(solution)/shard_map/ppermute | solution.py:306
  10.0 3.0 %collective-permute-start.2 = (s32[8,16]{1,0:T(8,128)S(1)}, s32[8,16]{1,0:T(8,128)S(1)}, u32[]{:S(2)}, u32[]{:S(2)}) collective-permute-start(s32[8,16]{1,0:T(8,128)S(1)} %fusion.9), channel_id=1, source_target_pairs={{0,4},{1,5},{2,6},{3,7},{4,0},{5,1},{6,2},{7,3},{8,12},{9,13},{10,... | collective-permute-start | bytes 1544 | tf_op jit(solution)/shard_map/ppermute | solution.py:306
  22.5 2.9 %collective-permute-start.6 = (bf16[128,256]{1,0:T(8,128)(2,1)S(1)}, bf16[128,256]{1,0:T(8,128)(2,1)S(1)}, u32[]{:S(2)}, u32[]{:S(2)}) collective-permute-start(bf16[128,256]{1,0:T(8,128)(2,1)S(1)} %get-tuple-element.51), channel_id=1, source_target_pairs={{0,4},{1,5},{2,6},{3,7},{4,0},{5,1},{6,2},{7,3},{8,12},{9,13},{10,... | collective-permute-start | bytes 196616 | tf_op jit(solution)/shard_map/ppermute | solution.py:55
  26.7 3.6 %collective-permute-start.8 = (bf16[128,256]{1,0:T(8,128)(2,1)S(1)}, bf16[128,256]{1,0:T(8,128)(2,1)S(1)}, u32[]{:S(2)}, u32[]{:S(2)}) collective-permute-start(bf16[128,256]{1,0:T(8,128)(2,1)S(1)} %get-tuple-element.53), channel_id=1, source_target_pairs={{0,6},{1,7},{2,4},{3,5},{4,2},{5,3},{6,0},{7,1},{8,14},{9,15},{10,... | collective-permute-start | bytes 196616 | tf_op jit(solution)/shard_map/ppermute | solution.py:55
  31.1 2.8 %copy-done = bf16[1,2,96,128,128]{4,3,2,1,0:T(8,128)(2,1)S(1)} copy-done((bf16[1,2,96,128,128]{4,3,2,1,0:T(8,128)(2,1)S(1)}, bf16[1,2,96,128,128]{4,3,2,1,0:T(8,128)(2,1)}, u32[]{:S(2)}) %copy-start) | copy-done | bytes 6291480
  35.2 2.2 %densify.3.refs_5_.refs_1_ = bf16[256,1152]{1,0:T(8,128)(2,1)S(1)} custom-call(s32[1]{0:T(128)} %bitcast.me_ref.refs_0_, s32[1,2,96]{2,1,0:T(2,128)S(1)} %copy-done.11, s32[1,2,96]{2,1,0:T(2,128)S(1)} %copy-done.9, s32[1,2,1]{2,1,0:T(2,128)S(1)} %copy.19.count_ref, bf16[1,2,96,128,128]{4,3,2,1,0:T(8,128)(2,1)S(1)} %copy-done), custom_call_target="tpu_custom_call" | custom-call | flops 31457280 | bytes 3145728 | tf_op jit(solution)/shard_map/densify/pallas_call | solution.py:97
  37.5 2.4 %middle.2 = (bf16[256,256]{1,0:T(8,128)(2,1)S(1)}, bf16[256,256]{1,0:T(8,128)(2,1)S(1)}, bf16[128,256]{1,0:T(8,128)(2,1)S(1)}, bf16[128,256]{1,0:T(8,128)(2,1)S(...) custom-call(s32[1]{0:T(128)} %bitcast.me_ref.refs_0_, ...), custom_call_target="tpu_custom_call" | custom-call | flops 184549376 | bytes 1441792 | tf_op jit(solution)/shard_map/middle/pallas_call | solution.py:388
  43.4 2.7 %collective-permute-start.13 = (bf16[128,256]{1,0:T(8,128)(2,1)S(1)}, bf16[128,256]{1,0:T(8,128)(2,1)S(1)}, u32[]{:S(2)}, u32[]{:S(2)}) collective-permute-start(bf16[128,256]{1,0:T(8,128)(2,1)S(1)} %get-tuple-element.59), channel_id=1, source_target_pairs={{0,4},{1,5},{2,6},{3,7},{4,0},{5,1},{6,2},{7,3},{8,12},{9,13},{10,... | collective-permute-start | bytes 196616 | tf_op jit(solution)/shard_map/ppermute | solution.py:55
  47.7 3.7 %collective-permute-start.15 = (bf16[128,256]{1,0:T(8,128)(2,1)S(1)}, bf16[128,256]{1,0:T(8,128)(2,1)S(1)}, u32[]{:S(2)}, u32[]{:S(2)}) collective-permute-start(bf16[128,256]{1,0:T(8,128)(2,1)S(1)} %get-tuple-element.61), channel_id=1, source_target_pairs={{0,6},{1,7},{2,4},{3,5},{4,2},{5,3},{6,0},{7,1},{8,14},{9,15},{10,... | collective-permute-start | bytes 196616 | tf_op jit(solution)/shard_map/ppermute | solution.py:55
  52.1 2.2 %collective-permute-done.15.refs_8_ = bf16[128,256]{1,0:T(8,128)(2,1)S(1)} collective-permute-done((bf16[128,256]{1,0:T(8,128)(2,1)S(1)}, bf16[128,256]{1,0:T(8,128)(2,1)S(1)}, u32[]{:S(2)}, u32[]{:S(2)}) %collective-permute-start.15) | collective-permute-done | bytes 65568 | tf_op jit(solution)/shard_map/ppermute | solution.py:55
  54.4 3.9 %collective-permute-done.16.refs_9_ = bf16[128,256]{1,0:T(8,128)(2,1)S(1)} collective-permute-done((bf16[128,256]{1,0:T(8,128)(2,1)S(1)}, bf16[128,256]{1,0:T(8,128)(2,1)S(1)}, u32[]{:S(2)}, u32[]{:S(2)}) %collective-permute-start.16) | collective-permute-done | bytes 65568 | tf_op jit(solution)/shard_map/ppermute | solution.py:55
  65.1 2.8 %copy-done.1 = bf16[1,2,96,128,128]{4,3,2,1,0:T(8,128)(2,1)S(1)} copy-done((bf16[1,2,96,128,128]{4,3,2,1,0:T(8,128)(2,1)S(1)}, bf16[1,2,96,128,128]{4,3,2,1,0:T(8,128)(2,1)}, u32[]{:S(2)}) %copy-start.1) | copy-done | bytes 6291480
  67.8 2.2 %densify.2.refs_5_.refs_1_ = bf16[256,1152]{1,0:T(8,128)(2,1)S(1)} custom-call(s32[1]{0:T(128)} %bitcast.me_ref.refs_0_, s32[1,2,96]{2,1,0:T(2,128)S(1)} %copy-done.12, s32[1,2,96]{2,1,0:T(2,128)S(1)} %copy-done.10, s32[1,2,1]{2,1,0:T(2,128)S(1)} %copy.19.count_ref, bf16[1,2,96,128,128]{4,3,2,1,0:T(8,128)(2,1)S(1)} %copy-done.1), custom_call_target="tpu_custom_call" | custom-call | flops 31457280 | bytes 3145728 | tf_op jit(solution)/shard_map/densify/pallas_call | solution.py:97
  70.1 3.4 %collective-permute-start.20 = (bf16[160,256]{1,0:T(8,128)(2,1)S(1)}, bf16[160,256]{1,0:T(8,128)(2,1)S(1)}, u32[]{:S(2)}, u32[]{:S(2)}) collective-permute-start(bf16[160,256]{1,0:T(8,128)(2,1)S(1)} %get-tuple-element.68), channel_id=1, source_target_pairs={{0,3},{1,2},{2,1},{3,0},{4,7},{5,6},{6,5},{7,4},{8,11},{9,10},{10,... | collective-permute-start | bytes 245768 | tf_op jit(solution)/shard_map/ppermute | solution.py:55
  73.5 2.7 %collective-permute-start.22 = (bf16[160,256]{1,0:T(8,128)(2,1)S(1)}, bf16[160,256]{1,0:T(8,128)(2,1)S(1)}, u32[]{:S(2)}, u32[]{:S(2)}) collective-permute-start(bf16[160,256]{1,0:T(8,128)(2,1)S(1)} %get-tuple-element.70), channel_id=1, source_target_pairs={{0,5},{1,4},{2,7},{3,6},{4,1},{5,0},{6,3},{7,2},{8,13},{9,12},{10,... | collective-permute-start | bytes 245768 | tf_op jit(solution)/shard_map/ppermute | solution.py:55
  77.1 4.1 %collective-permute-start.24 = (bf16[160,256]{1,0:T(8,128)(2,1)S(1)}, bf16[160,256]{1,0:T(8,128)(2,1)S(1)}, u32[]{:S(2)}, u32[]{:S(2)}) collective-permute-start(bf16[160,256]{1,0:T(8,128)(2,1)S(1)} %get-tuple-element.72), channel_id=1, source_target_pairs={{0,7},{1,6},{2,5},{3,4},{4,3},{5,2},{6,1},{7,0},{8,15},{9,14},{10,... | collective-permute-start | bytes 245768 | tf_op jit(solution)/shard_map/ppermute | solution.py:55
  81.4 5.0 %collective-permute-done.21.refs_10_ = bf16[160,256]{1,0:T(8,128)(2,1)S(1)} collective-permute-done((bf16[160,256]{1,0:T(8,128)(2,1)S(1)}, bf16[160,256]{1,0:T(8,128)(2,1)S(1)}, u32[]{:S(2)}, u32[]{:S(2)}) %collective-permute-start.21) | collective-permute-done | bytes 81952 | tf_op jit(solution)/shard_map/ppermute | solution.py:55
  87.5 3.2 %middle.3 = (bf16[256,256]{1,0:T(8,128)(2,1)S(1)}, bf16[256,256]{1,0:T(8,128)(2,1)}, bf16[192,256]{1,0:T(8,128)(2,1)S(1)}, bf16[192,256]{1,0:T(8,128)(2,1)S(1)},...) custom-call(s32[1]{0:T(128)} %bitcast.me_ref.refs_0_, ...), custom_call_target="tpu_custom_call", output_to_operand_aliasing={{9}: (14, {})} | custom-call | flops 184549376 | bytes 1441792 | tf_op jit(solution)/shard_map/middle/pallas_call | solution.py:388
  92.9 4.1 %collective-permute-start.26 = (bf16[192,256]{1,0:T(8,128)(2,1)S(1)}, bf16[192,256]{1,0:T(8,128)(2,1)S(1)}, u32[]{:S(2)}, u32[]{:S(2)}) collective-permute-start(bf16[192,256]{1,0:T(8,128)(2,1)S(1)} %get-tuple-element.78), channel_id=1, source_target_pairs={{0,2},{1,3},{2,0},{3,1},{4,6},{5,7},{6,4},{7,5},{8,10},{9,11},{10,... | collective-permute-start | bytes 294920 | tf_op jit(solution)/shard_map/ppermute | solution.py:55
  98.5 2.3 %collective-permute-start.29 = (bf16[192,256]{1,0:T(8,128)(2,1)S(1)}, bf16[192,256]{1,0:T(8,128)(2,1)S(1)}, u32[]{:S(2)}, u32[]{:S(2)}) collective-permute-start(bf16[192,256]{1,0:T(8,128)(2,1)S(1)} %get-tuple-element.81), channel_id=1, source_target_pairs={{0,5},{1,4},{2,7},{3,6},{4,1},{5,0},{6,3},{7,2},{8,13},{9,12},{10,... | collective-permute-start | bytes 294920 | tf_op jit(solution)/shard_map/ppermute | solution.py:55
  102.3 2.4 %collective-permute-start.31 = (bf16[192,256]{1,0:T(8,128)(2,1)S(1)}, bf16[192,256]{1,0:T(8,128)(2,1)S(1)}, u32[]{:S(2)}, u32[]{:S(2)}) collective-permute-start(bf16[192,256]{1,0:T(8,128)(2,1)S(1)} %get-tuple-element.83), channel_id=1, source_target_pairs={{0,7},{1,6},{2,5},{3,4},{4,3},{5,2},{6,1},{7,0},{8,15},{9,14},{10,... | collective-permute-start | bytes 294920 | tf_op jit(solution)/shard_map/ppermute | solution.py:55
  104.6 7.1 %collective-permute-done.28.refs_6_ = bf16[192,256]{1,0:T(8,128)(2,1)S(1)} collective-permute-done((bf16[192,256]{1,0:T(8,128)(2,1)S(1)}, bf16[192,256]{1,0:T(8,128)(2,1)S(1)}, u32[]{:S(2)}, u32[]{:S(2)}) %collective-permute-start.28) | collective-permute-done | bytes 98336 | tf_op jit(solution)/shard_map/ppermute | solution.py:55
  111.7 3.2 %collective-permute-done.29.refs_7_ = bf16[192,256]{1,0:T(8,128)(2,1)S(1)} collective-permute-done((bf16[192,256]{1,0:T(8,128)(2,1)S(1)}, bf16[192,256]{1,0:T(8,128)(2,1)S(1)}, u32[]{:S(2)}, u32[]{:S(2)}) %collective-permute-start.29) | collective-permute-done | bytes 98336 | tf_op jit(solution)/shard_map/ppermute | solution.py:55
  119.7 3.0 %collective-permute-start.36 = (bf16[32,256]{1,0:T(8,128)(2,1)S(1)}, bf16[32,256]{1,0:T(8,128)(2,1)S(1)}, u32[]{:S(2)}, u32[]{:S(2)}) collective-permute-start(bf16[32,256]{1,0:T(8,128)(2,1)S(1)} %get-tuple-element.89.refs_1_), channel_id=1, source_target_pairs={{0,5},{1,4},{2,7},{3,6},{4,1},{5,0},{6,3},{7,2},{8,13},{9,12},{10,... | collective-permute-start | bytes 49160 | tf_op jit(solution)/shard_map/ppermute | solution.py:55
  (100 shorter events, 51.2 us)
Async XLA Ops:
  19.0 7.7 %collective-permute-start.3 = (bf16[128,256]{1,0:T(8,128)(2,1)S(1)}, bf16[128,256]{1,0:T(8,128)(2,1)S(1)}, u32[]{:S(2)}, u32[]{:S(2)}) collective-permute-start(bf16[128,256]{1,0:T(8,128)(2,1)S(1)} %get-tuple-element.48), channel_id=1, source_target_pairs={{0,1},{1,0},{2,3},{3,2},{4,5},{5,4},{6,7},{7,6},{8,9},{9,8},{10,11... | collective-permute-start | bytes 196616 | tf_op jit(solution)/shard_map/ppermute | solution.py:55
  20.8 9.5 %collective-permute-start.4 = (bf16[128,256]{1,0:T(8,128)(2,1)S(1)}, bf16[128,256]{1,0:T(8,128)(2,1)S(1)}, u32[]{:S(2)}, u32[]{:S(2)}) collective-permute-start(bf16[128,256]{1,0:T(8,128)(2,1)S(1)} %get-tuple-element.49), channel_id=1, source_target_pairs={{0,2},{1,3},{2,0},{3,1},{4,6},{5,7},{6,4},{7,5},{8,10},{9,11},{10,... | collective-permute-start | bytes 196616 | tf_op jit(solution)/shard_map/ppermute | solution.py:55
  22.4 15.0 %collective-permute-start.5 = (bf16[128,256]{1,0:T(8,128)(2,1)S(1)}, bf16[128,256]{1,0:T(8,128)(2,1)S(1)}, u32[]{:S(2)}, u32[]{:S(2)}) collective-permute-start(bf16[128,256]{1,0:T(8,128)(2,1)S(1)} %get-tuple-element.50), channel_id=1, source_target_pairs={{0,3},{1,2},{2,1},{3,0},{4,7},{5,6},{6,5},{7,4},{8,11},{9,10},{10,... | collective-permute-start | bytes 196616 | tf_op jit(solution)/shard_map/ppermute | solution.py:55
  22.5 14.9 %collective-permute-start.6 = (bf16[128,256]{1,0:T(8,128)(2,1)S(1)}, bf16[128,256]{1,0:T(8,128)(2,1)S(1)}, u32[]{:S(2)}, u32[]{:S(2)}) collective-permute-start(bf16[128,256]{1,0:T(8,128)(2,1)S(1)} %get-tuple-element.51), channel_id=1, source_target_pairs={{0,4},{1,5},{2,6},{3,7},{4,0},{5,1},{6,2},{7,3},{8,12},{9,13},{10,... | collective-permute-start | bytes 196616 | tf_op jit(solution)/shard_map/ppermute | solution.py:55
  25.4 12.0 %collective-permute-start.7 = (bf16[128,256]{1,0:T(8,128)(2,1)S(1)}, bf16[128,256]{1,0:T(8,128)(2,1)S(1)}, u32[]{:S(2)}, u32[]{:S(2)}) collective-permute-start(bf16[128,256]{1,0:T(8,128)(2,1)S(1)} %get-tuple-element.52), channel_id=1, source_target_pairs={{0,5},{1,4},{2,7},{3,6},{4,1},{5,0},{6,3},{7,2},{8,13},{9,12},{10,... | collective-permute-start | bytes 196616 | tf_op jit(solution)/shard_map/ppermute | solution.py:55
  26.7 10.7 %collective-permute-start.8 = (bf16[128,256]{1,0:T(8,128)(2,1)S(1)}, bf16[128,256]{1,0:T(8,128)(2,1)S(1)}, u32[]{:S(2)}, u32[]{:S(2)}) collective-permute-start(bf16[128,256]{1,0:T(8,128)(2,1)S(1)} %get-tuple-element.53), channel_id=1, source_target_pairs={{0,6},{1,7},{2,4},{3,5},{4,2},{5,3},{6,0},{7,1},{8,14},{9,15},{10,... | collective-permute-start | bytes 196616 | tf_op jit(solution)/shard_map/ppermute | solution.py:55
  39.9 7.8 %collective-permute-start.10 = (bf16[128,256]{1,0:T(8,128)(2,1)S(1)}, bf16[128,256]{1,0:T(8,128)(2,1)S(1)}, u32[]{:S(2)}, u32[]{:S(2)}) collective-permute-start(bf16[128,256]{1,0:T(8,128)(2,1)S(1)} %get-tuple-element.56), channel_id=1, source_target_pairs={{0,1},{1,0},{2,3},{3,2},{4,5},{5,4},{6,7},{7,6},{8,9},{9,8},{10,11... | collective-permute-start | bytes 196616 | tf_op jit(solution)/shard_map/ppermute | solution.py:55
  41.8 9.5 %collective-permute-start.11 = (bf16[128,256]{1,0:T(8,128)(2,1)S(1)}, bf16[128,256]{1,0:T(8,128)(2,1)S(1)}, u32[]{:S(2)}, u32[]{:S(2)}) collective-permute-start(bf16[128,256]{1,0:T(8,128)(2,1)S(1)} %get-tuple-element.57), channel_id=1, source_target_pairs={{0,2},{1,3},{2,0},{3,1},{4,6},{5,7},{6,4},{7,5},{8,10},{9,11},{10,... | collective-permute-start | bytes 196616 | tf_op jit(solution)/shard_map/ppermute | solution.py:55
  41.8 9.6 %collective-permute-start.12 = (bf16[128,256]{1,0:T(8,128)(2,1)S(1)}, bf16[128,256]{1,0:T(8,128)(2,1)S(1)}, u32[]{:S(2)}, u32[]{:S(2)}) collective-permute-start(bf16[128,256]{1,0:T(8,128)(2,1)S(1)} %get-tuple-element.58), channel_id=1, source_target_pairs={{0,3},{1,2},{2,1},{3,0},{4,7},{5,6},{6,5},{7,4},{8,11},{9,10},{10,... | collective-permute-start | bytes 196616 | tf_op jit(solution)/shard_map/ppermute | solution.py:55
  43.4 8.0 %collective-permute-start.13 = (bf16[128,256]{1,0:T(8,128)(2,1)S(1)}, bf16[128,256]{1,0:T(8,128)(2,1)S(1)}, u32[]{:S(2)}, u32[]{:S(2)}) collective-permute-start(bf16[128,256]{1,0:T(8,128)(2,1)S(1)} %get-tuple-element.59), channel_id=1, source_target_pairs={{0,4},{1,5},{2,6},{3,7},{4,0},{5,1},{6,2},{7,3},{8,12},{9,13},{10,... | collective-permute-start | bytes 196616 | tf_op jit(solution)/shard_map/ppermute | solution.py:55
  64.5 11.7 %collective-permute-start.18 = (bf16[160,256]{1,0:T(8,128)(2,1)S(1)}, bf16[160,256]{1,0:T(8,128)(2,1)S(1)}, u32[]{:S(2)}, u32[]{:S(2)}) collective-permute-start(bf16[160,256]{1,0:T(8,128)(2,1)S(1)} %get-tuple-element.66), channel_id=1, source_target_pairs={{0,1},{1,0},{2,3},{3,2},{4,5},{5,4},{6,7},{7,6},{8,9},{9,8},{10,11... | collective-permute-start | bytes 245768 | tf_op jit(solution)/shard_map/ppermute | solution.py:55
  64.9 12.1 %collective-permute-start.19 = (bf16[160,256]{1,0:T(8,128)(2,1)S(1)}, bf16[160,256]{1,0:T(8,128)(2,1)S(1)}, u32[]{:S(2)}, u32[]{:S(2)}) collective-permute-start(bf16[160,256]{1,0:T(8,128)(2,1)S(1)} %get-tuple-element.67), channel_id=1, source_target_pairs={{0,2},{1,3},{2,0},{3,1},{4,6},{5,7},{6,4},{7,5},{8,10},{9,11},{10,... | collective-permute-start | bytes 245768 | tf_op jit(solution)/shard_map/ppermute | solution.py:55
  70.1 11.3 %collective-permute-start.20 = (bf16[160,256]{1,0:T(8,128)(2,1)S(1)}, bf16[160,256]{1,0:T(8,128)(2,1)S(1)}, u32[]{:S(2)}, u32[]{:S(2)}) collective-permute-start(bf16[160,256]{1,0:T(8,128)(2,1)S(1)} %get-tuple-element.68), channel_id=1, source_target_pairs={{0,3},{1,2},{2,1},{3,0},{4,7},{5,6},{6,5},{7,4},{8,11},{9,10},{10,... | collective-permute-start | bytes 245768 | tf_op jit(solution)/shard_map/ppermute | solution.py:55
  73.5 12.9 %collective-permute-start.21 = (bf16[160,256]{1,0:T(8,128)(2,1)S(1)}, bf16[160,256]{1,0:T(8,128)(2,1)S(1)}, u32[]{:S(2)}, u32[]{:S(2)}) collective-permute-start(bf16[160,256]{1,0:T(8,128)(2,1)S(1)} %get-tuple-element.69), channel_id=1, source_target_pairs={{0,4},{1,5},{2,6},{3,7},{4,0},{5,1},{6,2},{7,3},{8,12},{9,13},{10,... | collective-permute-start | bytes 245768 | tf_op jit(solution)/shard_map/ppermute | solution.py:55
  73.5 14.0 %collective-permute-start.22 = (bf16[160,256]{1,0:T(8,128)(2,1)S(1)}, bf16[160,256]{1,0:T(8,128)(2,1)S(1)}, u32[]{:S(2)}, u32[]{:S(2)}) collective-permute-start(bf16[160,256]{1,0:T(8,128)(2,1)S(1)} %get-tuple-element.70), channel_id=1, source_target_pairs={{0,5},{1,4},{2,7},{3,6},{4,1},{5,0},{6,3},{7,2},{8,13},{9,12},{10,... | collective-permute-start | bytes 245768 | tf_op jit(solution)/shard_map/ppermute | solution.py:55
  76.2 11.4 %collective-permute-start.23 = (bf16[160,256]{1,0:T(8,128)(2,1)S(1)}, bf16[160,256]{1,0:T(8,128)(2,1)S(1)}, u32[]{:S(2)}, u32[]{:S(2)}) collective-permute-start(bf16[160,256]{1,0:T(8,128)(2,1)S(1)} %get-tuple-element.71), channel_id=1, source_target_pairs={{0,6},{1,7},{2,4},{3,5},{4,2},{5,3},{6,0},{7,1},{8,14},{9,15},{10,... | collective-permute-start | bytes 245768 | tf_op jit(solution)/shard_map/ppermute | solution.py:55
  77.1 10.5 %collective-permute-start.24 = (bf16[160,256]{1,0:T(8,128)(2,1)S(1)}, bf16[160,256]{1,0:T(8,128)(2,1)S(1)}, u32[]{:S(2)}, u32[]{:S(2)}) collective-permute-start(bf16[160,256]{1,0:T(8,128)(2,1)S(1)} %get-tuple-element.72), channel_id=1, source_target_pairs={{0,7},{1,6},{2,5},{3,4},{4,3},{5,2},{6,1},{7,0},{8,15},{9,14},{10,... | collective-permute-start | bytes 245768 | tf_op jit(solution)/shard_map/ppermute | solution.py:55
  90.8 10.0 %collective-permute-start.25 = (bf16[192,256]{1,0:T(8,128)(2,1)S(1)}, bf16[192,256]{1,0:T(8,128)(2,1)S(1)}, u32[]{:S(2)}, u32[]{:S(2)}) collective-permute-start(bf16[192,256]{1,0:T(8,128)(2,1)S(1)} %get-tuple-element.77), channel_id=1, source_target_pairs={{0,1},{1,0},{2,3},{3,2},{4,5},{5,4},{6,7},{7,6},{8,9},{9,8},{10,11... | collective-permute-start | bytes 294920 | tf_op jit(solution)/shard_map/ppermute | solution.py:55
  92.9 9.4 %collective-permute-start.26 = (bf16[192,256]{1,0:T(8,128)(2,1)S(1)}, bf16[192,256]{1,0:T(8,128)(2,1)S(1)}, u32[]{:S(2)}, u32[]{:S(2)}) collective-permute-start(bf16[192,256]{1,0:T(8,128)(2,1)S(1)} %get-tuple-element.78), channel_id=1, source_target_pairs={{0,2},{1,3},{2,0},{3,1},{4,6},{5,7},{6,4},{7,5},{8,10},{9,11},{10,... | collective-permute-start | bytes 294920 | tf_op jit(solution)/shard_map/ppermute | solution.py:55
  97.0 14.8 %collective-permute-start.28 = (bf16[192,256]{1,0:T(8,128)(2,1)S(1)}, bf16[192,256]{1,0:T(8,128)(2,1)S(1)}, u32[]{:S(2)}, u32[]{:S(2)}) collective-permute-start(bf16[192,256]{1,0:T(8,128)(2,1)S(1)} %get-tuple-element.80), channel_id=1, source_target_pairs={{0,4},{1,5},{2,6},{3,7},{4,0},{5,1},{6,2},{7,3},{8,12},{9,13},{10,... | collective-permute-start | bytes 294920 | tf_op jit(solution)/shard_map/ppermute | solution.py:55
  98.5 16.4 %collective-permute-start.29 = (bf16[192,256]{1,0:T(8,128)(2,1)S(1)}, bf16[192,256]{1,0:T(8,128)(2,1)S(1)}, u32[]{:S(2)}, u32[]{:S(2)}) collective-permute-start(bf16[192,256]{1,0:T(8,128)(2,1)S(1)} %get-tuple-element.81), channel_id=1, source_target_pairs={{0,5},{1,4},{2,7},{3,6},{4,1},{5,0},{6,3},{7,2},{8,13},{9,12},{10,... | collective-permute-start | bytes 294920 | tf_op jit(solution)/shard_map/ppermute | solution.py:55
  100.8 14.1 %collective-permute-start.30 = (bf16[192,256]{1,0:T(8,128)(2,1)S(1)}, bf16[192,256]{1,0:T(8,128)(2,1)S(1)}, u32[]{:S(2)}, u32[]{:S(2)}) collective-permute-start(bf16[192,256]{1,0:T(8,128)(2,1)S(1)} %get-tuple-element.82), channel_id=1, source_target_pairs={{0,6},{1,7},{2,4},{3,5},{4,2},{5,3},{6,0},{7,1},{8,14},{9,15},{10,... | collective-permute-start | bytes 294920 | tf_op jit(solution)/shard_map/ppermute | solution.py:55
  102.3 12.7 %collective-permute-start.31 = (bf16[192,256]{1,0:T(8,128)(2,1)S(1)}, bf16[192,256]{1,0:T(8,128)(2,1)S(1)}, u32[]{:S(2)}, u32[]{:S(2)}) collective-permute-start(bf16[192,256]{1,0:T(8,128)(2,1)S(1)} %get-tuple-element.83), channel_id=1, source_target_pairs={{0,7},{1,6},{2,5},{3,4},{4,3},{5,2},{6,1},{7,0},{8,15},{9,14},{10,... | collective-permute-start | bytes 294920 | tf_op jit(solution)/shard_map/ppermute | solution.py:55
  116.0 9.6 %collective-permute-start.38 = (bf16[32,256]{1,0:T(8,128)(2,1)S(1)}, bf16[32,256]{1,0:T(8,128)(2,1)S(1)}, u32[]{:S(2)}, u32[]{:S(2)}) collective-permute-start(bf16[32,256]{1,0:T(8,128)(2,1)S(1)} %get-tuple-element.89.refs_1_), channel_id=1, source_target_pairs={{0,7},{1,6},{2,5},{3,4},{4,3},{5,2},{6,1},{7,0},{8,15},{9,14},{10,... | collective-permute-start | bytes 49160 | tf_op jit(solution)/shard_map/ppermute | solution.py:55
  (28 other events, 294.9 us)

commit v3 on v2

--- a/solution.py
+++ b/solution.py
@@ -143,12 +143,9 @@
             take(1)
     if c["final"]:
         support_all, acc_ref = take(2)
-        if c["sum_above"]:
-            (above_ref,) = take(1)
     image_ref, masked_ref = take(2)
     sends = take(n - 1)
     toward_ref = take(1)[0] if not c["entry"] else None
-    own_sum_ref = take(1)[0] if c["sum_above"] else None
     term_ref = take(1)[0] if c["final"] else None
     if c["toward"]:
         hold_ref, sem = take(2)
@@ -198,23 +195,10 @@
         else:
             toward_ref[...] = total
     if c["final"]:
-        part, room = c["part"], c["room"]
         term = lax.dot_general(
             support_ref[...], masked, (((0,), (0,)), ((), ())), preferred_element_type=F32
         )
-        term_ref[...] = acc_ref[...] + beta * term
-        at = tile
-        if c["sum_above"]:
-            total = above_ref[pl.ds(pl.multiple_of(me * part, 8), part), :]
-            for ref in got:
-                total = total + ref[tile + c["above_at"] : tile + c["above_at"] + part, :].astype(F32)
-            own_sum_ref[...] = total.astype(BF16)
-            for send in sends:
-                send[at : at + part, :] = own_sum_ref[...]
-            at += room
-        for k in range(1, n):
-            start = pl.multiple_of(dynamic_target(me, k, n) * part, 8)
-            sends[k - 1][at : at + part, :] = term_ref[pl.ds(start, part), :].astype(BF16)
+        term_ref[...] = (acc_ref[...] + beta * term).astype(BF16)
     if copy is not None:
         copy.wait()
 
@@ -226,56 +210,19 @@
         taken, refs[:count] = refs[:count], []
         return taken
 
-    n, tile, part, room = c["n"], c["tile"], c["part"], c["room"]
-    me_ref, adj_ref, own_ref = take(3)
-    me = me_ref[0]
-    got = take(n - 1)
+    adj_ref, own_ref = take(2)
+    got = take(c["n"] - 1)
     if c["tick"] > 0:
         take(1)
-    if c["final"]:
-        (acc_ref,) = take(1)
-        own_sum_ref = take(1)[0] if c["above"] else None
     (out_ref,) = take(1)
     grad_ref = None if c["final"] else take(1)[0]
-    if c["final"]:
-        last_sum_ref, weight_ref = take(2)
     hold_ref, sem = take(2)
-    if c["final"] and c["above"]:
-        hold_weight_ref, weight_sem = take(2)
-    grad = spread_of(adj_ref, got, own_ref, tile)
+    grad = spread_of(adj_ref, got, own_ref, c["tile"])
     hold_ref[...] = grad
     copy = pltpu.make_async_copy(hold_ref, out_ref.at[c["tick"], 0], sem)
     copy.start()
-    if c["final"]:
-        at = tile + (room if c["above"] else 0)
-        total = acc_ref[pl.ds(pl.multiple_of(me * part, 8), part), :]
-        for ref in got:
-            total = total + ref[at : at + part, :].astype(F32)
-        last_sum_ref[...] = total.astype(BF16)
-        if c["above"]:
-            place(hold_weight_ref, me, n, part, own_sum_ref, [ref.at[tile : tile + part, :] for ref in got])
-            weight_copy = pltpu.make_async_copy(hold_weight_ref, weight_ref.at[0, 1], weight_sem)
-            weight_copy.start()
-            weight_copy.wait()
-    else:
+    if grad_ref is not None:
         grad_ref[...] = grad
-    copy.wait()
-
-
-def place(whole_ref, me, n, part, own_ref, others):
-    whole_ref[pl.ds(pl.multiple_of(me * part, 8), part), :] = own_ref[...].astype(F32)
-    for k in range(1, n):
-        start = pl.multiple_of(dynamic_source(me, k, n) * part, 8)
-        whole_ref[pl.ds(start, part), :] = others[k - 1][...].astype(F32)
-
-
-def finish_kernel(n, part, *refs):
-    me_ref, own_ref = refs[:2]
-    others = refs[2 : n + 1]
-    weight_ref, hold_ref, sem = refs[n + 2 :]
-    place(hold_ref, me_ref[0], n, part, own_ref, others)
-    copy = pltpu.make_async_copy(hold_ref, weight_ref.at[0, 0], sem)
-    copy.start()
     copy.wait()
 
 
@@ -289,8 +236,6 @@
     rows_dev, width = grad_last.shape
     tile = tile_vals.shape[-1]
     row_tiles = rows_dev // tile
-    part = width // n
-    room = max(part, 16)
     me_arr = me.astype(jnp.int32).reshape(1)
     section_arr = section.astype(jnp.int32).reshape(1)
 
@@ -312,7 +257,7 @@
         return jax.ShapeDtypeStruct((rows, width), dtype)
 
     handoff = initial = passed = None
-    above_sum = None
+    weight_sums = [None] * layers
     weight_acc = [None] * layers
     for tick in range(ticks):
         final = tick == ticks - 1
@@ -326,13 +271,10 @@
             entry = layer == layers - 1
             c = dict(
                 n=n, tile=tile, width=width, layers=layers, layer=layer, tick=tick, sections=sections,
-                entry=entry, final=final, part=part, room=room,
+                entry=entry, final=final,
                 before=not entry and layer < layers - 2,
                 toward=layer == 0 and not entry,
-                sum_above=final and not entry,
-                above_at=0 if layer >= layers - 2 else room,
             )
-            message = tile + (room * (1 if entry else 2) if final else 0)
             operands = [me_arr, section_arr, picks, preact, weights]
             specs = [SMEM, SMEM, SMEM, ANY, ANY]
             aliases = {}
@@ -356,10 +298,7 @@
             if final:
                 operands += [support, weight_acc[layer]]
                 specs += [ANY, VMEM]
-                if c["sum_above"]:
-                    operands.append(above_sum)
-                    specs.append(VMEM)
-            outs = [shape(rows_dev, BF16)] * 2 + [shape(message, BF16)] * (n - 1)
+            outs = [shape(rows_dev, BF16)] * 2 + [shape(tile, BF16)] * (n - 1)
             out_specs = [VMEM] * (n + 1)
             scratch = []
             if not entry:
@@ -370,11 +309,8 @@
                 else:
                     outs.append(shape(rows_dev, F32))
                     out_specs.append(VMEM)
-            if c["sum_above"]:
-                outs.append(shape(part, BF16))
-                out_specs.append(VMEM)
             if final:
-                outs.append(shape(width, F32))
+                outs.append(shape(width, BF16))
                 out_specs.append(VMEM)
             scratch += [
                 pltpu.VMEM((rows_dev, width), BF16),
@@ -406,10 +342,13 @@
                 toward = rest.pop(0)
                 if c["toward"]:
                     initial = toward
-            if c["sum_above"]:
-                own_sum = rest.pop(0)
             if final:
-                above_sum = rest.pop(0)
+                term = rest.pop(0)
+                if not entry:
+                    term, weight_sums[layer + 1] = lax.optimization_barrier(
+                        (term, weight_sums[layer + 1])
+                    )
+                weight_sums[layer] = lax.psum(term, "rows")
             else:
                 beta = jnp.log(
                     BETA_SCALE / (layers * section + layer + 1).astype(F32) + 1.0
@@ -420,9 +359,9 @@
                 old = weight_acc[layer]
                 weight_acc[layer] = term if old is None else old + term
             got = exchange(sends)
-        c = dict(n=n, tile=tile, tick=tick, final=final, part=part, room=room, above=layers > 1)
-        operands = [me_arr, adj, image] + got
-        specs = [SMEM] + [VMEM] * (n + 1)
+        c = dict(n=n, tile=tile, tick=tick, final=final)
+        operands = [adj, image] + got
+        specs = [VMEM] * (n + 1)
         aliases = {}
         if tick > 0:
             aliases[len(operands)] = 0
@@ -431,13 +370,7 @@
         outs = [jax.ShapeDtypeStruct((ticks, 1, rows_dev, width), BF16)]
         out_specs = [ANY]
         scratch = [pltpu.VMEM((rows_dev, width), BF16), pltpu.SemaphoreType.DMA]
-        if final:
-            operands += [above_sum, own_sum]
-            specs += [VMEM, VMEM]
-            outs += [shape(part, BF16), jax.ShapeDtypeStruct((1, layers, width, width), F32)]
-            out_specs += [VMEM, ANY]
-            scratch += [pltpu.VMEM((width, width), F32), pltpu.SemaphoreType.DMA]
-        else:
+        if not final:
             outs.append(shape(rows_dev, BF16))
             out_specs.append(VMEM)
         results = pl.pallas_call(
@@ -454,22 +387,9 @@
             name="exit",
         )(*operands)
         handoff = results[0]
-        if final:
-            last_sum, weight_grad = results[1:]
-        else:
+        if not final:
             passed = results[1]
-    others = exchange([last_sum] * (n - 1))
-    weight_grad = pl.pallas_call(
-        functools.partial(finish_kernel, n, part),
-        out_shape=jax.ShapeDtypeStruct((1, layers, width, width), F32),
-        in_specs=[SMEM] + [VMEM] * n + [ANY],
-        out_specs=ANY,
-        scratch_shapes=[pltpu.VMEM((width, width), F32), pltpu.SemaphoreType.DMA],
-        input_output_aliases={n + 1: 0},
-        compiler_params=PARAMS,
-        name="finish",
-    )(me_arr, last_sum, *others, weight_grad)
-    return handoff, initial, weight_grad
+    return handoff, initial, jnp.stack(weight_sums).astype(F32)[None]
 
 
 def solution(mesh):

time: 130 us -> 232 us (1.78)
  waiting for transfers between devices: 32 us -> 129 us
  between operations: 1.09 us -> 14.5 us
  starting transfers between devices: 68.8 us -> 59.9 us
    psum x0 -> x2, waiting for transfers between devices: none -> 107 us  [shards(): weight_sums[layer] = lax.psum(term, 'rows')]
    ppermute x35 -> x28, waiting for transfers between devices: 25.5 us -> 15.1 us  [exchange(): got[k - 1] = lax.ppermute(messages[k - 1], 'rows', route)]
    ppermute x35 -> x28, starting transfers between devices: 59.5 us -> 50.4 us  [exchange(): got[k - 1] = lax.ppermute(messages[k - 1], 'rows', route)]
  transfers between devices with their start and end apart: 39 -> 34, of which waited for: 15 -> 16; matrix products, arithmetic and copies ran while one was open for 1% -> 1% of each run, Pallas kernels for 3% -> 4%
where the time goes in v3:
time: 232 us; the launch traced here: 233 us
  waiting for transfers between devices  129 us (56%)
  starting transfers between devices  59.9 us (26%)
  Pallas kernels  15.4 us (7%)
  between operations  14.5 us (6%)
  local copies, waits for them, and re-layouts  10.7 us (5%)
  other arithmetic  2.83 us (1%)
    psum x2, waiting for transfers between devices, shards(): weight_sums[layer] = lax.psum(term, 'rows')  107 us
    ppermute x28, starting transfers between devices, exchange(): got[k - 1] = lax.ppermute(messages[k - 1], 'rows', route)  50.4 us
    ppermute x28, waiting for transfers between devices, exchange(): got[k - 1] = lax.ppermute(messages[k - 1], 'rows', route)  15.1 us
    unnamed x27, local copies, waits for them, and re-layouts  10.6 us
    pallas_call x4, Pallas kernels, shards(): pl.pallas_call(functools.partial(layer_kernel, c), out_shape=outs, in_spe...  9.2 us
    ppermute x3, starting transfers between devices, shards(): picks = picks + lax.ppermute(picks, 'rows', [(i, i ^ k) for i in range(n)])  8.08 us
    ppermute x3, waiting for transfers between devices, shards(): picks = picks + lax.ppermute(picks, 'rows', [(i, i ^ k) for i in range(n)])  4.75 us
  transfers between devices with their start and end apart: 34, of which 16 were waited for; matrix products, arithmetic and copies ran while one was open for 1% of the time, Pallas kernels for 4%

profile of v3, /device:TPU:0, one launch (start us, length us, event | category | flops | bytes accessed | tf_op | source)
XLA Modules:
  0.0 232.5 jit_solution(15250184667003611950)
XLA Ops:
  8.2 2.9 %collective-permute-start = (s32[8,16]{1,0:T(8,128)S(1)}, s32[8,16]{1,0:T(8,128)S(1)}, u32[]{:S(2)}, u32[]{:S(2)}) collective-permute-start(s32[8,16]{1,0:T(8,128)S(1)} %broadcast_select_fusion), channel_id=1, source_target_pairs={{0,1},{1,0},{2,3},{3,2},{4,5},{5,4},{6,7},{7,6},{8,9},{9,8},{10,11... | collective-permute-start | bytes 1544 | tf_op jit(solution)/shard_map/ppermute | solution.py:251
  12.8 2.1 collective-permute-start.1
  16.6 3.0 %collective-permute-start.2 = (s32[8,16]{1,0:T(8,128)S(1)}, s32[8,16]{1,0:T(8,128)S(1)}, u32[]{:S(2)}, u32[]{:S(2)}) collective-permute-start(s32[8,16]{1,0:T(8,128)S(1)} %fusion.9), channel_id=1, source_target_pairs={{0,4},{1,5},{2,6},{3,7},{4,0},{5,1},{6,2},{7,3},{8,12},{9,13},{10,... | collective-permute-start | bytes 1544 | tf_op jit(solution)/shard_map/ppermute | solution.py:251
  29.1 2.9 %collective-permute-start.6 = (bf16[128,256]{1,0:T(8,128)(2,1)S(1)}, bf16[128,256]{1,0:T(8,128)(2,1)S(1)}, u32[]{:S(2)}, u32[]{:S(2)}) collective-permute-start(bf16[128,256]{1,0:T(8,128)(2,1)S(1)} %get-tuple-element.49), channel_id=1, source_target_pairs={{0,4},{1,5},{2,6},{3,7},{4,0},{5,1},{6,2},{7,3},{8,12},{9,13},{10,... | collective-permute-start | bytes 196616 | tf_op jit(solution)/shard_map/ppermute | solution.py:55
  33.3 3.6 %collective-permute-start.8 = (bf16[128,256]{1,0:T(8,128)(2,1)S(1)}, bf16[128,256]{1,0:T(8,128)(2,1)S(1)}, u32[]{:S(2)}, u32[]{:S(2)}) collective-permute-start(bf16[128,256]{1,0:T(8,128)(2,1)S(1)} %get-tuple-element.51), channel_id=1, source_target_pairs={{0,6},{1,7},{2,4},{3,5},{4,2},{5,3},{6,0},{7,1},{8,14},{9,15},{10,... | collective-permute-start | bytes 196616 | tf_op jit(solution)/shard_map/ppermute | solution.py:55
  37.7 2.8 %copy-done = bf16[1,2,96,128,128]{4,3,2,1,0:T(8,128)(2,1)S(1)} copy-done((bf16[1,2,96,128,128]{4,3,2,1,0:T(8,128)(2,1)S(1)}, bf16[1,2,96,128,128]{4,3,2,1,0:T(8,128)(2,1)}, u32[]{:S(2)}) %copy-start) | copy-done | bytes 6291480
  43.8 2.4 %middle.2 = (bf16[256,256]{1,0:T(8,128)(2,1)S(1)}, bf16[256,256]{1,0:T(8,128)(2,1)S(1)}, bf16[128,256]{1,0:T(8,128)(2,1)S(1)}, bf16[128,256]{1,0:T(8,128)(2,1)S(...) custom-call(s32[1]{0:T(128)} %bitcast.me_ref.refs_0_, ...), custom_call_target="tpu_custom_call" | custom-call | flops 184549376 | bytes 1441792 | tf_op jit(solution)/shard_map/middle/pallas_call | solution.py:324
  49.8 2.4 %collective-permute-start.13 = (bf16[128,256]{1,0:T(8,128)(2,1)S(1)}, bf16[128,256]{1,0:T(8,128)(2,1)S(1)}, u32[]{:S(2)}, u32[]{:S(2)}) collective-permute-start(bf16[128,256]{1,0:T(8,128)(2,1)S(1)} %get-tuple-element.57), channel_id=1, source_target_pairs={{0,4},{1,5},{2,6},{3,7},{4,0},{5,1},{6,2},{7,3},{8,12},{9,13},{10,... | collective-permute-start | bytes 196616 | tf_op jit(solution)/shard_map/ppermute | solution.py:55
  53.7 3.6 %collective-permute-start.15 = (bf16[128,256]{1,0:T(8,128)(2,1)S(1)}, bf16[128,256]{1,0:T(8,128)(2,1)S(1)}, u32[]{:S(2)}, u32[]{:S(2)}) collective-permute-start(bf16[128,256]{1,0:T(8,128)(2,1)S(1)} %get-tuple-element.59), channel_id=1, source_target_pairs={{0,6},{1,7},{2,4},{3,5},{4,2},{5,3},{6,0},{7,1},{8,14},{9,15},{10,... | collective-permute-start | bytes 196616 | tf_op jit(solution)/shard_map/ppermute | solution.py:55
  60.3 4.0 %collective-permute-done.16.refs_8_ = bf16[128,256]{1,0:T(8,128)(2,1)S(1)} collective-permute-done((bf16[128,256]{1,0:T(8,128)(2,1)S(1)}, bf16[128,256]{1,0:T(8,128)(2,1)S(1)}, u32[]{:S(2)}, u32[]{:S(2)}) %collective-permute-start.16) | collective-permute-done | bytes 65568 | tf_op jit(solution)/shard_map/ppermute | solution.py:55
  68.5 2.1 entry.3
  71.5 2.8 %copy-done.1 = bf16[1,2,96,128,128]{4,3,2,1,0:T(8,128)(2,1)S(1)} copy-done((bf16[1,2,96,128,128]{4,3,2,1,0:T(8,128)(2,1)S(1)}, bf16[1,2,96,128,128]{4,3,2,1,0:T(8,128)(2,1)}, u32[]{:S(2)}) %copy-start.1) | copy-done | bytes 6291480
  74.3 2.3 densify.2.refs_5_.refs_0_
  76.7 2.9 %collective-permute-start.20 = (bf16[128,256]{1,0:T(8,128)(2,1)S(1)}, bf16[128,256]{1,0:T(8,128)(2,1)S(1)}, u32[]{:S(2)}, u32[]{:S(2)}) collective-permute-start(bf16[128,256]{1,0:T(8,128)(2,1)S(1)} %get-tuple-element.66), channel_id=1, source_target_pairs={{0,3},{1,2},{2,1},{3,0},{4,7},{5,6},{6,5},{7,4},{8,11},{9,10},{10,... | collective-permute-start | bytes 196616 | tf_op jit(solution)/shard_map/ppermute | solution.py:55
  79.5 3.0 %collective-permute-start.22 = (bf16[128,256]{1,0:T(8,128)(2,1)S(1)}, bf16[128,256]{1,0:T(8,128)(2,1)S(1)}, u32[]{:S(2)}, u32[]{:S(2)}) collective-permute-start(bf16[128,256]{1,0:T(8,128)(2,1)S(1)} %get-tuple-element.68), channel_id=1, source_target_pairs={{0,5},{1,4},{2,7},{3,6},{4,1},{5,0},{6,3},{7,2},{8,13},{9,12},{10,... | collective-permute-start | bytes 196616 | tf_op jit(solution)/shard_map/ppermute | solution.py:55
  83.3 3.8 %collective-permute-start.24 = (bf16[128,256]{1,0:T(8,128)(2,1)S(1)}, bf16[128,256]{1,0:T(8,128)(2,1)S(1)}, u32[]{:S(2)}, u32[]{:S(2)}) collective-permute-start(bf16[128,256]{1,0:T(8,128)(2,1)S(1)} %get-tuple-element.70), channel_id=1, source_target_pairs={{0,7},{1,6},{2,5},{3,4},{4,3},{5,2},{6,1},{7,0},{8,15},{9,14},{10,... | collective-permute-start | bytes 196616 | tf_op jit(solution)/shard_map/ppermute | solution.py:55
  89.0 2.1 collective-permute-done.24.refs_13_
  91.1 3.3 %middle.3 = (bf16[256,256]{1,0:T(8,128)(2,1)S(1)}, bf16[256,256]{1,0:T(8,128)(2,1)}, bf16[128,256]{1,0:T(8,128)(2,1)S(1)}, bf16[128,256]{1,0:T(8,128)(2,1)S(1)},...) custom-call(s32[1]{0:T(128)} %bitcast.me_ref.refs_0_, ...), custom_call_target="tpu_custom_call", output_to_operand_aliasing={{9}: (14, {})} | custom-call | flops 184549376 | bytes 1441792 | tf_op jit(solution)/shard_map/middle/pallas_call | solution.py:324
  94.4 3.0 %collective-permute-start.25 = (bf16[128,256]{1,0:T(8,128)(2,1)S(1)}, bf16[128,256]{1,0:T(8,128)(2,1)S(1)}, u32[]{:S(2)}, u32[]{:S(2)}) collective-permute-start(bf16[128,256]{1,0:T(8,128)(2,1)S(1)} %get-tuple-element.74), channel_id=1, source_target_pairs={{0,1},{1,0},{2,3},{3,2},{4,5},{5,4},{6,7},{7,6},{8,9},{9,8},{10,11... | collective-permute-start | bytes 196616 | tf_op jit(solution)/shard_map/ppermute | solution.py:55
  97.4 3.8 %collective-permute-start.26 = (bf16[128,256]{1,0:T(8,128)(2,1)S(1)}, bf16[128,256]{1,0:T(8,128)(2,1)S(1)}, u32[]{:S(2)}, u32[]{:S(2)}) collective-permute-start(bf16[128,256]{1,0:T(8,128)(2,1)S(1)} %get-tuple-element.75), channel_id=1, source_target_pairs={{0,2},{1,3},{2,0},{3,1},{4,6},{5,7},{6,4},{7,5},{8,10},{9,11},{10,... | collective-permute-start | bytes 196616 | tf_op jit(solution)/shard_map/ppermute | solution.py:55
  101.3 49.7 %all-reduce.3.cloned.1.call-done = bf16[256,256]{1,0:T(8,128)(2,1)} async-done(((bf16[256,256]{1,0:T(8,128)(2,1)}), bf16[256,256]{1,0:T(8,128)(2,1)}) %all-reduce.3.cloned.1.call-update) | async-done | bytes 131088 | tf_op jit(solution)/shard_map/psum | solution.py:351
  155.8 2.2 collective-permute-start.30
  158.0 2.6 %collective-permute-start.31 = (bf16[128,256]{1,0:T(8,128)(2,1)S(1)}, bf16[128,256]{1,0:T(8,128)(2,1)S(1)}, u32[]{:S(2)}, u32[]{:S(2)}) collective-permute-start(bf16[128,256]{1,0:T(8,128)(2,1)S(1)} %get-tuple-element.80), channel_id=1, source_target_pairs={{0,7},{1,6},{2,5},{3,4},{4,3},{5,2},{6,1},{7,0},{8,15},{9,14},{10,... | collective-permute-start | bytes 196616 | tf_op jit(solution)/shard_map/ppermute | solution.py:55
  166.3 57.6 %all-reduce.5.cloned.1.call-done = bf16[1,1,256,256]{3,2,1,0:T(8,128)(2,1)} async-done(((bf16[1,1,256,256]{3,2,1,0:T(8,128)(2,1)}), bf16[1,1,256,256]{3,2,1,0:T(8,128)(2,1)}) %all-reduce.5.cloned.1.call-update) | async-done | bytes 131088 | tf_op jit(solution)/shard_map/psum | solution.py:351
  (92 shorter events, 47.3 us)
Async XLA Ops:
  7.2 143.8 %all-reduce.3.cloned.1.call-start = ((), (), s32[]{:S(2)}) async-start(), calls=%async_computation | async-start | bytes 262144 | tf_op jit(solution)/shard_map/psum | solution.py:351
  25.5 7.7 %collective-permute-start.3 = (bf16[128,256]{1,0:T(8,128)(2,1)S(1)}, bf16[128,256]{1,0:T(8,128)(2,1)S(1)}, u32[]{:S(2)}, u32[]{:S(2)}) collective-permute-start(bf16[128,256]{1,0:T(8,128)(2,1)S(1)} %get-tuple-element.46), channel_id=1, source_target_pairs={{0,1},{1,0},{2,3},{3,2},{4,5},{5,4},{6,7},{7,6},{8,9},{9,8},{10,11... | collective-permute-start | bytes 196616 | tf_op jit(solution)/shard_map/ppermute | solution.py:55
  27.4 9.5 %collective-permute-start.4 = (bf16[128,256]{1,0:T(8,128)(2,1)S(1)}, bf16[128,256]{1,0:T(8,128)(2,1)S(1)}, u32[]{:S(2)}, u32[]{:S(2)}) collective-permute-start(bf16[128,256]{1,0:T(8,128)(2,1)S(1)} %get-tuple-element.47), channel_id=1, source_target_pairs={{0,2},{1,3},{2,0},{3,1},{4,6},{5,7},{6,4},{7,5},{8,10},{9,11},{10,... | collective-permute-start | bytes 196616 | tf_op jit(solution)/shard_map/ppermute | solution.py:55
  29.0 14.7 %collective-permute-start.5 = (bf16[128,256]{1,0:T(8,128)(2,1)S(1)}, bf16[128,256]{1,0:T(8,128)(2,1)S(1)}, u32[]{:S(2)}, u32[]{:S(2)}) collective-permute-start(bf16[128,256]{1,0:T(8,128)(2,1)S(1)} %get-tuple-element.48), channel_id=1, source_target_pairs={{0,3},{1,2},{2,1},{3,0},{4,7},{5,6},{6,5},{7,4},{8,11},{9,10},{10,... | collective-permute-start | bytes 196616 | tf_op jit(solution)/shard_map/ppermute | solution.py:55
  29.1 14.7 %collective-permute-start.6 = (bf16[128,256]{1,0:T(8,128)(2,1)S(1)}, bf16[128,256]{1,0:T(8,128)(2,1)S(1)}, u32[]{:S(2)}, u32[]{:S(2)}) collective-permute-start(bf16[128,256]{1,0:T(8,128)(2,1)S(1)} %get-tuple-element.49), channel_id=1, source_target_pairs={{0,4},{1,5},{2,6},{3,7},{4,0},{5,1},{6,2},{7,3},{8,12},{9,13},{10,... | collective-permute-start | bytes 196616 | tf_op jit(solution)/shard_map/ppermute | solution.py:55
  32.0 11.7 %collective-permute-start.7 = (bf16[128,256]{1,0:T(8,128)(2,1)S(1)}, bf16[128,256]{1,0:T(8,128)(2,1)S(1)}, u32[]{:S(2)}, u32[]{:S(2)}) collective-permute-start(bf16[128,256]{1,0:T(8,128)(2,1)S(1)} %get-tuple-element.50), channel_id=1, source_target_pairs={{0,5},{1,4},{2,7},{3,6},{4,1},{5,0},{6,3},{7,2},{8,13},{9,12},{10,... | collective-permute-start | bytes 196616 | tf_op jit(solution)/shard_map/ppermute | solution.py:55
  33.3 10.5 %collective-permute-start.8 = (bf16[128,256]{1,0:T(8,128)(2,1)S(1)}, bf16[128,256]{1,0:T(8,128)(2,1)S(1)}, u32[]{:S(2)}, u32[]{:S(2)}) collective-permute-start(bf16[128,256]{1,0:T(8,128)(2,1)S(1)} %get-tuple-element.51), channel_id=1, source_target_pairs={{0,6},{1,7},{2,4},{3,5},{4,2},{5,3},{6,0},{7,1},{8,14},{9,15},{10,... | collective-permute-start | bytes 196616 | tf_op jit(solution)/shard_map/ppermute | solution.py:55
  46.2 7.5 %collective-permute-start.10 = (bf16[128,256]{1,0:T(8,128)(2,1)S(1)}, bf16[128,256]{1,0:T(8,128)(2,1)S(1)}, u32[]{:S(2)}, u32[]{:S(2)}) collective-permute-start(bf16[128,256]{1,0:T(8,128)(2,1)S(1)} %get-tuple-element.54), channel_id=1, source_target_pairs={{0,1},{1,0},{2,3},{3,2},{4,5},{5,4},{6,7},{7,6},{8,9},{9,8},{10,11... | collective-permute-start | bytes 196616 | tf_op jit(solution)/shard_map/ppermute | solution.py:55
  47.9 9.4 %collective-permute-start.11 = (bf16[128,256]{1,0:T(8,128)(2,1)S(1)}, bf16[128,256]{1,0:T(8,128)(2,1)S(1)}, u32[]{:S(2)}, u32[]{:S(2)}) collective-permute-start(bf16[128,256]{1,0:T(8,128)(2,1)S(1)} %get-tuple-element.55), channel_id=1, source_target_pairs={{0,2},{1,3},{2,0},{3,1},{4,6},{5,7},{6,4},{7,5},{8,10},{9,11},{10,... | collective-permute-start | bytes 196616 | tf_op jit(solution)/shard_map/ppermute | solution.py:55
  47.9 9.7 %collective-permute-start.12 = (bf16[128,256]{1,0:T(8,128)(2,1)S(1)}, bf16[128,256]{1,0:T(8,128)(2,1)S(1)}, u32[]{:S(2)}, u32[]{:S(2)}) collective-permute-start(bf16[128,256]{1,0:T(8,128)(2,1)S(1)} %get-tuple-element.56), channel_id=1, source_target_pairs={{0,3},{1,2},{2,1},{3,0},{4,7},{5,6},{6,5},{7,4},{8,11},{9,10},{10,... | collective-permute-start | bytes 196616 | tf_op jit(solution)/shard_map/ppermute | solution.py:55
  49.8 7.9 %collective-permute-start.13 = (bf16[128,256]{1,0:T(8,128)(2,1)S(1)}, bf16[128,256]{1,0:T(8,128)(2,1)S(1)}, u32[]{:S(2)}, u32[]{:S(2)}) collective-permute-start(bf16[128,256]{1,0:T(8,128)(2,1)S(1)} %get-tuple-element.57), channel_id=1, source_target_pairs={{0,4},{1,5},{2,6},{3,7},{4,0},{5,1},{6,2},{7,3},{8,12},{9,13},{10,... | collective-permute-start | bytes 196616 | tf_op jit(solution)/shard_map/ppermute | solution.py:55
  70.6 12.0 %collective-permute-start.18 = (bf16[128,256]{1,0:T(8,128)(2,1)S(1)}, bf16[128,256]{1,0:T(8,128)(2,1)S(1)}, u32[]{:S(2)}, u32[]{:S(2)}) collective-permute-start(bf16[128,256]{1,0:T(8,128)(2,1)S(1)} %get-tuple-element.64), channel_id=1, source_target_pairs={{0,1},{1,0},{2,3},{3,2},{4,5},{5,4},{6,7},{7,6},{8,9},{9,8},{10,11... | collective-permute-start | bytes 196616 | tf_op jit(solution)/shard_map/ppermute | solution.py:55
  71.4 11.9 %collective-permute-start.19 = (bf16[128,256]{1,0:T(8,128)(2,1)S(1)}, bf16[128,256]{1,0:T(8,128)(2,1)S(1)}, u32[]{:S(2)}, u32[]{:S(2)}) collective-permute-start(bf16[128,256]{1,0:T(8,128)(2,1)S(1)} %get-tuple-element.65), channel_id=1, source_target_pairs={{0,2},{1,3},{2,0},{3,1},{4,6},{5,7},{6,4},{7,5},{8,10},{9,11},{10,... | collective-permute-start | bytes 196616 | tf_op jit(solution)/shard_map/ppermute | solution.py:55
  76.6 147.3 %all-reduce.5.cloned.1.call-start = ((), (), s32[]{:S(2)}) async-start(), calls=%async_computation.1 | async-start | bytes 262144 | tf_op jit(solution)/shard_map/psum | solution.py:351
  76.7 10.7 %collective-permute-start.20 = (bf16[128,256]{1,0:T(8,128)(2,1)S(1)}, bf16[128,256]{1,0:T(8,128)(2,1)S(1)}, u32[]{:S(2)}, u32[]{:S(2)}) collective-permute-start(bf16[128,256]{1,0:T(8,128)(2,1)S(1)} %get-tuple-element.66), channel_id=1, source_target_pairs={{0,3},{1,2},{2,1},{3,0},{4,7},{5,6},{6,5},{7,4},{8,11},{9,10},{10,... | collective-permute-start | bytes 196616 | tf_op jit(solution)/shard_map/ppermute | solution.py:55
  79.5 7.9 %collective-permute-start.21 = (bf16[128,256]{1,0:T(8,128)(2,1)S(1)}, bf16[128,256]{1,0:T(8,128)(2,1)S(1)}, u32[]{:S(2)}, u32[]{:S(2)}) collective-permute-start(bf16[128,256]{1,0:T(8,128)(2,1)S(1)} %get-tuple-element.67), channel_id=1, source_target_pairs={{0,4},{1,5},{2,6},{3,7},{4,0},{5,1},{6,2},{7,3},{8,12},{9,13},{10,... | collective-permute-start | bytes 196616 | tf_op jit(solution)/shard_map/ppermute | solution.py:55
  79.5 8.8 %collective-permute-start.22 = (bf16[128,256]{1,0:T(8,128)(2,1)S(1)}, bf16[128,256]{1,0:T(8,128)(2,1)S(1)}, u32[]{:S(2)}, u32[]{:S(2)}) collective-permute-start(bf16[128,256]{1,0:T(8,128)(2,1)S(1)} %get-tuple-element.68), channel_id=1, source_target_pairs={{0,5},{1,4},{2,7},{3,6},{4,1},{5,0},{6,3},{7,2},{8,13},{9,12},{10,... | collective-permute-start | bytes 196616 | tf_op jit(solution)/shard_map/ppermute | solution.py:55
  83.3 7.7 %collective-permute-start.24 = (bf16[128,256]{1,0:T(8,128)(2,1)S(1)}, bf16[128,256]{1,0:T(8,128)(2,1)S(1)}, u32[]{:S(2)}, u32[]{:S(2)}) collective-permute-start(bf16[128,256]{1,0:T(8,128)(2,1)S(1)} %get-tuple-element.70), channel_id=1, source_target_pairs={{0,7},{1,6},{2,5},{3,4},{4,3},{5,2},{6,1},{7,0},{8,15},{9,14},{10,... | collective-permute-start | bytes 196616 | tf_op jit(solution)/shard_map/ppermute | solution.py:55
  94.4 61.4 %collective-permute-start.25 = (bf16[128,256]{1,0:T(8,128)(2,1)S(1)}, bf16[128,256]{1,0:T(8,128)(2,1)S(1)}, u32[]{:S(2)}, u32[]{:S(2)}) collective-permute-start(bf16[128,256]{1,0:T(8,128)(2,1)S(1)} %get-tuple-element.74), channel_id=1, source_target_pairs={{0,1},{1,0},{2,3},{3,2},{4,5},{5,4},{6,7},{7,6},{8,9},{9,8},{10,11... | collective-permute-start | bytes 196616 | tf_op jit(solution)/shard_map/ppermute | solution.py:55
  97.4 60.6 %collective-permute-start.26 = (bf16[128,256]{1,0:T(8,128)(2,1)S(1)}, bf16[128,256]{1,0:T(8,128)(2,1)S(1)}, u32[]{:S(2)}, u32[]{:S(2)}) collective-permute-start(bf16[128,256]{1,0:T(8,128)(2,1)S(1)} %get-tuple-element.75), channel_id=1, source_target_pairs={{0,2},{1,3},{2,0},{3,1},{4,6},{5,7},{6,4},{7,5},{8,10},{9,11},{10,... | collective-permute-start | bytes 196616 | tf_op jit(solution)/shard_map/ppermute | solution.py:55
  151.0 9.6 %collective-permute-start.27 = (bf16[128,256]{1,0:T(8,128)(2,1)S(1)}, bf16[128,256]{1,0:T(8,128)(2,1)S(1)}, u32[]{:S(2)}, u32[]{:S(2)}) collective-permute-start(bf16[128,256]{1,0:T(8,128)(2,1)S(1)} %get-tuple-element.76), channel_id=1, source_target_pairs={{0,3},{1,2},{2,1},{3,0},{4,7},{5,6},{6,5},{7,4},{8,11},{9,10},{10,... | collective-permute-start | bytes 196616 | tf_op jit(solution)/shard_map/ppermute | solution.py:55
  152.9 9.4 %collective-permute-start.28 = (bf16[128,256]{1,0:T(8,128)(2,1)S(1)}, bf16[128,256]{1,0:T(8,128)(2,1)S(1)}, u32[]{:S(2)}, u32[]{:S(2)}) collective-permute-start(bf16[128,256]{1,0:T(8,128)(2,1)S(1)} %get-tuple-element.77), channel_id=1, source_target_pairs={{0,4},{1,5},{2,6},{3,7},{4,0},{5,1},{6,2},{7,3},{8,12},{9,13},{10,... | collective-permute-start | bytes 196616 | tf_op jit(solution)/shard_map/ppermute | solution.py:55
  154.2 9.7 %collective-permute-start.29 = (bf16[128,256]{1,0:T(8,128)(2,1)S(1)}, bf16[128,256]{1,0:T(8,128)(2,1)S(1)}, u32[]{:S(2)}, u32[]{:S(2)}) collective-permute-start(bf16[128,256]{1,0:T(8,128)(2,1)S(1)} %get-tuple-element.78), channel_id=1, source_target_pairs={{0,5},{1,4},{2,7},{3,6},{4,1},{5,0},{6,3},{7,2},{8,13},{9,12},{10,... | collective-permute-start | bytes 196616 | tf_op jit(solution)/shard_map/ppermute | solution.py:55
  155.8 8.1 %collective-permute-start.30 = (bf16[128,256]{1,0:T(8,128)(2,1)S(1)}, bf16[128,256]{1,0:T(8,128)(2,1)S(1)}, u32[]{:S(2)}, u32[]{:S(2)}) collective-permute-start(bf16[128,256]{1,0:T(8,128)(2,1)S(1)} %get-tuple-element.79), channel_id=1, source_target_pairs={{0,6},{1,7},{2,4},{3,5},{4,2},{5,3},{6,0},{7,1},{8,14},{9,15},{10,... | collective-permute-start | bytes 196616 | tf_op jit(solution)/shard_map/ppermute | solution.py:55
  (23 other events, 267.4 us)
Sparse Core Ops, SparseCore 0:
  76.7 74.1 all-reduce.2
  154.7 69.1 all-reduce.4

commit v4 on v0

v4 whole, which is shorter than its diff:
```python
import functools

import jax
import jax.numpy as jnp
from jax import lax
from jax.experimental import pallas as pl
from jax.experimental.pallas import tpu as pltpu
from jax.sharding import PartitionSpec as P

ALPHA = 0.1
BETA_SCALE = 0.5
VMEM = pl.BlockSpec(memory_space=pltpu.VMEM)
SMEM = pl.BlockSpec(memory_space=pltpu.SMEM)
HBM = pl.BlockSpec(memory_space=pltpu.HBM)
PARAMS = pltpu.CompilerParams(vmem_limit_bytes=24 * 2**20)
F32 = jnp.float32
BF16 = jnp.bfloat16


def cost(flops, nbytes):
    return pl.CostEstimate(flops=flops, bytes_accessed=nbytes, transcendentals=0)


def swapped(block, k):
    n = lax.axis_size("rows")
    return lax.ppermute(block, "rows", [(i, i ^ k) for i in range(n)])


def passed_along(block, axis, distance):
    devices = range(lax.axis_size(axis))
    route = [(i - distance, i) for i in devices if i - distance in devices]
    return lax.ppermute(block, axis, route)


class Refs:
    def __init__(self, refs):
        self.refs = list(refs)

    def take(self, count=None):
        many = 1 if count is None else count
        taken, self.refs = self.refs[:many], self.refs[many:]
        return taken[0] if count is None else taken


class Call:
    def __init__(self):
        self.operands, self.specs, self.outs, self.out_specs, self.scratch = [], [], [], [], []
        self.aliases = {}

    def give(self, spec, *arrays):
        self.operands += arrays
        self.specs += [spec] * len(arrays)

    def want(self, spec, shape, dtype, count=1):
        self.outs += [jax.ShapeDtypeStruct(shape, dtype)] * count
        self.out_specs += [spec] * count

    def run(self, kernel, name, estimate, params=PARAMS):
        return pl.pallas_call(
            kernel,
            out_shape=self.outs,
            in_specs=self.specs,
            out_specs=self.out_specs,
            scratch_shapes=self.scratch,
            input_output_aliases=self.aliases,
            compiler_params=params,
            cost_estimate=estimate,
            name=name,
        )(*self.operands)


def densify_kernel(row_tiles, n, chunks, *refs):
    refs = Refs(refs)
    me_ref, rows_ref, cols_ref, count_ref, vals_ref = refs.take(5)
    ticks = vals_ref.shape[1]
    outs = refs.take(ticks)
    vals, acc, sems = refs.take(3)
    entries, tile = vals.shape[1:3]
    chunk = entries // chunks
    me = me_ref[0]
    copies = {}
    for t in range(ticks):
        for c in range(chunks):
            part = pl.ds(c * chunk, chunk)
            copies[t, c] = pltpu.make_async_copy(
                vals_ref.at[0, t, part], vals.at[t, part], sems.at[t, c]
            )
            copies[t, c].start()
    for t in range(ticks):
        acc[...] = jnp.zeros_like(acc)

        def add(e, carry):
            owner = lax.div(cols_ref[0, t, e], row_tiles)
            block = lax.rem(cols_ref[0, t, e], row_tiles)
            slot = jnp.bitwise_xor(owner, me)
            slot = jnp.where((owner == me) & (block > 0), n - 1 + block, slot)
            rows = pl.ds(pl.multiple_of(rows_ref[0, t, e] * tile, tile), tile)
            cols = pl.ds(pl.multiple_of(slot * tile, tile), tile)
            acc[rows, cols] += vals[t, e].astype(F32)
            return carry

        for c in range(chunks):
            copies[t, c].wait()
            stop = jnp.clip(count_ref[0, t, 0], c * chunk, (c + 1) * chunk)
            lax.fori_loop(c * chunk, stop, add, 0)
        outs[t][...] = acc[...].astype(BF16)


def densify(me, rows, cols, count, vals, row_tiles, n):
    _, ticks, entries, tile, _ = vals.shape
    chunks = 4 if entries % 4 == 0 else 1
    shape = (row_tiles * tile, (n + row_tiles - 1) * tile)
    call = Call()
    call.give(SMEM, me, rows, cols, count)
    call.give(HBM, vals)
    call.want(VMEM, shape, BF16, ticks)
    call.scratch = [
        pltpu.VMEM(vals.shape[1:], BF16),
        pltpu.VMEM(shape, F32),
        pltpu.SemaphoreType.DMA((ticks, chunks)),
    ]
    return call.run(
        functools.partial(densify_kernel, row_tiles, n, chunks),
        "densify",
        cost(ticks * entries * tile * tile * 20, ticks * entries * tile * tile * 2),
        pltpu.CompilerParams(vmem_limit_bytes=58 * 2**20),
    )


def tile_at(ref, index, tile):
    return ref[pl.ds(pl.multiple_of(index * tile, tile), tile), :]


def give_got(call, got):
    call.give(VMEM, got["far"], *got["near"], *got["relayed"])


def take_got(refs, c):
    h, tile = c["n"] // 2, c["tile"]
    far = refs.take()
    near = refs.take(h - 1) if c["own_sent"] else None
    relayed = refs.take(h - 1)
    if near is None:
        near = [ref.at[tile:, :] for ref in relayed]
    return far, near, relayed


def spread_of(adj_ref, own_ref, got, pick_ref, me, c):
    n, tile = c["n"], c["tile"]
    far, near, relayed = got
    far_index = pick_ref[0, c["from_tick"] * n + jnp.bitwise_xor(me, n // 2)]
    blocks = jnp.concatenate(
        [own_ref[:tile, :]]
        + [ref[:tile, :] for ref in near]
        + [tile_at(far, far_index, tile)]
        + [ref[:tile, :] for ref in relayed]
        + [own_ref[tile : c["rows"], :]],
        axis=0,
    )
    total = jnp.dot(adj_ref[...], blocks, preferred_element_type=F32)
    return ((1.0 - ALPHA) * total).astype(BF16)


def chunk_total(kept_ref, relayed, c):
    total = kept_ref[...]
    for ref in relayed:
        total = total + ref[c["tile"] : c["tile"] + c["part"], :].astype(F32)
    return total.astype(BF16)


def layer_kernel(c, *refs):
    refs = Refs(refs)
    n, tile, rows, width = c["n"], c["tile"], c["rows"], c["width"]
    h = n // 2
    me_ref, section_ref, preact_all, weight_all = refs.take(4)
    picks = refs.take(h)
    if c["entry"]:
        last_ref, passed_ref = refs.take(2)
    else:
        adj_ref, own_ref = refs.take(2)
        got = take_got(refs, c)
    if c["final"]:
        support_all, acc_ref = refs.take(2)
    if c["sum_before"]:
        kept_before = refs.take()
    payload_ref = refs.take()
    sends = refs.take(h - 1)
    if c["final"]:
        kept_ref = refs.take()
    else:
        masked_ref = refs.take()
    if c["sum_before"]:
        chunk_ref = refs.take()
    preact_ref, weight_ref, load_sems = refs.take(3)

    me = me_ref[0]
    section = section_ref[0]
    loads = [
        (preact_all.at[0, c["tick"], c["layer"]], preact_ref),
        (weight_all.at[0, c["layer"]], weight_ref),
    ]
    if c["final"]:
        support_ref, term_ref = refs.take(2)
        loads.append((support_all.at[0, c["tick"], c["layer"]], support_ref))
    loads = [pltpu.make_async_copy(a, b, load_sems.at[i]) for i, (a, b) in enumerate(loads)]
    for load in loads:
        load.start()
    step = (c["layers"] * section + c["layer"] + 1).astype(F32)
    beta = jnp.log(BETA_SCALE / jnp.full((1, width), step, F32) + 1.0)
    if not c["entry"]:
        grad = spread_of(adj_ref, own_ref, got, picks[0], me, c)
    for load in loads:
        load.wait()
    if c["entry"]:
        grad = jnp.where(section == c["sections"] - 1, last_ref[...], passed_ref[...])

    masked = jnp.where(preact_ref[...] > 0, grad, jnp.zeros_like(grad))
    product = lax.dot_general(
        masked, weight_ref[...], (((1,), (1,)), ((), ())), preferred_element_type=F32
    )
    image = ((1.0 - beta) * masked.astype(F32) + beta * product).astype(BF16)
    payload_ref[:rows, :] = image
    for k in range(1, h):
        sends[k - 1][...] = tile_at(payload_ref, picks[k][0, c["tick"] * n + me], tile)
    if c["final"]:
        term = lax.dot_general(
            support_ref[...], masked, (((0,), (0,)), ((), ())), preferred_element_type=F32
        )
        term_ref[...] = acc_ref[...] + beta * term
        half = width // 2
        mine = lax.div(me, h)
        payload_ref[rows:, :] = tile_at(term_ref, 1 - mine, half).astype(BF16)
        kept_ref[...] = tile_at(term_ref, mine, half)
    else:
        masked_ref[...] = masked
    if c["sum_before"]:
        chunk_ref[...] = chunk_total(kept_before, got[2], c)


def relay_kernel(c, *refs):
    refs = Refs(refs)
    n, tile, part = c["n"], c["tile"], c["part"]
    h = n // 2
    me_ref, far_ref = refs.take(2)
    picks = refs.take(h - 1)
    if not c["own_sends"]:
        own_ref = refs.take()
    if c["final"]:
        kept_ref = refs.take()
    sends = refs.take(h - 1)
    if c["final"]:
        kept_chunk, sum_ref = refs.take(2)
    me = me_ref[0]
    base = c["tick"] * n
    for k in range(1, h):
        index = picks[k - 1][0, base + jnp.bitwise_xor(me, h)]
        sends[k - 1][:tile, :] = tile_at(far_ref, index, tile)
        if not c["own_sends"]:
            sends[k - 1][tile:, :] = tile_at(own_ref, picks[k - 1][0, base + me], tile)
    if c["final"]:
        sum_ref[...] = kept_ref[...] + far_ref[c["rows"] :, :].astype(F32)
        place = lax.rem(me, h)
        for k in range(1, h):
            sends[k - 1][tile : tile + part, :] = tile_at(
                sum_ref, jnp.bitwise_xor(place, k), part
            ).astype(BF16)
        kept_chunk[...] = tile_at(sum_ref, place, part)


def exit_kernel(c, *refs):
    refs = Refs(refs)
    me_ref, pick_ref, adj_ref, own_ref = refs.take(4)
    got = take_got(refs, c)
    if c["tick"] > 0:
        refs.take()
    if c["final"]:
        kept_ref, above = refs.take(), refs.take(c["layers"] - 1)
    out_ref, extra_ref, hold_ref, sem = refs.take(4)
    grad = spread_of(adj_ref, own_ref, got, pick_ref, me_ref[0], c)
    hold_ref[...] = grad
    copy = pltpu.make_async_copy(hold_ref, out_ref.at[c["tick"], 0], sem)
    copy.start()
    if c["final"]:
        extra_ref[0] = chunk_total(kept_ref, got[2], c)
        for i, ref in enumerate(above):
            extra_ref[i + 1] = ref[...]
    else:
        extra_ref[...] = grad
    copy.wait()


def finish_kernel(n, part, *refs):
    refs = Refs(refs)
    me_ref = refs.take()
    sums = refs.take(n)
    out_ref, hold_ref, sems = refs.take(3)
    layers = hold_ref.shape[0]
    copies = []
    for layer in range(layers):
        for k in range(n):
            start = pl.multiple_of(jnp.bitwise_xor(me_ref[0], k) * part, 8)
            hold_ref[layer, pl.ds(start, part), :] = sums[k][layer].astype(F32)
        copy = pltpu.make_async_copy(hold_ref.at[layer], out_ref.at[0, layer], sems.at[layer])
        copy.start()
        copies.append(copy)
    for copy in copies:
        copy.wait()


def shards(grad_in, grad_last, support, preact, weights, tile_vals, tile_row, tile_col, tile_count):
    section = lax.axis_index("section")
    me = lax.axis_index("rows")
    n = lax.axis_size("rows")
    h = n // 2
    sections = lax.axis_size("section")
    ticks = support.shape[1]
    layers = support.shape[2]
    rows, width = grad_last.shape
    tile = tile_vals.shape[-1]
    row_tiles = rows // tile
    part = width // n
    room = max(part, 16)
    me_arr = me.astype(jnp.int32).reshape(1)
    section_arr = section.astype(jnp.int32).reshape(1)

    owner = tile_col[0] // row_tiles
    named = jnp.where(
        owner[:, :, None] == jnp.arange(n)[None, None, :], (tile_col[0] % row_tiles)[:, :, None], 0
    )
    pick = jnp.max(named, axis=1).reshape(1, ticks * n).astype(jnp.int32)
    picks = [pick] + [swapped(pick, k) for k in range(1, h)]

    adjs = densify(me_arr, tile_row, tile_col, tile_count, tile_vals, row_tiles, n)
    handoff = passed = kept = None
    weight_acc = [None] * layers
    chunks = []
    initial = []
    base = dict(
        n=n, tile=tile, rows=rows, width=width, layers=layers, sections=sections, part=part
    )
    layer_cost = cost(2 * rows * width * (width + (n + 1) * tile), (6 + 2 * n) * rows * width)
    small_cost = cost(rows * width, 2 * n * rows * width)
    for tick in range(ticks):
        final = tick == ticks - 1
        if tick > 0:
            passed = passed_along(passed, "section", -1)
        adj = adjs[tick]
        payload = got = None
        toward = 0.0
        own_sent = None
        for layer in reversed(range(layers)):
            entry = layer == layers - 1
            own_sends = not (tick == 0 and entry)
            c = dict(
                base, layer=layer, tick=tick, from_tick=tick, entry=entry, final=final,
                own_sends=own_sends, own_sent=own_sent, sum_before=final and not entry,
            )
            if own_sends:
                call = Call()
                call.give(SMEM, me_arr, section_arr)
                call.give(HBM, preact, weights)
                call.give(SMEM, *picks)
                if entry:
                    call.give(VMEM, grad_last, passed)
                else:
                    call.give(VMEM, adj, payload)
                    give_got(call, got)
                if final:
                    call.give(HBM, support)
                    call.give(VMEM, weight_acc[layer])
                if c["sum_before"]:
                    call.give(VMEM, kept)
                call.want(VMEM, (rows + (width // 2 if final else 0), width), BF16)
                call.want(VMEM, (tile, width), BF16, h - 1)
                if final:
                    call.want(VMEM, (width // 2, width), F32)
                else:
                    call.want(VMEM, (rows, width), BF16)
                if c["sum_before"]:
                    call.want(VMEM, (part, width), BF16)
                call.scratch = [
                    pltpu.VMEM((rows, width), BF16),
                    pltpu.VMEM((width, width), BF16),
                    pltpu.SemaphoreType.DMA((4,)),
                ]
                if final:
                    call.scratch.append(pltpu.VMEM((rows, width), BF16))
                    call.scratch.append(pltpu.VMEM((width, width), F32))
                results = Refs(
                    call.run(
                        functools.partial(layer_kernel, c), "entry" if entry else "middle", layer_cost
                    )
                )
            else:
                beta = jnp.log(BETA_SCALE / (layers * section + layer + 1).astype(F32) + 1.0)
                masked = jnp.where(preact[0, tick, layer] > 0, grad_in[0], jnp.zeros_like(grad_in[0]))
                product = jnp.dot(masked, weights[0, layer].T, preferred_element_type=F32)
                image = ((1.0 - beta) * masked.astype(F32) + beta * product).astype(BF16)
                results = Refs([image, masked])
            payload = results.take()
            sends = results.take(h - 1) if own_sends else []
            if final:
                kept_half = results.take()
            else:
                beta = jnp.log(BETA_SCALE / (layers * section + layer + 1).astype(F32) + 1.0)
                term = beta * jnp.dot(
                    support[0, tick, layer].T, results.take(), preferred_element_type=F32
                )
                old = weight_acc[layer]
                weight_acc[layer] = term if old is None else old + term
            if c["sum_before"]:
                chunks.insert(0, results.take())
            toward = toward + ALPHA * payload[:rows].astype(F32)

            far = swapped(payload, h)
            near = [swapped(send, k + 1) for k, send in enumerate(sends)]
            call = Call()
            call.give(SMEM, me_arr)
            call.give(VMEM, far)
            call.give(SMEM, *picks[1:])
            if not own_sends:
                call.give(VMEM, payload)
            if final:
                call.give(VMEM, kept_half)
            message = tile * (1 if own_sends else 2) + (room if final else 0)
            call.want(VMEM, (message, width), BF16, h - 1)
            if final:
                call.want(VMEM, (part, width), F32)
                call.scratch = [pltpu.VMEM((width // 2, width), F32)]
            results = Refs(call.run(functools.partial(relay_kernel, c), "relay", small_cost))
            relays = results.take(h - 1)
            if final:
                kept = results.take()
            relayed = [swapped(relay, k + 1) for k, relay in enumerate(relays)]
            got = dict(far=far, near=near, relayed=relayed)
            own_sent = own_sends
        initial.append(toward)
        c = dict(base, tick=tick, from_tick=tick, final=final, own_sent=own_sent)
        call = Call()
        call.give(SMEM, me_arr, pick)
        call.give(VMEM, adj, payload)
        give_got(call, got)
        if tick > 0:
            call.aliases[len(call.operands)] = 0
            call.give(HBM, handoff)
        if final:
            call.give(VMEM, kept, *chunks)
        call.want(HBM, (ticks, 1, rows, width), BF16)
        if final:
            call.want(VMEM, (layers, part, width), BF16)
        else:
            call.want(VMEM, (rows, width), BF16)
        call.scratch = [pltpu.VMEM((rows, width), BF16), pltpu.SemaphoreType.DMA]
        handoff, passed = call.run(functools.partial(exit_kernel, c), "exit", layer_cost)
    far = swapped(passed, h)
    near = [passed] + [swapped(passed, k) for k in range(1, h)]
    forwarded = [far] + [swapped(far, k) for k in range(1, h)]
    call = Call()
    call.give(SMEM, me_arr)
    call.give(VMEM, *near, *forwarded)
    call.want(HBM, (1, layers, width, width), F32)
    call.scratch = [pltpu.VMEM((layers, width, width), F32), pltpu.SemaphoreType.DMA((layers,))]
    (weight_grad,) = call.run(functools.partial(finish_kernel, n, part), "finish", small_cost)
    return handoff, jnp.stack(initial)[None], weight_grad


def solution(mesh):
    return jax.shard_map(
        shards,
        mesh=mesh,
        in_specs=(
            P("section", "rows", None),
            P("rows", None),
            P("section", None, None, "rows", None),
            P("section", None, None, "rows", None),
            P("section", None, None, None),
            P("section", None, "rows", None, None),
            P("section", None, "rows"),
            P("section", None, "rows"),
            P("section", None, "rows"),
        ),
        out_specs=(
            P(None, "section", "rows", None),
            P("section", None, "rows", None),
            P("section", None, None, None),
        ),
        check_vma=False,
    )
```

time: 409 us -> 108 us (0.26)
  waiting for transfers between devices: 228 us -> 34.8 us
  local copies, waits for them, and re-layouts: 82.6 us -> 3.7 us
  matrix products: 75.5 us -> 1.93 us
  starting transfers between devices: 2.16 us -> 47.8 us
  Pallas kernels: 0 us -> 16.6 us
  between operations: 14.2 us -> 1.12 us
  other arithmetic: 5.81 us -> 1.7 us
    all_gather x4 -> x0, waiting for transfers between devices: 157 us -> none  [shards(): gathered = lax.all_gather(image, 'rows', axis=0, tiled=True)]
    dot_general x16 -> x3, matrix products: 75.5 us -> 1.93 us  [the longest x1 1.48 us: shards(): product = jnp.dot(masked, weights[0, layer].T, preferred_element_type=F32)]
    psum x1 -> x0, waiting for transfers between devices: 68.5 us -> none  [shards(): weight_acc[layer] = weight_acc[layer] + lax.psum(term, 'rows')]
    dot_general x4 -> x0, local copies, waits for them, and re-layouts: 51 us -> none  [tile_product(): jnp.einsum('kab,kbf->kaf', values, blocks, preferred_element_type=jnp.flo...]
    ppermute x0 -> x35, starting transfers between devices: none -> 46.5 us  [swapped(): return lax.ppermute(block, 'rows', [(i, i ^ k) for i in range(n)])]
    ppermute x0 -> x35, waiting for transfers between devices: none -> 33.3 us  [swapped(): return lax.ppermute(block, 'rows', [(i, i ^ k) for i in range(n)])]
    gather x4 -> x0, local copies, waits for them, and re-layouts: 28.4 us -> none  [tile_product(): blocks = gathered.reshape(-1, tile, width)[index]]
    pallas_call x0 -> x11, Pallas kernels: none -> 16.6 us  [run(): pl.pallas_call(kernel, out_shape=self.outs, in_specs=self.specs, out_spec...]
  transfers between devices with their start and end apart: 6 -> 36, of which waited for: 6 -> 18; matrix products, arithmetic and copies ran while one was open for 3% -> 3% of each run, Pallas kernels for 0% -> 7%
where the time goes in v4:
time: 108 us
  starting transfers between devices  47.8 us (44%)
  waiting for transfers between devices  34.8 us (32%)
  Pallas kernels  16.6 us (15%)
  local copies, waits for them, and re-layouts  3.7 us (3%)
  matrix products  1.93 us (2%)
  other arithmetic  1.7 us (2%)
  between operations  1.12 us (1%)
    ppermute x35, starting transfers between devices, swapped(): return lax.ppermute(block, 'rows', [(i, i ^ k) for i in range(n)])  46.5 us
    ppermute x35, waiting for transfers between devices, swapped(): return lax.ppermute(block, 'rows', [(i, i ^ k) for i in range(n)])  33.3 us
    pallas_call x11, Pallas kernels, run(): pl.pallas_call(kernel, out_shape=self.outs, in_specs=self.specs, out_spec...  16.6 us
    unnamed x17, local copies, waits for them, and re-layouts  3.49 us
  transfers between devices with their start and end apart: 36, of which 18 were waited for; matrix products, arithmetic and copies ran while one was open for 3% of the time, Pallas kernels for 7%

profile of v4, /device:TPU:0, one launch (start us, length us, event | category | flops | bytes accessed | tf_op | source)
XLA Modules:
  0.0 107.7 jit_solution(6525756289509607032)
XLA Ops:
  2.3 4.1 %collective-permute-start.3 = (bf16[256,256]{1,0:T(8,128)(2,1)S(1)}, bf16[256,256]{1,0:T(8,128)(2,1)S(1)}, u32[]{:S(2)}, u32[]{:S(2)}) collective-permute-start(bf16[256,256]{1,0:T(8,128)(2,1)S(1)} %fusion.3.refs_5_.refs_9_), channel_id=1, source_target_pairs={{0,4},{1,5},{2,6},{3,7},{4,0},{5,1},{6,2},{7,3},{8,12},{9,13},{10,... | collective-permute-start | bytes 393224 | tf_op jit(solution)/shard_map/ppermute | solution.py:26
  8.7 1.6 %collective-permute-start.1 = (s32[1,16]{1,0:T(1,128)S(1)}, s32[1,16]{1,0:T(1,128)S(1)}, u32[]{:S(2)}, u32[]{:S(2)}) collective-permute-start(s32[1,16]{1,0:T(1,128)S(1)} %reshape.82.refs_4_.refs_1_), channel_id=1, source_target_pairs={{0,2},{1,3},{2,0},{3,1},{4,6},{5,7},{6,4},{7,5},{8,10},{9,11},{10,... | collective-permute-start | bytes 200 | tf_op jit(solution)/shard_map/ppermute | solution.py:26
  12.3 2.5 %collective-permute-done.2.refs_4_.refs_7_ = s32[1,16]{1,0:T(1,128)S(1)} collective-permute-done((s32[1,16]{1,0:T(1,128)S(1)}, s32[1,16]{1,0:T(1,128)S(1)}, u32[]{:S(2)}, u32[]{:S(2)}) %collective-permute-start.2) | collective-permute-done | bytes 96 | tf_op jit(solution)/shard_map/ppermute | solution.py:26
  16.4 2.5 %collective-permute-start.6 = (bf16[256,256]{1,0:T(8,128)(2,1)S(1)}, bf16[256,256]{1,0:T(8,128)(2,1)S(1)}, u32[]{:S(2)}, u32[]{:S(2)}) collective-permute-start(bf16[256,256]{1,0:T(8,128)(2,1)S(1)} %get-tuple-element.43), channel_id=1, source_target_pairs={{0,3},{1,2},{2,1},{3,0},{4,7},{5,6},{6,5},{7,4},{8,11},{9,10},{10,... | collective-permute-start | bytes 393224 | tf_op jit(solution)/shard_map/ppermute | solution.py:26
  20.2 5.4 %densify.1 = (bf16[256,1152]{1,0:T(8,128)(2,1)}, bf16[256,1152]{1,0:T(8,128)(2,1)}) custom-call(s32[1]{0:T(128)} %bitcast.refs_0_, s32[1,2,96]{2,1,0:T(2,128)} %refs_1_.1, s32[1,2,96]{2,1,0:T(2,128)} %refs_2_.4, s32[1,2,1]{2,1,0:T(2,128)} %copy.16.refs_3_, bf16[1,2,96,128,128]{4,3,2,1,0:T(8,128)(2,1)} %refs_4_.1), custom_call_target="tpu_custom_call" | custom-call | flops 62914560 | bytes 6291456 | tf_op jit(solution)/shard_map/densify/pallas_call | solution.py:59
  26.8 1.6 %middle.2 = (bf16[256,256]{1,0:T(8,128)(2,1)S(1)}, bf16[128,256]{1,0:T(8,128)(2,1)S(1)}, bf16[128,256]{1,0:T(8,128)(2,1)S(1)}, bf16[128,256]{1,0:T(8,128)(2,1)S(1)}, bf16[256,256]{1,0:T(8,128)(2,1)S(1)}) custom-call(s32[1]{0:T(128)} %bitcast.refs_0_, s32[1]{0:T(128)} %bitcast.2.refs_1_, bf16[1,2,2,256,256]{4,3,2,1,0:T(8,128)(2,1)S(1)} %copy-done, ...), custom_call_target="tpu_custom_call" | custom-call | flops 184549376 | bytes 1441792 | tf_op jit(solution)/shard_map/middle/pallas_call | solution.py:59
  29.0 2.5 %collective-permute-start.10 = (bf16[128,256]{1,0:T(8,128)(2,1)S(1)}, bf16[128,256]{1,0:T(8,128)(2,1)S(1)}, u32[]{:S(2)}, u32[]{:S(2)}) collective-permute-start(bf16[128,256]{1,0:T(8,128)(2,1)S(1)} %get-tuple-element.47), channel_id=1, source_target_pairs={{0,3},{1,2},{2,1},{3,0},{4,7},{5,6},{6,5},{7,4},{8,11},{9,10},{10,... | collective-permute-start | bytes 196616 | tf_op jit(solution)/shard_map/ppermute | solution.py:26
  32.5 3.3 %collective-permute-done.7.refs_1_.refs_4_ = bf16[256,256]{1,0:T(8,128)(2,1)S(1)} collective-permute-done((bf16[256,256]{1,0:T(8,128)(2,1)S(1)}, bf16[256,256]{1,0:T(8,128)(2,1)S(1)}, u32[]{:S(2)}, u32[]{:S(2)}) %collective-permute-start.7) | collective-permute-done | bytes 131104 | tf_op jit(solution)/shard_map/ppermute | solution.py:26
  37.6 2.4 %collective-permute-start.13 = (bf16[128,256]{1,0:T(8,128)(2,1)S(1)}, bf16[128,256]{1,0:T(8,128)(2,1)S(1)}, u32[]{:S(2)}, u32[]{:S(2)}) collective-permute-start(bf16[128,256]{1,0:T(8,128)(2,1)S(1)} %get-tuple-element.50), channel_id=1, source_target_pairs={{0,3},{1,2},{2,1},{3,0},{4,7},{5,6},{6,5},{7,4},{8,11},{9,10},{10,... | collective-permute-start | bytes 196616 | tf_op jit(solution)/shard_map/ppermute | solution.py:26
  44.0 1.6 %exit.2 = (bf16[2,1,256,256]{3,2,1,0:T(8,128)(2,1)}, bf16[256,256]{1,0:T(8,128)(2,1)S(1)}) custom-call(s32[1]{0:T(128)} %bitcast.refs_0_, s32[1,16]{1,0:T(1,128)S(1)} %reshape.82.refs_4_.refs_1_, bf16[256,1152]{1,0:T(8,128)(2,1)S(1)} %copy-done.5, bf16[256,256]{1,0:T(8,128)(2,1)S(1)} %get-tuple-element.44.refs_3_, ...), custom_call_target="tpu_custom_call" | custom-call | flops 184549376 | bytes 1441792 | tf_op jit(solution)/shard_map/exit/pallas_call | solution.py:59
  47.2 1.6 %collective-permute-done.14.refs_9_ = bf16[256,256]{1,0:T(8,128)(2,1)S(1)} collective-permute-done((bf16[256,256]{1,0:T(8,128)(2,1)S(1)}, bf16[256,256]{1,0:T(8,128)(2,1)S(1)}, u32[]{:S(2)}, u32[]{:S(2)}) %collective-permute-start.14) | collective-permute-done | bytes 131104 | tf_op jit(solution)/shard_map/ppermute | solution.py:32
  50.2 3.0 %collective-permute-start.15 = (bf16[384,256]{1,0:T(8,128)(2,1)S(1)}, bf16[384,256]{1,0:T(8,128)(2,1)S(1)}, u32[]{:S(2)}, u32[]{:S(2)}) collective-permute-start(bf16[384,256]{1,0:T(8,128)(2,1)S(1)} %get-tuple-element.52.refs_9_), channel_id=1, source_target_pairs={{0,4},{1,5},{2,6},{3,7},{4,0},{5,1},{6,2},{7,3},{8,12},{9,13},{10,... | collective-permute-start | bytes 589832 | tf_op jit(solution)/shard_map/ppermute | solution.py:26
  54.6 2.2 %collective-permute-start.18 = (bf16[128,256]{1,0:T(8,128)(2,1)S(1)}, bf16[128,256]{1,0:T(8,128)(2,1)S(1)}, u32[]{:S(2)}, u32[]{:S(2)}) collective-permute-start(bf16[128,256]{1,0:T(8,128)(2,1)S(1)} %get-tuple-element.55), channel_id=1, source_target_pairs={{0,3},{1,2},{2,1},{3,0},{4,7},{5,6},{6,5},{7,4},{8,11},{9,10},{10,... | collective-permute-start | bytes 196616 | tf_op jit(solution)/shard_map/ppermute | solution.py:26
  56.9 5.0 %collective-permute-done.15.refs_1_.refs_10_ = bf16[384,256]{1,0:T(8,128)(2,1)S(1)} collective-permute-done((bf16[384,256]{1,0:T(8,128)(2,1)S(1)}, bf16[384,256]{1,0:T(8,128)(2,1)S(1)}, u32[]{:S(2)}, u32[]{:S(2)}) %collective-permute-start.15) | collective-permute-done | bytes 196640 | tf_op jit(solution)/shard_map/ppermute | solution.py:26
  63.8 2.2 %collective-permute-start.21 = (bf16[160,256]{1,0:T(8,128)(2,1)S(1)}, bf16[160,256]{1,0:T(8,128)(2,1)S(1)}, u32[]{:S(2)}, u32[]{:S(2)}) collective-permute-start(bf16[160,256]{1,0:T(8,128)(2,1)S(1)} %get-tuple-element.59), channel_id=1, source_target_pairs={{0,3},{1,2},{2,1},{3,0},{4,7},{5,6},{6,5},{7,4},{8,11},{9,10},{10,... | collective-permute-start | bytes 245768 | tf_op jit(solution)/shard_map/ppermute | solution.py:26
  67.6 1.5 %collective-permute-done.20.refs_15_ = bf16[160,256]{1,0:T(8,128)(2,1)S(1)} collective-permute-done((bf16[160,256]{1,0:T(8,128)(2,1)S(1)}, bf16[160,256]{1,0:T(8,128)(2,1)S(1)}, u32[]{:S(2)}, u32[]{:S(2)}) %collective-permute-start.20) | collective-permute-done | bytes 81952 | tf_op jit(solution)/shard_map/ppermute | solution.py:26
  69.1 1.9 %collective-permute-done.21.refs_16_ = bf16[160,256]{1,0:T(8,128)(2,1)S(1)} collective-permute-done((bf16[160,256]{1,0:T(8,128)(2,1)S(1)}, bf16[160,256]{1,0:T(8,128)(2,1)S(1)}, u32[]{:S(2)}, u32[]{:S(2)}) %collective-permute-start.21) | collective-permute-done | bytes 81952 | tf_op jit(solution)/shard_map/ppermute | solution.py:26
  71.1 1.9 %middle.3 = (bf16[384,256]{1,0:T(8,128)(2,1)S(1)}, bf16[128,256]{1,0:T(8,128)(2,1)S(1)}, bf16[128,256]{1,0:T(8,128)(2,1)S(1)}, bf16[128,256]{1,0:T(8,128)(2,1)S(...) custom-call(s32[1]{0:T(128)} %bitcast.refs_0_, s32[1]{0:T(128)} %bitcast.2.refs_1_, ...), custom_call_target="tpu_custom_call" | custom-call | flops 184549376 | bytes 1441792 | tf_op jit(solution)/shard_map/middle/pallas_call | solution.py:59
  73.0 1.6 %collective-permute-start.22 = (bf16[384,256]{1,0:T(8,128)(2,1)S(1)}, bf16[384,256]{1,0:T(8,128)(2,1)S(1)}, u32[]{:S(2)}, u32[]{:S(2)}) collective-permute-start(bf16[384,256]{1,0:T(8,128)(2,1)S(1)} %get-tuple-element.62.refs_3_), channel_id=1, source_target_pairs={{0,4},{1,5},{2,6},{3,7},{4,0},{5,1},{6,2},{7,3},{8,12},{9,13},{10,... | collective-permute-start | bytes 589832 | tf_op jit(solution)/shard_map/ppermute | solution.py:26
  78.1 7.0 %collective-permute-done.22.refs_1_.refs_4_ = bf16[384,256]{1,0:T(8,128)(2,1)S(1)} collective-permute-done((bf16[384,256]{1,0:T(8,128)(2,1)S(1)}, bf16[384,256]{1,0:T(8,128)(2,1)S(1)}, u32[]{:S(2)}, u32[]{:S(2)}) %collective-permute-start.22) | collective-permute-done | bytes 196640 | tf_op jit(solution)/shard_map/ppermute | solution.py:26
  86.7 2.5 %collective-permute-start.28 = (bf16[160,256]{1,0:T(8,128)(2,1)S(1)}, bf16[160,256]{1,0:T(8,128)(2,1)S(1)}, u32[]{:S(2)}, u32[]{:S(2)}) collective-permute-start(bf16[160,256]{1,0:T(8,128)(2,1)S(1)} %get-tuple-element.69), channel_id=1, source_target_pairs={{0,3},{1,2},{2,1},{3,0},{4,7},{5,6},{6,5},{7,4},{8,11},{9,10},{10,... | collective-permute-start | bytes 245768 | tf_op jit(solution)/shard_map/ppermute | solution.py:26
  93.0 1.6 %exit.3 = (bf16[2,1,256,256]{3,2,1,0:T(8,128)(2,1)}, bf16[2,32,256]{2,1,0:T(8,128)(2,1)S(1)}) custom-call(s32[1]{0:T(128)} %bitcast.refs_0_, s32[1,16]{1,0:T(1,128)S(1)} %reshape.82.refs_4_.refs_1_, bf16[256,1152]{1,0:T(8,128)(2,1)S(1)} %copy-done.3, bf16[384,256]{1,0:T(8,128)(2,1)S(1)} %get-tuple-element.62.refs_3_, ...), custom_call_target="tpu_custom_call", output_to_operand_aliasing={{0}: (11, {})} | custom-call | flops 184549376 | bytes 1441792 | tf_op jit(solution)/shard_map/exit/pallas_call | solution.py:59
  94.5 1.9 %collective-permute-start.32 = (bf16[2,32,256]{2,1,0:T(8,128)(2,1)S(1)}, bf16[2,32,256]{2,1,0:T(8,128)(2,1)S(1)}, u32[]{:S(2)}, u32[]{:S(2)}) collective-permute-start(bf16[2,32,256]{2,1,0:T(8,128)(2,1)S(1)} %get-tuple-element.74.refs_1_), channel_id=1, source_target_pairs={{0,4},{1,5},{2,6},{3,7},{4,0},{5,1},{6,2},{7,3},{8,12},{9,13},{10,... | collective-permute-start | bytes 98312 | tf_op jit(solution)/shard_map/ppermute | solution.py:26
  104.9 2.0 %collective-permute-done.35.refs_8_ = bf16[2,32,256]{2,1,0:T(8,128)(2,1)S(1)} collective-permute-done((bf16[2,32,256]{2,1,0:T(8,128)(2,1)S(1)}, bf16[2,32,256]{2,1,0:T(8,128)(2,1)S(1)}, u32[]{:S(2)}, u32[]{:S(2)}) %collective-permute-start.35) | collective-permute-done | bytes 32800 | tf_op jit(solution)/shard_map/ppermute | solution.py:26
  (86 shorter events, 43.2 us)
Async XLA Ops:
  2.3 12.5 %collective-permute-start.3 = (bf16[256,256]{1,0:T(8,128)(2,1)S(1)}, bf16[256,256]{1,0:T(8,128)(2,1)S(1)}, u32[]{:S(2)}, u32[]{:S(2)}) collective-permute-start(bf16[256,256]{1,0:T(8,128)(2,1)S(1)} %fusion.3.refs_5_.refs_9_), channel_id=1, source_target_pairs={{0,4},{1,5},{2,6},{3,7},{4,0},{5,1},{6,2},{7,3},{8,12},{9,13},{10,... | collective-permute-start | bytes 393224 | tf_op jit(solution)/shard_map/ppermute | solution.py:26
  15.3 10.3 %collective-permute-start.4 = (bf16[256,256]{1,0:T(8,128)(2,1)S(1)}, bf16[256,256]{1,0:T(8,128)(2,1)S(1)}, u32[]{:S(2)}, u32[]{:S(2)}) collective-permute-start(bf16[256,256]{1,0:T(8,128)(2,1)S(1)} %get-tuple-element.41), channel_id=1, source_target_pairs={{0,1},{1,0},{2,3},{3,2},{4,5},{5,4},{6,7},{7,6},{8,9},{9,8},{10,11... | collective-permute-start | bytes 393224 | tf_op jit(solution)/shard_map/ppermute | solution.py:26
  16.0 9.7 %collective-permute-start.5 = (bf16[256,256]{1,0:T(8,128)(2,1)S(1)}, bf16[256,256]{1,0:T(8,128)(2,1)S(1)}, u32[]{:S(2)}, u32[]{:S(2)}) collective-permute-start(bf16[256,256]{1,0:T(8,128)(2,1)S(1)} %get-tuple-element.42), channel_id=1, source_target_pairs={{0,2},{1,3},{2,0},{3,1},{4,6},{5,7},{6,4},{7,5},{8,10},{9,11},{10,... | collective-permute-start | bytes 393224 | tf_op jit(solution)/shard_map/ppermute | solution.py:26
  16.4 9.2 %collective-permute-start.6 = (bf16[256,256]{1,0:T(8,128)(2,1)S(1)}, bf16[256,256]{1,0:T(8,128)(2,1)S(1)}, u32[]{:S(2)}, u32[]{:S(2)}) collective-permute-start(bf16[256,256]{1,0:T(8,128)(2,1)S(1)} %get-tuple-element.43), channel_id=1, source_target_pairs={{0,3},{1,2},{2,1},{3,0},{4,7},{5,6},{6,5},{7,4},{8,11},{9,10},{10,... | collective-permute-start | bytes 393224 | tf_op jit(solution)/shard_map/ppermute | solution.py:26
  28.4 7.4 %collective-permute-start.7 = (bf16[256,256]{1,0:T(8,128)(2,1)S(1)}, bf16[256,256]{1,0:T(8,128)(2,1)S(1)}, u32[]{:S(2)}, u32[]{:S(2)}) collective-permute-start(bf16[256,256]{1,0:T(8,128)(2,1)S(1)} %get-tuple-element.44.refs_3_), channel_id=1, source_target_pairs={{0,4},{1,5},{2,6},{3,7},{4,0},{5,1},{6,2},{7,3},{8,12},{9,13},{10,... | collective-permute-start | bytes 393224 | tf_op jit(solution)/shard_map/ppermute | solution.py:26
  29.0 8.5 %collective-permute-start.10 = (bf16[128,256]{1,0:T(8,128)(2,1)S(1)}, bf16[128,256]{1,0:T(8,128)(2,1)S(1)}, u32[]{:S(2)}, u32[]{:S(2)}) collective-permute-start(bf16[128,256]{1,0:T(8,128)(2,1)S(1)} %get-tuple-element.47), channel_id=1, source_target_pairs={{0,3},{1,2},{2,1},{3,0},{4,7},{5,6},{6,5},{7,4},{8,11},{9,10},{10,... | collective-permute-start | bytes 196616 | tf_op jit(solution)/shard_map/ppermute | solution.py:26
  31.5 8.4 %collective-permute-start.8 = (bf16[128,256]{1,0:T(8,128)(2,1)S(1)}, bf16[128,256]{1,0:T(8,128)(2,1)S(1)}, u32[]{:S(2)}, u32[]{:S(2)}) collective-permute-start(bf16[128,256]{1,0:T(8,128)(2,1)S(1)} %get-tuple-element.45), channel_id=1, source_target_pairs={{0,1},{1,0},{2,3},{3,2},{4,5},{5,4},{6,7},{7,6},{8,9},{9,8},{10,11... | collective-permute-start | bytes 196616 | tf_op jit(solution)/shard_map/ppermute | solution.py:26
  31.7 8.2 %collective-permute-start.9 = (bf16[128,256]{1,0:T(8,128)(2,1)S(1)}, bf16[128,256]{1,0:T(8,128)(2,1)S(1)}, u32[]{:S(2)}, u32[]{:S(2)}) collective-permute-start(bf16[128,256]{1,0:T(8,128)(2,1)S(1)} %get-tuple-element.46), channel_id=1, source_target_pairs={{0,2},{1,3},{2,0},{3,1},{4,6},{5,7},{6,4},{7,5},{8,10},{9,11},{10,... | collective-permute-start | bytes 196616 | tf_op jit(solution)/shard_map/ppermute | solution.py:26
  37.6 5.4 %collective-permute-start.13 = (bf16[128,256]{1,0:T(8,128)(2,1)S(1)}, bf16[128,256]{1,0:T(8,128)(2,1)S(1)}, u32[]{:S(2)}, u32[]{:S(2)}) collective-permute-start(bf16[128,256]{1,0:T(8,128)(2,1)S(1)} %get-tuple-element.50), channel_id=1, source_target_pairs={{0,3},{1,2},{2,1},{3,0},{4,7},{5,6},{6,5},{7,4},{8,11},{9,10},{10,... | collective-permute-start | bytes 196616 | tf_op jit(solution)/shard_map/ppermute | solution.py:26
  50.2 11.7 %collective-permute-start.15 = (bf16[384,256]{1,0:T(8,128)(2,1)S(1)}, bf16[384,256]{1,0:T(8,128)(2,1)S(1)}, u32[]{:S(2)}, u32[]{:S(2)}) collective-permute-start(bf16[384,256]{1,0:T(8,128)(2,1)S(1)} %get-tuple-element.52.refs_9_), channel_id=1, source_target_pairs={{0,4},{1,5},{2,6},{3,7},{4,0},{5,1},{6,2},{7,3},{8,12},{9,13},{10,... | collective-permute-start | bytes 589832 | tf_op jit(solution)/shard_map/ppermute | solution.py:26
  53.2 10.6 %collective-permute-start.16 = (bf16[128,256]{1,0:T(8,128)(2,1)S(1)}, bf16[128,256]{1,0:T(8,128)(2,1)S(1)}, u32[]{:S(2)}, u32[]{:S(2)}) collective-permute-start(bf16[128,256]{1,0:T(8,128)(2,1)S(1)} %get-tuple-element.53), channel_id=1, source_target_pairs={{0,1},{1,0},{2,3},{3,2},{4,5},{5,4},{6,7},{7,6},{8,9},{9,8},{10,11... | collective-permute-start | bytes 196616 | tf_op jit(solution)/shard_map/ppermute | solution.py:26
  54.3 12.0 %collective-permute-start.17 = (bf16[128,256]{1,0:T(8,128)(2,1)S(1)}, bf16[128,256]{1,0:T(8,128)(2,1)S(1)}, u32[]{:S(2)}, u32[]{:S(2)}) collective-permute-start(bf16[128,256]{1,0:T(8,128)(2,1)S(1)} %get-tuple-element.54), channel_id=1, source_target_pairs={{0,2},{1,3},{2,0},{3,1},{4,6},{5,7},{6,4},{7,5},{8,10},{9,11},{10,... | collective-permute-start | bytes 196616 | tf_op jit(solution)/shard_map/ppermute | solution.py:26
  54.6 11.6 %collective-permute-start.18 = (bf16[128,256]{1,0:T(8,128)(2,1)S(1)}, bf16[128,256]{1,0:T(8,128)(2,1)S(1)}, u32[]{:S(2)}, u32[]{:S(2)}) collective-permute-start(bf16[128,256]{1,0:T(8,128)(2,1)S(1)} %get-tuple-element.55), channel_id=1, source_target_pairs={{0,3},{1,2},{2,1},{3,0},{4,7},{5,6},{6,5},{7,4},{8,11},{9,10},{10,... | collective-permute-start | bytes 196616 | tf_op jit(solution)/shard_map/ppermute | solution.py:26
  63.8 5.3 %collective-permute-start.20 = (bf16[160,256]{1,0:T(8,128)(2,1)S(1)}, bf16[160,256]{1,0:T(8,128)(2,1)S(1)}, u32[]{:S(2)}, u32[]{:S(2)}) collective-permute-start(bf16[160,256]{1,0:T(8,128)(2,1)S(1)} %get-tuple-element.58), channel_id=1, source_target_pairs={{0,2},{1,3},{2,0},{3,1},{4,6},{5,7},{6,4},{7,5},{8,10},{9,11},{10,... | collective-permute-start | bytes 245768 | tf_op jit(solution)/shard_map/ppermute | solution.py:26
  63.8 7.2 %collective-permute-start.21 = (bf16[160,256]{1,0:T(8,128)(2,1)S(1)}, bf16[160,256]{1,0:T(8,128)(2,1)S(1)}, u32[]{:S(2)}, u32[]{:S(2)}) collective-permute-start(bf16[160,256]{1,0:T(8,128)(2,1)S(1)} %get-tuple-element.59), channel_id=1, source_target_pairs={{0,3},{1,2},{2,1},{3,0},{4,7},{5,6},{6,5},{7,4},{8,11},{9,10},{10,... | collective-permute-start | bytes 245768 | tf_op jit(solution)/shard_map/ppermute | solution.py:26
  73.0 12.0 %collective-permute-start.22 = (bf16[384,256]{1,0:T(8,128)(2,1)S(1)}, bf16[384,256]{1,0:T(8,128)(2,1)S(1)}, u32[]{:S(2)}, u32[]{:S(2)}) collective-permute-start(bf16[384,256]{1,0:T(8,128)(2,1)S(1)} %get-tuple-element.62.refs_3_), channel_id=1, source_target_pairs={{0,4},{1,5},{2,6},{3,7},{4,0},{5,1},{6,2},{7,3},{8,12},{9,13},{10,... | collective-permute-start | bytes 589832 | tf_op jit(solution)/shard_map/ppermute | solution.py:26
  74.6 12.1 %collective-permute-start.23 = (bf16[128,256]{1,0:T(8,128)(2,1)S(1)}, bf16[128,256]{1,0:T(8,128)(2,1)S(1)}, u32[]{:S(2)}, u32[]{:S(2)}) collective-permute-start(bf16[128,256]{1,0:T(8,128)(2,1)S(1)} %get-tuple-element.63), channel_id=1, source_target_pairs={{0,1},{1,0},{2,3},{3,2},{4,5},{5,4},{6,7},{7,6},{8,9},{9,8},{10,11... | collective-permute-start | bytes 196616 | tf_op jit(solution)/shard_map/ppermute | solution.py:26
  75.7 13.5 %collective-permute-start.24 = (bf16[128,256]{1,0:T(8,128)(2,1)S(1)}, bf16[128,256]{1,0:T(8,128)(2,1)S(1)}, u32[]{:S(2)}, u32[]{:S(2)}) collective-permute-start(bf16[128,256]{1,0:T(8,128)(2,1)S(1)} %get-tuple-element.64), channel_id=1, source_target_pairs={{0,2},{1,3},{2,0},{3,1},{4,6},{5,7},{6,4},{7,5},{8,10},{9,11},{10,... | collective-permute-start | bytes 196616 | tf_op jit(solution)/shard_map/ppermute | solution.py:26
  77.2 12.1 %collective-permute-start.25 = (bf16[128,256]{1,0:T(8,128)(2,1)S(1)}, bf16[128,256]{1,0:T(8,128)(2,1)S(1)}, u32[]{:S(2)}, u32[]{:S(2)}) collective-permute-start(bf16[128,256]{1,0:T(8,128)(2,1)S(1)} %get-tuple-element.65), channel_id=1, source_target_pairs={{0,3},{1,2},{2,1},{3,0},{4,7},{5,6},{6,5},{7,4},{8,11},{9,10},{10,... | collective-permute-start | bytes 196616 | tf_op jit(solution)/shard_map/ppermute | solution.py:26
  86.7 6.2 %collective-permute-start.28 = (bf16[160,256]{1,0:T(8,128)(2,1)S(1)}, bf16[160,256]{1,0:T(8,128)(2,1)S(1)}, u32[]{:S(2)}, u32[]{:S(2)}) collective-permute-start(bf16[160,256]{1,0:T(8,128)(2,1)S(1)} %get-tuple-element.69), channel_id=1, source_target_pairs={{0,3},{1,2},{2,1},{3,0},{4,7},{5,6},{6,5},{7,4},{8,11},{9,10},{10,... | collective-permute-start | bytes 245768 | tf_op jit(solution)/shard_map/ppermute | solution.py:26
  94.5 5.5 %collective-permute-start.32 = (bf16[2,32,256]{2,1,0:T(8,128)(2,1)S(1)}, bf16[2,32,256]{2,1,0:T(8,128)(2,1)S(1)}, u32[]{:S(2)}, u32[]{:S(2)}) collective-permute-start(bf16[2,32,256]{2,1,0:T(8,128)(2,1)S(1)} %get-tuple-element.74.refs_1_), channel_id=1, source_target_pairs={{0,4},{1,5},{2,6},{3,7},{4,0},{5,1},{6,2},{7,3},{8,12},{9,13},{10,... | collective-permute-start | bytes 98312 | tf_op jit(solution)/shard_map/ppermute | solution.py:26
  96.5 5.6 %collective-permute-start.29 = (bf16[2,32,256]{2,1,0:T(8,128)(2,1)S(1)}, bf16[2,32,256]{2,1,0:T(8,128)(2,1)S(1)}, u32[]{:S(2)}, u32[]{:S(2)}) collective-permute-start(bf16[2,32,256]{2,1,0:T(8,128)(2,1)S(1)} %get-tuple-element.74.refs_1_), channel_id=1, source_target_pairs={{0,1},{1,0},{2,3},{3,2},{4,5},{5,4},{6,7},{7,6},{8,9},{9,8},{10,11... | collective-permute-start | bytes 98312 | tf_op jit(solution)/shard_map/ppermute | solution.py:26
  97.4 7.0 %collective-permute-start.30 = (bf16[2,32,256]{2,1,0:T(8,128)(2,1)S(1)}, bf16[2,32,256]{2,1,0:T(8,128)(2,1)S(1)}, u32[]{:S(2)}, u32[]{:S(2)}) collective-permute-start(bf16[2,32,256]{2,1,0:T(8,128)(2,1)S(1)} %get-tuple-element.74.refs_1_), channel_id=1, source_target_pairs={{0,2},{1,3},{2,0},{3,1},{4,6},{5,7},{6,4},{7,5},{8,10},{9,11},{10,... | collective-permute-start | bytes 98312 | tf_op jit(solution)/shard_map/ppermute | solution.py:26
  98.5 5.8 %collective-permute-start.31 = (bf16[2,32,256]{2,1,0:T(8,128)(2,1)S(1)}, bf16[2,32,256]{2,1,0:T(8,128)(2,1)S(1)}, u32[]{:S(2)}, u32[]{:S(2)}) collective-permute-start(bf16[2,32,256]{2,1,0:T(8,128)(2,1)S(1)} %get-tuple-element.74.refs_1_), channel_id=1, source_target_pairs={{0,3},{1,2},{2,1},{3,0},{4,7},{5,6},{6,5},{7,4},{8,11},{9,10},{10,... | collective-permute-start | bytes 98312 | tf_op jit(solution)/shard_map/ppermute | solution.py:26
  (20 other events, 289.4 us)

commit v5 on v4

v5 whole, which is shorter than its diff:
```python
import functools

import jax
import jax.numpy as jnp
from jax import lax
from jax.experimental import pallas as pl
from jax.experimental.pallas import tpu as pltpu
from jax.sharding import PartitionSpec as P

ALPHA = 0.1
BETA_SCALE = 0.5
VMEM = pl.BlockSpec(memory_space=pltpu.VMEM)
SMEM = pl.BlockSpec(memory_space=pltpu.SMEM)
HBM = pl.BlockSpec(memory_space=pltpu.HBM)
PARAMS = pltpu.CompilerParams(vmem_limit_bytes=24 * 2**20)
F32 = jnp.float32
BF16 = jnp.bfloat16


def cost(flops, nbytes):
    return pl.CostEstimate(flops=flops, bytes_accessed=nbytes, transcendentals=0)


def swapped(block, k):
    n = lax.axis_size("rows")
    return lax.ppermute(block, "rows", [(i, i ^ k) for i in range(n)])


def passed_along(block, axis, distance):
    devices = range(lax.axis_size(axis))
    route = [(i - distance, i) for i in devices if i - distance in devices]
    return lax.ppermute(block, axis, route)


class Refs:
    def __init__(self, refs):
        self.refs = list(refs)

    def take(self, count=None):
        many = 1 if count is None else count
        taken, self.refs = self.refs[:many], self.refs[many:]
        return taken[0] if count is None else taken


class Call:
    def __init__(self):
        self.operands, self.specs, self.outs, self.out_specs, self.scratch = [], [], [], [], []
        self.aliases = {}

    def give(self, spec, *arrays):
        self.operands += arrays
        self.specs += [spec] * len(arrays)

    def want(self, spec, shape, dtype, count=1):
        self.outs += [jax.ShapeDtypeStruct(shape, dtype)] * count
        self.out_specs += [spec] * count

    def run(self, kernel, name, estimate, params=PARAMS):
        return pl.pallas_call(
            kernel,
            out_shape=self.outs,
            in_specs=self.specs,
            out_specs=self.out_specs,
            scratch_shapes=self.scratch,
            input_output_aliases=self.aliases,
            compiler_params=params,
            cost_estimate=estimate,
            name=name,
        )(*self.operands)


def densify_kernel(tick, row_tiles, n, chunks, *refs):
    me_ref, rows_ref, cols_ref, count_ref, vals_ref, out_ref, vals, acc, sems = refs
    entries, tile = vals.shape[:2]
    chunk = entries // chunks
    me = me_ref[0]
    copies = []
    for c in range(chunks):
        part = pl.ds(c * chunk, chunk)
        copies.append(
            pltpu.make_async_copy(vals_ref.at[0, tick, part], vals.at[part], sems.at[c])
        )
        copies[c].start()
    acc[...] = jnp.zeros_like(acc)

    def add(e, carry):
        owner = lax.div(cols_ref[0, tick, e], row_tiles)
        block = lax.rem(cols_ref[0, tick, e], row_tiles)
        slot = jnp.bitwise_xor(owner, me)
        slot = jnp.where((owner == me) & (block > 0), n - 1 + block, slot)
        rows = pl.ds(pl.multiple_of(rows_ref[0, tick, e] * tile, tile), tile)
        cols = pl.ds(pl.multiple_of(slot * tile, tile), tile)
        acc[rows, cols] += vals[e].astype(F32)
        return carry

    for c in range(chunks):
        copies[c].wait()
        stop = jnp.clip(count_ref[0, tick], c * chunk, (c + 1) * chunk)
        lax.fori_loop(c * chunk, stop, add, 0)
    out_ref[...] = acc[...].astype(BF16)


def densify(tick, me, rows, cols, count, vals, row_tiles, n):
    entries, tile = vals.shape[2:4]
    chunks = 4 if entries % 4 == 0 else 1
    shape = (row_tiles * tile, (n + row_tiles - 1) * tile)
    call = Call()
    call.give(SMEM, me, rows, cols, count)
    call.give(HBM, vals)
    call.want(VMEM, shape, BF16)
    call.scratch = [
        pltpu.VMEM(vals.shape[2:], BF16),
        pltpu.VMEM(shape, F32),
        pltpu.SemaphoreType.DMA((chunks,)),
    ]
    (adj,) = call.run(
        functools.partial(densify_kernel, tick, row_tiles, n, chunks),
        "densify",
        cost(entries * tile * tile * 20, entries * tile * tile * 2),
        pltpu.CompilerParams(vmem_limit_bytes=50 * 2**20),
    )
    return adj


def tile_at(ref, index, tile):
    return ref[pl.ds(pl.multiple_of(index * tile, tile), tile), :]


def take_got(refs, n):
    far, near, relayed = refs.take(), refs.take(n // 2 - 1), refs.take(n // 2 - 1)
    return far, near, relayed


def spread_of(adj_ref, own_ref, got, pick_ref, me, c):
    n, tile = c["n"], c["tile"]
    far, near, relayed = got

    def named(ref, k):
        index = pick_ref[0, c["tick"] * n + jnp.bitwise_xor(me, k)]
        return tile_at(ref, index, tile)

    if c["whole"]:
        near = [named(ref, k) for k, ref in enumerate(near, 1)]
        relayed = [named(ref, n // 2 + k) for k, ref in enumerate(relayed, 1)]
    else:
        near = [ref[:tile, :] for ref in near]
        relayed = [ref[...] for ref in relayed]
    blocks = jnp.concatenate(
        [own_ref[:tile, :]] + near + [named(far, n // 2)] + relayed + [own_ref[tile:, :]], axis=0
    )
    total = jnp.dot(adj_ref[...], blocks, preferred_element_type=F32)
    return ((1.0 - ALPHA) * total).astype(BF16)


def chunk_total(mine_ref, far_ref):
    return (mine_ref[...].astype(F32) + far_ref[...].astype(F32)).astype(BF16)


def layer_kernel(c, *refs):
    refs = Refs(refs)
    n, tile, width, chunk = c["n"], c["tile"], c["width"], c["chunk"]
    h = n // 2
    me_ref, section_ref, preact_all, weight_all = refs.take(4)
    picks = refs.take(h)
    if c["entry"]:
        last_ref, passed_ref = refs.take(2)
    else:
        adj_ref, own_ref = refs.take(2)
        got = take_got(refs, n)
    if c["final"]:
        support_all, acc_ref = refs.take(2)
    if c["sum_above"]:
        above_mine, above_far = refs.take(2)
    image_ref = refs.take()
    sends = refs.take(h - 1)
    out_ref = refs.take()
    if c["sum_above"]:
        above_ref = refs.take()
    preact_ref, weight_ref, load_sems = refs.take(3)

    me = me_ref[0]
    section = section_ref[0]
    loads = [
        (preact_all.at[0, c["tick"], c["layer"]], preact_ref),
        (weight_all.at[0, c["layer"]], weight_ref),
    ]
    if c["final"]:
        support_ref, term_ref = refs.take(2)
        loads.append((support_all.at[0, c["tick"], c["layer"]], support_ref))
    loads = [pltpu.make_async_copy(a, b, load_sems.at[i]) for i, (a, b) in enumerate(loads)]
    for load in loads:
        load.start()
    step = (c["layers"] * section + c["layer"] + 1).astype(F32)
    beta = jnp.log(BETA_SCALE / jnp.full((1, width), step, F32) + 1.0)
    if not c["entry"]:
        grad = spread_of(adj_ref, own_ref, got, picks[0], me, c)
    for load in loads:
        load.wait()
    if c["entry"]:
        grad = jnp.where(section == c["sections"] - 1, last_ref[...], passed_ref[...])

    masked = jnp.where(preact_ref[...] > 0, grad, jnp.zeros_like(grad))
    product = lax.dot_general(
        masked, weight_ref[...], (((1,), (1,)), ((), ())), preferred_element_type=F32
    )
    image = ((1.0 - beta) * masked.astype(F32) + beta * product).astype(BF16)
    image_ref[...] = image
    for k in range(1, h):
        sends[k - 1][:tile, :] = tile_at(image_ref, picks[k][0, c["tick"] * n + me], tile)
    if c["final"]:
        term = lax.dot_general(
            support_ref[...], masked, (((0,), (0,)), ((), ())), preferred_element_type=F32
        )
        term_ref[...] = acc_ref[...] + beta * term
        place = lax.rem(me, h)
        for k in range(1, h):
            sends[k - 1][tile : tile + chunk, :] = tile_at(
                term_ref, jnp.bitwise_xor(place, k), chunk
            ).astype(BF16)
        out_ref[...] = tile_at(term_ref, place, chunk)
    else:
        out_ref[...] = masked
    if c["sum_above"]:
        above_ref[...] = chunk_total(above_mine, above_far)
        for send in sends:
            send[tile + chunk :, :] = above_ref[...]


def relay_kernel(c, *refs):
    refs = Refs(refs)
    n, tile, chunk = c["n"], c["tile"], c["chunk"]
    h = n // 2
    me_ref, far_ref = refs.take(2)
    picks = refs.take(h - 1)
    if c["final"]:
        kept_ref, near = refs.take(), refs.take(h - 1)
    sends = refs.take(h - 1)
    me = me_ref[0]
    for k in range(1, h):
        index = picks[k - 1][0, c["tick"] * n + jnp.bitwise_xor(me, h)]
        sends[k - 1][...] = tile_at(far_ref, index, tile)
    if c["final"]:
        total = kept_ref[...]
        for ref in near:
            total = total + ref[tile : tile + chunk, :].astype(F32)
        refs.take()[...] = total.astype(BF16)


def exit_kernel(c, *refs):
    refs = Refs(refs)
    me_ref, pick_ref, adj_ref, own_ref = refs.take(4)
    got = take_got(refs, c["n"])
    if not c["final"]:
        refs.take()[...] = spread_of(adj_ref, own_ref, got, pick_ref, me_ref[0], c)
        return
    handed = refs.take(c["tick"])
    mine_ref, far_ref = refs.take(2)
    out_ref, sum_ref, hold_ref, sems = refs.take(4)
    copies = [
        pltpu.make_async_copy(ref, out_ref.at[t, 0], sems.at[t])
        for t, ref in enumerate(handed + [hold_ref])
    ]
    for copy in copies[:-1]:
        copy.start()
    sum_ref[...] = chunk_total(mine_ref, far_ref)
    hold_ref[...] = spread_of(adj_ref, own_ref, got, pick_ref, me_ref[0], c)
    copies[-1].start()
    for copy in copies:
        copy.wait()


def finish_kernel(h, layers, chunk, tile, *refs):
    refs = Refs(refs)
    me_ref = refs.take()
    sums = [refs.take(h) for layer in range(layers)]
    out_ref, hold_ref, sems = refs.take(3)
    place = lax.rem(me_ref[0], h)
    copies = []
    for layer in range(layers):
        for k in range(h):
            skip = tile + chunk if layer > 0 and k > 0 else 0
            start = pl.multiple_of(jnp.bitwise_xor(place, k) * chunk, chunk)
            hold_ref[layer, pl.ds(start, chunk), :] = sums[layer][k][skip:, :].astype(F32)
        copy = pltpu.make_async_copy(hold_ref.at[layer], out_ref.at[0, layer], sems.at[layer])
        copy.start()
        copies.append(copy)
    for copy in copies:
        copy.wait()


def shards(grad_in, grad_last, support, preact, weights, tile_vals, tile_row, tile_col, tile_count):
    section = lax.axis_index("section")
    me = lax.axis_index("rows")
    n = lax.axis_size("rows")
    h = n // 2
    sections = lax.axis_size("section")
    ticks = support.shape[1]
    layers = support.shape[2]
    rows, width = grad_last.shape
    tile = tile_vals.shape[-1]
    row_tiles = rows // tile
    chunk = width // h
    me_arr = me.astype(jnp.int32).reshape(1)
    section_arr = section.astype(jnp.int32).reshape(1)
    counts = tile_count.reshape(1, ticks)

    owner = tile_col[0] // row_tiles
    named = jnp.where(
        owner[:, :, None] == jnp.arange(n)[None, None, :], (tile_col[0] % row_tiles)[:, :, None], 0
    )
    pick = jnp.max(named, axis=1).reshape(1, ticks * n).astype(jnp.int32)
    picks = [pick] + [swapped(pick, k) for k in range(1, h)]

    handed = []
    passed = None
    weight_acc = [None] * layers
    weight_sums = [None] * layers
    initial = []
    base = dict(n=n, tile=tile, width=width, layers=layers, sections=sections, chunk=chunk)
    layer_cost = cost(2 * rows * width * (width + (n + 1) * tile), (6 + 2 * n) * rows * width)
    small_cost = cost(rows * width, 2 * n * rows * width)
    for tick in range(ticks):
        final = tick == ticks - 1
        if tick > 0:
            passed = passed_along(handed[-1], "section", -1)
        adj = densify(tick, me_arr, tile_row, tile_col, counts, tile_vals, row_tiles, n)
        image = got = whole = mine = None
        toward = 0.0
        for layer in reversed(range(layers)):
            entry = layer == layers - 1
            beta = jnp.log(BETA_SCALE / (layers * section + layer + 1).astype(F32) + 1.0)
            c = dict(
                base, layer=layer, tick=tick, entry=entry, final=final,
                sum_above=final and not entry, whole=whole,
            )
            if tick == 0 and entry:
                masked = jnp.where(
                    preact[0, tick, layer] > 0, grad_in[0], jnp.zeros_like(grad_in[0])
                )
                product = jnp.dot(masked, weights[0, layer].T, preferred_element_type=F32)
                image = ((1.0 - beta) * masked.astype(F32) + beta * product).astype(BF16)
                far = swapped(image, h)
                near = [swapped(image, k) for k in range(1, h)]
                got = [far, *near, *(swapped(far, k) for k in range(1, h))]
            else:
                call = Call()
                call.give(SMEM, me_arr, section_arr)
                call.give(HBM, preact, weights)
                call.give(SMEM, *picks)
                if entry:
                    call.give(VMEM, grad_last, passed)
                else:
                    call.give(VMEM, adj, image, *got)
                if final:
                    call.give(HBM, support)
                    call.give(VMEM, weight_acc[layer])
                if c["sum_above"]:
                    call.give(VMEM, mine, swapped(mine, h))
                message = tile + chunk * (final + c["sum_above"])
                call.want(VMEM, (rows, width), BF16)
                call.want(VMEM, (message, width), BF16, h - 1)
                if final:
                    call.want(VMEM, (chunk, width), F32)
                else:
                    call.want(VMEM, (rows, width), BF16)
                if c["sum_above"]:
                    call.want(VMEM, (chunk, width), BF16)
                call.scratch = [
                    pltpu.VMEM((rows, width), BF16),
                    pltpu.VMEM((width, width), BF16),
                    pltpu.SemaphoreType.DMA((3,)),
                ]
                if final:
                    call.scratch.append(pltpu.VMEM((rows, width), BF16))
                    call.scratch.append(pltpu.VMEM((width, width), F32))
                results = Refs(
                    call.run(
                        functools.partial(layer_kernel, c), "entry" if entry else "middle", layer_cost
                    )
                )
                image = results.take()
                sends = results.take(h - 1)
                kept = masked = results.take()
                far = swapped(image, h)
                near = [swapped(send, k) for k, send in enumerate(sends, 1)]
                if c["sum_above"]:
                    weight_sums[layer + 1] = [results.take(), *near]
                call = Call()
                call.give(SMEM, me_arr)
                call.give(VMEM, far)
                call.give(SMEM, *picks[1:])
                if final:
                    call.give(VMEM, kept, *near)
                call.want(VMEM, (tile, width), BF16, h - 1)
                if final:
                    call.want(VMEM, (chunk, width), BF16)
                results = Refs(call.run(functools.partial(relay_kernel, c), "relay", small_cost))
                relayed = [swapped(relay, k) for k, relay in enumerate(results.take(h - 1), 1)]
                if final:
                    mine = results.take()
                got = [far, *near, *relayed]
            whole = tick == 0 and entry
            toward = toward + ALPHA * image.astype(F32)
            if not final:
                term = beta * jnp.dot(
                    support[0, tick, layer].T, masked, preferred_element_type=F32
                )
                old = weight_acc[layer]
                weight_acc[layer] = term if old is None else old + term
        initial.append(toward)
        c = dict(base, tick=tick, final=final, whole=whole)
        call = Call()
        call.give(SMEM, me_arr, pick)
        call.give(VMEM, adj, image, *got)
        if final:
            call.give(VMEM, *handed, mine, swapped(mine, h))
            call.want(HBM, (ticks, 1, rows, width), BF16)
            call.want(VMEM, (chunk, width), BF16)
            call.scratch = [pltpu.VMEM((rows, width), BF16), pltpu.SemaphoreType.DMA((ticks,))]
        else:
            call.want(VMEM, (rows, width), BF16)
        results = call.run(functools.partial(exit_kernel, c), "exit", layer_cost)
        if final:
            handoff, last = results
        else:
            handed.append(results[0])
    weight_sums[0] = [last] + [swapped(last, k) for k in range(1, h)]
    call = Call()
    call.give(SMEM, me_arr)
    for sums in weight_sums:
        call.give(VMEM, *sums)
    call.want(HBM, (1, layers, width, width), F32)
    call.scratch = [pltpu.VMEM((layers, width, width), F32), pltpu.SemaphoreType.DMA((layers,))]
    (weight_grad,) = call.run(
        functools.partial(finish_kernel, h, layers, chunk, tile), "finish", small_cost
    )
    return handoff, jnp.stack(initial)[None], weight_grad


def solution(mesh):
    return jax.shard_map(
        shards,
        mesh=mesh,
        in_specs=(
            P("section", "rows", None),
            P("rows", None),
            P("section", None, None, "rows", None),
            P("section", None, None, "rows", None),
            P("section", None, None, None),
            P("section", None, "rows", None, None),
            P("section", None, "rows"),
            P("section", None, "rows"),
            P("section", None, "rows"),
        ),
        out_specs=(
            P(None, "section", "rows", None),
            P("section", None, "rows", None),
            P("section", None, None, None),
        ),
        check_vma=False,
    )
```

time: 108 us -> 100 us (0.926)
  waiting for transfers between devices: 34.8 us -> 28.8 us
  local copies, waits for them, and re-layouts: 3.7 us -> 2.26 us
    ppermute x35 -> x36, waiting for transfers between devices: 33.3 us -> 27.3 us  [swapped(): return lax.ppermute(block, 'rows', [(i, i ^ k) for i in range(n)])]
    unnamed x17 -> x22, local copies, waits for them, and re-layouts: 3.49 us -> 2.05 us
    ppermute x35 -> x36, starting transfers between devices: 46.5 us -> 46.5 us  [swapped(): return lax.ppermute(block, 'rows', [(i, i ^ k) for i in range(n)])]
  transfers between devices with their start and end apart: 36 -> 37, of which waited for: 18 -> 21; matrix products, arithmetic and copies ran while one was open for 3% -> 2% of each run, Pallas kernels for 7% -> 7%
where the time goes in v5:
time: 100 us; the launch traced here: 99.8 us
  starting transfers between devices  47.8 us (48%)
  waiting for transfers between devices  28.8 us (29%)
  Pallas kernels  16.2 us (16%)
  local copies, waits for them, and re-layouts  2.26 us (2%)
  matrix products  1.92 us (2%)
  other arithmetic  1.7 us (2%)
  between operations  1.11 us (1%)
    ppermute x36, starting transfers between devices, swapped(): return lax.ppermute(block, 'rows', [(i, i ^ k) for i in range(n)])  46.5 us
    ppermute x36, waiting for transfers between devices, swapped(): return lax.ppermute(block, 'rows', [(i, i ^ k) for i in range(n)])  27.3 us
    pallas_call x11, Pallas kernels, run(): pl.pallas_call(kernel, out_shape=self.outs, in_specs=self.specs, out_spec...  16.2 us
    unnamed x22, local copies, waits for them, and re-layouts  2.05 us
  transfers between devices with their start and end apart: 37, of which 21 were waited for; matrix products, arithmetic and copies ran while one was open for 2% of the time, Pallas kernels for 7%

profile of v5, /device:TPU:0, one launch (start us, length us, event | category | flops | bytes accessed | tf_op | source)
XLA Modules:
  0.0 99.8 jit_solution(10301003551988696855)
XLA Ops:
  2.2 4.0 %collective-permute-start.6 = (bf16[256,256]{1,0:T(8,128)(2,1)S(1)}, bf16[256,256]{1,0:T(8,128)(2,1)S(1)}, u32[]{:S(2)}, u32[]{:S(2)}) collective-permute-start(bf16[256,256]{1,0:T(8,128)(2,1)S(1)} %fusion.3.refs_9_), channel_id=1, source_target_pairs={{0,3},{1,2},{2,1},{3,0},{4,7},{5,6},{6,5},{7,4},{8,11},{9,10},{10,... | collective-permute-start | bytes 393224 | tf_op jit(solution)/shard_map/ppermute | solution.py:26
  6.3 2.6 %collective-permute-start.3 = (bf16[256,256]{1,0:T(8,128)(2,1)S(1)}, bf16[256,256]{1,0:T(8,128)(2,1)S(1)}, u32[]{:S(2)}, u32[]{:S(2)}) collective-permute-start(bf16[256,256]{1,0:T(8,128)(2,1)S(1)} %fusion.3.refs_9_), channel_id=1, source_target_pairs={{0,4},{1,5},{2,6},{3,7},{4,0},{5,1},{6,2},{7,3},{8,12},{9,13},{10,... | collective-permute-start | bytes 393224 | tf_op jit(solution)/shard_map/ppermute | solution.py:26
  10.2 1.6 %collective-permute-start.1 = (s32[1,16]{1,0:T(1,128)S(1)}, s32[1,16]{1,0:T(1,128)S(1)}, u32[]{:S(2)}, u32[]{:S(2)}) collective-permute-start(s32[1,16]{1,0:T(1,128)S(1)} %reshape.85.refs_4_.refs_1_), channel_id=1, source_target_pairs={{0,2},{1,3},{2,0},{3,1},{4,6},{5,7},{6,4},{7,5},{8,10},{9,11},{10,... | collective-permute-start | bytes 200 | tf_op jit(solution)/shard_map/ppermute | solution.py:26
  11.7 1.5 %collective-permute-start = (s32[1,16]{1,0:T(1,128)S(1)}, s32[1,16]{1,0:T(1,128)S(1)}, u32[]{:S(2)}, u32[]{:S(2)}) collective-permute-start(s32[1,16]{1,0:T(1,128)S(1)} %reshape.85.refs_4_.refs_1_), channel_id=1, source_target_pairs={{0,1},{1,0},{2,3},{3,2},{4,5},{5,4},{6,7},{7,6},{8,9},{9,8},{10,11... | collective-permute-start | bytes 200 | tf_op jit(solution)/shard_map/ppermute | solution.py:26
  15.8 1.9 %collective-permute-start.9 = (bf16[256,256]{1,0:T(8,128)(2,1)S(1)}, bf16[256,256]{1,0:T(8,128)(2,1)S(1)}, u32[]{:S(2)}, u32[]{:S(2)}) collective-permute-start(bf16[256,256]{1,0:T(8,128)(2,1)S(1)} %collective-permute-done.3.refs_10_), channel_id=1, source_target_pairs={{0,3},{1,2},{2,1},{3,0},{4,7},{5,6},{6,5},{7,4},{8,11},{9,10},{10,... | collective-permute-start | bytes 393224 | tf_op jit(solution)/shard_map/ppermute | solution.py:26
  21.3 3.0 %densify.3.refs_8_.refs_2_ = bf16[256,1152]{1,0:T(8,128)(2,1)S(1)} custom-call(s32[1]{0:T(128)} %bitcast.refs_0_, s32[1,2,96]{2,1,0:T(2,128)S(1)} %copy-done.6, s32[1,2,96]{2,1,0:T(2,128)S(1)} %copy-done.4, s32[1,2]{1,0:T(1,128)S(1)} %bitcast.59, bf16[1,2,96,128,128]{4,3,2,1,0:T(8,128)(2,1)} %refs_4_.3), custom_call_target="tpu_custom_call" | custom-call | flops 31457280 | bytes 3145728 | tf_op jit(solution)/shard_map/densify/pallas_call | solution.py:59
  25.1 1.6 %middle.2 = (bf16[256,256]{1,0:T(8,128)(2,1)S(1)}, bf16[128,256]{1,0:T(8,128)(2,1)S(1)}, bf16[128,256]{1,0:T(8,128)(2,1)S(1)}, bf16[128,256]{1,0:T(8,128)(2,1)S(1)}, bf16[256,256]{1,0:T(8,128)(2,1)S(1)}) custom-call(s32[1]{0:T(128)} %bitcast.refs_0_, s32[1]{0:T(128)} %bitcast.3.refs_1_, bf16[1,2,2,256,256]{4,3,2,1,0:T(8,128)(2,1)S(1)} %copy-done, ...), custom_call_target="tpu_custom_call" | custom-call | flops 184549376 | bytes 1441792 | tf_op jit(solution)/shard_map/middle/pallas_call | solution.py:59
  28.6 1.9 %collective-permute-start.12 = (bf16[128,256]{1,0:T(8,128)(2,1)S(1)}, bf16[128,256]{1,0:T(8,128)(2,1)S(1)}, u32[]{:S(2)}, u32[]{:S(2)}) collective-permute-start(bf16[128,256]{1,0:T(8,128)(2,1)S(1)} %get-tuple-element.34), channel_id=1, source_target_pairs={{0,2},{1,3},{2,0},{3,1},{4,6},{5,7},{6,4},{7,5},{8,10},{9,11},{10,... | collective-permute-start | bytes 196616 | tf_op jit(solution)/shard_map/ppermute | solution.py:26
  31.5 3.2 %collective-permute-done.10.refs_1_.refs_4_ = bf16[256,256]{1,0:T(8,128)(2,1)S(1)} collective-permute-done((bf16[256,256]{1,0:T(8,128)(2,1)S(1)}, bf16[256,256]{1,0:T(8,128)(2,1)S(1)}, u32[]{:S(2)}, u32[]{:S(2)}) %collective-permute-start.10) | collective-permute-done | bytes 131104 | tf_op jit(solution)/shard_map/ppermute | solution.py:26
  36.1 2.7 %collective-permute-start.16 = (bf16[128,256]{1,0:T(8,128)(2,1)S(1)}, bf16[128,256]{1,0:T(8,128)(2,1)S(1)}, u32[]{:S(2)}, u32[]{:S(2)}) collective-permute-start(bf16[128,256]{1,0:T(8,128)(2,1)S(1)} %get-tuple-element.38), channel_id=1, source_target_pairs={{0,3},{1,2},{2,1},{3,0},{4,7},{5,6},{6,5},{7,4},{8,11},{9,10},{10,... | collective-permute-start | bytes 196616 | tf_op jit(solution)/shard_map/ppermute | solution.py:26
  38.9 1.5 %collective-permute-done.14.refs_8_ = bf16[128,256]{1,0:T(8,128)(2,1)S(1)} collective-permute-done((bf16[128,256]{1,0:T(8,128)(2,1)S(1)}, bf16[128,256]{1,0:T(8,128)(2,1)S(1)}, u32[]{:S(2)}, u32[]{:S(2)}) %collective-permute-start.14) | collective-permute-done | bytes 65568 | tf_op jit(solution)/shard_map/ppermute | solution.py:26
  44.4 1.6 %collective-permute-done.17.refs_9_ = bf16[256,256]{1,0:T(8,128)(2,1)S(1)} collective-permute-done((bf16[256,256]{1,0:T(8,128)(2,1)S(1)}, bf16[256,256]{1,0:T(8,128)(2,1)S(1)}, u32[]{:S(2)}, u32[]{:S(2)}) %collective-permute-start.17) | collective-permute-done | bytes 131104 | tf_op jit(solution)/shard_map/ppermute | solution.py:32
  47.3 2.2 %collective-permute-start.18 = (bf16[256,256]{1,0:T(8,128)(2,1)S(1)}, bf16[256,256]{1,0:T(8,128)(2,1)S(1)}, u32[]{:S(2)}, u32[]{:S(2)}) collective-permute-start(bf16[256,256]{1,0:T(8,128)(2,1)S(1)} %get-tuple-element.39.refs_9_), channel_id=1, source_target_pairs={{0,4},{1,5},{2,6},{3,7},{4,0},{5,1},{6,2},{7,3},{8,12},{9,13},{10,... | collective-permute-start | bytes 393224 | tf_op jit(solution)/shard_map/ppermute | solution.py:26
  50.8 2.2 %collective-permute-start.21 = (bf16[192,256]{1,0:T(8,128)(2,1)S(1)}, bf16[192,256]{1,0:T(8,128)(2,1)S(1)}, u32[]{:S(2)}, u32[]{:S(2)}) collective-permute-start(bf16[192,256]{1,0:T(8,128)(2,1)S(1)} %get-tuple-element.42), channel_id=1, source_target_pairs={{0,3},{1,2},{2,1},{3,0},{4,7},{5,6},{6,5},{7,4},{8,11},{9,10},{10,... | collective-permute-start | bytes 294920 | tf_op jit(solution)/shard_map/ppermute | solution.py:26
  53.1 3.2 %densify.2.refs_8_.refs_2_ = bf16[256,1152]{1,0:T(8,128)(2,1)S(1)} custom-call(s32[1]{0:T(128)} %bitcast.refs_0_, s32[1,2,96]{2,1,0:T(2,128)S(1)} %copy-done.7, s32[1,2,96]{2,1,0:T(2,128)S(1)} %copy-done.5, s32[1,2]{1,0:T(1,128)S(1)} %bitcast.60, bf16[1,2,96,128,128]{4,3,2,1,0:T(8,128)(2,1)} %refs_4_.3), custom_call_target="tpu_custom_call" | custom-call | flops 31457280 | bytes 3145728 | tf_op jit(solution)/shard_map/densify/pallas_call | solution.py:59
  56.3 3.1 %collective-permute-done.21.refs_8_.refs_13_ = bf16[192,256]{1,0:T(8,128)(2,1)S(1)} collective-permute-done((bf16[192,256]{1,0:T(8,128)(2,1)S(1)}, bf16[192,256]{1,0:T(8,128)(2,1)S(1)}, u32[]{:S(2)}, u32[]{:S(2)}) %collective-permute-start.21) | collective-permute-done | bytes 98336 | tf_op jit(solution)/shard_map/ppermute | solution.py:26
  61.2 2.6 %collective-permute-start.23 = (bf16[128,256]{1,0:T(8,128)(2,1)S(1)}, bf16[128,256]{1,0:T(8,128)(2,1)S(1)}, u32[]{:S(2)}, u32[]{:S(2)}) collective-permute-start(bf16[128,256]{1,0:T(8,128)(2,1)S(1)} %get-tuple-element.45), channel_id=1, source_target_pairs={{0,2},{1,3},{2,0},{3,1},{4,6},{5,7},{6,4},{7,5},{8,10},{9,11},{10,... | collective-permute-start | bytes 196616 | tf_op jit(solution)/shard_map/ppermute | solution.py:26
  66.5 2.4 %collective-permute-done.24.refs_16_ = bf16[128,256]{1,0:T(8,128)(2,1)S(1)} collective-permute-done((bf16[128,256]{1,0:T(8,128)(2,1)S(1)}, bf16[128,256]{1,0:T(8,128)(2,1)S(1)}, u32[]{:S(2)}, u32[]{:S(2)}) %collective-permute-start.24) | collective-permute-done | bytes 65568 | tf_op jit(solution)/shard_map/ppermute | solution.py:26
  68.9 1.9 %middle.3 = (bf16[256,256]{1,0:T(8,128)(2,1)S(1)}, bf16[256,256]{1,0:T(8,128)(2,1)S(1)}, bf16[256,256]{1,0:T(8,128)(2,1)S(1)}, bf16[256,256]{1,0:T(8,128)(2,1)S(...) custom-call(s32[1]{0:T(128)} %bitcast.refs_0_, s32[1]{0:T(128)} %bitcast.3.refs_1_, ...), custom_call_target="tpu_custom_call" | custom-call | flops 184549376 | bytes 1441792 | tf_op jit(solution)/shard_map/middle/pallas_call | solution.py:59
  72.5 1.9 %collective-permute-start.29 = (bf16[256,256]{1,0:T(8,128)(2,1)S(1)}, bf16[256,256]{1,0:T(8,128)(2,1)S(1)}, u32[]{:S(2)}, u32[]{:S(2)}) collective-permute-start(bf16[256,256]{1,0:T(8,128)(2,1)S(1)} %get-tuple-element.52), channel_id=1, source_target_pairs={{0,3},{1,2},{2,1},{3,0},{4,7},{5,6},{6,5},{7,4},{8,11},{9,10},{10,... | collective-permute-start | bytes 393224 | tf_op jit(solution)/shard_map/ppermute | solution.py:26
  75.4 1.9 %collective-permute-done.27.refs_6_.refs_5_ = bf16[256,256]{1,0:T(8,128)(2,1)S(1)} collective-permute-done((bf16[256,256]{1,0:T(8,128)(2,1)S(1)}, bf16[256,256]{1,0:T(8,128)(2,1)S(1)}, u32[]{:S(2)}, u32[]{:S(2)}) %collective-permute-start.27) | collective-permute-done | bytes 131104 | tf_op jit(solution)/shard_map/ppermute | solution.py:26
  78.6 3.1 %collective-permute-done.29.refs_8_.refs_7_ = bf16[256,256]{1,0:T(8,128)(2,1)S(1)} collective-permute-done((bf16[256,256]{1,0:T(8,128)(2,1)S(1)}, bf16[256,256]{1,0:T(8,128)(2,1)S(1)}, u32[]{:S(2)}, u32[]{:S(2)}) %collective-permute-start.29) | collective-permute-done | bytes 131104 | tf_op jit(solution)/shard_map/ppermute | solution.py:26
  89.1 2.1 %collective-permute-done.32.refs_10_ = bf16[128,256]{1,0:T(8,128)(2,1)S(1)} collective-permute-done((bf16[128,256]{1,0:T(8,128)(2,1)S(1)}, bf16[128,256]{1,0:T(8,128)(2,1)S(1)}, u32[]{:S(2)}, u32[]{:S(2)}) %collective-permute-start.32) | collective-permute-done | bytes 65568 | tf_op jit(solution)/shard_map/ppermute | solution.py:26
  91.2 1.6 %exit.3 = (bf16[2,1,256,256]{3,2,1,0:T(8,128)(2,1)}, bf16[64,256]{1,0:T(8,128)(2,1)S(1)}) custom-call(s32[1]{0:T(128)} %bitcast.refs_0_, s32[1,16]{1,0:T(1,128)S(1)} %reshape.85.refs_4_.refs_1_, bf16[256,1152]{1,0:T(8,128)(2,1)S(1)} %densify.2.refs_8_.refs_2_, bf16[256,256]{1,0:T(8,128)(2,1)S(1)} %get-tuple-element.49.refs_3_, ...), custom_call_target="tpu_custom_call" | custom-call | flops 184549376 | bytes 1441792 | tf_op jit(solution)/shard_map/exit/pallas_call | solution.py:59
  (93 shorter events, 43.3 us)
Async XLA Ops:
  2.2 15.9 %collective-permute-start.6 = (bf16[256,256]{1,0:T(8,128)(2,1)S(1)}, bf16[256,256]{1,0:T(8,128)(2,1)S(1)}, u32[]{:S(2)}, u32[]{:S(2)}) collective-permute-start(bf16[256,256]{1,0:T(8,128)(2,1)S(1)} %fusion.3.refs_9_), channel_id=1, source_target_pairs={{0,3},{1,2},{2,1},{3,0},{4,7},{5,6},{6,5},{7,4},{8,11},{9,10},{10,... | collective-permute-start | bytes 393224 | tf_op jit(solution)/shard_map/ppermute | solution.py:26
  6.3 9.5 %collective-permute-start.3 = (bf16[256,256]{1,0:T(8,128)(2,1)S(1)}, bf16[256,256]{1,0:T(8,128)(2,1)S(1)}, u32[]{:S(2)}, u32[]{:S(2)}) collective-permute-start(bf16[256,256]{1,0:T(8,128)(2,1)S(1)} %fusion.3.refs_9_), channel_id=1, source_target_pairs={{0,4},{1,5},{2,6},{3,7},{4,0},{5,1},{6,2},{7,3},{8,12},{9,13},{10,... | collective-permute-start | bytes 393224 | tf_op jit(solution)/shard_map/ppermute | solution.py:26
  11.7 5.9 %collective-permute-start = (s32[1,16]{1,0:T(1,128)S(1)}, s32[1,16]{1,0:T(1,128)S(1)}, u32[]{:S(2)}, u32[]{:S(2)}) collective-permute-start(s32[1,16]{1,0:T(1,128)S(1)} %reshape.85.refs_4_.refs_1_), channel_id=1, source_target_pairs={{0,1},{1,0},{2,3},{3,2},{4,5},{5,4},{6,7},{7,6},{8,9},{9,8},{10,11... | collective-permute-start | bytes 200 | tf_op jit(solution)/shard_map/ppermute | solution.py:26
  14.2 10.2 %collective-permute-start.5 = (bf16[256,256]{1,0:T(8,128)(2,1)S(1)}, bf16[256,256]{1,0:T(8,128)(2,1)S(1)}, u32[]{:S(2)}, u32[]{:S(2)}) collective-permute-start(bf16[256,256]{1,0:T(8,128)(2,1)S(1)} %fusion.3.refs_9_), channel_id=1, source_target_pairs={{0,2},{1,3},{2,0},{3,1},{4,6},{5,7},{6,4},{7,5},{8,10},{9,11},{10,... | collective-permute-start | bytes 393224 | tf_op jit(solution)/shard_map/ppermute | solution.py:26
  14.6 9.8 %collective-permute-start.4 = (bf16[256,256]{1,0:T(8,128)(2,1)S(1)}, bf16[256,256]{1,0:T(8,128)(2,1)S(1)}, u32[]{:S(2)}, u32[]{:S(2)}) collective-permute-start(bf16[256,256]{1,0:T(8,128)(2,1)S(1)} %fusion.3.refs_9_), channel_id=1, source_target_pairs={{0,1},{1,0},{2,3},{3,2},{4,5},{5,4},{6,7},{7,6},{8,9},{9,8},{10,11... | collective-permute-start | bytes 393224 | tf_op jit(solution)/shard_map/ppermute | solution.py:26
  15.8 8.6 %collective-permute-start.9 = (bf16[256,256]{1,0:T(8,128)(2,1)S(1)}, bf16[256,256]{1,0:T(8,128)(2,1)S(1)}, u32[]{:S(2)}, u32[]{:S(2)}) collective-permute-start(bf16[256,256]{1,0:T(8,128)(2,1)S(1)} %collective-permute-done.3.refs_10_), channel_id=1, source_target_pairs={{0,3},{1,2},{2,1},{3,0},{4,7},{5,6},{6,5},{7,4},{8,11},{9,10},{10,... | collective-permute-start | bytes 393224 | tf_op jit(solution)/shard_map/ppermute | solution.py:26
  17.7 6.7 %collective-permute-start.8 = (bf16[256,256]{1,0:T(8,128)(2,1)S(1)}, bf16[256,256]{1,0:T(8,128)(2,1)S(1)}, u32[]{:S(2)}, u32[]{:S(2)}) collective-permute-start(bf16[256,256]{1,0:T(8,128)(2,1)S(1)} %collective-permute-done.3.refs_10_), channel_id=1, source_target_pairs={{0,2},{1,3},{2,0},{3,1},{4,6},{5,7},{6,4},{7,5},{8,10},{9,11},{10,... | collective-permute-start | bytes 393224 | tf_op jit(solution)/shard_map/ppermute | solution.py:26
  18.1 6.9 %collective-permute-start.7 = (bf16[256,256]{1,0:T(8,128)(2,1)S(1)}, bf16[256,256]{1,0:T(8,128)(2,1)S(1)}, u32[]{:S(2)}, u32[]{:S(2)}) collective-permute-start(bf16[256,256]{1,0:T(8,128)(2,1)S(1)} %collective-permute-done.3.refs_10_), channel_id=1, source_target_pairs={{0,1},{1,0},{2,3},{3,2},{4,5},{5,4},{6,7},{7,6},{8,9},{9,8},{10,11... | collective-permute-start | bytes 393224 | tf_op jit(solution)/shard_map/ppermute | solution.py:26
  26.7 8.0 %collective-permute-start.10 = (bf16[256,256]{1,0:T(8,128)(2,1)S(1)}, bf16[256,256]{1,0:T(8,128)(2,1)S(1)}, u32[]{:S(2)}, u32[]{:S(2)}) collective-permute-start(bf16[256,256]{1,0:T(8,128)(2,1)S(1)} %get-tuple-element.32.refs_3_), channel_id=1, source_target_pairs={{0,4},{1,5},{2,6},{3,7},{4,0},{5,1},{6,2},{7,3},{8,12},{9,13},{10,... | collective-permute-start | bytes 393224 | tf_op jit(solution)/shard_map/ppermute | solution.py:26
  28.0 8.1 %collective-permute-start.11 = (bf16[128,256]{1,0:T(8,128)(2,1)S(1)}, bf16[128,256]{1,0:T(8,128)(2,1)S(1)}, u32[]{:S(2)}, u32[]{:S(2)}) collective-permute-start(bf16[128,256]{1,0:T(8,128)(2,1)S(1)} %get-tuple-element.33), channel_id=1, source_target_pairs={{0,1},{1,0},{2,3},{3,2},{4,5},{5,4},{6,7},{7,6},{8,9},{9,8},{10,11... | collective-permute-start | bytes 196616 | tf_op jit(solution)/shard_map/ppermute | solution.py:26
  28.6 10.3 %collective-permute-start.12 = (bf16[128,256]{1,0:T(8,128)(2,1)S(1)}, bf16[128,256]{1,0:T(8,128)(2,1)S(1)}, u32[]{:S(2)}, u32[]{:S(2)}) collective-permute-start(bf16[128,256]{1,0:T(8,128)(2,1)S(1)} %get-tuple-element.34), channel_id=1, source_target_pairs={{0,2},{1,3},{2,0},{3,1},{4,6},{5,7},{6,4},{7,5},{8,10},{9,11},{10,... | collective-permute-start | bytes 196616 | tf_op jit(solution)/shard_map/ppermute | solution.py:26
  30.5 8.3 %collective-permute-start.13 = (bf16[128,256]{1,0:T(8,128)(2,1)S(1)}, bf16[128,256]{1,0:T(8,128)(2,1)S(1)}, u32[]{:S(2)}, u32[]{:S(2)}) collective-permute-start(bf16[128,256]{1,0:T(8,128)(2,1)S(1)} %get-tuple-element.35), channel_id=1, source_target_pairs={{0,3},{1,2},{2,1},{3,0},{4,7},{5,6},{6,5},{7,4},{8,11},{9,10},{10,... | collective-permute-start | bytes 196616 | tf_op jit(solution)/shard_map/ppermute | solution.py:26
  36.1 5.7 %collective-permute-start.16 = (bf16[128,256]{1,0:T(8,128)(2,1)S(1)}, bf16[128,256]{1,0:T(8,128)(2,1)S(1)}, u32[]{:S(2)}, u32[]{:S(2)}) collective-permute-start(bf16[128,256]{1,0:T(8,128)(2,1)S(1)} %get-tuple-element.38), channel_id=1, source_target_pairs={{0,3},{1,2},{2,1},{3,0},{4,7},{5,6},{6,5},{7,4},{8,11},{9,10},{10,... | collective-permute-start | bytes 196616 | tf_op jit(solution)/shard_map/ppermute | solution.py:26
  47.3 12.1 %collective-permute-start.18 = (bf16[256,256]{1,0:T(8,128)(2,1)S(1)}, bf16[256,256]{1,0:T(8,128)(2,1)S(1)}, u32[]{:S(2)}, u32[]{:S(2)}) collective-permute-start(bf16[256,256]{1,0:T(8,128)(2,1)S(1)} %get-tuple-element.39.refs_9_), channel_id=1, source_target_pairs={{0,4},{1,5},{2,6},{3,7},{4,0},{5,1},{6,2},{7,3},{8,12},{9,13},{10,... | collective-permute-start | bytes 393224 | tf_op jit(solution)/shard_map/ppermute | solution.py:26
  49.5 6.8 %collective-permute-start.19 = (bf16[192,256]{1,0:T(8,128)(2,1)S(1)}, bf16[192,256]{1,0:T(8,128)(2,1)S(1)}, u32[]{:S(2)}, u32[]{:S(2)}) collective-permute-start(bf16[192,256]{1,0:T(8,128)(2,1)S(1)} %get-tuple-element.40), channel_id=1, source_target_pairs={{0,1},{1,0},{2,3},{3,2},{4,5},{5,4},{6,7},{7,6},{8,9},{9,8},{10,11... | collective-permute-start | bytes 294920 | tf_op jit(solution)/shard_map/ppermute | solution.py:26
  50.2 6.1 %collective-permute-start.20 = (bf16[192,256]{1,0:T(8,128)(2,1)S(1)}, bf16[192,256]{1,0:T(8,128)(2,1)S(1)}, u32[]{:S(2)}, u32[]{:S(2)}) collective-permute-start(bf16[192,256]{1,0:T(8,128)(2,1)S(1)} %get-tuple-element.41), channel_id=1, source_target_pairs={{0,2},{1,3},{2,0},{3,1},{4,6},{5,7},{6,4},{7,5},{8,10},{9,11},{10,... | collective-permute-start | bytes 294920 | tf_op jit(solution)/shard_map/ppermute | solution.py:26
  50.8 8.7 %collective-permute-start.21 = (bf16[192,256]{1,0:T(8,128)(2,1)S(1)}, bf16[192,256]{1,0:T(8,128)(2,1)S(1)}, u32[]{:S(2)}, u32[]{:S(2)}) collective-permute-start(bf16[192,256]{1,0:T(8,128)(2,1)S(1)} %get-tuple-element.42), channel_id=1, source_target_pairs={{0,3},{1,2},{2,1},{3,0},{4,7},{5,6},{6,5},{7,4},{8,11},{9,10},{10,... | collective-permute-start | bytes 294920 | tf_op jit(solution)/shard_map/ppermute | solution.py:26
  61.2 5.3 %collective-permute-start.23 = (bf16[128,256]{1,0:T(8,128)(2,1)S(1)}, bf16[128,256]{1,0:T(8,128)(2,1)S(1)}, u32[]{:S(2)}, u32[]{:S(2)}) collective-permute-start(bf16[128,256]{1,0:T(8,128)(2,1)S(1)} %get-tuple-element.45), channel_id=1, source_target_pairs={{0,2},{1,3},{2,0},{3,1},{4,6},{5,7},{6,4},{7,5},{8,10},{9,11},{10,... | collective-permute-start | bytes 196616 | tf_op jit(solution)/shard_map/ppermute | solution.py:26
  63.8 5.2 %collective-permute-start.24 = (bf16[128,256]{1,0:T(8,128)(2,1)S(1)}, bf16[128,256]{1,0:T(8,128)(2,1)S(1)}, u32[]{:S(2)}, u32[]{:S(2)}) collective-permute-start(bf16[128,256]{1,0:T(8,128)(2,1)S(1)} %get-tuple-element.46), channel_id=1, source_target_pairs={{0,3},{1,2},{2,1},{3,0},{4,7},{5,6},{6,5},{7,4},{8,11},{9,10},{10,... | collective-permute-start | bytes 196616 | tf_op jit(solution)/shard_map/ppermute | solution.py:26
  70.9 6.4 %collective-permute-start.27 = (bf16[256,256]{1,0:T(8,128)(2,1)S(1)}, bf16[256,256]{1,0:T(8,128)(2,1)S(1)}, u32[]{:S(2)}, u32[]{:S(2)}) collective-permute-start(bf16[256,256]{1,0:T(8,128)(2,1)S(1)} %get-tuple-element.50), channel_id=1, source_target_pairs={{0,1},{1,0},{2,3},{3,2},{4,5},{5,4},{6,7},{7,6},{8,9},{9,8},{10,11... | collective-permute-start | bytes 393224 | tf_op jit(solution)/shard_map/ppermute | solution.py:26
  72.1 6.4 %collective-permute-start.28 = (bf16[256,256]{1,0:T(8,128)(2,1)S(1)}, bf16[256,256]{1,0:T(8,128)(2,1)S(1)}, u32[]{:S(2)}, u32[]{:S(2)}) collective-permute-start(bf16[256,256]{1,0:T(8,128)(2,1)S(1)} %get-tuple-element.51), channel_id=1, source_target_pairs={{0,2},{1,3},{2,0},{3,1},{4,6},{5,7},{6,4},{7,5},{8,10},{9,11},{10,... | collective-permute-start | bytes 393224 | tf_op jit(solution)/shard_map/ppermute | solution.py:26
  72.5 9.2 %collective-permute-start.29 = (bf16[256,256]{1,0:T(8,128)(2,1)S(1)}, bf16[256,256]{1,0:T(8,128)(2,1)S(1)}, u32[]{:S(2)}, u32[]{:S(2)}) collective-permute-start(bf16[256,256]{1,0:T(8,128)(2,1)S(1)} %get-tuple-element.52), channel_id=1, source_target_pairs={{0,3},{1,2},{2,1},{3,0},{4,7},{5,6},{6,5},{7,4},{8,11},{9,10},{10,... | collective-permute-start | bytes 393224 | tf_op jit(solution)/shard_map/ppermute | solution.py:26
  74.4 7.2 %collective-permute-start.26 = (bf16[256,256]{1,0:T(8,128)(2,1)S(1)}, bf16[256,256]{1,0:T(8,128)(2,1)S(1)}, u32[]{:S(2)}, u32[]{:S(2)}) collective-permute-start(bf16[256,256]{1,0:T(8,128)(2,1)S(1)} %get-tuple-element.49.refs_3_), channel_id=1, source_target_pairs={{0,4},{1,5},{2,6},{3,7},{4,0},{5,1},{6,2},{7,3},{8,12},{9,13},{10,... | collective-permute-start | bytes 393224 | tf_op jit(solution)/shard_map/ppermute | solution.py:26
  86.0 5.2 %collective-permute-start.32 = (bf16[128,256]{1,0:T(8,128)(2,1)S(1)}, bf16[128,256]{1,0:T(8,128)(2,1)S(1)}, u32[]{:S(2)}, u32[]{:S(2)}) collective-permute-start(bf16[128,256]{1,0:T(8,128)(2,1)S(1)} %get-tuple-element.56), channel_id=1, source_target_pairs={{0,3},{1,2},{2,1},{3,0},{4,7},{5,6},{6,5},{7,4},{8,11},{9,10},{10,... | collective-permute-start | bytes 196616 | tf_op jit(solution)/shard_map/ppermute | solution.py:26
  (24 other events, 313.6 us)

commit v6 on v5

--- a/solution.py
+++ b/solution.py
@@ -152,10 +152,6 @@
     return ((1.0 - ALPHA) * total).astype(BF16)
 
 
-def chunk_total(mine_ref, far_ref):
-    return (mine_ref[...].astype(F32) + far_ref[...].astype(F32)).astype(BF16)
-
-
 def layer_kernel(c, *refs):
     refs = Refs(refs)
     n, tile, width, chunk = c["n"], c["tile"], c["width"], c["chunk"]
@@ -169,13 +165,9 @@
         got = take_got(refs, n)
     if c["final"]:
         support_all, acc_ref = refs.take(2)
-    if c["sum_above"]:
-        above_mine, above_far = refs.take(2)
     image_ref = refs.take()
     sends = refs.take(h - 1)
     out_ref = refs.take()
-    if c["sum_above"]:
-        above_ref = refs.take()
     preact_ref, weight_ref, load_sems = refs.take(3)
 
     me = me_ref[0]
@@ -220,30 +212,33 @@
         out_ref[...] = tile_at(term_ref, place, chunk)
     else:
         out_ref[...] = masked
-    if c["sum_above"]:
-        above_ref[...] = chunk_total(above_mine, above_far)
-        for send in sends:
-            send[tile + chunk :, :] = above_ref[...]
 
 
 def relay_kernel(c, *refs):
     refs = Refs(refs)
-    n, tile, chunk = c["n"], c["tile"], c["chunk"]
+    n, tile = c["n"], c["tile"]
     h = n // 2
     me_ref, far_ref = refs.take(2)
     picks = refs.take(h - 1)
-    if c["final"]:
-        kept_ref, near = refs.take(), refs.take(h - 1)
     sends = refs.take(h - 1)
     me = me_ref[0]
     for k in range(1, h):
         index = picks[k - 1][0, c["tick"] * n + jnp.bitwise_xor(me, h)]
         sends[k - 1][...] = tile_at(far_ref, index, tile)
-    if c["final"]:
-        total = kept_ref[...]
-        for ref in near:
-            total = total + ref[tile : tile + chunk, :].astype(F32)
-        refs.take()[...] = total.astype(BF16)
+
+
+def half_sum_kernel(tile, kept_ref, *refs):
+    total = kept_ref[...]
+    for ref in refs[:-1]:
+        total = total + ref[tile:, :].astype(F32)
+    refs[-1][...] = total.astype(BF16)
+
+
+def total_kernel(layers, *refs):
+    for layer in range(layers):
+        mine_ref, far_ref = refs[2 * layer : 2 * layer + 2]
+        total = mine_ref[...].astype(F32) + far_ref[...].astype(F32)
+        refs[-1][layer] = total.astype(BF16)
 
 
 def exit_kernel(c, *refs):
@@ -254,33 +249,28 @@
         refs.take()[...] = spread_of(adj_ref, own_ref, got, pick_ref, me_ref[0], c)
         return
     handed = refs.take(c["tick"])
-    mine_ref, far_ref = refs.take(2)
-    out_ref, sum_ref, hold_ref, sems = refs.take(4)
+    out_ref, hold_ref, sems = refs.take(3)
     copies = [
         pltpu.make_async_copy(ref, out_ref.at[t, 0], sems.at[t])
         for t, ref in enumerate(handed + [hold_ref])
     ]
     for copy in copies[:-1]:
         copy.start()
-    sum_ref[...] = chunk_total(mine_ref, far_ref)
     hold_ref[...] = spread_of(adj_ref, own_ref, got, pick_ref, me_ref[0], c)
     copies[-1].start()
     for copy in copies:
         copy.wait()
 
 
-def finish_kernel(h, layers, chunk, tile, *refs):
-    refs = Refs(refs)
-    me_ref = refs.take()
-    sums = [refs.take(h) for layer in range(layers)]
-    out_ref, hold_ref, sems = refs.take(3)
+def finish_kernel(h, me_ref, *refs):
+    sums, (out_ref, hold_ref, sems) = refs[:h], refs[h:]
+    layers, chunk, _ = sums[0].shape
     place = lax.rem(me_ref[0], h)
     copies = []
     for layer in range(layers):
         for k in range(h):
-            skip = tile + chunk if layer > 0 and k > 0 else 0
             start = pl.multiple_of(jnp.bitwise_xor(place, k) * chunk, chunk)
-            hold_ref[layer, pl.ds(start, chunk), :] = sums[layer][k][skip:, :].astype(F32)
+            hold_ref[layer, pl.ds(start, chunk), :] = sums[k][layer].astype(F32)
         copy = pltpu.make_async_copy(hold_ref.at[layer], out_ref.at[0, layer], sems.at[layer])
         copy.start()
         copies.append(copy)
@@ -309,29 +299,34 @@
         owner[:, :, None] == jnp.arange(n)[None, None, :], (tile_col[0] % row_tiles)[:, :, None], 0
     )
     pick = jnp.max(named, axis=1).reshape(1, ticks * n).astype(jnp.int32)
-    picks = [pick] + [swapped(pick, k) for k in range(1, h)]
+    picks = None
 
     handed = []
     passed = None
     weight_acc = [None] * layers
-    weight_sums = [None] * layers
+    weight_sums = []
     initial = []
     base = dict(n=n, tile=tile, width=width, layers=layers, sections=sections, chunk=chunk)
     layer_cost = cost(2 * rows * width * (width + (n + 1) * tile), (6 + 2 * n) * rows * width)
     small_cost = cost(rows * width, 2 * n * rows * width)
+    relay_cost = cost(rows * width, 8 * n * rows * width)
+    densify_tick = functools.partial(
+        densify, me=me_arr, rows=tile_row, cols=tile_col, count=counts, vals=tile_vals,
+        row_tiles=row_tiles, n=n,
+    )
+    adj_next = densify_tick(0)
     for tick in range(ticks):
         final = tick == ticks - 1
         if tick > 0:
             passed = passed_along(handed[-1], "section", -1)
-        adj = densify(tick, me_arr, tile_row, tile_col, counts, tile_vals, row_tiles, n)
-        image = got = whole = mine = None
+        adj = adj_next
+        image = got = whole = None
         toward = 0.0
         for layer in reversed(range(layers)):
             entry = layer == layers - 1
             beta = jnp.log(BETA_SCALE / (layers * section + layer + 1).astype(F32) + 1.0)
             c = dict(
-                base, layer=layer, tick=tick, entry=entry, final=final,
-                sum_above=final and not entry, whole=whole,
+                base, layer=layer, tick=tick, entry=entry, final=final, whole=whole
             )
             if tick == 0 and entry:
                 masked = jnp.where(
@@ -342,6 +337,8 @@
                 far = swapped(image, h)
                 near = [swapped(image, k) for k in range(1, h)]
                 got = [far, *near, *(swapped(far, k) for k in range(1, h))]
+                pick, _ = lax.optimization_barrier((pick, far))
+                picks = [pick] + [swapped(pick, k) for k in range(1, h)]
             else:
                 call = Call()
                 call.give(SMEM, me_arr, section_arr)
@@ -354,17 +351,13 @@
                 if final:
                     call.give(HBM, support)
                     call.give(VMEM, weight_acc[layer])
-                if c["sum_above"]:
-                    call.give(VMEM, mine, swapped(mine, h))
-                message = tile + chunk * (final + c["sum_above"])
+                message = tile + (chunk if final else 0)
                 call.want(VMEM, (rows, width), BF16)
                 call.want(VMEM, (message, width), BF16, h - 1)
                 if final:
                     call.want(VMEM, (chunk, width), F32)
                 else:
                     call.want(VMEM, (rows, width), BF16)
-                if c["sum_above"]:
-                    call.want(VMEM, (chunk, width), BF16)
                 call.scratch = [
                     pltpu.VMEM((rows, width), BF16),
                     pltpu.VMEM((width, width), BF16),
@@ -383,21 +376,26 @@
                 kept = masked = results.take()
                 far = swapped(image, h)
                 near = [swapped(send, k) for k, send in enumerate(sends, 1)]
-                if c["sum_above"]:
-                    weight_sums[layer + 1] = [results.take(), *near]
+                if layer == 0 and not final:
+                    adj_next = densify_tick(tick + 1)
+                    far, adj_next = lax.optimization_barrier((far, adj_next))
                 call = Call()
                 call.give(SMEM, me_arr)
                 call.give(VMEM, far)
                 call.give(SMEM, *picks[1:])
+                call.want(VMEM, (tile, width), BF16, h - 1)
+                relays = call.run(functools.partial(relay_kernel, c), "relay", relay_cost)
+                relayed = [swapped(relay, k) for k, relay in enumerate(relays, 1)]
                 if final:
+                    kept, *_ = lax.optimization_barrier((kept, *relays))
+                    call = Call()
                     call.give(VMEM, kept, *near)
-                call.want(VMEM, (tile, width), BF16, h - 1)
-                if final:
                     call.want(VMEM, (chunk, width), BF16)
-                results = Refs(call.run(functools.partial(relay_kernel, c), "relay", small_cost))
-                relayed = [swapped(relay, k) for k, relay in enumerate(results.take(h - 1), 1)]
-                if final:
-                    mine = results.take()
+                    (mine,) = call.run(
+                        functools.partial(half_sum_kernel, tile), "half_sum", small_cost
+                    )
+                    relayed, mine = lax.optimization_barrier((relayed, mine))
+                    weight_sums = [mine, swapped(mine, h), *weight_sums]
                 got = [far, *near, *relayed]
             whole = tick == 0 and entry
             toward = toward + ALPHA * image.astype(F32)
@@ -413,28 +411,25 @@
         call.give(SMEM, me_arr, pick)
         call.give(VMEM, adj, image, *got)
         if final:
-            call.give(VMEM, *handed, mine, swapped(mine, h))
+            call.give(VMEM, *handed)
             call.want(HBM, (ticks, 1, rows, width), BF16)
-            call.want(VMEM, (chunk, width), BF16)
             call.scratch = [pltpu.VMEM((rows, width), BF16), pltpu.SemaphoreType.DMA((ticks,))]
         else:
             call.want(VMEM, (rows, width), BF16)
         results = call.run(functools.partial(exit_kernel, c), "exit", layer_cost)
-        if final:
-            handoff, last = results
-        else:
-            handed.append(results[0])
-    weight_sums[0] = [last] + [swapped(last, k) for k in range(1, h)]
+        handed.append(results[0])
+    weight_sums, got = lax.optimization_barrier((weight_sums, got))
+    call = Call()
+    call.give(VMEM, *weight_sums)
+    call.want(VMEM, (layers, chunk, width), BF16)
+    (total,) = call.run(functools.partial(total_kernel, layers), "total", small_cost)
     call = Call()
     call.give(SMEM, me_arr)
-    for sums in weight_sums:
-        call.give(VMEM, *sums)
+    call.give(VMEM, total, *(swapped(total, k) for k in range(1, h)))
     call.want(HBM, (1, layers, width, width), F32)
     call.scratch = [pltpu.VMEM((layers, width, width), F32), pltpu.SemaphoreType.DMA((layers,))]
-    (weight_grad,) = call.run(
-        functools.partial(finish_kernel, h, layers, chunk, tile), "finish", small_cost
-    )
-    return handoff, jnp.stack(initial)[None], weight_grad
+    (weight_grad,) = call.run(functools.partial(finish_kernel, h), "finish", small_cost)
+    return handed[-1], jnp.stack(initial)[None], weight_grad
 
 
 def solution(mesh):

time: 100 us -> 105 us (1.050)
  waiting for transfers between devices: 28.8 us -> 32.9 us
    ppermute x36, waiting for transfers between devices: 27.3 us -> 31.4 us  [swapped(): return lax.ppermute(block, 'rows', [(i, i ^ k) for i in range(n)])]
    pallas_call x11 -> x14, Pallas kernels: 16.2 us -> 15.5 us  [run(): pl.pallas_call(kernel, out_shape=self.outs, in_specs=self.specs, out_spec...]
  transfers between devices with their start and end apart: 37 -> 37, of which waited for: 21 -> 19; matrix products, arithmetic and copies ran while one was open for 2% -> 2% of each run, Pallas kernels for 7% -> 8%
where the time goes in v6:
time: 105 us; the launch traced here: 104 us
  starting transfers between devices  48.4 us (46%)
  waiting for transfers between devices  32.9 us (31%)
  Pallas kernels  15.5 us (15%)
  local copies, waits for them, and re-layouts  2.26 us (2%)
  matrix products  1.9 us (2%)
  other arithmetic  1.7 us (2%)
  between operations  1.14 us (1%)
    ppermute x36, starting transfers between devices, swapped(): return lax.ppermute(block, 'rows', [(i, i ^ k) for i in range(n)])  47.1 us
    ppermute x36, waiting for transfers between devices, swapped(): return lax.ppermute(block, 'rows', [(i, i ^ k) for i in range(n)])  31.4 us
    pallas_call x14, Pallas kernels, run(): pl.pallas_call(kernel, out_shape=self.outs, in_specs=self.specs, out_spec...  15.5 us
  transfers between devices with their start and end apart: 37, of which 19 were waited for; matrix products, arithmetic and copies ran while one was open for 2% of the time, Pallas kernels for 8%

profile of v6, /device:TPU:0, one launch (start us, length us, event | category | flops | bytes accessed | tf_op | source)
XLA Modules:
  0.0 103.8 jit_solution(8654717797603388953)
XLA Ops:
  2.2 4.1 %collective-permute-start = (bf16[256,256]{1,0:T(8,128)(2,1)S(1)}, bf16[256,256]{1,0:T(8,128)(2,1)S(1)}, u32[]{:S(2)}, u32[]{:S(2)}) collective-permute-start(bf16[256,256]{1,0:T(8,128)(2,1)S(1)} %fusion.3.refs_9_), channel_id=1, source_target_pairs={{0,4},{1,5},{2,6},{3,7},{4,0},{5,1},{6,2},{7,3},{8,12},{9,13},{10,... | collective-permute-start | bytes 393224 | tf_op jit(solution)/shard_map/ppermute | solution.py:26
  7.8 1.6 %collective-permute-start.5 = (bf16[256,256]{1,0:T(8,128)(2,1)S(1)}, bf16[256,256]{1,0:T(8,128)(2,1)S(1)}, u32[]{:S(2)}, u32[]{:S(2)}) collective-permute-start(bf16[256,256]{1,0:T(8,128)(2,1)S(1)} %fusion.3.refs_9_), channel_id=1, source_target_pairs={{0,2},{1,3},{2,0},{3,1},{4,6},{5,7},{6,4},{7,5},{8,10},{9,11},{10,... | collective-permute-start | bytes 393224 | tf_op jit(solution)/shard_map/ppermute | solution.py:26
  9.8 2.9 %collective-permute-done.refs_10_ = bf16[256,256]{1,0:T(8,128)(2,1)S(1)} collective-permute-done((bf16[256,256]{1,0:T(8,128)(2,1)S(1)}, bf16[256,256]{1,0:T(8,128)(2,1)S(1)}, u32[]{:S(2)}, u32[]{:S(2)}) %collective-permute-start) | collective-permute-done | bytes 131104 | tf_op jit(solution)/shard_map/ppermute | solution.py:26
  19.1 2.7 %densify.2.refs_8_.refs_2_ = bf16[256,1152]{1,0:T(8,128)(2,1)S(1)} custom-call(s32[1]{0:T(128)} %bitcast.refs_0_.me_ref, s32[1,2,96]{2,1,0:T(2,128)S(1)} %copy-done.5, s32[1,2,96]{2,1,0:T(2,128)S(1)} %copy-done.4, s32[1,2]{1,0:T(1,128)S(1)} %bitcast.59, bf16[1,2,96,128,128]{4,3,2,1,0:T(8,128)(2,1)} %refs_4_.3), custom_call_target="tpu_custom_call" | custom-call | flops 31457280 | bytes 3145728 | tf_op jit(solution)/shard_map/densify/pallas_call | solution.py:59
  21.9 1.8 %collective-permute-start.1 = (s32[1,16]{1,0:T(1,128)S(1)}, s32[1,16]{1,0:T(1,128)S(1)}, u32[]{:S(2)}, u32[]{:S(2)}) collective-permute-start(s32[1,16]{1,0:T(1,128)S(1)} %reshape.85.refs_4_.refs_1_), channel_id=1, source_target_pairs={{0,1},{1,0},{2,3},{3,2},{4,5},{5,4},{6,7},{7,6},{8,9},{9,8},{10,11... | collective-permute-start | bytes 200 | tf_op jit(solution)/shard_map/ppermute | solution.py:26
  25.5 2.3 %collective-permute-start.3 = (s32[1,16]{1,0:T(1,128)S(1)}, s32[1,16]{1,0:T(1,128)S(1)}, u32[]{:S(2)}, u32[]{:S(2)}) collective-permute-start(s32[1,16]{1,0:T(1,128)S(1)} %reshape.85.refs_4_.refs_1_), channel_id=1, source_target_pairs={{0,3},{1,2},{2,1},{3,0},{4,7},{5,6},{6,5},{7,4},{8,11},{9,10},{10,... | collective-permute-start | bytes 200 | tf_op jit(solution)/shard_map/ppermute | solution.py:26
  27.8 2.1 %collective-permute-done.3.refs_7_.refs_4_ = s32[1,16]{1,0:T(1,128)S(1)} collective-permute-done((s32[1,16]{1,0:T(1,128)S(1)}, s32[1,16]{1,0:T(1,128)S(1)}, u32[]{:S(2)}, u32[]{:S(2)}) %collective-permute-start.3) | collective-permute-done | bytes 96 | tf_op jit(solution)/shard_map/ppermute | solution.py:26
  30.0 1.7 %middle.2 = (bf16[256,256]{1,0:T(8,128)(2,1)S(1)}, bf16[128,256]{1,0:T(8,128)(2,1)S(1)}, bf16[128,256]{1,0:T(8,128)(2,1)S(1)}, bf16[128,256]{1,0:T(8,128)(2,1)S(1)}, bf16[256,256]{1,0:T(8,128)(2,1)S(1)}) custom-call(s32[1]{0:T(128)} %bitcast.refs_0_.me_ref, s32[1]{0:T(128)} %bitcast.7.refs_1_, bf16[1,2,2,256,256]{4,3,2,1,0:T(8,128)(2,1)S(1)} %copy-done, ...), custom_call_target="tpu_custom_call" | custom-call | flops 184549376 | bytes 1441792 | tf_op jit(solution)/shard_map/middle/pallas_call | solution.py:59
  31.6 2.5 %collective-permute-start.10 = (bf16[256,256]{1,0:T(8,128)(2,1)S(1)}, bf16[256,256]{1,0:T(8,128)(2,1)S(1)}, u32[]{:S(2)}, u32[]{:S(2)}) collective-permute-start(bf16[256,256]{1,0:T(8,128)(2,1)S(1)} %get-tuple-element.45.refs_3_), channel_id=1, source_target_pairs={{0,4},{1,5},{2,6},{3,7},{4,0},{5,1},{6,2},{7,3},{8,12},{9,13},{10,... | collective-permute-start | bytes 393224 | tf_op jit(solution)/shard_map/ppermute | solution.py:26
  34.1 1.6 %collective-permute-start.11 = (bf16[128,256]{1,0:T(8,128)(2,1)S(1)}, bf16[128,256]{1,0:T(8,128)(2,1)S(1)}, u32[]{:S(2)}, u32[]{:S(2)}) collective-permute-start(bf16[128,256]{1,0:T(8,128)(2,1)S(1)} %get-tuple-element.48), channel_id=1, source_target_pairs={{0,1},{1,0},{2,3},{3,2},{4,5},{5,4},{6,7},{7,6},{8,9},{9,8},{10,11... | collective-permute-start | bytes 196616 | tf_op jit(solution)/shard_map/ppermute | solution.py:26
  35.7 2.7 %densify.3.refs_8_.refs_2_ = bf16[256,1152]{1,0:T(8,128)(2,1)S(1)} custom-call(s32[1]{0:T(128)} %bitcast.refs_0_.me_ref, s32[1,2,96]{2,1,0:T(2,128)S(1)} %copy-done.5, s32[1,2,96]{2,1,0:T(2,128)S(1)} %copy-done.4, s32[1,2]{1,0:T(1,128)S(1)} %bitcast.60, bf16[1,2,96,128,128]{4,3,2,1,0:T(8,128)(2,1)} %refs_4_.3), custom_call_target="tpu_custom_call" | custom-call | flops 31457280 | bytes 3145728 | tf_op jit(solution)/shard_map/densify/pallas_call | solution.py:59
  38.5 2.6 %collective-permute-start.12 = (bf16[128,256]{1,0:T(8,128)(2,1)S(1)}, bf16[128,256]{1,0:T(8,128)(2,1)S(1)}, u32[]{:S(2)}, u32[]{:S(2)}) collective-permute-start(bf16[128,256]{1,0:T(8,128)(2,1)S(1)} %get-tuple-element.49), channel_id=1, source_target_pairs={{0,2},{1,3},{2,0},{3,1},{4,6},{5,7},{6,4},{7,5},{8,10},{9,11},{10,... | collective-permute-start | bytes 196616 | tf_op jit(solution)/shard_map/ppermute | solution.py:26
  41.6 1.6 %collective-permute-start.14 = (bf16[128,256]{1,0:T(8,128)(2,1)S(1)}, bf16[128,256]{1,0:T(8,128)(2,1)S(1)}, u32[]{:S(2)}, u32[]{:S(2)}) collective-permute-start(bf16[128,256]{1,0:T(8,128)(2,1)S(1)} %get-tuple-element.51), channel_id=1, source_target_pairs={{0,1},{1,0},{2,3},{3,2},{4,5},{5,4},{6,7},{7,6},{8,9},{9,8},{10,11... | collective-permute-start | bytes 196616 | tf_op jit(solution)/shard_map/ppermute | solution.py:26
  43.2 1.9 %collective-permute-start.15 = (bf16[128,256]{1,0:T(8,128)(2,1)S(1)}, bf16[128,256]{1,0:T(8,128)(2,1)S(1)}, u32[]{:S(2)}, u32[]{:S(2)}) collective-permute-start(bf16[128,256]{1,0:T(8,128)(2,1)S(1)} %get-tuple-element.52), channel_id=1, source_target_pairs={{0,2},{1,3},{2,0},{3,1},{4,6},{5,7},{6,4},{7,5},{8,10},{9,11},{10,... | collective-permute-start | bytes 196616 | tf_op jit(solution)/shard_map/ppermute | solution.py:26
  47.5 2.9 %collective-permute-done.16.refs_10_ = bf16[128,256]{1,0:T(8,128)(2,1)S(1)} collective-permute-done((bf16[128,256]{1,0:T(8,128)(2,1)S(1)}, bf16[128,256]{1,0:T(8,128)(2,1)S(1)}, u32[]{:S(2)}, u32[]{:S(2)}) %collective-permute-start.16) | collective-permute-done | bytes 65568 | tf_op jit(solution)/shard_map/ppermute | solution.py:26
  57.5 2.2 %collective-permute-start.21 = (bf16[192,256]{1,0:T(8,128)(2,1)S(1)}, bf16[192,256]{1,0:T(8,128)(2,1)S(1)}, u32[]{:S(2)}, u32[]{:S(2)}) collective-permute-start(bf16[192,256]{1,0:T(8,128)(2,1)S(1)} %get-tuple-element.57), channel_id=1, source_target_pairs={{0,3},{1,2},{2,1},{3,0},{4,7},{5,6},{6,5},{7,4},{8,11},{9,10},{10,... | collective-permute-start | bytes 294920 | tf_op jit(solution)/shard_map/ppermute | solution.py:26
  59.7 3.9 %collective-permute-done.18.refs_1_.refs_10_ = bf16[256,256]{1,0:T(8,128)(2,1)S(1)} collective-permute-done((bf16[256,256]{1,0:T(8,128)(2,1)S(1)}, bf16[256,256]{1,0:T(8,128)(2,1)S(1)}, u32[]{:S(2)}, u32[]{:S(2)}) %collective-permute-start.18) | collective-permute-done | bytes 131104 | tf_op jit(solution)/shard_map/ppermute | solution.py:26
  65.1 2.5 %collective-permute-start.24 = (bf16[128,256]{1,0:T(8,128)(2,1)S(1)}, bf16[128,256]{1,0:T(8,128)(2,1)S(1)}, u32[]{:S(2)}, u32[]{:S(2)}) collective-permute-start(bf16[128,256]{1,0:T(8,128)(2,1)S(1)} %get-tuple-element.60), channel_id=1, source_target_pairs={{0,3},{1,2},{2,1},{3,0},{4,7},{5,6},{6,5},{7,4},{8,11},{9,10},{10,... | collective-permute-start | bytes 196616 | tf_op jit(solution)/shard_map/ppermute | solution.py:26
  71.2 1.9 %middle.3 = (bf16[256,256]{1,0:T(8,128)(2,1)S(1)}, bf16[192,256]{1,0:T(8,128)(2,1)S(1)}, bf16[192,256]{1,0:T(8,128)(2,1)S(1)}, bf16[192,256]{1,0:T(8,128)(2,1)S(1)}, f32[64,256]{1,0:T(8,128)S(1)}) custom-call(s32[1]{0:T(128)} %bitcast.refs_0_.me_ref, s32[1]{0:T(128)} %bitcast.7.refs_1_, bf16[1,2,2,256,256]{4,3,2,1,0:T(8,128)(2,1)S(1)} %copy-done, ...), custom_call_target="tpu_custom_call" | custom-call | flops 184549376 | bytes 1441792 | tf_op jit(solution)/shard_map/middle/pallas_call | solution.py:59
  78.1 5.0 %collective-permute-done.25.refs_1_.refs_4_ = bf16[256,256]{1,0:T(8,128)(2,1)S(1)} collective-permute-done((bf16[256,256]{1,0:T(8,128)(2,1)S(1)}, bf16[256,256]{1,0:T(8,128)(2,1)S(1)}, u32[]{:S(2)}, u32[]{:S(2)}) %collective-permute-start.25) | collective-permute-done | bytes 131104 | tf_op jit(solution)/shard_map/ppermute | solution.py:26
  84.7 2.5 %collective-permute-start.31 = (bf16[128,256]{1,0:T(8,128)(2,1)S(1)}, bf16[128,256]{1,0:T(8,128)(2,1)S(1)}, u32[]{:S(2)}, u32[]{:S(2)}) collective-permute-start(bf16[128,256]{1,0:T(8,128)(2,1)S(1)} %get-tuple-element.73), channel_id=1, source_target_pairs={{0,3},{1,2},{2,1},{3,0},{4,7},{5,6},{6,5},{7,4},{8,11},{9,10},{10,... | collective-permute-start | bytes 196616 | tf_op jit(solution)/shard_map/ppermute | solution.py:26
  92.3 3.0 %collective-permute-done.32.refs_1_ = bf16[64,256]{1,0:T(8,128)(2,1)S(1)} collective-permute-done((bf16[64,256]{1,0:T(8,128)(2,1)S(1)}, bf16[64,256]{1,0:T(8,128)(2,1)S(1)}, u32[]{:S(2)}, u32[]{:S(2)}) %collective-permute-start.32) | collective-permute-done | bytes 32800 | tf_op jit(solution)/shard_map/ppermute | solution.py:26
  96.0 1.8 %collective-permute-start.35 = (bf16[2,64,256]{2,1,0:T(8,128)(2,1)S(1)}, bf16[2,64,256]{2,1,0:T(8,128)(2,1)S(1)}, u32[]{:S(2)}, u32[]{:S(2)}) collective-permute-start(bf16[2,64,256]{2,1,0:T(8,128)(2,1)S(1)} %total.1.refs_0_), channel_id=1, source_target_pairs={{0,2},{1,3},{2,0},{3,1},{4,6},{5,7},{6,4},{7,5},{8,10},{9,11},{10,... | collective-permute-start | bytes 196616 | tf_op jit(solution)/shard_map/ppermute | solution.py:26
  101.3 1.7 %collective-permute-done.36.refs_3_ = bf16[2,64,256]{2,1,0:T(8,128)(2,1)S(1)} collective-permute-done((bf16[2,64,256]{2,1,0:T(8,128)(2,1)S(1)}, bf16[2,64,256]{2,1,0:T(8,128)(2,1)S(1)}, u32[]{:S(2)}, u32[]{:S(2)}) %collective-permute-start.36) | collective-permute-done | bytes 65568 | tf_op jit(solution)/shard_map/ppermute | solution.py:26
  (92 shorter events, 43.0 us)
Async XLA Ops:
  2.2 10.5 %collective-permute-start = (bf16[256,256]{1,0:T(8,128)(2,1)S(1)}, bf16[256,256]{1,0:T(8,128)(2,1)S(1)}, u32[]{:S(2)}, u32[]{:S(2)}) collective-permute-start(bf16[256,256]{1,0:T(8,128)(2,1)S(1)} %fusion.3.refs_9_), channel_id=1, source_target_pairs={{0,4},{1,5},{2,6},{3,7},{4,0},{5,1},{6,2},{7,3},{8,12},{9,13},{10,... | collective-permute-start | bytes 393224 | tf_op jit(solution)/shard_map/ppermute | solution.py:26
  6.3 8.6 %collective-permute-start.4 = (bf16[256,256]{1,0:T(8,128)(2,1)S(1)}, bf16[256,256]{1,0:T(8,128)(2,1)S(1)}, u32[]{:S(2)}, u32[]{:S(2)}) collective-permute-start(bf16[256,256]{1,0:T(8,128)(2,1)S(1)} %fusion.3.refs_9_), channel_id=1, source_target_pairs={{0,1},{1,0},{2,3},{3,2},{4,5},{5,4},{6,7},{7,6},{8,9},{9,8},{10,11... | collective-permute-start | bytes 393224 | tf_op jit(solution)/shard_map/ppermute | solution.py:26
  7.8 14.1 %collective-permute-start.5 = (bf16[256,256]{1,0:T(8,128)(2,1)S(1)}, bf16[256,256]{1,0:T(8,128)(2,1)S(1)}, u32[]{:S(2)}, u32[]{:S(2)}) collective-permute-start(bf16[256,256]{1,0:T(8,128)(2,1)S(1)} %fusion.3.refs_9_), channel_id=1, source_target_pairs={{0,2},{1,3},{2,0},{3,1},{4,6},{5,7},{6,4},{7,5},{8,10},{9,11},{10,... | collective-permute-start | bytes 393224 | tf_op jit(solution)/shard_map/ppermute | solution.py:26
  9.4 14.3 %collective-permute-start.6 = (bf16[256,256]{1,0:T(8,128)(2,1)S(1)}, bf16[256,256]{1,0:T(8,128)(2,1)S(1)}, u32[]{:S(2)}, u32[]{:S(2)}) collective-permute-start(bf16[256,256]{1,0:T(8,128)(2,1)S(1)} %fusion.3.refs_9_), channel_id=1, source_target_pairs={{0,3},{1,2},{2,1},{3,0},{4,7},{5,6},{6,5},{7,4},{8,11},{9,10},{10,... | collective-permute-start | bytes 393224 | tf_op jit(solution)/shard_map/ppermute | solution.py:26
  12.7 17.2 %collective-permute-start.7 = (bf16[256,256]{1,0:T(8,128)(2,1)S(1)}, bf16[256,256]{1,0:T(8,128)(2,1)S(1)}, u32[]{:S(2)}, u32[]{:S(2)}) collective-permute-start(bf16[256,256]{1,0:T(8,128)(2,1)S(1)} %collective-permute-done.refs_10_), channel_id=1, source_target_pairs={{0,1},{1,0},{2,3},{3,2},{4,5},{5,4},{6,7},{7,6},{8,9},{9,8},{10,11... | collective-permute-start | bytes 393224 | tf_op jit(solution)/shard_map/ppermute | solution.py:26
  14.3 15.7 %collective-permute-start.8 = (bf16[256,256]{1,0:T(8,128)(2,1)S(1)}, bf16[256,256]{1,0:T(8,128)(2,1)S(1)}, u32[]{:S(2)}, u32[]{:S(2)}) collective-permute-start(bf16[256,256]{1,0:T(8,128)(2,1)S(1)} %collective-permute-done.refs_10_), channel_id=1, source_target_pairs={{0,2},{1,3},{2,0},{3,1},{4,6},{5,7},{6,4},{7,5},{8,10},{9,11},{10,... | collective-permute-start | bytes 393224 | tf_op jit(solution)/shard_map/ppermute | solution.py:26
  14.9 15.1 %collective-permute-start.9 = (bf16[256,256]{1,0:T(8,128)(2,1)S(1)}, bf16[256,256]{1,0:T(8,128)(2,1)S(1)}, u32[]{:S(2)}, u32[]{:S(2)}) collective-permute-start(bf16[256,256]{1,0:T(8,128)(2,1)S(1)} %collective-permute-done.refs_10_), channel_id=1, source_target_pairs={{0,3},{1,2},{2,1},{3,0},{4,7},{5,6},{6,5},{7,4},{8,11},{9,10},{10,... | collective-permute-start | bytes 393224 | tf_op jit(solution)/shard_map/ppermute | solution.py:26
  31.6 9.4 %collective-permute-start.10 = (bf16[256,256]{1,0:T(8,128)(2,1)S(1)}, bf16[256,256]{1,0:T(8,128)(2,1)S(1)}, u32[]{:S(2)}, u32[]{:S(2)}) collective-permute-start(bf16[256,256]{1,0:T(8,128)(2,1)S(1)} %get-tuple-element.45.refs_3_), channel_id=1, source_target_pairs={{0,4},{1,5},{2,6},{3,7},{4,0},{5,1},{6,2},{7,3},{8,12},{9,13},{10,... | collective-permute-start | bytes 393224 | tf_op jit(solution)/shard_map/ppermute | solution.py:26
  34.1 11.1 %collective-permute-start.11 = (bf16[128,256]{1,0:T(8,128)(2,1)S(1)}, bf16[128,256]{1,0:T(8,128)(2,1)S(1)}, u32[]{:S(2)}, u32[]{:S(2)}) collective-permute-start(bf16[128,256]{1,0:T(8,128)(2,1)S(1)} %get-tuple-element.48), channel_id=1, source_target_pairs={{0,1},{1,0},{2,3},{3,2},{4,5},{5,4},{6,7},{7,6},{8,9},{9,8},{10,11... | collective-permute-start | bytes 196616 | tf_op jit(solution)/shard_map/ppermute | solution.py:26
  38.5 6.7 %collective-permute-start.12 = (bf16[128,256]{1,0:T(8,128)(2,1)S(1)}, bf16[128,256]{1,0:T(8,128)(2,1)S(1)}, u32[]{:S(2)}, u32[]{:S(2)}) collective-permute-start(bf16[128,256]{1,0:T(8,128)(2,1)S(1)} %get-tuple-element.49), channel_id=1, source_target_pairs={{0,2},{1,3},{2,0},{3,1},{4,6},{5,7},{6,4},{7,5},{8,10},{9,11},{10,... | collective-permute-start | bytes 196616 | tf_op jit(solution)/shard_map/ppermute | solution.py:26
  41.1 5.3 %collective-permute-start.13 = (bf16[128,256]{1,0:T(8,128)(2,1)S(1)}, bf16[128,256]{1,0:T(8,128)(2,1)S(1)}, u32[]{:S(2)}, u32[]{:S(2)}) collective-permute-start(bf16[128,256]{1,0:T(8,128)(2,1)S(1)} %get-tuple-element.50), channel_id=1, source_target_pairs={{0,3},{1,2},{2,1},{3,0},{4,7},{5,6},{6,5},{7,4},{8,11},{9,10},{10,... | collective-permute-start | bytes 196616 | tf_op jit(solution)/shard_map/ppermute | solution.py:26
  45.2 5.2 %collective-permute-start.16 = (bf16[128,256]{1,0:T(8,128)(2,1)S(1)}, bf16[128,256]{1,0:T(8,128)(2,1)S(1)}, u32[]{:S(2)}, u32[]{:S(2)}) collective-permute-start(bf16[128,256]{1,0:T(8,128)(2,1)S(1)} %get-tuple-element.53), channel_id=1, source_target_pairs={{0,3},{1,2},{2,1},{3,0},{4,7},{5,6},{6,5},{7,4},{8,11},{9,10},{10,... | collective-permute-start | bytes 196616 | tf_op jit(solution)/shard_map/ppermute | solution.py:26
  55.9 7.7 %collective-permute-start.18 = (bf16[256,256]{1,0:T(8,128)(2,1)S(1)}, bf16[256,256]{1,0:T(8,128)(2,1)S(1)}, u32[]{:S(2)}, u32[]{:S(2)}) collective-permute-start(bf16[256,256]{1,0:T(8,128)(2,1)S(1)} %get-tuple-element.54.refs_9_), channel_id=1, source_target_pairs={{0,4},{1,5},{2,6},{3,7},{4,0},{5,1},{6,2},{7,3},{8,12},{9,13},{10,... | collective-permute-start | bytes 393224 | tf_op jit(solution)/shard_map/ppermute | solution.py:26
  56.0 9.2 %collective-permute-start.19 = (bf16[192,256]{1,0:T(8,128)(2,1)S(1)}, bf16[192,256]{1,0:T(8,128)(2,1)S(1)}, u32[]{:S(2)}, u32[]{:S(2)}) collective-permute-start(bf16[192,256]{1,0:T(8,128)(2,1)S(1)} %get-tuple-element.55), channel_id=1, source_target_pairs={{0,1},{1,0},{2,3},{3,2},{4,5},{5,4},{6,7},{7,6},{8,9},{9,8},{10,11... | collective-permute-start | bytes 294920 | tf_op jit(solution)/shard_map/ppermute | solution.py:26
  56.5 11.4 %collective-permute-start.20 = (bf16[192,256]{1,0:T(8,128)(2,1)S(1)}, bf16[192,256]{1,0:T(8,128)(2,1)S(1)}, u32[]{:S(2)}, u32[]{:S(2)}) collective-permute-start(bf16[192,256]{1,0:T(8,128)(2,1)S(1)} %get-tuple-element.56), channel_id=1, source_target_pairs={{0,2},{1,3},{2,0},{3,1},{4,6},{5,7},{6,4},{7,5},{8,10},{9,11},{10,... | collective-permute-start | bytes 294920 | tf_op jit(solution)/shard_map/ppermute | solution.py:26
  57.5 10.5 %collective-permute-start.21 = (bf16[192,256]{1,0:T(8,128)(2,1)S(1)}, bf16[192,256]{1,0:T(8,128)(2,1)S(1)}, u32[]{:S(2)}, u32[]{:S(2)}) collective-permute-start(bf16[192,256]{1,0:T(8,128)(2,1)S(1)} %get-tuple-element.57), channel_id=1, source_target_pairs={{0,3},{1,2},{2,1},{3,0},{4,7},{5,6},{6,5},{7,4},{8,11},{9,10},{10,... | collective-permute-start | bytes 294920 | tf_op jit(solution)/shard_map/ppermute | solution.py:26
  65.1 6.0 %collective-permute-start.24 = (bf16[128,256]{1,0:T(8,128)(2,1)S(1)}, bf16[128,256]{1,0:T(8,128)(2,1)S(1)}, u32[]{:S(2)}, u32[]{:S(2)}) collective-permute-start(bf16[128,256]{1,0:T(8,128)(2,1)S(1)} %get-tuple-element.60), channel_id=1, source_target_pairs={{0,3},{1,2},{2,1},{3,0},{4,7},{5,6},{6,5},{7,4},{8,11},{9,10},{10,... | collective-permute-start | bytes 196616 | tf_op jit(solution)/shard_map/ppermute | solution.py:26
  73.1 9.9 %collective-permute-start.25 = (bf16[256,256]{1,0:T(8,128)(2,1)S(1)}, bf16[256,256]{1,0:T(8,128)(2,1)S(1)}, u32[]{:S(2)}, u32[]{:S(2)}) collective-permute-start(bf16[256,256]{1,0:T(8,128)(2,1)S(1)} %get-tuple-element.67.refs_3_), channel_id=1, source_target_pairs={{0,4},{1,5},{2,6},{3,7},{4,0},{5,1},{6,2},{7,3},{8,12},{9,13},{10,... | collective-permute-start | bytes 393224 | tf_op jit(solution)/shard_map/ppermute | solution.py:26
  74.6 10.1 %collective-permute-start.26 = (bf16[192,256]{1,0:T(8,128)(2,1)S(1)}, bf16[192,256]{1,0:T(8,128)(2,1)S(1)}, u32[]{:S(2)}, u32[]{:S(2)}) collective-permute-start(bf16[192,256]{1,0:T(8,128)(2,1)S(1)} %get-tuple-element.68), channel_id=1, source_target_pairs={{0,1},{1,0},{2,3},{3,2},{4,5},{5,4},{6,7},{7,6},{8,9},{9,8},{10,11... | collective-permute-start | bytes 294920 | tf_op jit(solution)/shard_map/ppermute | solution.py:26
  76.1 11.1 %collective-permute-start.27 = (bf16[192,256]{1,0:T(8,128)(2,1)S(1)}, bf16[192,256]{1,0:T(8,128)(2,1)S(1)}, u32[]{:S(2)}, u32[]{:S(2)}) collective-permute-start(bf16[192,256]{1,0:T(8,128)(2,1)S(1)} %get-tuple-element.69), channel_id=1, source_target_pairs={{0,2},{1,3},{2,0},{3,1},{4,6},{5,7},{6,4},{7,5},{8,10},{9,11},{10,... | collective-permute-start | bytes 294920 | tf_op jit(solution)/shard_map/ppermute | solution.py:26
  76.7 10.6 %collective-permute-start.28 = (bf16[192,256]{1,0:T(8,128)(2,1)S(1)}, bf16[192,256]{1,0:T(8,128)(2,1)S(1)}, u32[]{:S(2)}, u32[]{:S(2)}) collective-permute-start(bf16[192,256]{1,0:T(8,128)(2,1)S(1)} %get-tuple-element.70), channel_id=1, source_target_pairs={{0,3},{1,2},{2,1},{3,0},{4,7},{5,6},{6,5},{7,4},{8,11},{9,10},{10,... | collective-permute-start | bytes 294920 | tf_op jit(solution)/shard_map/ppermute | solution.py:26
  84.7 5.8 %collective-permute-start.31 = (bf16[128,256]{1,0:T(8,128)(2,1)S(1)}, bf16[128,256]{1,0:T(8,128)(2,1)S(1)}, u32[]{:S(2)}, u32[]{:S(2)}) collective-permute-start(bf16[128,256]{1,0:T(8,128)(2,1)S(1)} %get-tuple-element.73), channel_id=1, source_target_pairs={{0,3},{1,2},{2,1},{3,0},{4,7},{5,6},{6,5},{7,4},{8,11},{9,10},{10,... | collective-permute-start | bytes 196616 | tf_op jit(solution)/shard_map/ppermute | solution.py:26
  95.3 6.0 %collective-permute-start.34 = (bf16[2,64,256]{2,1,0:T(8,128)(2,1)S(1)}, bf16[2,64,256]{2,1,0:T(8,128)(2,1)S(1)}, u32[]{:S(2)}, u32[]{:S(2)}) collective-permute-start(bf16[2,64,256]{2,1,0:T(8,128)(2,1)S(1)} %total.1.refs_0_), channel_id=1, source_target_pairs={{0,1},{1,0},{2,3},{3,2},{4,5},{5,4},{6,7},{7,6},{8,9},{9,8},{10,11... | collective-permute-start | bytes 196616 | tf_op jit(solution)/shard_map/ppermute | solution.py:26
  96.0 5.3 %collective-permute-start.35 = (bf16[2,64,256]{2,1,0:T(8,128)(2,1)S(1)}, bf16[2,64,256]{2,1,0:T(8,128)(2,1)S(1)}, u32[]{:S(2)}, u32[]{:S(2)}) collective-permute-start(bf16[2,64,256]{2,1,0:T(8,128)(2,1)S(1)} %total.1.refs_0_), channel_id=1, source_target_pairs={{0,2},{1,3},{2,0},{3,1},{4,6},{5,7},{6,4},{7,5},{8,10},{9,11},{10,... | collective-permute-start | bytes 196616 | tf_op jit(solution)/shard_map/ppermute | solution.py:26
  (22 other events, 247.0 us)

commit v7 on v6

--- a/solution.py
+++ b/solution.py
@@ -24,6 +24,11 @@
 def swapped(block, k):
     n = lax.axis_size("rows")
     return lax.ppermute(block, "rows", [(i, i ^ k) for i in range(n)])
+
+
+def shared(blocks):
+    moved = {k: swapped(block, k) for k, block in reversed(list(enumerate(blocks, 1)))}
+    return [moved[k] for k in sorted(moved)]
 
 
 def passed_along(block, axis, distance):
@@ -294,13 +299,6 @@
     section_arr = section.astype(jnp.int32).reshape(1)
     counts = tile_count.reshape(1, ticks)
 
-    owner = tile_col[0] // row_tiles
-    named = jnp.where(
-        owner[:, :, None] == jnp.arange(n)[None, None, :], (tile_col[0] % row_tiles)[:, :, None], 0
-    )
-    pick = jnp.max(named, axis=1).reshape(1, ticks * n).astype(jnp.int32)
-    picks = None
-
     handed = []
     passed = None
     weight_acc = [None] * layers
@@ -310,16 +308,10 @@
     layer_cost = cost(2 * rows * width * (width + (n + 1) * tile), (6 + 2 * n) * rows * width)
     small_cost = cost(rows * width, 2 * n * rows * width)
     relay_cost = cost(rows * width, 8 * n * rows * width)
-    densify_tick = functools.partial(
-        densify, me=me_arr, rows=tile_row, cols=tile_col, count=counts, vals=tile_vals,
-        row_tiles=row_tiles, n=n,
-    )
-    adj_next = densify_tick(0)
     for tick in range(ticks):
         final = tick == ticks - 1
         if tick > 0:
             passed = passed_along(handed[-1], "section", -1)
-        adj = adj_next
         image = got = whole = None
         toward = 0.0
         for layer in reversed(range(layers)):
@@ -335,10 +327,25 @@
                 product = jnp.dot(masked, weights[0, layer].T, preferred_element_type=F32)
                 image = ((1.0 - beta) * masked.astype(F32) + beta * product).astype(BF16)
                 far = swapped(image, h)
-                near = [swapped(image, k) for k in range(1, h)]
-                got = [far, *near, *(swapped(far, k) for k in range(1, h))]
-                pick, _ = lax.optimization_barrier((pick, far))
-                picks = [pick] + [swapped(pick, k) for k in range(1, h)]
+                near = shared([image] * (h - 1))
+                cols, _ = lax.optimization_barrier((tile_col[0], image))
+                owner = (cols // row_tiles)[:, :, None] == jnp.arange(n)[None, None, :]
+                pick = jnp.max(jnp.where(owner, (cols % row_tiles)[:, :, None], 0), axis=1)
+                pick = pick.reshape(1, ticks * n).astype(jnp.int32)
+                told = jnp.pad(pick.astype(BF16), ((0, 15), (0, width - ticks * n)))
+                build = functools.partial(
+                    densify, rows=tile_row, cols=tile_col, count=counts, vals=tile_vals,
+                    row_tiles=row_tiles, n=n,
+                )
+                far, adj = lax.optimization_barrier((far, build(0, me_arr)))
+                later, *_ = lax.optimization_barrier((me_arr, *near))
+                adjs = [adj] + [build(t, later) for t in range(1, ticks)]
+                adjs = lax.optimization_barrier(adjs)
+                relayed = shared([jnp.concatenate([far, told], axis=0)] * (h - 1))
+                picks = [pick] + [
+                    block[rows : rows + 1, : ticks * n].astype(jnp.int32) for block in relayed
+                ]
+                got = [far, *near, *relayed]
             else:
                 call = Call()
                 call.give(SMEM, me_arr, section_arr)
@@ -347,7 +354,7 @@
                 if entry:
                     call.give(VMEM, grad_last, passed)
                 else:
-                    call.give(VMEM, adj, image, *got)
+                    call.give(VMEM, adjs[tick], image, *got)
                 if final:
                     call.give(HBM, support)
                     call.give(VMEM, weight_acc[layer])
@@ -375,17 +382,14 @@
                 sends = results.take(h - 1)
                 kept = masked = results.take()
                 far = swapped(image, h)
-                near = [swapped(send, k) for k, send in enumerate(sends, 1)]
-                if layer == 0 and not final:
-                    adj_next = densify_tick(tick + 1)
-                    far, adj_next = lax.optimization_barrier((far, adj_next))
+                near = shared(sends)
                 call = Call()
                 call.give(SMEM, me_arr)
                 call.give(VMEM, far)
                 call.give(SMEM, *picks[1:])
                 call.want(VMEM, (tile, width), BF16, h - 1)
                 relays = call.run(functools.partial(relay_kernel, c), "relay", relay_cost)
-                relayed = [swapped(relay, k) for k, relay in enumerate(relays, 1)]
+                relayed = shared(relays)
                 if final:
                     kept, *_ = lax.optimization_barrier((kept, *relays))
                     call = Call()
@@ -394,8 +398,12 @@
                     (mine,) = call.run(
                         functools.partial(half_sum_kernel, tile), "half_sum", small_cost
                     )
-                    relayed, mine = lax.optimization_barrier((relayed, mine))
-                    weight_sums = [mine, swapped(mine, h), *weight_sums]
+                    if layer == 0:
+                        weight_sums = [mine, swapped(mine, h), *weight_sums]
+                        relayed, weight_sums = lax.optimization_barrier((relayed, weight_sums))
+                    else:
+                        relayed, mine = lax.optimization_barrier((relayed, mine))
+                        weight_sums = [mine, swapped(mine, h), *weight_sums]
                 got = [far, *near, *relayed]
             whole = tick == 0 and entry
             toward = toward + ALPHA * image.astype(F32)
@@ -409,7 +417,7 @@
         c = dict(base, tick=tick, final=final, whole=whole)
         call = Call()
         call.give(SMEM, me_arr, pick)
-        call.give(VMEM, adj, image, *got)
+        call.give(VMEM, adjs[tick], image, *got)
         if final:
             call.give(VMEM, *handed)
             call.want(HBM, (ticks, 1, rows, width), BF16)
@@ -418,14 +426,13 @@
             call.want(VMEM, (rows, width), BF16)
         results = call.run(functools.partial(exit_kernel, c), "exit", layer_cost)
         handed.append(results[0])
-    weight_sums, got = lax.optimization_barrier((weight_sums, got))
     call = Call()
     call.give(VMEM, *weight_sums)
     call.want(VMEM, (layers, chunk, width), BF16)
     (total,) = call.run(functools.partial(total_kernel, layers), "total", small_cost)
     call = Call()
     call.give(SMEM, me_arr)
-    call.give(VMEM, total, *(swapped(total, k) for k in range(1, h)))
+    call.give(VMEM, total, *shared([total] * (h - 1)))
     call.want(HBM, (1, layers, width, width), F32)
     call.scratch = [pltpu.VMEM((layers, width, width), F32), pltpu.SemaphoreType.DMA((layers,))]
     (weight_grad,) = call.run(functools.partial(finish_kernel, h), "finish", small_cost)

time: 105 us -> 97.1 us (0.925)
  waiting for transfers between devices: 32.9 us -> 22.8 us
  starting transfers between devices: 48.4 us -> 49.9 us
  Pallas kernels: 15.5 us -> 16.7 us
    ppermute x36 -> x33, waiting for transfers between devices: 31.4 us -> 21.2 us  [swapped(): return lax.ppermute(block, 'rows', [(i, i ^ k) for i in range(n)])]
    ppermute x36 -> x33, starting transfers between devices: 47.1 us -> 48.6 us  [swapped(): return lax.ppermute(block, 'rows', [(i, i ^ k) for i in range(n)])]
    pallas_call x14, Pallas kernels: 15.5 us -> 16.7 us  [run(): pl.pallas_call(kernel, out_shape=self.outs, in_specs=self.specs, out_spec...]
  transfers between devices with their start and end apart: 37 -> 34, of which waited for: 19 -> 14; matrix products, arithmetic and copies ran while one was open for 2% -> 2% of each run, Pallas kernels for 8% -> 10%
where the time goes in v7:
time: 97.1 us; the launch traced here: 96.4 us
  starting transfers between devices  49.9 us (51%)
  waiting for transfers between devices  22.8 us (23%)
  Pallas kernels  16.7 us (17%)
  local copies, waits for them, and re-layouts  2.26 us (2%)
  matrix products  1.85 us (2%)
  other arithmetic  1.74 us (2%)
  between operations  1.13 us (1%)
    ppermute x33, starting transfers between devices, swapped(): return lax.ppermute(block, 'rows', [(i, i ^ k) for i in range(n)])  48.6 us
    ppermute x33, waiting for transfers between devices, swapped(): return lax.ppermute(block, 'rows', [(i, i ^ k) for i in range(n)])  21.2 us
    pallas_call x14, Pallas kernels, run(): pl.pallas_call(kernel, out_shape=self.outs, in_specs=self.specs, out_spec...  16.7 us
    unnamed x18, local copies, waits for them, and re-layouts  2.05 us
  transfers between devices with their start and end apart: 34, of which 14 were waited for; matrix products, arithmetic and copies ran while one was open for 2% of the time, Pallas kernels for 10%

profile of v7, /device:TPU:0, one launch (start us, length us, event | category | flops | bytes accessed | tf_op | source)
XLA Modules:
  0.0 96.4 jit_solution(16681903606664485876)
XLA Ops:
  2.1 4.1 %collective-permute-start = (bf16[256,256]{1,0:T(8,128)(2,1)S(1)}, bf16[256,256]{1,0:T(8,128)(2,1)S(1)}, u32[]{:S(2)}, u32[]{:S(2)}) collective-permute-start(bf16[256,256]{1,0:T(8,128)(2,1)S(1)} %fusion.3.refs_9_), channel_id=1, source_target_pairs={{0,4},{1,5},{2,6},{3,7},{4,0},{5,1},{6,2},{7,3},{8,12},{9,13},{10,... | collective-permute-start | bytes 393224 | tf_op jit(solution)/shard_map/ppermute | solution.py:26
  9.2 3.2 %densify.2.refs_8_.refs_2_ = bf16[256,1152]{1,0:T(8,128)(2,1)S(1)} custom-call(s32[1]{0:T(128)} %bitcast.refs_0_.me_ref, s32[1,2,96]{2,1,0:T(2,128)S(1)} %copy-done.5, s32[1,2,96]{2,1,0:T(2,128)S(1)} %copy-done.4, s32[1,2]{1,0:T(1,128)S(1)} %bitcast.41, bf16[1,2,96,128,128]{4,3,2,1,0:T(8,128)(2,1)} %refs_4_.3), custom_call_target="tpu_custom_call" | custom-call | flops 31457280 | bytes 3145728 | tf_op jit(solution)/shard_map/densify/pallas_call | solution.py:64
  16.0 1.6 %collective-permute-start.3 = (bf16[256,256]{1,0:T(8,128)(2,1)S(1)}, bf16[256,256]{1,0:T(8,128)(2,1)S(1)}, u32[]{:S(2)}, u32[]{:S(2)}) collective-permute-start(bf16[256,256]{1,0:T(8,128)(2,1)S(1)} %fusion.3.refs_9_), channel_id=1, source_target_pairs={{0,3},{1,2},{2,1},{3,0},{4,7},{5,6},{6,5},{7,4},{8,11},{9,10},{10,... | collective-permute-start | bytes 393224 | tf_op jit(solution)/shard_map/ppermute | solution.py:26
  18.6 3.3 %collective-permute-done.1.refs_11_ = bf16[256,256]{1,0:T(8,128)(2,1)S(1)} collective-permute-done((bf16[256,256]{1,0:T(8,128)(2,1)S(1)}, bf16[256,256]{1,0:T(8,128)(2,1)S(1)}, u32[]{:S(2)}, u32[]{:S(2)}) %collective-permute-start.1) | collective-permute-done | bytes 131104 | tf_op jit(solution)/shard_map/ppermute | solution.py:26
  21.9 2.9 %collective-permute-start.6 = (bf16[272,256]{1,0:T(8,128)(2,1)S(1)}, bf16[272,256]{1,0:T(8,128)(2,1)S(1)}, u32[]{:S(2)}, u32[]{:S(2)}) collective-permute-start(bf16[272,256]{1,0:T(8,128)(2,1)S(1)} %fusion.5), channel_id=1, source_target_pairs={{0,3},{1,2},{2,1},{3,0},{4,7},{5,6},{6,5},{7,4},{8,11},{9,10},{10,... | collective-permute-start | bytes 417800 | tf_op jit(solution)/shard_map/ppermute | solution.py:26
  24.8 3.5 %densify.3.refs_8_.refs_2_ = bf16[256,1152]{1,0:T(8,128)(2,1)S(1)} custom-call(s32[1]{0:T(128)} %bitcast.refs_0_.me_ref, s32[1,2,96]{2,1,0:T(2,128)S(1)} %copy-done.5, s32[1,2,96]{2,1,0:T(2,128)S(1)} %copy-done.4, s32[1,2]{1,0:T(1,128)S(1)} %bitcast.42, bf16[1,2,96,128,128]{4,3,2,1,0:T(8,128)(2,1)} %refs_4_.3), custom_call_target="tpu_custom_call" | custom-call | flops 31457280 | bytes 3145728 | tf_op jit(solution)/shard_map/densify/pallas_call | solution.py:64
  28.4 1.7 %middle.2 = (bf16[256,256]{1,0:T(8,128)(2,1)S(1)}, bf16[128,256]{1,0:T(8,128)(2,1)S(1)}, bf16[128,256]{1,0:T(8,128)(2,1)S(1)}, bf16[128,256]{1,0:T(8,128)(2,1)S(1)}, bf16[256,256]{1,0:T(8,128)(2,1)S(1)}) custom-call(s32[1]{0:T(128)} %bitcast.refs_0_.me_ref, s32[1]{0:T(128)} %bitcast.8.refs_1_, bf16[1,2,2,256,256]{4,3,2,1,0:T(8,128)(2,1)S(1)} %copy-done, ...), custom_call_target="tpu_custom_call" | custom-call | flops 184549376 | bytes 1441792 | tf_op jit(solution)/shard_map/middle/pallas_call | solution.py:64
  30.1 4.3 %collective-permute-start.7 = (bf16[256,256]{1,0:T(8,128)(2,1)S(1)}, bf16[256,256]{1,0:T(8,128)(2,1)S(1)}, u32[]{:S(2)}, u32[]{:S(2)}) collective-permute-start(bf16[256,256]{1,0:T(8,128)(2,1)S(1)} %get-tuple-element.52.refs_3_), channel_id=1, source_target_pairs={{0,4},{1,5},{2,6},{3,7},{4,0},{5,1},{6,2},{7,3},{8,12},{9,13},{10,... | collective-permute-start | bytes 393224 | tf_op jit(solution)/shard_map/ppermute | solution.py:26
  34.4 2.7 %collective-permute-start.9 = (bf16[128,256]{1,0:T(8,128)(2,1)S(1)}, bf16[128,256]{1,0:T(8,128)(2,1)S(1)}, u32[]{:S(2)}, u32[]{:S(2)}) collective-permute-start(bf16[128,256]{1,0:T(8,128)(2,1)S(1)} %get-tuple-element.54), channel_id=1, source_target_pairs={{0,2},{1,3},{2,0},{3,1},{4,6},{5,7},{6,4},{7,5},{8,10},{9,11},{10,... | collective-permute-start | bytes 196616 | tf_op jit(solution)/shard_map/ppermute | solution.py:26
  39.4 1.9 %collective-permute-start.12 = (bf16[128,256]{1,0:T(8,128)(2,1)S(1)}, bf16[128,256]{1,0:T(8,128)(2,1)S(1)}, u32[]{:S(2)}, u32[]{:S(2)}) collective-permute-start(bf16[128,256]{1,0:T(8,128)(2,1)S(1)} %get-tuple-element.57), channel_id=1, source_target_pairs={{0,2},{1,3},{2,0},{3,1},{4,6},{5,7},{6,4},{7,5},{8,10},{9,11},{10,... | collective-permute-start | bytes 196616 | tf_op jit(solution)/shard_map/ppermute | solution.py:26
  41.3 1.6 %collective-permute-start.13 = (bf16[128,256]{1,0:T(8,128)(2,1)S(1)}, bf16[128,256]{1,0:T(8,128)(2,1)S(1)}, u32[]{:S(2)}, u32[]{:S(2)}) collective-permute-start(bf16[128,256]{1,0:T(8,128)(2,1)S(1)} %get-tuple-element.58), channel_id=1, source_target_pairs={{0,3},{1,2},{2,1},{3,0},{4,7},{5,6},{6,5},{7,4},{8,11},{9,10},{10,... | collective-permute-start | bytes 196616 | tf_op jit(solution)/shard_map/ppermute | solution.py:26
  43.7 2.7 %collective-permute-done.13.refs_10_ = bf16[128,256]{1,0:T(8,128)(2,1)S(1)} collective-permute-done((bf16[128,256]{1,0:T(8,128)(2,1)S(1)}, bf16[128,256]{1,0:T(8,128)(2,1)S(1)}, u32[]{:S(2)}, u32[]{:S(2)}) %collective-permute-start.13) | collective-permute-done | bytes 65568 | tf_op jit(solution)/shard_map/ppermute | solution.py:26
  52.0 2.8 %collective-permute-start.15 = (bf16[256,256]{1,0:T(8,128)(2,1)S(1)}, bf16[256,256]{1,0:T(8,128)(2,1)S(1)}, u32[]{:S(2)}, u32[]{:S(2)}) collective-permute-start(bf16[256,256]{1,0:T(8,128)(2,1)S(1)} %get-tuple-element.59.refs_9_), channel_id=1, source_target_pairs={{0,4},{1,5},{2,6},{3,7},{4,0},{5,1},{6,2},{7,3},{8,12},{9,13},{10,... | collective-permute-start | bytes 393224 | tf_op jit(solution)/shard_map/ppermute | solution.py:26
  56.2 2.2 %collective-permute-start.18 = (bf16[192,256]{1,0:T(8,128)(2,1)S(1)}, bf16[192,256]{1,0:T(8,128)(2,1)S(1)}, u32[]{:S(2)}, u32[]{:S(2)}) collective-permute-start(bf16[192,256]{1,0:T(8,128)(2,1)S(1)} %get-tuple-element.62), channel_id=1, source_target_pairs={{0,3},{1,2},{2,1},{3,0},{4,7},{5,6},{6,5},{7,4},{8,11},{9,10},{10,... | collective-permute-start | bytes 294920 | tf_op jit(solution)/shard_map/ppermute | solution.py:26
  58.4 2.6 %collective-permute-done.15.refs_1_.refs_10_ = bf16[256,256]{1,0:T(8,128)(2,1)S(1)} collective-permute-done((bf16[256,256]{1,0:T(8,128)(2,1)S(1)}, bf16[256,256]{1,0:T(8,128)(2,1)S(1)}, u32[]{:S(2)}, u32[]{:S(2)}) %collective-permute-start.15) | collective-permute-done | bytes 131104 | tf_op jit(solution)/shard_map/ppermute | solution.py:26
  63.1 2.1 %collective-permute-start.21 = (bf16[128,256]{1,0:T(8,128)(2,1)S(1)}, bf16[128,256]{1,0:T(8,128)(2,1)S(1)}, u32[]{:S(2)}, u32[]{:S(2)}) collective-permute-start(bf16[128,256]{1,0:T(8,128)(2,1)S(1)} %get-tuple-element.65), channel_id=1, source_target_pairs={{0,3},{1,2},{2,1},{3,0},{4,7},{5,6},{6,5},{7,4},{8,11},{9,10},{10,... | collective-permute-start | bytes 196616 | tf_op jit(solution)/shard_map/ppermute | solution.py:26
  65.4 2.3 %collective-permute-done.19.refs_14_ = bf16[128,256]{1,0:T(8,128)(2,1)S(1)} collective-permute-done((bf16[128,256]{1,0:T(8,128)(2,1)S(1)}, bf16[128,256]{1,0:T(8,128)(2,1)S(1)}, u32[]{:S(2)}, u32[]{:S(2)}) %collective-permute-start.19) | collective-permute-done | bytes 65568 | tf_op jit(solution)/shard_map/ppermute | solution.py:26
  69.0 1.9 %middle.3 = (bf16[256,256]{1,0:T(8,128)(2,1)S(1)}, bf16[192,256]{1,0:T(8,128)(2,1)S(1)}, bf16[192,256]{1,0:T(8,128)(2,1)S(1)}, bf16[192,256]{1,0:T(8,128)(2,1)S(1)}, f32[64,256]{1,0:T(8,128)S(1)}) custom-call(s32[1]{0:T(128)} %bitcast.refs_0_.me_ref, s32[1]{0:T(128)} %bitcast.8.refs_1_, bf16[1,2,2,256,256]{4,3,2,1,0:T(8,128)(2,1)S(1)} %copy-done, ...), custom_call_target="tpu_custom_call" | custom-call | flops 184549376 | bytes 1441792 | tf_op jit(solution)/shard_map/middle/pallas_call | solution.py:64
  73.0 1.8 %collective-permute-start.25 = (bf16[192,256]{1,0:T(8,128)(2,1)S(1)}, bf16[192,256]{1,0:T(8,128)(2,1)S(1)}, u32[]{:S(2)}, u32[]{:S(2)}) collective-permute-start(bf16[192,256]{1,0:T(8,128)(2,1)S(1)} %get-tuple-element.75), channel_id=1, source_target_pairs={{0,3},{1,2},{2,1},{3,0},{4,7},{5,6},{6,5},{7,4},{8,11},{9,10},{10,... | collective-permute-start | bytes 294920 | tf_op jit(solution)/shard_map/ppermute | solution.py:26
  74.8 2.7 %collective-permute-start.30 = (bf16[64,256]{1,0:T(8,128)(2,1)S(1)}, bf16[64,256]{1,0:T(8,128)(2,1)S(1)}, u32[]{:S(2)}, u32[]{:S(2)}) collective-permute-start(bf16[64,256]{1,0:T(8,128)(2,1)S(1)} %half_sum.2.refs_2_), channel_id=1, source_target_pairs={{0,4},{1,5},{2,6},{3,7},{4,0},{5,1},{6,2},{7,3},{8,12},{9,13},{10,... | collective-permute-start | bytes 98312 | tf_op jit(solution)/shard_map/ppermute | solution.py:26
  77.5 2.4 %collective-permute-done.22.refs_1_.refs_4_ = bf16[256,256]{1,0:T(8,128)(2,1)S(1)} collective-permute-done((bf16[256,256]{1,0:T(8,128)(2,1)S(1)}, bf16[256,256]{1,0:T(8,128)(2,1)S(1)}, u32[]{:S(2)}, u32[]{:S(2)}) %collective-permute-start.22) | collective-permute-done | bytes 131104 | tf_op jit(solution)/shard_map/ppermute | solution.py:26
  81.5 2.5 %collective-permute-start.28 = (bf16[128,256]{1,0:T(8,128)(2,1)S(1)}, bf16[128,256]{1,0:T(8,128)(2,1)S(1)}, u32[]{:S(2)}, u32[]{:S(2)}) collective-permute-start(bf16[128,256]{1,0:T(8,128)(2,1)S(1)} %get-tuple-element.78), channel_id=1, source_target_pairs={{0,3},{1,2},{2,1},{3,0},{4,7},{5,6},{6,5},{7,4},{8,11},{9,10},{10,... | collective-permute-start | bytes 196616 | tf_op jit(solution)/shard_map/ppermute | solution.py:26
  84.8 4.2 %collective-permute-done.29.refs_1_ = bf16[64,256]{1,0:T(8,128)(2,1)S(1)} collective-permute-done((bf16[64,256]{1,0:T(8,128)(2,1)S(1)}, bf16[64,256]{1,0:T(8,128)(2,1)S(1)}, u32[]{:S(2)}, u32[]{:S(2)}) %collective-permute-start.29) | collective-permute-done | bytes 32800 | tf_op jit(solution)/shard_map/ppermute | solution.py:26
  90.1 2.5 %collective-permute-start.33 = (bf16[2,64,256]{2,1,0:T(8,128)(2,1)S(1)}, bf16[2,64,256]{2,1,0:T(8,128)(2,1)S(1)}, u32[]{:S(2)}, u32[]{:S(2)}) collective-permute-start(bf16[2,64,256]{2,1,0:T(8,128)(2,1)S(1)} %total.1.refs_0_), channel_id=1, source_target_pairs={{0,3},{1,2},{2,1},{3,0},{4,7},{5,6},{6,5},{7,4},{8,11},{9,10},{10,... | collective-permute-start | bytes 196616 | tf_op jit(solution)/shard_map/ppermute | solution.py:26
  (91 shorter events, 31.8 us)
Async XLA Ops:
  2.1 10.4 %collective-permute-start = (bf16[256,256]{1,0:T(8,128)(2,1)S(1)}, bf16[256,256]{1,0:T(8,128)(2,1)S(1)}, u32[]{:S(2)}, u32[]{:S(2)}) collective-permute-start(bf16[256,256]{1,0:T(8,128)(2,1)S(1)} %fusion.3.refs_9_), channel_id=1, source_target_pairs={{0,4},{1,5},{2,6},{3,7},{4,0},{5,1},{6,2},{7,3},{8,12},{9,13},{10,... | collective-permute-start | bytes 393224 | tf_op jit(solution)/shard_map/ppermute | solution.py:26
  12.6 15.7 %collective-permute-start.4 = (bf16[272,256]{1,0:T(8,128)(2,1)S(1)}, bf16[272,256]{1,0:T(8,128)(2,1)S(1)}, u32[]{:S(2)}, u32[]{:S(2)}) collective-permute-start(bf16[272,256]{1,0:T(8,128)(2,1)S(1)} %fusion.5), channel_id=1, source_target_pairs={{0,1},{1,0},{2,3},{3,2},{4,5},{5,4},{6,7},{7,6},{8,9},{9,8},{10,11... | collective-permute-start | bytes 417800 | tf_op jit(solution)/shard_map/ppermute | solution.py:26
  14.2 7.7 %collective-permute-start.1 = (bf16[256,256]{1,0:T(8,128)(2,1)S(1)}, bf16[256,256]{1,0:T(8,128)(2,1)S(1)}, u32[]{:S(2)}, u32[]{:S(2)}) collective-permute-start(bf16[256,256]{1,0:T(8,128)(2,1)S(1)} %fusion.3.refs_9_), channel_id=1, source_target_pairs={{0,1},{1,0},{2,3},{3,2},{4,5},{5,4},{6,7},{7,6},{8,9},{9,8},{10,11... | collective-permute-start | bytes 393224 | tf_op jit(solution)/shard_map/ppermute | solution.py:26
  14.6 10.1 %collective-permute-start.2 = (bf16[256,256]{1,0:T(8,128)(2,1)S(1)}, bf16[256,256]{1,0:T(8,128)(2,1)S(1)}, u32[]{:S(2)}, u32[]{:S(2)}) collective-permute-start(bf16[256,256]{1,0:T(8,128)(2,1)S(1)} %fusion.3.refs_9_), channel_id=1, source_target_pairs={{0,2},{1,3},{2,0},{3,1},{4,6},{5,7},{6,4},{7,5},{8,10},{9,11},{10,... | collective-permute-start | bytes 393224 | tf_op jit(solution)/shard_map/ppermute | solution.py:26
  16.0 8.8 %collective-permute-start.3 = (bf16[256,256]{1,0:T(8,128)(2,1)S(1)}, bf16[256,256]{1,0:T(8,128)(2,1)S(1)}, u32[]{:S(2)}, u32[]{:S(2)}) collective-permute-start(bf16[256,256]{1,0:T(8,128)(2,1)S(1)} %fusion.3.refs_9_), channel_id=1, source_target_pairs={{0,3},{1,2},{2,1},{3,0},{4,7},{5,6},{6,5},{7,4},{8,11},{9,10},{10,... | collective-permute-start | bytes 393224 | tf_op jit(solution)/shard_map/ppermute | solution.py:26
  17.6 10.6 %collective-permute-start.5 = (bf16[272,256]{1,0:T(8,128)(2,1)S(1)}, bf16[272,256]{1,0:T(8,128)(2,1)S(1)}, u32[]{:S(2)}, u32[]{:S(2)}) collective-permute-start(bf16[272,256]{1,0:T(8,128)(2,1)S(1)} %fusion.5), channel_id=1, source_target_pairs={{0,2},{1,3},{2,0},{3,1},{4,6},{5,7},{6,4},{7,5},{8,10},{9,11},{10,... | collective-permute-start | bytes 417800 | tf_op jit(solution)/shard_map/ppermute | solution.py:26
  21.9 6.5 %collective-permute-start.6 = (bf16[272,256]{1,0:T(8,128)(2,1)S(1)}, bf16[272,256]{1,0:T(8,128)(2,1)S(1)}, u32[]{:S(2)}, u32[]{:S(2)}) collective-permute-start(bf16[272,256]{1,0:T(8,128)(2,1)S(1)} %fusion.5), channel_id=1, source_target_pairs={{0,3},{1,2},{2,1},{3,0},{4,7},{5,6},{6,5},{7,4},{8,11},{9,10},{10,... | collective-permute-start | bytes 417800 | tf_op jit(solution)/shard_map/ppermute | solution.py:26
  30.1 8.7 %collective-permute-start.7 = (bf16[256,256]{1,0:T(8,128)(2,1)S(1)}, bf16[256,256]{1,0:T(8,128)(2,1)S(1)}, u32[]{:S(2)}, u32[]{:S(2)}) collective-permute-start(bf16[256,256]{1,0:T(8,128)(2,1)S(1)} %get-tuple-element.52.refs_3_), channel_id=1, source_target_pairs={{0,4},{1,5},{2,6},{3,7},{4,0},{5,1},{6,2},{7,3},{8,12},{9,13},{10,... | collective-permute-start | bytes 393224 | tf_op jit(solution)/shard_map/ppermute | solution.py:26
  34.4 6.9 %collective-permute-start.8 = (bf16[128,256]{1,0:T(8,128)(2,1)S(1)}, bf16[128,256]{1,0:T(8,128)(2,1)S(1)}, u32[]{:S(2)}, u32[]{:S(2)}) collective-permute-start(bf16[128,256]{1,0:T(8,128)(2,1)S(1)} %get-tuple-element.53), channel_id=1, source_target_pairs={{0,1},{1,0},{2,3},{3,2},{4,5},{5,4},{6,7},{7,6},{8,9},{9,8},{10,11... | collective-permute-start | bytes 196616 | tf_op jit(solution)/shard_map/ppermute | solution.py:26
  34.4 8.5 %collective-permute-start.9 = (bf16[128,256]{1,0:T(8,128)(2,1)S(1)}, bf16[128,256]{1,0:T(8,128)(2,1)S(1)}, u32[]{:S(2)}, u32[]{:S(2)}) collective-permute-start(bf16[128,256]{1,0:T(8,128)(2,1)S(1)} %get-tuple-element.54), channel_id=1, source_target_pairs={{0,2},{1,3},{2,0},{3,1},{4,6},{5,7},{6,4},{7,5},{8,10},{9,11},{10,... | collective-permute-start | bytes 196616 | tf_op jit(solution)/shard_map/ppermute | solution.py:26
  52.0 9.0 %collective-permute-start.15 = (bf16[256,256]{1,0:T(8,128)(2,1)S(1)}, bf16[256,256]{1,0:T(8,128)(2,1)S(1)}, u32[]{:S(2)}, u32[]{:S(2)}) collective-permute-start(bf16[256,256]{1,0:T(8,128)(2,1)S(1)} %get-tuple-element.59.refs_9_), channel_id=1, source_target_pairs={{0,4},{1,5},{2,6},{3,7},{4,0},{5,1},{6,2},{7,3},{8,12},{9,13},{10,... | collective-permute-start | bytes 393224 | tf_op jit(solution)/shard_map/ppermute | solution.py:26
  54.8 8.3 %collective-permute-start.16 = (bf16[192,256]{1,0:T(8,128)(2,1)S(1)}, bf16[192,256]{1,0:T(8,128)(2,1)S(1)}, u32[]{:S(2)}, u32[]{:S(2)}) collective-permute-start(bf16[192,256]{1,0:T(8,128)(2,1)S(1)} %get-tuple-element.60), channel_id=1, source_target_pairs={{0,1},{1,0},{2,3},{3,2},{4,5},{5,4},{6,7},{7,6},{8,9},{9,8},{10,11... | collective-permute-start | bytes 294920 | tf_op jit(solution)/shard_map/ppermute | solution.py:26
  56.1 9.3 %collective-permute-start.17 = (bf16[192,256]{1,0:T(8,128)(2,1)S(1)}, bf16[192,256]{1,0:T(8,128)(2,1)S(1)}, u32[]{:S(2)}, u32[]{:S(2)}) collective-permute-start(bf16[192,256]{1,0:T(8,128)(2,1)S(1)} %get-tuple-element.61), channel_id=1, source_target_pairs={{0,2},{1,3},{2,0},{3,1},{4,6},{5,7},{6,4},{7,5},{8,10},{9,11},{10,... | collective-permute-start | bytes 294920 | tf_op jit(solution)/shard_map/ppermute | solution.py:26
  56.2 9.2 %collective-permute-start.18 = (bf16[192,256]{1,0:T(8,128)(2,1)S(1)}, bf16[192,256]{1,0:T(8,128)(2,1)S(1)}, u32[]{:S(2)}, u32[]{:S(2)}) collective-permute-start(bf16[192,256]{1,0:T(8,128)(2,1)S(1)} %get-tuple-element.62), channel_id=1, source_target_pairs={{0,3},{1,2},{2,1},{3,0},{4,7},{5,6},{6,5},{7,4},{8,11},{9,10},{10,... | collective-permute-start | bytes 294920 | tf_op jit(solution)/shard_map/ppermute | solution.py:26
  61.6 6.1 %collective-permute-start.19 = (bf16[128,256]{1,0:T(8,128)(2,1)S(1)}, bf16[128,256]{1,0:T(8,128)(2,1)S(1)}, u32[]{:S(2)}, u32[]{:S(2)}) collective-permute-start(bf16[128,256]{1,0:T(8,128)(2,1)S(1)} %get-tuple-element.63), channel_id=1, source_target_pairs={{0,1},{1,0},{2,3},{3,2},{4,5},{5,4},{6,7},{7,6},{8,9},{9,8},{10,11... | collective-permute-start | bytes 196616 | tf_op jit(solution)/shard_map/ppermute | solution.py:26
  70.9 9.0 %collective-permute-start.22 = (bf16[256,256]{1,0:T(8,128)(2,1)S(1)}, bf16[256,256]{1,0:T(8,128)(2,1)S(1)}, u32[]{:S(2)}, u32[]{:S(2)}) collective-permute-start(bf16[256,256]{1,0:T(8,128)(2,1)S(1)} %get-tuple-element.72.refs_3_), channel_id=1, source_target_pairs={{0,4},{1,5},{2,6},{3,7},{4,0},{5,1},{6,2},{7,3},{8,12},{9,13},{10,... | collective-permute-start | bytes 393224 | tf_op jit(solution)/shard_map/ppermute | solution.py:26
  71.3 10.2 %collective-permute-start.23 = (bf16[192,256]{1,0:T(8,128)(2,1)S(1)}, bf16[192,256]{1,0:T(8,128)(2,1)S(1)}, u32[]{:S(2)}, u32[]{:S(2)}) collective-permute-start(bf16[192,256]{1,0:T(8,128)(2,1)S(1)} %get-tuple-element.73), channel_id=1, source_target_pairs={{0,1},{1,0},{2,3},{3,2},{4,5},{5,4},{6,7},{7,6},{8,9},{9,8},{10,11... | collective-permute-start | bytes 294920 | tf_op jit(solution)/shard_map/ppermute | solution.py:26
  72.7 8.9 %collective-permute-start.24 = (bf16[192,256]{1,0:T(8,128)(2,1)S(1)}, bf16[192,256]{1,0:T(8,128)(2,1)S(1)}, u32[]{:S(2)}, u32[]{:S(2)}) collective-permute-start(bf16[192,256]{1,0:T(8,128)(2,1)S(1)} %get-tuple-element.74), channel_id=1, source_target_pairs={{0,2},{1,3},{2,0},{3,1},{4,6},{5,7},{6,4},{7,5},{8,10},{9,11},{10,... | collective-permute-start | bytes 294920 | tf_op jit(solution)/shard_map/ppermute | solution.py:26
  73.0 11.1 %collective-permute-start.25 = (bf16[192,256]{1,0:T(8,128)(2,1)S(1)}, bf16[192,256]{1,0:T(8,128)(2,1)S(1)}, u32[]{:S(2)}, u32[]{:S(2)}) collective-permute-start(bf16[192,256]{1,0:T(8,128)(2,1)S(1)} %get-tuple-element.75), channel_id=1, source_target_pairs={{0,3},{1,2},{2,1},{3,0},{4,7},{5,6},{6,5},{7,4},{8,11},{9,10},{10,... | collective-permute-start | bytes 294920 | tf_op jit(solution)/shard_map/ppermute | solution.py:26
  74.8 10.0 %collective-permute-start.30 = (bf16[64,256]{1,0:T(8,128)(2,1)S(1)}, bf16[64,256]{1,0:T(8,128)(2,1)S(1)}, u32[]{:S(2)}, u32[]{:S(2)}) collective-permute-start(bf16[64,256]{1,0:T(8,128)(2,1)S(1)} %half_sum.2.refs_2_), channel_id=1, source_target_pairs={{0,4},{1,5},{2,6},{3,7},{4,0},{5,1},{6,2},{7,3},{8,12},{9,13},{10,... | collective-permute-start | bytes 98312 | tf_op jit(solution)/shard_map/ppermute | solution.py:26
  80.5 8.5 %collective-permute-start.26 = (bf16[128,256]{1,0:T(8,128)(2,1)S(1)}, bf16[128,256]{1,0:T(8,128)(2,1)S(1)}, u32[]{:S(2)}, u32[]{:S(2)}) collective-permute-start(bf16[128,256]{1,0:T(8,128)(2,1)S(1)} %get-tuple-element.76), channel_id=1, source_target_pairs={{0,1},{1,0},{2,3},{3,2},{4,5},{5,4},{6,7},{7,6},{8,9},{9,8},{10,11... | collective-permute-start | bytes 196616 | tf_op jit(solution)/shard_map/ppermute | solution.py:26
  81.5 7.5 %collective-permute-start.27 = (bf16[128,256]{1,0:T(8,128)(2,1)S(1)}, bf16[128,256]{1,0:T(8,128)(2,1)S(1)}, u32[]{:S(2)}, u32[]{:S(2)}) collective-permute-start(bf16[128,256]{1,0:T(8,128)(2,1)S(1)} %get-tuple-element.77), channel_id=1, source_target_pairs={{0,2},{1,3},{2,0},{3,1},{4,6},{5,7},{6,4},{7,5},{8,10},{9,11},{10,... | collective-permute-start | bytes 196616 | tf_op jit(solution)/shard_map/ppermute | solution.py:26
  81.5 7.5 %collective-permute-start.28 = (bf16[128,256]{1,0:T(8,128)(2,1)S(1)}, bf16[128,256]{1,0:T(8,128)(2,1)S(1)}, u32[]{:S(2)}, u32[]{:S(2)}) collective-permute-start(bf16[128,256]{1,0:T(8,128)(2,1)S(1)} %get-tuple-element.78), channel_id=1, source_target_pairs={{0,3},{1,2},{2,1},{3,0},{4,7},{5,6},{6,5},{7,4},{8,11},{9,10},{10,... | collective-permute-start | bytes 196616 | tf_op jit(solution)/shard_map/ppermute | solution.py:26
  89.0 6.0 %collective-permute-start.31 = (bf16[2,64,256]{2,1,0:T(8,128)(2,1)S(1)}, bf16[2,64,256]{2,1,0:T(8,128)(2,1)S(1)}, u32[]{:S(2)}, u32[]{:S(2)}) collective-permute-start(bf16[2,64,256]{2,1,0:T(8,128)(2,1)S(1)} %total.1.refs_0_), channel_id=1, source_target_pairs={{0,1},{1,0},{2,3},{3,2},{4,5},{5,4},{6,7},{7,6},{8,9},{9,8},{10,11... | collective-permute-start | bytes 196616 | tf_op jit(solution)/shard_map/ppermute | solution.py:26
  (19 other events, 224.4 us)

commit v8 on v7

--- a/solution.py
+++ b/solution.py
@@ -75,10 +75,10 @@
 
 
 def densify_kernel(tick, row_tiles, n, chunks, *refs):
-    me_ref, rows_ref, cols_ref, count_ref, vals_ref, out_ref, vals, acc, sems = refs
+    rows_ref, cols_ref, count_ref, vals_ref, out_ref, vals, acc, sems = refs
     entries, tile = vals.shape[:2]
     chunk = entries // chunks
-    me = me_ref[0]
+    me = lax.axis_index("rows")
     copies = []
     for c in range(chunks):
         part = pl.ds(c * chunk, chunk)
@@ -105,12 +105,12 @@
     out_ref[...] = acc[...].astype(BF16)
 
 
-def densify(tick, me, rows, cols, count, vals, row_tiles, n):
+def densify(tick, rows, cols, count, vals, row_tiles, n):
     entries, tile = vals.shape[2:4]
     chunks = 4 if entries % 4 == 0 else 1
     shape = (row_tiles * tile, (n + row_tiles - 1) * tile)
     call = Call()
-    call.give(SMEM, me, rows, cols, count)
+    call.give(SMEM, rows, cols, count)
     call.give(HBM, vals)
     call.want(VMEM, shape, BF16)
     call.scratch = [
@@ -131,27 +131,45 @@
     return ref[pl.ds(pl.multiple_of(index * tile, tile), tile), :]
 
 
+def name_kernel(n, row_tiles, cols_ref, *out_refs):
+    me = lax.axis_index("rows")
+    ticks = cols_ref.shape[1]
+    width = out_refs[0].shape[1]
+    for t in range(ticks):
+        cols = cols_ref[0, t : t + 1, :]
+
+        def named(k):
+            index = cols - jnp.bitwise_xor(me, k) * row_tiles
+            index = jnp.where((index >= 0) & (index < row_tiles), index, 0)
+            most = jnp.max(index.astype(F32), axis=1, keepdims=True)
+            return jnp.broadcast_to(most, (1, width))
+
+        for k in range(1, n // 2):
+            out_refs[k][2 * t : 2 * t + 1, :] = named(k)
+            out_refs[k][2 * t + 1 : 2 * t + 2, :] = named(n // 2 + k)
+        out_refs[0][t : t + 1, :] = named(n // 2)
+
+
+def chosen(image_ref, row, rows, tile):
+    index = jnp.broadcast_to(row.astype(BF16), (tile, row.shape[1]))
+    result = image_ref[:tile, :]
+    for i in range(1, rows // tile):
+        result = jnp.where(index > i - 0.5, image_ref[i * tile : (i + 1) * tile, :], result)
+    return result
+
+
 def take_got(refs, n):
-    far, near, relayed = refs.take(), refs.take(n // 2 - 1), refs.take(n // 2 - 1)
-    return far, near, relayed
-
-
-def spread_of(adj_ref, own_ref, got, pick_ref, me, c):
-    n, tile = c["n"], c["tile"]
+    return refs.take(), refs.take(n // 2 - 1), refs.take(n // 2 - 1)
+
+
+def spread_of(adj_ref, own_ref, got, names_ref, c):
+    tile, rows = c["tile"], c["rows"]
     far, near, relayed = got
-
-    def named(ref, k):
-        index = pick_ref[0, c["tick"] * n + jnp.bitwise_xor(me, k)]
-        return tile_at(ref, index, tile)
-
-    if c["whole"]:
-        near = [named(ref, k) for k, ref in enumerate(near, 1)]
-        relayed = [named(ref, n // 2 + k) for k, ref in enumerate(relayed, 1)]
-    else:
-        near = [ref[:tile, :] for ref in near]
-        relayed = [ref[...] for ref in relayed]
+    far = chosen(far, names_ref[c["tick"] : c["tick"] + 1, :], rows, tile)
+    near = [ref[:tile, :] for ref in near]
+    relayed = [ref[...] for ref in relayed]
     blocks = jnp.concatenate(
-        [own_ref[:tile, :]] + near + [named(far, n // 2)] + relayed + [own_ref[tile:, :]], axis=0
+        [own_ref[:tile, :]] + near + [far] + relayed + [own_ref[tile:, :]], axis=0
     )
     total = jnp.dot(adj_ref[...], blocks, preferred_element_type=F32)
     return ((1.0 - ALPHA) * total).astype(BF16)
@@ -161,8 +179,8 @@
     refs = Refs(refs)
     n, tile, width, chunk = c["n"], c["tile"], c["width"], c["chunk"]
     h = n // 2
-    me_ref, section_ref, preact_all, weight_all = refs.take(4)
-    picks = refs.take(h)
+    preact_all, weight_all, names_ref = refs.take(3)
+    asked = refs.take(h - 1)
     if c["entry"]:
         last_ref, passed_ref = refs.take(2)
     else:
@@ -175,8 +193,7 @@
     out_ref = refs.take()
     preact_ref, weight_ref, load_sems = refs.take(3)
 
-    me = me_ref[0]
-    section = section_ref[0]
+    section = lax.axis_index("section")
     loads = [
         (preact_all.at[0, c["tick"], c["layer"]], preact_ref),
         (weight_all.at[0, c["layer"]], weight_ref),
@@ -190,7 +207,7 @@
     step = (c["layers"] * section + c["layer"] + 1).astype(F32)
     beta = jnp.log(BETA_SCALE / jnp.full((1, width), step, F32) + 1.0)
     if not c["entry"]:
-        grad = spread_of(adj_ref, own_ref, got, picks[0], me, c)
+        grad = spread_of(adj_ref, own_ref, got, names_ref, c)
     for load in loads:
         load.wait()
     if c["entry"]:
@@ -202,14 +219,15 @@
     )
     image = ((1.0 - beta) * masked.astype(F32) + beta * product).astype(BF16)
     image_ref[...] = image
-    for k in range(1, h):
-        sends[k - 1][:tile, :] = tile_at(image_ref, picks[k][0, c["tick"] * n + me], tile)
+    for send, asked_ref in zip(sends, asked):
+        row = asked_ref[2 * c["tick"] : 2 * c["tick"] + 1, :]
+        send[:tile, :] = chosen(image_ref, row, c["rows"], tile)
     if c["final"]:
         term = lax.dot_general(
             support_ref[...], masked, (((0,), (0,)), ((), ())), preferred_element_type=F32
         )
         term_ref[...] = acc_ref[...] + beta * term
-        place = lax.rem(me, h)
+        place = lax.rem(lax.axis_index("rows"), h)
         for k in range(1, h):
             sends[k - 1][tile : tile + chunk, :] = tile_at(
                 term_ref, jnp.bitwise_xor(place, k), chunk
@@ -219,17 +237,11 @@
         out_ref[...] = masked
 
 
-def relay_kernel(c, *refs):
-    refs = Refs(refs)
-    n, tile = c["n"], c["tile"]
-    h = n // 2
-    me_ref, far_ref = refs.take(2)
-    picks = refs.take(h - 1)
-    sends = refs.take(h - 1)
-    me = me_ref[0]
-    for k in range(1, h):
-        index = picks[k - 1][0, c["tick"] * n + jnp.bitwise_xor(me, h)]
-        sends[k - 1][...] = tile_at(far_ref, index, tile)
+def select_kernel(c, first, image_ref, *refs):
+    count = c["n"] // 2 - 1
+    for asked_ref, send in zip(refs[:count], refs[count:]):
+        row = 2 * c["tick"] + first
+        send[...] = chosen(image_ref, asked_ref[row : row + 1, :], c["rows"], c["tile"])
 
 
 def half_sum_kernel(tile, kept_ref, *refs):
@@ -248,10 +260,10 @@
 
 def exit_kernel(c, *refs):
     refs = Refs(refs)
-    me_ref, pick_ref, adj_ref, own_ref = refs.take(4)
+    names_ref, adj_ref, own_ref = refs.take(3)
     got = take_got(refs, c["n"])
     if not c["final"]:
-        refs.take()[...] = spread_of(adj_ref, own_ref, got, pick_ref, me_ref[0], c)
+        refs.take()[...] = spread_of(adj_ref, own_ref, got, names_ref, c)
         return
     handed = refs.take(c["tick"])
     out_ref, hold_ref, sems = refs.take(3)
@@ -261,16 +273,16 @@
     ]
     for copy in copies[:-1]:
         copy.start()
-    hold_ref[...] = spread_of(adj_ref, own_ref, got, pick_ref, me_ref[0], c)
+    hold_ref[...] = spread_of(adj_ref, own_ref, got, names_ref, c)
     copies[-1].start()
     for copy in copies:
         copy.wait()
 
 
-def finish_kernel(h, me_ref, *refs):
+def finish_kernel(h, *refs):
     sums, (out_ref, hold_ref, sems) = refs[:h], refs[h:]
     layers, chunk, _ = sums[0].shape
-    place = lax.rem(me_ref[0], h)
+    place = lax.rem(lax.axis_index("rows"), h)
     copies = []
     for layer in range(layers):
         for k in range(h):
@@ -285,7 +297,6 @@
 
 def shards(grad_in, grad_last, support, preact, weights, tile_vals, tile_row, tile_col, tile_count):
     section = lax.axis_index("section")
-    me = lax.axis_index("rows")
     n = lax.axis_size("rows")
     h = n // 2
     sections = lax.axis_size("section")
@@ -295,8 +306,6 @@
     tile = tile_vals.shape[-1]
     row_tiles = rows // tile
     chunk = width // h
-    me_arr = me.astype(jnp.int32).reshape(1)
-    section_arr = section.astype(jnp.int32).reshape(1)
     counts = tile_count.reshape(1, ticks)
 
     handed = []
@@ -304,53 +313,47 @@
     weight_acc = [None] * layers
     weight_sums = []
     initial = []
-    base = dict(n=n, tile=tile, width=width, layers=layers, sections=sections, chunk=chunk)
+    base = dict(n=n, tile=tile, rows=rows, width=width, layers=layers, sections=sections, chunk=chunk)
     layer_cost = cost(2 * rows * width * (width + (n + 1) * tile), (6 + 2 * n) * rows * width)
     small_cost = cost(rows * width, 2 * n * rows * width)
     relay_cost = cost(rows * width, 8 * n * rows * width)
+    call = Call()
+    call.give(VMEM, tile_col)
+    call.want(VMEM, (ticks, width), F32)
+    call.want(VMEM, (2 * ticks, width), F32, h - 1)
+    names, *asking = call.run(functools.partial(name_kernel, n, row_tiles), "name", small_cost)
+    asked = shared(asking)
+
+    def select(c, first, block):
+        call = Call()
+        call.give(VMEM, block, *asked)
+        call.want(VMEM, (tile, width), BF16, h - 1)
+        return call.run(functools.partial(select_kernel, c, first), "select", small_cost)
+
+    adjs = [None] * ticks
     for tick in range(ticks):
         final = tick == ticks - 1
         if tick > 0:
             passed = passed_along(handed[-1], "section", -1)
-        image = got = whole = None
+        image = got = None
         toward = 0.0
         for layer in reversed(range(layers)):
             entry = layer == layers - 1
             beta = jnp.log(BETA_SCALE / (layers * section + layer + 1).astype(F32) + 1.0)
             c = dict(
-                base, layer=layer, tick=tick, entry=entry, final=final, whole=whole
+                base, layer=layer, tick=tick, entry=entry, final=final
             )
-            if tick == 0 and entry:
-                masked = jnp.where(
-                    preact[0, tick, layer] > 0, grad_in[0], jnp.zeros_like(grad_in[0])
-                )
+            first = tick == 0 and entry
+            if first:
+                grad, *_ = lax.optimization_barrier((grad_in[0], *asking))
+                masked = jnp.where(preact[0, tick, layer] > 0, grad, jnp.zeros_like(grad))
                 product = jnp.dot(masked, weights[0, layer].T, preferred_element_type=F32)
                 image = ((1.0 - beta) * masked.astype(F32) + beta * product).astype(BF16)
-                far = swapped(image, h)
-                near = shared([image] * (h - 1))
-                cols, _ = lax.optimization_barrier((tile_col[0], image))
-                owner = (cols // row_tiles)[:, :, None] == jnp.arange(n)[None, None, :]
-                pick = jnp.max(jnp.where(owner, (cols % row_tiles)[:, :, None], 0), axis=1)
-                pick = pick.reshape(1, ticks * n).astype(jnp.int32)
-                told = jnp.pad(pick.astype(BF16), ((0, 15), (0, width - ticks * n)))
-                build = functools.partial(
-                    densify, rows=tile_row, cols=tile_col, count=counts, vals=tile_vals,
-                    row_tiles=row_tiles, n=n,
-                )
-                far, adj = lax.optimization_barrier((far, build(0, me_arr)))
-                later, *_ = lax.optimization_barrier((me_arr, *near))
-                adjs = [adj] + [build(t, later) for t in range(1, ticks)]
-                adjs = lax.optimization_barrier(adjs)
-                relayed = shared([jnp.concatenate([far, told], axis=0)] * (h - 1))
-                picks = [pick] + [
-                    block[rows : rows + 1, : ticks * n].astype(jnp.int32) for block in relayed
-                ]
-                got = [far, *near, *relayed]
+                sends = select(c, 0, image)
             else:
                 call = Call()
-                call.give(SMEM, me_arr, section_arr)
                 call.give(HBM, preact, weights)
-                call.give(SMEM, *picks)
+                call.give(VMEM, names, *asked)
                 if entry:
                     call.give(VMEM, grad_last, passed)
                 else:
@@ -381,31 +384,34 @@
                 image = results.take()
                 sends = results.take(h - 1)
                 kept = masked = results.take()
-                far = swapped(image, h)
-                near = shared(sends)
+            far = swapped(image, h)
+            near = shared(sends)
+            if first:
+                far, adjs[0] = lax.optimization_barrier((far, densify(0, tile_row, tile_col, counts, tile_vals, row_tiles, n)))
+            relays = select(c, 1, far)
+            relayed = shared(relays)
+            if first:
+                cols, *_ = lax.optimization_barrier((tile_col, *near))
+                adjs[1:] = [
+                    densify(t, tile_row, cols, counts, tile_vals, row_tiles, n)
+                    for t in range(1, ticks)
+                ]
+                adjs = list(lax.optimization_barrier(adjs))
+            if final:
+                kept, *_ = lax.optimization_barrier((kept, *relays))
                 call = Call()
-                call.give(SMEM, me_arr)
-                call.give(VMEM, far)
-                call.give(SMEM, *picks[1:])
-                call.want(VMEM, (tile, width), BF16, h - 1)
-                relays = call.run(functools.partial(relay_kernel, c), "relay", relay_cost)
-                relayed = shared(relays)
-                if final:
-                    kept, *_ = lax.optimization_barrier((kept, *relays))
-                    call = Call()
-                    call.give(VMEM, kept, *near)
-                    call.want(VMEM, (chunk, width), BF16)
-                    (mine,) = call.run(
-                        functools.partial(half_sum_kernel, tile), "half_sum", small_cost
-                    )
-                    if layer == 0:
-                        weight_sums = [mine, swapped(mine, h), *weight_sums]
-                        relayed, weight_sums = lax.optimization_barrier((relayed, weight_sums))
-                    else:
-                        relayed, mine = lax.optimization_barrier((relayed, mine))
-                        weight_sums = [mine, swapped(mine, h), *weight_sums]
-                got = [far, *near, *relayed]
-            whole = tick == 0 and entry
+                call.give(VMEM, kept, *near)
+                call.want(VMEM, (chunk, width), BF16)
+                (mine,) = call.run(
+                    functools.partial(half_sum_kernel, tile), "half_sum", small_cost
+                )
+                if layer == 0:
+                    weight_sums = [mine, swapped(mine, h), *weight_sums]
+                    relayed, weight_sums = lax.optimization_barrier((relayed, weight_sums))
+                else:
+                    relayed, mine = lax.optimization_barrier((relayed, mine))
+                    weight_sums = [mine, swapped(mine, h), *weight_sums]
+            got = [far, *near, *relayed]
             toward = toward + ALPHA * image.astype(F32)
             if not final:
                 term = beta * jnp.dot(
@@ -414,10 +420,9 @@
                 old = weight_acc[layer]
                 weight_acc[layer] = term if old is None else old + term
         initial.append(toward)
-        c = dict(base, tick=tick, final=final, whole=whole)
+        c = dict(base, tick=tick, final=final)
         call = Call()
-        call.give(SMEM, me_arr, pick)
-        call.give(VMEM, adjs[tick], image, *got)
+        call.give(VMEM, names, adjs[tick], image, *got)
         if final:
             call.give(VMEM, *handed)
             call.want(HBM, (ticks, 1, rows, width), BF16)
@@ -431,7 +436,6 @@
     call.want(VMEM, (layers, chunk, width), BF16)
     (total,) = call.run(functools.partial(total_kernel, layers), "total", small_cost)
     call = Call()
-    call.give(SMEM, me_arr)
     call.give(VMEM, total, *shared([total] * (h - 1)))
     call.want(HBM, (1, layers, width, width), F32)
     call.scratch = [pltpu.VMEM((layers, width, width), F32), pltpu.SemaphoreType.DMA((layers,))]

time: 97.1 us -> 93.6 us (0.964)
  waiting for transfers between devices: 22.8 us -> 30 us
  Pallas kernels: 16.7 us -> 11.6 us
  starting transfers between devices: 49.9 us -> 45 us
    ppermute x33 -> x36, waiting for transfers between devices: 21.2 us -> 28.4 us  [swapped(): return lax.ppermute(block, 'rows', [(i, i ^ k) for i in range(n)])]
    pallas_call x14 -> x17, Pallas kernels: 16.7 us -> 11.6 us  [run(): pl.pallas_call(kernel, out_shape=self.outs, in_specs=self.specs, out_spec...]
    ppermute x33 -> x36, starting transfers between devices: 48.6 us -> 43.7 us  [swapped(): return lax.ppermute(block, 'rows', [(i, i ^ k) for i in range(n)])]
  transfers between devices with their start and end apart: 34 -> 37, of which waited for: 14 -> 16; matrix products, arithmetic and copies ran while one was open for 2% -> 2% of each run, Pallas kernels for 10% -> 8%
where the time goes in v8:
time: 93.6 us; the launch traced here: 93.2 us
  starting transfers between devices  45 us (48%)
  waiting for transfers between devices  30 us (32%)
  Pallas kernels  11.6 us (12%)
  local copies, waits for them, and re-layouts  2.84 us (3%)
  matrix products  1.84 us (2%)
  between operations  1.12 us (1%)
    ppermute x36, starting transfers between devices, swapped(): return lax.ppermute(block, 'rows', [(i, i ^ k) for i in range(n)])  43.7 us
    ppermute x36, waiting for transfers between devices, swapped(): return lax.ppermute(block, 'rows', [(i, i ^ k) for i in range(n)])  28.4 us
    pallas_call x17, Pallas kernels, run(): pl.pallas_call(kernel, out_shape=self.outs, in_specs=self.specs, out_spec...  11.6 us
    unnamed x18, local copies, waits for them, and re-layouts  2.71 us
  transfers between devices with their start and end apart: 37, of which 16 were waited for; matrix products, arithmetic and copies ran while one was open for 2% of the time, Pallas kernels for 8%

profile of v8, /device:TPU:0, one launch (start us, length us, event | category | flops | bytes accessed | tf_op | source)
XLA Modules:
  0.0 93.2 jit_solution(17424407970262215565)
XLA Ops:
  2.9 4.1 %collective-permute-start = (bf16[256,256]{1,0:T(8,128)(2,1)S(1)}, bf16[256,256]{1,0:T(8,128)(2,1)S(1)}, u32[]{:S(2)}, u32[]{:S(2)}) collective-permute-start(bf16[256,256]{1,0:T(8,128)(2,1)S(1)} %fusion.3.image_ref.refs_7_), channel_id=1, source_target_pairs={{0,4},{1,5},{2,6},{3,7},{4,0},{5,1},{6,2},{7,3},{8,12},{9,13},{10,... | collective-permute-start | bytes 393224 | tf_op jit(solution)/shard_map/ppermute | solution.py:26
  7.0 1.5 %collective-permute-start.1 = (f32[4,256]{1,0:T(4,128)S(1)}, f32[4,256]{1,0:T(4,128)S(1)}, u32[]{:S(2)}, u32[]{:S(2)}) collective-permute-start(f32[4,256]{1,0:T(4,128)S(1)} %get-tuple-element.57), channel_id=1, source_target_pairs={{0,1},{1,0},{2,3},{3,2},{4,5},{5,4},{6,7},{7,6},{8,9},{9,8},{10,11... | collective-permute-start | bytes 12296 | tf_op jit(solution)/shard_map/ppermute | solution.py:26
  8.5 1.6 %collective-permute-start.2 = (f32[4,256]{1,0:T(4,128)S(1)}, f32[4,256]{1,0:T(4,128)S(1)}, u32[]{:S(2)}, u32[]{:S(2)}) collective-permute-start(f32[4,256]{1,0:T(4,128)S(1)} %get-tuple-element.58), channel_id=1, source_target_pairs={{0,2},{1,3},{2,0},{3,1},{4,6},{5,7},{6,4},{7,5},{8,10},{9,11},{10,... | collective-permute-start | bytes 12296 | tf_op jit(solution)/shard_map/ppermute | solution.py:26
  10.6 1.9 %collective-permute-done.2.refs_1_.refs_4_ = f32[4,256]{1,0:T(4,128)S(1)} collective-permute-done((f32[4,256]{1,0:T(4,128)S(1)}, f32[4,256]{1,0:T(4,128)S(1)}, u32[]{:S(2)}, u32[]{:S(2)}) %collective-permute-start.2) | collective-permute-done | bytes 4128 | tf_op jit(solution)/shard_map/ppermute | solution.py:26
  12.5 2.1 %collective-permute-done.3.refs_2_.refs_5_ = f32[4,256]{1,0:T(4,128)S(1)} collective-permute-done((f32[4,256]{1,0:T(4,128)S(1)}, f32[4,256]{1,0:T(4,128)S(1)}, u32[]{:S(2)}, u32[]{:S(2)}) %collective-permute-start.3) | collective-permute-done | bytes 4128 | tf_op jit(solution)/shard_map/ppermute | solution.py:26
  15.7 2.5 %collective-permute-start.6 = (bf16[128,256]{1,0:T(8,128)(2,1)S(1)}, bf16[128,256]{1,0:T(8,128)(2,1)S(1)}, u32[]{:S(2)}, u32[]{:S(2)}) collective-permute-start(bf16[128,256]{1,0:T(8,128)(2,1)S(1)} %get-tuple-element.64), channel_id=1, source_target_pairs={{0,3},{1,2},{2,1},{3,0},{4,7},{5,6},{6,5},{7,4},{8,11},{9,10},{10,... | collective-permute-start | bytes 196616 | tf_op jit(solution)/shard_map/ppermute | solution.py:26
  20.2 3.0 %densify.2.refs_6_.refs_1_ = bf16[256,1152]{1,0:T(8,128)(2,1)S(1)} custom-call(s32[1,2,96]{2,1,0:T(2,128)S(1)} %copy-done.6, s32[1,2,96]{2,1,0:T(2,128)S(1)} %copy-done.5, s32[1,2]{1,0:T(1,128)S(1)} %bitcast.29, bf16[1,2,96,128,128]{4,3,2,1,0:T(8,128)(2,1)} %refs_3_.3), custom_call_target="tpu_custom_call" | custom-call | flops 31457280 | bytes 3145728 | tf_op jit(solution)/shard_map/densify/pallas_call | solution.py:64
  24.5 2.3 %collective-permute-start.9 = (bf16[128,256]{1,0:T(8,128)(2,1)S(1)}, bf16[128,256]{1,0:T(8,128)(2,1)S(1)}, u32[]{:S(2)}, u32[]{:S(2)}) collective-permute-start(bf16[128,256]{1,0:T(8,128)(2,1)S(1)} %get-tuple-element.71), channel_id=1, source_target_pairs={{0,3},{1,2},{2,1},{3,0},{4,7},{5,6},{6,5},{7,4},{8,11},{9,10},{10,... | collective-permute-start | bytes 196616 | tf_op jit(solution)/shard_map/ppermute | solution.py:26
  26.9 2.8 %densify.3.refs_6_.refs_1_ = bf16[256,1152]{1,0:T(8,128)(2,1)S(1)} custom-call(s32[1,2,96]{2,1,0:T(2,128)S(1)} %copy-done.6, s32[1,2,96]{2,1,0:T(2,128)S(1)} %copy-done.5, s32[1,2]{1,0:T(1,128)S(1)} %bitcast.30, bf16[1,2,96,128,128]{4,3,2,1,0:T(8,128)(2,1)} %refs_3_.3), custom_call_target="tpu_custom_call" | custom-call | flops 31457280 | bytes 3145728 | tf_op jit(solution)/shard_map/densify/pallas_call | solution.py:64
  31.2 1.6 %collective-permute-start.11 = (bf16[128,256]{1,0:T(8,128)(2,1)S(1)}, bf16[128,256]{1,0:T(8,128)(2,1)S(1)}, u32[]{:S(2)}, u32[]{:S(2)}) collective-permute-start(bf16[128,256]{1,0:T(8,128)(2,1)S(1)} %get-tuple-element.73), channel_id=1, source_target_pairs={{0,1},{1,0},{2,3},{3,2},{4,5},{5,4},{6,7},{7,6},{8,9},{9,8},{10,11... | collective-permute-start | bytes 196616 | tf_op jit(solution)/shard_map/ppermute | solution.py:26
  34.7 3.3 %collective-permute-done.10.image_ref.refs_3_ = bf16[256,256]{1,0:T(8,128)(2,1)S(1)} collective-permute-done((bf16[256,256]{1,0:T(8,128)(2,1)S(1)}, bf16[256,256]{1,0:T(8,128)(2,1)S(1)}, u32[]{:S(2)}, u32[]{:S(2)}) %collective-permute-start.10) | collective-permute-done | bytes 131104 | tf_op jit(solution)/shard_map/ppermute | solution.py:26
  43.5 2.2 %collective-permute-done.16.refs_9_ = bf16[128,256]{1,0:T(8,128)(2,1)S(1)} collective-permute-done((bf16[128,256]{1,0:T(8,128)(2,1)S(1)}, bf16[128,256]{1,0:T(8,128)(2,1)S(1)}, u32[]{:S(2)}, u32[]{:S(2)}) %collective-permute-start.16) | collective-permute-done | bytes 65568 | tf_op jit(solution)/shard_map/ppermute | solution.py:26
  47.7 1.6 %collective-permute-done.17.refs_7_ = bf16[256,256]{1,0:T(8,128)(2,1)S(1)} collective-permute-done((bf16[256,256]{1,0:T(8,128)(2,1)S(1)}, bf16[256,256]{1,0:T(8,128)(2,1)S(1)}, u32[]{:S(2)}, u32[]{:S(2)}) %collective-permute-start.17) | collective-permute-done | bytes 131104 | tf_op jit(solution)/shard_map/ppermute | solution.py:37
  52.3 2.2 %collective-permute-start.21 = (bf16[192,256]{1,0:T(8,128)(2,1)S(1)}, bf16[192,256]{1,0:T(8,128)(2,1)S(1)}, u32[]{:S(2)}, u32[]{:S(2)}) collective-permute-start(bf16[192,256]{1,0:T(8,128)(2,1)S(1)} %get-tuple-element.82), channel_id=1, source_target_pairs={{0,3},{1,2},{2,1},{3,0},{4,7},{5,6},{6,5},{7,4},{8,11},{9,10},{10,... | collective-permute-start | bytes 294920 | tf_op jit(solution)/shard_map/ppermute | solution.py:26
  54.6 5.3 %collective-permute-done.18.image_ref.refs_8_ = bf16[256,256]{1,0:T(8,128)(2,1)S(1)} collective-permute-done((bf16[256,256]{1,0:T(8,128)(2,1)S(1)}, bf16[256,256]{1,0:T(8,128)(2,1)S(1)}, u32[]{:S(2)}, u32[]{:S(2)}) %collective-permute-start.18) | collective-permute-done | bytes 131104 | tf_op jit(solution)/shard_map/ppermute | solution.py:26
  60.0 3.4 %collective-permute-start.24 = (bf16[128,256]{1,0:T(8,128)(2,1)S(1)}, bf16[128,256]{1,0:T(8,128)(2,1)S(1)}, u32[]{:S(2)}, u32[]{:S(2)}) collective-permute-start(bf16[128,256]{1,0:T(8,128)(2,1)S(1)} %get-tuple-element.85), channel_id=1, source_target_pairs={{0,3},{1,2},{2,1},{3,0},{4,7},{5,6},{6,5},{7,4},{8,11},{9,10},{10,... | collective-permute-start | bytes 196616 | tf_op jit(solution)/shard_map/ppermute | solution.py:26
  65.0 2.1 %collective-permute-done.24.refs_14_ = bf16[128,256]{1,0:T(8,128)(2,1)S(1)} collective-permute-done((bf16[128,256]{1,0:T(8,128)(2,1)S(1)}, bf16[128,256]{1,0:T(8,128)(2,1)S(1)}, u32[]{:S(2)}, u32[]{:S(2)}) %collective-permute-start.24) | collective-permute-done | bytes 65568 | tf_op jit(solution)/shard_map/ppermute | solution.py:26
  69.2 1.5 %collective-permute-start.27 = (bf16[192,256]{1,0:T(8,128)(2,1)S(1)}, bf16[192,256]{1,0:T(8,128)(2,1)S(1)}, u32[]{:S(2)}, u32[]{:S(2)}) collective-permute-start(bf16[192,256]{1,0:T(8,128)(2,1)S(1)} %get-tuple-element.94), channel_id=1, source_target_pairs={{0,2},{1,3},{2,0},{3,1},{4,6},{5,7},{6,4},{7,5},{8,10},{9,11},{10,... | collective-permute-start | bytes 294920 | tf_op jit(solution)/shard_map/ppermute | solution.py:26
  70.7 1.4 %collective-permute-start.28 = (bf16[192,256]{1,0:T(8,128)(2,1)S(1)}, bf16[192,256]{1,0:T(8,128)(2,1)S(1)}, u32[]{:S(2)}, u32[]{:S(2)}) collective-permute-start(bf16[192,256]{1,0:T(8,128)(2,1)S(1)} %get-tuple-element.95), channel_id=1, source_target_pairs={{0,3},{1,2},{2,1},{3,0},{4,7},{5,6},{6,5},{7,4},{8,11},{9,10},{10,... | collective-permute-start | bytes 294920 | tf_op jit(solution)/shard_map/ppermute | solution.py:26
  72.1 2.9 %collective-permute-start.33 = (bf16[64,256]{1,0:T(8,128)(2,1)S(1)}, bf16[64,256]{1,0:T(8,128)(2,1)S(1)}, u32[]{:S(2)}, u32[]{:S(2)}) collective-permute-start(bf16[64,256]{1,0:T(8,128)(2,1)S(1)} %half_sum.2.refs_2_), channel_id=1, source_target_pairs={{0,4},{1,5},{2,6},{3,7},{4,0},{5,1},{6,2},{7,3},{8,12},{9,13},{10,... | collective-permute-start | bytes 98312 | tf_op jit(solution)/shard_map/ppermute | solution.py:26
  75.0 2.4 %collective-permute-done.25.image_ref.refs_3_ = bf16[256,256]{1,0:T(8,128)(2,1)S(1)} collective-permute-done((bf16[256,256]{1,0:T(8,128)(2,1)S(1)}, bf16[256,256]{1,0:T(8,128)(2,1)S(1)}, u32[]{:S(2)}, u32[]{:S(2)}) %collective-permute-start.25) | collective-permute-done | bytes 131104 | tf_op jit(solution)/shard_map/ppermute | solution.py:26
  78.2 2.7 %collective-permute-start.31 = (bf16[128,256]{1,0:T(8,128)(2,1)S(1)}, bf16[128,256]{1,0:T(8,128)(2,1)S(1)}, u32[]{:S(2)}, u32[]{:S(2)}) collective-permute-start(bf16[128,256]{1,0:T(8,128)(2,1)S(1)} %get-tuple-element.98), channel_id=1, source_target_pairs={{0,3},{1,2},{2,1},{3,0},{4,7},{5,6},{6,5},{7,4},{8,11},{9,10},{10,... | collective-permute-start | bytes 196616 | tf_op jit(solution)/shard_map/ppermute | solution.py:26
  81.1 4.7 %collective-permute-done.32.refs_1_ = bf16[64,256]{1,0:T(8,128)(2,1)S(1)} collective-permute-done((bf16[64,256]{1,0:T(8,128)(2,1)S(1)}, bf16[64,256]{1,0:T(8,128)(2,1)S(1)}, u32[]{:S(2)}, u32[]{:S(2)}) %collective-permute-start.32) | collective-permute-done | bytes 32800 | tf_op jit(solution)/shard_map/ppermute | solution.py:26
  86.8 2.7 %collective-permute-start.36 = (bf16[2,64,256]{2,1,0:T(8,128)(2,1)S(1)}, bf16[2,64,256]{2,1,0:T(8,128)(2,1)S(1)}, u32[]{:S(2)}, u32[]{:S(2)}) collective-permute-start(bf16[2,64,256]{2,1,0:T(8,128)(2,1)S(1)} %total.1.refs_0_), channel_id=1, source_target_pairs={{0,3},{1,2},{2,1},{3,0},{4,7},{5,6},{6,5},{7,4},{8,11},{9,10},{10,... | collective-permute-start | bytes 196616 | tf_op jit(solution)/shard_map/ppermute | solution.py:26
  (92 shorter events, 30.4 us)
Async XLA Ops:
  2.9 20.4 %collective-permute-start = (bf16[256,256]{1,0:T(8,128)(2,1)S(1)}, bf16[256,256]{1,0:T(8,128)(2,1)S(1)}, u32[]{:S(2)}, u32[]{:S(2)}) collective-permute-start(bf16[256,256]{1,0:T(8,128)(2,1)S(1)} %fusion.3.image_ref.refs_7_), channel_id=1, source_target_pairs={{0,4},{1,5},{2,6},{3,7},{4,0},{5,1},{6,2},{7,3},{8,12},{9,13},{10,... | collective-permute-start | bytes 393224 | tf_op jit(solution)/shard_map/ppermute | solution.py:26
  14.6 9.9 %collective-permute-start.4 = (bf16[128,256]{1,0:T(8,128)(2,1)S(1)}, bf16[128,256]{1,0:T(8,128)(2,1)S(1)}, u32[]{:S(2)}, u32[]{:S(2)}) collective-permute-start(bf16[128,256]{1,0:T(8,128)(2,1)S(1)} %get-tuple-element.62), channel_id=1, source_target_pairs={{0,1},{1,0},{2,3},{3,2},{4,5},{5,4},{6,7},{7,6},{8,9},{9,8},{10,11... | collective-permute-start | bytes 196616 | tf_op jit(solution)/shard_map/ppermute | solution.py:26
  15.2 11.7 %collective-permute-start.5 = (bf16[128,256]{1,0:T(8,128)(2,1)S(1)}, bf16[128,256]{1,0:T(8,128)(2,1)S(1)}, u32[]{:S(2)}, u32[]{:S(2)}) collective-permute-start(bf16[128,256]{1,0:T(8,128)(2,1)S(1)} %get-tuple-element.63), channel_id=1, source_target_pairs={{0,2},{1,3},{2,0},{3,1},{4,6},{5,7},{6,4},{7,5},{8,10},{9,11},{10,... | collective-permute-start | bytes 196616 | tf_op jit(solution)/shard_map/ppermute | solution.py:26
  15.7 11.2 %collective-permute-start.6 = (bf16[128,256]{1,0:T(8,128)(2,1)S(1)}, bf16[128,256]{1,0:T(8,128)(2,1)S(1)}, u32[]{:S(2)}, u32[]{:S(2)}) collective-permute-start(bf16[128,256]{1,0:T(8,128)(2,1)S(1)} %get-tuple-element.64), channel_id=1, source_target_pairs={{0,3},{1,2},{2,1},{3,0},{4,7},{5,6},{6,5},{7,4},{8,11},{9,10},{10,... | collective-permute-start | bytes 196616 | tf_op jit(solution)/shard_map/ppermute | solution.py:26
  23.3 6.4 %collective-permute-start.7 = (bf16[128,256]{1,0:T(8,128)(2,1)S(1)}, bf16[128,256]{1,0:T(8,128)(2,1)S(1)}, u32[]{:S(2)}, u32[]{:S(2)}) collective-permute-start(bf16[128,256]{1,0:T(8,128)(2,1)S(1)} %get-tuple-element.69), channel_id=1, source_target_pairs={{0,1},{1,0},{2,3},{3,2},{4,5},{5,4},{6,7},{7,6},{8,9},{9,8},{10,11... | collective-permute-start | bytes 196616 | tf_op jit(solution)/shard_map/ppermute | solution.py:26
  23.9 5.8 %collective-permute-start.8 = (bf16[128,256]{1,0:T(8,128)(2,1)S(1)}, bf16[128,256]{1,0:T(8,128)(2,1)S(1)}, u32[]{:S(2)}, u32[]{:S(2)}) collective-permute-start(bf16[128,256]{1,0:T(8,128)(2,1)S(1)} %get-tuple-element.70), channel_id=1, source_target_pairs={{0,2},{1,3},{2,0},{3,1},{4,6},{5,7},{6,4},{7,5},{8,10},{9,11},{10,... | collective-permute-start | bytes 196616 | tf_op jit(solution)/shard_map/ppermute | solution.py:26
  30.9 7.1 %collective-permute-start.10 = (bf16[256,256]{1,0:T(8,128)(2,1)S(1)}, bf16[256,256]{1,0:T(8,128)(2,1)S(1)}, u32[]{:S(2)}, u32[]{:S(2)}) collective-permute-start(bf16[256,256]{1,0:T(8,128)(2,1)S(1)} %get-tuple-element.72.refs_2_), channel_id=1, source_target_pairs={{0,4},{1,5},{2,6},{3,7},{4,0},{5,1},{6,2},{7,3},{8,12},{9,13},{10,... | collective-permute-start | bytes 393224 | tf_op jit(solution)/shard_map/ppermute | solution.py:26
  31.2 9.3 %collective-permute-start.11 = (bf16[128,256]{1,0:T(8,128)(2,1)S(1)}, bf16[128,256]{1,0:T(8,128)(2,1)S(1)}, u32[]{:S(2)}, u32[]{:S(2)}) collective-permute-start(bf16[128,256]{1,0:T(8,128)(2,1)S(1)} %get-tuple-element.73), channel_id=1, source_target_pairs={{0,1},{1,0},{2,3},{3,2},{4,5},{5,4},{6,7},{7,6},{8,9},{9,8},{10,11... | collective-permute-start | bytes 196616 | tf_op jit(solution)/shard_map/ppermute | solution.py:26
  32.8 8.8 %collective-permute-start.12 = (bf16[128,256]{1,0:T(8,128)(2,1)S(1)}, bf16[128,256]{1,0:T(8,128)(2,1)S(1)}, u32[]{:S(2)}, u32[]{:S(2)}) collective-permute-start(bf16[128,256]{1,0:T(8,128)(2,1)S(1)} %get-tuple-element.74), channel_id=1, source_target_pairs={{0,2},{1,3},{2,0},{3,1},{4,6},{5,7},{6,4},{7,5},{8,10},{9,11},{10,... | collective-permute-start | bytes 196616 | tf_op jit(solution)/shard_map/ppermute | solution.py:26
  33.8 7.7 %collective-permute-start.13 = (bf16[128,256]{1,0:T(8,128)(2,1)S(1)}, bf16[128,256]{1,0:T(8,128)(2,1)S(1)}, u32[]{:S(2)}, u32[]{:S(2)}) collective-permute-start(bf16[128,256]{1,0:T(8,128)(2,1)S(1)} %get-tuple-element.75), channel_id=1, source_target_pairs={{0,3},{1,2},{2,1},{3,0},{4,7},{5,6},{6,5},{7,4},{8,11},{9,10},{10,... | collective-permute-start | bytes 196616 | tf_op jit(solution)/shard_map/ppermute | solution.py:26
  50.1 9.8 %collective-permute-start.18 = (bf16[256,256]{1,0:T(8,128)(2,1)S(1)}, bf16[256,256]{1,0:T(8,128)(2,1)S(1)}, u32[]{:S(2)}, u32[]{:S(2)}) collective-permute-start(bf16[256,256]{1,0:T(8,128)(2,1)S(1)} %get-tuple-element.79.refs_7_), channel_id=1, source_target_pairs={{0,4},{1,5},{2,6},{3,7},{4,0},{5,1},{6,2},{7,3},{8,12},{9,13},{10,... | collective-permute-start | bytes 393224 | tf_op jit(solution)/shard_map/ppermute | solution.py:26
  50.9 9.1 %collective-permute-start.19 = (bf16[192,256]{1,0:T(8,128)(2,1)S(1)}, bf16[192,256]{1,0:T(8,128)(2,1)S(1)}, u32[]{:S(2)}, u32[]{:S(2)}) collective-permute-start(bf16[192,256]{1,0:T(8,128)(2,1)S(1)} %get-tuple-element.80), channel_id=1, source_target_pairs={{0,1},{1,0},{2,3},{3,2},{4,5},{5,4},{6,7},{7,6},{8,9},{9,8},{10,11... | collective-permute-start | bytes 294920 | tf_op jit(solution)/shard_map/ppermute | solution.py:26
  52.0 11.7 %collective-permute-start.20 = (bf16[192,256]{1,0:T(8,128)(2,1)S(1)}, bf16[192,256]{1,0:T(8,128)(2,1)S(1)}, u32[]{:S(2)}, u32[]{:S(2)}) collective-permute-start(bf16[192,256]{1,0:T(8,128)(2,1)S(1)} %get-tuple-element.81), channel_id=1, source_target_pairs={{0,2},{1,3},{2,0},{3,1},{4,6},{5,7},{6,4},{7,5},{8,10},{9,11},{10,... | collective-permute-start | bytes 294920 | tf_op jit(solution)/shard_map/ppermute | solution.py:26
  52.3 11.3 %collective-permute-start.21 = (bf16[192,256]{1,0:T(8,128)(2,1)S(1)}, bf16[192,256]{1,0:T(8,128)(2,1)S(1)}, u32[]{:S(2)}, u32[]{:S(2)}) collective-permute-start(bf16[192,256]{1,0:T(8,128)(2,1)S(1)} %get-tuple-element.82), channel_id=1, source_target_pairs={{0,3},{1,2},{2,1},{3,0},{4,7},{5,6},{6,5},{7,4},{8,11},{9,10},{10,... | collective-permute-start | bytes 294920 | tf_op jit(solution)/shard_map/ppermute | solution.py:26
  60.0 7.0 %collective-permute-start.24 = (bf16[128,256]{1,0:T(8,128)(2,1)S(1)}, bf16[128,256]{1,0:T(8,128)(2,1)S(1)}, u32[]{:S(2)}, u32[]{:S(2)}) collective-permute-start(bf16[128,256]{1,0:T(8,128)(2,1)S(1)} %get-tuple-element.85), channel_id=1, source_target_pairs={{0,3},{1,2},{2,1},{3,0},{4,7},{5,6},{6,5},{7,4},{8,11},{9,10},{10,... | collective-permute-start | bytes 196616 | tf_op jit(solution)/shard_map/ppermute | solution.py:26
  68.4 8.9 %collective-permute-start.25 = (bf16[256,256]{1,0:T(8,128)(2,1)S(1)}, bf16[256,256]{1,0:T(8,128)(2,1)S(1)}, u32[]{:S(2)}, u32[]{:S(2)}) collective-permute-start(bf16[256,256]{1,0:T(8,128)(2,1)S(1)} %get-tuple-element.92.refs_2_), channel_id=1, source_target_pairs={{0,4},{1,5},{2,6},{3,7},{4,0},{5,1},{6,2},{7,3},{8,12},{9,13},{10,... | collective-permute-start | bytes 393224 | tf_op jit(solution)/shard_map/ppermute | solution.py:26
  68.5 9.7 %collective-permute-start.26 = (bf16[192,256]{1,0:T(8,128)(2,1)S(1)}, bf16[192,256]{1,0:T(8,128)(2,1)S(1)}, u32[]{:S(2)}, u32[]{:S(2)}) collective-permute-start(bf16[192,256]{1,0:T(8,128)(2,1)S(1)} %get-tuple-element.93), channel_id=1, source_target_pairs={{0,1},{1,0},{2,3},{3,2},{4,5},{5,4},{6,7},{7,6},{8,9},{9,8},{10,11... | collective-permute-start | bytes 294920 | tf_op jit(solution)/shard_map/ppermute | solution.py:26
  69.2 9.0 %collective-permute-start.27 = (bf16[192,256]{1,0:T(8,128)(2,1)S(1)}, bf16[192,256]{1,0:T(8,128)(2,1)S(1)}, u32[]{:S(2)}, u32[]{:S(2)}) collective-permute-start(bf16[192,256]{1,0:T(8,128)(2,1)S(1)} %get-tuple-element.94), channel_id=1, source_target_pairs={{0,2},{1,3},{2,0},{3,1},{4,6},{5,7},{6,4},{7,5},{8,10},{9,11},{10,... | collective-permute-start | bytes 294920 | tf_op jit(solution)/shard_map/ppermute | solution.py:26
  70.7 10.3 %collective-permute-start.28 = (bf16[192,256]{1,0:T(8,128)(2,1)S(1)}, bf16[192,256]{1,0:T(8,128)(2,1)S(1)}, u32[]{:S(2)}, u32[]{:S(2)}) collective-permute-start(bf16[192,256]{1,0:T(8,128)(2,1)S(1)} %get-tuple-element.95), channel_id=1, source_target_pairs={{0,3},{1,2},{2,1},{3,0},{4,7},{5,6},{6,5},{7,4},{8,11},{9,10},{10,... | collective-permute-start | bytes 294920 | tf_op jit(solution)/shard_map/ppermute | solution.py:26
  72.1 9.0 %collective-permute-start.33 = (bf16[64,256]{1,0:T(8,128)(2,1)S(1)}, bf16[64,256]{1,0:T(8,128)(2,1)S(1)}, u32[]{:S(2)}, u32[]{:S(2)}) collective-permute-start(bf16[64,256]{1,0:T(8,128)(2,1)S(1)} %half_sum.2.refs_2_), channel_id=1, source_target_pairs={{0,4},{1,5},{2,6},{3,7},{4,0},{5,1},{6,2},{7,3},{8,12},{9,13},{10,... | collective-permute-start | bytes 98312 | tf_op jit(solution)/shard_map/ppermute | solution.py:26
  77.4 8.5 %collective-permute-start.29 = (bf16[128,256]{1,0:T(8,128)(2,1)S(1)}, bf16[128,256]{1,0:T(8,128)(2,1)S(1)}, u32[]{:S(2)}, u32[]{:S(2)}) collective-permute-start(bf16[128,256]{1,0:T(8,128)(2,1)S(1)} %get-tuple-element.96), channel_id=1, source_target_pairs={{0,1},{1,0},{2,3},{3,2},{4,5},{5,4},{6,7},{7,6},{8,9},{9,8},{10,11... | collective-permute-start | bytes 196616 | tf_op jit(solution)/shard_map/ppermute | solution.py:26
  78.2 7.7 %collective-permute-start.30 = (bf16[128,256]{1,0:T(8,128)(2,1)S(1)}, bf16[128,256]{1,0:T(8,128)(2,1)S(1)}, u32[]{:S(2)}, u32[]{:S(2)}) collective-permute-start(bf16[128,256]{1,0:T(8,128)(2,1)S(1)} %get-tuple-element.97), channel_id=1, source_target_pairs={{0,2},{1,3},{2,0},{3,1},{4,6},{5,7},{6,4},{7,5},{8,10},{9,11},{10,... | collective-permute-start | bytes 196616 | tf_op jit(solution)/shard_map/ppermute | solution.py:26
  78.2 7.7 %collective-permute-start.31 = (bf16[128,256]{1,0:T(8,128)(2,1)S(1)}, bf16[128,256]{1,0:T(8,128)(2,1)S(1)}, u32[]{:S(2)}, u32[]{:S(2)}) collective-permute-start(bf16[128,256]{1,0:T(8,128)(2,1)S(1)} %get-tuple-element.98), channel_id=1, source_target_pairs={{0,3},{1,2},{2,1},{3,0},{4,7},{5,6},{6,5},{7,4},{8,11},{9,10},{10,... | collective-permute-start | bytes 196616 | tf_op jit(solution)/shard_map/ppermute | solution.py:26
  86.8 5.6 %collective-permute-start.36 = (bf16[2,64,256]{2,1,0:T(8,128)(2,1)S(1)}, bf16[2,64,256]{2,1,0:T(8,128)(2,1)S(1)}, u32[]{:S(2)}, u32[]{:S(2)}) collective-permute-start(bf16[2,64,256]{2,1,0:T(8,128)(2,1)S(1)} %total.1.refs_0_), channel_id=1, source_target_pairs={{0,3},{1,2},{2,1},{3,0},{4,7},{5,6},{6,5},{7,4},{8,11},{9,10},{10,... | collective-permute-start | bytes 196616 | tf_op jit(solution)/shard_map/ppermute | solution.py:26
  (22 other events, 155.0 us)

commit v9 on v8

--- a/solution.py
+++ b/solution.py
@@ -345,11 +345,14 @@
             )
             first = tick == 0 and entry
             if first:
-                grad, *_ = lax.optimization_barrier((grad_in[0], *asking))
-                masked = jnp.where(preact[0, tick, layer] > 0, grad, jnp.zeros_like(grad))
+                masked = jnp.where(
+                    preact[0, tick, layer] > 0, grad_in[0], jnp.zeros_like(grad_in[0])
+                )
                 product = jnp.dot(masked, weights[0, layer].T, preferred_element_type=F32)
                 image = ((1.0 - beta) * masked.astype(F32) + beta * product).astype(BF16)
-                sends = select(c, 0, image)
+                adjs[0] = densify(0, tile_row, tile_col, counts, tile_vals, row_tiles, n)
+                ready, adjs[0] = lax.optimization_barrier((image, adjs[0]))
+                sends = select(c, 0, ready)
             else:
                 call = Call()
                 call.give(HBM, preact, weights)
@@ -386,8 +389,6 @@
                 kept = masked = results.take()
             far = swapped(image, h)
             near = shared(sends)
-            if first:
-                far, adjs[0] = lax.optimization_barrier((far, densify(0, tile_row, tile_col, counts, tile_vals, row_tiles, n)))
             relays = select(c, 1, far)
             relayed = shared(relays)
             if first:

time: 93.6 us -> 90.4 us (0.966)
  waiting for transfers between devices: 30 us -> 24.3 us
  starting transfers between devices: 45 us -> 47.4 us
    ppermute x36, waiting for transfers between devices: 28.4 us -> 22.7 us  [swapped(): return lax.ppermute(block, 'rows', [(i, i ^ k) for i in range(n)])]
    ppermute x36, starting transfers between devices: 43.7 us -> 46.1 us  [swapped(): return lax.ppermute(block, 'rows', [(i, i ^ k) for i in range(n)])]
  transfers between devices with their start and end apart: 37 -> 37, of which waited for: 16 -> 13; matrix products, arithmetic and copies ran while one was open for 2% -> 2% of each run, Pallas kernels for 8% -> 8%
where the time goes in v9:
time: 90.4 us; the launch traced here: 90.1 us
  starting transfers between devices  47.4 us (52%)
  waiting for transfers between devices  24.3 us (27%)
  Pallas kernels  11.7 us (13%)
  local copies, waits for them, and re-layouts  2.84 us (3%)
  matrix products  1.84 us (2%)
  between operations  1.17 us (1%)
  other arithmetic  0.91 us (1%)
    ppermute x36, starting transfers between devices, swapped(): return lax.ppermute(block, 'rows', [(i, i ^ k) for i in range(n)])  46.1 us
    ppermute x36, waiting for transfers between devices, swapped(): return lax.ppermute(block, 'rows', [(i, i ^ k) for i in range(n)])  22.7 us
    pallas_call x17, Pallas kernels, run(): pl.pallas_call(kernel, out_shape=self.outs, in_specs=self.specs, out_spec...  11.7 us
    unnamed x18, local copies, waits for them, and re-layouts  2.72 us
  transfers between devices with their start and end apart: 37, of which 13 were waited for; matrix products, arithmetic and copies ran while one was open for 2% of the time, Pallas kernels for 8%

profile of v9, /device:TPU:0, one launch (start us, length us, event | category | flops | bytes accessed | tf_op | source)
XLA Modules:
  0.0 90.1 jit_solution(2694494084223874183)
XLA Ops:
  2.1 4.1 %collective-permute-start.6 = (bf16[256,256]{1,0:T(8,128)(2,1)S(1)}, bf16[256,256]{1,0:T(8,128)(2,1)S(1)}, u32[]{:S(2)}, u32[]{:S(2)}) collective-permute-start(bf16[256,256]{1,0:T(8,128)(2,1)S(1)} %fusion.3.image_ref.refs_7_), channel_id=1, source_target_pairs={{0,4},{1,5},{2,6},{3,7},{4,0},{5,1},{6,2},{7,3},{8,12},{9,13},{10,... | collective-permute-start | bytes 393224 | tf_op jit(solution)/shard_map/ppermute | solution.py:26
  7.0 1.6 %collective-permute-start = (f32[4,256]{1,0:T(4,128)S(1)}, f32[4,256]{1,0:T(4,128)S(1)}, u32[]{:S(2)}, u32[]{:S(2)}) collective-permute-start(f32[4,256]{1,0:T(4,128)S(1)} %get-tuple-element.58), channel_id=1, source_target_pairs={{0,1},{1,0},{2,3},{3,2},{4,5},{5,4},{6,7},{7,6},{8,9},{9,8},{10,11... | collective-permute-start | bytes 12296 | tf_op jit(solution)/shard_map/ppermute | solution.py:26
  8.6 1.6 %collective-permute-start.1 = (f32[4,256]{1,0:T(4,128)S(1)}, f32[4,256]{1,0:T(4,128)S(1)}, u32[]{:S(2)}, u32[]{:S(2)}) collective-permute-start(f32[4,256]{1,0:T(4,128)S(1)} %get-tuple-element.59), channel_id=1, source_target_pairs={{0,2},{1,3},{2,0},{3,1},{4,6},{5,7},{6,4},{7,5},{8,10},{9,11},{10,... | collective-permute-start | bytes 12296 | tf_op jit(solution)/shard_map/ppermute | solution.py:26
  12.6 2.9 %densify.2.refs_6_.refs_1_ = bf16[256,1152]{1,0:T(8,128)(2,1)S(1)} custom-call(s32[1,2,96]{2,1,0:T(2,128)S(1)} %copy-done.6, s32[1,2,96]{2,1,0:T(2,128)S(1)} %copy-done.5, s32[1,2]{1,0:T(1,128)S(1)} %bitcast.37, bf16[1,2,96,128,128]{4,3,2,1,0:T(8,128)(2,1)} %refs_3_.3), custom_call_target="tpu_custom_call" | custom-call | flops 31457280 | bytes 3145728 | tf_op jit(solution)/shard_map/densify/pallas_call | solution.py:64
  15.6 1.7 %collective-permute-start.3 = (bf16[128,256]{1,0:T(8,128)(2,1)S(1)}, bf16[128,256]{1,0:T(8,128)(2,1)S(1)}, u32[]{:S(2)}, u32[]{:S(2)}) collective-permute-start(bf16[128,256]{1,0:T(8,128)(2,1)S(1)} %get-tuple-element.61), channel_id=1, source_target_pairs={{0,1},{1,0},{2,3},{3,2},{4,5},{5,4},{6,7},{7,6},{8,9},{9,8},{10,11... | collective-permute-start | bytes 196616 | tf_op jit(solution)/shard_map/ppermute | solution.py:26
  19.2 1.7 %collective-permute-start.7 = (bf16[128,256]{1,0:T(8,128)(2,1)S(1)}, bf16[128,256]{1,0:T(8,128)(2,1)S(1)}, u32[]{:S(2)}, u32[]{:S(2)}) collective-permute-start(bf16[128,256]{1,0:T(8,128)(2,1)S(1)} %get-tuple-element.67), channel_id=1, source_target_pairs={{0,1},{1,0},{2,3},{3,2},{4,5},{5,4},{6,7},{7,6},{8,9},{9,8},{10,11... | collective-permute-start | bytes 196616 | tf_op jit(solution)/shard_map/ppermute | solution.py:26
  24.5 3.0 %densify.3.refs_6_.refs_1_ = bf16[256,1152]{1,0:T(8,128)(2,1)S(1)} custom-call(s32[1,2,96]{2,1,0:T(2,128)S(1)} %copy-done.6, s32[1,2,96]{2,1,0:T(2,128)S(1)} %copy-done.5, s32[1,2]{1,0:T(1,128)S(1)} %bitcast.38, bf16[1,2,96,128,128]{4,3,2,1,0:T(8,128)(2,1)} %refs_3_.3), custom_call_target="tpu_custom_call" | custom-call | flops 31457280 | bytes 3145728 | tf_op jit(solution)/shard_map/densify/pallas_call | solution.py:64
  29.4 1.5 %collective-permute-start.11 = (bf16[128,256]{1,0:T(8,128)(2,1)S(1)}, bf16[128,256]{1,0:T(8,128)(2,1)S(1)}, u32[]{:S(2)}, u32[]{:S(2)}) collective-permute-start(bf16[128,256]{1,0:T(8,128)(2,1)S(1)} %get-tuple-element.71), channel_id=1, source_target_pairs={{0,1},{1,0},{2,3},{3,2},{4,5},{5,4},{6,7},{7,6},{8,9},{9,8},{10,11... | collective-permute-start | bytes 196616 | tf_op jit(solution)/shard_map/ppermute | solution.py:26
  32.9 3.3 %collective-permute-done.10.image_ref.refs_3_ = bf16[256,256]{1,0:T(8,128)(2,1)S(1)} collective-permute-done((bf16[256,256]{1,0:T(8,128)(2,1)S(1)}, bf16[256,256]{1,0:T(8,128)(2,1)S(1)}, u32[]{:S(2)}, u32[]{:S(2)}) %collective-permute-start.10) | collective-permute-done | bytes 131104 | tf_op jit(solution)/shard_map/ppermute | solution.py:26
  36.2 1.6 %collective-permute-start.15 = (bf16[128,256]{1,0:T(8,128)(2,1)S(1)}, bf16[128,256]{1,0:T(8,128)(2,1)S(1)}, u32[]{:S(2)}, u32[]{:S(2)}) collective-permute-start(bf16[128,256]{1,0:T(8,128)(2,1)S(1)} %get-tuple-element.75), channel_id=1, source_target_pairs={{0,2},{1,3},{2,0},{3,1},{4,6},{5,7},{6,4},{7,5},{8,10},{9,11},{10,... | collective-permute-start | bytes 196616 | tf_op jit(solution)/shard_map/ppermute | solution.py:26
  37.8 1.9 %collective-permute-start.16 = (bf16[128,256]{1,0:T(8,128)(2,1)S(1)}, bf16[128,256]{1,0:T(8,128)(2,1)S(1)}, u32[]{:S(2)}, u32[]{:S(2)}) collective-permute-start(bf16[128,256]{1,0:T(8,128)(2,1)S(1)} %get-tuple-element.76), channel_id=1, source_target_pairs={{0,3},{1,2},{2,1},{3,0},{4,7},{5,6},{6,5},{7,4},{8,11},{9,10},{10,... | collective-permute-start | bytes 196616 | tf_op jit(solution)/shard_map/ppermute | solution.py:26
  40.6 2.4 %collective-permute-done.16.refs_9_ = bf16[128,256]{1,0:T(8,128)(2,1)S(1)} collective-permute-done((bf16[128,256]{1,0:T(8,128)(2,1)S(1)}, bf16[128,256]{1,0:T(8,128)(2,1)S(1)}, u32[]{:S(2)}, u32[]{:S(2)}) %collective-permute-start.16) | collective-permute-done | bytes 65568 | tf_op jit(solution)/shard_map/ppermute | solution.py:26
  45.0 1.6 %collective-permute-done.17.refs_7_ = bf16[256,256]{1,0:T(8,128)(2,1)S(1)} collective-permute-done((bf16[256,256]{1,0:T(8,128)(2,1)S(1)}, bf16[256,256]{1,0:T(8,128)(2,1)S(1)}, u32[]{:S(2)}, u32[]{:S(2)}) %collective-permute-start.17) | collective-permute-done | bytes 131104 | tf_op jit(solution)/shard_map/ppermute | solution.py:37
  47.4 1.4 %collective-permute-start.18 = (bf16[256,256]{1,0:T(8,128)(2,1)S(1)}, bf16[256,256]{1,0:T(8,128)(2,1)S(1)}, u32[]{:S(2)}, u32[]{:S(2)}) collective-permute-start(bf16[256,256]{1,0:T(8,128)(2,1)S(1)} %get-tuple-element.77.refs_7_), channel_id=1, source_target_pairs={{0,4},{1,5},{2,6},{3,7},{4,0},{5,1},{6,2},{7,3},{8,12},{9,13},{10,... | collective-permute-start | bytes 393224 | tf_op jit(solution)/shard_map/ppermute | solution.py:26
  50.3 2.2 %collective-permute-start.21 = (bf16[192,256]{1,0:T(8,128)(2,1)S(1)}, bf16[192,256]{1,0:T(8,128)(2,1)S(1)}, u32[]{:S(2)}, u32[]{:S(2)}) collective-permute-start(bf16[192,256]{1,0:T(8,128)(2,1)S(1)} %get-tuple-element.80), channel_id=1, source_target_pairs={{0,3},{1,2},{2,1},{3,0},{4,7},{5,6},{6,5},{7,4},{8,11},{9,10},{10,... | collective-permute-start | bytes 294920 | tf_op jit(solution)/shard_map/ppermute | solution.py:26
  52.5 3.5 %collective-permute-done.18.image_ref.refs_8_ = bf16[256,256]{1,0:T(8,128)(2,1)S(1)} collective-permute-done((bf16[256,256]{1,0:T(8,128)(2,1)S(1)}, bf16[256,256]{1,0:T(8,128)(2,1)S(1)}, u32[]{:S(2)}, u32[]{:S(2)}) %collective-permute-start.18) | collective-permute-done | bytes 131104 | tf_op jit(solution)/shard_map/ppermute | solution.py:26
  56.2 3.4 %collective-permute-start.24 = (bf16[128,256]{1,0:T(8,128)(2,1)S(1)}, bf16[128,256]{1,0:T(8,128)(2,1)S(1)}, u32[]{:S(2)}, u32[]{:S(2)}) collective-permute-start(bf16[128,256]{1,0:T(8,128)(2,1)S(1)} %get-tuple-element.83), channel_id=1, source_target_pairs={{0,3},{1,2},{2,1},{3,0},{4,7},{5,6},{6,5},{7,4},{8,11},{9,10},{10,... | collective-permute-start | bytes 196616 | tf_op jit(solution)/shard_map/ppermute | solution.py:26
  61.2 2.5 %collective-permute-done.24.refs_14_ = bf16[128,256]{1,0:T(8,128)(2,1)S(1)} collective-permute-done((bf16[128,256]{1,0:T(8,128)(2,1)S(1)}, bf16[128,256]{1,0:T(8,128)(2,1)S(1)}, u32[]{:S(2)}, u32[]{:S(2)}) %collective-permute-start.24) | collective-permute-done | bytes 65568 | tf_op jit(solution)/shard_map/ppermute | solution.py:26
  65.3 2.2 %collective-permute-start.27 = (bf16[192,256]{1,0:T(8,128)(2,1)S(1)}, bf16[192,256]{1,0:T(8,128)(2,1)S(1)}, u32[]{:S(2)}, u32[]{:S(2)}) collective-permute-start(bf16[192,256]{1,0:T(8,128)(2,1)S(1)} %get-tuple-element.92), channel_id=1, source_target_pairs={{0,2},{1,3},{2,0},{3,1},{4,6},{5,7},{6,4},{7,5},{8,10},{9,11},{10,... | collective-permute-start | bytes 294920 | tf_op jit(solution)/shard_map/ppermute | solution.py:26
  68.7 2.9 %collective-permute-start.33 = (bf16[64,256]{1,0:T(8,128)(2,1)S(1)}, bf16[64,256]{1,0:T(8,128)(2,1)S(1)}, u32[]{:S(2)}, u32[]{:S(2)}) collective-permute-start(bf16[64,256]{1,0:T(8,128)(2,1)S(1)} %half_sum.2.refs_2_), channel_id=1, source_target_pairs={{0,4},{1,5},{2,6},{3,7},{4,0},{5,1},{6,2},{7,3},{8,12},{9,13},{10,... | collective-permute-start | bytes 98312 | tf_op jit(solution)/shard_map/ppermute | solution.py:26
  71.6 2.6 %collective-permute-done.25.image_ref.refs_3_ = bf16[256,256]{1,0:T(8,128)(2,1)S(1)} collective-permute-done((bf16[256,256]{1,0:T(8,128)(2,1)S(1)}, bf16[256,256]{1,0:T(8,128)(2,1)S(1)}, u32[]{:S(2)}, u32[]{:S(2)}) %collective-permute-start.25) | collective-permute-done | bytes 131104 | tf_op jit(solution)/shard_map/ppermute | solution.py:26
  75.2 2.6 %collective-permute-start.31 = (bf16[128,256]{1,0:T(8,128)(2,1)S(1)}, bf16[128,256]{1,0:T(8,128)(2,1)S(1)}, u32[]{:S(2)}, u32[]{:S(2)}) collective-permute-start(bf16[128,256]{1,0:T(8,128)(2,1)S(1)} %get-tuple-element.96), channel_id=1, source_target_pairs={{0,3},{1,2},{2,1},{3,0},{4,7},{5,6},{6,5},{7,4},{8,11},{9,10},{10,... | collective-permute-start | bytes 196616 | tf_op jit(solution)/shard_map/ppermute | solution.py:26
  79.0 3.8 %collective-permute-done.32.refs_1_ = bf16[64,256]{1,0:T(8,128)(2,1)S(1)} collective-permute-done((bf16[64,256]{1,0:T(8,128)(2,1)S(1)}, bf16[64,256]{1,0:T(8,128)(2,1)S(1)}, u32[]{:S(2)}, u32[]{:S(2)}) %collective-permute-start.32) | collective-permute-done | bytes 32800 | tf_op jit(solution)/shard_map/ppermute | solution.py:26
  83.8 2.5 %collective-permute-start.36 = (bf16[2,64,256]{2,1,0:T(8,128)(2,1)S(1)}, bf16[2,64,256]{2,1,0:T(8,128)(2,1)S(1)}, u32[]{:S(2)}, u32[]{:S(2)}) collective-permute-start(bf16[2,64,256]{2,1,0:T(8,128)(2,1)S(1)} %total.1.refs_0_), channel_id=1, source_target_pairs={{0,3},{1,2},{2,1},{3,0},{4,7},{5,6},{6,5},{7,4},{8,11},{9,10},{10,... | collective-permute-start | bytes 196616 | tf_op jit(solution)/shard_map/ppermute | solution.py:26
  (92 shorter events, 30.4 us)
Async XLA Ops:
  2.1 17.0 %collective-permute-start.6 = (bf16[256,256]{1,0:T(8,128)(2,1)S(1)}, bf16[256,256]{1,0:T(8,128)(2,1)S(1)}, u32[]{:S(2)}, u32[]{:S(2)}) collective-permute-start(bf16[256,256]{1,0:T(8,128)(2,1)S(1)} %fusion.3.image_ref.refs_7_), channel_id=1, source_target_pairs={{0,4},{1,5},{2,6},{3,7},{4,0},{5,1},{6,2},{7,3},{8,12},{9,13},{10,... | collective-permute-start | bytes 393224 | tf_op jit(solution)/shard_map/ppermute | solution.py:26
  7.0 8.5 %collective-permute-start = (f32[4,256]{1,0:T(4,128)S(1)}, f32[4,256]{1,0:T(4,128)S(1)}, u32[]{:S(2)}, u32[]{:S(2)}) collective-permute-start(f32[4,256]{1,0:T(4,128)S(1)} %get-tuple-element.58), channel_id=1, source_target_pairs={{0,1},{1,0},{2,3},{3,2},{4,5},{5,4},{6,7},{7,6},{8,9},{9,8},{10,11... | collective-permute-start | bytes 12296 | tf_op jit(solution)/shard_map/ppermute | solution.py:26
  8.6 7.0 %collective-permute-start.1 = (f32[4,256]{1,0:T(4,128)S(1)}, f32[4,256]{1,0:T(4,128)S(1)}, u32[]{:S(2)}, u32[]{:S(2)}) collective-permute-start(f32[4,256]{1,0:T(4,128)S(1)} %get-tuple-element.59), channel_id=1, source_target_pairs={{0,2},{1,3},{2,0},{3,1},{4,6},{5,7},{6,4},{7,5},{8,10},{9,11},{10,... | collective-permute-start | bytes 12296 | tf_op jit(solution)/shard_map/ppermute | solution.py:26
  15.6 6.7 %collective-permute-start.3 = (bf16[128,256]{1,0:T(8,128)(2,1)S(1)}, bf16[128,256]{1,0:T(8,128)(2,1)S(1)}, u32[]{:S(2)}, u32[]{:S(2)}) collective-permute-start(bf16[128,256]{1,0:T(8,128)(2,1)S(1)} %get-tuple-element.61), channel_id=1, source_target_pairs={{0,1},{1,0},{2,3},{3,2},{4,5},{5,4},{6,7},{7,6},{8,9},{9,8},{10,11... | collective-permute-start | bytes 196616 | tf_op jit(solution)/shard_map/ppermute | solution.py:26
  17.3 5.8 %collective-permute-start.4 = (bf16[128,256]{1,0:T(8,128)(2,1)S(1)}, bf16[128,256]{1,0:T(8,128)(2,1)S(1)}, u32[]{:S(2)}, u32[]{:S(2)}) collective-permute-start(bf16[128,256]{1,0:T(8,128)(2,1)S(1)} %get-tuple-element.62), channel_id=1, source_target_pairs={{0,2},{1,3},{2,0},{3,1},{4,6},{5,7},{6,4},{7,5},{8,10},{9,11},{10,... | collective-permute-start | bytes 196616 | tf_op jit(solution)/shard_map/ppermute | solution.py:26
  19.2 8.3 %collective-permute-start.7 = (bf16[128,256]{1,0:T(8,128)(2,1)S(1)}, bf16[128,256]{1,0:T(8,128)(2,1)S(1)}, u32[]{:S(2)}, u32[]{:S(2)}) collective-permute-start(bf16[128,256]{1,0:T(8,128)(2,1)S(1)} %get-tuple-element.67), channel_id=1, source_target_pairs={{0,1},{1,0},{2,3},{3,2},{4,5},{5,4},{6,7},{7,6},{8,9},{9,8},{10,11... | collective-permute-start | bytes 196616 | tf_op jit(solution)/shard_map/ppermute | solution.py:26
  20.9 6.6 %collective-permute-start.8 = (bf16[128,256]{1,0:T(8,128)(2,1)S(1)}, bf16[128,256]{1,0:T(8,128)(2,1)S(1)}, u32[]{:S(2)}, u32[]{:S(2)}) collective-permute-start(bf16[128,256]{1,0:T(8,128)(2,1)S(1)} %get-tuple-element.68), channel_id=1, source_target_pairs={{0,2},{1,3},{2,0},{3,1},{4,6},{5,7},{6,4},{7,5},{8,10},{9,11},{10,... | collective-permute-start | bytes 196616 | tf_op jit(solution)/shard_map/ppermute | solution.py:26
  28.7 7.4 %collective-permute-start.10 = (bf16[256,256]{1,0:T(8,128)(2,1)S(1)}, bf16[256,256]{1,0:T(8,128)(2,1)S(1)}, u32[]{:S(2)}, u32[]{:S(2)}) collective-permute-start(bf16[256,256]{1,0:T(8,128)(2,1)S(1)} %get-tuple-element.70.refs_2_), channel_id=1, source_target_pairs={{0,4},{1,5},{2,6},{3,7},{4,0},{5,1},{6,2},{7,3},{8,12},{9,13},{10,... | collective-permute-start | bytes 393224 | tf_op jit(solution)/shard_map/ppermute | solution.py:26
  29.4 8.4 %collective-permute-start.11 = (bf16[128,256]{1,0:T(8,128)(2,1)S(1)}, bf16[128,256]{1,0:T(8,128)(2,1)S(1)}, u32[]{:S(2)}, u32[]{:S(2)}) collective-permute-start(bf16[128,256]{1,0:T(8,128)(2,1)S(1)} %get-tuple-element.71), channel_id=1, source_target_pairs={{0,1},{1,0},{2,3},{3,2},{4,5},{5,4},{6,7},{7,6},{8,9},{9,8},{10,11... | collective-permute-start | bytes 196616 | tf_op jit(solution)/shard_map/ppermute | solution.py:26
  30.9 8.8 %collective-permute-start.12 = (bf16[128,256]{1,0:T(8,128)(2,1)S(1)}, bf16[128,256]{1,0:T(8,128)(2,1)S(1)}, u32[]{:S(2)}, u32[]{:S(2)}) collective-permute-start(bf16[128,256]{1,0:T(8,128)(2,1)S(1)} %get-tuple-element.72), channel_id=1, source_target_pairs={{0,2},{1,3},{2,0},{3,1},{4,6},{5,7},{6,4},{7,5},{8,10},{9,11},{10,... | collective-permute-start | bytes 196616 | tf_op jit(solution)/shard_map/ppermute | solution.py:26
  31.7 8.0 %collective-permute-start.13 = (bf16[128,256]{1,0:T(8,128)(2,1)S(1)}, bf16[128,256]{1,0:T(8,128)(2,1)S(1)}, u32[]{:S(2)}, u32[]{:S(2)}) collective-permute-start(bf16[128,256]{1,0:T(8,128)(2,1)S(1)} %get-tuple-element.73), channel_id=1, source_target_pairs={{0,3},{1,2},{2,1},{3,0},{4,7},{5,6},{6,5},{7,4},{8,11},{9,10},{10,... | collective-permute-start | bytes 196616 | tf_op jit(solution)/shard_map/ppermute | solution.py:26
  47.4 8.6 %collective-permute-start.18 = (bf16[256,256]{1,0:T(8,128)(2,1)S(1)}, bf16[256,256]{1,0:T(8,128)(2,1)S(1)}, u32[]{:S(2)}, u32[]{:S(2)}) collective-permute-start(bf16[256,256]{1,0:T(8,128)(2,1)S(1)} %get-tuple-element.77.refs_7_), channel_id=1, source_target_pairs={{0,4},{1,5},{2,6},{3,7},{4,0},{5,1},{6,2},{7,3},{8,12},{9,13},{10,... | collective-permute-start | bytes 393224 | tf_op jit(solution)/shard_map/ppermute | solution.py:26
  48.9 7.3 %collective-permute-start.19 = (bf16[192,256]{1,0:T(8,128)(2,1)S(1)}, bf16[192,256]{1,0:T(8,128)(2,1)S(1)}, u32[]{:S(2)}, u32[]{:S(2)}) collective-permute-start(bf16[192,256]{1,0:T(8,128)(2,1)S(1)} %get-tuple-element.78), channel_id=1, source_target_pairs={{0,1},{1,0},{2,3},{3,2},{4,5},{5,4},{6,7},{7,6},{8,9},{9,8},{10,11... | collective-permute-start | bytes 294920 | tf_op jit(solution)/shard_map/ppermute | solution.py:26
  49.5 10.4 %collective-permute-start.20 = (bf16[192,256]{1,0:T(8,128)(2,1)S(1)}, bf16[192,256]{1,0:T(8,128)(2,1)S(1)}, u32[]{:S(2)}, u32[]{:S(2)}) collective-permute-start(bf16[192,256]{1,0:T(8,128)(2,1)S(1)} %get-tuple-element.79), channel_id=1, source_target_pairs={{0,2},{1,3},{2,0},{3,1},{4,6},{5,7},{6,4},{7,5},{8,10},{9,11},{10,... | collective-permute-start | bytes 294920 | tf_op jit(solution)/shard_map/ppermute | solution.py:26
  50.3 9.6 %collective-permute-start.21 = (bf16[192,256]{1,0:T(8,128)(2,1)S(1)}, bf16[192,256]{1,0:T(8,128)(2,1)S(1)}, u32[]{:S(2)}, u32[]{:S(2)}) collective-permute-start(bf16[192,256]{1,0:T(8,128)(2,1)S(1)} %get-tuple-element.80), channel_id=1, source_target_pairs={{0,3},{1,2},{2,1},{3,0},{4,7},{5,6},{6,5},{7,4},{8,11},{9,10},{10,... | collective-permute-start | bytes 294920 | tf_op jit(solution)/shard_map/ppermute | solution.py:26
  56.2 7.5 %collective-permute-start.24 = (bf16[128,256]{1,0:T(8,128)(2,1)S(1)}, bf16[128,256]{1,0:T(8,128)(2,1)S(1)}, u32[]{:S(2)}, u32[]{:S(2)}) collective-permute-start(bf16[128,256]{1,0:T(8,128)(2,1)S(1)} %get-tuple-element.83), channel_id=1, source_target_pairs={{0,3},{1,2},{2,1},{3,0},{4,7},{5,6},{6,5},{7,4},{8,11},{9,10},{10,... | collective-permute-start | bytes 196616 | tf_op jit(solution)/shard_map/ppermute | solution.py:26
  65.0 9.2 %collective-permute-start.25 = (bf16[256,256]{1,0:T(8,128)(2,1)S(1)}, bf16[256,256]{1,0:T(8,128)(2,1)S(1)}, u32[]{:S(2)}, u32[]{:S(2)}) collective-permute-start(bf16[256,256]{1,0:T(8,128)(2,1)S(1)} %get-tuple-element.90.refs_2_), channel_id=1, source_target_pairs={{0,4},{1,5},{2,6},{3,7},{4,0},{5,1},{6,2},{7,3},{8,12},{9,13},{10,... | collective-permute-start | bytes 393224 | tf_op jit(solution)/shard_map/ppermute | solution.py:26
  65.1 10.1 %collective-permute-start.26 = (bf16[192,256]{1,0:T(8,128)(2,1)S(1)}, bf16[192,256]{1,0:T(8,128)(2,1)S(1)}, u32[]{:S(2)}, u32[]{:S(2)}) collective-permute-start(bf16[192,256]{1,0:T(8,128)(2,1)S(1)} %get-tuple-element.91), channel_id=1, source_target_pairs={{0,1},{1,0},{2,3},{3,2},{4,5},{5,4},{6,7},{7,6},{8,9},{9,8},{10,11... | collective-permute-start | bytes 294920 | tf_op jit(solution)/shard_map/ppermute | solution.py:26
  65.3 9.9 %collective-permute-start.27 = (bf16[192,256]{1,0:T(8,128)(2,1)S(1)}, bf16[192,256]{1,0:T(8,128)(2,1)S(1)}, u32[]{:S(2)}, u32[]{:S(2)}) collective-permute-start(bf16[192,256]{1,0:T(8,128)(2,1)S(1)} %get-tuple-element.92), channel_id=1, source_target_pairs={{0,2},{1,3},{2,0},{3,1},{4,6},{5,7},{6,4},{7,5},{8,10},{9,11},{10,... | collective-permute-start | bytes 294920 | tf_op jit(solution)/shard_map/ppermute | solution.py:26
  67.5 10.4 %collective-permute-start.28 = (bf16[192,256]{1,0:T(8,128)(2,1)S(1)}, bf16[192,256]{1,0:T(8,128)(2,1)S(1)}, u32[]{:S(2)}, u32[]{:S(2)}) collective-permute-start(bf16[192,256]{1,0:T(8,128)(2,1)S(1)} %get-tuple-element.93), channel_id=1, source_target_pairs={{0,3},{1,2},{2,1},{3,0},{4,7},{5,6},{6,5},{7,4},{8,11},{9,10},{10,... | collective-permute-start | bytes 294920 | tf_op jit(solution)/shard_map/ppermute | solution.py:26
  68.7 10.3 %collective-permute-start.33 = (bf16[64,256]{1,0:T(8,128)(2,1)S(1)}, bf16[64,256]{1,0:T(8,128)(2,1)S(1)}, u32[]{:S(2)}, u32[]{:S(2)}) collective-permute-start(bf16[64,256]{1,0:T(8,128)(2,1)S(1)} %half_sum.2.refs_2_), channel_id=1, source_target_pairs={{0,4},{1,5},{2,6},{3,7},{4,0},{5,1},{6,2},{7,3},{8,12},{9,13},{10,... | collective-permute-start | bytes 98312 | tf_op jit(solution)/shard_map/ppermute | solution.py:26
  74.3 8.5 %collective-permute-start.29 = (bf16[128,256]{1,0:T(8,128)(2,1)S(1)}, bf16[128,256]{1,0:T(8,128)(2,1)S(1)}, u32[]{:S(2)}, u32[]{:S(2)}) collective-permute-start(bf16[128,256]{1,0:T(8,128)(2,1)S(1)} %get-tuple-element.94), channel_id=1, source_target_pairs={{0,1},{1,0},{2,3},{3,2},{4,5},{5,4},{6,7},{7,6},{8,9},{9,8},{10,11... | collective-permute-start | bytes 196616 | tf_op jit(solution)/shard_map/ppermute | solution.py:26
  75.2 7.5 %collective-permute-start.30 = (bf16[128,256]{1,0:T(8,128)(2,1)S(1)}, bf16[128,256]{1,0:T(8,128)(2,1)S(1)}, u32[]{:S(2)}, u32[]{:S(2)}) collective-permute-start(bf16[128,256]{1,0:T(8,128)(2,1)S(1)} %get-tuple-element.95), channel_id=1, source_target_pairs={{0,2},{1,3},{2,0},{3,1},{4,6},{5,7},{6,4},{7,5},{8,10},{9,11},{10,... | collective-permute-start | bytes 196616 | tf_op jit(solution)/shard_map/ppermute | solution.py:26
  75.2 7.5 %collective-permute-start.31 = (bf16[128,256]{1,0:T(8,128)(2,1)S(1)}, bf16[128,256]{1,0:T(8,128)(2,1)S(1)}, u32[]{:S(2)}, u32[]{:S(2)}) collective-permute-start(bf16[128,256]{1,0:T(8,128)(2,1)S(1)} %get-tuple-element.96), channel_id=1, source_target_pairs={{0,3},{1,2},{2,1},{3,0},{4,7},{5,6},{6,5},{7,4},{8,11},{9,10},{10,... | collective-permute-start | bytes 196616 | tf_op jit(solution)/shard_map/ppermute | solution.py:26
  (22 other events, 185.4 us)

commit v10 on v9

--- a/solution.py
+++ b/solution.py
@@ -74,11 +74,17 @@
         )(*self.operands)
 
 
-def densify_kernel(tick, row_tiles, n, chunks, *refs):
-    rows_ref, cols_ref, count_ref, vals_ref, out_ref, vals, acc, sems = refs
+def packed(tile_row, tile_col, tile_count, row_tiles):
+    owner = jnp.bitwise_xor(tile_col // row_tiles, lax.axis_index("rows"))
+    words = (owner * row_tiles + tile_col % row_tiles) * row_tiles + tile_row
+    counts = tile_count.reshape(1, -1)
+    counts = jnp.pad(counts, ((0, 0), (0, words.shape[2] - counts.shape[1])))
+    return jnp.concatenate([words[0], counts], axis=0)
+
+
+def densify_kernel(tick, row_tiles, n, chunks, words_ref, vals_ref, out_ref, vals, acc, sems):
     entries, tile = vals.shape[:2]
     chunk = entries // chunks
-    me = lax.axis_index("rows")
     copies = []
     for c in range(chunks):
         part = pl.ds(c * chunk, chunk)
@@ -89,28 +95,30 @@
     acc[...] = jnp.zeros_like(acc)
 
     def add(e, carry):
-        owner = lax.div(cols_ref[0, tick, e], row_tiles)
-        block = lax.rem(cols_ref[0, tick, e], row_tiles)
-        slot = jnp.bitwise_xor(owner, me)
-        slot = jnp.where((owner == me) & (block > 0), n - 1 + block, slot)
-        rows = pl.ds(pl.multiple_of(rows_ref[0, tick, e] * tile, tile), tile)
+        word = words_ref[tick, e]
+        row = lax.rem(word, row_tiles)
+        block = lax.rem(lax.div(word, row_tiles), row_tiles)
+        slot = lax.div(word, row_tiles * row_tiles)
+        slot = jnp.where((slot == 0) & (block > 0), n - 1 + block, slot)
+        rows = pl.ds(pl.multiple_of(row * tile, tile), tile)
         cols = pl.ds(pl.multiple_of(slot * tile, tile), tile)
         acc[rows, cols] += vals[e].astype(F32)
         return carry
 
+    count = words_ref[words_ref.shape[0] - 1, tick]
     for c in range(chunks):
         copies[c].wait()
-        stop = jnp.clip(count_ref[0, tick], c * chunk, (c + 1) * chunk)
+        stop = jnp.clip(count, c * chunk, (c + 1) * chunk)
         lax.fori_loop(c * chunk, stop, add, 0)
     out_ref[...] = acc[...].astype(BF16)
 
 
-def densify(tick, rows, cols, count, vals, row_tiles, n):
+def densify(tick, words, vals, row_tiles, n):
     entries, tile = vals.shape[2:4]
     chunks = 4 if entries % 4 == 0 else 1
     shape = (row_tiles * tile, (n + row_tiles - 1) * tile)
     call = Call()
-    call.give(SMEM, rows, cols, count)
+    call.give(SMEM, words)
     call.give(HBM, vals)
     call.want(VMEM, shape, BF16)
     call.scratch = [
@@ -131,17 +139,15 @@
     return ref[pl.ds(pl.multiple_of(index * tile, tile), tile), :]
 
 
-def name_kernel(n, row_tiles, cols_ref, *out_refs):
-    me = lax.axis_index("rows")
-    ticks = cols_ref.shape[1]
-    width = out_refs[0].shape[1]
+def name_kernel(n, row_tiles, words_ref, *out_refs):
+    ticks, width = out_refs[0].shape
     for t in range(ticks):
-        cols = cols_ref[0, t : t + 1, :]
+        index = words_ref[t : t + 1, :] // row_tiles
 
         def named(k):
-            index = cols - jnp.bitwise_xor(me, k) * row_tiles
-            index = jnp.where((index >= 0) & (index < row_tiles), index, 0)
-            most = jnp.max(index.astype(F32), axis=1, keepdims=True)
+            block = index - k * row_tiles
+            block = jnp.where((block >= 0) & (block < row_tiles), block, 0)
+            most = jnp.max(block.astype(F32), axis=1, keepdims=True)
             return jnp.broadcast_to(most, (1, width))
 
         for k in range(1, n // 2):
@@ -158,8 +164,11 @@
     return result
 
 
-def take_got(refs, n):
-    return refs.take(), refs.take(n // 2 - 1), refs.take(n // 2 - 1)
+def take_got(refs, c):
+    far, near = refs.take(), refs.take(c["n"] // 2 - 1)
+    if c["joined"]:
+        return far, near, [ref.at[c["tile"] :, :] for ref in near]
+    return far, near, refs.take(c["n"] // 2 - 1)
 
 
 def spread_of(adj_ref, own_ref, got, names_ref, c):
@@ -185,7 +194,7 @@
         last_ref, passed_ref = refs.take(2)
     else:
         adj_ref, own_ref = refs.take(2)
-        got = take_got(refs, n)
+        got = take_got(refs, c)
     if c["final"]:
         support_all, acc_ref = refs.take(2)
     image_ref = refs.take()
@@ -237,11 +246,18 @@
         out_ref[...] = masked
 
 
-def select_kernel(c, first, image_ref, *refs):
-    count = c["n"] // 2 - 1
-    for asked_ref, send in zip(refs[:count], refs[count:]):
-        row = 2 * c["tick"] + first
-        send[...] = chosen(image_ref, asked_ref[row : row + 1, :], c["rows"], c["tile"])
+def forward_kernel(c, *refs):
+    refs = Refs(refs)
+    count, tile, rows = c["n"] // 2 - 1, c["tile"], c["rows"]
+    far_ref = refs.take()
+    own_ref = refs.take() if c["first"] else None
+    for asked_ref, send in zip(refs.take(count), refs.take(count)):
+        row = 2 * c["tick"]
+        if c["first"]:
+            send[:tile, :] = chosen(own_ref, asked_ref[row : row + 1, :], rows, tile)
+            send[tile:, :] = chosen(far_ref, asked_ref[row + 1 : row + 2, :], rows, tile)
+        else:
+            send[...] = chosen(far_ref, asked_ref[row + 1 : row + 2, :], rows, tile)
 
 
 def half_sum_kernel(tile, kept_ref, *refs):
@@ -261,7 +277,7 @@
 def exit_kernel(c, *refs):
     refs = Refs(refs)
     names_ref, adj_ref, own_ref = refs.take(3)
-    got = take_got(refs, c["n"])
+    got = take_got(refs, c)
     if not c["final"]:
         refs.take()[...] = spread_of(adj_ref, own_ref, got, names_ref, c)
         return
@@ -306,7 +322,7 @@
     tile = tile_vals.shape[-1]
     row_tiles = rows // tile
     chunk = width // h
-    counts = tile_count.reshape(1, ticks)
+    words = packed(tile_row, tile_col, tile_count, row_tiles)
 
     handed = []
     passed = None
@@ -318,41 +334,32 @@
     small_cost = cost(rows * width, 2 * n * rows * width)
     relay_cost = cost(rows * width, 8 * n * rows * width)
     call = Call()
-    call.give(VMEM, tile_col)
+    call.give(VMEM, words)
     call.want(VMEM, (ticks, width), F32)
     call.want(VMEM, (2 * ticks, width), F32, h - 1)
     names, *asking = call.run(functools.partial(name_kernel, n, row_tiles), "name", small_cost)
     asked = shared(asking)
-
-    def select(c, first, block):
-        call = Call()
-        call.give(VMEM, block, *asked)
-        call.want(VMEM, (tile, width), BF16, h - 1)
-        return call.run(functools.partial(select_kernel, c, first), "select", small_cost)
 
     adjs = [None] * ticks
     for tick in range(ticks):
         final = tick == ticks - 1
         if tick > 0:
             passed = passed_along(handed[-1], "section", -1)
-        image = got = None
+        image = got = joined = None
         toward = 0.0
         for layer in reversed(range(layers)):
             entry = layer == layers - 1
             beta = jnp.log(BETA_SCALE / (layers * section + layer + 1).astype(F32) + 1.0)
             c = dict(
-                base, layer=layer, tick=tick, entry=entry, final=final
+                base, layer=layer, tick=tick, entry=entry, final=final, joined=joined,
+                first=tick == 0 and entry,
             )
-            first = tick == 0 and entry
-            if first:
+            if c["first"]:
                 masked = jnp.where(
                     preact[0, tick, layer] > 0, grad_in[0], jnp.zeros_like(grad_in[0])
                 )
                 product = jnp.dot(masked, weights[0, layer].T, preferred_element_type=F32)
                 image = ((1.0 - beta) * masked.astype(F32) + beta * product).astype(BF16)
-                adjs[0] = densify(0, tile_row, tile_col, counts, tile_vals, row_tiles, n)
-                ready, adjs[0] = lax.optimization_barrier((image, adjs[0]))
-                sends = select(c, 0, ready)
             else:
                 call = Call()
                 call.give(HBM, preact, weights)
@@ -388,16 +395,21 @@
                 sends = results.take(h - 1)
                 kept = masked = results.take()
             far = swapped(image, h)
-            near = shared(sends)
-            relays = select(c, 1, far)
+            near = [] if c["first"] else shared(sends)
+            call = Call()
+            call.give(VMEM, far)
+            if c["first"]:
+                adjs[0] = densify(0, words, tile_vals, row_tiles, n)
+                ready, adjs[0] = lax.optimization_barrier((image, adjs[0]))
+                call.give(VMEM, ready)
+            call.give(VMEM, *asked)
+            call.want(VMEM, (tile * (1 + c["first"]), width), BF16, h - 1)
+            relays = call.run(functools.partial(forward_kernel, c), "forward", small_cost)
             relayed = shared(relays)
-            if first:
-                cols, *_ = lax.optimization_barrier((tile_col, *near))
-                adjs[1:] = [
-                    densify(t, tile_row, cols, counts, tile_vals, row_tiles, n)
-                    for t in range(1, ticks)
-                ]
-                adjs = list(lax.optimization_barrier(adjs))
+            if layer == 0 and not final:
+                later, *_ = lax.optimization_barrier((words, *near))
+                adjs[tick + 1] = densify(tick + 1, later, tile_vals, row_tiles, n)
+                relayed, adjs[tick + 1] = lax.optimization_barrier((relayed, adjs[tick + 1]))
             if final:
                 kept, *_ = lax.optimization_barrier((kept, *relays))
                 call = Call()
@@ -406,13 +418,11 @@
                 (mine,) = call.run(
                     functools.partial(half_sum_kernel, tile), "half_sum", small_cost
                 )
-                if layer == 0:
-                    weight_sums = [mine, swapped(mine, h), *weight_sums]
-                    relayed, weight_sums = lax.optimization_barrier((relayed, weight_sums))
-                else:
+                if layer > 0:
                     relayed, mine = lax.optimization_barrier((relayed, mine))
-                    weight_sums = [mine, swapped(mine, h), *weight_sums]
+                weight_sums = [mine, swapped(mine, h), *weight_sums]
             got = [far, *near, *relayed]
+            joined = c["first"]
             toward = toward + ALPHA * image.astype(F32)
             if not final:
                 term = beta * jnp.dot(
@@ -421,7 +431,7 @@
                 old = weight_acc[layer]
                 weight_acc[layer] = term if old is None else old + term
         initial.append(toward)
-        c = dict(base, tick=tick, final=final)
+        c = dict(base, tick=tick, final=final, joined=joined)
         call = Call()
         call.give(VMEM, names, adjs[tick], image, *got)
         if final:

time: 90.4 us -> 87.2 us (0.965)
  starting transfers between devices: 47.4 us -> 43.4 us
  local copies, waits for them, and re-layouts: 2.84 us -> 0.16 us
  Pallas kernels: 11.7 us -> 13.2 us
  other arithmetic: 0.91 us -> 2.28 us
    ppermute x36 -> x33, starting transfers between devices: 46.1 us -> 42.1 us  [swapped(): return lax.ppermute(block, 'rows', [(i, i ^ k) for i in range(n)])]
    unnamed x18 -> x10, local copies, waits for them, and re-layouts: 2.72 us -> 0.03 us
    pallas_call x17 -> x16, Pallas kernels: 11.7 us -> 13.2 us  [run(): pl.pallas_call(kernel, out_shape=self.outs, in_specs=self.specs, out_spec...]
    ppermute x36 -> x33, waiting for transfers between devices: 22.7 us -> 23.3 us  [swapped(): return lax.ppermute(block, 'rows', [(i, i ^ k) for i in range(n)])]
  transfers between devices with their start and end apart: 37 -> 34, of which waited for: 13 -> 16; matrix products, arithmetic and copies ran while one was open for 2% -> 3% of each run, Pallas kernels for 8% -> 10%
where the time goes in v10:
time: 87.2 us; the launch traced here: 86.9 us
  starting transfers between devices  43.4 us (50%)
  waiting for transfers between devices  24.8 us (28%)
  Pallas kernels  13.2 us (15%)
  other arithmetic  2.28 us (3%)
  matrix products  1.9 us (2%)
  between operations  1.1 us (1%)
    ppermute x33, starting transfers between devices, swapped(): return lax.ppermute(block, 'rows', [(i, i ^ k) for i in range(n)])  42.1 us
    ppermute x33, waiting for transfers between devices, swapped(): return lax.ppermute(block, 'rows', [(i, i ^ k) for i in range(n)])  23.3 us
    pallas_call x16, Pallas kernels, run(): pl.pallas_call(kernel, out_shape=self.outs, in_specs=self.specs, out_spec...  13.2 us
  transfers between devices with their start and end apart: 34, of which 16 were waited for; matrix products, arithmetic and copies ran while one was open for 3% of the time, Pallas kernels for 10%

profile of v10, /device:TPU:0, one launch (start us, length us, event | category | flops | bytes accessed | tf_op | source)
XLA Modules:
  0.0 86.9 jit_solution(16495603413482328215)
XLA Ops:
  0.7 1.4 %fusion.3.refs_1_.refs_7_ = bf16[256,256]{1,0:T(8,128)(2,1)S(1)} fusion(bf16[1,256,256]{2,1,0:T(8,128)(2,1)} %param.9, bf16[1,2,256,256]{3,2,1,0:T(8,128)(2,1)} %refs_1_.5, f32[]{:T(128)S(6)} %log.6, f32[]{:T(128)S(6)} %sub.10, bf16[1,2,2,256,256]{4,3,2,1,0:T(8,128)(2,1)} %refs_0_.5), kind=kOutput, calls=%fused_computation.6 | convolution fusion | flops 34144256 | bytes 786440 | tf_op jit(solution)/shard_map/dot_general | solution.py:361
  2.2 4.1 %collective-permute-start.3 = (bf16[256,256]{1,0:T(8,128)(2,1)S(1)}, bf16[256,256]{1,0:T(8,128)(2,1)S(1)}, u32[]{:S(2)}, u32[]{:S(2)}) collective-permute-start(bf16[256,256]{1,0:T(8,128)(2,1)S(1)} %fusion.3.refs_1_.refs_7_), channel_id=1, source_target_pairs={{0,4},{1,5},{2,6},{3,7},{4,0},{5,1},{6,2},{7,3},{8,12},{9,13},{10,... | collective-permute-start | bytes 393224 | tf_op jit(solution)/shard_map/ppermute | solution.py:26
  7.8 1.6 %collective-permute-start = (f32[4,256]{1,0:T(4,128)S(1)}, f32[4,256]{1,0:T(4,128)S(1)}, u32[]{:S(2)}, u32[]{:S(2)}) collective-permute-start(f32[4,256]{1,0:T(4,128)S(1)} %get-tuple-element.48), channel_id=1, source_target_pairs={{0,1},{1,0},{2,3},{3,2},{4,5},{5,4},{6,7},{7,6},{8,9},{9,8},{10,11... | collective-permute-start | bytes 12296 | tf_op jit(solution)/shard_map/ppermute | solution.py:26
  9.3 1.6 %collective-permute-start.1 = (f32[4,256]{1,0:T(4,128)S(1)}, f32[4,256]{1,0:T(4,128)S(1)}, u32[]{:S(2)}, u32[]{:S(2)}) collective-permute-start(f32[4,256]{1,0:T(4,128)S(1)} %get-tuple-element.49), channel_id=1, source_target_pairs={{0,2},{1,3},{2,0},{3,1},{4,6},{5,7},{6,4},{7,5},{8,10},{9,11},{10,... | collective-permute-start | bytes 12296 | tf_op jit(solution)/shard_map/ppermute | solution.py:26
  11.3 3.7 %densify.2.refs_6_.refs_1_ = bf16[256,1152]{1,0:T(8,128)(2,1)S(1)} custom-call(s32[3,96]{1,0:T(4,128)S(1)} %pad_add_fusion.words_ref, bf16[1,2,96,128,128]{4,3,2,1,0:T(8,128)(2,1)} %vals_ref.3), custom_call_target="tpu_custom_call" | custom-call | flops 31457280 | bytes 3145728 | tf_op jit(solution)/shard_map/densify/pallas_call | solution.py:64
  19.0 2.7 %collective-permute-done.4.refs_9_ = bf16[256,256]{1,0:T(8,128)(2,1)S(1)} collective-permute-done((bf16[256,256]{1,0:T(8,128)(2,1)S(1)}, bf16[256,256]{1,0:T(8,128)(2,1)S(1)}, u32[]{:S(2)}, u32[]{:S(2)}) %collective-permute-start.4) | collective-permute-done | bytes 131104 | tf_op jit(solution)/shard_map/ppermute | solution.py:26
  21.8 2.3 %collective-permute-done.6.refs_11_ = bf16[256,256]{1,0:T(8,128)(2,1)S(1)} collective-permute-done((bf16[256,256]{1,0:T(8,128)(2,1)S(1)}, bf16[256,256]{1,0:T(8,128)(2,1)S(1)}, u32[]{:S(2)}, u32[]{:S(2)}) %collective-permute-start.6) | collective-permute-done | bytes 131104 | tf_op jit(solution)/shard_map/ppermute | solution.py:26
  27.1 1.7 %collective-permute-start.12 = (bf16[128,256]{1,0:T(8,128)(2,1)S(1)}, bf16[128,256]{1,0:T(8,128)(2,1)S(1)}, u32[]{:S(2)}, u32[]{:S(2)}) collective-permute-start(bf16[128,256]{1,0:T(8,128)(2,1)S(1)} %get-tuple-element.61), channel_id=1, source_target_pairs={{0,2},{1,3},{2,0},{3,1},{4,6},{5,7},{6,4},{7,5},{8,10},{9,11},{10,... | collective-permute-start | bytes 196616 | tf_op jit(solution)/shard_map/ppermute | solution.py:26
  29.7 2.9 %collective-permute-done.7.refs_0_.refs_3_ = bf16[256,256]{1,0:T(8,128)(2,1)S(1)} collective-permute-done((bf16[256,256]{1,0:T(8,128)(2,1)S(1)}, bf16[256,256]{1,0:T(8,128)(2,1)S(1)}, u32[]{:S(2)}, u32[]{:S(2)}) %collective-permute-start.7) | collective-permute-done | bytes 131104 | tf_op jit(solution)/shard_map/ppermute | solution.py:26
  33.6 2.6 %collective-permute-start.10 = (bf16[128,256]{1,0:T(8,128)(2,1)S(1)}, bf16[128,256]{1,0:T(8,128)(2,1)S(1)}, u32[]{:S(2)}, u32[]{:S(2)}) collective-permute-start(bf16[128,256]{1,0:T(8,128)(2,1)S(1)} %get-tuple-element.59), channel_id=1, source_target_pairs={{0,3},{1,2},{2,1},{3,0},{4,7},{5,6},{6,5},{7,4},{8,11},{9,10},{10,... | collective-permute-start | bytes 196616 | tf_op jit(solution)/shard_map/ppermute | solution.py:26
  36.2 3.8 %densify.3.refs_6_.refs_1_ = bf16[256,1152]{1,0:T(8,128)(2,1)S(1)} custom-call(s32[3,96]{1,0:T(4,128)S(1)} %pad_add_fusion.words_ref, bf16[1,2,96,128,128]{4,3,2,1,0:T(8,128)(2,1)} %vals_ref.3), custom_call_target="tpu_custom_call" | custom-call | flops 31457280 | bytes 3145728 | tf_op jit(solution)/shard_map/densify/pallas_call | solution.py:64
  42.1 1.5 %collective-permute-done.14.refs_7_ = bf16[256,256]{1,0:T(8,128)(2,1)S(1)} collective-permute-done((bf16[256,256]{1,0:T(8,128)(2,1)S(1)}, bf16[256,256]{1,0:T(8,128)(2,1)S(1)}, u32[]{:S(2)}, u32[]{:S(2)}) %collective-permute-start.14) | collective-permute-done | bytes 131104 | tf_op jit(solution)/shard_map/ppermute | solution.py:37
  44.5 1.6 %collective-permute-start.15 = (bf16[256,256]{1,0:T(8,128)(2,1)S(1)}, bf16[256,256]{1,0:T(8,128)(2,1)S(1)}, u32[]{:S(2)}, u32[]{:S(2)}) collective-permute-start(bf16[256,256]{1,0:T(8,128)(2,1)S(1)} %get-tuple-element.68.refs_7_), channel_id=1, source_target_pairs={{0,4},{1,5},{2,6},{3,7},{4,0},{5,1},{6,2},{7,3},{8,12},{9,13},{10,... | collective-permute-start | bytes 393224 | tf_op jit(solution)/shard_map/ppermute | solution.py:26
  48.3 1.4 %collective-permute-start.18 = (bf16[192,256]{1,0:T(8,128)(2,1)S(1)}, bf16[192,256]{1,0:T(8,128)(2,1)S(1)}, u32[]{:S(2)}, u32[]{:S(2)}) collective-permute-start(bf16[192,256]{1,0:T(8,128)(2,1)S(1)} %get-tuple-element.71), channel_id=1, source_target_pairs={{0,3},{1,2},{2,1},{3,0},{4,7},{5,6},{6,5},{7,4},{8,11},{9,10},{10,... | collective-permute-start | bytes 294920 | tf_op jit(solution)/shard_map/ppermute | solution.py:26
  49.7 4.3 %collective-permute-done.15.refs_0_.refs_8_ = bf16[256,256]{1,0:T(8,128)(2,1)S(1)} collective-permute-done((bf16[256,256]{1,0:T(8,128)(2,1)S(1)}, bf16[256,256]{1,0:T(8,128)(2,1)S(1)}, u32[]{:S(2)}, u32[]{:S(2)}) %collective-permute-start.15) | collective-permute-done | bytes 131104 | tf_op jit(solution)/shard_map/ppermute | solution.py:26
  54.4 3.2 %collective-permute-start.21 = (bf16[128,256]{1,0:T(8,128)(2,1)S(1)}, bf16[128,256]{1,0:T(8,128)(2,1)S(1)}, u32[]{:S(2)}, u32[]{:S(2)}) collective-permute-start(bf16[128,256]{1,0:T(8,128)(2,1)S(1)} %get-tuple-element.74), channel_id=1, source_target_pairs={{0,3},{1,2},{2,1},{3,0},{4,7},{5,6},{6,5},{7,4},{8,11},{9,10},{10,... | collective-permute-start | bytes 196616 | tf_op jit(solution)/shard_map/ppermute | solution.py:26
  59.2 2.1 %collective-permute-done.21.refs_14_ = bf16[128,256]{1,0:T(8,128)(2,1)S(1)} collective-permute-done((bf16[128,256]{1,0:T(8,128)(2,1)S(1)}, bf16[128,256]{1,0:T(8,128)(2,1)S(1)}, u32[]{:S(2)}, u32[]{:S(2)}) %collective-permute-start.21) | collective-permute-done | bytes 65568 | tf_op jit(solution)/shard_map/ppermute | solution.py:26
  62.6 1.8 %collective-permute-start.22 = (bf16[256,256]{1,0:T(8,128)(2,1)S(1)}, bf16[256,256]{1,0:T(8,128)(2,1)S(1)}, u32[]{:S(2)}, u32[]{:S(2)}) collective-permute-start(bf16[256,256]{1,0:T(8,128)(2,1)S(1)} %get-tuple-element.81.refs_2_), channel_id=1, source_target_pairs={{0,4},{1,5},{2,6},{3,7},{4,0},{5,1},{6,2},{7,3},{8,12},{9,13},{10,... | collective-permute-start | bytes 393224 | tf_op jit(solution)/shard_map/ppermute | solution.py:26
  64.4 1.5 %collective-permute-start.23 = (bf16[192,256]{1,0:T(8,128)(2,1)S(1)}, bf16[192,256]{1,0:T(8,128)(2,1)S(1)}, u32[]{:S(2)}, u32[]{:S(2)}) collective-permute-start(bf16[192,256]{1,0:T(8,128)(2,1)S(1)} %get-tuple-element.82), channel_id=1, source_target_pairs={{0,1},{1,0},{2,3},{3,2},{4,5},{5,4},{6,7},{7,6},{8,9},{9,8},{10,11... | collective-permute-start | bytes 294920 | tf_op jit(solution)/shard_map/ppermute | solution.py:26
  69.2 2.2 %collective-permute-done.22.refs_0_.refs_3_ = bf16[256,256]{1,0:T(8,128)(2,1)S(1)} collective-permute-done((bf16[256,256]{1,0:T(8,128)(2,1)S(1)}, bf16[256,256]{1,0:T(8,128)(2,1)S(1)}, u32[]{:S(2)}, u32[]{:S(2)}) %collective-permute-start.22) | collective-permute-done | bytes 131104 | tf_op jit(solution)/shard_map/ppermute | solution.py:26
  74.8 2.4 %collective-permute-start.27 = (bf16[128,256]{1,0:T(8,128)(2,1)S(1)}, bf16[128,256]{1,0:T(8,128)(2,1)S(1)}, u32[]{:S(2)}, u32[]{:S(2)}) collective-permute-start(bf16[128,256]{1,0:T(8,128)(2,1)S(1)} %get-tuple-element.86), channel_id=1, source_target_pairs={{0,2},{1,3},{2,0},{3,1},{4,6},{5,7},{6,4},{7,5},{8,10},{9,11},{10,... | collective-permute-start | bytes 196616 | tf_op jit(solution)/shard_map/ppermute | solution.py:26
  77.5 1.9 %collective-permute-done.29.refs_1_ = bf16[64,256]{1,0:T(8,128)(2,1)S(1)} collective-permute-done((bf16[64,256]{1,0:T(8,128)(2,1)S(1)}, bf16[64,256]{1,0:T(8,128)(2,1)S(1)}, u32[]{:S(2)}, u32[]{:S(2)}) %collective-permute-start.29) | collective-permute-done | bytes 32800 | tf_op jit(solution)/shard_map/ppermute | solution.py:26
  79.4 1.5 %collective-permute-start.31 = (bf16[2,64,256]{2,1,0:T(8,128)(2,1)S(1)}, bf16[2,64,256]{2,1,0:T(8,128)(2,1)S(1)}, u32[]{:S(2)}, u32[]{:S(2)}) collective-permute-start(bf16[2,64,256]{2,1,0:T(8,128)(2,1)S(1)} %total.1.refs_0_), channel_id=1, source_target_pairs={{0,1},{1,0},{2,3},{3,2},{4,5},{5,4},{6,7},{7,6},{8,9},{9,8},{10,11... | collective-permute-start | bytes 196616 | tf_op jit(solution)/shard_map/ppermute | solution.py:26
  80.9 2.0 %collective-permute-start.33 = (bf16[2,64,256]{2,1,0:T(8,128)(2,1)S(1)}, bf16[2,64,256]{2,1,0:T(8,128)(2,1)S(1)}, u32[]{:S(2)}, u32[]{:S(2)}) collective-permute-start(bf16[2,64,256]{2,1,0:T(8,128)(2,1)S(1)} %total.1.refs_0_), channel_id=1, source_target_pairs={{0,3},{1,2},{2,1},{3,0},{4,7},{5,6},{6,5},{7,4},{8,11},{9,10},{10,... | collective-permute-start | bytes 196616 | tf_op jit(solution)/shard_map/ppermute | solution.py:26
  (79 shorter events, 29.9 us)
Async XLA Ops:
  2.2 13.2 %collective-permute-start.3 = (bf16[256,256]{1,0:T(8,128)(2,1)S(1)}, bf16[256,256]{1,0:T(8,128)(2,1)S(1)}, u32[]{:S(2)}, u32[]{:S(2)}) collective-permute-start(bf16[256,256]{1,0:T(8,128)(2,1)S(1)} %fusion.3.refs_1_.refs_7_), channel_id=1, source_target_pairs={{0,4},{1,5},{2,6},{3,7},{4,0},{5,1},{6,2},{7,3},{8,12},{9,13},{10,... | collective-permute-start | bytes 393224 | tf_op jit(solution)/shard_map/ppermute | solution.py:26
  7.8 7.3 %collective-permute-start = (f32[4,256]{1,0:T(4,128)S(1)}, f32[4,256]{1,0:T(4,128)S(1)}, u32[]{:S(2)}, u32[]{:S(2)}) collective-permute-start(f32[4,256]{1,0:T(4,128)S(1)} %get-tuple-element.48), channel_id=1, source_target_pairs={{0,1},{1,0},{2,3},{3,2},{4,5},{5,4},{6,7},{7,6},{8,9},{9,8},{10,11... | collective-permute-start | bytes 12296 | tf_op jit(solution)/shard_map/ppermute | solution.py:26
  15.5 6.3 %collective-permute-start.4 = (bf16[256,256]{1,0:T(8,128)(2,1)S(1)}, bf16[256,256]{1,0:T(8,128)(2,1)S(1)}, u32[]{:S(2)}, u32[]{:S(2)}) collective-permute-start(bf16[256,256]{1,0:T(8,128)(2,1)S(1)} %get-tuple-element.53), channel_id=1, source_target_pairs={{0,1},{1,0},{2,3},{3,2},{4,5},{5,4},{6,7},{7,6},{8,9},{9,8},{10,11... | collective-permute-start | bytes 393224 | tf_op jit(solution)/shard_map/ppermute | solution.py:26
  18.2 5.9 %collective-permute-start.6 = (bf16[256,256]{1,0:T(8,128)(2,1)S(1)}, bf16[256,256]{1,0:T(8,128)(2,1)S(1)}, u32[]{:S(2)}, u32[]{:S(2)}) collective-permute-start(bf16[256,256]{1,0:T(8,128)(2,1)S(1)} %get-tuple-element.55), channel_id=1, source_target_pairs={{0,3},{1,2},{2,1},{3,0},{4,7},{5,6},{6,5},{7,4},{8,11},{9,10},{10,... | collective-permute-start | bytes 393224 | tf_op jit(solution)/shard_map/ppermute | solution.py:26
  25.1 7.4 %collective-permute-start.7 = (bf16[256,256]{1,0:T(8,128)(2,1)S(1)}, bf16[256,256]{1,0:T(8,128)(2,1)S(1)}, u32[]{:S(2)}, u32[]{:S(2)}) collective-permute-start(bf16[256,256]{1,0:T(8,128)(2,1)S(1)} %get-tuple-element.56.refs_2_), channel_id=1, source_target_pairs={{0,4},{1,5},{2,6},{3,7},{4,0},{5,1},{6,2},{7,3},{8,12},{9,13},{10,... | collective-permute-start | bytes 393224 | tf_op jit(solution)/shard_map/ppermute | solution.py:26
  26.2 7.4 %collective-permute-start.11 = (bf16[128,256]{1,0:T(8,128)(2,1)S(1)}, bf16[128,256]{1,0:T(8,128)(2,1)S(1)}, u32[]{:S(2)}, u32[]{:S(2)}) collective-permute-start(bf16[128,256]{1,0:T(8,128)(2,1)S(1)} %get-tuple-element.60), channel_id=1, source_target_pairs={{0,1},{1,0},{2,3},{3,2},{4,5},{5,4},{6,7},{7,6},{8,9},{9,8},{10,11... | collective-permute-start | bytes 196616 | tf_op jit(solution)/shard_map/ppermute | solution.py:26
  27.1 9.1 %collective-permute-start.12 = (bf16[128,256]{1,0:T(8,128)(2,1)S(1)}, bf16[128,256]{1,0:T(8,128)(2,1)S(1)}, u32[]{:S(2)}, u32[]{:S(2)}) collective-permute-start(bf16[128,256]{1,0:T(8,128)(2,1)S(1)} %get-tuple-element.61), channel_id=1, source_target_pairs={{0,2},{1,3},{2,0},{3,1},{4,6},{5,7},{6,4},{7,5},{8,10},{9,11},{10,... | collective-permute-start | bytes 196616 | tf_op jit(solution)/shard_map/ppermute | solution.py:26
  28.8 7.4 %collective-permute-start.13 = (bf16[128,256]{1,0:T(8,128)(2,1)S(1)}, bf16[128,256]{1,0:T(8,128)(2,1)S(1)}, u32[]{:S(2)}, u32[]{:S(2)}) collective-permute-start(bf16[128,256]{1,0:T(8,128)(2,1)S(1)} %get-tuple-element.62), channel_id=1, source_target_pairs={{0,3},{1,2},{2,1},{3,0},{4,7},{5,6},{6,5},{7,4},{8,11},{9,10},{10,... | collective-permute-start | bytes 196616 | tf_op jit(solution)/shard_map/ppermute | solution.py:26
  32.6 7.4 %collective-permute-start.8 = (bf16[128,256]{1,0:T(8,128)(2,1)S(1)}, bf16[128,256]{1,0:T(8,128)(2,1)S(1)}, u32[]{:S(2)}, u32[]{:S(2)}) collective-permute-start(bf16[128,256]{1,0:T(8,128)(2,1)S(1)} %get-tuple-element.57), channel_id=1, source_target_pairs={{0,1},{1,0},{2,3},{3,2},{4,5},{5,4},{6,7},{7,6},{8,9},{9,8},{10,11... | collective-permute-start | bytes 196616 | tf_op jit(solution)/shard_map/ppermute | solution.py:26
  33.3 6.8 %collective-permute-start.9 = (bf16[128,256]{1,0:T(8,128)(2,1)S(1)}, bf16[128,256]{1,0:T(8,128)(2,1)S(1)}, u32[]{:S(2)}, u32[]{:S(2)}) collective-permute-start(bf16[128,256]{1,0:T(8,128)(2,1)S(1)} %get-tuple-element.58), channel_id=1, source_target_pairs={{0,2},{1,3},{2,0},{3,1},{4,6},{5,7},{6,4},{7,5},{8,10},{9,11},{10,... | collective-permute-start | bytes 196616 | tf_op jit(solution)/shard_map/ppermute | solution.py:26
  33.6 6.5 %collective-permute-start.10 = (bf16[128,256]{1,0:T(8,128)(2,1)S(1)}, bf16[128,256]{1,0:T(8,128)(2,1)S(1)}, u32[]{:S(2)}, u32[]{:S(2)}) collective-permute-start(bf16[128,256]{1,0:T(8,128)(2,1)S(1)} %get-tuple-element.59), channel_id=1, source_target_pairs={{0,3},{1,2},{2,1},{3,0},{4,7},{5,6},{6,5},{7,4},{8,11},{9,10},{10,... | collective-permute-start | bytes 196616 | tf_op jit(solution)/shard_map/ppermute | solution.py:26
  44.5 9.5 %collective-permute-start.15 = (bf16[256,256]{1,0:T(8,128)(2,1)S(1)}, bf16[256,256]{1,0:T(8,128)(2,1)S(1)}, u32[]{:S(2)}, u32[]{:S(2)}) collective-permute-start(bf16[256,256]{1,0:T(8,128)(2,1)S(1)} %get-tuple-element.68.refs_7_), channel_id=1, source_target_pairs={{0,4},{1,5},{2,6},{3,7},{4,0},{5,1},{6,2},{7,3},{8,12},{9,13},{10,... | collective-permute-start | bytes 393224 | tf_op jit(solution)/shard_map/ppermute | solution.py:26
  46.1 8.3 %collective-permute-start.16 = (bf16[192,256]{1,0:T(8,128)(2,1)S(1)}, bf16[192,256]{1,0:T(8,128)(2,1)S(1)}, u32[]{:S(2)}, u32[]{:S(2)}) collective-permute-start(bf16[192,256]{1,0:T(8,128)(2,1)S(1)} %get-tuple-element.69), channel_id=1, source_target_pairs={{0,1},{1,0},{2,3},{3,2},{4,5},{5,4},{6,7},{7,6},{8,9},{9,8},{10,11... | collective-permute-start | bytes 294920 | tf_op jit(solution)/shard_map/ppermute | solution.py:26
  47.2 10.6 %collective-permute-start.17 = (bf16[192,256]{1,0:T(8,128)(2,1)S(1)}, bf16[192,256]{1,0:T(8,128)(2,1)S(1)}, u32[]{:S(2)}, u32[]{:S(2)}) collective-permute-start(bf16[192,256]{1,0:T(8,128)(2,1)S(1)} %get-tuple-element.70), channel_id=1, source_target_pairs={{0,2},{1,3},{2,0},{3,1},{4,6},{5,7},{6,4},{7,5},{8,10},{9,11},{10,... | collective-permute-start | bytes 294920 | tf_op jit(solution)/shard_map/ppermute | solution.py:26
  48.3 9.6 %collective-permute-start.18 = (bf16[192,256]{1,0:T(8,128)(2,1)S(1)}, bf16[192,256]{1,0:T(8,128)(2,1)S(1)}, u32[]{:S(2)}, u32[]{:S(2)}) collective-permute-start(bf16[192,256]{1,0:T(8,128)(2,1)S(1)} %get-tuple-element.71), channel_id=1, source_target_pairs={{0,3},{1,2},{2,1},{3,0},{4,7},{5,6},{6,5},{7,4},{8,11},{9,10},{10,... | collective-permute-start | bytes 294920 | tf_op jit(solution)/shard_map/ppermute | solution.py:26
  54.4 6.9 %collective-permute-start.21 = (bf16[128,256]{1,0:T(8,128)(2,1)S(1)}, bf16[128,256]{1,0:T(8,128)(2,1)S(1)}, u32[]{:S(2)}, u32[]{:S(2)}) collective-permute-start(bf16[128,256]{1,0:T(8,128)(2,1)S(1)} %get-tuple-element.74), channel_id=1, source_target_pairs={{0,3},{1,2},{2,1},{3,0},{4,7},{5,6},{6,5},{7,4},{8,11},{9,10},{10,... | collective-permute-start | bytes 196616 | tf_op jit(solution)/shard_map/ppermute | solution.py:26
  62.6 8.8 %collective-permute-start.22 = (bf16[256,256]{1,0:T(8,128)(2,1)S(1)}, bf16[256,256]{1,0:T(8,128)(2,1)S(1)}, u32[]{:S(2)}, u32[]{:S(2)}) collective-permute-start(bf16[256,256]{1,0:T(8,128)(2,1)S(1)} %get-tuple-element.81.refs_2_), channel_id=1, source_target_pairs={{0,4},{1,5},{2,6},{3,7},{4,0},{5,1},{6,2},{7,3},{8,12},{9,13},{10,... | collective-permute-start | bytes 393224 | tf_op jit(solution)/shard_map/ppermute | solution.py:26
  64.4 8.0 %collective-permute-start.23 = (bf16[192,256]{1,0:T(8,128)(2,1)S(1)}, bf16[192,256]{1,0:T(8,128)(2,1)S(1)}, u32[]{:S(2)}, u32[]{:S(2)}) collective-permute-start(bf16[192,256]{1,0:T(8,128)(2,1)S(1)} %get-tuple-element.82), channel_id=1, source_target_pairs={{0,1},{1,0},{2,3},{3,2},{4,5},{5,4},{6,7},{7,6},{8,9},{9,8},{10,11... | collective-permute-start | bytes 294920 | tf_op jit(solution)/shard_map/ppermute | solution.py:26
  65.9 7.3 %collective-permute-start.24 = (bf16[192,256]{1,0:T(8,128)(2,1)S(1)}, bf16[192,256]{1,0:T(8,128)(2,1)S(1)}, u32[]{:S(2)}, u32[]{:S(2)}) collective-permute-start(bf16[192,256]{1,0:T(8,128)(2,1)S(1)} %get-tuple-element.83), channel_id=1, source_target_pairs={{0,2},{1,3},{2,0},{3,1},{4,6},{5,7},{6,4},{7,5},{8,10},{9,11},{10,... | collective-permute-start | bytes 294920 | tf_op jit(solution)/shard_map/ppermute | solution.py:26
  66.5 7.9 %collective-permute-start.25 = (bf16[192,256]{1,0:T(8,128)(2,1)S(1)}, bf16[192,256]{1,0:T(8,128)(2,1)S(1)}, u32[]{:S(2)}, u32[]{:S(2)}) collective-permute-start(bf16[192,256]{1,0:T(8,128)(2,1)S(1)} %get-tuple-element.84), channel_id=1, source_target_pairs={{0,3},{1,2},{2,1},{3,0},{4,7},{5,6},{6,5},{7,4},{8,11},{9,10},{10,... | collective-permute-start | bytes 294920 | tf_op jit(solution)/shard_map/ppermute | solution.py:26
  67.9 9.5 %collective-permute-start.30 = (bf16[64,256]{1,0:T(8,128)(2,1)S(1)}, bf16[64,256]{1,0:T(8,128)(2,1)S(1)}, u32[]{:S(2)}, u32[]{:S(2)}) collective-permute-start(bf16[64,256]{1,0:T(8,128)(2,1)S(1)} %half_sum.2.refs_2_), channel_id=1, source_target_pairs={{0,4},{1,5},{2,6},{3,7},{4,0},{5,1},{6,2},{7,3},{8,12},{9,13},{10,... | collective-permute-start | bytes 98312 | tf_op jit(solution)/shard_map/ppermute | solution.py:26
  71.4 9.4 %collective-permute-start.26 = (bf16[128,256]{1,0:T(8,128)(2,1)S(1)}, bf16[128,256]{1,0:T(8,128)(2,1)S(1)}, u32[]{:S(2)}, u32[]{:S(2)}) collective-permute-start(bf16[128,256]{1,0:T(8,128)(2,1)S(1)} %get-tuple-element.85), channel_id=1, source_target_pairs={{0,1},{1,0},{2,3},{3,2},{4,5},{5,4},{6,7},{7,6},{8,9},{9,8},{10,11... | collective-permute-start | bytes 196616 | tf_op jit(solution)/shard_map/ppermute | solution.py:26
  74.8 8.9 %collective-permute-start.27 = (bf16[128,256]{1,0:T(8,128)(2,1)S(1)}, bf16[128,256]{1,0:T(8,128)(2,1)S(1)}, u32[]{:S(2)}, u32[]{:S(2)}) collective-permute-start(bf16[128,256]{1,0:T(8,128)(2,1)S(1)} %get-tuple-element.86), channel_id=1, source_target_pairs={{0,2},{1,3},{2,0},{3,1},{4,6},{5,7},{6,4},{7,5},{8,10},{9,11},{10,... | collective-permute-start | bytes 196616 | tf_op jit(solution)/shard_map/ppermute | solution.py:26
  77.3 6.5 %collective-permute-start.28 = (bf16[128,256]{1,0:T(8,128)(2,1)S(1)}, bf16[128,256]{1,0:T(8,128)(2,1)S(1)}, u32[]{:S(2)}, u32[]{:S(2)}) collective-permute-start(bf16[128,256]{1,0:T(8,128)(2,1)S(1)} %get-tuple-element.87), channel_id=1, source_target_pairs={{0,3},{1,2},{2,1},{3,0},{4,7},{5,6},{6,5},{7,4},{8,11},{9,10},{10,... | collective-permute-start | bytes 196616 | tf_op jit(solution)/shard_map/ppermute | solution.py:26
  (15 other events, 177.0 us)

commit v11 on v10

--- a/solution.py
+++ b/solution.py
@@ -228,9 +228,10 @@
     )
     image = ((1.0 - beta) * masked.astype(F32) + beta * product).astype(BF16)
     image_ref[...] = image
-    for send, asked_ref in zip(sends, asked):
-        row = asked_ref[2 * c["tick"] : 2 * c["tick"] + 1, :]
-        send[:tile, :] = chosen(image_ref, row, c["rows"], tile)
+    if not c["join"]:
+        for send, asked_ref in zip(sends, asked):
+            row = asked_ref[2 * c["tick"] : 2 * c["tick"] + 1, :]
+            send[:tile, :] = chosen(image_ref, row, c["rows"], tile)
     if c["final"]:
         term = lax.dot_general(
             support_ref[...], masked, (((0,), (0,)), ((), ())), preferred_element_type=F32
@@ -238,9 +239,11 @@
         term_ref[...] = acc_ref[...] + beta * term
         place = lax.rem(lax.axis_index("rows"), h)
         for k in range(1, h):
-            sends[k - 1][tile : tile + chunk, :] = tile_at(
-                term_ref, jnp.bitwise_xor(place, k), chunk
-            ).astype(BF16)
+            part = tile_at(term_ref, jnp.bitwise_xor(place, k), chunk).astype(BF16)
+            if c["join"]:
+                sends[k - 1][...] = part
+            else:
+                sends[k - 1][tile : tile + chunk, :] = part
         out_ref[...] = tile_at(term_ref, place, chunk)
     else:
         out_ref[...] = masked
@@ -250,20 +253,20 @@
     refs = Refs(refs)
     count, tile, rows = c["n"] // 2 - 1, c["tile"], c["rows"]
     far_ref = refs.take()
-    own_ref = refs.take() if c["first"] else None
+    own_ref = refs.take() if c["join"] else None
     for asked_ref, send in zip(refs.take(count), refs.take(count)):
         row = 2 * c["tick"]
-        if c["first"]:
+        if c["join"]:
             send[:tile, :] = chosen(own_ref, asked_ref[row : row + 1, :], rows, tile)
             send[tile:, :] = chosen(far_ref, asked_ref[row + 1 : row + 2, :], rows, tile)
         else:
             send[...] = chosen(far_ref, asked_ref[row + 1 : row + 2, :], rows, tile)
 
 
-def half_sum_kernel(tile, kept_ref, *refs):
+def half_sum_kernel(kept_ref, *refs):
     total = kept_ref[...]
     for ref in refs[:-1]:
-        total = total + ref[tile:, :].astype(F32)
+        total = total + ref[ref.shape[0] - total.shape[0] :, :].astype(F32)
     refs[-1][...] = total.astype(BF16)
 
 
@@ -354,6 +357,7 @@
                 base, layer=layer, tick=tick, entry=entry, final=final, joined=joined,
                 first=tick == 0 and entry,
             )
+            c["join"] = c["first"] or (final and layer == 0)
             if c["first"]:
                 masked = jnp.where(
                     preact[0, tick, layer] > 0, grad_in[0], jnp.zeros_like(grad_in[0])
@@ -371,7 +375,7 @@
                 if final:
                     call.give(HBM, support)
                     call.give(VMEM, weight_acc[layer])
-                message = tile + (chunk if final else 0)
+                message = (0 if c["join"] else tile) + (chunk if final else 0)
                 call.want(VMEM, (rows, width), BF16)
                 call.want(VMEM, (message, width), BF16, h - 1)
                 if final:
@@ -396,14 +400,16 @@
                 kept = masked = results.take()
             far = swapped(image, h)
             near = [] if c["first"] else shared(sends)
-            call = Call()
-            call.give(VMEM, far)
+            ready = image
             if c["first"]:
                 adjs[0] = densify(0, words, tile_vals, row_tiles, n)
                 ready, adjs[0] = lax.optimization_barrier((image, adjs[0]))
+            call = Call()
+            call.give(VMEM, far)
+            if c["join"]:
                 call.give(VMEM, ready)
             call.give(VMEM, *asked)
-            call.want(VMEM, (tile * (1 + c["first"]), width), BF16, h - 1)
+            call.want(VMEM, (tile * (1 + c["join"]), width), BF16, h - 1)
             relays = call.run(functools.partial(forward_kernel, c), "forward", small_cost)
             relayed = shared(relays)
             if layer == 0 and not final:
@@ -411,18 +417,21 @@
                 adjs[tick + 1] = densify(tick + 1, later, tile_vals, row_tiles, n)
                 relayed, adjs[tick + 1] = lax.optimization_barrier((relayed, adjs[tick + 1]))
             if final:
-                kept, *_ = lax.optimization_barrier((kept, *relays))
+                if layer > 0:
+                    kept, *_ = lax.optimization_barrier((kept, *relays))
                 call = Call()
                 call.give(VMEM, kept, *near)
                 call.want(VMEM, (chunk, width), BF16)
                 (mine,) = call.run(
-                    functools.partial(half_sum_kernel, tile), "half_sum", small_cost
+                    half_sum_kernel, "half_sum", small_cost
                 )
                 if layer > 0:
                     relayed, mine = lax.optimization_barrier((relayed, mine))
+                else:
+                    mine, _ = lax.optimization_barrier((mine, far))
                 weight_sums = [mine, swapped(mine, h), *weight_sums]
-            got = [far, *near, *relayed]
-            joined = c["first"]
+            got = [far, *relayed] if c["join"] else [far, *near, *relayed]
+            joined = c["join"]
             toward = toward + ALPHA * image.astype(F32)
             if not final:
                 term = beta * jnp.dot(

time: 87.2 us -> 89.7 us (1.029)
  starting transfers between devices: 43.4 us -> 45.8 us
  waiting for transfers between devices: 24.8 us -> 26.6 us
  Pallas kernels: 13.2 us -> 11.9 us
    ppermute x33, starting transfers between devices: 42.1 us -> 44.5 us  [swapped(): return lax.ppermute(block, 'rows', [(i, i ^ k) for i in range(n)])]
    ppermute x33, waiting for transfers between devices: 23.3 us -> 25.1 us  [swapped(): return lax.ppermute(block, 'rows', [(i, i ^ k) for i in range(n)])]
    pallas_call x16, Pallas kernels: 13.2 us -> 11.9 us  [run(): pl.pallas_call(kernel, out_shape=self.outs, in_specs=self.specs, out_spec...]
  transfers between devices with their start and end apart: 34 -> 34, of which waited for: 16 -> 16; matrix products, arithmetic and copies ran while one was open for 3% -> 3% of each run, Pallas kernels for 10% -> 8%
where the time goes in v11:
time: 89.7 us; the launch traced here: 89.8 us
  starting transfers between devices  45.8 us (51%)
  waiting for transfers between devices  26.6 us (30%)
  Pallas kernels  11.9 us (13%)
  other arithmetic  2.29 us (3%)
  matrix products  1.9 us (2%)
  between operations  1.13 us (1%)
    ppermute x33, starting transfers between devices, swapped(): return lax.ppermute(block, 'rows', [(i, i ^ k) for i in range(n)])  44.5 us
    ppermute x33, waiting for transfers between devices, swapped(): return lax.ppermute(block, 'rows', [(i, i ^ k) for i in range(n)])  25.1 us
    pallas_call x16, Pallas kernels, run(): pl.pallas_call(kernel, out_shape=self.outs, in_specs=self.specs, out_spec...  11.9 us
  transfers between devices with their start and end apart: 34, of which 16 were waited for; matrix products, arithmetic and copies ran while one was open for 3% of the time, Pallas kernels for 8%

profile of v11, /device:TPU:0, one launch (start us, length us, event | category | flops | bytes accessed | tf_op | source)
XLA Modules:
  0.0 89.8 jit_solution(14826131538821780193)
XLA Ops:
  2.2 4.1 %collective-permute-start.3 = (bf16[256,256]{1,0:T(8,128)(2,1)S(1)}, bf16[256,256]{1,0:T(8,128)(2,1)S(1)}, u32[]{:S(2)}, u32[]{:S(2)}) collective-permute-start(bf16[256,256]{1,0:T(8,128)(2,1)S(1)} %fusion.3.refs_1_.refs_7_), channel_id=1, source_target_pairs={{0,4},{1,5},{2,6},{3,7},{4,0},{5,1},{6,2},{7,3},{8,12},{9,13},{10,... | collective-permute-start | bytes 393224 | tf_op jit(solution)/shard_map/ppermute | solution.py:26
  7.8 1.6 %collective-permute-start = (f32[4,256]{1,0:T(4,128)S(1)}, f32[4,256]{1,0:T(4,128)S(1)}, u32[]{:S(2)}, u32[]{:S(2)}) collective-permute-start(f32[4,256]{1,0:T(4,128)S(1)} %get-tuple-element.48), channel_id=1, source_target_pairs={{0,1},{1,0},{2,3},{3,2},{4,5},{5,4},{6,7},{7,6},{8,9},{9,8},{10,11... | collective-permute-start | bytes 12296 | tf_op jit(solution)/shard_map/ppermute | solution.py:26
  9.3 1.6 %collective-permute-start.1 = (f32[4,256]{1,0:T(4,128)S(1)}, f32[4,256]{1,0:T(4,128)S(1)}, u32[]{:S(2)}, u32[]{:S(2)}) collective-permute-start(f32[4,256]{1,0:T(4,128)S(1)} %get-tuple-element.49), channel_id=1, source_target_pairs={{0,2},{1,3},{2,0},{3,1},{4,6},{5,7},{6,4},{7,5},{8,10},{9,11},{10,... | collective-permute-start | bytes 12296 | tf_op jit(solution)/shard_map/ppermute | solution.py:26
  11.3 3.2 %densify.2.refs_6_.refs_1_ = bf16[256,1152]{1,0:T(8,128)(2,1)S(1)} custom-call(s32[3,96]{1,0:T(4,128)S(1)} %pad_add_fusion.words_ref, bf16[1,2,96,128,128]{4,3,2,1,0:T(8,128)(2,1)} %vals_ref.3), custom_call_target="tpu_custom_call" | custom-call | flops 31457280 | bytes 3145728 | tf_op jit(solution)/shard_map/densify/pallas_call | solution.py:64
  17.4 1.7 %collective-permute-start.6 = (bf16[256,256]{1,0:T(8,128)(2,1)S(1)}, bf16[256,256]{1,0:T(8,128)(2,1)S(1)}, u32[]{:S(2)}, u32[]{:S(2)}) collective-permute-start(bf16[256,256]{1,0:T(8,128)(2,1)S(1)} %get-tuple-element.55), channel_id=1, source_target_pairs={{0,3},{1,2},{2,1},{3,0},{4,7},{5,6},{6,5},{7,4},{8,11},{9,10},{10,... | collective-permute-start | bytes 393224 | tf_op jit(solution)/shard_map/ppermute | solution.py:26
  19.0 2.7 %collective-permute-done.4.refs_9_ = bf16[256,256]{1,0:T(8,128)(2,1)S(1)} collective-permute-done((bf16[256,256]{1,0:T(8,128)(2,1)S(1)}, bf16[256,256]{1,0:T(8,128)(2,1)S(1)}, u32[]{:S(2)}, u32[]{:S(2)}) %collective-permute-start.4) | collective-permute-done | bytes 131104 | tf_op jit(solution)/shard_map/ppermute | solution.py:26
  21.9 2.3 %collective-permute-done.6.refs_11_ = bf16[256,256]{1,0:T(8,128)(2,1)S(1)} collective-permute-done((bf16[256,256]{1,0:T(8,128)(2,1)S(1)}, bf16[256,256]{1,0:T(8,128)(2,1)S(1)}, u32[]{:S(2)}, u32[]{:S(2)}) %collective-permute-start.6) | collective-permute-done | bytes 131104 | tf_op jit(solution)/shard_map/ppermute | solution.py:26
  27.1 1.7 %collective-permute-start.12 = (bf16[128,256]{1,0:T(8,128)(2,1)S(1)}, bf16[128,256]{1,0:T(8,128)(2,1)S(1)}, u32[]{:S(2)}, u32[]{:S(2)}) collective-permute-start(bf16[128,256]{1,0:T(8,128)(2,1)S(1)} %get-tuple-element.61), channel_id=1, source_target_pairs={{0,2},{1,3},{2,0},{3,1},{4,6},{5,7},{6,4},{7,5},{8,10},{9,11},{10,... | collective-permute-start | bytes 196616 | tf_op jit(solution)/shard_map/ppermute | solution.py:26
  29.7 2.9 %collective-permute-done.7.refs_0_.refs_3_ = bf16[256,256]{1,0:T(8,128)(2,1)S(1)} collective-permute-done((bf16[256,256]{1,0:T(8,128)(2,1)S(1)}, bf16[256,256]{1,0:T(8,128)(2,1)S(1)}, u32[]{:S(2)}, u32[]{:S(2)}) %collective-permute-start.7) | collective-permute-done | bytes 131104 | tf_op jit(solution)/shard_map/ppermute | solution.py:26
  33.9 2.3 %collective-permute-start.10 = (bf16[128,256]{1,0:T(8,128)(2,1)S(1)}, bf16[128,256]{1,0:T(8,128)(2,1)S(1)}, u32[]{:S(2)}, u32[]{:S(2)}) collective-permute-start(bf16[128,256]{1,0:T(8,128)(2,1)S(1)} %get-tuple-element.59), channel_id=1, source_target_pairs={{0,3},{1,2},{2,1},{3,0},{4,7},{5,6},{6,5},{7,4},{8,11},{9,10},{10,... | collective-permute-start | bytes 196616 | tf_op jit(solution)/shard_map/ppermute | solution.py:26
  36.2 3.0 %densify.3.refs_6_.refs_1_ = bf16[256,1152]{1,0:T(8,128)(2,1)S(1)} custom-call(s32[3,96]{1,0:T(4,128)S(1)} %pad_add_fusion.words_ref, bf16[1,2,96,128,128]{4,3,2,1,0:T(8,128)(2,1)} %vals_ref.3), custom_call_target="tpu_custom_call" | custom-call | flops 31457280 | bytes 3145728 | tf_op jit(solution)/shard_map/densify/pallas_call | solution.py:64
  43.6 2.8 %collective-permute-start.15 = (bf16[256,256]{1,0:T(8,128)(2,1)S(1)}, bf16[256,256]{1,0:T(8,128)(2,1)S(1)}, u32[]{:S(2)}, u32[]{:S(2)}) collective-permute-start(bf16[256,256]{1,0:T(8,128)(2,1)S(1)} %get-tuple-element.68.refs_7_), channel_id=1, source_target_pairs={{0,4},{1,5},{2,6},{3,7},{4,0},{5,1},{6,2},{7,3},{8,12},{9,13},{10,... | collective-permute-start | bytes 393224 | tf_op jit(solution)/shard_map/ppermute | solution.py:26
  47.2 1.7 %collective-permute-start.17 = (bf16[192,256]{1,0:T(8,128)(2,1)S(1)}, bf16[192,256]{1,0:T(8,128)(2,1)S(1)}, u32[]{:S(2)}, u32[]{:S(2)}) collective-permute-start(bf16[192,256]{1,0:T(8,128)(2,1)S(1)} %get-tuple-element.70), channel_id=1, source_target_pairs={{0,2},{1,3},{2,0},{3,1},{4,6},{5,7},{6,4},{7,5},{8,10},{9,11},{10,... | collective-permute-start | bytes 294920 | tf_op jit(solution)/shard_map/ppermute | solution.py:26
  50.1 1.8 %collective-permute-done.15.refs_0_.refs_8_ = bf16[256,256]{1,0:T(8,128)(2,1)S(1)} collective-permute-done((bf16[256,256]{1,0:T(8,128)(2,1)S(1)}, bf16[256,256]{1,0:T(8,128)(2,1)S(1)}, u32[]{:S(2)}, u32[]{:S(2)}) %collective-permute-start.15) | collective-permute-done | bytes 131104 | tf_op jit(solution)/shard_map/ppermute | solution.py:26
  52.1 3.2 %collective-permute-start.20 = (bf16[128,256]{1,0:T(8,128)(2,1)S(1)}, bf16[128,256]{1,0:T(8,128)(2,1)S(1)}, u32[]{:S(2)}, u32[]{:S(2)}) collective-permute-start(bf16[128,256]{1,0:T(8,128)(2,1)S(1)} %get-tuple-element.73), channel_id=1, source_target_pairs={{0,2},{1,3},{2,0},{3,1},{4,6},{5,7},{6,4},{7,5},{8,10},{9,11},{10,... | collective-permute-start | bytes 196616 | tf_op jit(solution)/shard_map/ppermute | solution.py:26
  56.7 1.6 %collective-permute-done.19.refs_12_ = bf16[128,256]{1,0:T(8,128)(2,1)S(1)} collective-permute-done((bf16[128,256]{1,0:T(8,128)(2,1)S(1)}, bf16[128,256]{1,0:T(8,128)(2,1)S(1)}, u32[]{:S(2)}, u32[]{:S(2)}) %collective-permute-start.19) | collective-permute-done | bytes 65568 | tf_op jit(solution)/shard_map/ppermute | solution.py:26
  58.3 2.2 %collective-permute-done.21.refs_14_ = bf16[128,256]{1,0:T(8,128)(2,1)S(1)} collective-permute-done((bf16[128,256]{1,0:T(8,128)(2,1)S(1)}, bf16[128,256]{1,0:T(8,128)(2,1)S(1)}, u32[]{:S(2)}, u32[]{:S(2)}) %collective-permute-start.21) | collective-permute-done | bytes 65568 | tf_op jit(solution)/shard_map/ppermute | solution.py:26
  61.8 3.4 %collective-permute-start.22 = (bf16[256,256]{1,0:T(8,128)(2,1)S(1)}, bf16[256,256]{1,0:T(8,128)(2,1)S(1)}, u32[]{:S(2)}, u32[]{:S(2)}) collective-permute-start(bf16[256,256]{1,0:T(8,128)(2,1)S(1)} %get-tuple-element.81.refs_1_.refs_2_), channel_id=1, source_target_pairs={{0,4},{1,5},{2,6},{3,7},{4,0},{5,1},{6,2},{7,3},{8,12},{9,13},{10,... | collective-permute-start | bytes 393224 | tf_op jit(solution)/shard_map/ppermute | solution.py:26
  66.8 1.9 %collective-permute-start.28 = (bf16[64,256]{1,0:T(8,128)(2,1)S(1)}, bf16[64,256]{1,0:T(8,128)(2,1)S(1)}, u32[]{:S(2)}, u32[]{:S(2)}) collective-permute-start(bf16[64,256]{1,0:T(8,128)(2,1)S(1)} %get-tuple-element.88), channel_id=1, source_target_pairs={{0,3},{1,2},{2,1},{3,0},{4,7},{5,6},{6,5},{7,4},{8,11},{9,10},{10,... | collective-permute-start | bytes 98312 | tf_op jit(solution)/shard_map/ppermute | solution.py:26
  73.0 2.9 %collective-permute-start.24 = (bf16[256,256]{1,0:T(8,128)(2,1)S(1)}, bf16[256,256]{1,0:T(8,128)(2,1)S(1)}, u32[]{:S(2)}, u32[]{:S(2)}) collective-permute-start(bf16[256,256]{1,0:T(8,128)(2,1)S(1)} %get-tuple-element.83), channel_id=1, source_target_pairs={{0,2},{1,3},{2,0},{3,1},{4,6},{5,7},{6,4},{7,5},{8,10},{9,11},{10,... | collective-permute-start | bytes 393224 | tf_op jit(solution)/shard_map/ppermute | solution.py:26
  77.8 1.8 %collective-permute-start.32 = (bf16[2,64,256]{2,1,0:T(8,128)(2,1)S(1)}, bf16[2,64,256]{2,1,0:T(8,128)(2,1)S(1)}, u32[]{:S(2)}, u32[]{:S(2)}) collective-permute-start(bf16[2,64,256]{2,1,0:T(8,128)(2,1)S(1)} %total.1.refs_0_), channel_id=1, source_target_pairs={{0,2},{1,3},{2,0},{3,1},{4,6},{5,7},{6,4},{7,5},{8,10},{9,11},{10,... | collective-permute-start | bytes 196616 | tf_op jit(solution)/shard_map/ppermute | solution.py:26
  79.6 3.1 %collective-permute-done.31.refs_1_ = bf16[2,64,256]{2,1,0:T(8,128)(2,1)S(1)} collective-permute-done((bf16[2,64,256]{2,1,0:T(8,128)(2,1)S(1)}, bf16[2,64,256]{2,1,0:T(8,128)(2,1)S(1)}, u32[]{:S(2)}, u32[]{:S(2)}) %collective-permute-start.31) | collective-permute-done | bytes 65568 | tf_op jit(solution)/shard_map/ppermute | solution.py:26
  82.7 1.8 %collective-permute-start.33 = (bf16[2,64,256]{2,1,0:T(8,128)(2,1)S(1)}, bf16[2,64,256]{2,1,0:T(8,128)(2,1)S(1)}, u32[]{:S(2)}, u32[]{:S(2)}) collective-permute-start(bf16[2,64,256]{2,1,0:T(8,128)(2,1)S(1)} %total.1.refs_0_), channel_id=1, source_target_pairs={{0,3},{1,2},{2,1},{3,0},{4,7},{5,6},{6,5},{7,4},{8,11},{9,10},{10,... | collective-permute-start | bytes 196616 | tf_op jit(solution)/shard_map/ppermute | solution.py:26
  85.3 2.5 %collective-permute-done.33.refs_3_ = bf16[2,64,256]{2,1,0:T(8,128)(2,1)S(1)} collective-permute-done((bf16[2,64,256]{2,1,0:T(8,128)(2,1)S(1)}, bf16[2,64,256]{2,1,0:T(8,128)(2,1)S(1)}, u32[]{:S(2)}, u32[]{:S(2)}) %collective-permute-start.33) | collective-permute-done | bytes 65568 | tf_op jit(solution)/shard_map/ppermute | solution.py:26
  (79 shorter events, 30.9 us)
Async XLA Ops:
  2.2 13.2 %collective-permute-start.3 = (bf16[256,256]{1,0:T(8,128)(2,1)S(1)}, bf16[256,256]{1,0:T(8,128)(2,1)S(1)}, u32[]{:S(2)}, u32[]{:S(2)}) collective-permute-start(bf16[256,256]{1,0:T(8,128)(2,1)S(1)} %fusion.3.refs_1_.refs_7_), channel_id=1, source_target_pairs={{0,4},{1,5},{2,6},{3,7},{4,0},{5,1},{6,2},{7,3},{8,12},{9,13},{10,... | collective-permute-start | bytes 393224 | tf_op jit(solution)/shard_map/ppermute | solution.py:26
  7.8 6.8 %collective-permute-start = (f32[4,256]{1,0:T(4,128)S(1)}, f32[4,256]{1,0:T(4,128)S(1)}, u32[]{:S(2)}, u32[]{:S(2)}) collective-permute-start(f32[4,256]{1,0:T(4,128)S(1)} %get-tuple-element.48), channel_id=1, source_target_pairs={{0,1},{1,0},{2,3},{3,2},{4,5},{5,4},{6,7},{7,6},{8,9},{9,8},{10,11... | collective-permute-start | bytes 12296 | tf_op jit(solution)/shard_map/ppermute | solution.py:26
  15.5 6.2 %collective-permute-start.4 = (bf16[256,256]{1,0:T(8,128)(2,1)S(1)}, bf16[256,256]{1,0:T(8,128)(2,1)S(1)}, u32[]{:S(2)}, u32[]{:S(2)}) collective-permute-start(bf16[256,256]{1,0:T(8,128)(2,1)S(1)} %get-tuple-element.53), channel_id=1, source_target_pairs={{0,1},{1,0},{2,3},{3,2},{4,5},{5,4},{6,7},{7,6},{8,9},{9,8},{10,11... | collective-permute-start | bytes 393224 | tf_op jit(solution)/shard_map/ppermute | solution.py:26
  16.3 5.5 %collective-permute-start.5 = (bf16[256,256]{1,0:T(8,128)(2,1)S(1)}, bf16[256,256]{1,0:T(8,128)(2,1)S(1)}, u32[]{:S(2)}, u32[]{:S(2)}) collective-permute-start(bf16[256,256]{1,0:T(8,128)(2,1)S(1)} %get-tuple-element.54), channel_id=1, source_target_pairs={{0,2},{1,3},{2,0},{3,1},{4,6},{5,7},{6,4},{7,5},{8,10},{9,11},{10,... | collective-permute-start | bytes 393224 | tf_op jit(solution)/shard_map/ppermute | solution.py:26
  17.4 6.8 %collective-permute-start.6 = (bf16[256,256]{1,0:T(8,128)(2,1)S(1)}, bf16[256,256]{1,0:T(8,128)(2,1)S(1)}, u32[]{:S(2)}, u32[]{:S(2)}) collective-permute-start(bf16[256,256]{1,0:T(8,128)(2,1)S(1)} %get-tuple-element.55), channel_id=1, source_target_pairs={{0,3},{1,2},{2,1},{3,0},{4,7},{5,6},{6,5},{7,4},{8,11},{9,10},{10,... | collective-permute-start | bytes 393224 | tf_op jit(solution)/shard_map/ppermute | solution.py:26
  25.2 7.4 %collective-permute-start.7 = (bf16[256,256]{1,0:T(8,128)(2,1)S(1)}, bf16[256,256]{1,0:T(8,128)(2,1)S(1)}, u32[]{:S(2)}, u32[]{:S(2)}) collective-permute-start(bf16[256,256]{1,0:T(8,128)(2,1)S(1)} %get-tuple-element.56.refs_2_), channel_id=1, source_target_pairs={{0,4},{1,5},{2,6},{3,7},{4,0},{5,1},{6,2},{7,3},{8,12},{9,13},{10,... | collective-permute-start | bytes 393224 | tf_op jit(solution)/shard_map/ppermute | solution.py:26
  26.2 7.7 %collective-permute-start.11 = (bf16[128,256]{1,0:T(8,128)(2,1)S(1)}, bf16[128,256]{1,0:T(8,128)(2,1)S(1)}, u32[]{:S(2)}, u32[]{:S(2)}) collective-permute-start(bf16[128,256]{1,0:T(8,128)(2,1)S(1)} %get-tuple-element.60), channel_id=1, source_target_pairs={{0,1},{1,0},{2,3},{3,2},{4,5},{5,4},{6,7},{7,6},{8,9},{9,8},{10,11... | collective-permute-start | bytes 196616 | tf_op jit(solution)/shard_map/ppermute | solution.py:26
  27.1 9.1 %collective-permute-start.12 = (bf16[128,256]{1,0:T(8,128)(2,1)S(1)}, bf16[128,256]{1,0:T(8,128)(2,1)S(1)}, u32[]{:S(2)}, u32[]{:S(2)}) collective-permute-start(bf16[128,256]{1,0:T(8,128)(2,1)S(1)} %get-tuple-element.61), channel_id=1, source_target_pairs={{0,2},{1,3},{2,0},{3,1},{4,6},{5,7},{6,4},{7,5},{8,10},{9,11},{10,... | collective-permute-start | bytes 196616 | tf_op jit(solution)/shard_map/ppermute | solution.py:26
  28.8 7.4 %collective-permute-start.13 = (bf16[128,256]{1,0:T(8,128)(2,1)S(1)}, bf16[128,256]{1,0:T(8,128)(2,1)S(1)}, u32[]{:S(2)}, u32[]{:S(2)}) collective-permute-start(bf16[128,256]{1,0:T(8,128)(2,1)S(1)} %get-tuple-element.62), channel_id=1, source_target_pairs={{0,3},{1,2},{2,1},{3,0},{4,7},{5,6},{6,5},{7,4},{8,11},{9,10},{10,... | collective-permute-start | bytes 196616 | tf_op jit(solution)/shard_map/ppermute | solution.py:26
  32.6 6.5 %collective-permute-start.8 = (bf16[128,256]{1,0:T(8,128)(2,1)S(1)}, bf16[128,256]{1,0:T(8,128)(2,1)S(1)}, u32[]{:S(2)}, u32[]{:S(2)}) collective-permute-start(bf16[128,256]{1,0:T(8,128)(2,1)S(1)} %get-tuple-element.57), channel_id=1, source_target_pairs={{0,1},{1,0},{2,3},{3,2},{4,5},{5,4},{6,7},{7,6},{8,9},{9,8},{10,11... | collective-permute-start | bytes 196616 | tf_op jit(solution)/shard_map/ppermute | solution.py:26
  32.7 6.5 %collective-permute-start.9 = (bf16[128,256]{1,0:T(8,128)(2,1)S(1)}, bf16[128,256]{1,0:T(8,128)(2,1)S(1)}, u32[]{:S(2)}, u32[]{:S(2)}) collective-permute-start(bf16[128,256]{1,0:T(8,128)(2,1)S(1)} %get-tuple-element.58), channel_id=1, source_target_pairs={{0,2},{1,3},{2,0},{3,1},{4,6},{5,7},{6,4},{7,5},{8,10},{9,11},{10,... | collective-permute-start | bytes 196616 | tf_op jit(solution)/shard_map/ppermute | solution.py:26
  43.6 8.3 %collective-permute-start.15 = (bf16[256,256]{1,0:T(8,128)(2,1)S(1)}, bf16[256,256]{1,0:T(8,128)(2,1)S(1)}, u32[]{:S(2)}, u32[]{:S(2)}) collective-permute-start(bf16[256,256]{1,0:T(8,128)(2,1)S(1)} %get-tuple-element.68.refs_7_), channel_id=1, source_target_pairs={{0,4},{1,5},{2,6},{3,7},{4,0},{5,1},{6,2},{7,3},{8,12},{9,13},{10,... | collective-permute-start | bytes 393224 | tf_op jit(solution)/shard_map/ppermute | solution.py:26
  46.5 8.8 %collective-permute-start.16 = (bf16[192,256]{1,0:T(8,128)(2,1)S(1)}, bf16[192,256]{1,0:T(8,128)(2,1)S(1)}, u32[]{:S(2)}, u32[]{:S(2)}) collective-permute-start(bf16[192,256]{1,0:T(8,128)(2,1)S(1)} %get-tuple-element.69), channel_id=1, source_target_pairs={{0,1},{1,0},{2,3},{3,2},{4,5},{5,4},{6,7},{7,6},{8,9},{9,8},{10,11... | collective-permute-start | bytes 294920 | tf_op jit(solution)/shard_map/ppermute | solution.py:26
  47.2 8.6 %collective-permute-start.17 = (bf16[192,256]{1,0:T(8,128)(2,1)S(1)}, bf16[192,256]{1,0:T(8,128)(2,1)S(1)}, u32[]{:S(2)}, u32[]{:S(2)}) collective-permute-start(bf16[192,256]{1,0:T(8,128)(2,1)S(1)} %get-tuple-element.70), channel_id=1, source_target_pairs={{0,2},{1,3},{2,0},{3,1},{4,6},{5,7},{6,4},{7,5},{8,10},{9,11},{10,... | collective-permute-start | bytes 294920 | tf_op jit(solution)/shard_map/ppermute | solution.py:26
  48.9 7.7 %collective-permute-start.18 = (bf16[192,256]{1,0:T(8,128)(2,1)S(1)}, bf16[192,256]{1,0:T(8,128)(2,1)S(1)}, u32[]{:S(2)}, u32[]{:S(2)}) collective-permute-start(bf16[192,256]{1,0:T(8,128)(2,1)S(1)} %get-tuple-element.71), channel_id=1, source_target_pairs={{0,3},{1,2},{2,1},{3,0},{4,7},{5,6},{6,5},{7,4},{8,11},{9,10},{10,... | collective-permute-start | bytes 294920 | tf_op jit(solution)/shard_map/ppermute | solution.py:26
  52.0 6.3 %collective-permute-start.19 = (bf16[128,256]{1,0:T(8,128)(2,1)S(1)}, bf16[128,256]{1,0:T(8,128)(2,1)S(1)}, u32[]{:S(2)}, u32[]{:S(2)}) collective-permute-start(bf16[128,256]{1,0:T(8,128)(2,1)S(1)} %get-tuple-element.72), channel_id=1, source_target_pairs={{0,1},{1,0},{2,3},{3,2},{4,5},{5,4},{6,7},{7,6},{8,9},{9,8},{10,11... | collective-permute-start | bytes 196616 | tf_op jit(solution)/shard_map/ppermute | solution.py:26
  52.1 6.2 %collective-permute-start.20 = (bf16[128,256]{1,0:T(8,128)(2,1)S(1)}, bf16[128,256]{1,0:T(8,128)(2,1)S(1)}, u32[]{:S(2)}, u32[]{:S(2)}) collective-permute-start(bf16[128,256]{1,0:T(8,128)(2,1)S(1)} %get-tuple-element.73), channel_id=1, source_target_pairs={{0,2},{1,3},{2,0},{3,1},{4,6},{5,7},{6,4},{7,5},{8,10},{9,11},{10,... | collective-permute-start | bytes 196616 | tf_op jit(solution)/shard_map/ppermute | solution.py:26
  61.8 10.2 %collective-permute-start.22 = (bf16[256,256]{1,0:T(8,128)(2,1)S(1)}, bf16[256,256]{1,0:T(8,128)(2,1)S(1)}, u32[]{:S(2)}, u32[]{:S(2)}) collective-permute-start(bf16[256,256]{1,0:T(8,128)(2,1)S(1)} %get-tuple-element.81.refs_1_.refs_2_), channel_id=1, source_target_pairs={{0,4},{1,5},{2,6},{3,7},{4,0},{5,1},{6,2},{7,3},{8,12},{9,13},{10,... | collective-permute-start | bytes 393224 | tf_op jit(solution)/shard_map/ppermute | solution.py:26
  68.7 7.4 %collective-permute-start.30 = (bf16[64,256]{1,0:T(8,128)(2,1)S(1)}, bf16[64,256]{1,0:T(8,128)(2,1)S(1)}, u32[]{:S(2)}, u32[]{:S(2)}) collective-permute-start(bf16[64,256]{1,0:T(8,128)(2,1)S(1)} %half_sum.2.refs_2_), channel_id=1, source_target_pairs={{0,4},{1,5},{2,6},{3,7},{4,0},{5,1},{6,2},{7,3},{8,12},{9,13},{10,... | collective-permute-start | bytes 98312 | tf_op jit(solution)/shard_map/ppermute | solution.py:26
  72.2 16.5 %collective-permute-start.23 = (bf16[256,256]{1,0:T(8,128)(2,1)S(1)}, bf16[256,256]{1,0:T(8,128)(2,1)S(1)}, u32[]{:S(2)}, u32[]{:S(2)}) collective-permute-start(bf16[256,256]{1,0:T(8,128)(2,1)S(1)} %get-tuple-element.82), channel_id=1, source_target_pairs={{0,1},{1,0},{2,3},{3,2},{4,5},{5,4},{6,7},{7,6},{8,9},{9,8},{10,11... | collective-permute-start | bytes 393224 | tf_op jit(solution)/shard_map/ppermute | solution.py:26
  73.0 15.8 %collective-permute-start.24 = (bf16[256,256]{1,0:T(8,128)(2,1)S(1)}, bf16[256,256]{1,0:T(8,128)(2,1)S(1)}, u32[]{:S(2)}, u32[]{:S(2)}) collective-permute-start(bf16[256,256]{1,0:T(8,128)(2,1)S(1)} %get-tuple-element.83), channel_id=1, source_target_pairs={{0,2},{1,3},{2,0},{3,1},{4,6},{5,7},{6,4},{7,5},{8,10},{9,11},{10,... | collective-permute-start | bytes 393224 | tf_op jit(solution)/shard_map/ppermute | solution.py:26
  75.9 12.8 %collective-permute-start.25 = (bf16[256,256]{1,0:T(8,128)(2,1)S(1)}, bf16[256,256]{1,0:T(8,128)(2,1)S(1)}, u32[]{:S(2)}, u32[]{:S(2)}) collective-permute-start(bf16[256,256]{1,0:T(8,128)(2,1)S(1)} %get-tuple-element.84), channel_id=1, source_target_pairs={{0,3},{1,2},{2,1},{3,0},{4,7},{5,6},{6,5},{7,4},{8,11},{9,10},{10,... | collective-permute-start | bytes 393224 | tf_op jit(solution)/shard_map/ppermute | solution.py:26
  77.1 5.6 %collective-permute-start.31 = (bf16[2,64,256]{2,1,0:T(8,128)(2,1)S(1)}, bf16[2,64,256]{2,1,0:T(8,128)(2,1)S(1)}, u32[]{:S(2)}, u32[]{:S(2)}) collective-permute-start(bf16[2,64,256]{2,1,0:T(8,128)(2,1)S(1)} %total.1.refs_0_), channel_id=1, source_target_pairs={{0,1},{1,0},{2,3},{3,2},{4,5},{5,4},{6,7},{7,6},{8,9},{9,8},{10,11... | collective-permute-start | bytes 196616 | tf_op jit(solution)/shard_map/ppermute | solution.py:26
  77.8 7.5 %collective-permute-start.32 = (bf16[2,64,256]{2,1,0:T(8,128)(2,1)S(1)}, bf16[2,64,256]{2,1,0:T(8,128)(2,1)S(1)}, u32[]{:S(2)}, u32[]{:S(2)}) collective-permute-start(bf16[2,64,256]{2,1,0:T(8,128)(2,1)S(1)} %total.1.refs_0_), channel_id=1, source_target_pairs={{0,2},{1,3},{2,0},{3,1},{4,6},{5,7},{6,4},{7,5},{8,10},{9,11},{10,... | collective-permute-start | bytes 196616 | tf_op jit(solution)/shard_map/ppermute | solution.py:26
  (15 other events, 175.8 us)

commit v12 on v11

--- a/solution.py
+++ b/solution.py
@@ -26,15 +26,22 @@
     return lax.ppermute(block, "rows", [(i, i ^ k) for i in range(n)])
 
 
-def shared(blocks):
-    moved = {k: swapped(block, k) for k, block in reversed(list(enumerate(blocks, 1)))}
+def lowered(block, k):
+    n, sections = lax.axis_size("rows"), lax.axis_size("section")
+    route = [
+        (s * n + i, (s - 1) % sections * n + (i ^ k)) for s in range(sections) for i in range(n)
+    ]
+    return lax.ppermute(block, ("section", "rows"), route)
+
+
+def raised(block):
+    sections = lax.axis_size("section")
+    return lax.ppermute(block, "section", [(s, (s + 1) % sections) for s in range(sections)])
+
+
+def shared(blocks, move=swapped):
+    moved = {k: move(block, k) for k, block in reversed(list(enumerate(blocks, 1)))}
     return [moved[k] for k in sorted(moved)]
-
-
-def passed_along(block, axis, distance):
-    devices = range(lax.axis_size(axis))
-    route = [(i - distance, i) for i in devices if i - distance in devices]
-    return lax.ppermute(block, axis, route)
 
 
 class Refs:
@@ -156,6 +163,25 @@
         out_refs[0][t : t + 1, :] = named(n // 2)
 
 
+def pack_kernel(tick, layer, preact_all, weight_all, *refs):
+    asked, (out_ref, sems) = refs[:-2], refs[-2:]
+    rows, width = preact_all.shape[-2:]
+    loads = [
+        pltpu.make_async_copy(preact_all.at[0, tick, layer], out_ref.at[:rows], sems.at[0]),
+        pltpu.make_async_copy(
+            weight_all.at[0, layer], out_ref.at[rows : rows + width], sems.at[1]
+        ),
+    ]
+    for load in loads:
+        load.start()
+    used = sum(ref.shape[0] for ref in asked)
+    rest = out_ref.shape[0] - rows - width - used
+    parts = [ref[...] for ref in asked] + ([jnp.zeros((rest, width), F32)] if rest else [])
+    out_ref[rows + width :, :] = jnp.concatenate(parts, axis=0).astype(BF16)
+    for load in loads:
+        load.wait()
+
+
 def chosen(image_ref, row, rows, tile):
     index = jnp.broadcast_to(row.astype(BF16), (tile, row.shape[1]))
     result = image_ref[:tile, :]
@@ -176,12 +202,23 @@
     far, near, relayed = got
     far = chosen(far, names_ref[c["tick"] : c["tick"] + 1, :], rows, tile)
     near = [ref[:tile, :] for ref in near]
-    relayed = [ref[...] for ref in relayed]
+    relayed = [ref[:tile, :] for ref in relayed]
     blocks = jnp.concatenate(
         [own_ref[:tile, :]] + near + [far] + relayed + [own_ref[tile:, :]], axis=0
     )
     total = jnp.dot(adj_ref[...], blocks, preferred_element_type=F32)
     return ((1.0 - ALPHA) * total).astype(BF16)
+
+
+def image_of(c, section, layer, grad, preact, weight):
+    step = (c["layers"] * section + layer + 1).astype(F32)
+    beta = jnp.log(BETA_SCALE / jnp.full((1, c["width"]), step, F32) + 1.0)
+    masked = jnp.where(preact > 0, grad, jnp.zeros_like(grad))
+    product = lax.dot_general(
+        masked, weight, (((1,), (1,)), ((), ())), preferred_element_type=F32
+    )
+    image = ((1.0 - beta) * masked.astype(F32) + beta * product).astype(BF16)
+    return beta, masked, image
 
 
 def layer_kernel(c, *refs):
@@ -198,7 +235,7 @@
     if c["final"]:
         support_all, acc_ref = refs.take(2)
     image_ref = refs.take()
-    sends = refs.take(h - 1)
+    sends = refs.take(h - 1) if c["final"] or not c["entry"] else []
     out_ref = refs.take()
     preact_ref, weight_ref, load_sems = refs.take(3)
 
@@ -213,8 +250,6 @@
     loads = [pltpu.make_async_copy(a, b, load_sems.at[i]) for i, (a, b) in enumerate(loads)]
     for load in loads:
         load.start()
-    step = (c["layers"] * section + c["layer"] + 1).astype(F32)
-    beta = jnp.log(BETA_SCALE / jnp.full((1, width), step, F32) + 1.0)
     if not c["entry"]:
         grad = spread_of(adj_ref, own_ref, got, names_ref, c)
     for load in loads:
@@ -222,13 +257,11 @@
     if c["entry"]:
         grad = jnp.where(section == c["sections"] - 1, last_ref[...], passed_ref[...])
 
-    masked = jnp.where(preact_ref[...] > 0, grad, jnp.zeros_like(grad))
-    product = lax.dot_general(
-        masked, weight_ref[...], (((1,), (1,)), ((), ())), preferred_element_type=F32
-    )
-    image = ((1.0 - beta) * masked.astype(F32) + beta * product).astype(BF16)
+    beta, masked, image = image_of(
+        c, section, c["layer"], grad, preact_ref[...], weight_ref[...]
+    )
     image_ref[...] = image
-    if not c["join"]:
+    if not c["entry"]:
         for send, asked_ref in zip(sends, asked):
             row = asked_ref[2 * c["tick"] : 2 * c["tick"] + 1, :]
             send[:tile, :] = chosen(image_ref, row, c["rows"], tile)
@@ -240,7 +273,7 @@
         place = lax.rem(lax.axis_index("rows"), h)
         for k in range(1, h):
             part = tile_at(term_ref, jnp.bitwise_xor(place, k), chunk).astype(BF16)
-            if c["join"]:
+            if c["entry"]:
                 sends[k - 1][...] = part
             else:
                 sends[k - 1][tile : tile + chunk, :] = part
@@ -253,10 +286,11 @@
     refs = Refs(refs)
     count, tile, rows = c["n"] // 2 - 1, c["tile"], c["rows"]
     far_ref = refs.take()
-    own_ref = refs.take() if c["join"] else None
-    for asked_ref, send in zip(refs.take(count), refs.take(count)):
+    own_ref = refs.take() if c["first"] else None
+    asked = refs.take(count)
+    for asked_ref, send in zip(asked, refs.take(count)):
         row = 2 * c["tick"]
-        if c["join"]:
+        if c["first"]:
             send[:tile, :] = chosen(own_ref, asked_ref[row : row + 1, :], rows, tile)
             send[tile:, :] = chosen(far_ref, asked_ref[row + 1 : row + 2, :], rows, tile)
         else:
@@ -277,13 +311,33 @@
         refs[-1][layer] = total.astype(BF16)
 
 
+def turn_kernel(c, *refs):
+    refs = Refs(refs)
+    names_ref, adj_ref, own_ref = refs.take(3)
+    got = take_got(refs, c)
+    below_ref, last_ref = refs.take(2)
+    grad_ref, image_ref = refs.take(2)
+    sends = refs.take(c["n"] // 2 - 1)
+    tile, rows, width = c["tile"], c["rows"], c["width"]
+    grad = spread_of(adj_ref, own_ref, got, names_ref, c)
+    grad_ref[...] = grad
+    section = lax.axis_index("section")
+    grad = jnp.where(section == 0, last_ref[...], grad)
+    below = jnp.where(section == 0, c["sections"], section) - 1
+    _, _, image = image_of(
+        c, below, c["layers"] - 1, grad, below_ref[:rows, :], below_ref[rows : rows + width, :]
+    )
+    image_ref[...] = image
+    asked = below_ref[rows + width :, :].astype(F32)
+    for k, send in enumerate(sends):
+        row = 2 * (k * c["ticks"] + c["tick"] + 1)
+        send[...] = chosen(image_ref, asked[row : row + 1, :], rows, tile)
+
+
 def exit_kernel(c, *refs):
     refs = Refs(refs)
     names_ref, adj_ref, own_ref = refs.take(3)
     got = take_got(refs, c)
-    if not c["final"]:
-        refs.take()[...] = spread_of(adj_ref, own_ref, got, names_ref, c)
-        return
     handed = refs.take(c["tick"])
     out_ref, hold_ref, sems = refs.take(3)
     copies = [
@@ -328,11 +382,14 @@
     words = packed(tile_row, tile_col, tile_count, row_tiles)
 
     handed = []
-    passed = None
+    turned = None
     weight_acc = [None] * layers
     weight_sums = []
     initial = []
-    base = dict(n=n, tile=tile, rows=rows, width=width, layers=layers, sections=sections, chunk=chunk)
+    base = dict(
+        n=n, tile=tile, rows=rows, width=width, layers=layers, sections=sections, chunk=chunk,
+        ticks=ticks,
+    )
     layer_cost = cost(2 * rows * width * (width + (n + 1) * tile), (6 + 2 * n) * rows * width)
     small_cost = cost(rows * width, 2 * n * rows * width)
     relay_cost = cost(rows * width, 8 * n * rows * width)
@@ -347,7 +404,7 @@
     for tick in range(ticks):
         final = tick == ticks - 1
         if tick > 0:
-            passed = passed_along(handed[-1], "section", -1)
+            passed = lowered(handed[-1], 0)
         image = got = joined = None
         toward = 0.0
         for layer in reversed(range(layers)):
@@ -357,7 +414,6 @@
                 base, layer=layer, tick=tick, entry=entry, final=final, joined=joined,
                 first=tick == 0 and entry,
             )
-            c["join"] = c["first"] or (final and layer == 0)
             if c["first"]:
                 masked = jnp.where(
                     preact[0, tick, layer] > 0, grad_in[0], jnp.zeros_like(grad_in[0])
@@ -375,9 +431,10 @@
                 if final:
                     call.give(HBM, support)
                     call.give(VMEM, weight_acc[layer])
-                message = (0 if c["join"] else tile) + (chunk if final else 0)
+                message = (0 if entry else tile) + (chunk if final else 0)
                 call.want(VMEM, (rows, width), BF16)
-                call.want(VMEM, (message, width), BF16, h - 1)
+                if message:
+                    call.want(VMEM, (message, width), BF16, h - 1)
                 if final:
                     call.want(VMEM, (chunk, width), F32)
                 else:
@@ -392,24 +449,35 @@
                     call.scratch.append(pltpu.VMEM((width, width), F32))
                 results = Refs(
                     call.run(
-                        functools.partial(layer_kernel, c), "entry" if entry else "middle", layer_cost
+                        functools.partial(layer_kernel, c),
+                        "home" if entry else "middle",
+                        layer_cost,
                     )
                 )
                 image = results.take()
-                sends = results.take(h - 1)
+                sends = results.take(h - 1) if message else []
                 kept = masked = results.take()
-            far = swapped(image, h)
-            near = [] if c["first"] else shared(sends)
+            parts = near = []
+            if turned is not None:
+                far = lowered(turned[0], h)
+                near = shared(turned[1:], lowered)
+                far, *near = lax.optimization_barrier((far, *near))
+                turned = None
+                if final:
+                    parts = shared(sends)
+            else:
+                far = swapped(image, h)
+                near = parts = [] if c["first"] else shared(sends)
             ready = image
             if c["first"]:
                 adjs[0] = densify(0, words, tile_vals, row_tiles, n)
                 ready, adjs[0] = lax.optimization_barrier((image, adjs[0]))
             call = Call()
             call.give(VMEM, far)
-            if c["join"]:
+            if c["first"]:
                 call.give(VMEM, ready)
             call.give(VMEM, *asked)
-            call.want(VMEM, (tile * (1 + c["join"]), width), BF16, h - 1)
+            call.want(VMEM, (tile * (1 + c["first"]), width), BF16, h - 1)
             relays = call.run(functools.partial(forward_kernel, c), "forward", small_cost)
             relayed = shared(relays)
             if layer == 0 and not final:
@@ -417,21 +485,19 @@
                 adjs[tick + 1] = densify(tick + 1, later, tile_vals, row_tiles, n)
                 relayed, adjs[tick + 1] = lax.optimization_barrier((relayed, adjs[tick + 1]))
             if final:
-                if layer > 0:
+                if not entry:
                     kept, *_ = lax.optimization_barrier((kept, *relays))
                 call = Call()
-                call.give(VMEM, kept, *near)
+                call.give(VMEM, kept, *parts)
                 call.want(VMEM, (chunk, width), BF16)
                 (mine,) = call.run(
                     half_sum_kernel, "half_sum", small_cost
                 )
                 if layer > 0:
                     relayed, mine = lax.optimization_barrier((relayed, mine))
-                else:
-                    mine, _ = lax.optimization_barrier((mine, far))
                 weight_sums = [mine, swapped(mine, h), *weight_sums]
-            got = [far, *relayed] if c["join"] else [far, *near, *relayed]
-            joined = c["join"]
+            got = [far, *near, *relayed]
+            joined = c["first"]
             toward = toward + ALPHA * image.astype(F32)
             if not final:
                 term = beta * jnp.dot(
@@ -443,14 +509,26 @@
         c = dict(base, tick=tick, final=final, joined=joined)
         call = Call()
         call.give(VMEM, names, adjs[tick], image, *got)
-        if final:
-            call.give(VMEM, *handed)
-            call.want(HBM, (ticks, 1, rows, width), BF16)
-            call.scratch = [pltpu.VMEM((rows, width), BF16), pltpu.SemaphoreType.DMA((ticks,))]
-        else:
-            call.want(VMEM, (rows, width), BF16)
-        results = call.run(functools.partial(exit_kernel, c), "exit", layer_cost)
-        handed.append(results[0])
+        if not final:
+            up = Call()
+            up.give(HBM, preact, weights)
+            up.give(VMEM, *asked)
+            length = rows + width + -(-2 * ticks * (h - 1) // 16) * 16
+            up.want(VMEM, (length, width), BF16)
+            up.scratch = [pltpu.SemaphoreType.DMA((2,))]
+            (pack,) = up.run(
+                functools.partial(pack_kernel, tick + 1, layers - 1), "pack", small_cost
+            )
+            call.give(VMEM, raised(pack), grad_last)
+            call.want(VMEM, (rows, width), BF16, 2)
+            call.want(VMEM, (tile, width), BF16, h - 1)
+            grad, *turned = call.run(functools.partial(turn_kernel, c), "turn", layer_cost)
+            handed.append(grad)
+            continue
+        call.give(VMEM, *handed)
+        call.want(HBM, (ticks, 1, rows, width), BF16)
+        call.scratch = [pltpu.VMEM((rows, width), BF16), pltpu.SemaphoreType.DMA((ticks,))]
+        (handoff,) = call.run(functools.partial(exit_kernel, c), "exit", layer_cost)
     call = Call()
     call.give(VMEM, *weight_sums)
     call.want(VMEM, (layers, chunk, width), BF16)
@@ -460,7 +538,7 @@
     call.want(HBM, (1, layers, width, width), F32)
     call.scratch = [pltpu.VMEM((layers, width, width), F32), pltpu.SemaphoreType.DMA((layers,))]
     (weight_grad,) = call.run(functools.partial(finish_kernel, h), "finish", small_cost)
-    return handed[-1], jnp.stack(initial)[None], weight_grad
+    return handoff, jnp.stack(initial)[None], weight_grad
 
 
 def solution(mesh):

time: 89.7 us -> 87.5 us (0.975)
  waiting for transfers between devices: 26.6 us -> 17 us
  starting transfers between devices: 45.8 us -> 48.3 us
  local copies, waits for them, and re-layouts: 0.16 us -> 2.31 us
  Pallas kernels: 11.9 us -> 13.8 us
    ppermute x33 -> x32, waiting for transfers between devices: 25.1 us -> 17 us  [swapped(): return lax.ppermute(block, 'rows', [(i, i ^ k) for i in range(n)])]
    ppermute x1 -> x6, starting transfers between devices: 1.29 us -> 5.47 us  [the longest x5 5.41 us: lowered(): return lax.ppermute(block, ('section', 'rows'), route)]
    pallas_call x16 -> x17, Pallas kernels: 11.9 us -> 13.8 us  [run(): pl.pallas_call(kernel, out_shape=self.outs, in_specs=self.specs, out_spec...]
    ppermute x33 -> x32, starting transfers between devices: 44.5 us -> 42.8 us  [swapped(): return lax.ppermute(block, 'rows', [(i, i ^ k) for i in range(n)])]
    ppermute x1 -> x6, waiting for transfers between devices: 1.54 us -> 0.02 us  [the longest x5 0.01 us: lowered(): return lax.ppermute(block, ('section', 'rows'), route)]
    unnamed x10 -> x14, local copies, waits for them, and re-layouts: 0.03 us -> 1.24 us
    mul x1, local copies, waits for them, and re-layouts: 0.13 us -> 1.08 us  [shards(): beta * jnp.dot(support[0, tick, layer].T, masked, preferred_element_type=...]
  transfers between devices with their start and end apart: 34 -> 38, of which waited for: 16 -> 11; matrix products, arithmetic and copies ran while one was open for 3% -> 5% of each run, Pallas kernels for 8% -> 12%
where the time goes in v12:
time: 87.5 us; the launch traced here: 87.4 us
  starting transfers between devices  48.3 us (55%)
  waiting for transfers between devices  17 us (19%)
  Pallas kernels  13.8 us (16%)
  matrix products  2.6 us (3%)
  local copies, waits for them, and re-layouts  2.31 us (3%)
  other arithmetic  2.28 us (3%)
  between operations  1.15 us (1%)
    ppermute x32, starting transfers between devices, swapped(): return lax.ppermute(block, 'rows', [(i, i ^ k) for i in range(n)])  42.8 us
    ppermute x32, waiting for transfers between devices, swapped(): return lax.ppermute(block, 'rows', [(i, i ^ k) for i in range(n)])  17 us
    pallas_call x17, Pallas kernels, run(): pl.pallas_call(kernel, out_shape=self.outs, in_specs=self.specs, out_spec...  13.8 us
    ppermute x5, starting transfers between devices, lowered(): return lax.ppermute(block, ('section', 'rows'), route)  5.41 us
  transfers between devices with their start and end apart: 38, of which 11 were waited for; matrix products, arithmetic and copies ran while one was open for 5% of the time, Pallas kernels for 12%

profile of v12, /device:TPU:0, one launch (start us, length us, event | category | flops | bytes accessed | tf_op | source)
XLA Modules:
  0.0 87.4 jit_solution(17793981797009059542)
XLA Ops:
  2.2 4.1 %collective-permute-start.3 = (bf16[256,256]{1,0:T(8,128)(2,1)S(1)}, bf16[256,256]{1,0:T(8,128)(2,1)S(1)}, u32[]{:S(2)}, u32[]{:S(2)}) collective-permute-start(bf16[256,256]{1,0:T(8,128)(2,1)S(1)} %fusion.3.refs_1_.refs_7_), channel_id=1, source_target_pairs={{0,4},{1,5},{2,6},{3,7},{4,0},{5,1},{6,2},{7,3},{8,12},{9,13},{10,... | collective-permute-start | bytes 393224 | tf_op jit(solution)/shard_map/ppermute | solution.py:26
  7.8 1.6 %collective-permute-start = (f32[4,256]{1,0:T(4,128)S(1)}, f32[4,256]{1,0:T(4,128)S(1)}, u32[]{:S(2)}, u32[]{:S(2)}) collective-permute-start(f32[4,256]{1,0:T(4,128)S(1)} %get-tuple-element.56), channel_id=1, source_target_pairs={{0,1},{1,0},{2,3},{3,2},{4,5},{5,4},{6,7},{7,6},{8,9},{9,8},{10,11... | collective-permute-start | bytes 12296 | tf_op jit(solution)/shard_map/ppermute | solution.py:26
  9.3 1.6 %collective-permute-start.1 = (f32[4,256]{1,0:T(4,128)S(1)}, f32[4,256]{1,0:T(4,128)S(1)}, u32[]{:S(2)}, u32[]{:S(2)}) collective-permute-start(f32[4,256]{1,0:T(4,128)S(1)} %get-tuple-element.57), channel_id=1, source_target_pairs={{0,2},{1,3},{2,0},{3,1},{4,6},{5,7},{6,4},{7,5},{8,10},{9,11},{10,... | collective-permute-start | bytes 12296 | tf_op jit(solution)/shard_map/ppermute | solution.py:26
  11.3 2.8 %densify.2.refs_6_.refs_1_ = bf16[256,1152]{1,0:T(8,128)(2,1)S(1)} custom-call(s32[3,96]{1,0:T(4,128)S(1)} %pad_add_fusion.words_ref, bf16[1,2,96,128,128]{4,3,2,1,0:T(8,128)(2,1)} %vals_ref.3), custom_call_target="tpu_custom_call" | custom-call | flops 31457280 | bytes 3145728 | tf_op jit(solution)/shard_map/densify/pallas_call | solution.py:71
  16.3 1.9 %collective-permute-start.5 = (bf16[256,256]{1,0:T(8,128)(2,1)S(1)}, bf16[256,256]{1,0:T(8,128)(2,1)S(1)}, u32[]{:S(2)}, u32[]{:S(2)}) collective-permute-start(bf16[256,256]{1,0:T(8,128)(2,1)S(1)} %get-tuple-element.62), channel_id=1, source_target_pairs={{0,2},{1,3},{2,0},{3,1},{4,6},{5,7},{6,4},{7,5},{8,10},{9,11},{10,... | collective-permute-start | bytes 393224 | tf_op jit(solution)/shard_map/ppermute | solution.py:26
  19.4 2.5 %collective-permute-done.4.refs_9_ = bf16[256,256]{1,0:T(8,128)(2,1)S(1)} collective-permute-done((bf16[256,256]{1,0:T(8,128)(2,1)S(1)}, bf16[256,256]{1,0:T(8,128)(2,1)S(1)}, u32[]{:S(2)}, u32[]{:S(2)}) %collective-permute-start.4) | collective-permute-done | bytes 131104 | tf_op jit(solution)/shard_map/ppermute | solution.py:26
  22.0 2.1 %collective-permute-done.6.refs_11_ = bf16[256,256]{1,0:T(8,128)(2,1)S(1)} collective-permute-done((bf16[256,256]{1,0:T(8,128)(2,1)S(1)}, bf16[256,256]{1,0:T(8,128)(2,1)S(1)}, u32[]{:S(2)}, u32[]{:S(2)}) %collective-permute-start.6) | collective-permute-done | bytes 131104 | tf_op jit(solution)/shard_map/ppermute | solution.py:26
  27.1 1.7 %collective-permute-start.12 = (bf16[128,256]{1,0:T(8,128)(2,1)S(1)}, bf16[128,256]{1,0:T(8,128)(2,1)S(1)}, u32[]{:S(2)}, u32[]{:S(2)}) collective-permute-start(bf16[128,256]{1,0:T(8,128)(2,1)S(1)} %get-tuple-element.69), channel_id=1, source_target_pairs={{0,2},{1,3},{2,0},{3,1},{4,6},{5,7},{6,4},{7,5},{8,10},{9,11},{10,... | collective-permute-start | bytes 196616 | tf_op jit(solution)/shard_map/ppermute | solution.py:26
  29.7 2.9 %collective-permute-done.7.refs_0_.refs_3_ = bf16[256,256]{1,0:T(8,128)(2,1)S(1)} collective-permute-done((bf16[256,256]{1,0:T(8,128)(2,1)S(1)}, bf16[256,256]{1,0:T(8,128)(2,1)S(1)}, u32[]{:S(2)}, u32[]{:S(2)}) %collective-permute-start.7) | collective-permute-done | bytes 131104 | tf_op jit(solution)/shard_map/ppermute | solution.py:26
  33.4 2.7 %collective-permute-start.10 = (bf16[128,256]{1,0:T(8,128)(2,1)S(1)}, bf16[128,256]{1,0:T(8,128)(2,1)S(1)}, u32[]{:S(2)}, u32[]{:S(2)}) collective-permute-start(bf16[128,256]{1,0:T(8,128)(2,1)S(1)} %get-tuple-element.67), channel_id=1, source_target_pairs={{0,3},{1,2},{2,1},{3,0},{4,7},{5,6},{6,5},{7,4},{8,11},{9,10},{10,... | collective-permute-start | bytes 196616 | tf_op jit(solution)/shard_map/ppermute | solution.py:26
  36.1 3.4 %densify.3.refs_6_.refs_1_ = bf16[256,1152]{1,0:T(8,128)(2,1)S(1)} custom-call(s32[3,96]{1,0:T(4,128)S(1)} %pad_add_fusion.words_ref, bf16[1,2,96,128,128]{4,3,2,1,0:T(8,128)(2,1)} %vals_ref.3), custom_call_target="tpu_custom_call" | custom-call | flops 31457280 | bytes 3145728 | tf_op jit(solution)/shard_map/densify/pallas_call | solution.py:71
  40.8 2.6 %collective-permute-start.16 = (bf16[256,256]{1,0:T(8,128)(2,1)}, bf16[256,256]{1,0:T(8,128)(2,1)S(1)}, u32[]{:S(2)}, u32[]{:S(2)}) collective-permute-start(bf16[256,256]{1,0:T(8,128)(2,1)} %get-tuple-element.78), channel_id=1, source_target_pairs={{0,28},{1,29},{2,30},{3,31},{4,24},{5,25},{6,26},{7,27},{8,4},{9,5... | collective-permute-start | bytes 393224 | tf_op jit(solution)/shard_map/ppermute | solution.py:34
  52.5 1.6 %collective-permute-start.20 = (bf16[128,256]{1,0:T(8,128)(2,1)S(1)}, bf16[128,256]{1,0:T(8,128)(2,1)S(1)}, u32[]{:S(2)}, u32[]{:S(2)}) collective-permute-start(bf16[128,256]{1,0:T(8,128)(2,1)S(1)} %get-tuple-element.86), channel_id=1, source_target_pairs={{0,1},{1,0},{2,3},{3,2},{4,5},{5,4},{6,7},{7,6},{8,9},{9,8},{10,11... | collective-permute-start | bytes 196616 | tf_op jit(solution)/shard_map/ppermute | solution.py:26
  54.1 1.9 %collective-permute-start.22 = (bf16[128,256]{1,0:T(8,128)(2,1)S(1)}, bf16[128,256]{1,0:T(8,128)(2,1)S(1)}, u32[]{:S(2)}, u32[]{:S(2)}) collective-permute-start(bf16[128,256]{1,0:T(8,128)(2,1)S(1)} %get-tuple-element.88), channel_id=1, source_target_pairs={{0,3},{1,2},{2,1},{3,0},{4,7},{5,6},{6,5},{7,4},{8,11},{9,10},{10,... | collective-permute-start | bytes 196616 | tf_op jit(solution)/shard_map/ppermute | solution.py:26
  56.7 2.4 %collective-permute-start.25 = (bf16[64,256]{1,0:T(8,128)(2,1)}, bf16[64,256]{1,0:T(8,128)(2,1)S(1)}, u32[]{:S(2)}, u32[]{:S(2)}) collective-permute-start(bf16[64,256]{1,0:T(8,128)(2,1)} %copy-done.4), channel_id=1, source_target_pairs={{0,3},{1,2},{2,1},{3,0},{4,7},{5,6},{6,5},{7,4},{8,11},{9,10},{10,... | collective-permute-start | bytes 98312 | tf_op jit(solution)/shard_map/ppermute | solution.py:26
  59.3 1.9 %collective-permute-done.24.refs_1_ = bf16[64,256]{1,0:T(8,128)(2,1)S(1)} collective-permute-done((bf16[64,256]{1,0:T(8,128)(2,1)}, bf16[64,256]{1,0:T(8,128)(2,1)S(1)}, u32[]{:S(2)}, u32[]{:S(2)}) %collective-permute-start.24) | collective-permute-done | bytes 32800 | tf_op jit(solution)/shard_map/ppermute | solution.py:26
  63.2 1.6 %collective-permute-start.26 = (bf16[256,256]{1,0:T(8,128)(2,1)S(1)}, bf16[256,256]{1,0:T(8,128)(2,1)S(1)}, u32[]{:S(2)}, u32[]{:S(2)}) collective-permute-start(bf16[256,256]{1,0:T(8,128)(2,1)S(1)} %get-tuple-element.97.refs_2_), channel_id=1, source_target_pairs={{0,4},{1,5},{2,6},{3,7},{4,0},{5,1},{6,2},{7,3},{8,12},{9,13},{10,... | collective-permute-start | bytes 393224 | tf_op jit(solution)/shard_map/ppermute | solution.py:26
  66.6 1.7 %collective-permute-start.29 = (bf16[192,256]{1,0:T(8,128)(2,1)S(1)}, bf16[192,256]{1,0:T(8,128)(2,1)S(1)}, u32[]{:S(2)}, u32[]{:S(2)}) collective-permute-start(bf16[192,256]{1,0:T(8,128)(2,1)S(1)} %get-tuple-element.100), channel_id=1, source_target_pairs={{0,3},{1,2},{2,1},{3,0},{4,7},{5,6},{6,5},{7,4},{8,11},{9,10},{10,... | collective-permute-start | bytes 294920 | tf_op jit(solution)/shard_map/ppermute | solution.py:26
  68.3 1.4 %collective-permute-start.34 = (bf16[64,256]{1,0:T(8,128)(2,1)S(1)}, bf16[64,256]{1,0:T(8,128)(2,1)S(1)}, u32[]{:S(2)}, u32[]{:S(2)}) collective-permute-start(bf16[64,256]{1,0:T(8,128)(2,1)S(1)} %half_sum.2.refs_2_), channel_id=1, source_target_pairs={{0,4},{1,5},{2,6},{3,7},{4,0},{5,1},{6,2},{7,3},{8,12},{9,13},{10,... | collective-permute-start | bytes 98312 | tf_op jit(solution)/shard_map/ppermute | solution.py:26
  69.7 1.9 %collective-permute-done.26.refs_0_.refs_3_ = bf16[256,256]{1,0:T(8,128)(2,1)S(1)} collective-permute-done((bf16[256,256]{1,0:T(8,128)(2,1)S(1)}, bf16[256,256]{1,0:T(8,128)(2,1)S(1)}, u32[]{:S(2)}, u32[]{:S(2)}) %collective-permute-start.26) | collective-permute-done | bytes 131104 | tf_op jit(solution)/shard_map/ppermute | solution.py:26
  71.7 2.3 %collective-permute-start.30 = (bf16[128,256]{1,0:T(8,128)(2,1)S(1)}, bf16[128,256]{1,0:T(8,128)(2,1)S(1)}, u32[]{:S(2)}, u32[]{:S(2)}) collective-permute-start(bf16[128,256]{1,0:T(8,128)(2,1)S(1)} %get-tuple-element.101), channel_id=1, source_target_pairs={{0,1},{1,0},{2,3},{3,2},{4,5},{5,4},{6,7},{7,6},{8,9},{9,8},{10,11... | collective-permute-start | bytes 196616 | tf_op jit(solution)/shard_map/ppermute | solution.py:26
  75.4 1.9 %collective-permute-start.31 = (bf16[128,256]{1,0:T(8,128)(2,1)S(1)}, bf16[128,256]{1,0:T(8,128)(2,1)S(1)}, u32[]{:S(2)}, u32[]{:S(2)}) collective-permute-start(bf16[128,256]{1,0:T(8,128)(2,1)S(1)} %get-tuple-element.102), channel_id=1, source_target_pairs={{0,2},{1,3},{2,0},{3,1},{4,6},{5,7},{6,4},{7,5},{8,10},{9,11},{10,... | collective-permute-start | bytes 196616 | tf_op jit(solution)/shard_map/ppermute | solution.py:26
  78.2 1.8 %collective-permute-done.33.refs_1_ = bf16[64,256]{1,0:T(8,128)(2,1)S(1)} collective-permute-done((bf16[64,256]{1,0:T(8,128)(2,1)S(1)}, bf16[64,256]{1,0:T(8,128)(2,1)S(1)}, u32[]{:S(2)}, u32[]{:S(2)}) %collective-permute-start.33) | collective-permute-done | bytes 32800 | tf_op jit(solution)/shard_map/ppermute | solution.py:26
  80.9 2.8 %collective-permute-start.37 = (bf16[2,64,256]{2,1,0:T(8,128)(2,1)S(1)}, bf16[2,64,256]{2,1,0:T(8,128)(2,1)S(1)}, u32[]{:S(2)}, u32[]{:S(2)}) collective-permute-start(bf16[2,64,256]{2,1,0:T(8,128)(2,1)S(1)} %total.1.refs_0_), channel_id=1, source_target_pairs={{0,3},{1,2},{2,1},{3,0},{4,7},{5,6},{6,5},{7,4},{8,11},{9,10},{10,... | collective-permute-start | bytes 196616 | tf_op jit(solution)/shard_map/ppermute | solution.py:26
  (92 shorter events, 33.1 us)
Async XLA Ops:
  2.2 13.2 %collective-permute-start.3 = (bf16[256,256]{1,0:T(8,128)(2,1)S(1)}, bf16[256,256]{1,0:T(8,128)(2,1)S(1)}, u32[]{:S(2)}, u32[]{:S(2)}) collective-permute-start(bf16[256,256]{1,0:T(8,128)(2,1)S(1)} %fusion.3.refs_1_.refs_7_), channel_id=1, source_target_pairs={{0,4},{1,5},{2,6},{3,7},{4,0},{5,1},{6,2},{7,3},{8,12},{9,13},{10,... | collective-permute-start | bytes 393224 | tf_op jit(solution)/shard_map/ppermute | solution.py:26
  7.8 6.4 %collective-permute-start = (f32[4,256]{1,0:T(4,128)S(1)}, f32[4,256]{1,0:T(4,128)S(1)}, u32[]{:S(2)}, u32[]{:S(2)}) collective-permute-start(f32[4,256]{1,0:T(4,128)S(1)} %get-tuple-element.56), channel_id=1, source_target_pairs={{0,1},{1,0},{2,3},{3,2},{4,5},{5,4},{6,7},{7,6},{8,9},{9,8},{10,11... | collective-permute-start | bytes 12296 | tf_op jit(solution)/shard_map/ppermute | solution.py:26
  15.5 6.4 %collective-permute-start.4 = (bf16[256,256]{1,0:T(8,128)(2,1)S(1)}, bf16[256,256]{1,0:T(8,128)(2,1)S(1)}, u32[]{:S(2)}, u32[]{:S(2)}) collective-permute-start(bf16[256,256]{1,0:T(8,128)(2,1)S(1)} %get-tuple-element.61), channel_id=1, source_target_pairs={{0,1},{1,0},{2,3},{3,2},{4,5},{5,4},{6,7},{7,6},{8,9},{9,8},{10,11... | collective-permute-start | bytes 393224 | tf_op jit(solution)/shard_map/ppermute | solution.py:26
  19.4 20.2 %collective-permute-start.14 = (bf16[528,256]{1,0:T(8,128)(2,1)S(1)}, bf16[528,256]{1,0:T(8,128)(2,1)S(1)}, u32[]{:S(2)}, u32[]{:S(2)}) collective-permute-start(bf16[528,256]{1,0:T(8,128)(2,1)S(1)} %pack.1), channel_id=1, source_target_pairs={{0,8},{8,16},{16,24},{24,0},{1,9},{9,17},{17,25},{25,1},{2,10},{10... | collective-permute-start | bytes 811016 | tf_op jit(solution)/shard_map/ppermute | solution.py:39
  25.1 7.4 %collective-permute-start.7 = (bf16[256,256]{1,0:T(8,128)(2,1)S(1)}, bf16[256,256]{1,0:T(8,128)(2,1)S(1)}, u32[]{:S(2)}, u32[]{:S(2)}) collective-permute-start(bf16[256,256]{1,0:T(8,128)(2,1)S(1)} %get-tuple-element.64.refs_2_), channel_id=1, source_target_pairs={{0,4},{1,5},{2,6},{3,7},{4,0},{5,1},{6,2},{7,3},{8,12},{9,13},{10,... | collective-permute-start | bytes 393224 | tf_op jit(solution)/shard_map/ppermute | solution.py:26
  26.2 7.2 %collective-permute-start.11 = (bf16[128,256]{1,0:T(8,128)(2,1)S(1)}, bf16[128,256]{1,0:T(8,128)(2,1)S(1)}, u32[]{:S(2)}, u32[]{:S(2)}) collective-permute-start(bf16[128,256]{1,0:T(8,128)(2,1)S(1)} %get-tuple-element.68), channel_id=1, source_target_pairs={{0,1},{1,0},{2,3},{3,2},{4,5},{5,4},{6,7},{7,6},{8,9},{9,8},{10,11... | collective-permute-start | bytes 196616 | tf_op jit(solution)/shard_map/ppermute | solution.py:26
  28.8 7.3 %collective-permute-start.13 = (bf16[128,256]{1,0:T(8,128)(2,1)S(1)}, bf16[128,256]{1,0:T(8,128)(2,1)S(1)}, u32[]{:S(2)}, u32[]{:S(2)}) collective-permute-start(bf16[128,256]{1,0:T(8,128)(2,1)S(1)} %get-tuple-element.70), channel_id=1, source_target_pairs={{0,3},{1,2},{2,1},{3,0},{4,7},{5,6},{6,5},{7,4},{8,11},{9,10},{10,... | collective-permute-start | bytes 196616 | tf_op jit(solution)/shard_map/ppermute | solution.py:26
  32.6 7.0 %collective-permute-start.8 = (bf16[128,256]{1,0:T(8,128)(2,1)S(1)}, bf16[128,256]{1,0:T(8,128)(2,1)S(1)}, u32[]{:S(2)}, u32[]{:S(2)}) collective-permute-start(bf16[128,256]{1,0:T(8,128)(2,1)S(1)} %get-tuple-element.65), channel_id=1, source_target_pairs={{0,1},{1,0},{2,3},{3,2},{4,5},{5,4},{6,7},{7,6},{8,9},{9,8},{10,11... | collective-permute-start | bytes 196616 | tf_op jit(solution)/shard_map/ppermute | solution.py:26
  40.8 7.4 %collective-permute-start.15 = (bf16[256,256]{1,0:T(8,128)(2,1)S(1)}, bf16[256,256]{1,0:T(8,128)(2,1)S(1)}, u32[]{:S(2)}, u32[]{:S(2)}) collective-permute-start(bf16[256,256]{1,0:T(8,128)(2,1)S(1)} %get-tuple-element.76.refs_10_), channel_id=1, source_target_pairs={{0,24},{1,25},{2,26},{3,27},{4,28},{5,29},{6,30},{7,31},{8,0},{9,1... | collective-permute-start | bytes 393224 | tf_op jit(solution)/shard_map/ppermute | solution.py:34
  40.8 11.6 %collective-permute-start.16 = (bf16[256,256]{1,0:T(8,128)(2,1)}, bf16[256,256]{1,0:T(8,128)(2,1)S(1)}, u32[]{:S(2)}, u32[]{:S(2)}) collective-permute-start(bf16[256,256]{1,0:T(8,128)(2,1)} %get-tuple-element.78), channel_id=1, source_target_pairs={{0,28},{1,29},{2,30},{3,31},{4,24},{5,25},{6,26},{7,27},{8,4},{9,5... | collective-permute-start | bytes 393224 | tf_op jit(solution)/shard_map/ppermute | solution.py:34
  43.5 8.9 %collective-permute-start.17 = (bf16[128,256]{1,0:T(8,128)(2,1)}, bf16[128,256]{1,0:T(8,128)(2,1)S(1)}, u32[]{:S(2)}, u32[]{:S(2)}) collective-permute-start(bf16[128,256]{1,0:T(8,128)(2,1)} %get-tuple-element.79), channel_id=1, source_target_pairs={{0,25},{1,24},{2,27},{3,26},{4,29},{5,28},{6,31},{7,30},{8,1},{9,0... | collective-permute-start | bytes 196616 | tf_op jit(solution)/shard_map/ppermute | solution.py:34
  44.5 7.9 %collective-permute-start.18 = (bf16[128,256]{1,0:T(8,128)(2,1)}, bf16[128,256]{1,0:T(8,128)(2,1)S(1)}, u32[]{:S(2)}, u32[]{:S(2)}) collective-permute-start(bf16[128,256]{1,0:T(8,128)(2,1)} %get-tuple-element.80), channel_id=1, source_target_pairs={{0,26},{1,27},{2,24},{3,25},{4,30},{5,31},{6,28},{7,29},{8,2},{9,3... | collective-permute-start | bytes 196616 | tf_op jit(solution)/shard_map/ppermute | solution.py:34
  45.2 7.2 %collective-permute-start.19 = (bf16[128,256]{1,0:T(8,128)(2,1)S(1)}, bf16[128,256]{1,0:T(8,128)(2,1)S(1)}, u32[]{:S(2)}, u32[]{:S(2)}) collective-permute-start(bf16[128,256]{1,0:T(8,128)(2,1)S(1)} %get-tuple-element.81), channel_id=1, source_target_pairs={{0,27},{1,26},{2,25},{3,24},{4,31},{5,30},{6,29},{7,28},{8,3},{9,2... | collective-permute-start | bytes 196616 | tf_op jit(solution)/shard_map/ppermute | solution.py:34
  52.5 9.3 %collective-permute-start.20 = (bf16[128,256]{1,0:T(8,128)(2,1)S(1)}, bf16[128,256]{1,0:T(8,128)(2,1)S(1)}, u32[]{:S(2)}, u32[]{:S(2)}) collective-permute-start(bf16[128,256]{1,0:T(8,128)(2,1)S(1)} %get-tuple-element.86), channel_id=1, source_target_pairs={{0,1},{1,0},{2,3},{3,2},{4,5},{5,4},{6,7},{7,6},{8,9},{9,8},{10,11... | collective-permute-start | bytes 196616 | tf_op jit(solution)/shard_map/ppermute | solution.py:26
  54.1 7.7 %collective-permute-start.21 = (bf16[128,256]{1,0:T(8,128)(2,1)S(1)}, bf16[128,256]{1,0:T(8,128)(2,1)S(1)}, u32[]{:S(2)}, u32[]{:S(2)}) collective-permute-start(bf16[128,256]{1,0:T(8,128)(2,1)S(1)} %get-tuple-element.87), channel_id=1, source_target_pairs={{0,2},{1,3},{2,0},{3,1},{4,6},{5,7},{6,4},{7,5},{8,10},{9,11},{10,... | collective-permute-start | bytes 196616 | tf_op jit(solution)/shard_map/ppermute | solution.py:26
  54.1 7.7 %collective-permute-start.22 = (bf16[128,256]{1,0:T(8,128)(2,1)S(1)}, bf16[128,256]{1,0:T(8,128)(2,1)S(1)}, u32[]{:S(2)}, u32[]{:S(2)}) collective-permute-start(bf16[128,256]{1,0:T(8,128)(2,1)S(1)} %get-tuple-element.88), channel_id=1, source_target_pairs={{0,3},{1,2},{2,1},{3,0},{4,7},{5,6},{6,5},{7,4},{8,11},{9,10},{10,... | collective-permute-start | bytes 196616 | tf_op jit(solution)/shard_map/ppermute | solution.py:26
  63.2 8.5 %collective-permute-start.26 = (bf16[256,256]{1,0:T(8,128)(2,1)S(1)}, bf16[256,256]{1,0:T(8,128)(2,1)S(1)}, u32[]{:S(2)}, u32[]{:S(2)}) collective-permute-start(bf16[256,256]{1,0:T(8,128)(2,1)S(1)} %get-tuple-element.97.refs_2_), channel_id=1, source_target_pairs={{0,4},{1,5},{2,6},{3,7},{4,0},{5,1},{6,2},{7,3},{8,12},{9,13},{10,... | collective-permute-start | bytes 393224 | tf_op jit(solution)/shard_map/ppermute | solution.py:26
  64.8 9.2 %collective-permute-start.27 = (bf16[192,256]{1,0:T(8,128)(2,1)S(1)}, bf16[192,256]{1,0:T(8,128)(2,1)S(1)}, u32[]{:S(2)}, u32[]{:S(2)}) collective-permute-start(bf16[192,256]{1,0:T(8,128)(2,1)S(1)} %get-tuple-element.98), channel_id=1, source_target_pairs={{0,1},{1,0},{2,3},{3,2},{4,5},{5,4},{6,7},{7,6},{8,9},{9,8},{10,11... | collective-permute-start | bytes 294920 | tf_op jit(solution)/shard_map/ppermute | solution.py:26
  65.6 8.4 %collective-permute-start.28 = (bf16[192,256]{1,0:T(8,128)(2,1)S(1)}, bf16[192,256]{1,0:T(8,128)(2,1)S(1)}, u32[]{:S(2)}, u32[]{:S(2)}) collective-permute-start(bf16[192,256]{1,0:T(8,128)(2,1)S(1)} %get-tuple-element.99), channel_id=1, source_target_pairs={{0,2},{1,3},{2,0},{3,1},{4,6},{5,7},{6,4},{7,5},{8,10},{9,11},{10,... | collective-permute-start | bytes 294920 | tf_op jit(solution)/shard_map/ppermute | solution.py:26
  66.6 8.4 %collective-permute-start.29 = (bf16[192,256]{1,0:T(8,128)(2,1)S(1)}, bf16[192,256]{1,0:T(8,128)(2,1)S(1)}, u32[]{:S(2)}, u32[]{:S(2)}) collective-permute-start(bf16[192,256]{1,0:T(8,128)(2,1)S(1)} %get-tuple-element.100), channel_id=1, source_target_pairs={{0,3},{1,2},{2,1},{3,0},{4,7},{5,6},{6,5},{7,4},{8,11},{9,10},{10,... | collective-permute-start | bytes 294920 | tf_op jit(solution)/shard_map/ppermute | solution.py:26
  68.3 9.9 %collective-permute-start.34 = (bf16[64,256]{1,0:T(8,128)(2,1)S(1)}, bf16[64,256]{1,0:T(8,128)(2,1)S(1)}, u32[]{:S(2)}, u32[]{:S(2)}) collective-permute-start(bf16[64,256]{1,0:T(8,128)(2,1)S(1)} %half_sum.2.refs_2_), channel_id=1, source_target_pairs={{0,4},{1,5},{2,6},{3,7},{4,0},{5,1},{6,2},{7,3},{8,12},{9,13},{10,... | collective-permute-start | bytes 98312 | tf_op jit(solution)/shard_map/ppermute | solution.py:26
  71.7 9.2 %collective-permute-start.30 = (bf16[128,256]{1,0:T(8,128)(2,1)S(1)}, bf16[128,256]{1,0:T(8,128)(2,1)S(1)}, u32[]{:S(2)}, u32[]{:S(2)}) collective-permute-start(bf16[128,256]{1,0:T(8,128)(2,1)S(1)} %get-tuple-element.101), channel_id=1, source_target_pairs={{0,1},{1,0},{2,3},{3,2},{4,5},{5,4},{6,7},{7,6},{8,9},{9,8},{10,11... | collective-permute-start | bytes 196616 | tf_op jit(solution)/shard_map/ppermute | solution.py:26
  75.4 9.1 %collective-permute-start.31 = (bf16[128,256]{1,0:T(8,128)(2,1)S(1)}, bf16[128,256]{1,0:T(8,128)(2,1)S(1)}, u32[]{:S(2)}, u32[]{:S(2)}) collective-permute-start(bf16[128,256]{1,0:T(8,128)(2,1)S(1)} %get-tuple-element.102), channel_id=1, source_target_pairs={{0,2},{1,3},{2,0},{3,1},{4,6},{5,7},{6,4},{7,5},{8,10},{9,11},{10,... | collective-permute-start | bytes 196616 | tf_op jit(solution)/shard_map/ppermute | solution.py:26
  77.3 7.2 %collective-permute-start.32 = (bf16[128,256]{1,0:T(8,128)(2,1)S(1)}, bf16[128,256]{1,0:T(8,128)(2,1)S(1)}, u32[]{:S(2)}, u32[]{:S(2)}) collective-permute-start(bf16[128,256]{1,0:T(8,128)(2,1)S(1)} %get-tuple-element.103), channel_id=1, source_target_pairs={{0,3},{1,2},{2,1},{3,0},{4,7},{5,6},{6,5},{7,4},{8,11},{9,10},{10,... | collective-permute-start | bytes 196616 | tf_op jit(solution)/shard_map/ppermute | solution.py:26
  (21 other events, 204.4 us)

commit v13 on v12

--- a/solution.py
+++ b/solution.py
@@ -234,8 +234,10 @@
         got = take_got(refs, c)
     if c["final"]:
         support_all, acc_ref = refs.take(2)
+        pending = refs.take(c["pending"])
     image_ref = refs.take()
-    sends = refs.take(h - 1) if c["final"] or not c["entry"] else []
+    sends = [] if c["entry"] else refs.take(h - 1)
+    parts = refs.take(h - 1) if c["final"] and c["layer"] else []
     out_ref = refs.take()
     preact_ref, weight_ref, load_sems = refs.take(3)
 
@@ -273,10 +275,12 @@
         place = lax.rem(lax.axis_index("rows"), h)
         for k in range(1, h):
             part = tile_at(term_ref, jnp.bitwise_xor(place, k), chunk).astype(BF16)
-            if c["entry"]:
-                sends[k - 1][...] = part
+            if c["layer"]:
+                parts[k - 1][...] = part
             else:
                 sends[k - 1][tile : tile + chunk, :] = part
+                for i, ref in enumerate(pending[k - 1 :: h - 1], 1):
+                    sends[k - 1][tile + i * chunk : tile + (i + 1) * chunk, :] = ref[...]
         out_ref[...] = tile_at(term_ref, place, chunk)
     else:
         out_ref[...] = masked
@@ -297,18 +301,19 @@
             send[...] = chosen(far_ref, asked_ref[row + 1 : row + 2, :], rows, tile)
 
 
-def half_sum_kernel(kept_ref, *refs):
-    total = kept_ref[...]
-    for ref in refs[:-1]:
-        total = total + ref[ref.shape[0] - total.shape[0] :, :].astype(F32)
-    refs[-1][...] = total.astype(BF16)
-
-
-def total_kernel(layers, *refs):
+def half_sum_kernel(layers, tile, *refs):
+    out_ref = refs[-1]
+    chunk = out_ref.shape[1]
     for layer in range(layers):
-        mine_ref, far_ref = refs[2 * layer : 2 * layer + 2]
-        total = mine_ref[...].astype(F32) + far_ref[...].astype(F32)
-        refs[-1][layer] = total.astype(BF16)
+        total = refs[layer][...]
+        at = tile + layer * chunk
+        for ref in refs[layers:-1]:
+            total = total + ref[at : at + chunk, :].astype(F32)
+        out_ref[layer] = total.astype(BF16)
+
+
+def total_kernel(mine_ref, far_ref, out_ref):
+    out_ref[...] = (mine_ref[...].astype(F32) + far_ref[...].astype(F32)).astype(BF16)
 
 
 def turn_kernel(c, *refs):
@@ -384,7 +389,7 @@
     handed = []
     turned = None
     weight_acc = [None] * layers
-    weight_sums = []
+    kept_chunks, pending = [], []
     initial = []
     base = dict(
         n=n, tile=tile, rows=rows, width=width, layers=layers, sections=sections, chunk=chunk,
@@ -412,7 +417,7 @@
             beta = jnp.log(BETA_SCALE / (layers * section + layer + 1).astype(F32) + 1.0)
             c = dict(
                 base, layer=layer, tick=tick, entry=entry, final=final, joined=joined,
-                first=tick == 0 and entry,
+                first=tick == 0 and entry, pending=0 if layer else len(pending),
             )
             if c["first"]:
                 masked = jnp.where(
@@ -431,10 +436,14 @@
                 if final:
                     call.give(HBM, support)
                     call.give(VMEM, weight_acc[layer])
-                message = (0 if entry else tile) + (chunk if final else 0)
+                    if layer == 0:
+                        call.give(VMEM, *pending)
                 call.want(VMEM, (rows, width), BF16)
-                if message:
+                if not entry:
+                    message = tile + (layers * chunk if final and layer == 0 else 0)
                     call.want(VMEM, (message, width), BF16, h - 1)
+                if final and layer:
+                    call.want(VMEM, (chunk, width), BF16, h - 1)
                 if final:
                     call.want(VMEM, (chunk, width), F32)
                 else:
@@ -455,9 +464,10 @@
                     )
                 )
                 image = results.take()
-                sends = results.take(h - 1) if message else []
+                sends = [] if entry else results.take(h - 1)
+                if final and layer:
+                    pending = results.take(h - 1) + pending
                 kept = masked = results.take()
-            parts = near = []
             if turned is not None:
                 far = lowered(turned[0], h)
                 near = shared(turned[1:], lowered)
@@ -467,7 +477,7 @@
                     parts = shared(sends)
             else:
                 far = swapped(image, h)
-                near = parts = [] if c["first"] else shared(sends)
+                near = [] if c["first"] else shared(sends)
             ready = image
             if c["first"]:
                 adjs[0] = densify(0, words, tile_vals, row_tiles, n)
@@ -485,17 +495,15 @@
                 adjs[tick + 1] = densify(tick + 1, later, tile_vals, row_tiles, n)
                 relayed, adjs[tick + 1] = lax.optimization_barrier((relayed, adjs[tick + 1]))
             if final:
-                if not entry:
-                    kept, *_ = lax.optimization_barrier((kept, *relays))
+                kept_chunks.insert(0, kept)
+            if final and layer == 0:
+                kept, _ = lax.optimization_barrier((kept_chunks, relays))
                 call = Call()
-                call.give(VMEM, kept, *parts)
-                call.want(VMEM, (chunk, width), BF16)
+                call.give(VMEM, *kept, *near)
+                call.want(VMEM, (layers, chunk, width), BF16)
                 (mine,) = call.run(
-                    half_sum_kernel, "half_sum", small_cost
+                    functools.partial(half_sum_kernel, layers, tile), "half_sum", small_cost
                 )
-                if layer > 0:
-                    relayed, mine = lax.optimization_barrier((relayed, mine))
-                weight_sums = [mine, swapped(mine, h), *weight_sums]
             got = [far, *near, *relayed]
             joined = c["first"]
             toward = toward + ALPHA * image.astype(F32)
@@ -530,9 +538,9 @@
         call.scratch = [pltpu.VMEM((rows, width), BF16), pltpu.SemaphoreType.DMA((ticks,))]
         (handoff,) = call.run(functools.partial(exit_kernel, c), "exit", layer_cost)
     call = Call()
-    call.give(VMEM, *weight_sums)
+    call.give(VMEM, mine, swapped(mine, h))
     call.want(VMEM, (layers, chunk, width), BF16)
-    (total,) = call.run(functools.partial(total_kernel, layers), "total", small_cost)
+    (total,) = call.run(total_kernel, "total", small_cost)
     call = Call()
     call.give(VMEM, total, *shared([total] * (h - 1)))
     call.want(HBM, (1, layers, width, width), F32)

time: 87.5 us -> 84.8 us (0.969)
  starting transfers between devices: 48.3 us -> 42.5 us
  waiting for transfers between devices: 17 us -> 22 us
  local copies, waits for them, and re-layouts: 2.31 us -> 1.1 us
    ppermute x32 -> x28, starting transfers between devices: 42.8 us -> 36.3 us  [swapped(): return lax.ppermute(block, 'rows', [(i, i ^ k) for i in range(n)])]
    ppermute x5, waiting for transfers between devices: 0.01 us -> 2.98 us  [lowered(): return lax.ppermute(block, ('section', 'rows'), route)]
    ppermute x32 -> x28, waiting for transfers between devices: 17 us -> 19 us  [swapped(): return lax.ppermute(block, 'rows', [(i, i ^ k) for i in range(n)])]
    unnamed x14 -> x10, local copies, waits for them, and re-layouts: 1.24 us -> 0.03 us
    pallas_call x17 -> x16, Pallas kernels: 13.8 us -> 13 us  [run(): pl.pallas_call(kernel, out_shape=self.outs, in_specs=self.specs, out_spec...]
  transfers between devices with their start and end apart: 38 -> 34, of which waited for: 11 -> 15; matrix products, arithmetic and copies ran while one was open for 5% -> 5% of each run, Pallas kernels for 12% -> 12%
where the time goes in v13:
time: 84.8 us; the launch traced here: 84.6 us
  starting transfers between devices  42.5 us (50%)
  waiting for transfers between devices  22 us (26%)
  Pallas kernels  13 us (15%)
  matrix products  2.6 us (3%)
  other arithmetic  2.28 us (3%)
  between operations  1.11 us (1%)
  local copies, waits for them, and re-layouts  1.1 us (1%)
    ppermute x28, starting transfers between devices, swapped(): return lax.ppermute(block, 'rows', [(i, i ^ k) for i in range(n)])  36.3 us
    ppermute x28, waiting for transfers between devices, swapped(): return lax.ppermute(block, 'rows', [(i, i ^ k) for i in range(n)])  19 us
    pallas_call x16, Pallas kernels, run(): pl.pallas_call(kernel, out_shape=self.outs, in_specs=self.specs, out_spec...  13 us
    ppermute x5, starting transfers between devices, lowered(): return lax.ppermute(block, ('section', 'rows'), route)  6.17 us
    ppermute x5, waiting for transfers between devices, lowered(): return lax.ppermute(block, ('section', 'rows'), route)  2.98 us
  transfers between devices with their start and end apart: 34, of which 15 were waited for; matrix products, arithmetic and copies ran while one was open for 5% of the time, Pallas kernels for 12%

profile of v13, /device:TPU:0, one launch (start us, length us, event | category | flops | bytes accessed | tf_op | source)
XLA Modules:
  0.0 84.6 jit_solution(16570534785247034175)
XLA Ops:
  2.2 4.1 %collective-permute-start.3 = (bf16[256,256]{1,0:T(8,128)(2,1)S(1)}, bf16[256,256]{1,0:T(8,128)(2,1)S(1)}, u32[]{:S(2)}, u32[]{:S(2)}) collective-permute-start(bf16[256,256]{1,0:T(8,128)(2,1)S(1)} %fusion.3.refs_1_.refs_7_), channel_id=1, source_target_pairs={{0,4},{1,5},{2,6},{3,7},{4,0},{5,1},{6,2},{7,3},{8,12},{9,13},{10,... | collective-permute-start | bytes 393224 | tf_op jit(solution)/shard_map/ppermute | solution.py:26
  7.8 1.6 %collective-permute-start = (f32[4,256]{1,0:T(4,128)S(1)}, f32[4,256]{1,0:T(4,128)S(1)}, u32[]{:S(2)}, u32[]{:S(2)}) collective-permute-start(f32[4,256]{1,0:T(4,128)S(1)} %get-tuple-element.53), channel_id=1, source_target_pairs={{0,1},{1,0},{2,3},{3,2},{4,5},{5,4},{6,7},{7,6},{8,9},{9,8},{10,11... | collective-permute-start | bytes 12296 | tf_op jit(solution)/shard_map/ppermute | solution.py:26
  9.3 1.6 %collective-permute-start.1 = (f32[4,256]{1,0:T(4,128)S(1)}, f32[4,256]{1,0:T(4,128)S(1)}, u32[]{:S(2)}, u32[]{:S(2)}) collective-permute-start(f32[4,256]{1,0:T(4,128)S(1)} %get-tuple-element.54), channel_id=1, source_target_pairs={{0,2},{1,3},{2,0},{3,1},{4,6},{5,7},{6,4},{7,5},{8,10},{9,11},{10,... | collective-permute-start | bytes 12296 | tf_op jit(solution)/shard_map/ppermute | solution.py:26
  11.3 3.6 %densify.2.refs_6_.refs_1_ = bf16[256,1152]{1,0:T(8,128)(2,1)S(1)} custom-call(s32[3,96]{1,0:T(4,128)S(1)} %pad_add_fusion.words_ref, bf16[1,2,96,128,128]{4,3,2,1,0:T(8,128)(2,1)} %vals_ref.3), custom_call_target="tpu_custom_call" | custom-call | flops 31457280 | bytes 3145728 | tf_op jit(solution)/shard_map/densify/pallas_call | solution.py:71
  16.1 2.2 %collective-permute-start.5 = (bf16[256,256]{1,0:T(8,128)(2,1)S(1)}, bf16[256,256]{1,0:T(8,128)(2,1)S(1)}, u32[]{:S(2)}, u32[]{:S(2)}) collective-permute-start(bf16[256,256]{1,0:T(8,128)(2,1)S(1)} %get-tuple-element.59), channel_id=1, source_target_pairs={{0,2},{1,3},{2,0},{3,1},{4,6},{5,7},{6,4},{7,5},{8,10},{9,11},{10,... | collective-permute-start | bytes 393224 | tf_op jit(solution)/shard_map/ppermute | solution.py:26
  19.4 2.5 %collective-permute-done.4.refs_9_ = bf16[256,256]{1,0:T(8,128)(2,1)S(1)} collective-permute-done((bf16[256,256]{1,0:T(8,128)(2,1)S(1)}, bf16[256,256]{1,0:T(8,128)(2,1)S(1)}, u32[]{:S(2)}, u32[]{:S(2)}) %collective-permute-start.4) | collective-permute-done | bytes 131104 | tf_op jit(solution)/shard_map/ppermute | solution.py:26
  22.0 2.2 %collective-permute-done.6.refs_11_ = bf16[256,256]{1,0:T(8,128)(2,1)S(1)} collective-permute-done((bf16[256,256]{1,0:T(8,128)(2,1)S(1)}, bf16[256,256]{1,0:T(8,128)(2,1)S(1)}, u32[]{:S(2)}, u32[]{:S(2)}) %collective-permute-start.6) | collective-permute-done | bytes 131104 | tf_op jit(solution)/shard_map/ppermute | solution.py:26
  27.0 1.7 %collective-permute-start.12 = (bf16[128,256]{1,0:T(8,128)(2,1)S(1)}, bf16[128,256]{1,0:T(8,128)(2,1)S(1)}, u32[]{:S(2)}, u32[]{:S(2)}) collective-permute-start(bf16[128,256]{1,0:T(8,128)(2,1)S(1)} %get-tuple-element.66), channel_id=1, source_target_pairs={{0,2},{1,3},{2,0},{3,1},{4,6},{5,7},{6,4},{7,5},{8,10},{9,11},{10,... | collective-permute-start | bytes 196616 | tf_op jit(solution)/shard_map/ppermute | solution.py:26
  29.7 2.9 %collective-permute-done.7.refs_0_.refs_3_ = bf16[256,256]{1,0:T(8,128)(2,1)S(1)} collective-permute-done((bf16[256,256]{1,0:T(8,128)(2,1)S(1)}, bf16[256,256]{1,0:T(8,128)(2,1)S(1)}, u32[]{:S(2)}, u32[]{:S(2)}) %collective-permute-start.7) | collective-permute-done | bytes 131104 | tf_op jit(solution)/shard_map/ppermute | solution.py:26
  33.4 2.8 %collective-permute-start.10 = (bf16[128,256]{1,0:T(8,128)(2,1)S(1)}, bf16[128,256]{1,0:T(8,128)(2,1)S(1)}, u32[]{:S(2)}, u32[]{:S(2)}) collective-permute-start(bf16[128,256]{1,0:T(8,128)(2,1)S(1)} %get-tuple-element.64), channel_id=1, source_target_pairs={{0,3},{1,2},{2,1},{3,0},{4,7},{5,6},{6,5},{7,4},{8,11},{9,10},{10,... | collective-permute-start | bytes 196616 | tf_op jit(solution)/shard_map/ppermute | solution.py:26
  36.1 3.3 %densify.3.refs_6_.refs_1_ = bf16[256,1152]{1,0:T(8,128)(2,1)S(1)} custom-call(s32[3,96]{1,0:T(4,128)S(1)} %pad_add_fusion.words_ref, bf16[1,2,96,128,128]{4,3,2,1,0:T(8,128)(2,1)} %vals_ref.3), custom_call_target="tpu_custom_call" | custom-call | flops 31457280 | bytes 3145728 | tf_op jit(solution)/shard_map/densify/pallas_call | solution.py:71
  40.1 3.7 %collective-permute-start.17 = (bf16[128,256]{1,0:T(8,128)(2,1)S(1)}, bf16[128,256]{1,0:T(8,128)(2,1)S(1)}, u32[]{:S(2)}, u32[]{:S(2)}) collective-permute-start(bf16[128,256]{1,0:T(8,128)(2,1)S(1)} %get-tuple-element.76), channel_id=1, source_target_pairs={{0,25},{1,24},{2,27},{3,26},{4,29},{5,28},{6,31},{7,30},{8,1},{9,0... | collective-permute-start | bytes 196616 | tf_op jit(solution)/shard_map/ppermute | solution.py:34
  43.8 2.3 %collective-permute-start.19 = (bf16[128,256]{1,0:T(8,128)(2,1)S(1)}, bf16[128,256]{1,0:T(8,128)(2,1)S(1)}, u32[]{:S(2)}, u32[]{:S(2)}) collective-permute-start(bf16[128,256]{1,0:T(8,128)(2,1)S(1)} %get-tuple-element.78), channel_id=1, source_target_pairs={{0,27},{1,26},{2,25},{3,24},{4,31},{5,30},{6,29},{7,28},{8,3},{9,2... | collective-permute-start | bytes 196616 | tf_op jit(solution)/shard_map/ppermute | solution.py:34
  48.3 2.1 %collective-permute-done.18.refs_10_ = bf16[128,256]{1,0:T(8,128)(2,1)S(1)} collective-permute-done((bf16[128,256]{1,0:T(8,128)(2,1)S(1)}, bf16[128,256]{1,0:T(8,128)(2,1)S(1)}, u32[]{:S(2)}, u32[]{:S(2)}) %collective-permute-start.18) | collective-permute-done | bytes 65568 | tf_op jit(solution)/shard_map/ppermute | solution.py:34
  51.3 1.8 %collective-permute-start.20 = (bf16[128,256]{1,0:T(8,128)(2,1)S(1)}, bf16[128,256]{1,0:T(8,128)(2,1)S(1)}, u32[]{:S(2)}, u32[]{:S(2)}) collective-permute-start(bf16[128,256]{1,0:T(8,128)(2,1)S(1)} %get-tuple-element.83), channel_id=1, source_target_pairs={{0,1},{1,0},{2,3},{3,2},{4,5},{5,4},{6,7},{7,6},{8,9},{9,8},{10,11... | collective-permute-start | bytes 196616 | tf_op jit(solution)/shard_map/ppermute | solution.py:26
  53.1 1.8 %collective-permute-start.22 = (bf16[128,256]{1,0:T(8,128)(2,1)S(1)}, bf16[128,256]{1,0:T(8,128)(2,1)S(1)}, u32[]{:S(2)}, u32[]{:S(2)}) collective-permute-start(bf16[128,256]{1,0:T(8,128)(2,1)S(1)} %get-tuple-element.85), channel_id=1, source_target_pairs={{0,3},{1,2},{2,1},{3,0},{4,7},{5,6},{6,5},{7,4},{8,11},{9,10},{10,... | collective-permute-start | bytes 196616 | tf_op jit(solution)/shard_map/ppermute | solution.py:26
  55.9 1.7 %collective-permute-done.21.refs_13_ = bf16[128,256]{1,0:T(8,128)(2,1)S(1)} collective-permute-done((bf16[128,256]{1,0:T(8,128)(2,1)S(1)}, bf16[128,256]{1,0:T(8,128)(2,1)S(1)}, u32[]{:S(2)}, u32[]{:S(2)}) %collective-permute-start.21) | collective-permute-done | bytes 65568 | tf_op jit(solution)/shard_map/ppermute | solution.py:26
  59.8 2.0 %collective-permute-start.23 = (bf16[256,256]{1,0:T(8,128)(2,1)S(1)}, bf16[256,256]{1,0:T(8,128)(2,1)S(1)}, u32[]{:S(2)}, u32[]{:S(2)}) collective-permute-start(bf16[256,256]{1,0:T(8,128)(2,1)S(1)} %get-tuple-element.90.refs_2_), channel_id=1, source_target_pairs={{0,4},{1,5},{2,6},{3,7},{4,0},{5,1},{6,2},{7,3},{8,12},{9,13},{10,... | collective-permute-start | bytes 393224 | tf_op jit(solution)/shard_map/ppermute | solution.py:26
  63.1 2.2 %collective-permute-start.26 = (bf16[256,256]{1,0:T(8,128)(2,1)S(1)}, bf16[256,256]{1,0:T(8,128)(2,1)S(1)}, u32[]{:S(2)}, u32[]{:S(2)}) collective-permute-start(bf16[256,256]{1,0:T(8,128)(2,1)S(1)} %get-tuple-element.93), channel_id=1, source_target_pairs={{0,3},{1,2},{2,1},{3,0},{4,7},{5,6},{6,5},{7,4},{8,11},{9,10},{10,... | collective-permute-start | bytes 393224 | tf_op jit(solution)/shard_map/ppermute | solution.py:26
  65.4 3.1 %collective-permute-done.23.refs_0_.refs_3_ = bf16[256,256]{1,0:T(8,128)(2,1)S(1)} collective-permute-done((bf16[256,256]{1,0:T(8,128)(2,1)S(1)}, bf16[256,256]{1,0:T(8,128)(2,1)S(1)}, u32[]{:S(2)}, u32[]{:S(2)}) %collective-permute-start.23) | collective-permute-done | bytes 131104 | tf_op jit(solution)/shard_map/ppermute | solution.py:26
  71.3 1.6 %collective-permute-start.30 = (bf16[2,64,256]{2,1,0:T(8,128)(2,1)S(1)}, bf16[2,64,256]{2,1,0:T(8,128)(2,1)S(1)}, u32[]{:S(2)}, u32[]{:S(2)}) collective-permute-start(bf16[2,64,256]{2,1,0:T(8,128)(2,1)S(1)} %half_sum.1.mine_ref), channel_id=1, source_target_pairs={{0,4},{1,5},{2,6},{3,7},{4,0},{5,1},{6,2},{7,3},{8,12},{9,13},{10,... | collective-permute-start | bytes 196616 | tf_op jit(solution)/shard_map/ppermute | solution.py:26
  75.2 1.6 %collective-permute-done.30.far_ref = bf16[2,64,256]{2,1,0:T(8,128)(2,1)S(1)} collective-permute-done((bf16[2,64,256]{2,1,0:T(8,128)(2,1)S(1)}, bf16[2,64,256]{2,1,0:T(8,128)(2,1)S(1)}, u32[]{:S(2)}, u32[]{:S(2)}) %collective-permute-start.30) | collective-permute-done | bytes 65568 | tf_op jit(solution)/shard_map/ppermute | solution.py:26
  76.9 1.7 %collective-permute-start.31 = (bf16[2,64,256]{2,1,0:T(8,128)(2,1)S(1)}, bf16[2,64,256]{2,1,0:T(8,128)(2,1)S(1)}, u32[]{:S(2)}, u32[]{:S(2)}) collective-permute-start(bf16[2,64,256]{2,1,0:T(8,128)(2,1)S(1)} %total.1.refs_0_), channel_id=1, source_target_pairs={{0,1},{1,0},{2,3},{3,2},{4,5},{5,4},{6,7},{7,6},{8,9},{9,8},{10,11... | collective-permute-start | bytes 196616 | tf_op jit(solution)/shard_map/ppermute | solution.py:26
  78.6 1.9 %collective-permute-start.33 = (bf16[2,64,256]{2,1,0:T(8,128)(2,1)S(1)}, bf16[2,64,256]{2,1,0:T(8,128)(2,1)S(1)}, u32[]{:S(2)}, u32[]{:S(2)}) collective-permute-start(bf16[2,64,256]{2,1,0:T(8,128)(2,1)S(1)} %total.1.refs_0_), channel_id=1, source_target_pairs={{0,3},{1,2},{2,1},{3,0},{4,7},{5,6},{6,5},{7,4},{8,11},{9,10},{10,... | collective-permute-start | bytes 196616 | tf_op jit(solution)/shard_map/ppermute | solution.py:26
  (79 shorter events, 27.6 us)
Async XLA Ops:
  2.2 13.2 %collective-permute-start.3 = (bf16[256,256]{1,0:T(8,128)(2,1)S(1)}, bf16[256,256]{1,0:T(8,128)(2,1)S(1)}, u32[]{:S(2)}, u32[]{:S(2)}) collective-permute-start(bf16[256,256]{1,0:T(8,128)(2,1)S(1)} %fusion.3.refs_1_.refs_7_), channel_id=1, source_target_pairs={{0,4},{1,5},{2,6},{3,7},{4,0},{5,1},{6,2},{7,3},{8,12},{9,13},{10,... | collective-permute-start | bytes 393224 | tf_op jit(solution)/shard_map/ppermute | solution.py:26
  7.8 7.2 %collective-permute-start = (f32[4,256]{1,0:T(4,128)S(1)}, f32[4,256]{1,0:T(4,128)S(1)}, u32[]{:S(2)}, u32[]{:S(2)}) collective-permute-start(f32[4,256]{1,0:T(4,128)S(1)} %get-tuple-element.53), channel_id=1, source_target_pairs={{0,1},{1,0},{2,3},{3,2},{4,5},{5,4},{6,7},{7,6},{8,9},{9,8},{10,11... | collective-permute-start | bytes 12296 | tf_op jit(solution)/shard_map/ppermute | solution.py:26
  15.5 6.4 %collective-permute-start.4 = (bf16[256,256]{1,0:T(8,128)(2,1)S(1)}, bf16[256,256]{1,0:T(8,128)(2,1)S(1)}, u32[]{:S(2)}, u32[]{:S(2)}) collective-permute-start(bf16[256,256]{1,0:T(8,128)(2,1)S(1)} %get-tuple-element.58), channel_id=1, source_target_pairs={{0,1},{1,0},{2,3},{3,2},{4,5},{5,4},{6,7},{7,6},{8,9},{9,8},{10,11... | collective-permute-start | bytes 393224 | tf_op jit(solution)/shard_map/ppermute | solution.py:26
  16.1 5.9 %collective-permute-start.5 = (bf16[256,256]{1,0:T(8,128)(2,1)S(1)}, bf16[256,256]{1,0:T(8,128)(2,1)S(1)}, u32[]{:S(2)}, u32[]{:S(2)}) collective-permute-start(bf16[256,256]{1,0:T(8,128)(2,1)S(1)} %get-tuple-element.59), channel_id=1, source_target_pairs={{0,2},{1,3},{2,0},{3,1},{4,6},{5,7},{6,4},{7,5},{8,10},{9,11},{10,... | collective-permute-start | bytes 393224 | tf_op jit(solution)/shard_map/ppermute | solution.py:26
  19.4 20.1 %collective-permute-start.14 = (bf16[528,256]{1,0:T(8,128)(2,1)S(1)}, bf16[528,256]{1,0:T(8,128)(2,1)S(1)}, u32[]{:S(2)}, u32[]{:S(2)}) collective-permute-start(bf16[528,256]{1,0:T(8,128)(2,1)S(1)} %pack.1), channel_id=1, source_target_pairs={{0,8},{8,16},{16,24},{24,0},{1,9},{9,17},{17,25},{25,1},{2,10},{10... | collective-permute-start | bytes 811016 | tf_op jit(solution)/shard_map/ppermute | solution.py:39
  25.2 7.4 %collective-permute-start.7 = (bf16[256,256]{1,0:T(8,128)(2,1)S(1)}, bf16[256,256]{1,0:T(8,128)(2,1)S(1)}, u32[]{:S(2)}, u32[]{:S(2)}) collective-permute-start(bf16[256,256]{1,0:T(8,128)(2,1)S(1)} %get-tuple-element.61.refs_2_), channel_id=1, source_target_pairs={{0,4},{1,5},{2,6},{3,7},{4,0},{5,1},{6,2},{7,3},{8,12},{9,13},{10,... | collective-permute-start | bytes 393224 | tf_op jit(solution)/shard_map/ppermute | solution.py:26
  26.2 7.1 %collective-permute-start.11 = (bf16[128,256]{1,0:T(8,128)(2,1)S(1)}, bf16[128,256]{1,0:T(8,128)(2,1)S(1)}, u32[]{:S(2)}, u32[]{:S(2)}) collective-permute-start(bf16[128,256]{1,0:T(8,128)(2,1)S(1)} %get-tuple-element.65), channel_id=1, source_target_pairs={{0,1},{1,0},{2,3},{3,2},{4,5},{5,4},{6,7},{7,6},{8,9},{9,8},{10,11... | collective-permute-start | bytes 196616 | tf_op jit(solution)/shard_map/ppermute | solution.py:26
  27.0 6.3 %collective-permute-start.12 = (bf16[128,256]{1,0:T(8,128)(2,1)S(1)}, bf16[128,256]{1,0:T(8,128)(2,1)S(1)}, u32[]{:S(2)}, u32[]{:S(2)}) collective-permute-start(bf16[128,256]{1,0:T(8,128)(2,1)S(1)} %get-tuple-element.66), channel_id=1, source_target_pairs={{0,2},{1,3},{2,0},{3,1},{4,6},{5,7},{6,4},{7,5},{8,10},{9,11},{10,... | collective-permute-start | bytes 196616 | tf_op jit(solution)/shard_map/ppermute | solution.py:26
  28.8 7.4 %collective-permute-start.13 = (bf16[128,256]{1,0:T(8,128)(2,1)S(1)}, bf16[128,256]{1,0:T(8,128)(2,1)S(1)}, u32[]{:S(2)}, u32[]{:S(2)}) collective-permute-start(bf16[128,256]{1,0:T(8,128)(2,1)S(1)} %get-tuple-element.67), channel_id=1, source_target_pairs={{0,3},{1,2},{2,1},{3,0},{4,7},{5,6},{6,5},{7,4},{8,11},{9,10},{10,... | collective-permute-start | bytes 196616 | tf_op jit(solution)/shard_map/ppermute | solution.py:26
  32.6 6.9 %collective-permute-start.8 = (bf16[128,256]{1,0:T(8,128)(2,1)S(1)}, bf16[128,256]{1,0:T(8,128)(2,1)S(1)}, u32[]{:S(2)}, u32[]{:S(2)}) collective-permute-start(bf16[128,256]{1,0:T(8,128)(2,1)S(1)} %get-tuple-element.62), channel_id=1, source_target_pairs={{0,1},{1,0},{2,3},{3,2},{4,5},{5,4},{6,7},{7,6},{8,9},{9,8},{10,11... | collective-permute-start | bytes 196616 | tf_op jit(solution)/shard_map/ppermute | solution.py:26
  33.3 6.1 %collective-permute-start.9 = (bf16[128,256]{1,0:T(8,128)(2,1)S(1)}, bf16[128,256]{1,0:T(8,128)(2,1)S(1)}, u32[]{:S(2)}, u32[]{:S(2)}) collective-permute-start(bf16[128,256]{1,0:T(8,128)(2,1)S(1)} %get-tuple-element.63), channel_id=1, source_target_pairs={{0,2},{1,3},{2,0},{3,1},{4,6},{5,7},{6,4},{7,5},{8,10},{9,11},{10,... | collective-permute-start | bytes 196616 | tf_op jit(solution)/shard_map/ppermute | solution.py:26
  33.4 6.1 %collective-permute-start.10 = (bf16[128,256]{1,0:T(8,128)(2,1)S(1)}, bf16[128,256]{1,0:T(8,128)(2,1)S(1)}, u32[]{:S(2)}, u32[]{:S(2)}) collective-permute-start(bf16[128,256]{1,0:T(8,128)(2,1)S(1)} %get-tuple-element.64), channel_id=1, source_target_pairs={{0,3},{1,2},{2,1},{3,0},{4,7},{5,6},{6,5},{7,4},{8,11},{9,10},{10,... | collective-permute-start | bytes 196616 | tf_op jit(solution)/shard_map/ppermute | solution.py:26
  40.0 11.3 %collective-permute-start.16 = (bf16[256,256]{1,0:T(8,128)(2,1)S(1)}, bf16[256,256]{1,0:T(8,128)(2,1)S(1)}, u32[]{:S(2)}, u32[]{:S(2)}) collective-permute-start(bf16[256,256]{1,0:T(8,128)(2,1)S(1)} %get-tuple-element.75), channel_id=1, source_target_pairs={{0,28},{1,29},{2,30},{3,31},{4,24},{5,25},{6,26},{7,27},{8,4},{9,5... | collective-permute-start | bytes 393224 | tf_op jit(solution)/shard_map/ppermute | solution.py:34
  40.1 8.2 %collective-permute-start.17 = (bf16[128,256]{1,0:T(8,128)(2,1)S(1)}, bf16[128,256]{1,0:T(8,128)(2,1)S(1)}, u32[]{:S(2)}, u32[]{:S(2)}) collective-permute-start(bf16[128,256]{1,0:T(8,128)(2,1)S(1)} %get-tuple-element.76), channel_id=1, source_target_pairs={{0,25},{1,24},{2,27},{3,26},{4,29},{5,28},{6,31},{7,30},{8,1},{9,0... | collective-permute-start | bytes 196616 | tf_op jit(solution)/shard_map/ppermute | solution.py:34
  43.8 6.6 %collective-permute-start.18 = (bf16[128,256]{1,0:T(8,128)(2,1)S(1)}, bf16[128,256]{1,0:T(8,128)(2,1)S(1)}, u32[]{:S(2)}, u32[]{:S(2)}) collective-permute-start(bf16[128,256]{1,0:T(8,128)(2,1)S(1)} %get-tuple-element.77), channel_id=1, source_target_pairs={{0,26},{1,27},{2,24},{3,25},{4,30},{5,31},{6,28},{7,29},{8,2},{9,3... | collective-permute-start | bytes 196616 | tf_op jit(solution)/shard_map/ppermute | solution.py:34
  43.8 7.5 %collective-permute-start.19 = (bf16[128,256]{1,0:T(8,128)(2,1)S(1)}, bf16[128,256]{1,0:T(8,128)(2,1)S(1)}, u32[]{:S(2)}, u32[]{:S(2)}) collective-permute-start(bf16[128,256]{1,0:T(8,128)(2,1)S(1)} %get-tuple-element.78), channel_id=1, source_target_pairs={{0,27},{1,26},{2,25},{3,24},{4,31},{5,30},{6,29},{7,28},{8,3},{9,2... | collective-permute-start | bytes 196616 | tf_op jit(solution)/shard_map/ppermute | solution.py:34
  48.2 6.9 %collective-permute-start.15 = (bf16[256,256]{1,0:T(8,128)(2,1)S(1)}, bf16[256,256]{1,0:T(8,128)(2,1)S(1)}, u32[]{:S(2)}, u32[]{:S(2)}) collective-permute-start(bf16[256,256]{1,0:T(8,128)(2,1)S(1)} %get-tuple-element.73.refs_10_), channel_id=1, source_target_pairs={{0,24},{1,25},{2,26},{3,27},{4,28},{5,29},{6,30},{7,31},{8,0},{9,1... | collective-permute-start | bytes 393224 | tf_op jit(solution)/shard_map/ppermute | solution.py:34
  59.8 8.7 %collective-permute-start.23 = (bf16[256,256]{1,0:T(8,128)(2,1)S(1)}, bf16[256,256]{1,0:T(8,128)(2,1)S(1)}, u32[]{:S(2)}, u32[]{:S(2)}) collective-permute-start(bf16[256,256]{1,0:T(8,128)(2,1)S(1)} %get-tuple-element.90.refs_2_), channel_id=1, source_target_pairs={{0,4},{1,5},{2,6},{3,7},{4,0},{5,1},{6,2},{7,3},{8,12},{9,13},{10,... | collective-permute-start | bytes 393224 | tf_op jit(solution)/shard_map/ppermute | solution.py:26
  61.8 7.3 %collective-permute-start.24 = (bf16[256,256]{1,0:T(8,128)(2,1)S(1)}, bf16[256,256]{1,0:T(8,128)(2,1)S(1)}, u32[]{:S(2)}, u32[]{:S(2)}) collective-permute-start(bf16[256,256]{1,0:T(8,128)(2,1)S(1)} %get-tuple-element.91), channel_id=1, source_target_pairs={{0,1},{1,0},{2,3},{3,2},{4,5},{5,4},{6,7},{7,6},{8,9},{9,8},{10,11... | collective-permute-start | bytes 393224 | tf_op jit(solution)/shard_map/ppermute | solution.py:26
  62.2 7.7 %collective-permute-start.25 = (bf16[256,256]{1,0:T(8,128)(2,1)S(1)}, bf16[256,256]{1,0:T(8,128)(2,1)S(1)}, u32[]{:S(2)}, u32[]{:S(2)}) collective-permute-start(bf16[256,256]{1,0:T(8,128)(2,1)S(1)} %get-tuple-element.92), channel_id=1, source_target_pairs={{0,2},{1,3},{2,0},{3,1},{4,6},{5,7},{6,4},{7,5},{8,10},{9,11},{10,... | collective-permute-start | bytes 393224 | tf_op jit(solution)/shard_map/ppermute | solution.py:26
  63.1 8.2 %collective-permute-start.26 = (bf16[256,256]{1,0:T(8,128)(2,1)S(1)}, bf16[256,256]{1,0:T(8,128)(2,1)S(1)}, u32[]{:S(2)}, u32[]{:S(2)}) collective-permute-start(bf16[256,256]{1,0:T(8,128)(2,1)S(1)} %get-tuple-element.93), channel_id=1, source_target_pairs={{0,3},{1,2},{2,1},{3,0},{4,7},{5,6},{6,5},{7,4},{8,11},{9,10},{10,... | collective-permute-start | bytes 393224 | tf_op jit(solution)/shard_map/ppermute | solution.py:26
  68.5 10.0 %collective-permute-start.27 = (bf16[128,256]{1,0:T(8,128)(2,1)S(1)}, bf16[128,256]{1,0:T(8,128)(2,1)S(1)}, u32[]{:S(2)}, u32[]{:S(2)}) collective-permute-start(bf16[128,256]{1,0:T(8,128)(2,1)S(1)} %get-tuple-element.94), channel_id=1, source_target_pairs={{0,1},{1,0},{2,3},{3,2},{4,5},{5,4},{6,7},{7,6},{8,9},{9,8},{10,11... | collective-permute-start | bytes 196616 | tf_op jit(solution)/shard_map/ppermute | solution.py:26
  73.0 8.3 %collective-permute-start.28 = (bf16[128,256]{1,0:T(8,128)(2,1)S(1)}, bf16[128,256]{1,0:T(8,128)(2,1)S(1)}, u32[]{:S(2)}, u32[]{:S(2)}) collective-permute-start(bf16[128,256]{1,0:T(8,128)(2,1)S(1)} %get-tuple-element.95), channel_id=1, source_target_pairs={{0,2},{1,3},{2,0},{3,1},{4,6},{5,7},{6,4},{7,5},{8,10},{9,11},{10,... | collective-permute-start | bytes 196616 | tf_op jit(solution)/shard_map/ppermute | solution.py:26
  74.0 7.3 %collective-permute-start.29 = (bf16[128,256]{1,0:T(8,128)(2,1)S(1)}, bf16[128,256]{1,0:T(8,128)(2,1)S(1)}, u32[]{:S(2)}, u32[]{:S(2)}) collective-permute-start(bf16[128,256]{1,0:T(8,128)(2,1)S(1)} %get-tuple-element.96), channel_id=1, source_target_pairs={{0,3},{1,2},{2,1},{3,0},{4,7},{5,6},{6,5},{7,4},{8,11},{9,10},{10,... | collective-permute-start | bytes 196616 | tf_op jit(solution)/shard_map/ppermute | solution.py:26
  (15 other events, 174.7 us)

commit v14 on v13

--- a/solution.py
+++ b/solution.py
@@ -84,9 +84,8 @@
 def packed(tile_row, tile_col, tile_count, row_tiles):
     owner = jnp.bitwise_xor(tile_col // row_tiles, lax.axis_index("rows"))
     words = (owner * row_tiles + tile_col % row_tiles) * row_tiles + tile_row
-    counts = tile_count.reshape(1, -1)
-    counts = jnp.pad(counts, ((0, 0), (0, words.shape[2] - counts.shape[1])))
-    return jnp.concatenate([words[0], counts], axis=0)
+    live = lax.broadcasted_iota(jnp.int32, words.shape, 2) < tile_count
+    return jnp.where(live, words, -1)[0]
 
 
 def densify_kernel(tick, row_tiles, n, chunks, words_ref, vals_ref, out_ref, vals, acc, sems):
@@ -101,7 +100,7 @@
         copies[c].start()
     acc[...] = jnp.zeros_like(acc)
 
-    def add(e, carry):
+    def add(e):
         word = words_ref[tick, e]
         row = lax.rem(word, row_tiles)
         block = lax.rem(lax.div(word, row_tiles), row_tiles)
@@ -110,13 +109,16 @@
         rows = pl.ds(pl.multiple_of(row * tile, tile), tile)
         cols = pl.ds(pl.multiple_of(slot * tile, tile), tile)
         acc[rows, cols] += vals[e].astype(F32)
-        return carry
-
-    count = words_ref[words_ref.shape[0] - 1, tick]
+
     for c in range(chunks):
         copies[c].wait()
-        stop = jnp.clip(count, c * chunk, (c + 1) * chunk)
-        lax.fori_loop(c * chunk, stop, add, 0)
+
+        @pl.loop(c * chunk, (c + 1) * chunk)
+        def _(e):
+            @pl.when(words_ref[tick, e] >= 0)
+            def _():
+                add(e)
+
     out_ref[...] = acc[...].astype(BF16)
 
 
@@ -149,7 +151,8 @@
 def name_kernel(n, row_tiles, words_ref, *out_refs):
     ticks, width = out_refs[0].shape
     for t in range(ticks):
-        index = words_ref[t : t + 1, :] // row_tiles
+        words = words_ref[t : t + 1, :]
+        index = jnp.where(words < 0, -1, words // row_tiles)
 
         def named(k):
             block = index - k * row_tiles
@@ -239,23 +242,13 @@
     sends = [] if c["entry"] else refs.take(h - 1)
     parts = refs.take(h - 1) if c["final"] and c["layer"] else []
     out_ref = refs.take()
-    preact_ref, weight_ref, load_sems = refs.take(3)
-
+    if c["final"]:
+        term_ref = refs.take()
+    preact_ref = preact_all.at[0, c["tick"], c["layer"]]
+    weight_ref = weight_all.at[0, c["layer"]]
     section = lax.axis_index("section")
-    loads = [
-        (preact_all.at[0, c["tick"], c["layer"]], preact_ref),
-        (weight_all.at[0, c["layer"]], weight_ref),
-    ]
-    if c["final"]:
-        support_ref, term_ref = refs.take(2)
-        loads.append((support_all.at[0, c["tick"], c["layer"]], support_ref))
-    loads = [pltpu.make_async_copy(a, b, load_sems.at[i]) for i, (a, b) in enumerate(loads)]
-    for load in loads:
-        load.start()
     if not c["entry"]:
         grad = spread_of(adj_ref, own_ref, got, names_ref, c)
-    for load in loads:
-        load.wait()
     if c["entry"]:
         grad = jnp.where(section == c["sections"] - 1, last_ref[...], passed_ref[...])
 
@@ -269,7 +262,10 @@
             send[:tile, :] = chosen(image_ref, row, c["rows"], tile)
     if c["final"]:
         term = lax.dot_general(
-            support_ref[...], masked, (((0,), (0,)), ((), ())), preferred_element_type=F32
+            support_all[0, c["tick"], c["layer"]],
+            masked,
+            (((0,), (0,)), ((), ())),
+            preferred_element_type=F32,
         )
         term_ref[...] = acc_ref[...] + beta * term
         place = lax.rem(lax.axis_index("rows"), h)
@@ -427,15 +423,13 @@
                 image = ((1.0 - beta) * masked.astype(F32) + beta * product).astype(BF16)
             else:
                 call = Call()
-                call.give(HBM, preact, weights)
-                call.give(VMEM, names, *asked)
+                call.give(VMEM, preact, weights, names, *asked)
                 if entry:
                     call.give(VMEM, grad_last, passed)
                 else:
                     call.give(VMEM, adjs[tick], image, *got)
                 if final:
-                    call.give(HBM, support)
-                    call.give(VMEM, weight_acc[layer])
+                    call.give(VMEM, support, weight_acc[layer])
                     if layer == 0:
                         call.give(VMEM, *pending)
                 call.want(VMEM, (rows, width), BF16)
@@ -448,14 +442,8 @@
                     call.want(VMEM, (chunk, width), F32)
                 else:
                     call.want(VMEM, (rows, width), BF16)
-                call.scratch = [
-                    pltpu.VMEM((rows, width), BF16),
-                    pltpu.VMEM((width, width), BF16),
-                    pltpu.SemaphoreType.DMA((3,)),
-                ]
                 if final:
-                    call.scratch.append(pltpu.VMEM((rows, width), BF16))
-                    call.scratch.append(pltpu.VMEM((width, width), F32))
+                    call.scratch = [pltpu.VMEM((width, width), F32)]
                 results = Refs(
                     call.run(
                         functools.partial(layer_kernel, c),
@@ -490,8 +478,8 @@
             call.want(VMEM, (tile * (1 + c["first"]), width), BF16, h - 1)
             relays = call.run(functools.partial(forward_kernel, c), "forward", small_cost)
             relayed = shared(relays)
-            if layer == 0 and not final:
-                later, *_ = lax.optimization_barrier((words, *near))
+            if entry and not final:
+                later, _ = lax.optimization_barrier((words, relays))
                 adjs[tick + 1] = densify(tick + 1, later, tile_vals, row_tiles, n)
                 relayed, adjs[tick + 1] = lax.optimization_barrier((relayed, adjs[tick + 1]))
             if final:

time: 84.8 us -> 86.3 us (1.018)
  waiting for transfers between devices: 22 us -> 25.8 us
  starting transfers between devices: 42.5 us -> 41.3 us
    ppermute x28, waiting for transfers between devices: 19 us -> 22.8 us  [swapped(): return lax.ppermute(block, 'rows', [(i, i ^ k) for i in range(n)])]
    ppermute x28, starting transfers between devices: 36.3 us -> 34.9 us  [swapped(): return lax.ppermute(block, 'rows', [(i, i ^ k) for i in range(n)])]
  transfers between devices with their start and end apart: 34 -> 34, of which waited for: 15 -> 14; matrix products, arithmetic and copies ran while one was open for 5% -> 4% of each run, Pallas kernels for 12% -> 13%
where the time goes in v14:
time: 86.3 us; the launch traced here: 86.8 us
  starting transfers between devices  41.3 us (48%)
  waiting for transfers between devices  25.8 us (30%)
  Pallas kernels  13.2 us (15%)
  matrix products  2.6 us (3%)
  other arithmetic  1.67 us (2%)
  between operations  1.11 us (1%)
  local copies, waits for them, and re-layouts  1.1 us (1%)
    ppermute x28, starting transfers between devices, swapped(): return lax.ppermute(block, 'rows', [(i, i ^ k) for i in range(n)])  34.9 us
    ppermute x28, waiting for transfers between devices, swapped(): return lax.ppermute(block, 'rows', [(i, i ^ k) for i in range(n)])  22.8 us
    pallas_call x16, Pallas kernels, run(): pl.pallas_call(kernel, out_shape=self.outs, in_specs=self.specs, out_spec...  13.2 us
    ppermute x5, starting transfers between devices, lowered(): return lax.ppermute(block, ('section', 'rows'), route)  6.36 us
    ppermute x5, waiting for transfers between devices, lowered(): return lax.ppermute(block, ('section', 'rows'), route)  2.91 us
  transfers between devices with their start and end apart: 34, of which 14 were waited for; matrix products, arithmetic and copies ran while one was open for 4% of the time, Pallas kernels for 13%

profile of v14, /device:TPU:0, one launch (start us, length us, event | category | flops | bytes accessed | tf_op | source)
XLA Modules:
  0.0 86.8 jit_solution(13268824270538889550)
XLA Ops:
  0.7 1.4 %fusion.3.refs_1_.refs_7_ = bf16[256,256]{1,0:T(8,128)(2,1)S(1)} fusion(bf16[1,256,256]{2,1,0:T(8,128)(2,1)} %param.9, bf16[1,2,256,256]{3,2,1,0:T(8,128)(2,1)} %refs_1_.5, f32[]{:T(128)S(6)} %log.6, f32[]{:T(128)S(6)} %sub.10, bf16[1,2,2,256,256]{4,3,2,1,0:T(8,128)(2,1)} %refs_0_.5), kind=kOutput, calls=%fused_computation.6 | convolution fusion | flops 34144256 | bytes 786440 | tf_op jit(solution)/shard_map/dot_general | solution.py:422
  2.2 4.1 %collective-permute-start = (bf16[256,256]{1,0:T(8,128)(2,1)S(1)}, bf16[256,256]{1,0:T(8,128)(2,1)S(1)}, u32[]{:S(2)}, u32[]{:S(2)}) collective-permute-start(bf16[256,256]{1,0:T(8,128)(2,1)S(1)} %fusion.3.refs_1_.refs_7_), channel_id=1, source_target_pairs={{0,4},{1,5},{2,6},{3,7},{4,0},{5,1},{6,2},{7,3},{8,12},{9,13},{10,... | collective-permute-start | bytes 393224 | tf_op jit(solution)/shard_map/ppermute | solution.py:26
  7.2 1.6 %collective-permute-start.1 = (f32[4,256]{1,0:T(4,128)S(1)}, f32[4,256]{1,0:T(4,128)S(1)}, u32[]{:S(2)}, u32[]{:S(2)}) collective-permute-start(f32[4,256]{1,0:T(4,128)S(1)} %get-tuple-element.54), channel_id=1, source_target_pairs={{0,1},{1,0},{2,3},{3,2},{4,5},{5,4},{6,7},{7,6},{8,9},{9,8},{10,11... | collective-permute-start | bytes 12296 | tf_op jit(solution)/shard_map/ppermute | solution.py:26
  8.7 1.6 %collective-permute-start.2 = (f32[4,256]{1,0:T(4,128)S(1)}, f32[4,256]{1,0:T(4,128)S(1)}, u32[]{:S(2)}, u32[]{:S(2)}) collective-permute-start(f32[4,256]{1,0:T(4,128)S(1)} %get-tuple-element.55), channel_id=1, source_target_pairs={{0,2},{1,3},{2,0},{3,1},{4,6},{5,7},{6,4},{7,5},{8,10},{9,11},{10,... | collective-permute-start | bytes 12296 | tf_op jit(solution)/shard_map/ppermute | solution.py:26
  10.7 4.1 %densify.2.refs_6_.refs_1_ = bf16[256,1152]{1,0:T(8,128)(2,1)S(1)} custom-call(s32[2,96]{1,0:T(2,128)S(1)} %fusion.15.words_ref, bf16[1,2,96,128,128]{4,3,2,1,0:T(8,128)(2,1)} %vals_ref.3), custom_call_target="tpu_custom_call" | custom-call | flops 31457280 | bytes 3145728 | tf_op jit(solution)/shard_map/densify/pallas_call | solution.py:71
  15.0 1.7 %collective-permute-start.4 = (bf16[256,256]{1,0:T(8,128)(2,1)S(1)}, bf16[256,256]{1,0:T(8,128)(2,1)S(1)}, u32[]{:S(2)}, u32[]{:S(2)}) collective-permute-start(bf16[256,256]{1,0:T(8,128)(2,1)S(1)} %get-tuple-element.57), channel_id=1, source_target_pairs={{0,1},{1,0},{2,3},{3,2},{4,5},{5,4},{6,7},{7,6},{8,9},{9,8},{10,11... | collective-permute-start | bytes 393224 | tf_op jit(solution)/shard_map/ppermute | solution.py:26
  16.7 1.8 %collective-permute-start.5 = (bf16[256,256]{1,0:T(8,128)(2,1)S(1)}, bf16[256,256]{1,0:T(8,128)(2,1)S(1)}, u32[]{:S(2)}, u32[]{:S(2)}) collective-permute-start(bf16[256,256]{1,0:T(8,128)(2,1)S(1)} %get-tuple-element.58), channel_id=1, source_target_pairs={{0,2},{1,3},{2,0},{3,1},{4,6},{5,7},{6,4},{7,5},{8,10},{9,11},{10,... | collective-permute-start | bytes 393224 | tf_op jit(solution)/shard_map/ppermute | solution.py:26
  18.9 4.7 %densify.3.refs_6_.refs_1_ = bf16[256,1152]{1,0:T(8,128)(2,1)S(1)} custom-call(s32[2,96]{1,0:T(2,128)S(1)} %fusion.15.words_ref, bf16[1,2,96,128,128]{4,3,2,1,0:T(8,128)(2,1)} %vals_ref.3), custom_call_target="tpu_custom_call" | custom-call | flops 31457280 | bytes 3145728 | tf_op jit(solution)/shard_map/densify/pallas_call | solution.py:71
  25.2 1.5 %collective-permute-start.8 = (bf16[128,256]{1,0:T(8,128)(2,1)S(1)}, bf16[128,256]{1,0:T(8,128)(2,1)S(1)}, u32[]{:S(2)}, u32[]{:S(2)}) collective-permute-start(bf16[128,256]{1,0:T(8,128)(2,1)S(1)} %get-tuple-element.67), channel_id=1, source_target_pairs={{0,1},{1,0},{2,3},{3,2},{4,5},{5,4},{6,7},{7,6},{8,9},{9,8},{10,11... | collective-permute-start | bytes 196616 | tf_op jit(solution)/shard_map/ppermute | solution.py:26
  26.7 1.6 %collective-permute-start.9 = (bf16[128,256]{1,0:T(8,128)(2,1)S(1)}, bf16[128,256]{1,0:T(8,128)(2,1)S(1)}, u32[]{:S(2)}, u32[]{:S(2)}) collective-permute-start(bf16[128,256]{1,0:T(8,128)(2,1)S(1)} %get-tuple-element.68), channel_id=1, source_target_pairs={{0,2},{1,3},{2,0},{3,1},{4,6},{5,7},{6,4},{7,5},{8,10},{9,11},{10,... | collective-permute-start | bytes 196616 | tf_op jit(solution)/shard_map/ppermute | solution.py:26
  28.7 5.9 %collective-permute-done.7.refs_0_.refs_3_ = bf16[256,256]{1,0:T(8,128)(2,1)S(1)} collective-permute-done((bf16[256,256]{1,0:T(8,128)(2,1)S(1)}, bf16[256,256]{1,0:T(8,128)(2,1)S(1)}, u32[]{:S(2)}, u32[]{:S(2)}) %collective-permute-start.7) | collective-permute-done | bytes 131104 | tf_op jit(solution)/shard_map/ppermute | solution.py:26
  35.7 2.5 %collective-permute-start.13 = (bf16[128,256]{1,0:T(8,128)(2,1)S(1)}, bf16[128,256]{1,0:T(8,128)(2,1)S(1)}, u32[]{:S(2)}, u32[]{:S(2)}) collective-permute-start(bf16[128,256]{1,0:T(8,128)(2,1)S(1)} %get-tuple-element.72), channel_id=1, source_target_pairs={{0,3},{1,2},{2,1},{3,0},{4,7},{5,6},{6,5},{7,4},{8,11},{9,10},{10,... | collective-permute-start | bytes 196616 | tf_op jit(solution)/shard_map/ppermute | solution.py:26
  42.4 2.0 %collective-permute-start.17 = (bf16[128,256]{1,0:T(8,128)(2,1)S(1)}, bf16[128,256]{1,0:T(8,128)(2,1)S(1)}, u32[]{:S(2)}, u32[]{:S(2)}) collective-permute-start(bf16[128,256]{1,0:T(8,128)(2,1)S(1)} %get-tuple-element.76), channel_id=1, source_target_pairs={{0,25},{1,24},{2,27},{3,26},{4,29},{5,28},{6,31},{7,30},{8,1},{9,0... | collective-permute-start | bytes 196616 | tf_op jit(solution)/shard_map/ppermute | solution.py:34
  44.5 3.5 %collective-permute-start.19 = (bf16[128,256]{1,0:T(8,128)(2,1)S(1)}, bf16[128,256]{1,0:T(8,128)(2,1)S(1)}, u32[]{:S(2)}, u32[]{:S(2)}) collective-permute-start(bf16[128,256]{1,0:T(8,128)(2,1)S(1)} %get-tuple-element.78), channel_id=1, source_target_pairs={{0,27},{1,26},{2,25},{3,24},{4,31},{5,30},{6,29},{7,28},{8,3},{9,2... | collective-permute-start | bytes 196616 | tf_op jit(solution)/shard_map/ppermute | solution.py:34
  50.2 2.9 %collective-permute-done.19.refs_11_ = bf16[128,256]{1,0:T(8,128)(2,1)S(1)} collective-permute-done((bf16[128,256]{1,0:T(8,128)(2,1)S(1)}, bf16[128,256]{1,0:T(8,128)(2,1)S(1)}, u32[]{:S(2)}, u32[]{:S(2)}) %collective-permute-start.19) | collective-permute-done | bytes 65568 | tf_op jit(solution)/shard_map/ppermute | solution.py:34
  54.0 2.7 %collective-permute-start.22 = (bf16[128,256]{1,0:T(8,128)(2,1)S(1)}, bf16[128,256]{1,0:T(8,128)(2,1)S(1)}, u32[]{:S(2)}, u32[]{:S(2)}) collective-permute-start(bf16[128,256]{1,0:T(8,128)(2,1)S(1)} %get-tuple-element.85), channel_id=1, source_target_pairs={{0,3},{1,2},{2,1},{3,0},{4,7},{5,6},{6,5},{7,4},{8,11},{9,10},{10,... | collective-permute-start | bytes 196616 | tf_op jit(solution)/shard_map/ppermute | solution.py:26
  57.5 1.4 %collective-permute-done.21.refs_13_ = bf16[128,256]{1,0:T(8,128)(2,1)S(1)} collective-permute-done((bf16[128,256]{1,0:T(8,128)(2,1)S(1)}, bf16[128,256]{1,0:T(8,128)(2,1)S(1)}, u32[]{:S(2)}, u32[]{:S(2)}) %collective-permute-start.21) | collective-permute-done | bytes 65568 | tf_op jit(solution)/shard_map/ppermute | solution.py:26
  58.9 1.4 %collective-permute-done.22.refs_14_ = bf16[128,256]{1,0:T(8,128)(2,1)S(1)} collective-permute-done((bf16[128,256]{1,0:T(8,128)(2,1)S(1)}, bf16[128,256]{1,0:T(8,128)(2,1)S(1)}, u32[]{:S(2)}, u32[]{:S(2)}) %collective-permute-start.22) | collective-permute-done | bytes 65568 | tf_op jit(solution)/shard_map/ppermute | solution.py:26
  62.3 1.6 %collective-permute-start.24 = (bf16[256,256]{1,0:T(8,128)(2,1)S(1)}, bf16[256,256]{1,0:T(8,128)(2,1)S(1)}, u32[]{:S(2)}, u32[]{:S(2)}) collective-permute-start(bf16[256,256]{1,0:T(8,128)(2,1)S(1)} %get-tuple-element.91), channel_id=1, source_target_pairs={{0,1},{1,0},{2,3},{3,2},{4,5},{5,4},{6,7},{7,6},{8,9},{9,8},{10,11... | collective-permute-start | bytes 393224 | tf_op jit(solution)/shard_map/ppermute | solution.py:26
  65.9 4.0 %collective-permute-done.23.refs_0_.refs_3_ = bf16[256,256]{1,0:T(8,128)(2,1)S(1)} collective-permute-done((bf16[256,256]{1,0:T(8,128)(2,1)S(1)}, bf16[256,256]{1,0:T(8,128)(2,1)S(1)}, u32[]{:S(2)}, u32[]{:S(2)}) %collective-permute-start.23) | collective-permute-done | bytes 131104 | tf_op jit(solution)/shard_map/ppermute | solution.py:26
  71.2 2.2 %collective-permute-done.26.refs_6_.refs_4_ = bf16[256,256]{1,0:T(8,128)(2,1)S(1)} collective-permute-done((bf16[256,256]{1,0:T(8,128)(2,1)S(1)}, bf16[256,256]{1,0:T(8,128)(2,1)S(1)}, u32[]{:S(2)}, u32[]{:S(2)}) %collective-permute-start.26) | collective-permute-done | bytes 131104 | tf_op jit(solution)/shard_map/ppermute | solution.py:26
  74.3 2.7 %collective-permute-start.28 = (bf16[128,256]{1,0:T(8,128)(2,1)S(1)}, bf16[128,256]{1,0:T(8,128)(2,1)S(1)}, u32[]{:S(2)}, u32[]{:S(2)}) collective-permute-start(bf16[128,256]{1,0:T(8,128)(2,1)S(1)} %get-tuple-element.95), channel_id=1, source_target_pairs={{0,2},{1,3},{2,0},{3,1},{4,6},{5,7},{6,4},{7,5},{8,10},{9,11},{10,... | collective-permute-start | bytes 196616 | tf_op jit(solution)/shard_map/ppermute | solution.py:26
  77.3 2.1 %collective-permute-done.30.far_ref = bf16[2,64,256]{2,1,0:T(8,128)(2,1)S(1)} collective-permute-done((bf16[2,64,256]{2,1,0:T(8,128)(2,1)S(1)}, bf16[2,64,256]{2,1,0:T(8,128)(2,1)S(1)}, u32[]{:S(2)}, u32[]{:S(2)}) %collective-permute-start.30) | collective-permute-done | bytes 65568 | tf_op jit(solution)/shard_map/ppermute | solution.py:26
  80.6 2.4 %collective-permute-start.33 = (bf16[2,64,256]{2,1,0:T(8,128)(2,1)S(1)}, bf16[2,64,256]{2,1,0:T(8,128)(2,1)S(1)}, u32[]{:S(2)}, u32[]{:S(2)}) collective-permute-start(bf16[2,64,256]{2,1,0:T(8,128)(2,1)S(1)} %total.1.refs_0_), channel_id=1, source_target_pairs={{0,3},{1,2},{2,1},{3,0},{4,7},{5,6},{6,5},{7,4},{8,11},{9,10},{10,... | collective-permute-start | bytes 196616 | tf_op jit(solution)/shard_map/ppermute | solution.py:26
  (78 shorter events, 24.2 us)
Async XLA Ops:
  2.2 12.7 %collective-permute-start = (bf16[256,256]{1,0:T(8,128)(2,1)S(1)}, bf16[256,256]{1,0:T(8,128)(2,1)S(1)}, u32[]{:S(2)}, u32[]{:S(2)}) collective-permute-start(bf16[256,256]{1,0:T(8,128)(2,1)S(1)} %fusion.3.refs_1_.refs_7_), channel_id=1, source_target_pairs={{0,4},{1,5},{2,6},{3,7},{4,0},{5,1},{6,2},{7,3},{8,12},{9,13},{10,... | collective-permute-start | bytes 393224 | tf_op jit(solution)/shard_map/ppermute | solution.py:26
  7.2 7.7 %collective-permute-start.1 = (f32[4,256]{1,0:T(4,128)S(1)}, f32[4,256]{1,0:T(4,128)S(1)}, u32[]{:S(2)}, u32[]{:S(2)}) collective-permute-start(f32[4,256]{1,0:T(4,128)S(1)} %get-tuple-element.54), channel_id=1, source_target_pairs={{0,1},{1,0},{2,3},{3,2},{4,5},{5,4},{6,7},{7,6},{8,9},{9,8},{10,11... | collective-permute-start | bytes 12296 | tf_op jit(solution)/shard_map/ppermute | solution.py:26
  8.7 6.2 %collective-permute-start.2 = (f32[4,256]{1,0:T(4,128)S(1)}, f32[4,256]{1,0:T(4,128)S(1)}, u32[]{:S(2)}, u32[]{:S(2)}) collective-permute-start(f32[4,256]{1,0:T(4,128)S(1)} %get-tuple-element.55), channel_id=1, source_target_pairs={{0,2},{1,3},{2,0},{3,1},{4,6},{5,7},{6,4},{7,5},{8,10},{9,11},{10,... | collective-permute-start | bytes 12296 | tf_op jit(solution)/shard_map/ppermute | solution.py:26
  15.0 8.7 %collective-permute-start.4 = (bf16[256,256]{1,0:T(8,128)(2,1)S(1)}, bf16[256,256]{1,0:T(8,128)(2,1)S(1)}, u32[]{:S(2)}, u32[]{:S(2)}) collective-permute-start(bf16[256,256]{1,0:T(8,128)(2,1)S(1)} %get-tuple-element.57), channel_id=1, source_target_pairs={{0,1},{1,0},{2,3},{3,2},{4,5},{5,4},{6,7},{7,6},{8,9},{9,8},{10,11... | collective-permute-start | bytes 393224 | tf_op jit(solution)/shard_map/ppermute | solution.py:26
  16.7 6.9 %collective-permute-start.5 = (bf16[256,256]{1,0:T(8,128)(2,1)S(1)}, bf16[256,256]{1,0:T(8,128)(2,1)S(1)}, u32[]{:S(2)}, u32[]{:S(2)}) collective-permute-start(bf16[256,256]{1,0:T(8,128)(2,1)S(1)} %get-tuple-element.58), channel_id=1, source_target_pairs={{0,2},{1,3},{2,0},{3,1},{4,6},{5,7},{6,4},{7,5},{8,10},{9,11},{10,... | collective-permute-start | bytes 393224 | tf_op jit(solution)/shard_map/ppermute | solution.py:26
  18.5 5.9 %collective-permute-start.6 = (bf16[256,256]{1,0:T(8,128)(2,1)S(1)}, bf16[256,256]{1,0:T(8,128)(2,1)S(1)}, u32[]{:S(2)}, u32[]{:S(2)}) collective-permute-start(bf16[256,256]{1,0:T(8,128)(2,1)S(1)} %get-tuple-element.59), channel_id=1, source_target_pairs={{0,3},{1,2},{2,1},{3,0},{4,7},{5,6},{6,5},{7,4},{8,11},{9,10},{10,... | collective-permute-start | bytes 393224 | tf_op jit(solution)/shard_map/ppermute | solution.py:26
  18.9 16.8 %collective-permute-start.14 = (bf16[528,256]{1,0:T(8,128)(2,1)S(1)}, bf16[528,256]{1,0:T(8,128)(2,1)S(1)}, u32[]{:S(2)}, u32[]{:S(2)}) collective-permute-start(bf16[528,256]{1,0:T(8,128)(2,1)S(1)} %pack.1), channel_id=1, source_target_pairs={{0,8},{8,16},{16,24},{24,0},{1,9},{9,17},{17,25},{25,1},{2,10},{10... | collective-permute-start | bytes 811016 | tf_op jit(solution)/shard_map/ppermute | solution.py:39
  24.9 9.8 %collective-permute-start.7 = (bf16[256,256]{1,0:T(8,128)(2,1)S(1)}, bf16[256,256]{1,0:T(8,128)(2,1)S(1)}, u32[]{:S(2)}, u32[]{:S(2)}) collective-permute-start(bf16[256,256]{1,0:T(8,128)(2,1)S(1)} %get-tuple-element.66.refs_2_), channel_id=1, source_target_pairs={{0,4},{1,5},{2,6},{3,7},{4,0},{5,1},{6,2},{7,3},{8,12},{9,13},{10,... | collective-permute-start | bytes 393224 | tf_op jit(solution)/shard_map/ppermute | solution.py:26
  25.2 10.5 %collective-permute-start.8 = (bf16[128,256]{1,0:T(8,128)(2,1)S(1)}, bf16[128,256]{1,0:T(8,128)(2,1)S(1)}, u32[]{:S(2)}, u32[]{:S(2)}) collective-permute-start(bf16[128,256]{1,0:T(8,128)(2,1)S(1)} %get-tuple-element.67), channel_id=1, source_target_pairs={{0,1},{1,0},{2,3},{3,2},{4,5},{5,4},{6,7},{7,6},{8,9},{9,8},{10,11... | collective-permute-start | bytes 196616 | tf_op jit(solution)/shard_map/ppermute | solution.py:26
  26.7 11.5 %collective-permute-start.9 = (bf16[128,256]{1,0:T(8,128)(2,1)S(1)}, bf16[128,256]{1,0:T(8,128)(2,1)S(1)}, u32[]{:S(2)}, u32[]{:S(2)}) collective-permute-start(bf16[128,256]{1,0:T(8,128)(2,1)S(1)} %get-tuple-element.68), channel_id=1, source_target_pairs={{0,2},{1,3},{2,0},{3,1},{4,6},{5,7},{6,4},{7,5},{8,10},{9,11},{10,... | collective-permute-start | bytes 196616 | tf_op jit(solution)/shard_map/ppermute | solution.py:26
  28.3 9.9 %collective-permute-start.10 = (bf16[128,256]{1,0:T(8,128)(2,1)S(1)}, bf16[128,256]{1,0:T(8,128)(2,1)S(1)}, u32[]{:S(2)}, u32[]{:S(2)}) collective-permute-start(bf16[128,256]{1,0:T(8,128)(2,1)S(1)} %get-tuple-element.69), channel_id=1, source_target_pairs={{0,3},{1,2},{2,1},{3,0},{4,7},{5,6},{6,5},{7,4},{8,11},{9,10},{10,... | collective-permute-start | bytes 196616 | tf_op jit(solution)/shard_map/ppermute | solution.py:26
  41.7 11.4 %collective-permute-start.16 = (bf16[256,256]{1,0:T(8,128)(2,1)S(1)}, bf16[256,256]{1,0:T(8,128)(2,1)S(1)}, u32[]{:S(2)}, u32[]{:S(2)}) collective-permute-start(bf16[256,256]{1,0:T(8,128)(2,1)S(1)} %get-tuple-element.75), channel_id=1, source_target_pairs={{0,28},{1,29},{2,30},{3,31},{4,24},{5,25},{6,26},{7,27},{8,4},{9,5... | collective-permute-start | bytes 393224 | tf_op jit(solution)/shard_map/ppermute | solution.py:34
  42.4 7.8 %collective-permute-start.17 = (bf16[128,256]{1,0:T(8,128)(2,1)S(1)}, bf16[128,256]{1,0:T(8,128)(2,1)S(1)}, u32[]{:S(2)}, u32[]{:S(2)}) collective-permute-start(bf16[128,256]{1,0:T(8,128)(2,1)S(1)} %get-tuple-element.76), channel_id=1, source_target_pairs={{0,25},{1,24},{2,27},{3,26},{4,29},{5,28},{6,31},{7,30},{8,1},{9,0... | collective-permute-start | bytes 196616 | tf_op jit(solution)/shard_map/ppermute | solution.py:34
  44.5 8.6 %collective-permute-start.19 = (bf16[128,256]{1,0:T(8,128)(2,1)S(1)}, bf16[128,256]{1,0:T(8,128)(2,1)S(1)}, u32[]{:S(2)}, u32[]{:S(2)}) collective-permute-start(bf16[128,256]{1,0:T(8,128)(2,1)S(1)} %get-tuple-element.78), channel_id=1, source_target_pairs={{0,27},{1,26},{2,25},{3,24},{4,31},{5,30},{6,29},{7,28},{8,3},{9,2... | collective-permute-start | bytes 196616 | tf_op jit(solution)/shard_map/ppermute | solution.py:34
  50.1 6.8 %collective-permute-start.15 = (bf16[256,256]{1,0:T(8,128)(2,1)S(1)}, bf16[256,256]{1,0:T(8,128)(2,1)S(1)}, u32[]{:S(2)}, u32[]{:S(2)}) collective-permute-start(bf16[256,256]{1,0:T(8,128)(2,1)S(1)} %get-tuple-element.73.refs_10_), channel_id=1, source_target_pairs={{0,24},{1,25},{2,26},{3,27},{4,28},{5,29},{6,30},{7,31},{8,0},{9,1... | collective-permute-start | bytes 393224 | tf_op jit(solution)/shard_map/ppermute | solution.py:34
  54.0 6.4 %collective-permute-start.22 = (bf16[128,256]{1,0:T(8,128)(2,1)S(1)}, bf16[128,256]{1,0:T(8,128)(2,1)S(1)}, u32[]{:S(2)}, u32[]{:S(2)}) collective-permute-start(bf16[128,256]{1,0:T(8,128)(2,1)S(1)} %get-tuple-element.85), channel_id=1, source_target_pairs={{0,3},{1,2},{2,1},{3,0},{4,7},{5,6},{6,5},{7,4},{8,11},{9,10},{10,... | collective-permute-start | bytes 196616 | tf_op jit(solution)/shard_map/ppermute | solution.py:26
  61.0 8.9 %collective-permute-start.23 = (bf16[256,256]{1,0:T(8,128)(2,1)S(1)}, bf16[256,256]{1,0:T(8,128)(2,1)S(1)}, u32[]{:S(2)}, u32[]{:S(2)}) collective-permute-start(bf16[256,256]{1,0:T(8,128)(2,1)S(1)} %get-tuple-element.90.refs_2_), channel_id=1, source_target_pairs={{0,4},{1,5},{2,6},{3,7},{4,0},{5,1},{6,2},{7,3},{8,12},{9,13},{10,... | collective-permute-start | bytes 393224 | tf_op jit(solution)/shard_map/ppermute | solution.py:26
  62.3 8.1 %collective-permute-start.24 = (bf16[256,256]{1,0:T(8,128)(2,1)S(1)}, bf16[256,256]{1,0:T(8,128)(2,1)S(1)}, u32[]{:S(2)}, u32[]{:S(2)}) collective-permute-start(bf16[256,256]{1,0:T(8,128)(2,1)S(1)} %get-tuple-element.91), channel_id=1, source_target_pairs={{0,1},{1,0},{2,3},{3,2},{4,5},{5,4},{6,7},{7,6},{8,9},{9,8},{10,11... | collective-permute-start | bytes 393224 | tf_op jit(solution)/shard_map/ppermute | solution.py:26
  63.9 7.3 %collective-permute-start.25 = (bf16[256,256]{1,0:T(8,128)(2,1)S(1)}, bf16[256,256]{1,0:T(8,128)(2,1)S(1)}, u32[]{:S(2)}, u32[]{:S(2)}) collective-permute-start(bf16[256,256]{1,0:T(8,128)(2,1)S(1)} %get-tuple-element.92), channel_id=1, source_target_pairs={{0,2},{1,3},{2,0},{3,1},{4,6},{5,7},{6,4},{7,5},{8,10},{9,11},{10,... | collective-permute-start | bytes 393224 | tf_op jit(solution)/shard_map/ppermute | solution.py:26
  64.5 8.9 %collective-permute-start.26 = (bf16[256,256]{1,0:T(8,128)(2,1)S(1)}, bf16[256,256]{1,0:T(8,128)(2,1)S(1)}, u32[]{:S(2)}, u32[]{:S(2)}) collective-permute-start(bf16[256,256]{1,0:T(8,128)(2,1)S(1)} %get-tuple-element.93), channel_id=1, source_target_pairs={{0,3},{1,2},{2,1},{3,0},{4,7},{5,6},{6,5},{7,4},{8,11},{9,10},{10,... | collective-permute-start | bytes 393224 | tf_op jit(solution)/shard_map/ppermute | solution.py:26
  69.9 10.7 %collective-permute-start.27 = (bf16[128,256]{1,0:T(8,128)(2,1)S(1)}, bf16[128,256]{1,0:T(8,128)(2,1)S(1)}, u32[]{:S(2)}, u32[]{:S(2)}) collective-permute-start(bf16[128,256]{1,0:T(8,128)(2,1)S(1)} %get-tuple-element.94), channel_id=1, source_target_pairs={{0,1},{1,0},{2,3},{3,2},{4,5},{5,4},{6,7},{7,6},{8,9},{9,8},{10,11... | collective-permute-start | bytes 196616 | tf_op jit(solution)/shard_map/ppermute | solution.py:26
  73.4 6.0 %collective-permute-start.30 = (bf16[2,64,256]{2,1,0:T(8,128)(2,1)S(1)}, bf16[2,64,256]{2,1,0:T(8,128)(2,1)S(1)}, u32[]{:S(2)}, u32[]{:S(2)}) collective-permute-start(bf16[2,64,256]{2,1,0:T(8,128)(2,1)S(1)} %half_sum.1.mine_ref), channel_id=1, source_target_pairs={{0,4},{1,5},{2,6},{3,7},{4,0},{5,1},{6,2},{7,3},{8,12},{9,13},{10,... | collective-permute-start | bytes 196616 | tf_op jit(solution)/shard_map/ppermute | solution.py:26
  74.3 9.5 %collective-permute-start.28 = (bf16[128,256]{1,0:T(8,128)(2,1)S(1)}, bf16[128,256]{1,0:T(8,128)(2,1)S(1)}, u32[]{:S(2)}, u32[]{:S(2)}) collective-permute-start(bf16[128,256]{1,0:T(8,128)(2,1)S(1)} %get-tuple-element.95), channel_id=1, source_target_pairs={{0,2},{1,3},{2,0},{3,1},{4,6},{5,7},{6,4},{7,5},{8,10},{9,11},{10,... | collective-permute-start | bytes 196616 | tf_op jit(solution)/shard_map/ppermute | solution.py:26
  77.0 6.8 %collective-permute-start.29 = (bf16[128,256]{1,0:T(8,128)(2,1)S(1)}, bf16[128,256]{1,0:T(8,128)(2,1)S(1)}, u32[]{:S(2)}, u32[]{:S(2)}) collective-permute-start(bf16[128,256]{1,0:T(8,128)(2,1)S(1)} %get-tuple-element.96), channel_id=1, source_target_pairs={{0,3},{1,2},{2,1},{3,0},{4,7},{5,6},{6,5},{7,4},{8,11},{9,10},{10,... | collective-permute-start | bytes 196616 | tf_op jit(solution)/shard_map/ppermute | solution.py:26
  (15 other events, 178.2 us)

commit v15 on v14

--- a/solution.py
+++ b/solution.py
@@ -81,9 +81,13 @@
         )(*self.operands)
 
 
+COUNT_UNIT = 1 << 16
+
+
 def packed(tile_row, tile_col, tile_count, row_tiles):
     owner = jnp.bitwise_xor(tile_col // row_tiles, lax.axis_index("rows"))
     words = (owner * row_tiles + tile_col % row_tiles) * row_tiles + tile_row
+    words = words + tile_count * COUNT_UNIT
     live = lax.broadcasted_iota(jnp.int32, words.shape, 2) < tile_count
     return jnp.where(live, words, -1)[0]
 
@@ -101,7 +105,7 @@
     acc[...] = jnp.zeros_like(acc)
 
     def add(e):
-        word = words_ref[tick, e]
+        word = lax.rem(words_ref[tick, e], COUNT_UNIT)
         row = lax.rem(word, row_tiles)
         block = lax.rem(lax.div(word, row_tiles), row_tiles)
         slot = lax.div(word, row_tiles * row_tiles)
@@ -110,14 +114,19 @@
         cols = pl.ds(pl.multiple_of(slot * tile, tile), tile)
         acc[rows, cols] += vals[e].astype(F32)
 
+    count = lax.div(jnp.maximum(words_ref[tick, 0], 0), COUNT_UNIT)
     for c in range(chunks):
         copies[c].wait()
-
-        @pl.loop(c * chunk, (c + 1) * chunk)
-        def _(e):
-            @pl.when(words_ref[tick, e] >= 0)
-            def _():
-                add(e)
+        live = jnp.clip(count - c * chunk, 0, chunk)
+
+        @pl.loop(0, live // 2)
+        def _(i):
+            add(c * chunk + 2 * i)
+            add(c * chunk + 2 * i + 1)
+
+        @pl.when(live % 2 == 1)
+        def _():
+            add(c * chunk + live - 1)
 
     out_ref[...] = acc[...].astype(BF16)
 
@@ -152,7 +161,7 @@
     ticks, width = out_refs[0].shape
     for t in range(ticks):
         words = words_ref[t : t + 1, :]
-        index = jnp.where(words < 0, -1, words // row_tiles)
+        index = jnp.where(words < 0, -1, words % COUNT_UNIT // row_tiles)
 
         def named(k):
             block = index - k * row_tiles

time: 86.3 us -> 86.2 us (level)
  Pallas kernels: 13.2 us -> 9.95 us
  waiting for transfers between devices: 25.8 us -> 27.3 us
    pallas_call x16, Pallas kernels: 13.2 us -> 9.95 us  [run(): pl.pallas_call(kernel, out_shape=self.outs, in_specs=self.specs, out_spec...]
    ppermute x28, starting transfers between devices: 34.9 us -> 36.5 us  [swapped(): return lax.ppermute(block, 'rows', [(i, i ^ k) for i in range(n)])]
    ppermute x28, waiting for transfers between devices: 22.8 us -> 24.3 us  [swapped(): return lax.ppermute(block, 'rows', [(i, i ^ k) for i in range(n)])]
    ppermute x5, starting transfers between devices: 6.36 us -> 5.12 us  [lowered(): return lax.ppermute(block, ('section', 'rows'), route)]
  transfers between devices with their start and end apart: 34 -> 34, of which waited for: 14 -> 16; matrix products, arithmetic and copies ran while one was open for 4% -> 5% of each run, Pallas kernels for 13% -> 9%
where the time goes in v15:
time: 86.2 us; the launch traced here: 86 us
  starting transfers between devices  41.7 us (48%)
  waiting for transfers between devices  27.3 us (32%)
  Pallas kernels  9.95 us (12%)
  matrix products  2.6 us (3%)
  other arithmetic  2.33 us (3%)
  local copies, waits for them, and re-layouts  1.1 us (1%)
  between operations  1.1 us (1%)
    ppermute x28, starting transfers between devices, swapped(): return lax.ppermute(block, 'rows', [(i, i ^ k) for i in range(n)])  36.5 us
    ppermute x28, waiting for transfers between devices, swapped(): return lax.ppermute(block, 'rows', [(i, i ^ k) for i in range(n)])  24.3 us
    pallas_call x16, Pallas kernels, run(): pl.pallas_call(kernel, out_shape=self.outs, in_specs=self.specs, out_spec...  9.95 us
    ppermute x5, starting transfers between devices, lowered(): return lax.ppermute(block, ('section', 'rows'), route)  5.12 us
    ppermute x5, waiting for transfers between devices, lowered(): return lax.ppermute(block, ('section', 'rows'), route)  3.01 us
  transfers between devices with their start and end apart: 34, of which 16 were waited for; matrix products, arithmetic and copies ran while one was open for 5% of the time, Pallas kernels for 9%

profile of v15, /device:TPU:0, one launch (start us, length us, event | category | flops | bytes accessed | tf_op | source)
XLA Modules:
  0.0 86.0 jit_solution(9472944399182342018)
XLA Ops:
  2.2 4.1 %collective-permute-start = (bf16[256,256]{1,0:T(8,128)(2,1)S(1)}, bf16[256,256]{1,0:T(8,128)(2,1)S(1)}, u32[]{:S(2)}, u32[]{:S(2)}) collective-permute-start(bf16[256,256]{1,0:T(8,128)(2,1)S(1)} %fusion.3.refs_1_.refs_7_), channel_id=1, source_target_pairs={{0,4},{1,5},{2,6},{3,7},{4,0},{5,1},{6,2},{7,3},{8,12},{9,13},{10,... | collective-permute-start | bytes 393224 | tf_op jit(solution)/shard_map/ppermute | solution.py:26
  7.8 1.6 %collective-permute-start.1 = (f32[4,256]{1,0:T(4,128)S(1)}, f32[4,256]{1,0:T(4,128)S(1)}, u32[]{:S(2)}, u32[]{:S(2)}) collective-permute-start(f32[4,256]{1,0:T(4,128)S(1)} %get-tuple-element.54), channel_id=1, source_target_pairs={{0,1},{1,0},{2,3},{3,2},{4,5},{5,4},{6,7},{7,6},{8,9},{9,8},{10,11... | collective-permute-start | bytes 12296 | tf_op jit(solution)/shard_map/ppermute | solution.py:26
  9.4 1.6 %collective-permute-start.2 = (f32[4,256]{1,0:T(4,128)S(1)}, f32[4,256]{1,0:T(4,128)S(1)}, u32[]{:S(2)}, u32[]{:S(2)}) collective-permute-start(f32[4,256]{1,0:T(4,128)S(1)} %get-tuple-element.55), channel_id=1, source_target_pairs={{0,2},{1,3},{2,0},{3,1},{4,6},{5,7},{6,4},{7,5},{8,10},{9,11},{10,... | collective-permute-start | bytes 12296 | tf_op jit(solution)/shard_map/ppermute | solution.py:26
  11.4 2.7 %densify.2.refs_6_.refs_1_ = bf16[256,1152]{1,0:T(8,128)(2,1)S(1)} custom-call(s32[2,96]{1,0:T(2,128)S(1)} %fusion.15.words_ref, bf16[1,2,96,128,128]{4,3,2,1,0:T(8,128)(2,1)} %vals_ref.3), custom_call_target="tpu_custom_call" | custom-call | flops 31457280 | bytes 3145728 | tf_op jit(solution)/shard_map/densify/pallas_call | solution.py:71
  17.6 1.5 %collective-permute-start.6 = (bf16[256,256]{1,0:T(8,128)(2,1)S(1)}, bf16[256,256]{1,0:T(8,128)(2,1)S(1)}, u32[]{:S(2)}, u32[]{:S(2)}) collective-permute-start(bf16[256,256]{1,0:T(8,128)(2,1)S(1)} %get-tuple-element.59), channel_id=1, source_target_pairs={{0,3},{1,2},{2,1},{3,0},{4,7},{5,6},{6,5},{7,4},{8,11},{9,10},{10,... | collective-permute-start | bytes 393224 | tf_op jit(solution)/shard_map/ppermute | solution.py:26
  19.5 2.9 %densify.3.refs_6_.refs_1_ = bf16[256,1152]{1,0:T(8,128)(2,1)S(1)} custom-call(s32[2,96]{1,0:T(2,128)S(1)} %fusion.15.words_ref, bf16[1,2,96,128,128]{4,3,2,1,0:T(8,128)(2,1)} %vals_ref.3), custom_call_target="tpu_custom_call" | custom-call | flops 31457280 | bytes 3145728 | tf_op jit(solution)/shard_map/densify/pallas_call | solution.py:71
  22.4 1.5 %collective-permute-done.6.refs_11_ = bf16[256,256]{1,0:T(8,128)(2,1)S(1)} collective-permute-done((bf16[256,256]{1,0:T(8,128)(2,1)S(1)}, bf16[256,256]{1,0:T(8,128)(2,1)S(1)}, u32[]{:S(2)}, u32[]{:S(2)}) %collective-permute-start.6) | collective-permute-done | bytes 131104 | tf_op jit(solution)/shard_map/ppermute | solution.py:26
  26.6 1.7 %collective-permute-start.9 = (bf16[128,256]{1,0:T(8,128)(2,1)S(1)}, bf16[128,256]{1,0:T(8,128)(2,1)S(1)}, u32[]{:S(2)}, u32[]{:S(2)}) collective-permute-start(bf16[128,256]{1,0:T(8,128)(2,1)S(1)} %get-tuple-element.68), channel_id=1, source_target_pairs={{0,2},{1,3},{2,0},{3,1},{4,6},{5,7},{6,4},{7,5},{8,10},{9,11},{10,... | collective-permute-start | bytes 196616 | tf_op jit(solution)/shard_map/ppermute | solution.py:26
  29.2 5.0 %collective-permute-done.7.refs_0_.refs_3_ = bf16[256,256]{1,0:T(8,128)(2,1)S(1)} collective-permute-done((bf16[256,256]{1,0:T(8,128)(2,1)S(1)}, bf16[256,256]{1,0:T(8,128)(2,1)S(1)}, u32[]{:S(2)}, u32[]{:S(2)}) %collective-permute-start.7) | collective-permute-done | bytes 131104 | tf_op jit(solution)/shard_map/ppermute | solution.py:26
  34.9 3.0 %collective-permute-start.13 = (bf16[128,256]{1,0:T(8,128)(2,1)S(1)}, bf16[128,256]{1,0:T(8,128)(2,1)S(1)}, u32[]{:S(2)}, u32[]{:S(2)}) collective-permute-start(bf16[128,256]{1,0:T(8,128)(2,1)S(1)} %get-tuple-element.72), channel_id=1, source_target_pairs={{0,3},{1,2},{2,1},{3,0},{4,7},{5,6},{6,5},{7,4},{8,11},{9,10},{10,... | collective-permute-start | bytes 196616 | tf_op jit(solution)/shard_map/ppermute | solution.py:26
  39.3 1.5 %collective-permute-done.13.refs_9_ = bf16[128,256]{1,0:T(8,128)(2,1)S(1)} collective-permute-done((bf16[128,256]{1,0:T(8,128)(2,1)S(1)}, bf16[128,256]{1,0:T(8,128)(2,1)S(1)}, u32[]{:S(2)}, u32[]{:S(2)}) %collective-permute-start.13) | collective-permute-done | bytes 65568 | tf_op jit(solution)/shard_map/ppermute | solution.py:26
  41.4 1.9 %collective-permute-start.17 = (bf16[128,256]{1,0:T(8,128)(2,1)S(1)}, bf16[128,256]{1,0:T(8,128)(2,1)S(1)}, u32[]{:S(2)}, u32[]{:S(2)}) collective-permute-start(bf16[128,256]{1,0:T(8,128)(2,1)S(1)} %get-tuple-element.76), channel_id=1, source_target_pairs={{0,25},{1,24},{2,27},{3,26},{4,29},{5,28},{6,31},{7,30},{8,1},{9,0... | collective-permute-start | bytes 196616 | tf_op jit(solution)/shard_map/ppermute | solution.py:34
  43.3 3.1 %collective-permute-start.19 = (bf16[128,256]{1,0:T(8,128)(2,1)S(1)}, bf16[128,256]{1,0:T(8,128)(2,1)S(1)}, u32[]{:S(2)}, u32[]{:S(2)}) collective-permute-start(bf16[128,256]{1,0:T(8,128)(2,1)S(1)} %get-tuple-element.78), channel_id=1, source_target_pairs={{0,27},{1,26},{2,25},{3,24},{4,31},{5,30},{6,29},{7,28},{8,3},{9,2... | collective-permute-start | bytes 196616 | tf_op jit(solution)/shard_map/ppermute | solution.py:34
  48.6 1.5 %collective-permute-done.18.refs_10_ = bf16[128,256]{1,0:T(8,128)(2,1)S(1)} collective-permute-done((bf16[128,256]{1,0:T(8,128)(2,1)S(1)}, bf16[128,256]{1,0:T(8,128)(2,1)S(1)}, u32[]{:S(2)}, u32[]{:S(2)}) %collective-permute-start.18) | collective-permute-done | bytes 65568 | tf_op jit(solution)/shard_map/ppermute | solution.py:34
  50.0 1.6 %collective-permute-done.19.refs_11_ = bf16[128,256]{1,0:T(8,128)(2,1)S(1)} collective-permute-done((bf16[128,256]{1,0:T(8,128)(2,1)S(1)}, bf16[128,256]{1,0:T(8,128)(2,1)S(1)}, u32[]{:S(2)}, u32[]{:S(2)}) %collective-permute-start.19) | collective-permute-done | bytes 65568 | tf_op jit(solution)/shard_map/ppermute | solution.py:34
  52.9 2.2 %collective-permute-start.22 = (bf16[128,256]{1,0:T(8,128)(2,1)S(1)}, bf16[128,256]{1,0:T(8,128)(2,1)S(1)}, u32[]{:S(2)}, u32[]{:S(2)}) collective-permute-start(bf16[128,256]{1,0:T(8,128)(2,1)S(1)} %get-tuple-element.85), channel_id=1, source_target_pairs={{0,3},{1,2},{2,1},{3,0},{4,7},{5,6},{6,5},{7,4},{8,11},{9,10},{10,... | collective-permute-start | bytes 196616 | tf_op jit(solution)/shard_map/ppermute | solution.py:26
  59.2 2.0 %collective-permute-start.23 = (bf16[256,256]{1,0:T(8,128)(2,1)S(1)}, bf16[256,256]{1,0:T(8,128)(2,1)S(1)}, u32[]{:S(2)}, u32[]{:S(2)}) collective-permute-start(bf16[256,256]{1,0:T(8,128)(2,1)S(1)} %get-tuple-element.90.refs_2_), channel_id=1, source_target_pairs={{0,4},{1,5},{2,6},{3,7},{4,0},{5,1},{6,2},{7,3},{8,12},{9,13},{10,... | collective-permute-start | bytes 393224 | tf_op jit(solution)/shard_map/ppermute | solution.py:26
  61.2 1.7 %collective-permute-start.24 = (bf16[256,256]{1,0:T(8,128)(2,1)S(1)}, bf16[256,256]{1,0:T(8,128)(2,1)S(1)}, u32[]{:S(2)}, u32[]{:S(2)}) collective-permute-start(bf16[256,256]{1,0:T(8,128)(2,1)S(1)} %get-tuple-element.91), channel_id=1, source_target_pairs={{0,1},{1,0},{2,3},{3,2},{4,5},{5,4},{6,7},{7,6},{8,9},{9,8},{10,11... | collective-permute-start | bytes 393224 | tf_op jit(solution)/shard_map/ppermute | solution.py:26
  64.7 2.7 %collective-permute-done.23.refs_0_.refs_3_ = bf16[256,256]{1,0:T(8,128)(2,1)S(1)} collective-permute-done((bf16[256,256]{1,0:T(8,128)(2,1)S(1)}, bf16[256,256]{1,0:T(8,128)(2,1)S(1)}, u32[]{:S(2)}, u32[]{:S(2)}) %collective-permute-start.23) | collective-permute-done | bytes 131104 | tf_op jit(solution)/shard_map/ppermute | solution.py:26
  67.4 1.8 %collective-permute-start.27 = (bf16[128,256]{1,0:T(8,128)(2,1)S(1)}, bf16[128,256]{1,0:T(8,128)(2,1)S(1)}, u32[]{:S(2)}, u32[]{:S(2)}) collective-permute-start(bf16[128,256]{1,0:T(8,128)(2,1)S(1)} %get-tuple-element.94), channel_id=1, source_target_pairs={{0,1},{1,0},{2,3},{3,2},{4,5},{5,4},{6,7},{7,6},{8,9},{9,8},{10,11... | collective-permute-start | bytes 196616 | tf_op jit(solution)/shard_map/ppermute | solution.py:26
  69.8 3.0 %collective-permute-done.26.refs_6_.refs_4_ = bf16[256,256]{1,0:T(8,128)(2,1)S(1)} collective-permute-done((bf16[256,256]{1,0:T(8,128)(2,1)S(1)}, bf16[256,256]{1,0:T(8,128)(2,1)S(1)}, u32[]{:S(2)}, u32[]{:S(2)}) %collective-permute-start.26) | collective-permute-done | bytes 131104 | tf_op jit(solution)/shard_map/ppermute | solution.py:26
  73.0 1.9 %collective-permute-start.28 = (bf16[128,256]{1,0:T(8,128)(2,1)S(1)}, bf16[128,256]{1,0:T(8,128)(2,1)S(1)}, u32[]{:S(2)}, u32[]{:S(2)}) collective-permute-start(bf16[128,256]{1,0:T(8,128)(2,1)S(1)} %get-tuple-element.95), channel_id=1, source_target_pairs={{0,2},{1,3},{2,0},{3,1},{4,6},{5,7},{6,4},{7,5},{8,10},{9,11},{10,... | collective-permute-start | bytes 196616 | tf_op jit(solution)/shard_map/ppermute | solution.py:26
  75.5 3.2 %collective-permute-done.30.far_ref = bf16[2,64,256]{2,1,0:T(8,128)(2,1)S(1)} collective-permute-done((bf16[2,64,256]{2,1,0:T(8,128)(2,1)S(1)}, bf16[2,64,256]{2,1,0:T(8,128)(2,1)S(1)}, u32[]{:S(2)}, u32[]{:S(2)}) %collective-permute-start.30) | collective-permute-done | bytes 65568 | tf_op jit(solution)/shard_map/ppermute | solution.py:26
  79.3 2.9 %collective-permute-start.33 = (bf16[2,64,256]{2,1,0:T(8,128)(2,1)S(1)}, bf16[2,64,256]{2,1,0:T(8,128)(2,1)S(1)}, u32[]{:S(2)}, u32[]{:S(2)}) collective-permute-start(bf16[2,64,256]{2,1,0:T(8,128)(2,1)S(1)} %total.1.refs_0_), channel_id=1, source_target_pairs={{0,3},{1,2},{2,1},{3,0},{4,7},{5,6},{6,5},{7,4},{8,11},{9,10},{10,... | collective-permute-start | bytes 196616 | tf_op jit(solution)/shard_map/ppermute | solution.py:26
  (79 shorter events, 28.5 us)
Async XLA Ops:
  2.2 13.3 %collective-permute-start = (bf16[256,256]{1,0:T(8,128)(2,1)S(1)}, bf16[256,256]{1,0:T(8,128)(2,1)S(1)}, u32[]{:S(2)}, u32[]{:S(2)}) collective-permute-start(bf16[256,256]{1,0:T(8,128)(2,1)S(1)} %fusion.3.refs_1_.refs_7_), channel_id=1, source_target_pairs={{0,4},{1,5},{2,6},{3,7},{4,0},{5,1},{6,2},{7,3},{8,12},{9,13},{10,... | collective-permute-start | bytes 393224 | tf_op jit(solution)/shard_map/ppermute | solution.py:26
  7.8 6.3 %collective-permute-start.1 = (f32[4,256]{1,0:T(4,128)S(1)}, f32[4,256]{1,0:T(4,128)S(1)}, u32[]{:S(2)}, u32[]{:S(2)}) collective-permute-start(f32[4,256]{1,0:T(4,128)S(1)} %get-tuple-element.54), channel_id=1, source_target_pairs={{0,1},{1,0},{2,3},{3,2},{4,5},{5,4},{6,7},{7,6},{8,9},{9,8},{10,11... | collective-permute-start | bytes 12296 | tf_op jit(solution)/shard_map/ppermute | solution.py:26
  15.5 6.8 %collective-permute-start.4 = (bf16[256,256]{1,0:T(8,128)(2,1)S(1)}, bf16[256,256]{1,0:T(8,128)(2,1)S(1)}, u32[]{:S(2)}, u32[]{:S(2)}) collective-permute-start(bf16[256,256]{1,0:T(8,128)(2,1)S(1)} %get-tuple-element.57), channel_id=1, source_target_pairs={{0,1},{1,0},{2,3},{3,2},{4,5},{5,4},{6,7},{7,6},{8,9},{9,8},{10,11... | collective-permute-start | bytes 393224 | tf_op jit(solution)/shard_map/ppermute | solution.py:26
  16.4 6.0 %collective-permute-start.5 = (bf16[256,256]{1,0:T(8,128)(2,1)S(1)}, bf16[256,256]{1,0:T(8,128)(2,1)S(1)}, u32[]{:S(2)}, u32[]{:S(2)}) collective-permute-start(bf16[256,256]{1,0:T(8,128)(2,1)S(1)} %get-tuple-element.58), channel_id=1, source_target_pairs={{0,2},{1,3},{2,0},{3,1},{4,6},{5,7},{6,4},{7,5},{8,10},{9,11},{10,... | collective-permute-start | bytes 393224 | tf_op jit(solution)/shard_map/ppermute | solution.py:26
  17.6 6.3 %collective-permute-start.6 = (bf16[256,256]{1,0:T(8,128)(2,1)S(1)}, bf16[256,256]{1,0:T(8,128)(2,1)S(1)}, u32[]{:S(2)}, u32[]{:S(2)}) collective-permute-start(bf16[256,256]{1,0:T(8,128)(2,1)S(1)} %get-tuple-element.59), channel_id=1, source_target_pairs={{0,3},{1,2},{2,1},{3,0},{4,7},{5,6},{6,5},{7,4},{8,11},{9,10},{10,... | collective-permute-start | bytes 393224 | tf_op jit(solution)/shard_map/ppermute | solution.py:26
  19.4 15.4 %collective-permute-start.14 = (bf16[528,256]{1,0:T(8,128)(2,1)S(1)}, bf16[528,256]{1,0:T(8,128)(2,1)S(1)}, u32[]{:S(2)}, u32[]{:S(2)}) collective-permute-start(bf16[528,256]{1,0:T(8,128)(2,1)S(1)} %pack.1), channel_id=1, source_target_pairs={{0,8},{8,16},{16,24},{24,0},{1,9},{9,17},{17,25},{25,1},{2,10},{10... | collective-permute-start | bytes 811016 | tf_op jit(solution)/shard_map/ppermute | solution.py:39
  24.4 9.8 %collective-permute-start.7 = (bf16[256,256]{1,0:T(8,128)(2,1)S(1)}, bf16[256,256]{1,0:T(8,128)(2,1)S(1)}, u32[]{:S(2)}, u32[]{:S(2)}) collective-permute-start(bf16[256,256]{1,0:T(8,128)(2,1)S(1)} %get-tuple-element.66.refs_2_), channel_id=1, source_target_pairs={{0,4},{1,5},{2,6},{3,7},{4,0},{5,1},{6,2},{7,3},{8,12},{9,13},{10,... | collective-permute-start | bytes 393224 | tf_op jit(solution)/shard_map/ppermute | solution.py:26
  25.8 9.1 %collective-permute-start.8 = (bf16[128,256]{1,0:T(8,128)(2,1)S(1)}, bf16[128,256]{1,0:T(8,128)(2,1)S(1)}, u32[]{:S(2)}, u32[]{:S(2)}) collective-permute-start(bf16[128,256]{1,0:T(8,128)(2,1)S(1)} %get-tuple-element.67), channel_id=1, source_target_pairs={{0,1},{1,0},{2,3},{3,2},{4,5},{5,4},{6,7},{7,6},{8,9},{9,8},{10,11... | collective-permute-start | bytes 196616 | tf_op jit(solution)/shard_map/ppermute | solution.py:26
  26.6 11.3 %collective-permute-start.9 = (bf16[128,256]{1,0:T(8,128)(2,1)S(1)}, bf16[128,256]{1,0:T(8,128)(2,1)S(1)}, u32[]{:S(2)}, u32[]{:S(2)}) collective-permute-start(bf16[128,256]{1,0:T(8,128)(2,1)S(1)} %get-tuple-element.68), channel_id=1, source_target_pairs={{0,2},{1,3},{2,0},{3,1},{4,6},{5,7},{6,4},{7,5},{8,10},{9,11},{10,... | collective-permute-start | bytes 196616 | tf_op jit(solution)/shard_map/ppermute | solution.py:26
  28.3 9.5 %collective-permute-start.10 = (bf16[128,256]{1,0:T(8,128)(2,1)S(1)}, bf16[128,256]{1,0:T(8,128)(2,1)S(1)}, u32[]{:S(2)}, u32[]{:S(2)}) collective-permute-start(bf16[128,256]{1,0:T(8,128)(2,1)S(1)} %get-tuple-element.69), channel_id=1, source_target_pairs={{0,3},{1,2},{2,1},{3,0},{4,7},{5,6},{6,5},{7,4},{8,11},{9,10},{10,... | collective-permute-start | bytes 196616 | tf_op jit(solution)/shard_map/ppermute | solution.py:26
  34.9 5.9 %collective-permute-start.13 = (bf16[128,256]{1,0:T(8,128)(2,1)S(1)}, bf16[128,256]{1,0:T(8,128)(2,1)S(1)}, u32[]{:S(2)}, u32[]{:S(2)}) collective-permute-start(bf16[128,256]{1,0:T(8,128)(2,1)S(1)} %get-tuple-element.72), channel_id=1, source_target_pairs={{0,3},{1,2},{2,1},{3,0},{4,7},{5,6},{6,5},{7,4},{8,11},{9,10},{10,... | collective-permute-start | bytes 196616 | tf_op jit(solution)/shard_map/ppermute | solution.py:26
  41.3 10.3 %collective-permute-start.16 = (bf16[256,256]{1,0:T(8,128)(2,1)S(1)}, bf16[256,256]{1,0:T(8,128)(2,1)S(1)}, u32[]{:S(2)}, u32[]{:S(2)}) collective-permute-start(bf16[256,256]{1,0:T(8,128)(2,1)S(1)} %get-tuple-element.75), channel_id=1, source_target_pairs={{0,28},{1,29},{2,30},{3,31},{4,24},{5,25},{6,26},{7,27},{8,4},{9,5... | collective-permute-start | bytes 393224 | tf_op jit(solution)/shard_map/ppermute | solution.py:34
  41.4 7.2 %collective-permute-start.17 = (bf16[128,256]{1,0:T(8,128)(2,1)S(1)}, bf16[128,256]{1,0:T(8,128)(2,1)S(1)}, u32[]{:S(2)}, u32[]{:S(2)}) collective-permute-start(bf16[128,256]{1,0:T(8,128)(2,1)S(1)} %get-tuple-element.76), channel_id=1, source_target_pairs={{0,25},{1,24},{2,27},{3,26},{4,29},{5,28},{6,31},{7,30},{8,1},{9,0... | collective-permute-start | bytes 196616 | tf_op jit(solution)/shard_map/ppermute | solution.py:34
  43.3 6.7 %collective-permute-start.18 = (bf16[128,256]{1,0:T(8,128)(2,1)S(1)}, bf16[128,256]{1,0:T(8,128)(2,1)S(1)}, u32[]{:S(2)}, u32[]{:S(2)}) collective-permute-start(bf16[128,256]{1,0:T(8,128)(2,1)S(1)} %get-tuple-element.77), channel_id=1, source_target_pairs={{0,26},{1,27},{2,24},{3,25},{4,30},{5,31},{6,28},{7,29},{8,2},{9,3... | collective-permute-start | bytes 196616 | tf_op jit(solution)/shard_map/ppermute | solution.py:34
  43.3 8.2 %collective-permute-start.19 = (bf16[128,256]{1,0:T(8,128)(2,1)S(1)}, bf16[128,256]{1,0:T(8,128)(2,1)S(1)}, u32[]{:S(2)}, u32[]{:S(2)}) collective-permute-start(bf16[128,256]{1,0:T(8,128)(2,1)S(1)} %get-tuple-element.78), channel_id=1, source_target_pairs={{0,27},{1,26},{2,25},{3,24},{4,31},{5,30},{6,29},{7,28},{8,3},{9,2... | collective-permute-start | bytes 196616 | tf_op jit(solution)/shard_map/ppermute | solution.py:34
  48.5 6.9 %collective-permute-start.15 = (bf16[256,256]{1,0:T(8,128)(2,1)S(1)}, bf16[256,256]{1,0:T(8,128)(2,1)S(1)}, u32[]{:S(2)}, u32[]{:S(2)}) collective-permute-start(bf16[256,256]{1,0:T(8,128)(2,1)S(1)} %get-tuple-element.73.refs_10_), channel_id=1, source_target_pairs={{0,24},{1,25},{2,26},{3,27},{4,28},{5,29},{6,30},{7,31},{8,0},{9,1... | collective-permute-start | bytes 393224 | tf_op jit(solution)/shard_map/ppermute | solution.py:34
  59.2 8.2 %collective-permute-start.23 = (bf16[256,256]{1,0:T(8,128)(2,1)S(1)}, bf16[256,256]{1,0:T(8,128)(2,1)S(1)}, u32[]{:S(2)}, u32[]{:S(2)}) collective-permute-start(bf16[256,256]{1,0:T(8,128)(2,1)S(1)} %get-tuple-element.90.refs_2_), channel_id=1, source_target_pairs={{0,4},{1,5},{2,6},{3,7},{4,0},{5,1},{6,2},{7,3},{8,12},{9,13},{10,... | collective-permute-start | bytes 393224 | tf_op jit(solution)/shard_map/ppermute | solution.py:26
  61.2 8.0 %collective-permute-start.24 = (bf16[256,256]{1,0:T(8,128)(2,1)S(1)}, bf16[256,256]{1,0:T(8,128)(2,1)S(1)}, u32[]{:S(2)}, u32[]{:S(2)}) collective-permute-start(bf16[256,256]{1,0:T(8,128)(2,1)S(1)} %get-tuple-element.91), channel_id=1, source_target_pairs={{0,1},{1,0},{2,3},{3,2},{4,5},{5,4},{6,7},{7,6},{8,9},{9,8},{10,11... | collective-permute-start | bytes 393224 | tf_op jit(solution)/shard_map/ppermute | solution.py:26
  62.8 7.0 %collective-permute-start.25 = (bf16[256,256]{1,0:T(8,128)(2,1)S(1)}, bf16[256,256]{1,0:T(8,128)(2,1)S(1)}, u32[]{:S(2)}, u32[]{:S(2)}) collective-permute-start(bf16[256,256]{1,0:T(8,128)(2,1)S(1)} %get-tuple-element.92), channel_id=1, source_target_pairs={{0,2},{1,3},{2,0},{3,1},{4,6},{5,7},{6,4},{7,5},{8,10},{9,11},{10,... | collective-permute-start | bytes 393224 | tf_op jit(solution)/shard_map/ppermute | solution.py:26
  63.4 9.4 %collective-permute-start.26 = (bf16[256,256]{1,0:T(8,128)(2,1)S(1)}, bf16[256,256]{1,0:T(8,128)(2,1)S(1)}, u32[]{:S(2)}, u32[]{:S(2)}) collective-permute-start(bf16[256,256]{1,0:T(8,128)(2,1)S(1)} %get-tuple-element.93), channel_id=1, source_target_pairs={{0,3},{1,2},{2,1},{3,0},{4,7},{5,6},{6,5},{7,4},{8,11},{9,10},{10,... | collective-permute-start | bytes 393224 | tf_op jit(solution)/shard_map/ppermute | solution.py:26
  67.4 11.9 %collective-permute-start.27 = (bf16[128,256]{1,0:T(8,128)(2,1)S(1)}, bf16[128,256]{1,0:T(8,128)(2,1)S(1)}, u32[]{:S(2)}, u32[]{:S(2)}) collective-permute-start(bf16[128,256]{1,0:T(8,128)(2,1)S(1)} %get-tuple-element.94), channel_id=1, source_target_pairs={{0,1},{1,0},{2,3},{3,2},{4,5},{5,4},{6,7},{7,6},{8,9},{9,8},{10,11... | collective-permute-start | bytes 196616 | tf_op jit(solution)/shard_map/ppermute | solution.py:26
  73.0 10.1 %collective-permute-start.28 = (bf16[128,256]{1,0:T(8,128)(2,1)S(1)}, bf16[128,256]{1,0:T(8,128)(2,1)S(1)}, u32[]{:S(2)}, u32[]{:S(2)}) collective-permute-start(bf16[128,256]{1,0:T(8,128)(2,1)S(1)} %get-tuple-element.95), channel_id=1, source_target_pairs={{0,2},{1,3},{2,0},{3,1},{4,6},{5,7},{6,4},{7,5},{8,10},{9,11},{10,... | collective-permute-start | bytes 196616 | tf_op jit(solution)/shard_map/ppermute | solution.py:26
  74.9 8.2 %collective-permute-start.29 = (bf16[128,256]{1,0:T(8,128)(2,1)S(1)}, bf16[128,256]{1,0:T(8,128)(2,1)S(1)}, u32[]{:S(2)}, u32[]{:S(2)}) collective-permute-start(bf16[128,256]{1,0:T(8,128)(2,1)S(1)} %get-tuple-element.96), channel_id=1, source_target_pairs={{0,3},{1,2},{2,1},{3,0},{4,7},{5,6},{6,5},{7,4},{8,11},{9,10},{10,... | collective-permute-start | bytes 196616 | tf_op jit(solution)/shard_map/ppermute | solution.py:26
  79.3 5.9 %collective-permute-start.33 = (bf16[2,64,256]{2,1,0:T(8,128)(2,1)S(1)}, bf16[2,64,256]{2,1,0:T(8,128)(2,1)S(1)}, u32[]{:S(2)}, u32[]{:S(2)}) collective-permute-start(bf16[2,64,256]{2,1,0:T(8,128)(2,1)S(1)} %total.1.refs_0_), channel_id=1, source_target_pairs={{0,3},{1,2},{2,1},{3,0},{4,7},{5,6},{6,5},{7,4},{8,11},{9,10},{10,... | collective-permute-start | bytes 196616 | tf_op jit(solution)/shard_map/ppermute | solution.py:26
  (15 other events, 176.9 us)

commit v16 on v15

--- a/solution.py
+++ b/solution.py
@@ -81,13 +81,9 @@
         )(*self.operands)
 
 
-COUNT_UNIT = 1 << 16
-
-
 def packed(tile_row, tile_col, tile_count, row_tiles):
     owner = jnp.bitwise_xor(tile_col // row_tiles, lax.axis_index("rows"))
     words = (owner * row_tiles + tile_col % row_tiles) * row_tiles + tile_row
-    words = words + tile_count * COUNT_UNIT
     live = lax.broadcasted_iota(jnp.int32, words.shape, 2) < tile_count
     return jnp.where(live, words, -1)[0]
 
@@ -105,7 +101,7 @@
     acc[...] = jnp.zeros_like(acc)
 
     def add(e):
-        word = lax.rem(words_ref[tick, e], COUNT_UNIT)
+        word = words_ref[tick, e]
         row = lax.rem(word, row_tiles)
         block = lax.rem(lax.div(word, row_tiles), row_tiles)
         slot = lax.div(word, row_tiles * row_tiles)
@@ -114,7 +110,12 @@
         cols = pl.ds(pl.multiple_of(slot * tile, tile), tile)
         acc[rows, cols] += vals[e].astype(F32)
 
-    count = lax.div(jnp.maximum(words_ref[tick, 0], 0), COUNT_UNIT)
+    count, step = jnp.int32(0), 1 << (entries.bit_length() - 1)
+    while step:
+        probe = count + step
+        live = (probe <= entries) & (words_ref[tick, jnp.minimum(probe, entries) - 1] >= 0)
+        count = jnp.where(live, probe, count)
+        step //= 2
     for c in range(chunks):
         copies[c].wait()
         live = jnp.clip(count - c * chunk, 0, chunk)
@@ -161,7 +162,7 @@
     ticks, width = out_refs[0].shape
     for t in range(ticks):
         words = words_ref[t : t + 1, :]
-        index = jnp.where(words < 0, -1, words % COUNT_UNIT // row_tiles)
+        index = jnp.where(words < 0, -1, words // row_tiles)
 
         def named(k):
             block = index - k * row_tiles
@@ -487,8 +488,8 @@
             call.want(VMEM, (tile * (1 + c["first"]), width), BF16, h - 1)
             relays = call.run(functools.partial(forward_kernel, c), "forward", small_cost)
             relayed = shared(relays)
-            if entry and not final:
-                later, _ = lax.optimization_barrier((words, relays))
+            if layer == 0 and not final:
+                later, *_ = lax.optimization_barrier((words, *near))
                 adjs[tick + 1] = densify(tick + 1, later, tile_vals, row_tiles, n)
                 relayed, adjs[tick + 1] = lax.optimization_barrier((relayed, adjs[tick + 1]))
             if final:

time: 86.2 us -> 83.1 us (0.964)
  waiting for transfers between devices: 27.3 us -> 20.9 us
  starting transfers between devices: 41.7 us -> 44.8 us
    ppermute x28, waiting for transfers between devices: 24.3 us -> 17.5 us  [swapped(): return lax.ppermute(block, 'rows', [(i, i ^ k) for i in range(n)])]
    ppermute x5, starting transfers between devices: 5.12 us -> 7.32 us  [lowered(): return lax.ppermute(block, ('section', 'rows'), route)]
    ppermute x28, starting transfers between devices: 36.5 us -> 37.5 us  [swapped(): return lax.ppermute(block, 'rows', [(i, i ^ k) for i in range(n)])]
    pallas_call x16, Pallas kernels: 9.95 us -> 10.8 us  [run(): pl.pallas_call(kernel, out_shape=self.outs, in_specs=self.specs, out_spec...]
  transfers between devices with their start and end apart: 34 -> 34, of which waited for: 16 -> 15; matrix products, arithmetic and copies ran while one was open for 5% -> 5% of each run, Pallas kernels for 9% -> 11%
where the time goes in v16:
time: 83.1 us; the launch traced here: 83 us
  starting transfers between devices  44.8 us (54%)
  waiting for transfers between devices  20.9 us (25%)
  Pallas kernels  10.8 us (13%)
  matrix products  2.6 us (3%)
  other arithmetic  1.67 us (2%)
  local copies, waits for them, and re-layouts  1.1 us (1%)
  between operations  1.08 us (1%)
    ppermute x28, starting transfers between devices, swapped(): return lax.ppermute(block, 'rows', [(i, i ^ k) for i in range(n)])  37.5 us
    ppermute x28, waiting for transfers between devices, swapped(): return lax.ppermute(block, 'rows', [(i, i ^ k) for i in range(n)])  17.5 us
    pallas_call x16, Pallas kernels, run(): pl.pallas_call(kernel, out_shape=self.outs, in_specs=self.specs, out_spec...  10.8 us
    ppermute x5, starting transfers between devices, lowered(): return lax.ppermute(block, ('section', 'rows'), route)  7.32 us
    ppermute x5, waiting for transfers between devices, lowered(): return lax.ppermute(block, ('section', 'rows'), route)  3.34 us
  transfers between devices with their start and end apart: 34, of which 15 were waited for; matrix products, arithmetic and copies ran while one was open for 5% of the time, Pallas kernels for 11%

profile of v16, /device:TPU:0, one launch (start us, length us, event | category | flops | bytes accessed | tf_op | source)
XLA Modules:
  0.0 83.0 jit_solution(8904355273662045376)
XLA Ops:
  2.2 4.1 %collective-permute-start.3 = (bf16[256,256]{1,0:T(8,128)(2,1)S(1)}, bf16[256,256]{1,0:T(8,128)(2,1)S(1)}, u32[]{:S(2)}, u32[]{:S(2)}) collective-permute-start(bf16[256,256]{1,0:T(8,128)(2,1)S(1)} %fusion.3.refs_1_.refs_7_), channel_id=1, source_target_pairs={{0,4},{1,5},{2,6},{3,7},{4,0},{5,1},{6,2},{7,3},{8,12},{9,13},{10,... | collective-permute-start | bytes 393224 | tf_op jit(solution)/shard_map/ppermute | solution.py:26
  7.2 1.6 %collective-permute-start = (f32[4,256]{1,0:T(4,128)S(1)}, f32[4,256]{1,0:T(4,128)S(1)}, u32[]{:S(2)}, u32[]{:S(2)}) collective-permute-start(f32[4,256]{1,0:T(4,128)S(1)} %get-tuple-element.53), channel_id=1, source_target_pairs={{0,1},{1,0},{2,3},{3,2},{4,5},{5,4},{6,7},{7,6},{8,9},{9,8},{10,11... | collective-permute-start | bytes 12296 | tf_op jit(solution)/shard_map/ppermute | solution.py:26
  8.7 1.6 %collective-permute-start.1 = (f32[4,256]{1,0:T(4,128)S(1)}, f32[4,256]{1,0:T(4,128)S(1)}, u32[]{:S(2)}, u32[]{:S(2)}) collective-permute-start(f32[4,256]{1,0:T(4,128)S(1)} %get-tuple-element.54), channel_id=1, source_target_pairs={{0,2},{1,3},{2,0},{3,1},{4,6},{5,7},{6,4},{7,5},{8,10},{9,11},{10,... | collective-permute-start | bytes 12296 | tf_op jit(solution)/shard_map/ppermute | solution.py:26
  10.7 3.3 %densify.2.refs_6_.refs_1_ = bf16[256,1152]{1,0:T(8,128)(2,1)S(1)} custom-call(s32[2,96]{1,0:T(2,128)S(1)} %fusion.15.words_ref, bf16[1,2,96,128,128]{4,3,2,1,0:T(8,128)(2,1)} %vals_ref.3), custom_call_target="tpu_custom_call" | custom-call | flops 31457280 | bytes 3145728 | tf_op jit(solution)/shard_map/densify/pallas_call | solution.py:71
  16.6 1.8 %collective-permute-start.6 = (bf16[256,256]{1,0:T(8,128)(2,1)S(1)}, bf16[256,256]{1,0:T(8,128)(2,1)S(1)}, u32[]{:S(2)}, u32[]{:S(2)}) collective-permute-start(bf16[256,256]{1,0:T(8,128)(2,1)S(1)} %get-tuple-element.60), channel_id=1, source_target_pairs={{0,3},{1,2},{2,1},{3,0},{4,7},{5,6},{6,5},{7,4},{8,11},{9,10},{10,... | collective-permute-start | bytes 393224 | tf_op jit(solution)/shard_map/ppermute | solution.py:26
  18.8 2.3 %collective-permute-done.4.refs_9_ = bf16[256,256]{1,0:T(8,128)(2,1)S(1)} collective-permute-done((bf16[256,256]{1,0:T(8,128)(2,1)S(1)}, bf16[256,256]{1,0:T(8,128)(2,1)S(1)}, u32[]{:S(2)}, u32[]{:S(2)}) %collective-permute-start.4) | collective-permute-done | bytes 131104 | tf_op jit(solution)/shard_map/ppermute | solution.py:26
  21.1 1.7 %collective-permute-done.6.refs_11_ = bf16[256,256]{1,0:T(8,128)(2,1)S(1)} collective-permute-done((bf16[256,256]{1,0:T(8,128)(2,1)S(1)}, bf16[256,256]{1,0:T(8,128)(2,1)S(1)}, u32[]{:S(2)}, u32[]{:S(2)}) %collective-permute-start.6) | collective-permute-done | bytes 131104 | tf_op jit(solution)/shard_map/ppermute | solution.py:26
  23.3 1.8 %collective-permute-start.7 = (bf16[256,256]{1,0:T(8,128)(2,1)S(1)}, bf16[256,256]{1,0:T(8,128)(2,1)S(1)}, u32[]{:S(2)}, u32[]{:S(2)}) collective-permute-start(bf16[256,256]{1,0:T(8,128)(2,1)S(1)} %get-tuple-element.61.refs_2_), channel_id=1, source_target_pairs={{0,4},{1,5},{2,6},{3,7},{4,0},{5,1},{6,2},{7,3},{8,12},{9,13},{10,... | collective-permute-start | bytes 393224 | tf_op jit(solution)/shard_map/ppermute | solution.py:26
  26.6 1.7 %collective-permute-start.12 = (bf16[128,256]{1,0:T(8,128)(2,1)S(1)}, bf16[128,256]{1,0:T(8,128)(2,1)S(1)}, u32[]{:S(2)}, u32[]{:S(2)}) collective-permute-start(bf16[128,256]{1,0:T(8,128)(2,1)S(1)} %get-tuple-element.66), channel_id=1, source_target_pairs={{0,2},{1,3},{2,0},{3,1},{4,6},{5,7},{6,4},{7,5},{8,10},{9,11},{10,... | collective-permute-start | bytes 196616 | tf_op jit(solution)/shard_map/ppermute | solution.py:26
  28.6 2.0 %collective-permute-done.7.refs_0_.refs_3_ = bf16[256,256]{1,0:T(8,128)(2,1)S(1)} collective-permute-done((bf16[256,256]{1,0:T(8,128)(2,1)S(1)}, bf16[256,256]{1,0:T(8,128)(2,1)S(1)}, u32[]{:S(2)}, u32[]{:S(2)}) %collective-permute-start.7) | collective-permute-done | bytes 131104 | tf_op jit(solution)/shard_map/ppermute | solution.py:26
  30.7 1.7 %collective-permute-start.8 = (bf16[128,256]{1,0:T(8,128)(2,1)S(1)}, bf16[128,256]{1,0:T(8,128)(2,1)S(1)}, u32[]{:S(2)}, u32[]{:S(2)}) collective-permute-start(bf16[128,256]{1,0:T(8,128)(2,1)S(1)} %get-tuple-element.62), channel_id=1, source_target_pairs={{0,1},{1,0},{2,3},{3,2},{4,5},{5,4},{6,7},{7,6},{8,9},{9,8},{10,11... | collective-permute-start | bytes 196616 | tf_op jit(solution)/shard_map/ppermute | solution.py:26
  34.2 3.2 %densify.3.refs_6_.refs_1_ = bf16[256,1152]{1,0:T(8,128)(2,1)S(1)} custom-call(s32[2,96]{1,0:T(2,128)S(1)} %fusion.15.words_ref, bf16[1,2,96,128,128]{4,3,2,1,0:T(8,128)(2,1)} %vals_ref.3), custom_call_target="tpu_custom_call" | custom-call | flops 31457280 | bytes 3145728 | tf_op jit(solution)/shard_map/densify/pallas_call | solution.py:71
  38.6 1.7 %collective-permute-start.16 = (bf16[256,256]{1,0:T(8,128)(2,1)S(1)}, bf16[256,256]{1,0:T(8,128)(2,1)S(1)}, u32[]{:S(2)}, u32[]{:S(2)}) collective-permute-start(bf16[256,256]{1,0:T(8,128)(2,1)S(1)} %get-tuple-element.75), channel_id=1, source_target_pairs={{0,28},{1,29},{2,30},{3,31},{4,24},{5,25},{6,26},{7,27},{8,4},{9,5... | collective-permute-start | bytes 393224 | tf_op jit(solution)/shard_map/ppermute | solution.py:34
  40.3 2.9 %collective-permute-start.17 = (bf16[128,256]{1,0:T(8,128)(2,1)S(1)}, bf16[128,256]{1,0:T(8,128)(2,1)S(1)}, u32[]{:S(2)}, u32[]{:S(2)}) collective-permute-start(bf16[128,256]{1,0:T(8,128)(2,1)S(1)} %get-tuple-element.76), channel_id=1, source_target_pairs={{0,25},{1,24},{2,27},{3,26},{4,29},{5,28},{6,31},{7,30},{8,1},{9,0... | collective-permute-start | bytes 196616 | tf_op jit(solution)/shard_map/ppermute | solution.py:34
  43.2 2.7 %collective-permute-start.19 = (bf16[128,256]{1,0:T(8,128)(2,1)S(1)}, bf16[128,256]{1,0:T(8,128)(2,1)S(1)}, u32[]{:S(2)}, u32[]{:S(2)}) collective-permute-start(bf16[128,256]{1,0:T(8,128)(2,1)S(1)} %get-tuple-element.78), channel_id=1, source_target_pairs={{0,27},{1,26},{2,25},{3,24},{4,31},{5,30},{6,29},{7,28},{8,3},{9,2... | collective-permute-start | bytes 196616 | tf_op jit(solution)/shard_map/ppermute | solution.py:34
  48.1 1.5 %collective-permute-done.18.refs_10_ = bf16[128,256]{1,0:T(8,128)(2,1)S(1)} collective-permute-done((bf16[128,256]{1,0:T(8,128)(2,1)S(1)}, bf16[128,256]{1,0:T(8,128)(2,1)S(1)}, u32[]{:S(2)}, u32[]{:S(2)}) %collective-permute-start.18) | collective-permute-done | bytes 65568 | tf_op jit(solution)/shard_map/ppermute | solution.py:34
  49.6 1.8 %collective-permute-done.19.refs_11_ = bf16[128,256]{1,0:T(8,128)(2,1)S(1)} collective-permute-done((bf16[128,256]{1,0:T(8,128)(2,1)S(1)}, bf16[128,256]{1,0:T(8,128)(2,1)S(1)}, u32[]{:S(2)}, u32[]{:S(2)}) %collective-permute-start.19) | collective-permute-done | bytes 65568 | tf_op jit(solution)/shard_map/ppermute | solution.py:34
  52.5 2.4 %collective-permute-start.22 = (bf16[128,256]{1,0:T(8,128)(2,1)S(1)}, bf16[128,256]{1,0:T(8,128)(2,1)S(1)}, u32[]{:S(2)}, u32[]{:S(2)}) collective-permute-start(bf16[128,256]{1,0:T(8,128)(2,1)S(1)} %get-tuple-element.85), channel_id=1, source_target_pairs={{0,3},{1,2},{2,1},{3,0},{4,7},{5,6},{6,5},{7,4},{8,11},{9,10},{10,... | collective-permute-start | bytes 196616 | tf_op jit(solution)/shard_map/ppermute | solution.py:26
  60.0 1.5 %collective-permute-start.24 = (bf16[256,256]{1,0:T(8,128)(2,1)S(1)}, bf16[256,256]{1,0:T(8,128)(2,1)S(1)}, u32[]{:S(2)}, u32[]{:S(2)}) collective-permute-start(bf16[256,256]{1,0:T(8,128)(2,1)S(1)} %get-tuple-element.91), channel_id=1, source_target_pairs={{0,1},{1,0},{2,3},{3,2},{4,5},{5,4},{6,7},{7,6},{8,9},{9,8},{10,11... | collective-permute-start | bytes 393224 | tf_op jit(solution)/shard_map/ppermute | solution.py:26
  61.5 2.0 %collective-permute-start.26 = (bf16[256,256]{1,0:T(8,128)(2,1)S(1)}, bf16[256,256]{1,0:T(8,128)(2,1)S(1)}, u32[]{:S(2)}, u32[]{:S(2)}) collective-permute-start(bf16[256,256]{1,0:T(8,128)(2,1)S(1)} %get-tuple-element.93), channel_id=1, source_target_pairs={{0,3},{1,2},{2,1},{3,0},{4,7},{5,6},{6,5},{7,4},{8,11},{9,10},{10,... | collective-permute-start | bytes 393224 | tf_op jit(solution)/shard_map/ppermute | solution.py:26
  67.5 2.2 %collective-permute-done.26.refs_6_.refs_4_ = bf16[256,256]{1,0:T(8,128)(2,1)S(1)} collective-permute-done((bf16[256,256]{1,0:T(8,128)(2,1)S(1)}, bf16[256,256]{1,0:T(8,128)(2,1)S(1)}, u32[]{:S(2)}, u32[]{:S(2)}) %collective-permute-start.26) | collective-permute-done | bytes 131104 | tf_op jit(solution)/shard_map/ppermute | solution.py:26
  71.1 1.6 %collective-permute-start.28 = (bf16[128,256]{1,0:T(8,128)(2,1)S(1)}, bf16[128,256]{1,0:T(8,128)(2,1)S(1)}, u32[]{:S(2)}, u32[]{:S(2)}) collective-permute-start(bf16[128,256]{1,0:T(8,128)(2,1)S(1)} %get-tuple-element.95), channel_id=1, source_target_pairs={{0,2},{1,3},{2,0},{3,1},{4,6},{5,7},{6,4},{7,5},{8,10},{9,11},{10,... | collective-permute-start | bytes 196616 | tf_op jit(solution)/shard_map/ppermute | solution.py:26
  73.7 1.9 %collective-permute-done.30.far_ref = bf16[2,64,256]{2,1,0:T(8,128)(2,1)S(1)} collective-permute-done((bf16[2,64,256]{2,1,0:T(8,128)(2,1)S(1)}, bf16[2,64,256]{2,1,0:T(8,128)(2,1)S(1)}, u32[]{:S(2)}, u32[]{:S(2)}) %collective-permute-start.30) | collective-permute-done | bytes 65568 | tf_op jit(solution)/shard_map/ppermute | solution.py:26
  76.6 2.7 %collective-permute-start.33 = (bf16[2,64,256]{2,1,0:T(8,128)(2,1)S(1)}, bf16[2,64,256]{2,1,0:T(8,128)(2,1)S(1)}, u32[]{:S(2)}, u32[]{:S(2)}) collective-permute-start(bf16[2,64,256]{2,1,0:T(8,128)(2,1)S(1)} %total.1.refs_0_), channel_id=1, source_target_pairs={{0,3},{1,2},{2,1},{3,0},{4,7},{5,6},{6,5},{7,4},{8,11},{9,10},{10,... | collective-permute-start | bytes 196616 | tf_op jit(solution)/shard_map/ppermute | solution.py:26
  (78 shorter events, 30.4 us)
Async XLA Ops:
  2.2 12.6 %collective-permute-start.3 = (bf16[256,256]{1,0:T(8,128)(2,1)S(1)}, bf16[256,256]{1,0:T(8,128)(2,1)S(1)}, u32[]{:S(2)}, u32[]{:S(2)}) collective-permute-start(bf16[256,256]{1,0:T(8,128)(2,1)S(1)} %fusion.3.refs_1_.refs_7_), channel_id=1, source_target_pairs={{0,4},{1,5},{2,6},{3,7},{4,0},{5,1},{6,2},{7,3},{8,12},{9,13},{10,... | collective-permute-start | bytes 393224 | tf_op jit(solution)/shard_map/ppermute | solution.py:26
  7.2 6.9 %collective-permute-start = (f32[4,256]{1,0:T(4,128)S(1)}, f32[4,256]{1,0:T(4,128)S(1)}, u32[]{:S(2)}, u32[]{:S(2)}) collective-permute-start(f32[4,256]{1,0:T(4,128)S(1)} %get-tuple-element.53), channel_id=1, source_target_pairs={{0,1},{1,0},{2,3},{3,2},{4,5},{5,4},{6,7},{7,6},{8,9},{9,8},{10,11... | collective-permute-start | bytes 12296 | tf_op jit(solution)/shard_map/ppermute | solution.py:26
  14.9 6.2 %collective-permute-start.4 = (bf16[256,256]{1,0:T(8,128)(2,1)S(1)}, bf16[256,256]{1,0:T(8,128)(2,1)S(1)}, u32[]{:S(2)}, u32[]{:S(2)}) collective-permute-start(bf16[256,256]{1,0:T(8,128)(2,1)S(1)} %get-tuple-element.58), channel_id=1, source_target_pairs={{0,1},{1,0},{2,3},{3,2},{4,5},{5,4},{6,7},{7,6},{8,9},{9,8},{10,11... | collective-permute-start | bytes 393224 | tf_op jit(solution)/shard_map/ppermute | solution.py:26
  15.5 5.6 %collective-permute-start.5 = (bf16[256,256]{1,0:T(8,128)(2,1)S(1)}, bf16[256,256]{1,0:T(8,128)(2,1)S(1)}, u32[]{:S(2)}, u32[]{:S(2)}) collective-permute-start(bf16[256,256]{1,0:T(8,128)(2,1)S(1)} %get-tuple-element.59), channel_id=1, source_target_pairs={{0,2},{1,3},{2,0},{3,1},{4,6},{5,7},{6,4},{7,5},{8,10},{9,11},{10,... | collective-permute-start | bytes 393224 | tf_op jit(solution)/shard_map/ppermute | solution.py:26
  16.6 6.2 %collective-permute-start.6 = (bf16[256,256]{1,0:T(8,128)(2,1)S(1)}, bf16[256,256]{1,0:T(8,128)(2,1)S(1)}, u32[]{:S(2)}, u32[]{:S(2)}) collective-permute-start(bf16[256,256]{1,0:T(8,128)(2,1)S(1)} %get-tuple-element.60), channel_id=1, source_target_pairs={{0,3},{1,2},{2,1},{3,0},{4,7},{5,6},{6,5},{7,4},{8,11},{9,10},{10,... | collective-permute-start | bytes 393224 | tf_op jit(solution)/shard_map/ppermute | solution.py:26
  18.8 19.3 %collective-permute-start.14 = (bf16[528,256]{1,0:T(8,128)(2,1)S(1)}, bf16[528,256]{1,0:T(8,128)(2,1)S(1)}, u32[]{:S(2)}, u32[]{:S(2)}) collective-permute-start(bf16[528,256]{1,0:T(8,128)(2,1)S(1)} %pack.1), channel_id=1, source_target_pairs={{0,8},{8,16},{16,24},{24,0},{1,9},{9,17},{17,25},{25,1},{2,10},{10... | collective-permute-start | bytes 811016 | tf_op jit(solution)/shard_map/ppermute | solution.py:39
  23.3 7.4 %collective-permute-start.7 = (bf16[256,256]{1,0:T(8,128)(2,1)S(1)}, bf16[256,256]{1,0:T(8,128)(2,1)S(1)}, u32[]{:S(2)}, u32[]{:S(2)}) collective-permute-start(bf16[256,256]{1,0:T(8,128)(2,1)S(1)} %get-tuple-element.61.refs_2_), channel_id=1, source_target_pairs={{0,4},{1,5},{2,6},{3,7},{4,0},{5,1},{6,2},{7,3},{8,12},{9,13},{10,... | collective-permute-start | bytes 393224 | tf_op jit(solution)/shard_map/ppermute | solution.py:26
  25.1 7.2 %collective-permute-start.11 = (bf16[128,256]{1,0:T(8,128)(2,1)S(1)}, bf16[128,256]{1,0:T(8,128)(2,1)S(1)}, u32[]{:S(2)}, u32[]{:S(2)}) collective-permute-start(bf16[128,256]{1,0:T(8,128)(2,1)S(1)} %get-tuple-element.65), channel_id=1, source_target_pairs={{0,1},{1,0},{2,3},{3,2},{4,5},{5,4},{6,7},{7,6},{8,9},{9,8},{10,11... | collective-permute-start | bytes 196616 | tf_op jit(solution)/shard_map/ppermute | solution.py:26
  26.6 6.4 %collective-permute-start.12 = (bf16[128,256]{1,0:T(8,128)(2,1)S(1)}, bf16[128,256]{1,0:T(8,128)(2,1)S(1)}, u32[]{:S(2)}, u32[]{:S(2)}) collective-permute-start(bf16[128,256]{1,0:T(8,128)(2,1)S(1)} %get-tuple-element.66), channel_id=1, source_target_pairs={{0,2},{1,3},{2,0},{3,1},{4,6},{5,7},{6,4},{7,5},{8,10},{9,11},{10,... | collective-permute-start | bytes 196616 | tf_op jit(solution)/shard_map/ppermute | solution.py:26
  28.3 5.9 %collective-permute-start.13 = (bf16[128,256]{1,0:T(8,128)(2,1)S(1)}, bf16[128,256]{1,0:T(8,128)(2,1)S(1)}, u32[]{:S(2)}, u32[]{:S(2)}) collective-permute-start(bf16[128,256]{1,0:T(8,128)(2,1)S(1)} %get-tuple-element.67), channel_id=1, source_target_pairs={{0,3},{1,2},{2,1},{3,0},{4,7},{5,6},{6,5},{7,4},{8,11},{9,10},{10,... | collective-permute-start | bytes 196616 | tf_op jit(solution)/shard_map/ppermute | solution.py:26
  30.7 6.7 %collective-permute-start.8 = (bf16[128,256]{1,0:T(8,128)(2,1)S(1)}, bf16[128,256]{1,0:T(8,128)(2,1)S(1)}, u32[]{:S(2)}, u32[]{:S(2)}) collective-permute-start(bf16[128,256]{1,0:T(8,128)(2,1)S(1)} %get-tuple-element.62), channel_id=1, source_target_pairs={{0,1},{1,0},{2,3},{3,2},{4,5},{5,4},{6,7},{7,6},{8,9},{9,8},{10,11... | collective-permute-start | bytes 196616 | tf_op jit(solution)/shard_map/ppermute | solution.py:26
  38.6 12.8 %collective-permute-start.16 = (bf16[256,256]{1,0:T(8,128)(2,1)S(1)}, bf16[256,256]{1,0:T(8,128)(2,1)S(1)}, u32[]{:S(2)}, u32[]{:S(2)}) collective-permute-start(bf16[256,256]{1,0:T(8,128)(2,1)S(1)} %get-tuple-element.75), channel_id=1, source_target_pairs={{0,28},{1,29},{2,30},{3,31},{4,24},{5,25},{6,26},{7,27},{8,4},{9,5... | collective-permute-start | bytes 393224 | tf_op jit(solution)/shard_map/ppermute | solution.py:34
  40.3 7.8 %collective-permute-start.17 = (bf16[128,256]{1,0:T(8,128)(2,1)S(1)}, bf16[128,256]{1,0:T(8,128)(2,1)S(1)}, u32[]{:S(2)}, u32[]{:S(2)}) collective-permute-start(bf16[128,256]{1,0:T(8,128)(2,1)S(1)} %get-tuple-element.76), channel_id=1, source_target_pairs={{0,25},{1,24},{2,27},{3,26},{4,29},{5,28},{6,31},{7,30},{8,1},{9,0... | collective-permute-start | bytes 196616 | tf_op jit(solution)/shard_map/ppermute | solution.py:34
  43.2 6.4 %collective-permute-start.18 = (bf16[128,256]{1,0:T(8,128)(2,1)S(1)}, bf16[128,256]{1,0:T(8,128)(2,1)S(1)}, u32[]{:S(2)}, u32[]{:S(2)}) collective-permute-start(bf16[128,256]{1,0:T(8,128)(2,1)S(1)} %get-tuple-element.77), channel_id=1, source_target_pairs={{0,26},{1,27},{2,24},{3,25},{4,30},{5,31},{6,28},{7,29},{8,2},{9,3... | collective-permute-start | bytes 196616 | tf_op jit(solution)/shard_map/ppermute | solution.py:34
  43.2 8.2 %collective-permute-start.19 = (bf16[128,256]{1,0:T(8,128)(2,1)S(1)}, bf16[128,256]{1,0:T(8,128)(2,1)S(1)}, u32[]{:S(2)}, u32[]{:S(2)}) collective-permute-start(bf16[128,256]{1,0:T(8,128)(2,1)S(1)} %get-tuple-element.78), channel_id=1, source_target_pairs={{0,27},{1,26},{2,25},{3,24},{4,31},{5,30},{6,29},{7,28},{8,3},{9,2... | collective-permute-start | bytes 196616 | tf_op jit(solution)/shard_map/ppermute | solution.py:34
  48.0 7.2 %collective-permute-start.15 = (bf16[256,256]{1,0:T(8,128)(2,1)S(1)}, bf16[256,256]{1,0:T(8,128)(2,1)S(1)}, u32[]{:S(2)}, u32[]{:S(2)}) collective-permute-start(bf16[256,256]{1,0:T(8,128)(2,1)S(1)} %get-tuple-element.73.refs_10_), channel_id=1, source_target_pairs={{0,24},{1,25},{2,26},{3,27},{4,28},{5,29},{6,30},{7,31},{8,0},{9,1... | collective-permute-start | bytes 393224 | tf_op jit(solution)/shard_map/ppermute | solution.py:34
  58.6 6.4 %collective-permute-start.23 = (bf16[256,256]{1,0:T(8,128)(2,1)S(1)}, bf16[256,256]{1,0:T(8,128)(2,1)S(1)}, u32[]{:S(2)}, u32[]{:S(2)}) collective-permute-start(bf16[256,256]{1,0:T(8,128)(2,1)S(1)} %get-tuple-element.90.refs_2_), channel_id=1, source_target_pairs={{0,4},{1,5},{2,6},{3,7},{4,0},{5,1},{6,2},{7,3},{8,12},{9,13},{10,... | collective-permute-start | bytes 393224 | tf_op jit(solution)/shard_map/ppermute | solution.py:26
  60.0 6.4 %collective-permute-start.24 = (bf16[256,256]{1,0:T(8,128)(2,1)S(1)}, bf16[256,256]{1,0:T(8,128)(2,1)S(1)}, u32[]{:S(2)}, u32[]{:S(2)}) collective-permute-start(bf16[256,256]{1,0:T(8,128)(2,1)S(1)} %get-tuple-element.91), channel_id=1, source_target_pairs={{0,1},{1,0},{2,3},{3,2},{4,5},{5,4},{6,7},{7,6},{8,9},{9,8},{10,11... | collective-permute-start | bytes 393224 | tf_op jit(solution)/shard_map/ppermute | solution.py:26
  61.5 6.0 %collective-permute-start.25 = (bf16[256,256]{1,0:T(8,128)(2,1)S(1)}, bf16[256,256]{1,0:T(8,128)(2,1)S(1)}, u32[]{:S(2)}, u32[]{:S(2)}) collective-permute-start(bf16[256,256]{1,0:T(8,128)(2,1)S(1)} %get-tuple-element.92), channel_id=1, source_target_pairs={{0,2},{1,3},{2,0},{3,1},{4,6},{5,7},{6,4},{7,5},{8,10},{9,11},{10,... | collective-permute-start | bytes 393224 | tf_op jit(solution)/shard_map/ppermute | solution.py:26
  61.5 8.1 %collective-permute-start.26 = (bf16[256,256]{1,0:T(8,128)(2,1)S(1)}, bf16[256,256]{1,0:T(8,128)(2,1)S(1)}, u32[]{:S(2)}, u32[]{:S(2)}) collective-permute-start(bf16[256,256]{1,0:T(8,128)(2,1)S(1)} %get-tuple-element.93), channel_id=1, source_target_pairs={{0,3},{1,2},{2,1},{3,0},{4,7},{5,6},{6,5},{7,4},{8,11},{9,10},{10,... | collective-permute-start | bytes 393224 | tf_op jit(solution)/shard_map/ppermute | solution.py:26
  65.0 11.5 %collective-permute-start.27 = (bf16[128,256]{1,0:T(8,128)(2,1)S(1)}, bf16[128,256]{1,0:T(8,128)(2,1)S(1)}, u32[]{:S(2)}, u32[]{:S(2)}) collective-permute-start(bf16[128,256]{1,0:T(8,128)(2,1)S(1)} %get-tuple-element.94), channel_id=1, source_target_pairs={{0,1},{1,0},{2,3},{3,2},{4,5},{5,4},{6,7},{7,6},{8,9},{9,8},{10,11... | collective-permute-start | bytes 196616 | tf_op jit(solution)/shard_map/ppermute | solution.py:26
  69.7 5.9 %collective-permute-start.30 = (bf16[2,64,256]{2,1,0:T(8,128)(2,1)S(1)}, bf16[2,64,256]{2,1,0:T(8,128)(2,1)S(1)}, u32[]{:S(2)}, u32[]{:S(2)}) collective-permute-start(bf16[2,64,256]{2,1,0:T(8,128)(2,1)S(1)} %half_sum.1.mine_ref), channel_id=1, source_target_pairs={{0,4},{1,5},{2,6},{3,7},{4,0},{5,1},{6,2},{7,3},{8,12},{9,13},{10,... | collective-permute-start | bytes 196616 | tf_op jit(solution)/shard_map/ppermute | solution.py:26
  71.1 9.0 %collective-permute-start.28 = (bf16[128,256]{1,0:T(8,128)(2,1)S(1)}, bf16[128,256]{1,0:T(8,128)(2,1)S(1)}, u32[]{:S(2)}, u32[]{:S(2)}) collective-permute-start(bf16[128,256]{1,0:T(8,128)(2,1)S(1)} %get-tuple-element.95), channel_id=1, source_target_pairs={{0,2},{1,3},{2,0},{3,1},{4,6},{5,7},{6,4},{7,5},{8,10},{9,11},{10,... | collective-permute-start | bytes 196616 | tf_op jit(solution)/shard_map/ppermute | solution.py:26
  72.6 7.4 %collective-permute-start.29 = (bf16[128,256]{1,0:T(8,128)(2,1)S(1)}, bf16[128,256]{1,0:T(8,128)(2,1)S(1)}, u32[]{:S(2)}, u32[]{:S(2)}) collective-permute-start(bf16[128,256]{1,0:T(8,128)(2,1)S(1)} %get-tuple-element.96), channel_id=1, source_target_pairs={{0,3},{1,2},{2,1},{3,0},{4,7},{5,6},{6,5},{7,4},{8,11},{9,10},{10,... | collective-permute-start | bytes 196616 | tf_op jit(solution)/shard_map/ppermute | solution.py:26
  (15 other events, 173.8 us)

commit v17 on v16

--- a/solution.py
+++ b/solution.py
@@ -39,8 +39,8 @@
     return lax.ppermute(block, "section", [(s, (s + 1) % sections) for s in range(sections)])
 
 
-def shared(blocks, move=swapped):
-    moved = {k: move(block, k) for k, block in reversed(list(enumerate(blocks, 1)))}
+def shared(blocks):
+    moved = {k: swapped(block, k) for k, block in reversed(list(enumerate(blocks, 1)))}
     return [moved[k] for k in sorted(moved)]
 
 
@@ -176,21 +176,14 @@
         out_refs[0][t : t + 1, :] = named(n // 2)
 
 
-def pack_kernel(tick, layer, preact_all, weight_all, *refs):
-    asked, (out_ref, sems) = refs[:-2], refs[-2:]
-    rows, width = preact_all.shape[-2:]
+def pack_kernel(tick, layer, preact_all, weight_all, out_ref, sems):
+    rows = preact_all.shape[-2]
     loads = [
         pltpu.make_async_copy(preact_all.at[0, tick, layer], out_ref.at[:rows], sems.at[0]),
-        pltpu.make_async_copy(
-            weight_all.at[0, layer], out_ref.at[rows : rows + width], sems.at[1]
-        ),
+        pltpu.make_async_copy(weight_all.at[0, layer], out_ref.at[rows:], sems.at[1]),
     ]
     for load in loads:
         load.start()
-    used = sum(ref.shape[0] for ref in asked)
-    rest = out_ref.shape[0] - rows - width - used
-    parts = [ref[...] for ref in asked] + ([jnp.zeros((rest, width), F32)] if rest else [])
-    out_ref[rows + width :, :] = jnp.concatenate(parts, axis=0).astype(BF16)
     for load in loads:
         load.wait()
 
@@ -296,11 +289,11 @@
     refs = Refs(refs)
     count, tile, rows = c["n"] // 2 - 1, c["tile"], c["rows"]
     far_ref = refs.take()
-    own_ref = refs.take() if c["first"] else None
+    own_ref = refs.take() if c["entry"] else None
     asked = refs.take(count)
     for asked_ref, send in zip(asked, refs.take(count)):
         row = 2 * c["tick"]
-        if c["first"]:
+        if c["entry"]:
             send[:tile, :] = chosen(own_ref, asked_ref[row : row + 1, :], rows, tile)
             send[tile:, :] = chosen(far_ref, asked_ref[row + 1 : row + 2, :], rows, tile)
         else:
@@ -328,21 +321,16 @@
     got = take_got(refs, c)
     below_ref, last_ref = refs.take(2)
     grad_ref, image_ref = refs.take(2)
-    sends = refs.take(c["n"] // 2 - 1)
-    tile, rows, width = c["tile"], c["rows"], c["width"]
+    rows = c["rows"]
     grad = spread_of(adj_ref, own_ref, got, names_ref, c)
     grad_ref[...] = grad
     section = lax.axis_index("section")
     grad = jnp.where(section == 0, last_ref[...], grad)
     below = jnp.where(section == 0, c["sections"], section) - 1
     _, _, image = image_of(
-        c, below, c["layers"] - 1, grad, below_ref[:rows, :], below_ref[rows : rows + width, :]
+        c, below, c["layers"] - 1, grad, below_ref[:rows, :], below_ref[rows:, :]
     )
     image_ref[...] = image
-    asked = below_ref[rows + width :, :].astype(F32)
-    for k, send in enumerate(sends):
-        row = 2 * (k * c["ticks"] + c["tick"] + 1)
-        send[...] = chosen(image_ref, asked[row : row + 1, :], rows, tile)
 
 
 def exit_kernel(c, *refs):
@@ -467,25 +455,21 @@
                     pending = results.take(h - 1) + pending
                 kept = masked = results.take()
             if turned is not None:
-                far = lowered(turned[0], h)
-                near = shared(turned[1:], lowered)
-                far, *near = lax.optimization_barrier((far, *near))
+                far = lowered(turned, h)
                 turned = None
-                if final:
-                    parts = shared(sends)
             else:
                 far = swapped(image, h)
-                near = [] if c["first"] else shared(sends)
+            near = [] if entry else shared(sends)
             ready = image
             if c["first"]:
                 adjs[0] = densify(0, words, tile_vals, row_tiles, n)
                 ready, adjs[0] = lax.optimization_barrier((image, adjs[0]))
             call = Call()
             call.give(VMEM, far)
-            if c["first"]:
+            if entry:
                 call.give(VMEM, ready)
             call.give(VMEM, *asked)
-            call.want(VMEM, (tile * (1 + c["first"]), width), BF16, h - 1)
+            call.want(VMEM, (tile * (1 + entry), width), BF16, h - 1)
             relays = call.run(functools.partial(forward_kernel, c), "forward", small_cost)
             relayed = shared(relays)
             if layer == 0 and not final:
@@ -503,7 +487,7 @@
                     functools.partial(half_sum_kernel, layers, tile), "half_sum", small_cost
                 )
             got = [far, *near, *relayed]
-            joined = c["first"]
+            joined = entry
             toward = toward + ALPHA * image.astype(F32)
             if not final:
                 term = beta * jnp.dot(
@@ -518,17 +502,14 @@
         if not final:
             up = Call()
             up.give(HBM, preact, weights)
-            up.give(VMEM, *asked)
-            length = rows + width + -(-2 * ticks * (h - 1) // 16) * 16
-            up.want(VMEM, (length, width), BF16)
+            up.want(VMEM, (rows + width, width), BF16)
             up.scratch = [pltpu.SemaphoreType.DMA((2,))]
             (pack,) = up.run(
                 functools.partial(pack_kernel, tick + 1, layers - 1), "pack", small_cost
             )
             call.give(VMEM, raised(pack), grad_last)
             call.want(VMEM, (rows, width), BF16, 2)
-            call.want(VMEM, (tile, width), BF16, h - 1)
-            grad, *turned = call.run(functools.partial(turn_kernel, c), "turn", layer_cost)
+            grad, turned = call.run(functools.partial(turn_kernel, c), "turn", layer_cost)
             handed.append(grad)
             continue
         call.give(VMEM, *handed)

time: 83.1 us -> 85.8 us (1.032)
  waiting for transfers between devices: 20.9 us -> 31 us
  starting transfers between devices: 44.8 us -> 38.9 us
  local copies, waits for them, and re-layouts: 1.1 us -> 0.16 us
    ppermute x28, waiting for transfers between devices: 17.5 us -> 26.1 us  [swapped(): return lax.ppermute(block, 'rows', [(i, i ^ k) for i in range(n)])]
    ppermute x28, starting transfers between devices: 37.5 us -> 34.3 us  [swapped(): return lax.ppermute(block, 'rows', [(i, i ^ k) for i in range(n)])]
    ppermute x5 -> x2, starting transfers between devices: 7.32 us -> 4.51 us  [lowered(): return lax.ppermute(block, ('section', 'rows'), route)]
    ppermute x5 -> x2, waiting for transfers between devices: 3.34 us -> 4.93 us  [lowered(): return lax.ppermute(block, ('section', 'rows'), route)]
    mul x1, local copies, waits for them, and re-layouts: 1.08 us -> 0.13 us  [shards(): beta * jnp.dot(support[0, tick, layer].T, masked, preferred_element_type=...]
  transfers between devices with their start and end apart: 34 -> 31, of which waited for: 15 -> 13; matrix products, arithmetic and copies ran while one was open for 5% -> 3% of each run, Pallas kernels for 11% -> 10%
where the time goes in v17:
time: 85.8 us
  starting transfers between devices  38.9 us (45%)
  waiting for transfers between devices  31 us (36%)
  Pallas kernels  11 us (13%)
  matrix products  1.9 us (2%)
  other arithmetic  1.67 us (2%)
  between operations  1.09 us (1%)
    ppermute x28, starting transfers between devices, swapped(): return lax.ppermute(block, 'rows', [(i, i ^ k) for i in range(n)])  34.3 us
    ppermute x28, waiting for transfers between devices, swapped(): return lax.ppermute(block, 'rows', [(i, i ^ k) for i in range(n)])  26.1 us
    pallas_call x16, Pallas kernels, run(): pl.pallas_call(kernel, out_shape=self.outs, in_specs=self.specs, out_spec...  11 us
    ppermute x2, waiting for transfers between devices, lowered(): return lax.ppermute(block, ('section', 'rows'), route)  4.93 us
    ppermute x2, starting transfers between devices, lowered(): return lax.ppermute(block, ('section', 'rows'), route)  4.51 us
  transfers between devices with their start and end apart: 31, of which 13 were waited for; matrix products, arithmetic and copies ran while one was open for 3% of the time, Pallas kernels for 10%

profile of v17, /device:TPU:0, one launch (start us, length us, event | category | flops | bytes accessed | tf_op | source)
XLA Modules:
  0.0 85.8 jit_solution(14579076147695901937)
XLA Ops:
  2.2 4.1 %collective-permute-start.3 = (bf16[256,256]{1,0:T(8,128)(2,1)S(1)}, bf16[256,256]{1,0:T(8,128)(2,1)S(1)}, u32[]{:S(2)}, u32[]{:S(2)}) collective-permute-start(bf16[256,256]{1,0:T(8,128)(2,1)S(1)} %fusion.3.refs_1_.refs_7_), channel_id=1, source_target_pairs={{0,4},{1,5},{2,6},{3,7},{4,0},{5,1},{6,2},{7,3},{8,12},{9,13},{10,... | collective-permute-start | bytes 393224 | tf_op jit(solution)/shard_map/ppermute | solution.py:26
  7.2 1.6 %collective-permute-start = (f32[4,256]{1,0:T(4,128)S(1)}, f32[4,256]{1,0:T(4,128)S(1)}, u32[]{:S(2)}, u32[]{:S(2)}) collective-permute-start(f32[4,256]{1,0:T(4,128)S(1)} %get-tuple-element.46), channel_id=1, source_target_pairs={{0,1},{1,0},{2,3},{3,2},{4,5},{5,4},{6,7},{7,6},{8,9},{9,8},{10,11... | collective-permute-start | bytes 12296 | tf_op jit(solution)/shard_map/ppermute | solution.py:26
  8.7 1.6 %collective-permute-start.1 = (f32[4,256]{1,0:T(4,128)S(1)}, f32[4,256]{1,0:T(4,128)S(1)}, u32[]{:S(2)}, u32[]{:S(2)}) collective-permute-start(f32[4,256]{1,0:T(4,128)S(1)} %get-tuple-element.47), channel_id=1, source_target_pairs={{0,2},{1,3},{2,0},{3,1},{4,6},{5,7},{6,4},{7,5},{8,10},{9,11},{10,... | collective-permute-start | bytes 12296 | tf_op jit(solution)/shard_map/ppermute | solution.py:26
  10.7 3.3 %densify.2.refs_6_.refs_1_ = bf16[256,1152]{1,0:T(8,128)(2,1)S(1)} custom-call(s32[2,96]{1,0:T(2,128)S(1)} %fusion.15.words_ref, bf16[1,2,96,128,128]{4,3,2,1,0:T(8,128)(2,1)} %vals_ref.3), custom_call_target="tpu_custom_call" | custom-call | flops 31457280 | bytes 3145728 | tf_op jit(solution)/shard_map/densify/pallas_call | solution.py:71
  15.5 1.6 %collective-permute-start.5 = (bf16[256,256]{1,0:T(8,128)(2,1)S(1)}, bf16[256,256]{1,0:T(8,128)(2,1)S(1)}, u32[]{:S(2)}, u32[]{:S(2)}) collective-permute-start(bf16[256,256]{1,0:T(8,128)(2,1)S(1)} %get-tuple-element.52), channel_id=1, source_target_pairs={{0,2},{1,3},{2,0},{3,1},{4,6},{5,7},{6,4},{7,5},{8,10},{9,11},{10,... | collective-permute-start | bytes 393224 | tf_op jit(solution)/shard_map/ppermute | solution.py:26
  18.8 2.3 %collective-permute-done.4.refs_9_ = bf16[256,256]{1,0:T(8,128)(2,1)S(1)} collective-permute-done((bf16[256,256]{1,0:T(8,128)(2,1)S(1)}, bf16[256,256]{1,0:T(8,128)(2,1)S(1)}, u32[]{:S(2)}, u32[]{:S(2)}) %collective-permute-start.4) | collective-permute-done | bytes 131104 | tf_op jit(solution)/shard_map/ppermute | solution.py:26
  21.1 1.8 %collective-permute-done.6.refs_11_ = bf16[256,256]{1,0:T(8,128)(2,1)S(1)} collective-permute-done((bf16[256,256]{1,0:T(8,128)(2,1)S(1)}, bf16[256,256]{1,0:T(8,128)(2,1)S(1)}, u32[]{:S(2)}, u32[]{:S(2)}) %collective-permute-start.6) | collective-permute-done | bytes 131104 | tf_op jit(solution)/shard_map/ppermute | solution.py:26
  23.5 1.6 %collective-permute-start.7 = (bf16[256,256]{1,0:T(8,128)(2,1)S(1)}, bf16[256,256]{1,0:T(8,128)(2,1)S(1)}, u32[]{:S(2)}, u32[]{:S(2)}) collective-permute-start(bf16[256,256]{1,0:T(8,128)(2,1)S(1)} %get-tuple-element.54.refs_2_), channel_id=1, source_target_pairs={{0,4},{1,5},{2,6},{3,7},{4,0},{5,1},{6,2},{7,3},{8,12},{9,13},{10,... | collective-permute-start | bytes 393224 | tf_op jit(solution)/shard_map/ppermute | solution.py:26
  26.6 1.7 %collective-permute-start.12 = (bf16[128,256]{1,0:T(8,128)(2,1)S(1)}, bf16[128,256]{1,0:T(8,128)(2,1)S(1)}, u32[]{:S(2)}, u32[]{:S(2)}) collective-permute-start(bf16[128,256]{1,0:T(8,128)(2,1)S(1)} %get-tuple-element.59), channel_id=1, source_target_pairs={{0,2},{1,3},{2,0},{3,1},{4,6},{5,7},{6,4},{7,5},{8,10},{9,11},{10,... | collective-permute-start | bytes 196616 | tf_op jit(solution)/shard_map/ppermute | solution.py:26
  28.6 2.3 %collective-permute-done.7.refs_0_.refs_3_ = bf16[256,256]{1,0:T(8,128)(2,1)S(1)} collective-permute-done((bf16[256,256]{1,0:T(8,128)(2,1)S(1)}, bf16[256,256]{1,0:T(8,128)(2,1)S(1)}, u32[]{:S(2)}, u32[]{:S(2)}) %collective-permute-start.7) | collective-permute-done | bytes 131104 | tf_op jit(solution)/shard_map/ppermute | solution.py:26
  34.4 3.4 %densify.3.refs_6_.refs_1_ = bf16[256,1152]{1,0:T(8,128)(2,1)S(1)} custom-call(s32[2,96]{1,0:T(2,128)S(1)} %fusion.15.words_ref, bf16[1,2,96,128,128]{4,3,2,1,0:T(8,128)(2,1)} %vals_ref.3), custom_call_target="tpu_custom_call" | custom-call | flops 31457280 | bytes 3145728 | tf_op jit(solution)/shard_map/densify/pallas_call | solution.py:71
  38.7 4.4 %collective-permute-start.16 = (bf16[256,256]{1,0:T(8,128)(2,1)S(1)}, bf16[256,256]{1,0:T(8,128)(2,1)S(1)}, u32[]{:S(2)}, u32[]{:S(2)}) collective-permute-start(bf16[256,256]{1,0:T(8,128)(2,1)S(1)} %get-tuple-element.68), channel_id=1, source_target_pairs={{0,28},{1,29},{2,30},{3,31},{4,24},{5,25},{6,26},{7,27},{8,4},{9,5... | collective-permute-start | bytes 393224 | tf_op jit(solution)/shard_map/ppermute | solution.py:34
  43.9 4.9 %collective-permute-done.16.refs_0_.refs_8_ = bf16[256,256]{1,0:T(8,128)(2,1)S(1)} collective-permute-done((bf16[256,256]{1,0:T(8,128)(2,1)S(1)}, bf16[256,256]{1,0:T(8,128)(2,1)S(1)}, u32[]{:S(2)}, u32[]{:S(2)}) %collective-permute-start.16) | collective-permute-done | bytes 131104 | tf_op jit(solution)/shard_map/ppermute | solution.py:34
  50.1 2.3 %collective-permute-start.19 = (bf16[256,256]{1,0:T(8,128)(2,1)S(1)}, bf16[256,256]{1,0:T(8,128)(2,1)S(1)}, u32[]{:S(2)}, u32[]{:S(2)}) collective-permute-start(bf16[256,256]{1,0:T(8,128)(2,1)S(1)} %get-tuple-element.71), channel_id=1, source_target_pairs={{0,3},{1,2},{2,1},{3,0},{4,7},{5,6},{6,5},{7,4},{8,11},{9,10},{10,... | collective-permute-start | bytes 393224 | tf_op jit(solution)/shard_map/ppermute | solution.py:26
  52.7 2.6 %collective-permute-done.17.refs_9_ = bf16[256,256]{1,0:T(8,128)(2,1)S(1)} collective-permute-done((bf16[256,256]{1,0:T(8,128)(2,1)S(1)}, bf16[256,256]{1,0:T(8,128)(2,1)S(1)}, u32[]{:S(2)}, u32[]{:S(2)}) %collective-permute-start.17) | collective-permute-done | bytes 131104 | tf_op jit(solution)/shard_map/ppermute | solution.py:26
  55.3 4.0 %collective-permute-done.19.refs_11_ = bf16[256,256]{1,0:T(8,128)(2,1)S(1)} collective-permute-done((bf16[256,256]{1,0:T(8,128)(2,1)S(1)}, bf16[256,256]{1,0:T(8,128)(2,1)S(1)}, u32[]{:S(2)}, u32[]{:S(2)}) %collective-permute-start.19) | collective-permute-done | bytes 131104 | tf_op jit(solution)/shard_map/ppermute | solution.py:26
  60.6 1.5 %collective-permute-start.21 = (bf16[256,256]{1,0:T(8,128)(2,1)S(1)}, bf16[256,256]{1,0:T(8,128)(2,1)S(1)}, u32[]{:S(2)}, u32[]{:S(2)}) collective-permute-start(bf16[256,256]{1,0:T(8,128)(2,1)S(1)} %get-tuple-element.77), channel_id=1, source_target_pairs={{0,1},{1,0},{2,3},{3,2},{4,5},{5,4},{6,7},{7,6},{8,9},{9,8},{10,11... | collective-permute-start | bytes 393224 | tf_op jit(solution)/shard_map/ppermute | solution.py:26
  62.1 1.8 %collective-permute-start.22 = (bf16[256,256]{1,0:T(8,128)(2,1)S(1)}, bf16[256,256]{1,0:T(8,128)(2,1)S(1)}, u32[]{:S(2)}, u32[]{:S(2)}) collective-permute-start(bf16[256,256]{1,0:T(8,128)(2,1)S(1)} %get-tuple-element.78), channel_id=1, source_target_pairs={{0,2},{1,3},{2,0},{3,1},{4,6},{5,7},{6,4},{7,5},{8,10},{9,11},{10,... | collective-permute-start | bytes 393224 | tf_op jit(solution)/shard_map/ppermute | solution.py:26
  64.1 4.9 %collective-permute-done.20.refs_0_.refs_3_ = bf16[256,256]{1,0:T(8,128)(2,1)S(1)} collective-permute-done((bf16[256,256]{1,0:T(8,128)(2,1)S(1)}, bf16[256,256]{1,0:T(8,128)(2,1)S(1)}, u32[]{:S(2)}, u32[]{:S(2)}) %collective-permute-start.20) | collective-permute-done | bytes 131104 | tf_op jit(solution)/shard_map/ppermute | solution.py:26
  69.5 1.5 %collective-permute-done.22.refs_5_.refs_3_ = bf16[256,256]{1,0:T(8,128)(2,1)S(1)} collective-permute-done((bf16[256,256]{1,0:T(8,128)(2,1)S(1)}, bf16[256,256]{1,0:T(8,128)(2,1)S(1)}, u32[]{:S(2)}, u32[]{:S(2)}) %collective-permute-start.22) | collective-permute-done | bytes 131104 | tf_op jit(solution)/shard_map/ppermute | solution.py:26
  71.0 1.8 %collective-permute-done.23.refs_6_.refs_4_ = bf16[256,256]{1,0:T(8,128)(2,1)S(1)} collective-permute-done((bf16[256,256]{1,0:T(8,128)(2,1)S(1)}, bf16[256,256]{1,0:T(8,128)(2,1)S(1)}, u32[]{:S(2)}, u32[]{:S(2)}) %collective-permute-start.23) | collective-permute-done | bytes 131104 | tf_op jit(solution)/shard_map/ppermute | solution.py:26
  73.0 2.5 %collective-permute-start.25 = (bf16[128,256]{1,0:T(8,128)(2,1)S(1)}, bf16[128,256]{1,0:T(8,128)(2,1)S(1)}, u32[]{:S(2)}, u32[]{:S(2)}) collective-permute-start(bf16[128,256]{1,0:T(8,128)(2,1)S(1)} %get-tuple-element.81), channel_id=1, source_target_pairs={{0,2},{1,3},{2,0},{3,1},{4,6},{5,7},{6,4},{7,5},{8,10},{9,11},{10,... | collective-permute-start | bytes 196616 | tf_op jit(solution)/shard_map/ppermute | solution.py:26
  75.8 2.7 %collective-permute-done.27.far_ref = bf16[2,64,256]{2,1,0:T(8,128)(2,1)S(1)} collective-permute-done((bf16[2,64,256]{2,1,0:T(8,128)(2,1)S(1)}, bf16[2,64,256]{2,1,0:T(8,128)(2,1)S(1)}, u32[]{:S(2)}, u32[]{:S(2)}) %collective-permute-start.27) | collective-permute-done | bytes 65568 | tf_op jit(solution)/shard_map/ppermute | solution.py:26
  79.4 2.6 %collective-permute-start.30 = (bf16[2,64,256]{2,1,0:T(8,128)(2,1)S(1)}, bf16[2,64,256]{2,1,0:T(8,128)(2,1)S(1)}, u32[]{:S(2)}, u32[]{:S(2)}) collective-permute-start(bf16[2,64,256]{2,1,0:T(8,128)(2,1)S(1)} %total.1.refs_0_), channel_id=1, source_target_pairs={{0,3},{1,2},{2,1},{3,0},{4,7},{5,6},{6,5},{7,4},{8,11},{9,10},{10,... | collective-permute-start | bytes 196616 | tf_op jit(solution)/shard_map/ppermute | solution.py:26
  (72 shorter events, 21.8 us)
Async XLA Ops:
  2.2 12.6 %collective-permute-start.3 = (bf16[256,256]{1,0:T(8,128)(2,1)S(1)}, bf16[256,256]{1,0:T(8,128)(2,1)S(1)}, u32[]{:S(2)}, u32[]{:S(2)}) collective-permute-start(bf16[256,256]{1,0:T(8,128)(2,1)S(1)} %fusion.3.refs_1_.refs_7_), channel_id=1, source_target_pairs={{0,4},{1,5},{2,6},{3,7},{4,0},{5,1},{6,2},{7,3},{8,12},{9,13},{10,... | collective-permute-start | bytes 393224 | tf_op jit(solution)/shard_map/ppermute | solution.py:26
  7.2 6.9 %collective-permute-start = (f32[4,256]{1,0:T(4,128)S(1)}, f32[4,256]{1,0:T(4,128)S(1)}, u32[]{:S(2)}, u32[]{:S(2)}) collective-permute-start(f32[4,256]{1,0:T(4,128)S(1)} %get-tuple-element.46), channel_id=1, source_target_pairs={{0,1},{1,0},{2,3},{3,2},{4,5},{5,4},{6,7},{7,6},{8,9},{9,8},{10,11... | collective-permute-start | bytes 12296 | tf_op jit(solution)/shard_map/ppermute | solution.py:26
  14.9 6.2 %collective-permute-start.4 = (bf16[256,256]{1,0:T(8,128)(2,1)S(1)}, bf16[256,256]{1,0:T(8,128)(2,1)S(1)}, u32[]{:S(2)}, u32[]{:S(2)}) collective-permute-start(bf16[256,256]{1,0:T(8,128)(2,1)S(1)} %get-tuple-element.51), channel_id=1, source_target_pairs={{0,1},{1,0},{2,3},{3,2},{4,5},{5,4},{6,7},{7,6},{8,9},{9,8},{10,11... | collective-permute-start | bytes 393224 | tf_op jit(solution)/shard_map/ppermute | solution.py:26
  15.5 5.6 %collective-permute-start.5 = (bf16[256,256]{1,0:T(8,128)(2,1)S(1)}, bf16[256,256]{1,0:T(8,128)(2,1)S(1)}, u32[]{:S(2)}, u32[]{:S(2)}) collective-permute-start(bf16[256,256]{1,0:T(8,128)(2,1)S(1)} %get-tuple-element.52), channel_id=1, source_target_pairs={{0,2},{1,3},{2,0},{3,1},{4,6},{5,7},{6,4},{7,5},{8,10},{9,11},{10,... | collective-permute-start | bytes 393224 | tf_op jit(solution)/shard_map/ppermute | solution.py:26
  17.1 5.9 %collective-permute-start.6 = (bf16[256,256]{1,0:T(8,128)(2,1)S(1)}, bf16[256,256]{1,0:T(8,128)(2,1)S(1)}, u32[]{:S(2)}, u32[]{:S(2)}) collective-permute-start(bf16[256,256]{1,0:T(8,128)(2,1)S(1)} %get-tuple-element.53), channel_id=1, source_target_pairs={{0,3},{1,2},{2,1},{3,0},{4,7},{5,6},{6,5},{7,4},{8,11},{9,10},{10,... | collective-permute-start | bytes 393224 | tf_op jit(solution)/shard_map/ppermute | solution.py:26
  18.8 19.3 %collective-permute-start.14 = (bf16[512,256]{1,0:T(8,128)(2,1)S(1)}, bf16[512,256]{1,0:T(8,128)(2,1)S(1)}, u32[]{:S(2)}, u32[]{:S(2)}) collective-permute-start(bf16[512,256]{1,0:T(8,128)(2,1)S(1)} %pack.1), channel_id=1, source_target_pairs={{0,8},{8,16},{16,24},{24,0},{1,9},{9,17},{17,25},{25,1},{2,10},{10... | collective-permute-start | bytes 786440 | tf_op jit(solution)/shard_map/ppermute | solution.py:39
  23.5 7.4 %collective-permute-start.7 = (bf16[256,256]{1,0:T(8,128)(2,1)S(1)}, bf16[256,256]{1,0:T(8,128)(2,1)S(1)}, u32[]{:S(2)}, u32[]{:S(2)}) collective-permute-start(bf16[256,256]{1,0:T(8,128)(2,1)S(1)} %get-tuple-element.54.refs_2_), channel_id=1, source_target_pairs={{0,4},{1,5},{2,6},{3,7},{4,0},{5,1},{6,2},{7,3},{8,12},{9,13},{10,... | collective-permute-start | bytes 393224 | tf_op jit(solution)/shard_map/ppermute | solution.py:26
  25.1 7.2 %collective-permute-start.11 = (bf16[128,256]{1,0:T(8,128)(2,1)S(1)}, bf16[128,256]{1,0:T(8,128)(2,1)S(1)}, u32[]{:S(2)}, u32[]{:S(2)}) collective-permute-start(bf16[128,256]{1,0:T(8,128)(2,1)S(1)} %get-tuple-element.58), channel_id=1, source_target_pairs={{0,1},{1,0},{2,3},{3,2},{4,5},{5,4},{6,7},{7,6},{8,9},{9,8},{10,11... | collective-permute-start | bytes 196616 | tf_op jit(solution)/shard_map/ppermute | solution.py:26
  26.6 6.4 %collective-permute-start.12 = (bf16[128,256]{1,0:T(8,128)(2,1)S(1)}, bf16[128,256]{1,0:T(8,128)(2,1)S(1)}, u32[]{:S(2)}, u32[]{:S(2)}) collective-permute-start(bf16[128,256]{1,0:T(8,128)(2,1)S(1)} %get-tuple-element.59), channel_id=1, source_target_pairs={{0,2},{1,3},{2,0},{3,1},{4,6},{5,7},{6,4},{7,5},{8,10},{9,11},{10,... | collective-permute-start | bytes 196616 | tf_op jit(solution)/shard_map/ppermute | solution.py:26
  28.3 6.2 %collective-permute-start.13 = (bf16[128,256]{1,0:T(8,128)(2,1)S(1)}, bf16[128,256]{1,0:T(8,128)(2,1)S(1)}, u32[]{:S(2)}, u32[]{:S(2)}) collective-permute-start(bf16[128,256]{1,0:T(8,128)(2,1)S(1)} %get-tuple-element.60), channel_id=1, source_target_pairs={{0,3},{1,2},{2,1},{3,0},{4,7},{5,6},{6,5},{7,4},{8,11},{9,10},{10,... | collective-permute-start | bytes 196616 | tf_op jit(solution)/shard_map/ppermute | solution.py:26
  30.9 6.9 %collective-permute-start.8 = (bf16[128,256]{1,0:T(8,128)(2,1)S(1)}, bf16[128,256]{1,0:T(8,128)(2,1)S(1)}, u32[]{:S(2)}, u32[]{:S(2)}) collective-permute-start(bf16[128,256]{1,0:T(8,128)(2,1)S(1)} %get-tuple-element.55), channel_id=1, source_target_pairs={{0,1},{1,0},{2,3},{3,2},{4,5},{5,4},{6,7},{7,6},{8,9},{9,8},{10,11... | collective-permute-start | bytes 196616 | tf_op jit(solution)/shard_map/ppermute | solution.py:26
  38.7 10.2 %collective-permute-start.16 = (bf16[256,256]{1,0:T(8,128)(2,1)S(1)}, bf16[256,256]{1,0:T(8,128)(2,1)S(1)}, u32[]{:S(2)}, u32[]{:S(2)}) collective-permute-start(bf16[256,256]{1,0:T(8,128)(2,1)S(1)} %get-tuple-element.68), channel_id=1, source_target_pairs={{0,28},{1,29},{2,30},{3,31},{4,24},{5,25},{6,26},{7,27},{8,4},{9,5... | collective-permute-start | bytes 393224 | tf_op jit(solution)/shard_map/ppermute | solution.py:34
  48.9 6.4 %collective-permute-start.17 = (bf16[256,256]{1,0:T(8,128)(2,1)S(1)}, bf16[256,256]{1,0:T(8,128)(2,1)S(1)}, u32[]{:S(2)}, u32[]{:S(2)}) collective-permute-start(bf16[256,256]{1,0:T(8,128)(2,1)S(1)} %get-tuple-element.69), channel_id=1, source_target_pairs={{0,1},{1,0},{2,3},{3,2},{4,5},{5,4},{6,7},{7,6},{8,9},{9,8},{10,11... | collective-permute-start | bytes 393224 | tf_op jit(solution)/shard_map/ppermute | solution.py:26
  49.0 6.3 %collective-permute-start.18 = (bf16[256,256]{1,0:T(8,128)(2,1)S(1)}, bf16[256,256]{1,0:T(8,128)(2,1)S(1)}, u32[]{:S(2)}, u32[]{:S(2)}) collective-permute-start(bf16[256,256]{1,0:T(8,128)(2,1)S(1)} %get-tuple-element.70), channel_id=1, source_target_pairs={{0,2},{1,3},{2,0},{3,1},{4,6},{5,7},{6,4},{7,5},{8,10},{9,11},{10,... | collective-permute-start | bytes 393224 | tf_op jit(solution)/shard_map/ppermute | solution.py:26
  50.1 9.2 %collective-permute-start.19 = (bf16[256,256]{1,0:T(8,128)(2,1)S(1)}, bf16[256,256]{1,0:T(8,128)(2,1)S(1)}, u32[]{:S(2)}, u32[]{:S(2)}) collective-permute-start(bf16[256,256]{1,0:T(8,128)(2,1)S(1)} %get-tuple-element.71), channel_id=1, source_target_pairs={{0,3},{1,2},{2,1},{3,0},{4,7},{5,6},{6,5},{7,4},{8,11},{9,10},{10,... | collective-permute-start | bytes 393224 | tf_op jit(solution)/shard_map/ppermute | solution.py:26
  60.0 9.1 %collective-permute-start.20 = (bf16[256,256]{1,0:T(8,128)(2,1)S(1)}, bf16[256,256]{1,0:T(8,128)(2,1)S(1)}, u32[]{:S(2)}, u32[]{:S(2)}) collective-permute-start(bf16[256,256]{1,0:T(8,128)(2,1)S(1)} %get-tuple-element.76.refs_2_), channel_id=1, source_target_pairs={{0,4},{1,5},{2,6},{3,7},{4,0},{5,1},{6,2},{7,3},{8,12},{9,13},{10,... | collective-permute-start | bytes 393224 | tf_op jit(solution)/shard_map/ppermute | solution.py:26
  60.6 8.9 %collective-permute-start.21 = (bf16[256,256]{1,0:T(8,128)(2,1)S(1)}, bf16[256,256]{1,0:T(8,128)(2,1)S(1)}, u32[]{:S(2)}, u32[]{:S(2)}) collective-permute-start(bf16[256,256]{1,0:T(8,128)(2,1)S(1)} %get-tuple-element.77), channel_id=1, source_target_pairs={{0,1},{1,0},{2,3},{3,2},{4,5},{5,4},{6,7},{7,6},{8,9},{9,8},{10,11... | collective-permute-start | bytes 393224 | tf_op jit(solution)/shard_map/ppermute | solution.py:26
  62.1 8.9 %collective-permute-start.22 = (bf16[256,256]{1,0:T(8,128)(2,1)S(1)}, bf16[256,256]{1,0:T(8,128)(2,1)S(1)}, u32[]{:S(2)}, u32[]{:S(2)}) collective-permute-start(bf16[256,256]{1,0:T(8,128)(2,1)S(1)} %get-tuple-element.78), channel_id=1, source_target_pairs={{0,2},{1,3},{2,0},{3,1},{4,6},{5,7},{6,4},{7,5},{8,10},{9,11},{10,... | collective-permute-start | bytes 393224 | tf_op jit(solution)/shard_map/ppermute | solution.py:26
  63.9 8.9 %collective-permute-start.23 = (bf16[256,256]{1,0:T(8,128)(2,1)S(1)}, bf16[256,256]{1,0:T(8,128)(2,1)S(1)}, u32[]{:S(2)}, u32[]{:S(2)}) collective-permute-start(bf16[256,256]{1,0:T(8,128)(2,1)S(1)} %get-tuple-element.79), channel_id=1, source_target_pairs={{0,3},{1,2},{2,1},{3,0},{4,7},{5,6},{6,5},{7,4},{8,11},{9,10},{10,... | collective-permute-start | bytes 393224 | tf_op jit(solution)/shard_map/ppermute | solution.py:26
  69.1 10.4 %collective-permute-start.24 = (bf16[128,256]{1,0:T(8,128)(2,1)S(1)}, bf16[128,256]{1,0:T(8,128)(2,1)S(1)}, u32[]{:S(2)}, u32[]{:S(2)}) collective-permute-start(bf16[128,256]{1,0:T(8,128)(2,1)S(1)} %get-tuple-element.80), channel_id=1, source_target_pairs={{0,1},{1,0},{2,3},{3,2},{4,5},{5,4},{6,7},{7,6},{8,9},{9,8},{10,11... | collective-permute-start | bytes 196616 | tf_op jit(solution)/shard_map/ppermute | solution.py:26
  72.9 5.6 %collective-permute-start.27 = (bf16[2,64,256]{2,1,0:T(8,128)(2,1)S(1)}, bf16[2,64,256]{2,1,0:T(8,128)(2,1)S(1)}, u32[]{:S(2)}, u32[]{:S(2)}) collective-permute-start(bf16[2,64,256]{2,1,0:T(8,128)(2,1)S(1)} %half_sum.1.mine_ref), channel_id=1, source_target_pairs={{0,4},{1,5},{2,6},{3,7},{4,0},{5,1},{6,2},{7,3},{8,12},{9,13},{10,... | collective-permute-start | bytes 196616 | tf_op jit(solution)/shard_map/ppermute | solution.py:26
  73.0 9.9 %collective-permute-start.25 = (bf16[128,256]{1,0:T(8,128)(2,1)S(1)}, bf16[128,256]{1,0:T(8,128)(2,1)S(1)}, u32[]{:S(2)}, u32[]{:S(2)}) collective-permute-start(bf16[128,256]{1,0:T(8,128)(2,1)S(1)} %get-tuple-element.81), channel_id=1, source_target_pairs={{0,2},{1,3},{2,0},{3,1},{4,6},{5,7},{6,4},{7,5},{8,10},{9,11},{10,... | collective-permute-start | bytes 196616 | tf_op jit(solution)/shard_map/ppermute | solution.py:26
  75.4 7.4 %collective-permute-start.26 = (bf16[128,256]{1,0:T(8,128)(2,1)S(1)}, bf16[128,256]{1,0:T(8,128)(2,1)S(1)}, u32[]{:S(2)}, u32[]{:S(2)}) collective-permute-start(bf16[128,256]{1,0:T(8,128)(2,1)S(1)} %get-tuple-element.82), channel_id=1, source_target_pairs={{0,3},{1,2},{2,1},{3,0},{4,7},{5,6},{6,5},{7,4},{8,11},{9,10},{10,... | collective-permute-start | bytes 196616 | tf_op jit(solution)/shard_map/ppermute | solution.py:26
  79.4 5.5 %collective-permute-start.30 = (bf16[2,64,256]{2,1,0:T(8,128)(2,1)S(1)}, bf16[2,64,256]{2,1,0:T(8,128)(2,1)S(1)}, u32[]{:S(2)}, u32[]{:S(2)}) collective-permute-start(bf16[2,64,256]{2,1,0:T(8,128)(2,1)S(1)} %total.1.refs_0_), channel_id=1, source_target_pairs={{0,3},{1,2},{2,1},{3,0},{4,7},{5,6},{6,5},{7,4},{8,11},{9,10},{10,... | collective-permute-start | bytes 196616 | tf_op jit(solution)/shard_map/ppermute | solution.py:26
  (12 other events, 153.3 us)

commit v18 on v16

--- a/solution.py
+++ b/solution.py
@@ -432,6 +432,12 @@
                 product = jnp.dot(masked, weights[0, layer].T, preferred_element_type=F32)
                 image = ((1.0 - beta) * masked.astype(F32) + beta * product).astype(BF16)
             else:
+                if turned is not None:
+                    lowered_far = lowered(turned[0], h)
+                    nearest, *others = shared(turned[1:], lowered)
+                    lowered_far, *others = lax.optimization_barrier((lowered_far, *others))
+                    passed, nearest = lax.optimization_barrier((passed, nearest))
+                    lowered_near = [nearest, *others]
                 call = Call()
                 call.give(VMEM, preact, weights, names, *asked)
                 if entry:
@@ -467,12 +473,8 @@
                     pending = results.take(h - 1) + pending
                 kept = masked = results.take()
             if turned is not None:
-                far = lowered(turned[0], h)
-                near = shared(turned[1:], lowered)
-                far, *near = lax.optimization_barrier((far, *near))
+                far, near = lowered_far, lowered_near
                 turned = None
-                if final:
-                    parts = shared(sends)
             else:
                 far = swapped(image, h)
                 near = [] if c["first"] else shared(sends)

time: 83.1 us -> 83.4 us (level)
  waiting for transfers between devices: 20.9 us -> 23.6 us
  starting transfers between devices: 44.8 us -> 43.3 us
  Pallas kernels: 10.8 us -> 9.63 us
    ppermute x28, waiting for transfers between devices: 17.5 us -> 21.8 us  [swapped(): return lax.ppermute(block, 'rows', [(i, i ^ k) for i in range(n)])]
    ppermute x28, starting transfers between devices: 37.5 us -> 35.9 us  [swapped(): return lax.ppermute(block, 'rows', [(i, i ^ k) for i in range(n)])]
    ppermute x5, waiting for transfers between devices: 3.34 us -> 1.82 us  [lowered(): return lax.ppermute(block, ('section', 'rows'), route)]
    pallas_call x16, Pallas kernels: 10.8 us -> 9.63 us  [run(): pl.pallas_call(kernel, out_shape=self.outs, in_specs=self.specs, out_spec...]
  transfers between devices with their start and end apart: 34 -> 34, of which waited for: 15 -> 14; matrix products, arithmetic and copies ran while one was open for 5% -> 5% of each run, Pallas kernels for 11% -> 9%
where the time goes in v18:
time: 83.4 us; the launch traced here: 83.1 us
  starting transfers between devices  43.3 us (52%)
  waiting for transfers between devices  23.6 us (28%)
  Pallas kernels  9.63 us (12%)
  matrix products  2.6 us (3%)
  other arithmetic  1.67 us (2%)
  local copies, waits for them, and re-layouts  1.1 us (1%)
  between operations  1.07 us (1%)
    ppermute x28, starting transfers between devices, swapped(): return lax.ppermute(block, 'rows', [(i, i ^ k) for i in range(n)])  35.9 us
    ppermute x28, waiting for transfers between devices, swapped(): return lax.ppermute(block, 'rows', [(i, i ^ k) for i in range(n)])  21.8 us
    pallas_call x16, Pallas kernels, run(): pl.pallas_call(kernel, out_shape=self.outs, in_specs=self.specs, out_spec...  9.63 us
    ppermute x5, starting transfers between devices, lowered(): return lax.ppermute(block, ('section', 'rows'), route)  7.38 us
    ppermute x5, waiting for transfers between devices, lowered(): return lax.ppermute(block, ('section', 'rows'), route)  1.82 us
  transfers between devices with their start and end apart: 34, of which 14 were waited for; matrix products, arithmetic and copies ran while one was open for 5% of the time, Pallas kernels for 9%

profile of v18, /device:TPU:0, one launch (start us, length us, event | category | flops | bytes accessed | tf_op | source)
XLA Modules:
  0.0 83.1 jit_solution(8903328794247925523)
XLA Ops:
  2.2 4.1 %collective-permute-start.3 = (bf16[256,256]{1,0:T(8,128)(2,1)S(1)}, bf16[256,256]{1,0:T(8,128)(2,1)S(1)}, u32[]{:S(2)}, u32[]{:S(2)}) collective-permute-start(bf16[256,256]{1,0:T(8,128)(2,1)S(1)} %fusion.3.refs_1_.refs_7_), channel_id=1, source_target_pairs={{0,4},{1,5},{2,6},{3,7},{4,0},{5,1},{6,2},{7,3},{8,12},{9,13},{10,... | collective-permute-start | bytes 393224 | tf_op jit(solution)/shard_map/ppermute | solution.py:26
  7.2 1.6 %collective-permute-start = (f32[4,256]{1,0:T(4,128)S(1)}, f32[4,256]{1,0:T(4,128)S(1)}, u32[]{:S(2)}, u32[]{:S(2)}) collective-permute-start(f32[4,256]{1,0:T(4,128)S(1)} %get-tuple-element.54), channel_id=1, source_target_pairs={{0,1},{1,0},{2,3},{3,2},{4,5},{5,4},{6,7},{7,6},{8,9},{9,8},{10,11... | collective-permute-start | bytes 12296 | tf_op jit(solution)/shard_map/ppermute | solution.py:26
  8.7 1.6 %collective-permute-start.1 = (f32[4,256]{1,0:T(4,128)S(1)}, f32[4,256]{1,0:T(4,128)S(1)}, u32[]{:S(2)}, u32[]{:S(2)}) collective-permute-start(f32[4,256]{1,0:T(4,128)S(1)} %get-tuple-element.55), channel_id=1, source_target_pairs={{0,2},{1,3},{2,0},{3,1},{4,6},{5,7},{6,4},{7,5},{8,10},{9,11},{10,... | collective-permute-start | bytes 12296 | tf_op jit(solution)/shard_map/ppermute | solution.py:26
  10.7 2.5 %densify.2.refs_6_.refs_1_ = bf16[256,1152]{1,0:T(8,128)(2,1)S(1)} custom-call(s32[2,96]{1,0:T(2,128)S(1)} %fusion.15.words_ref, bf16[1,2,96,128,128]{4,3,2,1,0:T(8,128)(2,1)} %vals_ref.3), custom_call_target="tpu_custom_call" | custom-call | flops 31457280 | bytes 3145728 | tf_op jit(solution)/shard_map/densify/pallas_call | solution.py:71
  13.3 1.5 %collective-permute-done.2.refs_4_.refs_5_.refs_3_.refs_2_ = f32[4,256]{1,0:T(4,128)S(1)} collective-permute-done((f32[4,256]{1,0:T(4,128)S(1)}, f32[4,256]{1,0:T(4,128)S(1)}, u32[]{:S(2)}, u32[]{:S(2)}) %collective-permute-start.2) | collective-permute-done | bytes 4128 | tf_op jit(solution)/shard_map/ppermute | solution.py:26
  15.5 1.8 %collective-permute-start.5 = (bf16[256,256]{1,0:T(8,128)(2,1)S(1)}, bf16[256,256]{1,0:T(8,128)(2,1)S(1)}, u32[]{:S(2)}, u32[]{:S(2)}) collective-permute-start(bf16[256,256]{1,0:T(8,128)(2,1)S(1)} %get-tuple-element.60), channel_id=1, source_target_pairs={{0,2},{1,3},{2,0},{3,1},{4,6},{5,7},{6,4},{7,5},{8,10},{9,11},{10,... | collective-permute-start | bytes 393224 | tf_op jit(solution)/shard_map/ppermute | solution.py:26
  18.8 2.5 %collective-permute-done.4.refs_9_ = bf16[256,256]{1,0:T(8,128)(2,1)S(1)} collective-permute-done((bf16[256,256]{1,0:T(8,128)(2,1)S(1)}, bf16[256,256]{1,0:T(8,128)(2,1)S(1)}, u32[]{:S(2)}, u32[]{:S(2)}) %collective-permute-start.4) | collective-permute-done | bytes 131104 | tf_op jit(solution)/shard_map/ppermute | solution.py:26
  21.3 1.9 %collective-permute-done.6.refs_11_ = bf16[256,256]{1,0:T(8,128)(2,1)S(1)} collective-permute-done((bf16[256,256]{1,0:T(8,128)(2,1)S(1)}, bf16[256,256]{1,0:T(8,128)(2,1)S(1)}, u32[]{:S(2)}, u32[]{:S(2)}) %collective-permute-start.6) | collective-permute-done | bytes 131104 | tf_op jit(solution)/shard_map/ppermute | solution.py:26
  26.6 1.7 %collective-permute-start.12 = (bf16[128,256]{1,0:T(8,128)(2,1)S(1)}, bf16[128,256]{1,0:T(8,128)(2,1)S(1)}, u32[]{:S(2)}, u32[]{:S(2)}) collective-permute-start(bf16[128,256]{1,0:T(8,128)(2,1)S(1)} %get-tuple-element.67), channel_id=1, source_target_pairs={{0,2},{1,3},{2,0},{3,1},{4,6},{5,7},{6,4},{7,5},{8,10},{9,11},{10,... | collective-permute-start | bytes 196616 | tf_op jit(solution)/shard_map/ppermute | solution.py:26
  28.6 2.5 %collective-permute-done.7.refs_0_.refs_3_ = bf16[256,256]{1,0:T(8,128)(2,1)S(1)} collective-permute-done((bf16[256,256]{1,0:T(8,128)(2,1)S(1)}, bf16[256,256]{1,0:T(8,128)(2,1)S(1)}, u32[]{:S(2)}, u32[]{:S(2)}) %collective-permute-start.7) | collective-permute-done | bytes 131104 | tf_op jit(solution)/shard_map/ppermute | solution.py:26
  32.9 1.7 %collective-permute-start.10 = (bf16[128,256]{1,0:T(8,128)(2,1)S(1)}, bf16[128,256]{1,0:T(8,128)(2,1)S(1)}, u32[]{:S(2)}, u32[]{:S(2)}) collective-permute-start(bf16[128,256]{1,0:T(8,128)(2,1)S(1)} %get-tuple-element.65), channel_id=1, source_target_pairs={{0,3},{1,2},{2,1},{3,0},{4,7},{5,6},{6,5},{7,4},{8,11},{9,10},{10,... | collective-permute-start | bytes 196616 | tf_op jit(solution)/shard_map/ppermute | solution.py:26
  34.7 2.7 %densify.3.refs_6_.refs_1_ = bf16[256,1152]{1,0:T(8,128)(2,1)S(1)} custom-call(s32[2,96]{1,0:T(2,128)S(1)} %fusion.15.words_ref, bf16[1,2,96,128,128]{4,3,2,1,0:T(8,128)(2,1)} %vals_ref.3), custom_call_target="tpu_custom_call" | custom-call | flops 31457280 | bytes 3145728 | tf_op jit(solution)/shard_map/densify/pallas_call | solution.py:71
  38.6 1.7 %collective-permute-start.17 = (bf16[256,256]{1,0:T(8,128)(2,1)S(1)}, bf16[256,256]{1,0:T(8,128)(2,1)S(1)}, u32[]{:S(2)}, u32[]{:S(2)}) collective-permute-start(bf16[256,256]{1,0:T(8,128)(2,1)S(1)} %get-tuple-element.78), channel_id=1, source_target_pairs={{0,28},{1,29},{2,30},{3,31},{4,24},{5,25},{6,26},{7,27},{8,4},{9,5... | collective-permute-start | bytes 393224 | tf_op jit(solution)/shard_map/ppermute | solution.py:34
  40.3 2.6 %collective-permute-start.18 = (bf16[128,256]{1,0:T(8,128)(2,1)S(1)}, bf16[128,256]{1,0:T(8,128)(2,1)S(1)}, u32[]{:S(2)}, u32[]{:S(2)}) collective-permute-start(bf16[128,256]{1,0:T(8,128)(2,1)S(1)} %get-tuple-element.79), channel_id=1, source_target_pairs={{0,26},{1,27},{2,24},{3,25},{4,30},{5,31},{6,28},{7,29},{8,2},{9,3... | collective-permute-start | bytes 196616 | tf_op jit(solution)/shard_map/ppermute | solution.py:34
  45.5 1.5 %collective-permute-start.15 = (bf16[256,256]{1,0:T(8,128)(2,1)S(1)}, bf16[256,256]{1,0:T(8,128)(2,1)S(1)}, u32[]{:S(2)}, u32[]{:S(2)}) collective-permute-start(bf16[256,256]{1,0:T(8,128)(2,1)S(1)} %get-tuple-element.74.refs_10_), channel_id=1, source_target_pairs={{0,24},{1,25},{2,26},{3,27},{4,28},{5,29},{6,30},{7,31},{8,0},{9,1... | collective-permute-start | bytes 393224 | tf_op jit(solution)/shard_map/ppermute | solution.py:34
  48.1 1.8 %collective-permute-done.19.refs_11_ = bf16[128,256]{1,0:T(8,128)(2,1)S(1)} collective-permute-done((bf16[128,256]{1,0:T(8,128)(2,1)S(1)}, bf16[128,256]{1,0:T(8,128)(2,1)S(1)}, u32[]{:S(2)}, u32[]{:S(2)}) %collective-permute-start.19) | collective-permute-done | bytes 65568 | tf_op jit(solution)/shard_map/ppermute | solution.py:34
  51.2 2.3 %collective-permute-start.22 = (bf16[128,256]{1,0:T(8,128)(2,1)S(1)}, bf16[128,256]{1,0:T(8,128)(2,1)S(1)}, u32[]{:S(2)}, u32[]{:S(2)}) collective-permute-start(bf16[128,256]{1,0:T(8,128)(2,1)S(1)} %get-tuple-element.87), channel_id=1, source_target_pairs={{0,3},{1,2},{2,1},{3,0},{4,7},{5,6},{6,5},{7,4},{8,11},{9,10},{10,... | collective-permute-start | bytes 196616 | tf_op jit(solution)/shard_map/ppermute | solution.py:26
  54.3 1.9 %collective-permute-done.21.refs_13_ = bf16[128,256]{1,0:T(8,128)(2,1)S(1)} collective-permute-done((bf16[128,256]{1,0:T(8,128)(2,1)S(1)}, bf16[128,256]{1,0:T(8,128)(2,1)S(1)}, u32[]{:S(2)}, u32[]{:S(2)}) %collective-permute-start.21) | collective-permute-done | bytes 65568 | tf_op jit(solution)/shard_map/ppermute | solution.py:26
  60.5 1.6 %collective-permute-start.26 = (bf16[256,256]{1,0:T(8,128)(2,1)S(1)}, bf16[256,256]{1,0:T(8,128)(2,1)S(1)}, u32[]{:S(2)}, u32[]{:S(2)}) collective-permute-start(bf16[256,256]{1,0:T(8,128)(2,1)S(1)} %get-tuple-element.95), channel_id=1, source_target_pairs={{0,3},{1,2},{2,1},{3,0},{4,7},{5,6},{6,5},{7,4},{8,11},{9,10},{10,... | collective-permute-start | bytes 393224 | tf_op jit(solution)/shard_map/ppermute | solution.py:26
  62.2 3.8 %collective-permute-done.23.refs_0_.refs_3_ = bf16[256,256]{1,0:T(8,128)(2,1)S(1)} collective-permute-done((bf16[256,256]{1,0:T(8,128)(2,1)S(1)}, bf16[256,256]{1,0:T(8,128)(2,1)S(1)}, u32[]{:S(2)}, u32[]{:S(2)}) %collective-permute-start.23) | collective-permute-done | bytes 131104 | tf_op jit(solution)/shard_map/ppermute | solution.py:26
  67.6 2.5 %collective-permute-done.26.refs_6_.refs_4_ = bf16[256,256]{1,0:T(8,128)(2,1)S(1)} collective-permute-done((bf16[256,256]{1,0:T(8,128)(2,1)S(1)}, bf16[256,256]{1,0:T(8,128)(2,1)S(1)}, u32[]{:S(2)}, u32[]{:S(2)}) %collective-permute-start.26) | collective-permute-done | bytes 131104 | tf_op jit(solution)/shard_map/ppermute | solution.py:26
  71.9 1.9 %collective-permute-start.29 = (bf16[128,256]{1,0:T(8,128)(2,1)S(1)}, bf16[128,256]{1,0:T(8,128)(2,1)S(1)}, u32[]{:S(2)}, u32[]{:S(2)}) collective-permute-start(bf16[128,256]{1,0:T(8,128)(2,1)S(1)} %get-tuple-element.98), channel_id=1, source_target_pairs={{0,3},{1,2},{2,1},{3,0},{4,7},{5,6},{6,5},{7,4},{8,11},{9,10},{10,... | collective-permute-start | bytes 196616 | tf_op jit(solution)/shard_map/ppermute | solution.py:26
  73.8 2.0 %collective-permute-done.30.far_ref = bf16[2,64,256]{2,1,0:T(8,128)(2,1)S(1)} collective-permute-done((bf16[2,64,256]{2,1,0:T(8,128)(2,1)S(1)}, bf16[2,64,256]{2,1,0:T(8,128)(2,1)S(1)}, u32[]{:S(2)}, u32[]{:S(2)}) %collective-permute-start.30) | collective-permute-done | bytes 65568 | tf_op jit(solution)/shard_map/ppermute | solution.py:26
  76.7 2.6 %collective-permute-start.33 = (bf16[2,64,256]{2,1,0:T(8,128)(2,1)S(1)}, bf16[2,64,256]{2,1,0:T(8,128)(2,1)S(1)}, u32[]{:S(2)}, u32[]{:S(2)}) collective-permute-start(bf16[2,64,256]{2,1,0:T(8,128)(2,1)S(1)} %total.1.refs_0_), channel_id=1, source_target_pairs={{0,3},{1,2},{2,1},{3,0},{4,7},{5,6},{6,5},{7,4},{8,11},{9,10},{10,... | collective-permute-start | bytes 196616 | tf_op jit(solution)/shard_map/ppermute | solution.py:26
  (78 shorter events, 29.9 us)
Async XLA Ops:
  2.2 12.6 %collective-permute-start.3 = (bf16[256,256]{1,0:T(8,128)(2,1)S(1)}, bf16[256,256]{1,0:T(8,128)(2,1)S(1)}, u32[]{:S(2)}, u32[]{:S(2)}) collective-permute-start(bf16[256,256]{1,0:T(8,128)(2,1)S(1)} %fusion.3.refs_1_.refs_7_), channel_id=1, source_target_pairs={{0,4},{1,5},{2,6},{3,7},{4,0},{5,1},{6,2},{7,3},{8,12},{9,13},{10,... | collective-permute-start | bytes 393224 | tf_op jit(solution)/shard_map/ppermute | solution.py:26
  7.2 6.1 %collective-permute-start = (f32[4,256]{1,0:T(4,128)S(1)}, f32[4,256]{1,0:T(4,128)S(1)}, u32[]{:S(2)}, u32[]{:S(2)}) collective-permute-start(f32[4,256]{1,0:T(4,128)S(1)} %get-tuple-element.54), channel_id=1, source_target_pairs={{0,1},{1,0},{2,3},{3,2},{4,5},{5,4},{6,7},{7,6},{8,9},{9,8},{10,11... | collective-permute-start | bytes 12296 | tf_op jit(solution)/shard_map/ppermute | solution.py:26
  14.9 6.4 %collective-permute-start.4 = (bf16[256,256]{1,0:T(8,128)(2,1)S(1)}, bf16[256,256]{1,0:T(8,128)(2,1)S(1)}, u32[]{:S(2)}, u32[]{:S(2)}) collective-permute-start(bf16[256,256]{1,0:T(8,128)(2,1)S(1)} %get-tuple-element.59), channel_id=1, source_target_pairs={{0,1},{1,0},{2,3},{3,2},{4,5},{5,4},{6,7},{7,6},{8,9},{9,8},{10,11... | collective-permute-start | bytes 393224 | tf_op jit(solution)/shard_map/ppermute | solution.py:26
  15.5 5.8 %collective-permute-start.5 = (bf16[256,256]{1,0:T(8,128)(2,1)S(1)}, bf16[256,256]{1,0:T(8,128)(2,1)S(1)}, u32[]{:S(2)}, u32[]{:S(2)}) collective-permute-start(bf16[256,256]{1,0:T(8,128)(2,1)S(1)} %get-tuple-element.60), channel_id=1, source_target_pairs={{0,2},{1,3},{2,0},{3,1},{4,6},{5,7},{6,4},{7,5},{8,10},{9,11},{10,... | collective-permute-start | bytes 393224 | tf_op jit(solution)/shard_map/ppermute | solution.py:26
  17.2 5.9 %collective-permute-start.6 = (bf16[256,256]{1,0:T(8,128)(2,1)S(1)}, bf16[256,256]{1,0:T(8,128)(2,1)S(1)}, u32[]{:S(2)}, u32[]{:S(2)}) collective-permute-start(bf16[256,256]{1,0:T(8,128)(2,1)S(1)} %get-tuple-element.61), channel_id=1, source_target_pairs={{0,3},{1,2},{2,1},{3,0},{4,7},{5,6},{6,5},{7,4},{8,11},{9,10},{10,... | collective-permute-start | bytes 393224 | tf_op jit(solution)/shard_map/ppermute | solution.py:26
  18.8 19.3 %collective-permute-start.14 = (bf16[528,256]{1,0:T(8,128)(2,1)S(1)}, bf16[528,256]{1,0:T(8,128)(2,1)S(1)}, u32[]{:S(2)}, u32[]{:S(2)}) collective-permute-start(bf16[528,256]{1,0:T(8,128)(2,1)S(1)} %pack.1), channel_id=1, source_target_pairs={{0,8},{8,16},{16,24},{24,0},{1,9},{9,17},{17,25},{25,1},{2,10},{10... | collective-permute-start | bytes 811016 | tf_op jit(solution)/shard_map/ppermute | solution.py:39
  23.7 7.4 %collective-permute-start.7 = (bf16[256,256]{1,0:T(8,128)(2,1)S(1)}, bf16[256,256]{1,0:T(8,128)(2,1)S(1)}, u32[]{:S(2)}, u32[]{:S(2)}) collective-permute-start(bf16[256,256]{1,0:T(8,128)(2,1)S(1)} %get-tuple-element.62.refs_2_), channel_id=1, source_target_pairs={{0,4},{1,5},{2,6},{3,7},{4,0},{5,1},{6,2},{7,3},{8,12},{9,13},{10,... | collective-permute-start | bytes 393224 | tf_op jit(solution)/shard_map/ppermute | solution.py:26
  25.1 7.2 %collective-permute-start.11 = (bf16[128,256]{1,0:T(8,128)(2,1)S(1)}, bf16[128,256]{1,0:T(8,128)(2,1)S(1)}, u32[]{:S(2)}, u32[]{:S(2)}) collective-permute-start(bf16[128,256]{1,0:T(8,128)(2,1)S(1)} %get-tuple-element.66), channel_id=1, source_target_pairs={{0,1},{1,0},{2,3},{3,2},{4,5},{5,4},{6,7},{7,6},{8,9},{9,8},{10,11... | collective-permute-start | bytes 196616 | tf_op jit(solution)/shard_map/ppermute | solution.py:26
  26.6 6.4 %collective-permute-start.12 = (bf16[128,256]{1,0:T(8,128)(2,1)S(1)}, bf16[128,256]{1,0:T(8,128)(2,1)S(1)}, u32[]{:S(2)}, u32[]{:S(2)}) collective-permute-start(bf16[128,256]{1,0:T(8,128)(2,1)S(1)} %get-tuple-element.67), channel_id=1, source_target_pairs={{0,2},{1,3},{2,0},{3,1},{4,6},{5,7},{6,4},{7,5},{8,10},{9,11},{10,... | collective-permute-start | bytes 196616 | tf_op jit(solution)/shard_map/ppermute | solution.py:26
  28.3 6.4 %collective-permute-start.13 = (bf16[128,256]{1,0:T(8,128)(2,1)S(1)}, bf16[128,256]{1,0:T(8,128)(2,1)S(1)}, u32[]{:S(2)}, u32[]{:S(2)}) collective-permute-start(bf16[128,256]{1,0:T(8,128)(2,1)S(1)} %get-tuple-element.68), channel_id=1, source_target_pairs={{0,3},{1,2},{2,1},{3,0},{4,7},{5,6},{6,5},{7,4},{8,11},{9,10},{10,... | collective-permute-start | bytes 196616 | tf_op jit(solution)/shard_map/ppermute | solution.py:26
  31.1 6.3 %collective-permute-start.8 = (bf16[128,256]{1,0:T(8,128)(2,1)S(1)}, bf16[128,256]{1,0:T(8,128)(2,1)S(1)}, u32[]{:S(2)}, u32[]{:S(2)}) collective-permute-start(bf16[128,256]{1,0:T(8,128)(2,1)S(1)} %get-tuple-element.63), channel_id=1, source_target_pairs={{0,1},{1,0},{2,3},{3,2},{4,5},{5,4},{6,7},{7,6},{8,9},{9,8},{10,11... | collective-permute-start | bytes 196616 | tf_op jit(solution)/shard_map/ppermute | solution.py:26
  38.6 11.3 %collective-permute-start.17 = (bf16[256,256]{1,0:T(8,128)(2,1)S(1)}, bf16[256,256]{1,0:T(8,128)(2,1)S(1)}, u32[]{:S(2)}, u32[]{:S(2)}) collective-permute-start(bf16[256,256]{1,0:T(8,128)(2,1)S(1)} %get-tuple-element.78), channel_id=1, source_target_pairs={{0,28},{1,29},{2,30},{3,31},{4,24},{5,25},{6,26},{7,27},{8,4},{9,5... | collective-permute-start | bytes 393224 | tf_op jit(solution)/shard_map/ppermute | solution.py:34
  40.3 7.8 %collective-permute-start.18 = (bf16[128,256]{1,0:T(8,128)(2,1)S(1)}, bf16[128,256]{1,0:T(8,128)(2,1)S(1)}, u32[]{:S(2)}, u32[]{:S(2)}) collective-permute-start(bf16[128,256]{1,0:T(8,128)(2,1)S(1)} %get-tuple-element.79), channel_id=1, source_target_pairs={{0,26},{1,27},{2,24},{3,25},{4,30},{5,31},{6,28},{7,29},{8,2},{9,3... | collective-permute-start | bytes 196616 | tf_op jit(solution)/shard_map/ppermute | solution.py:34
  42.9 7.0 %collective-permute-start.19 = (bf16[128,256]{1,0:T(8,128)(2,1)S(1)}, bf16[128,256]{1,0:T(8,128)(2,1)S(1)}, u32[]{:S(2)}, u32[]{:S(2)}) collective-permute-start(bf16[128,256]{1,0:T(8,128)(2,1)S(1)} %get-tuple-element.80), channel_id=1, source_target_pairs={{0,27},{1,26},{2,25},{3,24},{4,31},{5,30},{6,29},{7,28},{8,3},{9,2... | collective-permute-start | bytes 196616 | tf_op jit(solution)/shard_map/ppermute | solution.py:34
  45.5 8.2 %collective-permute-start.15 = (bf16[256,256]{1,0:T(8,128)(2,1)S(1)}, bf16[256,256]{1,0:T(8,128)(2,1)S(1)}, u32[]{:S(2)}, u32[]{:S(2)}) collective-permute-start(bf16[256,256]{1,0:T(8,128)(2,1)S(1)} %get-tuple-element.74.refs_10_), channel_id=1, source_target_pairs={{0,24},{1,25},{2,26},{3,27},{4,28},{5,29},{6,30},{7,31},{8,0},{9,1... | collective-permute-start | bytes 393224 | tf_op jit(solution)/shard_map/ppermute | solution.py:34
  47.1 6.7 %collective-permute-start.16 = (bf16[128,256]{1,0:T(8,128)(2,1)S(1)}, bf16[128,256]{1,0:T(8,128)(2,1)S(1)}, u32[]{:S(2)}, u32[]{:S(2)}) collective-permute-start(bf16[128,256]{1,0:T(8,128)(2,1)S(1)} %get-tuple-element.75), channel_id=1, source_target_pairs={{0,25},{1,24},{2,27},{3,26},{4,29},{5,28},{6,31},{7,30},{8,1},{9,0... | collective-permute-start | bytes 196616 | tf_op jit(solution)/shard_map/ppermute | solution.py:34
  51.2 5.9 %collective-permute-start.22 = (bf16[128,256]{1,0:T(8,128)(2,1)S(1)}, bf16[128,256]{1,0:T(8,128)(2,1)S(1)}, u32[]{:S(2)}, u32[]{:S(2)}) collective-permute-start(bf16[128,256]{1,0:T(8,128)(2,1)S(1)} %get-tuple-element.87), channel_id=1, source_target_pairs={{0,3},{1,2},{2,1},{3,0},{4,7},{5,6},{6,5},{7,4},{8,11},{9,10},{10,... | collective-permute-start | bytes 196616 | tf_op jit(solution)/shard_map/ppermute | solution.py:26
  57.8 8.3 %collective-permute-start.23 = (bf16[256,256]{1,0:T(8,128)(2,1)S(1)}, bf16[256,256]{1,0:T(8,128)(2,1)S(1)}, u32[]{:S(2)}, u32[]{:S(2)}) collective-permute-start(bf16[256,256]{1,0:T(8,128)(2,1)S(1)} %get-tuple-element.92.refs_2_), channel_id=1, source_target_pairs={{0,4},{1,5},{2,6},{3,7},{4,0},{5,1},{6,2},{7,3},{8,12},{9,13},{10,... | collective-permute-start | bytes 393224 | tf_op jit(solution)/shard_map/ppermute | solution.py:26
  58.7 8.5 %collective-permute-start.24 = (bf16[256,256]{1,0:T(8,128)(2,1)S(1)}, bf16[256,256]{1,0:T(8,128)(2,1)S(1)}, u32[]{:S(2)}, u32[]{:S(2)}) collective-permute-start(bf16[256,256]{1,0:T(8,128)(2,1)S(1)} %get-tuple-element.93), channel_id=1, source_target_pairs={{0,1},{1,0},{2,3},{3,2},{4,5},{5,4},{6,7},{7,6},{8,9},{9,8},{10,11... | collective-permute-start | bytes 393224 | tf_op jit(solution)/shard_map/ppermute | solution.py:26
  59.5 8.0 %collective-permute-start.25 = (bf16[256,256]{1,0:T(8,128)(2,1)S(1)}, bf16[256,256]{1,0:T(8,128)(2,1)S(1)}, u32[]{:S(2)}, u32[]{:S(2)}) collective-permute-start(bf16[256,256]{1,0:T(8,128)(2,1)S(1)} %get-tuple-element.94), channel_id=1, source_target_pairs={{0,2},{1,3},{2,0},{3,1},{4,6},{5,7},{6,4},{7,5},{8,10},{9,11},{10,... | collective-permute-start | bytes 393224 | tf_op jit(solution)/shard_map/ppermute | solution.py:26
  60.5 9.5 %collective-permute-start.26 = (bf16[256,256]{1,0:T(8,128)(2,1)S(1)}, bf16[256,256]{1,0:T(8,128)(2,1)S(1)}, u32[]{:S(2)}, u32[]{:S(2)}) collective-permute-start(bf16[256,256]{1,0:T(8,128)(2,1)S(1)} %get-tuple-element.95), channel_id=1, source_target_pairs={{0,3},{1,2},{2,1},{3,0},{4,7},{5,6},{6,5},{7,4},{8,11},{9,10},{10,... | collective-permute-start | bytes 393224 | tf_op jit(solution)/shard_map/ppermute | solution.py:26
  66.0 10.6 %collective-permute-start.27 = (bf16[128,256]{1,0:T(8,128)(2,1)S(1)}, bf16[128,256]{1,0:T(8,128)(2,1)S(1)}, u32[]{:S(2)}, u32[]{:S(2)}) collective-permute-start(bf16[128,256]{1,0:T(8,128)(2,1)S(1)} %get-tuple-element.96), channel_id=1, source_target_pairs={{0,1},{1,0},{2,3},{3,2},{4,5},{5,4},{6,7},{7,6},{8,9},{9,8},{10,11... | collective-permute-start | bytes 196616 | tf_op jit(solution)/shard_map/ppermute | solution.py:26
  70.6 9.6 %collective-permute-start.28 = (bf16[128,256]{1,0:T(8,128)(2,1)S(1)}, bf16[128,256]{1,0:T(8,128)(2,1)S(1)}, u32[]{:S(2)}, u32[]{:S(2)}) collective-permute-start(bf16[128,256]{1,0:T(8,128)(2,1)S(1)} %get-tuple-element.97), channel_id=1, source_target_pairs={{0,2},{1,3},{2,0},{3,1},{4,6},{5,7},{6,4},{7,5},{8,10},{9,11},{10,... | collective-permute-start | bytes 196616 | tf_op jit(solution)/shard_map/ppermute | solution.py:26
  71.9 8.2 %collective-permute-start.29 = (bf16[128,256]{1,0:T(8,128)(2,1)S(1)}, bf16[128,256]{1,0:T(8,128)(2,1)S(1)}, u32[]{:S(2)}, u32[]{:S(2)}) collective-permute-start(bf16[128,256]{1,0:T(8,128)(2,1)S(1)} %get-tuple-element.98), channel_id=1, source_target_pairs={{0,3},{1,2},{2,1},{3,0},{4,7},{5,6},{6,5},{7,4},{8,11},{9,10},{10,... | collective-permute-start | bytes 196616 | tf_op jit(solution)/shard_map/ppermute | solution.py:26
  (15 other events, 170.4 us)

commit v19 on v18

--- a/solution.py
+++ b/solution.py
@@ -434,10 +434,10 @@
             else:
                 if turned is not None:
                     lowered_far = lowered(turned[0], h)
-                    nearest, *others = shared(turned[1:], lowered)
-                    lowered_far, *others = lax.optimization_barrier((lowered_far, *others))
-                    passed, nearest = lax.optimization_barrier((passed, nearest))
-                    lowered_near = [nearest, *others]
+                    *others, farthest = shared(turned[1:], lowered)
+                    lowered_far, farthest = lax.optimization_barrier((lowered_far, farthest))
+                    passed, others = lax.optimization_barrier((passed, others))
+                    lowered_near = [*others, farthest]
                 call = Call()
                 call.give(VMEM, preact, weights, names, *asked)
                 if entry:
@@ -490,6 +490,8 @@
             call.want(VMEM, (tile * (1 + c["first"]), width), BF16, h - 1)
             relays = call.run(functools.partial(forward_kernel, c), "forward", small_cost)
             relayed = shared(relays)
+            if c["first"]:
+                asked_later, _ = lax.optimization_barrier((asked, relays))
             if layer == 0 and not final:
                 later, *_ = lax.optimization_barrier((words, *near))
                 adjs[tick + 1] = densify(tick + 1, later, tile_vals, row_tiles, n)
@@ -513,6 +515,8 @@
                 )
                 old = weight_acc[layer]
                 weight_acc[layer] = term if old is None else old + term
+                if c["first"]:
+                    got, weight_acc[layer] = lax.optimization_barrier((got, weight_acc[layer]))
         initial.append(toward)
         c = dict(base, tick=tick, final=final, joined=joined)
         call = Call()
@@ -520,7 +524,7 @@
         if not final:
             up = Call()
             up.give(HBM, preact, weights)
-            up.give(VMEM, *asked)
+            up.give(VMEM, *asked_later)
             length = rows + width + -(-2 * ticks * (h - 1) // 16) * 16
             up.want(VMEM, (length, width), BF16)
             up.scratch = [pltpu.SemaphoreType.DMA((2,))]

time: 83.4 us -> 85.4 us (1.024)
  Pallas kernels: 9.63 us -> 13.2 us
  waiting for transfers between devices: 23.6 us -> 20.5 us
  starting transfers between devices: 43.3 us -> 44.5 us
    pallas_call x16, Pallas kernels: 9.63 us -> 13.2 us  [run(): pl.pallas_call(kernel, out_shape=self.outs, in_specs=self.specs, out_spec...]
    ppermute x28, waiting for transfers between devices: 21.8 us -> 18.8 us  [swapped(): return lax.ppermute(block, 'rows', [(i, i ^ k) for i in range(n)])]
    ppermute x28, starting transfers between devices: 35.9 us -> 37.1 us  [swapped(): return lax.ppermute(block, 'rows', [(i, i ^ k) for i in range(n)])]
    optimization_barrier x0 -> x1, local copies, waits for them, and re-layouts: none -> 1.08 us  [shards(): got, weight_acc[layer] = lax.optimization_barrier((got, weight_acc[layer]))]
    mul x1 -> x0, local copies, waits for them, and re-layouts: 1.08 us -> none  [shards(): beta * jnp.dot(support[0, tick, layer].T, masked, preferred_element_type=...]
  transfers between devices with their start and end apart: 34 -> 34, of which waited for: 14 -> 13; matrix products, arithmetic and copies ran while one was open for 5% -> 5% of each run, Pallas kernels for 9% -> 11%
where the time goes in v19:
time: 85.4 us; the launch traced here: 85.3 us
  starting transfers between devices  44.5 us (52%)
  waiting for transfers between devices  20.5 us (24%)
  Pallas kernels  13.2 us (15%)
  matrix products  2.63 us (3%)
  local copies, waits for them, and re-layouts  1.73 us (2%)
  other arithmetic  1.67 us (2%)
  between operations  1.09 us (1%)
    ppermute x28, starting transfers between devices, swapped(): return lax.ppermute(block, 'rows', [(i, i ^ k) for i in range(n)])  37.1 us
    ppermute x28, waiting for transfers between devices, swapped(): return lax.ppermute(block, 'rows', [(i, i ^ k) for i in range(n)])  18.8 us
    pallas_call x16, Pallas kernels, run(): pl.pallas_call(kernel, out_shape=self.outs, in_specs=self.specs, out_spec...  13.2 us
    ppermute x5, starting transfers between devices, lowered(): return lax.ppermute(block, ('section', 'rows'), route)  7.32 us
    ppermute x5, waiting for transfers between devices, lowered(): return lax.ppermute(block, ('section', 'rows'), route)  1.76 us
  transfers between devices with their start and end apart: 34, of which 13 were waited for; matrix products, arithmetic and copies ran while one was open for 5% of the time, Pallas kernels for 11%

profile of v19, /device:TPU:0, one launch (start us, length us, event | category | flops | bytes accessed | tf_op | source)
XLA Modules:
  0.0 85.3 jit_solution(10886499903642193275)
XLA Ops:
  2.2 4.1 %collective-permute-start.3 = (bf16[256,256]{1,0:T(8,128)(2,1)S(1)}, bf16[256,256]{1,0:T(8,128)(2,1)S(1)}, u32[]{:S(2)}, u32[]{:S(2)}) collective-permute-start(bf16[256,256]{1,0:T(8,128)(2,1)S(1)} %fusion.3.refs_1_.refs_7_), channel_id=1, source_target_pairs={{0,4},{1,5},{2,6},{3,7},{4,0},{5,1},{6,2},{7,3},{8,12},{9,13},{10,... | collective-permute-start | bytes 393224 | tf_op jit(solution)/shard_map/ppermute | solution.py:26
  7.2 1.6 %collective-permute-start = (f32[4,256]{1,0:T(4,128)S(1)}, f32[4,256]{1,0:T(4,128)S(1)}, u32[]{:S(2)}, u32[]{:S(2)}) collective-permute-start(f32[4,256]{1,0:T(4,128)S(1)} %get-tuple-element.62), channel_id=1, source_target_pairs={{0,1},{1,0},{2,3},{3,2},{4,5},{5,4},{6,7},{7,6},{8,9},{9,8},{10,11... | collective-permute-start | bytes 12296 | tf_op jit(solution)/shard_map/ppermute | solution.py:26
  8.8 1.6 %collective-permute-start.1 = (f32[4,256]{1,0:T(4,128)S(1)}, f32[4,256]{1,0:T(4,128)S(1)}, u32[]{:S(2)}, u32[]{:S(2)}) collective-permute-start(f32[4,256]{1,0:T(4,128)S(1)} %get-tuple-element.63), channel_id=1, source_target_pairs={{0,2},{1,3},{2,0},{3,1},{4,6},{5,7},{6,4},{7,5},{8,10},{9,11},{10,... | collective-permute-start | bytes 12296 | tf_op jit(solution)/shard_map/ppermute | solution.py:26
  10.8 3.3 %densify.2.refs_6_.refs_1_ = bf16[256,1152]{1,0:T(8,128)(2,1)S(1)} custom-call(s32[2,96]{1,0:T(2,128)S(1)} %fusion.15.words_ref, bf16[1,2,96,128,128]{4,3,2,1,0:T(8,128)(2,1)} %vals_ref.3), custom_call_target="tpu_custom_call" | custom-call | flops 31457280 | bytes 3145728 | tf_op jit(solution)/shard_map/densify/pallas_call | solution.py:71
  15.5 1.7 %collective-permute-start.5 = (bf16[256,256]{1,0:T(8,128)(2,1)S(1)}, bf16[256,256]{1,0:T(8,128)(2,1)S(1)}, u32[]{:S(2)}, u32[]{:S(2)}) collective-permute-start(bf16[256,256]{1,0:T(8,128)(2,1)S(1)} %get-tuple-element.68), channel_id=1, source_target_pairs={{0,2},{1,3},{2,0},{3,1},{4,6},{5,7},{6,4},{7,5},{8,10},{9,11},{10,... | collective-permute-start | bytes 393224 | tf_op jit(solution)/shard_map/ppermute | solution.py:26
  19.8 1.5 %collective-permute-done.4.refs_9_ = bf16[256,256]{1,0:T(8,128)(2,1)S(1)} collective-permute-done((bf16[256,256]{1,0:T(8,128)(2,1)S(1)}, bf16[256,256]{1,0:T(8,128)(2,1)S(1)}, u32[]{:S(2)}, u32[]{:S(2)}) %collective-permute-start.4) | collective-permute-done | bytes 131104 | tf_op jit(solution)/shard_map/ppermute | solution.py:26
  21.4 1.8 %collective-permute-done.6.refs_11_ = bf16[256,256]{1,0:T(8,128)(2,1)S(1)} collective-permute-done((bf16[256,256]{1,0:T(8,128)(2,1)S(1)}, bf16[256,256]{1,0:T(8,128)(2,1)S(1)}, u32[]{:S(2)}, u32[]{:S(2)}) %collective-permute-start.6) | collective-permute-done | bytes 131104 | tf_op jit(solution)/shard_map/ppermute | solution.py:26
  26.6 1.7 %collective-permute-start.12 = (bf16[128,256]{1,0:T(8,128)(2,1)S(1)}, bf16[128,256]{1,0:T(8,128)(2,1)S(1)}, u32[]{:S(2)}, u32[]{:S(2)}) collective-permute-start(bf16[128,256]{1,0:T(8,128)(2,1)S(1)} %get-tuple-element.79), channel_id=1, source_target_pairs={{0,2},{1,3},{2,0},{3,1},{4,6},{5,7},{6,4},{7,5},{8,10},{9,11},{10,... | collective-permute-start | bytes 196616 | tf_op jit(solution)/shard_map/ppermute | solution.py:26
  28.6 2.5 %collective-permute-done.7.refs_0_.refs_3_ = bf16[256,256]{1,0:T(8,128)(2,1)S(1)} collective-permute-done((bf16[256,256]{1,0:T(8,128)(2,1)S(1)}, bf16[256,256]{1,0:T(8,128)(2,1)S(1)}, u32[]{:S(2)}, u32[]{:S(2)}) %collective-permute-start.7) | collective-permute-done | bytes 131104 | tf_op jit(solution)/shard_map/ppermute | solution.py:26
  33.0 1.8 %collective-permute-start.10 = (bf16[128,256]{1,0:T(8,128)(2,1)S(1)}, bf16[128,256]{1,0:T(8,128)(2,1)S(1)}, u32[]{:S(2)}, u32[]{:S(2)}) collective-permute-start(bf16[128,256]{1,0:T(8,128)(2,1)S(1)} %get-tuple-element.77), channel_id=1, source_target_pairs={{0,3},{1,2},{2,1},{3,0},{4,7},{5,6},{6,5},{7,4},{8,11},{9,10},{10,... | collective-permute-start | bytes 196616 | tf_op jit(solution)/shard_map/ppermute | solution.py:26
  34.8 3.3 %densify.3.refs_6_.refs_1_ = bf16[256,1152]{1,0:T(8,128)(2,1)S(1)} custom-call(s32[2,96]{1,0:T(2,128)S(1)} %fusion.15.words_ref, bf16[1,2,96,128,128]{4,3,2,1,0:T(8,128)(2,1)} %vals_ref.3), custom_call_target="tpu_custom_call" | custom-call | flops 31457280 | bytes 3145728 | tf_op jit(solution)/shard_map/densify/pallas_call | solution.py:71
  40.0 1.6 %collective-permute-start.18 = (bf16[256,256]{1,0:T(8,128)(2,1)}, bf16[256,256]{1,0:T(8,128)(2,1)S(1)}, u32[]{:S(2)}, u32[]{:S(2)}) collective-permute-start(bf16[256,256]{1,0:T(8,128)(2,1)} %get-tuple-element.95), channel_id=1, source_target_pairs={{0,28},{1,29},{2,30},{3,31},{4,24},{5,25},{6,26},{7,27},{8,4},{9,5... | collective-permute-start | bytes 393224 | tf_op jit(solution)/shard_map/ppermute | solution.py:34
  41.6 3.3 %collective-permute-start.19 = (bf16[128,256]{1,0:T(8,128)(2,1)}, bf16[128,256]{1,0:T(8,128)(2,1)S(1)}, u32[]{:S(2)}, u32[]{:S(2)}) collective-permute-start(bf16[128,256]{1,0:T(8,128)(2,1)} %get-tuple-element.96), channel_id=1, source_target_pairs={{0,27},{1,26},{2,25},{3,24},{4,31},{5,30},{6,29},{7,28},{8,3},{9,2... | collective-permute-start | bytes 196616 | tf_op jit(solution)/shard_map/ppermute | solution.py:34
  47.4 1.8 %collective-permute-done.18.refs_0_.refs_8_ = bf16[256,256]{1,0:T(8,128)(2,1)S(1)} collective-permute-done((bf16[256,256]{1,0:T(8,128)(2,1)}, bf16[256,256]{1,0:T(8,128)(2,1)S(1)}, u32[]{:S(2)}, u32[]{:S(2)}) %collective-permute-start.18) | collective-permute-done | bytes 131104 | tf_op jit(solution)/shard_map/ppermute | solution.py:34
  50.3 1.7 %collective-permute-start.21 = (bf16[128,256]{1,0:T(8,128)(2,1)}, bf16[128,256]{1,0:T(8,128)(2,1)}, u32[]{:S(2)}, u32[]{:S(2)}) collective-permute-start(bf16[128,256]{1,0:T(8,128)(2,1)} %get-tuple-element.102), channel_id=1, source_target_pairs={{0,2},{1,3},{2,0},{3,1},{4,6},{5,7},{6,4},{7,5},{8,10},{9,11},{10,... | collective-permute-start | bytes 196616 | tf_op jit(solution)/shard_map/ppermute | solution.py:26
  55.0 3.2 %collective-permute-done.22.refs_14_ = bf16[128,256]{1,0:T(8,128)(2,1)} collective-permute-done((bf16[128,256]{1,0:T(8,128)(2,1)}, bf16[128,256]{1,0:T(8,128)(2,1)}, u32[]{:S(2)}, u32[]{:S(2)}) %collective-permute-start.22) | collective-permute-done | bytes 65568 | tf_op jit(solution)/shard_map/ppermute | solution.py:26
  58.2 1.5 %middle.3 = (bf16[256,256]{1,0:T(8,128)(2,1)S(1)}, bf16[256,256]{1,0:T(8,128)(2,1)S(1)}, bf16[256,256]{1,0:T(8,128)(2,1)S(1)}, bf16[256,256]{1,0:T(8,128)(2,1)S(1)}, f32[64,256]{1,0:T(8,128)S(1)}) custom-call(bf16[1,2,2,256,256]{4,3,2,1,0:T(8,128)(2,1)S(1)} %copy-done, bf16[1,2,256,256]{3,2,1,0:T(8,128)(2,1)S(1)} %copy-done.1, ...), custom_call_target="tpu_custom_call" | custom-call | flops 184549376 | bytes 1441792 | tf_op jit(solution)/shard_map/middle/pallas_call | solution.py:71
  59.7 2.0 %collective-permute-start.23 = (bf16[256,256]{1,0:T(8,128)(2,1)S(1)}, bf16[256,256]{1,0:T(8,128)(2,1)S(1)}, u32[]{:S(2)}, u32[]{:S(2)}) collective-permute-start(bf16[256,256]{1,0:T(8,128)(2,1)S(1)} %get-tuple-element.108.refs_2_), channel_id=1, source_target_pairs={{0,4},{1,5},{2,6},{3,7},{4,0},{5,1},{6,2},{7,3},{8,12},{9,13},{10,... | collective-permute-start | bytes 393224 | tf_op jit(solution)/shard_map/ppermute | solution.py:26
  63.2 2.0 %collective-permute-start.26 = (bf16[256,256]{1,0:T(8,128)(2,1)S(1)}, bf16[256,256]{1,0:T(8,128)(2,1)S(1)}, u32[]{:S(2)}, u32[]{:S(2)}) collective-permute-start(bf16[256,256]{1,0:T(8,128)(2,1)S(1)} %get-tuple-element.111), channel_id=1, source_target_pairs={{0,3},{1,2},{2,1},{3,0},{4,7},{5,6},{6,5},{7,4},{8,11},{9,10},{10,... | collective-permute-start | bytes 393224 | tf_op jit(solution)/shard_map/ppermute | solution.py:26
  65.2 3.9 %collective-permute-done.23.refs_0_.refs_3_ = bf16[256,256]{1,0:T(8,128)(2,1)S(1)} collective-permute-done((bf16[256,256]{1,0:T(8,128)(2,1)S(1)}, bf16[256,256]{1,0:T(8,128)(2,1)S(1)}, u32[]{:S(2)}, u32[]{:S(2)}) %collective-permute-start.23) | collective-permute-done | bytes 131104 | tf_op jit(solution)/shard_map/ppermute | solution.py:26
  70.0 2.1 %collective-permute-done.26.refs_6_.refs_4_ = bf16[256,256]{1,0:T(8,128)(2,1)S(1)} collective-permute-done((bf16[256,256]{1,0:T(8,128)(2,1)S(1)}, bf16[256,256]{1,0:T(8,128)(2,1)S(1)}, u32[]{:S(2)}, u32[]{:S(2)}) %collective-permute-start.26) | collective-permute-done | bytes 131104 | tf_op jit(solution)/shard_map/ppermute | solution.py:26
  73.3 1.7 %collective-permute-start.28 = (bf16[128,256]{1,0:T(8,128)(2,1)S(1)}, bf16[128,256]{1,0:T(8,128)(2,1)S(1)}, u32[]{:S(2)}, u32[]{:S(2)}) collective-permute-start(bf16[128,256]{1,0:T(8,128)(2,1)S(1)} %get-tuple-element.113), channel_id=1, source_target_pairs={{0,2},{1,3},{2,0},{3,1},{4,6},{5,7},{6,4},{7,5},{8,10},{9,11},{10,... | collective-permute-start | bytes 196616 | tf_op jit(solution)/shard_map/ppermute | solution.py:26
  77.4 1.5 %collective-permute-start.31 = (bf16[2,64,256]{2,1,0:T(8,128)(2,1)S(1)}, bf16[2,64,256]{2,1,0:T(8,128)(2,1)S(1)}, u32[]{:S(2)}, u32[]{:S(2)}) collective-permute-start(bf16[2,64,256]{2,1,0:T(8,128)(2,1)S(1)} %total.1.refs_0_), channel_id=1, source_target_pairs={{0,1},{1,0},{2,3},{3,2},{4,5},{5,4},{6,7},{7,6},{8,9},{9,8},{10,11... | collective-permute-start | bytes 196616 | tf_op jit(solution)/shard_map/ppermute | solution.py:26
  79.3 1.7 %collective-permute-start.33 = (bf16[2,64,256]{2,1,0:T(8,128)(2,1)S(1)}, bf16[2,64,256]{2,1,0:T(8,128)(2,1)S(1)}, u32[]{:S(2)}, u32[]{:S(2)}) collective-permute-start(bf16[2,64,256]{2,1,0:T(8,128)(2,1)S(1)} %total.1.refs_0_), channel_id=1, source_target_pairs={{0,3},{1,2},{2,1},{3,0},{4,7},{5,6},{6,5},{7,4},{8,11},{9,10},{10,... | collective-permute-start | bytes 196616 | tf_op jit(solution)/shard_map/ppermute | solution.py:26
  (80 shorter events, 31.4 us)
Async XLA Ops:
  2.2 12.6 %collective-permute-start.3 = (bf16[256,256]{1,0:T(8,128)(2,1)S(1)}, bf16[256,256]{1,0:T(8,128)(2,1)S(1)}, u32[]{:S(2)}, u32[]{:S(2)}) collective-permute-start(bf16[256,256]{1,0:T(8,128)(2,1)S(1)} %fusion.3.refs_1_.refs_7_), channel_id=1, source_target_pairs={{0,4},{1,5},{2,6},{3,7},{4,0},{5,1},{6,2},{7,3},{8,12},{9,13},{10,... | collective-permute-start | bytes 393224 | tf_op jit(solution)/shard_map/ppermute | solution.py:26
  7.2 6.8 %collective-permute-start = (f32[4,256]{1,0:T(4,128)S(1)}, f32[4,256]{1,0:T(4,128)S(1)}, u32[]{:S(2)}, u32[]{:S(2)}) collective-permute-start(f32[4,256]{1,0:T(4,128)S(1)} %get-tuple-element.62), channel_id=1, source_target_pairs={{0,1},{1,0},{2,3},{3,2},{4,5},{5,4},{6,7},{7,6},{8,9},{9,8},{10,11... | collective-permute-start | bytes 12296 | tf_op jit(solution)/shard_map/ppermute | solution.py:26
  14.9 6.4 %collective-permute-start.4 = (bf16[256,256]{1,0:T(8,128)(2,1)S(1)}, bf16[256,256]{1,0:T(8,128)(2,1)S(1)}, u32[]{:S(2)}, u32[]{:S(2)}) collective-permute-start(bf16[256,256]{1,0:T(8,128)(2,1)S(1)} %get-tuple-element.67), channel_id=1, source_target_pairs={{0,1},{1,0},{2,3},{3,2},{4,5},{5,4},{6,7},{7,6},{8,9},{9,8},{10,11... | collective-permute-start | bytes 393224 | tf_op jit(solution)/shard_map/ppermute | solution.py:26
  15.5 5.8 %collective-permute-start.5 = (bf16[256,256]{1,0:T(8,128)(2,1)S(1)}, bf16[256,256]{1,0:T(8,128)(2,1)S(1)}, u32[]{:S(2)}, u32[]{:S(2)}) collective-permute-start(bf16[256,256]{1,0:T(8,128)(2,1)S(1)} %get-tuple-element.68), channel_id=1, source_target_pairs={{0,2},{1,3},{2,0},{3,1},{4,6},{5,7},{6,4},{7,5},{8,10},{9,11},{10,... | collective-permute-start | bytes 393224 | tf_op jit(solution)/shard_map/ppermute | solution.py:26
  17.2 6.0 %collective-permute-start.6 = (bf16[256,256]{1,0:T(8,128)(2,1)S(1)}, bf16[256,256]{1,0:T(8,128)(2,1)S(1)}, u32[]{:S(2)}, u32[]{:S(2)}) collective-permute-start(bf16[256,256]{1,0:T(8,128)(2,1)S(1)} %get-tuple-element.69), channel_id=1, source_target_pairs={{0,3},{1,2},{2,1},{3,0},{4,7},{5,6},{6,5},{7,4},{8,11},{9,10},{10,... | collective-permute-start | bytes 393224 | tf_op jit(solution)/shard_map/ppermute | solution.py:26
  18.8 19.3 %collective-permute-start.14 = (bf16[528,256]{1,0:T(8,128)(2,1)S(1)}, bf16[528,256]{1,0:T(8,128)(2,1)S(1)}, u32[]{:S(2)}, u32[]{:S(2)}) collective-permute-start(bf16[528,256]{1,0:T(8,128)(2,1)S(1)} %pack.1), channel_id=1, source_target_pairs={{0,8},{8,16},{16,24},{24,0},{1,9},{9,17},{17,25},{25,1},{2,10},{10... | collective-permute-start | bytes 811016 | tf_op jit(solution)/shard_map/ppermute | solution.py:39
  23.7 7.5 %collective-permute-start.7 = (bf16[256,256]{1,0:T(8,128)(2,1)S(1)}, bf16[256,256]{1,0:T(8,128)(2,1)S(1)}, u32[]{:S(2)}, u32[]{:S(2)}) collective-permute-start(bf16[256,256]{1,0:T(8,128)(2,1)S(1)} %get-tuple-element.74.refs_2_), channel_id=1, source_target_pairs={{0,4},{1,5},{2,6},{3,7},{4,0},{5,1},{6,2},{7,3},{8,12},{9,13},{10,... | collective-permute-start | bytes 393224 | tf_op jit(solution)/shard_map/ppermute | solution.py:26
  25.2 7.2 %collective-permute-start.11 = (bf16[128,256]{1,0:T(8,128)(2,1)S(1)}, bf16[128,256]{1,0:T(8,128)(2,1)S(1)}, u32[]{:S(2)}, u32[]{:S(2)}) collective-permute-start(bf16[128,256]{1,0:T(8,128)(2,1)S(1)} %get-tuple-element.78), channel_id=1, source_target_pairs={{0,1},{1,0},{2,3},{3,2},{4,5},{5,4},{6,7},{7,6},{8,9},{9,8},{10,11... | collective-permute-start | bytes 196616 | tf_op jit(solution)/shard_map/ppermute | solution.py:26
  26.6 6.4 %collective-permute-start.12 = (bf16[128,256]{1,0:T(8,128)(2,1)S(1)}, bf16[128,256]{1,0:T(8,128)(2,1)S(1)}, u32[]{:S(2)}, u32[]{:S(2)}) collective-permute-start(bf16[128,256]{1,0:T(8,128)(2,1)S(1)} %get-tuple-element.79), channel_id=1, source_target_pairs={{0,2},{1,3},{2,0},{3,1},{4,6},{5,7},{6,4},{7,5},{8,10},{9,11},{10,... | collective-permute-start | bytes 196616 | tf_op jit(solution)/shard_map/ppermute | solution.py:26
  28.4 6.4 %collective-permute-start.13 = (bf16[128,256]{1,0:T(8,128)(2,1)S(1)}, bf16[128,256]{1,0:T(8,128)(2,1)S(1)}, u32[]{:S(2)}, u32[]{:S(2)}) collective-permute-start(bf16[128,256]{1,0:T(8,128)(2,1)S(1)} %get-tuple-element.80), channel_id=1, source_target_pairs={{0,3},{1,2},{2,1},{3,0},{4,7},{5,6},{6,5},{7,4},{8,11},{9,10},{10,... | collective-permute-start | bytes 196616 | tf_op jit(solution)/shard_map/ppermute | solution.py:26
  31.2 6.8 %collective-permute-start.8 = (bf16[128,256]{1,0:T(8,128)(2,1)S(1)}, bf16[128,256]{1,0:T(8,128)(2,1)S(1)}, u32[]{:S(2)}, u32[]{:S(2)}) collective-permute-start(bf16[128,256]{1,0:T(8,128)(2,1)S(1)} %get-tuple-element.75), channel_id=1, source_target_pairs={{0,1},{1,0},{2,3},{3,2},{4,5},{5,4},{6,7},{7,6},{8,9},{9,8},{10,11... | collective-permute-start | bytes 196616 | tf_op jit(solution)/shard_map/ppermute | solution.py:26
  40.0 9.2 %collective-permute-start.18 = (bf16[256,256]{1,0:T(8,128)(2,1)}, bf16[256,256]{1,0:T(8,128)(2,1)S(1)}, u32[]{:S(2)}, u32[]{:S(2)}) collective-permute-start(bf16[256,256]{1,0:T(8,128)(2,1)} %get-tuple-element.95), channel_id=1, source_target_pairs={{0,28},{1,29},{2,30},{3,31},{4,24},{5,25},{6,26},{7,27},{8,4},{9,5... | collective-permute-start | bytes 393224 | tf_op jit(solution)/shard_map/ppermute | solution.py:34
  41.6 5.8 %collective-permute-start.19 = (bf16[128,256]{1,0:T(8,128)(2,1)}, bf16[128,256]{1,0:T(8,128)(2,1)S(1)}, u32[]{:S(2)}, u32[]{:S(2)}) collective-permute-start(bf16[128,256]{1,0:T(8,128)(2,1)} %get-tuple-element.96), channel_id=1, source_target_pairs={{0,27},{1,26},{2,25},{3,24},{4,31},{5,30},{6,29},{7,28},{8,3},{9,2... | collective-permute-start | bytes 196616 | tf_op jit(solution)/shard_map/ppermute | solution.py:34
  44.9 7.1 %collective-permute-start.16 = (bf16[128,256]{1,0:T(8,128)(2,1)}, bf16[128,256]{1,0:T(8,128)(2,1)S(1)}, u32[]{:S(2)}, u32[]{:S(2)}) collective-permute-start(bf16[128,256]{1,0:T(8,128)(2,1)} %get-tuple-element.90), channel_id=1, source_target_pairs={{0,25},{1,24},{2,27},{3,26},{4,29},{5,28},{6,31},{7,30},{8,1},{9,0... | collective-permute-start | bytes 196616 | tf_op jit(solution)/shard_map/ppermute | solution.py:34
  45.0 9.7 %collective-permute-start.15 = (bf16[256,256]{1,0:T(8,128)(2,1)S(1)}, bf16[256,256]{1,0:T(8,128)(2,1)S(1)}, u32[]{:S(2)}, u32[]{:S(2)}) collective-permute-start(bf16[256,256]{1,0:T(8,128)(2,1)S(1)} %get-tuple-element.89.refs_10_), channel_id=1, source_target_pairs={{0,24},{1,25},{2,26},{3,27},{4,28},{5,29},{6,30},{7,31},{8,0},{9,1... | collective-permute-start | bytes 393224 | tf_op jit(solution)/shard_map/ppermute | solution.py:34
  45.9 8.7 %collective-permute-start.17 = (bf16[128,256]{1,0:T(8,128)(2,1)}, bf16[128,256]{1,0:T(8,128)(2,1)S(1)}, u32[]{:S(2)}, u32[]{:S(2)}) collective-permute-start(bf16[128,256]{1,0:T(8,128)(2,1)} %copy-done.4), channel_id=1, source_target_pairs={{0,26},{1,27},{2,24},{3,25},{4,30},{5,31},{6,28},{7,29},{8,2},{9,3... | collective-permute-start | bytes 196616 | tf_op jit(solution)/shard_map/ppermute | solution.py:34
  52.0 6.1 %collective-permute-start.22 = (bf16[128,256]{1,0:T(8,128)(2,1)}, bf16[128,256]{1,0:T(8,128)(2,1)}, u32[]{:S(2)}, u32[]{:S(2)}) collective-permute-start(bf16[128,256]{1,0:T(8,128)(2,1)} %get-tuple-element.103), channel_id=1, source_target_pairs={{0,3},{1,2},{2,1},{3,0},{4,7},{5,6},{6,5},{7,4},{8,11},{9,10},{10,... | collective-permute-start | bytes 196616 | tf_op jit(solution)/shard_map/ppermute | solution.py:26
  59.7 9.4 %collective-permute-start.23 = (bf16[256,256]{1,0:T(8,128)(2,1)S(1)}, bf16[256,256]{1,0:T(8,128)(2,1)S(1)}, u32[]{:S(2)}, u32[]{:S(2)}) collective-permute-start(bf16[256,256]{1,0:T(8,128)(2,1)S(1)} %get-tuple-element.108.refs_2_), channel_id=1, source_target_pairs={{0,4},{1,5},{2,6},{3,7},{4,0},{5,1},{6,2},{7,3},{8,12},{9,13},{10,... | collective-permute-start | bytes 393224 | tf_op jit(solution)/shard_map/ppermute | solution.py:26
  61.7 8.2 %collective-permute-start.24 = (bf16[256,256]{1,0:T(8,128)(2,1)S(1)}, bf16[256,256]{1,0:T(8,128)(2,1)S(1)}, u32[]{:S(2)}, u32[]{:S(2)}) collective-permute-start(bf16[256,256]{1,0:T(8,128)(2,1)S(1)} %get-tuple-element.109), channel_id=1, source_target_pairs={{0,1},{1,0},{2,3},{3,2},{4,5},{5,4},{6,7},{7,6},{8,9},{9,8},{10,11... | collective-permute-start | bytes 393224 | tf_op jit(solution)/shard_map/ppermute | solution.py:26
  62.2 7.9 %collective-permute-start.25 = (bf16[256,256]{1,0:T(8,128)(2,1)S(1)}, bf16[256,256]{1,0:T(8,128)(2,1)S(1)}, u32[]{:S(2)}, u32[]{:S(2)}) collective-permute-start(bf16[256,256]{1,0:T(8,128)(2,1)S(1)} %get-tuple-element.110), channel_id=1, source_target_pairs={{0,2},{1,3},{2,0},{3,1},{4,6},{5,7},{6,4},{7,5},{8,10},{9,11},{10,... | collective-permute-start | bytes 393224 | tf_op jit(solution)/shard_map/ppermute | solution.py:26
  63.2 8.9 %collective-permute-start.26 = (bf16[256,256]{1,0:T(8,128)(2,1)S(1)}, bf16[256,256]{1,0:T(8,128)(2,1)S(1)}, u32[]{:S(2)}, u32[]{:S(2)}) collective-permute-start(bf16[256,256]{1,0:T(8,128)(2,1)S(1)} %get-tuple-element.111), channel_id=1, source_target_pairs={{0,3},{1,2},{2,1},{3,0},{4,7},{5,6},{6,5},{7,4},{8,11},{9,10},{10,... | collective-permute-start | bytes 393224 | tf_op jit(solution)/shard_map/ppermute | solution.py:26
  69.1 10.2 %collective-permute-start.27 = (bf16[128,256]{1,0:T(8,128)(2,1)S(1)}, bf16[128,256]{1,0:T(8,128)(2,1)S(1)}, u32[]{:S(2)}, u32[]{:S(2)}) collective-permute-start(bf16[128,256]{1,0:T(8,128)(2,1)S(1)} %get-tuple-element.112), channel_id=1, source_target_pairs={{0,1},{1,0},{2,3},{3,2},{4,5},{5,4},{6,7},{7,6},{8,9},{9,8},{10,11... | collective-permute-start | bytes 196616 | tf_op jit(solution)/shard_map/ppermute | solution.py:26
  73.3 8.6 %collective-permute-start.28 = (bf16[128,256]{1,0:T(8,128)(2,1)S(1)}, bf16[128,256]{1,0:T(8,128)(2,1)S(1)}, u32[]{:S(2)}, u32[]{:S(2)}) collective-permute-start(bf16[128,256]{1,0:T(8,128)(2,1)S(1)} %get-tuple-element.113), channel_id=1, source_target_pairs={{0,2},{1,3},{2,0},{3,1},{4,6},{5,7},{6,4},{7,5},{8,10},{9,11},{10,... | collective-permute-start | bytes 196616 | tf_op jit(solution)/shard_map/ppermute | solution.py:26
  75.0 6.8 %collective-permute-start.29 = (bf16[128,256]{1,0:T(8,128)(2,1)S(1)}, bf16[128,256]{1,0:T(8,128)(2,1)S(1)}, u32[]{:S(2)}, u32[]{:S(2)}) collective-permute-start(bf16[128,256]{1,0:T(8,128)(2,1)S(1)} %get-tuple-element.114), channel_id=1, source_target_pairs={{0,3},{1,2},{2,1},{3,0},{4,7},{5,6},{6,5},{7,4},{8,11},{9,10},{10,... | collective-permute-start | bytes 196616 | tf_op jit(solution)/shard_map/ppermute | solution.py:26
  (16 other events, 147.5 us)

commit v20 on v19

--- a/solution.py
+++ b/solution.py
@@ -149,7 +149,7 @@
         functools.partial(densify_kernel, tick, row_tiles, n, chunks),
         "densify",
         cost(entries * tile * tile * 20, entries * tile * tile * 2),
-        pltpu.CompilerParams(vmem_limit_bytes=50 * 2**20),
+        pltpu.CompilerParams(vmem_limit_bytes=48 * 2**20),
     )
     return adj
 

time: 85.4 us -> 85.3 us (level)
  transfers between devices with their start and end apart: 34 -> 34, of which waited for: 13 -> 14; matrix products, arithmetic and copies ran while one was open for 5% -> 5% of each run, Pallas kernels for 11% -> 11%
where the time goes in v20:
time: 85.3 us; the launch traced here: 85.1 us
  starting transfers between devices  44.4 us (52%)
  waiting for transfers between devices  20.8 us (24%)
  Pallas kernels  12.8 us (15%)
  matrix products  2.63 us (3%)
  local copies, waits for them, and re-layouts  1.73 us (2%)
  other arithmetic  1.67 us (2%)
  between operations  1.08 us (1%)
    ppermute x28, starting transfers between devices, swapped(): return lax.ppermute(block, 'rows', [(i, i ^ k) for i in range(n)])  37 us
    ppermute x28, waiting for transfers between devices, swapped(): return lax.ppermute(block, 'rows', [(i, i ^ k) for i in range(n)])  19 us
    pallas_call x16, Pallas kernels, run(): pl.pallas_call(kernel, out_shape=self.outs, in_specs=self.specs, out_spec...  12.8 us
    ppermute x5, starting transfers between devices, lowered(): return lax.ppermute(block, ('section', 'rows'), route)  7.32 us
    ppermute x5, waiting for transfers between devices, lowered(): return lax.ppermute(block, ('section', 'rows'), route)  1.76 us
  transfers between devices with their start and end apart: 34, of which 14 were waited for; matrix products, arithmetic and copies ran while one was open for 5% of the time, Pallas kernels for 11%

profile of v20, /device:TPU:0, one launch (start us, length us, event | category | flops | bytes accessed | tf_op | source)
XLA Modules:
  0.0 85.1 jit_solution(12048716647230121205)
XLA Ops:
  2.2 4.1 %collective-permute-start.3 = (bf16[256,256]{1,0:T(8,128)(2,1)S(1)}, bf16[256,256]{1,0:T(8,128)(2,1)S(1)}, u32[]{:S(2)}, u32[]{:S(2)}) collective-permute-start(bf16[256,256]{1,0:T(8,128)(2,1)S(1)} %fusion.3.refs_1_.refs_7_), channel_id=1, source_target_pairs={{0,4},{1,5},{2,6},{3,7},{4,0},{5,1},{6,2},{7,3},{8,12},{9,13},{10,... | collective-permute-start | bytes 393224 | tf_op jit(solution)/shard_map/ppermute | solution.py:26
  7.2 1.6 %collective-permute-start = (f32[4,256]{1,0:T(4,128)S(1)}, f32[4,256]{1,0:T(4,128)S(1)}, u32[]{:S(2)}, u32[]{:S(2)}) collective-permute-start(f32[4,256]{1,0:T(4,128)S(1)} %get-tuple-element.62), channel_id=1, source_target_pairs={{0,1},{1,0},{2,3},{3,2},{4,5},{5,4},{6,7},{7,6},{8,9},{9,8},{10,11... | collective-permute-start | bytes 12296 | tf_op jit(solution)/shard_map/ppermute | solution.py:26
  8.8 1.6 %collective-permute-start.1 = (f32[4,256]{1,0:T(4,128)S(1)}, f32[4,256]{1,0:T(4,128)S(1)}, u32[]{:S(2)}, u32[]{:S(2)}) collective-permute-start(f32[4,256]{1,0:T(4,128)S(1)} %get-tuple-element.63), channel_id=1, source_target_pairs={{0,2},{1,3},{2,0},{3,1},{4,6},{5,7},{6,4},{7,5},{8,10},{9,11},{10,... | collective-permute-start | bytes 12296 | tf_op jit(solution)/shard_map/ppermute | solution.py:26
  10.8 3.0 %densify.2.refs_6_.refs_1_ = bf16[256,1152]{1,0:T(8,128)(2,1)S(1)} custom-call(s32[2,96]{1,0:T(2,128)S(1)} %fusion.15.words_ref, bf16[1,2,96,128,128]{4,3,2,1,0:T(8,128)(2,1)} %vals_ref.3), custom_call_target="tpu_custom_call" | custom-call | flops 31457280 | bytes 3145728 | tf_op jit(solution)/shard_map/densify/pallas_call | solution.py:71
  15.5 1.5 %collective-permute-start.5 = (bf16[256,256]{1,0:T(8,128)(2,1)S(1)}, bf16[256,256]{1,0:T(8,128)(2,1)S(1)}, u32[]{:S(2)}, u32[]{:S(2)}) collective-permute-start(bf16[256,256]{1,0:T(8,128)(2,1)S(1)} %get-tuple-element.68), channel_id=1, source_target_pairs={{0,2},{1,3},{2,0},{3,1},{4,6},{5,7},{6,4},{7,5},{8,10},{9,11},{10,... | collective-permute-start | bytes 393224 | tf_op jit(solution)/shard_map/ppermute | solution.py:26
  17.0 1.5 %collective-permute-start.6 = (bf16[256,256]{1,0:T(8,128)(2,1)S(1)}, bf16[256,256]{1,0:T(8,128)(2,1)S(1)}, u32[]{:S(2)}, u32[]{:S(2)}) collective-permute-start(bf16[256,256]{1,0:T(8,128)(2,1)S(1)} %get-tuple-element.69), channel_id=1, source_target_pairs={{0,3},{1,2},{2,1},{3,0},{4,7},{5,6},{6,5},{7,4},{8,11},{9,10},{10,... | collective-permute-start | bytes 393224 | tf_op jit(solution)/shard_map/ppermute | solution.py:26
  21.2 1.6 %collective-permute-done.6.refs_11_ = bf16[256,256]{1,0:T(8,128)(2,1)S(1)} collective-permute-done((bf16[256,256]{1,0:T(8,128)(2,1)S(1)}, bf16[256,256]{1,0:T(8,128)(2,1)S(1)}, u32[]{:S(2)}, u32[]{:S(2)}) %collective-permute-start.6) | collective-permute-done | bytes 131104 | tf_op jit(solution)/shard_map/ppermute | solution.py:26
  23.4 1.8 %collective-permute-start.7 = (bf16[256,256]{1,0:T(8,128)(2,1)S(1)}, bf16[256,256]{1,0:T(8,128)(2,1)S(1)}, u32[]{:S(2)}, u32[]{:S(2)}) collective-permute-start(bf16[256,256]{1,0:T(8,128)(2,1)S(1)} %get-tuple-element.74.refs_2_), channel_id=1, source_target_pairs={{0,4},{1,5},{2,6},{3,7},{4,0},{5,1},{6,2},{7,3},{8,12},{9,13},{10,... | collective-permute-start | bytes 393224 | tf_op jit(solution)/shard_map/ppermute | solution.py:26
  26.6 1.7 %collective-permute-start.12 = (bf16[128,256]{1,0:T(8,128)(2,1)S(1)}, bf16[128,256]{1,0:T(8,128)(2,1)S(1)}, u32[]{:S(2)}, u32[]{:S(2)}) collective-permute-start(bf16[128,256]{1,0:T(8,128)(2,1)S(1)} %get-tuple-element.79), channel_id=1, source_target_pairs={{0,2},{1,3},{2,0},{3,1},{4,6},{5,7},{6,4},{7,5},{8,10},{9,11},{10,... | collective-permute-start | bytes 196616 | tf_op jit(solution)/shard_map/ppermute | solution.py:26
  28.6 2.5 %collective-permute-done.7.refs_0_.refs_3_ = bf16[256,256]{1,0:T(8,128)(2,1)S(1)} collective-permute-done((bf16[256,256]{1,0:T(8,128)(2,1)S(1)}, bf16[256,256]{1,0:T(8,128)(2,1)S(1)}, u32[]{:S(2)}, u32[]{:S(2)}) %collective-permute-start.7) | collective-permute-done | bytes 131104 | tf_op jit(solution)/shard_map/ppermute | solution.py:26
  33.0 1.8 %collective-permute-start.10 = (bf16[128,256]{1,0:T(8,128)(2,1)S(1)}, bf16[128,256]{1,0:T(8,128)(2,1)S(1)}, u32[]{:S(2)}, u32[]{:S(2)}) collective-permute-start(bf16[128,256]{1,0:T(8,128)(2,1)S(1)} %get-tuple-element.77), channel_id=1, source_target_pairs={{0,3},{1,2},{2,1},{3,0},{4,7},{5,6},{6,5},{7,4},{8,11},{9,10},{10,... | collective-permute-start | bytes 196616 | tf_op jit(solution)/shard_map/ppermute | solution.py:26
  34.8 3.1 %densify.3.refs_6_.refs_1_ = bf16[256,1152]{1,0:T(8,128)(2,1)S(1)} custom-call(s32[2,96]{1,0:T(2,128)S(1)} %fusion.15.words_ref, bf16[1,2,96,128,128]{4,3,2,1,0:T(8,128)(2,1)} %vals_ref.3), custom_call_target="tpu_custom_call" | custom-call | flops 31457280 | bytes 3145728 | tf_op jit(solution)/shard_map/densify/pallas_call | solution.py:71
  40.0 1.6 %collective-permute-start.18 = (bf16[256,256]{1,0:T(8,128)(2,1)}, bf16[256,256]{1,0:T(8,128)(2,1)S(1)}, u32[]{:S(2)}, u32[]{:S(2)}) collective-permute-start(bf16[256,256]{1,0:T(8,128)(2,1)} %get-tuple-element.95), channel_id=1, source_target_pairs={{0,28},{1,29},{2,30},{3,31},{4,24},{5,25},{6,26},{7,27},{8,4},{9,5... | collective-permute-start | bytes 393224 | tf_op jit(solution)/shard_map/ppermute | solution.py:34
  41.6 3.1 %collective-permute-start.19 = (bf16[128,256]{1,0:T(8,128)(2,1)}, bf16[128,256]{1,0:T(8,128)(2,1)S(1)}, u32[]{:S(2)}, u32[]{:S(2)}) collective-permute-start(bf16[128,256]{1,0:T(8,128)(2,1)} %get-tuple-element.96), channel_id=1, source_target_pairs={{0,27},{1,26},{2,25},{3,24},{4,31},{5,30},{6,29},{7,28},{8,3},{9,2... | collective-permute-start | bytes 196616 | tf_op jit(solution)/shard_map/ppermute | solution.py:34
  47.4 1.8 %collective-permute-done.18.refs_0_.refs_8_ = bf16[256,256]{1,0:T(8,128)(2,1)S(1)} collective-permute-done((bf16[256,256]{1,0:T(8,128)(2,1)}, bf16[256,256]{1,0:T(8,128)(2,1)S(1)}, u32[]{:S(2)}, u32[]{:S(2)}) %collective-permute-start.18) | collective-permute-done | bytes 131104 | tf_op jit(solution)/shard_map/ppermute | solution.py:34
  55.7 2.7 %collective-permute-done.22.refs_14_ = bf16[128,256]{1,0:T(8,128)(2,1)} collective-permute-done((bf16[128,256]{1,0:T(8,128)(2,1)}, bf16[128,256]{1,0:T(8,128)(2,1)}, u32[]{:S(2)}, u32[]{:S(2)}) %collective-permute-start.22) | collective-permute-done | bytes 65568 | tf_op jit(solution)/shard_map/ppermute | solution.py:26
  58.4 1.5 %middle.3 = (bf16[256,256]{1,0:T(8,128)(2,1)S(1)}, bf16[256,256]{1,0:T(8,128)(2,1)S(1)}, bf16[256,256]{1,0:T(8,128)(2,1)S(1)}, bf16[256,256]{1,0:T(8,128)(2,1)S(1)}, f32[64,256]{1,0:T(8,128)S(1)}) custom-call(bf16[1,2,2,256,256]{4,3,2,1,0:T(8,128)(2,1)S(1)} %copy-done, bf16[1,2,256,256]{3,2,1,0:T(8,128)(2,1)S(1)} %copy-done.1, ...), custom_call_target="tpu_custom_call" | custom-call | flops 184549376 | bytes 1441792 | tf_op jit(solution)/shard_map/middle/pallas_call | solution.py:71
  59.9 1.9 %collective-permute-start.23 = (bf16[256,256]{1,0:T(8,128)(2,1)S(1)}, bf16[256,256]{1,0:T(8,128)(2,1)S(1)}, u32[]{:S(2)}, u32[]{:S(2)}) collective-permute-start(bf16[256,256]{1,0:T(8,128)(2,1)S(1)} %get-tuple-element.108.refs_2_), channel_id=1, source_target_pairs={{0,4},{1,5},{2,6},{3,7},{4,0},{5,1},{6,2},{7,3},{8,12},{9,13},{10,... | collective-permute-start | bytes 393224 | tf_op jit(solution)/shard_map/ppermute | solution.py:26
  63.1 2.2 %collective-permute-start.26 = (bf16[256,256]{1,0:T(8,128)(2,1)S(1)}, bf16[256,256]{1,0:T(8,128)(2,1)S(1)}, u32[]{:S(2)}, u32[]{:S(2)}) collective-permute-start(bf16[256,256]{1,0:T(8,128)(2,1)S(1)} %get-tuple-element.111), channel_id=1, source_target_pairs={{0,3},{1,2},{2,1},{3,0},{4,7},{5,6},{6,5},{7,4},{8,11},{9,10},{10,... | collective-permute-start | bytes 393224 | tf_op jit(solution)/shard_map/ppermute | solution.py:26
  65.3 3.9 %collective-permute-done.23.refs_0_.refs_3_ = bf16[256,256]{1,0:T(8,128)(2,1)S(1)} collective-permute-done((bf16[256,256]{1,0:T(8,128)(2,1)S(1)}, bf16[256,256]{1,0:T(8,128)(2,1)S(1)}, u32[]{:S(2)}, u32[]{:S(2)}) %collective-permute-start.23) | collective-permute-done | bytes 131104 | tf_op jit(solution)/shard_map/ppermute | solution.py:26
  70.3 2.0 %collective-permute-done.26.refs_6_.refs_4_ = bf16[256,256]{1,0:T(8,128)(2,1)S(1)} collective-permute-done((bf16[256,256]{1,0:T(8,128)(2,1)S(1)}, bf16[256,256]{1,0:T(8,128)(2,1)S(1)}, u32[]{:S(2)}, u32[]{:S(2)}) %collective-permute-start.26) | collective-permute-done | bytes 131104 | tf_op jit(solution)/shard_map/ppermute | solution.py:26
  73.4 1.7 %collective-permute-start.28 = (bf16[128,256]{1,0:T(8,128)(2,1)S(1)}, bf16[128,256]{1,0:T(8,128)(2,1)S(1)}, u32[]{:S(2)}, u32[]{:S(2)}) collective-permute-start(bf16[128,256]{1,0:T(8,128)(2,1)S(1)} %get-tuple-element.113), channel_id=1, source_target_pairs={{0,2},{1,3},{2,0},{3,1},{4,6},{5,7},{6,4},{7,5},{8,10},{9,11},{10,... | collective-permute-start | bytes 196616 | tf_op jit(solution)/shard_map/ppermute | solution.py:26
  76.1 1.6 %collective-permute-done.30.far_ref = bf16[2,64,256]{2,1,0:T(8,128)(2,1)S(1)} collective-permute-done((bf16[2,64,256]{2,1,0:T(8,128)(2,1)S(1)}, bf16[2,64,256]{2,1,0:T(8,128)(2,1)S(1)}, u32[]{:S(2)}, u32[]{:S(2)}) %collective-permute-start.30) | collective-permute-done | bytes 65568 | tf_op jit(solution)/shard_map/ppermute | solution.py:26
  79.1 2.2 %collective-permute-start.33 = (bf16[2,64,256]{2,1,0:T(8,128)(2,1)S(1)}, bf16[2,64,256]{2,1,0:T(8,128)(2,1)S(1)}, u32[]{:S(2)}, u32[]{:S(2)}) collective-permute-start(bf16[2,64,256]{2,1,0:T(8,128)(2,1)S(1)} %total.1.refs_0_), channel_id=1, source_target_pairs={{0,3},{1,2},{2,1},{3,0},{4,7},{5,6},{6,5},{7,4},{8,11},{9,10},{10,... | collective-permute-start | bytes 196616 | tf_op jit(solution)/shard_map/ppermute | solution.py:26
  (80 shorter events, 32.0 us)
Async XLA Ops:
  2.2 12.6 %collective-permute-start.3 = (bf16[256,256]{1,0:T(8,128)(2,1)S(1)}, bf16[256,256]{1,0:T(8,128)(2,1)S(1)}, u32[]{:S(2)}, u32[]{:S(2)}) collective-permute-start(bf16[256,256]{1,0:T(8,128)(2,1)S(1)} %fusion.3.refs_1_.refs_7_), channel_id=1, source_target_pairs={{0,4},{1,5},{2,6},{3,7},{4,0},{5,1},{6,2},{7,3},{8,12},{9,13},{10,... | collective-permute-start | bytes 393224 | tf_op jit(solution)/shard_map/ppermute | solution.py:26
  7.2 6.6 %collective-permute-start = (f32[4,256]{1,0:T(4,128)S(1)}, f32[4,256]{1,0:T(4,128)S(1)}, u32[]{:S(2)}, u32[]{:S(2)}) collective-permute-start(f32[4,256]{1,0:T(4,128)S(1)} %get-tuple-element.62), channel_id=1, source_target_pairs={{0,1},{1,0},{2,3},{3,2},{4,5},{5,4},{6,7},{7,6},{8,9},{9,8},{10,11... | collective-permute-start | bytes 12296 | tf_op jit(solution)/shard_map/ppermute | solution.py:26
  14.9 6.3 %collective-permute-start.4 = (bf16[256,256]{1,0:T(8,128)(2,1)S(1)}, bf16[256,256]{1,0:T(8,128)(2,1)S(1)}, u32[]{:S(2)}, u32[]{:S(2)}) collective-permute-start(bf16[256,256]{1,0:T(8,128)(2,1)S(1)} %get-tuple-element.67), channel_id=1, source_target_pairs={{0,1},{1,0},{2,3},{3,2},{4,5},{5,4},{6,7},{7,6},{8,9},{9,8},{10,11... | collective-permute-start | bytes 393224 | tf_op jit(solution)/shard_map/ppermute | solution.py:26
  15.5 5.7 %collective-permute-start.5 = (bf16[256,256]{1,0:T(8,128)(2,1)S(1)}, bf16[256,256]{1,0:T(8,128)(2,1)S(1)}, u32[]{:S(2)}, u32[]{:S(2)}) collective-permute-start(bf16[256,256]{1,0:T(8,128)(2,1)S(1)} %get-tuple-element.68), channel_id=1, source_target_pairs={{0,2},{1,3},{2,0},{3,1},{4,6},{5,7},{6,4},{7,5},{8,10},{9,11},{10,... | collective-permute-start | bytes 393224 | tf_op jit(solution)/shard_map/ppermute | solution.py:26
  17.0 5.9 %collective-permute-start.6 = (bf16[256,256]{1,0:T(8,128)(2,1)S(1)}, bf16[256,256]{1,0:T(8,128)(2,1)S(1)}, u32[]{:S(2)}, u32[]{:S(2)}) collective-permute-start(bf16[256,256]{1,0:T(8,128)(2,1)S(1)} %get-tuple-element.69), channel_id=1, source_target_pairs={{0,3},{1,2},{2,1},{3,0},{4,7},{5,6},{6,5},{7,4},{8,11},{9,10},{10,... | collective-permute-start | bytes 393224 | tf_op jit(solution)/shard_map/ppermute | solution.py:26
  18.8 19.3 %collective-permute-start.14 = (bf16[528,256]{1,0:T(8,128)(2,1)S(1)}, bf16[528,256]{1,0:T(8,128)(2,1)S(1)}, u32[]{:S(2)}, u32[]{:S(2)}) collective-permute-start(bf16[528,256]{1,0:T(8,128)(2,1)S(1)} %pack.1), channel_id=1, source_target_pairs={{0,8},{8,16},{16,24},{24,0},{1,9},{9,17},{17,25},{25,1},{2,10},{10... | collective-permute-start | bytes 811016 | tf_op jit(solution)/shard_map/ppermute | solution.py:39
  23.4 7.8 %collective-permute-start.7 = (bf16[256,256]{1,0:T(8,128)(2,1)S(1)}, bf16[256,256]{1,0:T(8,128)(2,1)S(1)}, u32[]{:S(2)}, u32[]{:S(2)}) collective-permute-start(bf16[256,256]{1,0:T(8,128)(2,1)S(1)} %get-tuple-element.74.refs_2_), channel_id=1, source_target_pairs={{0,4},{1,5},{2,6},{3,7},{4,0},{5,1},{6,2},{7,3},{8,12},{9,13},{10,... | collective-permute-start | bytes 393224 | tf_op jit(solution)/shard_map/ppermute | solution.py:26
  25.2 7.2 %collective-permute-start.11 = (bf16[128,256]{1,0:T(8,128)(2,1)S(1)}, bf16[128,256]{1,0:T(8,128)(2,1)S(1)}, u32[]{:S(2)}, u32[]{:S(2)}) collective-permute-start(bf16[128,256]{1,0:T(8,128)(2,1)S(1)} %get-tuple-element.78), channel_id=1, source_target_pairs={{0,1},{1,0},{2,3},{3,2},{4,5},{5,4},{6,7},{7,6},{8,9},{9,8},{10,11... | collective-permute-start | bytes 196616 | tf_op jit(solution)/shard_map/ppermute | solution.py:26
  26.6 6.4 %collective-permute-start.12 = (bf16[128,256]{1,0:T(8,128)(2,1)S(1)}, bf16[128,256]{1,0:T(8,128)(2,1)S(1)}, u32[]{:S(2)}, u32[]{:S(2)}) collective-permute-start(bf16[128,256]{1,0:T(8,128)(2,1)S(1)} %get-tuple-element.79), channel_id=1, source_target_pairs={{0,2},{1,3},{2,0},{3,1},{4,6},{5,7},{6,4},{7,5},{8,10},{9,11},{10,... | collective-permute-start | bytes 196616 | tf_op jit(solution)/shard_map/ppermute | solution.py:26
  28.4 6.4 %collective-permute-start.13 = (bf16[128,256]{1,0:T(8,128)(2,1)S(1)}, bf16[128,256]{1,0:T(8,128)(2,1)S(1)}, u32[]{:S(2)}, u32[]{:S(2)}) collective-permute-start(bf16[128,256]{1,0:T(8,128)(2,1)S(1)} %get-tuple-element.80), channel_id=1, source_target_pairs={{0,3},{1,2},{2,1},{3,0},{4,7},{5,6},{6,5},{7,4},{8,11},{9,10},{10,... | collective-permute-start | bytes 196616 | tf_op jit(solution)/shard_map/ppermute | solution.py:26
  31.2 6.7 %collective-permute-start.8 = (bf16[128,256]{1,0:T(8,128)(2,1)S(1)}, bf16[128,256]{1,0:T(8,128)(2,1)S(1)}, u32[]{:S(2)}, u32[]{:S(2)}) collective-permute-start(bf16[128,256]{1,0:T(8,128)(2,1)S(1)} %get-tuple-element.75), channel_id=1, source_target_pairs={{0,1},{1,0},{2,3},{3,2},{4,5},{5,4},{6,7},{7,6},{8,9},{9,8},{10,11... | collective-permute-start | bytes 196616 | tf_op jit(solution)/shard_map/ppermute | solution.py:26
  40.0 9.2 %collective-permute-start.18 = (bf16[256,256]{1,0:T(8,128)(2,1)}, bf16[256,256]{1,0:T(8,128)(2,1)S(1)}, u32[]{:S(2)}, u32[]{:S(2)}) collective-permute-start(bf16[256,256]{1,0:T(8,128)(2,1)} %get-tuple-element.95), channel_id=1, source_target_pairs={{0,28},{1,29},{2,30},{3,31},{4,24},{5,25},{6,26},{7,27},{8,4},{9,5... | collective-permute-start | bytes 393224 | tf_op jit(solution)/shard_map/ppermute | solution.py:34
  41.6 5.8 %collective-permute-start.19 = (bf16[128,256]{1,0:T(8,128)(2,1)}, bf16[128,256]{1,0:T(8,128)(2,1)S(1)}, u32[]{:S(2)}, u32[]{:S(2)}) collective-permute-start(bf16[128,256]{1,0:T(8,128)(2,1)} %get-tuple-element.96), channel_id=1, source_target_pairs={{0,27},{1,26},{2,25},{3,24},{4,31},{5,30},{6,29},{7,28},{8,3},{9,2... | collective-permute-start | bytes 196616 | tf_op jit(solution)/shard_map/ppermute | solution.py:34
  44.7 7.5 %collective-permute-start.16 = (bf16[128,256]{1,0:T(8,128)(2,1)}, bf16[128,256]{1,0:T(8,128)(2,1)S(1)}, u32[]{:S(2)}, u32[]{:S(2)}) collective-permute-start(bf16[128,256]{1,0:T(8,128)(2,1)} %get-tuple-element.90), channel_id=1, source_target_pairs={{0,25},{1,24},{2,27},{3,26},{4,29},{5,28},{6,31},{7,30},{8,1},{9,0... | collective-permute-start | bytes 196616 | tf_op jit(solution)/shard_map/ppermute | solution.py:34
  44.8 9.8 %collective-permute-start.15 = (bf16[256,256]{1,0:T(8,128)(2,1)S(1)}, bf16[256,256]{1,0:T(8,128)(2,1)S(1)}, u32[]{:S(2)}, u32[]{:S(2)}) collective-permute-start(bf16[256,256]{1,0:T(8,128)(2,1)S(1)} %get-tuple-element.89.refs_10_), channel_id=1, source_target_pairs={{0,24},{1,25},{2,26},{3,27},{4,28},{5,29},{6,30},{7,31},{8,0},{9,1... | collective-permute-start | bytes 393224 | tf_op jit(solution)/shard_map/ppermute | solution.py:34
  45.9 8.7 %collective-permute-start.17 = (bf16[128,256]{1,0:T(8,128)(2,1)}, bf16[128,256]{1,0:T(8,128)(2,1)S(1)}, u32[]{:S(2)}, u32[]{:S(2)}) collective-permute-start(bf16[128,256]{1,0:T(8,128)(2,1)} %copy-done.4), channel_id=1, source_target_pairs={{0,26},{1,27},{2,24},{3,25},{4,30},{5,31},{6,28},{7,29},{8,2},{9,3... | collective-permute-start | bytes 196616 | tf_op jit(solution)/shard_map/ppermute | solution.py:34
  52.2 6.1 %collective-permute-start.22 = (bf16[128,256]{1,0:T(8,128)(2,1)}, bf16[128,256]{1,0:T(8,128)(2,1)}, u32[]{:S(2)}, u32[]{:S(2)}) collective-permute-start(bf16[128,256]{1,0:T(8,128)(2,1)} %get-tuple-element.103), channel_id=1, source_target_pairs={{0,3},{1,2},{2,1},{3,0},{4,7},{5,6},{6,5},{7,4},{8,11},{9,10},{10,... | collective-permute-start | bytes 196616 | tf_op jit(solution)/shard_map/ppermute | solution.py:26
  59.9 9.4 %collective-permute-start.23 = (bf16[256,256]{1,0:T(8,128)(2,1)S(1)}, bf16[256,256]{1,0:T(8,128)(2,1)S(1)}, u32[]{:S(2)}, u32[]{:S(2)}) collective-permute-start(bf16[256,256]{1,0:T(8,128)(2,1)S(1)} %get-tuple-element.108.refs_2_), channel_id=1, source_target_pairs={{0,4},{1,5},{2,6},{3,7},{4,0},{5,1},{6,2},{7,3},{8,12},{9,13},{10,... | collective-permute-start | bytes 393224 | tf_op jit(solution)/shard_map/ppermute | solution.py:26
  61.8 8.4 %collective-permute-start.24 = (bf16[256,256]{1,0:T(8,128)(2,1)S(1)}, bf16[256,256]{1,0:T(8,128)(2,1)S(1)}, u32[]{:S(2)}, u32[]{:S(2)}) collective-permute-start(bf16[256,256]{1,0:T(8,128)(2,1)S(1)} %get-tuple-element.109), channel_id=1, source_target_pairs={{0,1},{1,0},{2,3},{3,2},{4,5},{5,4},{6,7},{7,6},{8,9},{9,8},{10,11... | collective-permute-start | bytes 393224 | tf_op jit(solution)/shard_map/ppermute | solution.py:26
  62.7 7.6 %collective-permute-start.25 = (bf16[256,256]{1,0:T(8,128)(2,1)S(1)}, bf16[256,256]{1,0:T(8,128)(2,1)S(1)}, u32[]{:S(2)}, u32[]{:S(2)}) collective-permute-start(bf16[256,256]{1,0:T(8,128)(2,1)S(1)} %get-tuple-element.110), channel_id=1, source_target_pairs={{0,2},{1,3},{2,0},{3,1},{4,6},{5,7},{6,4},{7,5},{8,10},{9,11},{10,... | collective-permute-start | bytes 393224 | tf_op jit(solution)/shard_map/ppermute | solution.py:26
  63.1 9.2 %collective-permute-start.26 = (bf16[256,256]{1,0:T(8,128)(2,1)S(1)}, bf16[256,256]{1,0:T(8,128)(2,1)S(1)}, u32[]{:S(2)}, u32[]{:S(2)}) collective-permute-start(bf16[256,256]{1,0:T(8,128)(2,1)S(1)} %get-tuple-element.111), channel_id=1, source_target_pairs={{0,3},{1,2},{2,1},{3,0},{4,7},{5,6},{6,5},{7,4},{8,11},{9,10},{10,... | collective-permute-start | bytes 393224 | tf_op jit(solution)/shard_map/ppermute | solution.py:26
  69.3 9.8 %collective-permute-start.27 = (bf16[128,256]{1,0:T(8,128)(2,1)S(1)}, bf16[128,256]{1,0:T(8,128)(2,1)S(1)}, u32[]{:S(2)}, u32[]{:S(2)}) collective-permute-start(bf16[128,256]{1,0:T(8,128)(2,1)S(1)} %get-tuple-element.112), channel_id=1, source_target_pairs={{0,1},{1,0},{2,3},{3,2},{4,5},{5,4},{6,7},{7,6},{8,9},{9,8},{10,11... | collective-permute-start | bytes 196616 | tf_op jit(solution)/shard_map/ppermute | solution.py:26
  73.4 8.8 %collective-permute-start.28 = (bf16[128,256]{1,0:T(8,128)(2,1)S(1)}, bf16[128,256]{1,0:T(8,128)(2,1)S(1)}, u32[]{:S(2)}, u32[]{:S(2)}) collective-permute-start(bf16[128,256]{1,0:T(8,128)(2,1)S(1)} %get-tuple-element.113), channel_id=1, source_target_pairs={{0,2},{1,3},{2,0},{3,1},{4,6},{5,7},{6,4},{7,5},{8,10},{9,11},{10,... | collective-permute-start | bytes 196616 | tf_op jit(solution)/shard_map/ppermute | solution.py:26
  75.1 7.0 %collective-permute-start.29 = (bf16[128,256]{1,0:T(8,128)(2,1)S(1)}, bf16[128,256]{1,0:T(8,128)(2,1)S(1)}, u32[]{:S(2)}, u32[]{:S(2)}) collective-permute-start(bf16[128,256]{1,0:T(8,128)(2,1)S(1)} %get-tuple-element.114), channel_id=1, source_target_pairs={{0,3},{1,2},{2,1},{3,0},{4,7},{5,6},{6,5},{7,4},{8,11},{9,10},{10,... | collective-permute-start | bytes 196616 | tf_op jit(solution)/shard_map/ppermute | solution.py:26
  (16 other events, 147.6 us)

commit v21 on v19

--- a/solution.py
+++ b/solution.py
@@ -490,8 +490,6 @@
             call.want(VMEM, (tile * (1 + c["first"]), width), BF16, h - 1)
             relays = call.run(functools.partial(forward_kernel, c), "forward", small_cost)
             relayed = shared(relays)
-            if c["first"]:
-                asked_later, _ = lax.optimization_barrier((asked, relays))
             if layer == 0 and not final:
                 later, *_ = lax.optimization_barrier((words, *near))
                 adjs[tick + 1] = densify(tick + 1, later, tile_vals, row_tiles, n)
@@ -515,8 +513,6 @@
                 )
                 old = weight_acc[layer]
                 weight_acc[layer] = term if old is None else old + term
-                if c["first"]:
-                    got, weight_acc[layer] = lax.optimization_barrier((got, weight_acc[layer]))
         initial.append(toward)
         c = dict(base, tick=tick, final=final, joined=joined)
         call = Call()
@@ -524,7 +520,7 @@
         if not final:
             up = Call()
             up.give(HBM, preact, weights)
-            up.give(VMEM, *asked_later)
+            up.give(VMEM, *asked)
             length = rows + width + -(-2 * ticks * (h - 1) // 16) * 16
             up.want(VMEM, (length, width), BF16)
             up.scratch = [pltpu.SemaphoreType.DMA((2,))]

time: 85.4 us -> 83.4 us (0.977)
  waiting for transfers between devices: 20.5 us -> 22.8 us
  Pallas kernels: 13.2 us -> 11 us
  starting transfers between devices: 44.5 us -> 43 us
    pallas_call x16, Pallas kernels: 13.2 us -> 11 us  [run(): pl.pallas_call(kernel, out_shape=self.outs, in_specs=self.specs, out_spec...]
    ppermute x28, waiting for transfers between devices: 18.8 us -> 20.9 us  [swapped(): return lax.ppermute(block, 'rows', [(i, i ^ k) for i in range(n)])]
    ppermute x28, starting transfers between devices: 37.1 us -> 35.6 us  [swapped(): return lax.ppermute(block, 'rows', [(i, i ^ k) for i in range(n)])]
    optimization_barrier x1 -> x0, local copies, waits for them, and re-layouts: 1.08 us -> none  [shards(): got, weight_acc[layer] = lax.optimization_barrier((got, weight_acc[layer]))]
    mul x0 -> x1, local copies, waits for them, and re-layouts: none -> 1.08 us  [shards(): beta * jnp.dot(support[0, tick, layer].T, masked, preferred_element_type=...]
  transfers between devices with their start and end apart: 34 -> 34, of which waited for: 13 -> 15; matrix products, arithmetic and copies ran while one was open for 5% -> 5% of each run, Pallas kernels for 11% -> 11%
where the time goes in v21:
time: 83.4 us; the launch traced here: 83.2 us
  starting transfers between devices  43 us (52%)
  waiting for transfers between devices  22.8 us (27%)
  Pallas kernels  11 us (13%)
  matrix products  2.6 us (3%)
  other arithmetic  1.67 us (2%)
  local copies, waits for them, and re-layouts  1.1 us (1%)
  between operations  1.08 us (1%)
    ppermute x28, starting transfers between devices, swapped(): return lax.ppermute(block, 'rows', [(i, i ^ k) for i in range(n)])  35.6 us
    ppermute x28, waiting for transfers between devices, swapped(): return lax.ppermute(block, 'rows', [(i, i ^ k) for i in range(n)])  20.9 us
    pallas_call x16, Pallas kernels, run(): pl.pallas_call(kernel, out_shape=self.outs, in_specs=self.specs, out_spec...  11 us
    ppermute x5, starting transfers between devices, lowered(): return lax.ppermute(block, ('section', 'rows'), route)  7.37 us
    ppermute x5, waiting for transfers between devices, lowered(): return lax.ppermute(block, ('section', 'rows'), route)  1.96 us
  transfers between devices with their start and end apart: 34, of which 15 were waited for; matrix products, arithmetic and copies ran while one was open for 5% of the time, Pallas kernels for 11%

profile of v21, /device:TPU:0, one launch (start us, length us, event | category | flops | bytes accessed | tf_op | source)
XLA Modules:
  0.0 83.2 jit_solution(17028193534063115987)
XLA Ops:
  2.2 4.1 %collective-permute-start.3 = (bf16[256,256]{1,0:T(8,128)(2,1)S(1)}, bf16[256,256]{1,0:T(8,128)(2,1)S(1)}, u32[]{:S(2)}, u32[]{:S(2)}) collective-permute-start(bf16[256,256]{1,0:T(8,128)(2,1)S(1)} %fusion.3.refs_1_.refs_7_), channel_id=1, source_target_pairs={{0,4},{1,5},{2,6},{3,7},{4,0},{5,1},{6,2},{7,3},{8,12},{9,13},{10,... | collective-permute-start | bytes 393224 | tf_op jit(solution)/shard_map/ppermute | solution.py:26
  7.2 1.6 %collective-permute-start = (f32[4,256]{1,0:T(4,128)S(1)}, f32[4,256]{1,0:T(4,128)S(1)}, u32[]{:S(2)}, u32[]{:S(2)}) collective-permute-start(f32[4,256]{1,0:T(4,128)S(1)} %get-tuple-element.54), channel_id=1, source_target_pairs={{0,1},{1,0},{2,3},{3,2},{4,5},{5,4},{6,7},{7,6},{8,9},{9,8},{10,11... | collective-permute-start | bytes 12296 | tf_op jit(solution)/shard_map/ppermute | solution.py:26
  8.7 1.6 %collective-permute-start.1 = (f32[4,256]{1,0:T(4,128)S(1)}, f32[4,256]{1,0:T(4,128)S(1)}, u32[]{:S(2)}, u32[]{:S(2)}) collective-permute-start(f32[4,256]{1,0:T(4,128)S(1)} %get-tuple-element.55), channel_id=1, source_target_pairs={{0,2},{1,3},{2,0},{3,1},{4,6},{5,7},{6,4},{7,5},{8,10},{9,11},{10,... | collective-permute-start | bytes 12296 | tf_op jit(solution)/shard_map/ppermute | solution.py:26
  10.7 3.3 %densify.2.refs_6_.refs_1_ = bf16[256,1152]{1,0:T(8,128)(2,1)S(1)} custom-call(s32[2,96]{1,0:T(2,128)S(1)} %fusion.15.words_ref, bf16[1,2,96,128,128]{4,3,2,1,0:T(8,128)(2,1)} %vals_ref.3), custom_call_target="tpu_custom_call" | custom-call | flops 31457280 | bytes 3145728 | tf_op jit(solution)/shard_map/densify/pallas_call | solution.py:71
  15.6 1.6 %collective-permute-start.5 = (bf16[256,256]{1,0:T(8,128)(2,1)S(1)}, bf16[256,256]{1,0:T(8,128)(2,1)S(1)}, u32[]{:S(2)}, u32[]{:S(2)}) collective-permute-start(bf16[256,256]{1,0:T(8,128)(2,1)S(1)} %get-tuple-element.60), channel_id=1, source_target_pairs={{0,2},{1,3},{2,0},{3,1},{4,6},{5,7},{6,4},{7,5},{8,10},{9,11},{10,... | collective-permute-start | bytes 393224 | tf_op jit(solution)/shard_map/ppermute | solution.py:26
  18.8 2.5 %collective-permute-done.4.refs_9_ = bf16[256,256]{1,0:T(8,128)(2,1)S(1)} collective-permute-done((bf16[256,256]{1,0:T(8,128)(2,1)S(1)}, bf16[256,256]{1,0:T(8,128)(2,1)S(1)}, u32[]{:S(2)}, u32[]{:S(2)}) %collective-permute-start.4) | collective-permute-done | bytes 131104 | tf_op jit(solution)/shard_map/ppermute | solution.py:26
  21.3 1.8 %collective-permute-done.6.refs_11_ = bf16[256,256]{1,0:T(8,128)(2,1)S(1)} collective-permute-done((bf16[256,256]{1,0:T(8,128)(2,1)S(1)}, bf16[256,256]{1,0:T(8,128)(2,1)S(1)}, u32[]{:S(2)}, u32[]{:S(2)}) %collective-permute-start.6) | collective-permute-done | bytes 131104 | tf_op jit(solution)/shard_map/ppermute | solution.py:26
  23.6 1.5 %collective-permute-start.7 = (bf16[256,256]{1,0:T(8,128)(2,1)S(1)}, bf16[256,256]{1,0:T(8,128)(2,1)S(1)}, u32[]{:S(2)}, u32[]{:S(2)}) collective-permute-start(bf16[256,256]{1,0:T(8,128)(2,1)S(1)} %get-tuple-element.62.refs_2_), channel_id=1, source_target_pairs={{0,4},{1,5},{2,6},{3,7},{4,0},{5,1},{6,2},{7,3},{8,12},{9,13},{10,... | collective-permute-start | bytes 393224 | tf_op jit(solution)/shard_map/ppermute | solution.py:26
  26.6 1.7 %collective-permute-start.12 = (bf16[128,256]{1,0:T(8,128)(2,1)S(1)}, bf16[128,256]{1,0:T(8,128)(2,1)S(1)}, u32[]{:S(2)}, u32[]{:S(2)}) collective-permute-start(bf16[128,256]{1,0:T(8,128)(2,1)S(1)} %get-tuple-element.67), channel_id=1, source_target_pairs={{0,2},{1,3},{2,0},{3,1},{4,6},{5,7},{6,4},{7,5},{8,10},{9,11},{10,... | collective-permute-start | bytes 196616 | tf_op jit(solution)/shard_map/ppermute | solution.py:26
  28.6 2.4 %collective-permute-done.7.refs_0_.refs_3_ = bf16[256,256]{1,0:T(8,128)(2,1)S(1)} collective-permute-done((bf16[256,256]{1,0:T(8,128)(2,1)S(1)}, bf16[256,256]{1,0:T(8,128)(2,1)S(1)}, u32[]{:S(2)}, u32[]{:S(2)}) %collective-permute-start.7) | collective-permute-done | bytes 131104 | tf_op jit(solution)/shard_map/ppermute | solution.py:26
  32.9 1.7 %collective-permute-start.10 = (bf16[128,256]{1,0:T(8,128)(2,1)S(1)}, bf16[128,256]{1,0:T(8,128)(2,1)S(1)}, u32[]{:S(2)}, u32[]{:S(2)}) collective-permute-start(bf16[128,256]{1,0:T(8,128)(2,1)S(1)} %get-tuple-element.65), channel_id=1, source_target_pairs={{0,3},{1,2},{2,1},{3,0},{4,7},{5,6},{6,5},{7,4},{8,11},{9,10},{10,... | collective-permute-start | bytes 196616 | tf_op jit(solution)/shard_map/ppermute | solution.py:26
  34.6 3.3 %densify.3.refs_6_.refs_1_ = bf16[256,1152]{1,0:T(8,128)(2,1)S(1)} custom-call(s32[2,96]{1,0:T(2,128)S(1)} %fusion.15.words_ref, bf16[1,2,96,128,128]{4,3,2,1,0:T(8,128)(2,1)} %vals_ref.3), custom_call_target="tpu_custom_call" | custom-call | flops 31457280 | bytes 3145728 | tf_op jit(solution)/shard_map/densify/pallas_call | solution.py:71
  38.7 4.5 %collective-permute-start.18 = (bf16[256,256]{1,0:T(8,128)(2,1)S(1)}, bf16[256,256]{1,0:T(8,128)(2,1)S(1)}, u32[]{:S(2)}, u32[]{:S(2)}) collective-permute-start(bf16[256,256]{1,0:T(8,128)(2,1)S(1)} %get-tuple-element.79), channel_id=1, source_target_pairs={{0,28},{1,29},{2,30},{3,31},{4,24},{5,25},{6,26},{7,27},{8,4},{9,5... | collective-permute-start | bytes 393224 | tf_op jit(solution)/shard_map/ppermute | solution.py:34
  48.1 1.9 %collective-permute-done.19.refs_11_ = bf16[128,256]{1,0:T(8,128)(2,1)S(1)} collective-permute-done((bf16[128,256]{1,0:T(8,128)(2,1)S(1)}, bf16[128,256]{1,0:T(8,128)(2,1)S(1)}, u32[]{:S(2)}, u32[]{:S(2)}) %collective-permute-start.19) | collective-permute-done | bytes 65568 | tf_op jit(solution)/shard_map/ppermute | solution.py:34
  51.4 2.3 %collective-permute-start.22 = (bf16[128,256]{1,0:T(8,128)(2,1)S(1)}, bf16[128,256]{1,0:T(8,128)(2,1)S(1)}, u32[]{:S(2)}, u32[]{:S(2)}) collective-permute-start(bf16[128,256]{1,0:T(8,128)(2,1)S(1)} %get-tuple-element.87), channel_id=1, source_target_pairs={{0,3},{1,2},{2,1},{3,0},{4,7},{5,6},{6,5},{7,4},{8,11},{9,10},{10,... | collective-permute-start | bytes 196616 | tf_op jit(solution)/shard_map/ppermute | solution.py:26
  58.3 1.5 %collective-permute-start.24 = (bf16[256,256]{1,0:T(8,128)(2,1)S(1)}, bf16[256,256]{1,0:T(8,128)(2,1)S(1)}, u32[]{:S(2)}, u32[]{:S(2)}) collective-permute-start(bf16[256,256]{1,0:T(8,128)(2,1)S(1)} %get-tuple-element.93), channel_id=1, source_target_pairs={{0,1},{1,0},{2,3},{3,2},{4,5},{5,4},{6,7},{7,6},{8,9},{9,8},{10,11... | collective-permute-start | bytes 393224 | tf_op jit(solution)/shard_map/ppermute | solution.py:26
  60.3 1.5 %collective-permute-start.26 = (bf16[256,256]{1,0:T(8,128)(2,1)S(1)}, bf16[256,256]{1,0:T(8,128)(2,1)S(1)}, u32[]{:S(2)}, u32[]{:S(2)}) collective-permute-start(bf16[256,256]{1,0:T(8,128)(2,1)S(1)} %get-tuple-element.95), channel_id=1, source_target_pairs={{0,3},{1,2},{2,1},{3,0},{4,7},{5,6},{6,5},{7,4},{8,11},{9,10},{10,... | collective-permute-start | bytes 393224 | tf_op jit(solution)/shard_map/ppermute | solution.py:26
  61.9 4.4 %collective-permute-done.23.refs_0_.refs_3_ = bf16[256,256]{1,0:T(8,128)(2,1)S(1)} collective-permute-done((bf16[256,256]{1,0:T(8,128)(2,1)S(1)}, bf16[256,256]{1,0:T(8,128)(2,1)S(1)}, u32[]{:S(2)}, u32[]{:S(2)}) %collective-permute-start.23) | collective-permute-done | bytes 131104 | tf_op jit(solution)/shard_map/ppermute | solution.py:26
  67.8 1.9 %collective-permute-done.26.refs_6_.refs_4_ = bf16[256,256]{1,0:T(8,128)(2,1)S(1)} collective-permute-done((bf16[256,256]{1,0:T(8,128)(2,1)S(1)}, bf16[256,256]{1,0:T(8,128)(2,1)S(1)}, u32[]{:S(2)}, u32[]{:S(2)}) %collective-permute-start.26) | collective-permute-done | bytes 131104 | tf_op jit(solution)/shard_map/ppermute | solution.py:26
  69.7 1.5 %collective-permute-start.30 = (bf16[2,64,256]{2,1,0:T(8,128)(2,1)S(1)}, bf16[2,64,256]{2,1,0:T(8,128)(2,1)S(1)}, u32[]{:S(2)}, u32[]{:S(2)}) collective-permute-start(bf16[2,64,256]{2,1,0:T(8,128)(2,1)S(1)} %half_sum.1.mine_ref), channel_id=1, source_target_pairs={{0,4},{1,5},{2,6},{3,7},{4,0},{5,1},{6,2},{7,3},{8,12},{9,13},{10,... | collective-permute-start | bytes 196616 | tf_op jit(solution)/shard_map/ppermute | solution.py:26
  71.3 1.8 %collective-permute-start.28 = (bf16[128,256]{1,0:T(8,128)(2,1)S(1)}, bf16[128,256]{1,0:T(8,128)(2,1)S(1)}, u32[]{:S(2)}, u32[]{:S(2)}) collective-permute-start(bf16[128,256]{1,0:T(8,128)(2,1)S(1)} %get-tuple-element.97), channel_id=1, source_target_pairs={{0,2},{1,3},{2,0},{3,1},{4,6},{5,7},{6,4},{7,5},{8,10},{9,11},{10,... | collective-permute-start | bytes 196616 | tf_op jit(solution)/shard_map/ppermute | solution.py:26
  73.9 1.5 %collective-permute-done.30.far_ref = bf16[2,64,256]{2,1,0:T(8,128)(2,1)S(1)} collective-permute-done((bf16[2,64,256]{2,1,0:T(8,128)(2,1)S(1)}, bf16[2,64,256]{2,1,0:T(8,128)(2,1)S(1)}, u32[]{:S(2)}, u32[]{:S(2)}) %collective-permute-start.30) | collective-permute-done | bytes 65568 | tf_op jit(solution)/shard_map/ppermute | solution.py:26
  75.5 1.7 %collective-permute-start.31 = (bf16[2,64,256]{2,1,0:T(8,128)(2,1)S(1)}, bf16[2,64,256]{2,1,0:T(8,128)(2,1)S(1)}, u32[]{:S(2)}, u32[]{:S(2)}) collective-permute-start(bf16[2,64,256]{2,1,0:T(8,128)(2,1)S(1)} %total.1.refs_0_), channel_id=1, source_target_pairs={{0,1},{1,0},{2,3},{3,2},{4,5},{5,4},{6,7},{7,6},{8,9},{9,8},{10,11... | collective-permute-start | bytes 196616 | tf_op jit(solution)/shard_map/ppermute | solution.py:26
  77.3 1.8 %collective-permute-start.33 = (bf16[2,64,256]{2,1,0:T(8,128)(2,1)S(1)}, bf16[2,64,256]{2,1,0:T(8,128)(2,1)S(1)}, u32[]{:S(2)}, u32[]{:S(2)}) collective-permute-start(bf16[2,64,256]{2,1,0:T(8,128)(2,1)S(1)} %total.1.refs_0_), channel_id=1, source_target_pairs={{0,3},{1,2},{2,1},{3,0},{4,7},{5,6},{6,5},{7,4},{8,11},{9,10},{10,... | collective-permute-start | bytes 196616 | tf_op jit(solution)/shard_map/ppermute | solution.py:26
  (78 shorter events, 28.9 us)
Async XLA Ops:
  2.2 12.6 %collective-permute-start.3 = (bf16[256,256]{1,0:T(8,128)(2,1)S(1)}, bf16[256,256]{1,0:T(8,128)(2,1)S(1)}, u32[]{:S(2)}, u32[]{:S(2)}) collective-permute-start(bf16[256,256]{1,0:T(8,128)(2,1)S(1)} %fusion.3.refs_1_.refs_7_), channel_id=1, source_target_pairs={{0,4},{1,5},{2,6},{3,7},{4,0},{5,1},{6,2},{7,3},{8,12},{9,13},{10,... | collective-permute-start | bytes 393224 | tf_op jit(solution)/shard_map/ppermute | solution.py:26
  7.2 6.9 %collective-permute-start = (f32[4,256]{1,0:T(4,128)S(1)}, f32[4,256]{1,0:T(4,128)S(1)}, u32[]{:S(2)}, u32[]{:S(2)}) collective-permute-start(f32[4,256]{1,0:T(4,128)S(1)} %get-tuple-element.54), channel_id=1, source_target_pairs={{0,1},{1,0},{2,3},{3,2},{4,5},{5,4},{6,7},{7,6},{8,9},{9,8},{10,11... | collective-permute-start | bytes 12296 | tf_op jit(solution)/shard_map/ppermute | solution.py:26
  14.9 6.4 %collective-permute-start.4 = (bf16[256,256]{1,0:T(8,128)(2,1)S(1)}, bf16[256,256]{1,0:T(8,128)(2,1)S(1)}, u32[]{:S(2)}, u32[]{:S(2)}) collective-permute-start(bf16[256,256]{1,0:T(8,128)(2,1)S(1)} %get-tuple-element.59), channel_id=1, source_target_pairs={{0,1},{1,0},{2,3},{3,2},{4,5},{5,4},{6,7},{7,6},{8,9},{9,8},{10,11... | collective-permute-start | bytes 393224 | tf_op jit(solution)/shard_map/ppermute | solution.py:26
  17.2 5.9 %collective-permute-start.6 = (bf16[256,256]{1,0:T(8,128)(2,1)S(1)}, bf16[256,256]{1,0:T(8,128)(2,1)S(1)}, u32[]{:S(2)}, u32[]{:S(2)}) collective-permute-start(bf16[256,256]{1,0:T(8,128)(2,1)S(1)} %get-tuple-element.61), channel_id=1, source_target_pairs={{0,3},{1,2},{2,1},{3,0},{4,7},{5,6},{6,5},{7,4},{8,11},{9,10},{10,... | collective-permute-start | bytes 393224 | tf_op jit(solution)/shard_map/ppermute | solution.py:26
  18.8 19.3 %collective-permute-start.14 = (bf16[528,256]{1,0:T(8,128)(2,1)S(1)}, bf16[528,256]{1,0:T(8,128)(2,1)S(1)}, u32[]{:S(2)}, u32[]{:S(2)}) collective-permute-start(bf16[528,256]{1,0:T(8,128)(2,1)S(1)} %pack.1), channel_id=1, source_target_pairs={{0,8},{8,16},{16,24},{24,0},{1,9},{9,17},{17,25},{25,1},{2,10},{10... | collective-permute-start | bytes 811016 | tf_op jit(solution)/shard_map/ppermute | solution.py:39
  23.6 7.4 %collective-permute-start.7 = (bf16[256,256]{1,0:T(8,128)(2,1)S(1)}, bf16[256,256]{1,0:T(8,128)(2,1)S(1)}, u32[]{:S(2)}, u32[]{:S(2)}) collective-permute-start(bf16[256,256]{1,0:T(8,128)(2,1)S(1)} %get-tuple-element.62.refs_2_), channel_id=1, source_target_pairs={{0,4},{1,5},{2,6},{3,7},{4,0},{5,1},{6,2},{7,3},{8,12},{9,13},{10,... | collective-permute-start | bytes 393224 | tf_op jit(solution)/shard_map/ppermute | solution.py:26
  25.1 7.2 %collective-permute-start.11 = (bf16[128,256]{1,0:T(8,128)(2,1)S(1)}, bf16[128,256]{1,0:T(8,128)(2,1)S(1)}, u32[]{:S(2)}, u32[]{:S(2)}) collective-permute-start(bf16[128,256]{1,0:T(8,128)(2,1)S(1)} %get-tuple-element.66), channel_id=1, source_target_pairs={{0,1},{1,0},{2,3},{3,2},{4,5},{5,4},{6,7},{7,6},{8,9},{9,8},{10,11... | collective-permute-start | bytes 196616 | tf_op jit(solution)/shard_map/ppermute | solution.py:26
  26.6 6.4 %collective-permute-start.12 = (bf16[128,256]{1,0:T(8,128)(2,1)S(1)}, bf16[128,256]{1,0:T(8,128)(2,1)S(1)}, u32[]{:S(2)}, u32[]{:S(2)}) collective-permute-start(bf16[128,256]{1,0:T(8,128)(2,1)S(1)} %get-tuple-element.67), channel_id=1, source_target_pairs={{0,2},{1,3},{2,0},{3,1},{4,6},{5,7},{6,4},{7,5},{8,10},{9,11},{10,... | collective-permute-start | bytes 196616 | tf_op jit(solution)/shard_map/ppermute | solution.py:26
  28.3 6.3 %collective-permute-start.13 = (bf16[128,256]{1,0:T(8,128)(2,1)S(1)}, bf16[128,256]{1,0:T(8,128)(2,1)S(1)}, u32[]{:S(2)}, u32[]{:S(2)}) collective-permute-start(bf16[128,256]{1,0:T(8,128)(2,1)S(1)} %get-tuple-element.68), channel_id=1, source_target_pairs={{0,3},{1,2},{2,1},{3,0},{4,7},{5,6},{6,5},{7,4},{8,11},{9,10},{10,... | collective-permute-start | bytes 196616 | tf_op jit(solution)/shard_map/ppermute | solution.py:26
  31.0 6.9 %collective-permute-start.8 = (bf16[128,256]{1,0:T(8,128)(2,1)S(1)}, bf16[128,256]{1,0:T(8,128)(2,1)S(1)}, u32[]{:S(2)}, u32[]{:S(2)}) collective-permute-start(bf16[128,256]{1,0:T(8,128)(2,1)S(1)} %get-tuple-element.63), channel_id=1, source_target_pairs={{0,1},{1,0},{2,3},{3,2},{4,5},{5,4},{6,7},{7,6},{8,9},{9,8},{10,11... | collective-permute-start | bytes 196616 | tf_op jit(solution)/shard_map/ppermute | solution.py:26
  38.6 12.8 %collective-permute-start.16 = (bf16[128,256]{1,0:T(8,128)(2,1)S(1)}, bf16[128,256]{1,0:T(8,128)(2,1)S(1)}, u32[]{:S(2)}, u32[]{:S(2)}) collective-permute-start(bf16[128,256]{1,0:T(8,128)(2,1)S(1)} %get-tuple-element.75), channel_id=1, source_target_pairs={{0,25},{1,24},{2,27},{3,26},{4,29},{5,28},{6,31},{7,30},{8,1},{9,0... | collective-permute-start | bytes 196616 | tf_op jit(solution)/shard_map/ppermute | solution.py:34
  38.7 11.4 %collective-permute-start.18 = (bf16[256,256]{1,0:T(8,128)(2,1)S(1)}, bf16[256,256]{1,0:T(8,128)(2,1)S(1)}, u32[]{:S(2)}, u32[]{:S(2)}) collective-permute-start(bf16[256,256]{1,0:T(8,128)(2,1)S(1)} %get-tuple-element.79), channel_id=1, source_target_pairs={{0,28},{1,29},{2,30},{3,31},{4,24},{5,25},{6,26},{7,27},{8,4},{9,5... | collective-permute-start | bytes 393224 | tf_op jit(solution)/shard_map/ppermute | solution.py:34
  43.2 6.8 %collective-permute-start.19 = (bf16[128,256]{1,0:T(8,128)(2,1)S(1)}, bf16[128,256]{1,0:T(8,128)(2,1)S(1)}, u32[]{:S(2)}, u32[]{:S(2)}) collective-permute-start(bf16[128,256]{1,0:T(8,128)(2,1)S(1)} %get-tuple-element.80), channel_id=1, source_target_pairs={{0,27},{1,26},{2,25},{3,24},{4,31},{5,30},{6,29},{7,28},{8,3},{9,2... | collective-permute-start | bytes 196616 | tf_op jit(solution)/shard_map/ppermute | solution.py:34
  45.6 8.3 %collective-permute-start.15 = (bf16[256,256]{1,0:T(8,128)(2,1)S(1)}, bf16[256,256]{1,0:T(8,128)(2,1)S(1)}, u32[]{:S(2)}, u32[]{:S(2)}) collective-permute-start(bf16[256,256]{1,0:T(8,128)(2,1)S(1)} %get-tuple-element.74.refs_10_), channel_id=1, source_target_pairs={{0,24},{1,25},{2,26},{3,27},{4,28},{5,29},{6,30},{7,31},{8,0},{9,1... | collective-permute-start | bytes 393224 | tf_op jit(solution)/shard_map/ppermute | solution.py:34
  46.7 7.2 %collective-permute-start.17 = (bf16[128,256]{1,0:T(8,128)(2,1)S(1)}, bf16[128,256]{1,0:T(8,128)(2,1)S(1)}, u32[]{:S(2)}, u32[]{:S(2)}) collective-permute-start(bf16[128,256]{1,0:T(8,128)(2,1)S(1)} %get-tuple-element.76), channel_id=1, source_target_pairs={{0,26},{1,27},{2,24},{3,25},{4,30},{5,31},{6,28},{7,29},{8,2},{9,3... | collective-permute-start | bytes 196616 | tf_op jit(solution)/shard_map/ppermute | solution.py:34
  51.4 6.2 %collective-permute-start.22 = (bf16[128,256]{1,0:T(8,128)(2,1)S(1)}, bf16[128,256]{1,0:T(8,128)(2,1)S(1)}, u32[]{:S(2)}, u32[]{:S(2)}) collective-permute-start(bf16[128,256]{1,0:T(8,128)(2,1)S(1)} %get-tuple-element.87), channel_id=1, source_target_pairs={{0,3},{1,2},{2,1},{3,0},{4,7},{5,6},{6,5},{7,4},{8,11},{9,10},{10,... | collective-permute-start | bytes 196616 | tf_op jit(solution)/shard_map/ppermute | solution.py:26
  58.2 8.1 %collective-permute-start.23 = (bf16[256,256]{1,0:T(8,128)(2,1)S(1)}, bf16[256,256]{1,0:T(8,128)(2,1)S(1)}, u32[]{:S(2)}, u32[]{:S(2)}) collective-permute-start(bf16[256,256]{1,0:T(8,128)(2,1)S(1)} %get-tuple-element.92.refs_2_), channel_id=1, source_target_pairs={{0,4},{1,5},{2,6},{3,7},{4,0},{5,1},{6,2},{7,3},{8,12},{9,13},{10,... | collective-permute-start | bytes 393224 | tf_op jit(solution)/shard_map/ppermute | solution.py:26
  58.3 8.9 %collective-permute-start.24 = (bf16[256,256]{1,0:T(8,128)(2,1)S(1)}, bf16[256,256]{1,0:T(8,128)(2,1)S(1)}, u32[]{:S(2)}, u32[]{:S(2)}) collective-permute-start(bf16[256,256]{1,0:T(8,128)(2,1)S(1)} %get-tuple-element.93), channel_id=1, source_target_pairs={{0,1},{1,0},{2,3},{3,2},{4,5},{5,4},{6,7},{7,6},{8,9},{9,8},{10,11... | collective-permute-start | bytes 393224 | tf_op jit(solution)/shard_map/ppermute | solution.py:26
  59.7 8.0 %collective-permute-start.25 = (bf16[256,256]{1,0:T(8,128)(2,1)S(1)}, bf16[256,256]{1,0:T(8,128)(2,1)S(1)}, u32[]{:S(2)}, u32[]{:S(2)}) collective-permute-start(bf16[256,256]{1,0:T(8,128)(2,1)S(1)} %get-tuple-element.94), channel_id=1, source_target_pairs={{0,2},{1,3},{2,0},{3,1},{4,6},{5,7},{6,4},{7,5},{8,10},{9,11},{10,... | collective-permute-start | bytes 393224 | tf_op jit(solution)/shard_map/ppermute | solution.py:26
  60.3 9.4 %collective-permute-start.26 = (bf16[256,256]{1,0:T(8,128)(2,1)S(1)}, bf16[256,256]{1,0:T(8,128)(2,1)S(1)}, u32[]{:S(2)}, u32[]{:S(2)}) collective-permute-start(bf16[256,256]{1,0:T(8,128)(2,1)S(1)} %get-tuple-element.95), channel_id=1, source_target_pairs={{0,3},{1,2},{2,1},{3,0},{4,7},{5,6},{6,5},{7,4},{8,11},{9,10},{10,... | collective-permute-start | bytes 393224 | tf_op jit(solution)/shard_map/ppermute | solution.py:26
  66.3 11.0 %collective-permute-start.27 = (bf16[128,256]{1,0:T(8,128)(2,1)S(1)}, bf16[128,256]{1,0:T(8,128)(2,1)S(1)}, u32[]{:S(2)}, u32[]{:S(2)}) collective-permute-start(bf16[128,256]{1,0:T(8,128)(2,1)S(1)} %get-tuple-element.96), channel_id=1, source_target_pairs={{0,1},{1,0},{2,3},{3,2},{4,5},{5,4},{6,7},{7,6},{8,9},{9,8},{10,11... | collective-permute-start | bytes 196616 | tf_op jit(solution)/shard_map/ppermute | solution.py:26
  69.7 5.7 %collective-permute-start.30 = (bf16[2,64,256]{2,1,0:T(8,128)(2,1)S(1)}, bf16[2,64,256]{2,1,0:T(8,128)(2,1)S(1)}, u32[]{:S(2)}, u32[]{:S(2)}) collective-permute-start(bf16[2,64,256]{2,1,0:T(8,128)(2,1)S(1)} %half_sum.1.mine_ref), channel_id=1, source_target_pairs={{0,4},{1,5},{2,6},{3,7},{4,0},{5,1},{6,2},{7,3},{8,12},{9,13},{10,... | collective-permute-start | bytes 196616 | tf_op jit(solution)/shard_map/ppermute | solution.py:26
  71.3 8.6 %collective-permute-start.28 = (bf16[128,256]{1,0:T(8,128)(2,1)S(1)}, bf16[128,256]{1,0:T(8,128)(2,1)S(1)}, u32[]{:S(2)}, u32[]{:S(2)}) collective-permute-start(bf16[128,256]{1,0:T(8,128)(2,1)S(1)} %get-tuple-element.97), channel_id=1, source_target_pairs={{0,2},{1,3},{2,0},{3,1},{4,6},{5,7},{6,4},{7,5},{8,10},{9,11},{10,... | collective-permute-start | bytes 196616 | tf_op jit(solution)/shard_map/ppermute | solution.py:26
  73.0 6.8 %collective-permute-start.29 = (bf16[128,256]{1,0:T(8,128)(2,1)S(1)}, bf16[128,256]{1,0:T(8,128)(2,1)S(1)}, u32[]{:S(2)}, u32[]{:S(2)}) collective-permute-start(bf16[128,256]{1,0:T(8,128)(2,1)S(1)} %get-tuple-element.98), channel_id=1, source_target_pairs={{0,3},{1,2},{2,1},{3,0},{4,7},{5,6},{6,5},{7,4},{8,11},{9,10},{10,... | collective-permute-start | bytes 196616 | tf_op jit(solution)/shard_map/ppermute | solution.py:26
  (15 other events, 169.5 us)

commit v22 on v18

--- a/solution.py
+++ b/solution.py
@@ -536,7 +536,8 @@
         call.give(VMEM, *handed)
         call.want(HBM, (ticks, 1, rows, width), BF16)
         call.scratch = [pltpu.VMEM((rows, width), BF16), pltpu.SemaphoreType.DMA((ticks,))]
-        (handoff,) = call.run(functools.partial(exit_kernel, c), "exit", layer_cost)
+        exit_cost = cost(16 * 2 * rows * width * (n + 1) * tile, 16 * 2 * n * rows * width)
+        (handoff,) = call.run(functools.partial(exit_kernel, c), "exit", exit_cost)
     call = Call()
     call.give(VMEM, mine, swapped(mine, h))
     call.want(VMEM, (layers, chunk, width), BF16)

time: 83.4 us -> 87.5 us (1.049)
  Pallas kernels: 9.63 us -> 12.5 us
  starting transfers between devices: 43.3 us -> 44.4 us
    pallas_call x16, Pallas kernels: 9.63 us -> 12.5 us  [run(): pl.pallas_call(kernel, out_shape=self.outs, in_specs=self.specs, out_spec...]
    ppermute x5, waiting for transfers between devices: 1.82 us -> 4.66 us  [lowered(): return lax.ppermute(block, ('section', 'rows'), route)]
    ppermute x28, waiting for transfers between devices: 21.8 us -> 19.1 us  [swapped(): return lax.ppermute(block, 'rows', [(i, i ^ k) for i in range(n)])]
    ppermute x28, starting transfers between devices: 35.9 us -> 37.3 us  [swapped(): return lax.ppermute(block, 'rows', [(i, i ^ k) for i in range(n)])]
  transfers between devices with their start and end apart: 34 -> 34, of which waited for: 14 -> 14; matrix products, arithmetic and copies ran while one was open for 5% -> 5% of each run, Pallas kernels for 9% -> 10%
where the time goes in v22:
time: 87.5 us; the launch traced here: 87.3 us
  starting transfers between devices  44.4 us (51%)
  waiting for transfers between devices  23.8 us (27%)
  Pallas kernels  12.5 us (14%)
  matrix products  2.63 us (3%)
  other arithmetic  1.71 us (2%)
  local copies, waits for them, and re-layouts  1.1 us (1%)
  between operations  1.08 us (1%)
    ppermute x28, starting transfers between devices, swapped(): return lax.ppermute(block, 'rows', [(i, i ^ k) for i in range(n)])  37.3 us
    ppermute x28, waiting for transfers between devices, swapped(): return lax.ppermute(block, 'rows', [(i, i ^ k) for i in range(n)])  19.1 us
    pallas_call x16, Pallas kernels, run(): pl.pallas_call(kernel, out_shape=self.outs, in_specs=self.specs, out_spec...  12.5 us
    ppermute x5, starting transfers between devices, lowered(): return lax.ppermute(block, ('section', 'rows'), route)  7.04 us
    ppermute x5, waiting for transfers between devices, lowered(): return lax.ppermute(block, ('section', 'rows'), route)  4.66 us
  transfers between devices with their start and end apart: 34, of which 14 were waited for; matrix products, arithmetic and copies ran while one was open for 5% of the time, Pallas kernels for 10%

profile of v22, /device:TPU:0, one launch (start us, length us, event | category | flops | bytes accessed | tf_op | source)
XLA Modules:
  0.0 87.3 jit_solution(13596694529735084830)
XLA Ops:
  2.2 4.1 %collective-permute-start.3 = (bf16[256,256]{1,0:T(8,128)(2,1)S(1)}, bf16[256,256]{1,0:T(8,128)(2,1)S(1)}, u32[]{:S(2)}, u32[]{:S(2)}) collective-permute-start(bf16[256,256]{1,0:T(8,128)(2,1)S(1)} %fusion.3.refs_1_.refs_7_), channel_id=1, source_target_pairs={{0,4},{1,5},{2,6},{3,7},{4,0},{5,1},{6,2},{7,3},{8,12},{9,13},{10,... | collective-permute-start | bytes 393224 | tf_op jit(solution)/shard_map/ppermute | solution.py:26
  7.2 1.6 %collective-permute-start = (f32[4,256]{1,0:T(4,128)S(1)}, f32[4,256]{1,0:T(4,128)S(1)}, u32[]{:S(2)}, u32[]{:S(2)}) collective-permute-start(f32[4,256]{1,0:T(4,128)S(1)} %get-tuple-element.54), channel_id=1, source_target_pairs={{0,1},{1,0},{2,3},{3,2},{4,5},{5,4},{6,7},{7,6},{8,9},{9,8},{10,11... | collective-permute-start | bytes 12296 | tf_op jit(solution)/shard_map/ppermute | solution.py:26
  8.8 1.6 %collective-permute-start.1 = (f32[4,256]{1,0:T(4,128)S(1)}, f32[4,256]{1,0:T(4,128)S(1)}, u32[]{:S(2)}, u32[]{:S(2)}) collective-permute-start(f32[4,256]{1,0:T(4,128)S(1)} %get-tuple-element.55), channel_id=1, source_target_pairs={{0,2},{1,3},{2,0},{3,1},{4,6},{5,7},{6,4},{7,5},{8,10},{9,11},{10,... | collective-permute-start | bytes 12296 | tf_op jit(solution)/shard_map/ppermute | solution.py:26
  10.8 3.3 %densify.2.refs_6_.refs_1_ = bf16[256,1152]{1,0:T(8,128)(2,1)S(1)} custom-call(s32[2,96]{1,0:T(2,128)S(1)} %fusion.15.words_ref, bf16[1,2,96,128,128]{4,3,2,1,0:T(8,128)(2,1)} %vals_ref.3), custom_call_target="tpu_custom_call" | custom-call | flops 31457280 | bytes 3145728 | tf_op jit(solution)/shard_map/densify/pallas_call | solution.py:71
  16.7 1.8 %collective-permute-start.6 = (bf16[256,256]{1,0:T(8,128)(2,1)S(1)}, bf16[256,256]{1,0:T(8,128)(2,1)S(1)}, u32[]{:S(2)}, u32[]{:S(2)}) collective-permute-start(bf16[256,256]{1,0:T(8,128)(2,1)S(1)} %get-tuple-element.61), channel_id=1, source_target_pairs={{0,3},{1,2},{2,1},{3,0},{4,7},{5,6},{6,5},{7,4},{8,11},{9,10},{10,... | collective-permute-start | bytes 393224 | tf_op jit(solution)/shard_map/ppermute | solution.py:26
  18.5 2.7 %collective-permute-done.4.refs_9_ = bf16[256,256]{1,0:T(8,128)(2,1)S(1)} collective-permute-done((bf16[256,256]{1,0:T(8,128)(2,1)S(1)}, bf16[256,256]{1,0:T(8,128)(2,1)S(1)}, u32[]{:S(2)}, u32[]{:S(2)}) %collective-permute-start.4) | collective-permute-done | bytes 131104 | tf_op jit(solution)/shard_map/ppermute | solution.py:26
  21.2 1.7 %collective-permute-done.6.refs_11_ = bf16[256,256]{1,0:T(8,128)(2,1)S(1)} collective-permute-done((bf16[256,256]{1,0:T(8,128)(2,1)S(1)}, bf16[256,256]{1,0:T(8,128)(2,1)S(1)}, u32[]{:S(2)}, u32[]{:S(2)}) %collective-permute-start.6) | collective-permute-done | bytes 131104 | tf_op jit(solution)/shard_map/ppermute | solution.py:26
  24.0 1.7 %collective-permute-start.7 = (bf16[256,256]{1,0:T(8,128)(2,1)S(1)}, bf16[256,256]{1,0:T(8,128)(2,1)S(1)}, u32[]{:S(2)}, u32[]{:S(2)}) collective-permute-start(bf16[256,256]{1,0:T(8,128)(2,1)S(1)} %get-tuple-element.62.refs_2_), channel_id=1, source_target_pairs={{0,4},{1,5},{2,6},{3,7},{4,0},{5,1},{6,2},{7,3},{8,12},{9,13},{10,... | collective-permute-start | bytes 393224 | tf_op jit(solution)/shard_map/ppermute | solution.py:26
  27.2 1.7 %collective-permute-start.12 = (bf16[128,256]{1,0:T(8,128)(2,1)S(1)}, bf16[128,256]{1,0:T(8,128)(2,1)S(1)}, u32[]{:S(2)}, u32[]{:S(2)}) collective-permute-start(bf16[128,256]{1,0:T(8,128)(2,1)S(1)} %get-tuple-element.67), channel_id=1, source_target_pairs={{0,2},{1,3},{2,0},{3,1},{4,6},{5,7},{6,4},{7,5},{8,10},{9,11},{10,... | collective-permute-start | bytes 196616 | tf_op jit(solution)/shard_map/ppermute | solution.py:26
  29.7 1.6 %collective-permute-done.7.refs_0_.refs_3_ = bf16[256,256]{1,0:T(8,128)(2,1)S(1)} collective-permute-done((bf16[256,256]{1,0:T(8,128)(2,1)S(1)}, bf16[256,256]{1,0:T(8,128)(2,1)S(1)}, u32[]{:S(2)}, u32[]{:S(2)}) %collective-permute-start.7) | collective-permute-done | bytes 131104 | tf_op jit(solution)/shard_map/ppermute | solution.py:26
  37.6 2.6 %densify.3.refs_6_.refs_1_ = bf16[256,1152]{1,0:T(8,128)(2,1)S(1)} custom-call(s32[2,96]{1,0:T(2,128)S(1)} %fusion.15.words_ref, bf16[1,2,96,128,128]{4,3,2,1,0:T(8,128)(2,1)} %vals_ref.3), custom_call_target="tpu_custom_call" | custom-call | flops 31457280 | bytes 3145728 | tf_op jit(solution)/shard_map/densify/pallas_call | solution.py:71
  41.8 2.2 %collective-permute-start.17 = (bf16[256,256]{1,0:T(8,128)(2,1)S(1)}, bf16[256,256]{1,0:T(8,128)(2,1)S(1)}, u32[]{:S(2)}, u32[]{:S(2)}) collective-permute-start(bf16[256,256]{1,0:T(8,128)(2,1)S(1)} %get-tuple-element.78), channel_id=1, source_target_pairs={{0,28},{1,29},{2,30},{3,31},{4,24},{5,25},{6,26},{7,27},{8,4},{9,5... | collective-permute-start | bytes 393224 | tf_op jit(solution)/shard_map/ppermute | solution.py:34
  44.0 2.6 %collective-permute-start.18 = (bf16[128,256]{1,0:T(8,128)(2,1)S(1)}, bf16[128,256]{1,0:T(8,128)(2,1)S(1)}, u32[]{:S(2)}, u32[]{:S(2)}) collective-permute-start(bf16[128,256]{1,0:T(8,128)(2,1)S(1)} %get-tuple-element.79), channel_id=1, source_target_pairs={{0,26},{1,27},{2,24},{3,25},{4,30},{5,31},{6,28},{7,29},{8,2},{9,3... | collective-permute-start | bytes 196616 | tf_op jit(solution)/shard_map/ppermute | solution.py:34
  46.5 1.7 %collective-permute-start.19 = (bf16[128,256]{1,0:T(8,128)(2,1)S(1)}, bf16[128,256]{1,0:T(8,128)(2,1)S(1)}, u32[]{:S(2)}, u32[]{:S(2)}) collective-permute-start(bf16[128,256]{1,0:T(8,128)(2,1)S(1)} %get-tuple-element.80), channel_id=1, source_target_pairs={{0,27},{1,26},{2,25},{3,24},{4,31},{5,30},{6,29},{7,28},{8,3},{9,2... | collective-permute-start | bytes 196616 | tf_op jit(solution)/shard_map/ppermute | solution.py:34
  49.2 4.3 %collective-permute-done.19.refs_11_ = bf16[128,256]{1,0:T(8,128)(2,1)S(1)} collective-permute-done((bf16[128,256]{1,0:T(8,128)(2,1)S(1)}, bf16[128,256]{1,0:T(8,128)(2,1)S(1)}, u32[]{:S(2)}, u32[]{:S(2)}) %collective-permute-start.19) | collective-permute-done | bytes 65568 | tf_op jit(solution)/shard_map/ppermute | solution.py:34
  54.7 2.4 %collective-permute-start.22 = (bf16[128,256]{1,0:T(8,128)(2,1)S(1)}, bf16[128,256]{1,0:T(8,128)(2,1)S(1)}, u32[]{:S(2)}, u32[]{:S(2)}) collective-permute-start(bf16[128,256]{1,0:T(8,128)(2,1)S(1)} %get-tuple-element.87), channel_id=1, source_target_pairs={{0,3},{1,2},{2,1},{3,0},{4,7},{5,6},{6,5},{7,4},{8,11},{9,10},{10,... | collective-permute-start | bytes 196616 | tf_op jit(solution)/shard_map/ppermute | solution.py:26
  59.2 2.1 %collective-permute-done.22.refs_14_ = bf16[128,256]{1,0:T(8,128)(2,1)S(1)} collective-permute-done((bf16[128,256]{1,0:T(8,128)(2,1)S(1)}, bf16[128,256]{1,0:T(8,128)(2,1)S(1)}, u32[]{:S(2)}, u32[]{:S(2)}) %collective-permute-start.22) | collective-permute-done | bytes 65568 | tf_op jit(solution)/shard_map/ppermute | solution.py:26
  64.7 2.0 %collective-permute-start.26 = (bf16[256,256]{1,0:T(8,128)(2,1)S(1)}, bf16[256,256]{1,0:T(8,128)(2,1)S(1)}, u32[]{:S(2)}, u32[]{:S(2)}) collective-permute-start(bf16[256,256]{1,0:T(8,128)(2,1)S(1)} %get-tuple-element.95), channel_id=1, source_target_pairs={{0,3},{1,2},{2,1},{3,0},{4,7},{5,6},{6,5},{7,4},{8,11},{9,10},{10,... | collective-permute-start | bytes 393224 | tf_op jit(solution)/shard_map/ppermute | solution.py:26
  66.7 3.1 %collective-permute-done.23.refs_0_.refs_3_ = bf16[256,256]{1,0:T(8,128)(2,1)S(1)} collective-permute-done((bf16[256,256]{1,0:T(8,128)(2,1)S(1)}, bf16[256,256]{1,0:T(8,128)(2,1)S(1)}, u32[]{:S(2)}, u32[]{:S(2)}) %collective-permute-start.23) | collective-permute-done | bytes 131104 | tf_op jit(solution)/shard_map/ppermute | solution.py:26
  69.9 1.6 %collective-permute-start.27 = (bf16[128,256]{1,0:T(8,128)(2,1)S(1)}, bf16[128,256]{1,0:T(8,128)(2,1)S(1)}, u32[]{:S(2)}, u32[]{:S(2)}) collective-permute-start(bf16[128,256]{1,0:T(8,128)(2,1)S(1)} %get-tuple-element.96), channel_id=1, source_target_pairs={{0,1},{1,0},{2,3},{3,2},{4,5},{5,4},{6,7},{7,6},{8,9},{9,8},{10,11... | collective-permute-start | bytes 196616 | tf_op jit(solution)/shard_map/ppermute | solution.py:26
  71.4 2.0 %collective-permute-start.29 = (bf16[128,256]{1,0:T(8,128)(2,1)S(1)}, bf16[128,256]{1,0:T(8,128)(2,1)S(1)}, u32[]{:S(2)}, u32[]{:S(2)}) collective-permute-start(bf16[128,256]{1,0:T(8,128)(2,1)S(1)} %get-tuple-element.98), channel_id=1, source_target_pairs={{0,3},{1,2},{2,1},{3,0},{4,7},{5,6},{6,5},{7,4},{8,11},{9,10},{10,... | collective-permute-start | bytes 196616 | tf_op jit(solution)/shard_map/ppermute | solution.py:26
  74.0 2.0 %collective-permute-start.30 = (bf16[2,64,256]{2,1,0:T(8,128)(2,1)S(1)}, bf16[2,64,256]{2,1,0:T(8,128)(2,1)S(1)}, u32[]{:S(2)}, u32[]{:S(2)}) collective-permute-start(bf16[2,64,256]{2,1,0:T(8,128)(2,1)S(1)} %half_sum.1.mine_ref), channel_id=1, source_target_pairs={{0,4},{1,5},{2,6},{3,7},{4,0},{5,1},{6,2},{7,3},{8,12},{9,13},{10,... | collective-permute-start | bytes 196616 | tf_op jit(solution)/shard_map/ppermute | solution.py:26
  76.8 3.1 %collective-permute-done.30.far_ref = bf16[2,64,256]{2,1,0:T(8,128)(2,1)S(1)} collective-permute-done((bf16[2,64,256]{2,1,0:T(8,128)(2,1)S(1)}, bf16[2,64,256]{2,1,0:T(8,128)(2,1)S(1)}, u32[]{:S(2)}, u32[]{:S(2)}) %collective-permute-start.30) | collective-permute-done | bytes 65568 | tf_op jit(solution)/shard_map/ppermute | solution.py:26
  80.9 2.6 %collective-permute-start.33 = (bf16[2,64,256]{2,1,0:T(8,128)(2,1)S(1)}, bf16[2,64,256]{2,1,0:T(8,128)(2,1)S(1)}, u32[]{:S(2)}, u32[]{:S(2)}) collective-permute-start(bf16[2,64,256]{2,1,0:T(8,128)(2,1)S(1)} %total.1.refs_0_), channel_id=1, source_target_pairs={{0,3},{1,2},{2,1},{3,0},{4,7},{5,6},{6,5},{7,4},{8,11},{9,10},{10,... | collective-permute-start | bytes 196616 | tf_op jit(solution)/shard_map/ppermute | solution.py:26
  (78 shorter events, 30.2 us)
Async XLA Ops:
  2.2 12.7 %collective-permute-start.3 = (bf16[256,256]{1,0:T(8,128)(2,1)S(1)}, bf16[256,256]{1,0:T(8,128)(2,1)S(1)}, u32[]{:S(2)}, u32[]{:S(2)}) collective-permute-start(bf16[256,256]{1,0:T(8,128)(2,1)S(1)} %fusion.3.refs_1_.refs_7_), channel_id=1, source_target_pairs={{0,4},{1,5},{2,6},{3,7},{4,0},{5,1},{6,2},{7,3},{8,12},{9,13},{10,... | collective-permute-start | bytes 393224 | tf_op jit(solution)/shard_map/ppermute | solution.py:26
  7.2 6.8 %collective-permute-start = (f32[4,256]{1,0:T(4,128)S(1)}, f32[4,256]{1,0:T(4,128)S(1)}, u32[]{:S(2)}, u32[]{:S(2)}) collective-permute-start(f32[4,256]{1,0:T(4,128)S(1)} %get-tuple-element.54), channel_id=1, source_target_pairs={{0,1},{1,0},{2,3},{3,2},{4,5},{5,4},{6,7},{7,6},{8,9},{9,8},{10,11... | collective-permute-start | bytes 12296 | tf_op jit(solution)/shard_map/ppermute | solution.py:26
  14.9 6.2 %collective-permute-start.4 = (bf16[256,256]{1,0:T(8,128)(2,1)S(1)}, bf16[256,256]{1,0:T(8,128)(2,1)S(1)}, u32[]{:S(2)}, u32[]{:S(2)}) collective-permute-start(bf16[256,256]{1,0:T(8,128)(2,1)S(1)} %get-tuple-element.59), channel_id=1, source_target_pairs={{0,1},{1,0},{2,3},{3,2},{4,5},{5,4},{6,7},{7,6},{8,9},{9,8},{10,11... | collective-permute-start | bytes 393224 | tf_op jit(solution)/shard_map/ppermute | solution.py:26
  16.7 6.1 %collective-permute-start.6 = (bf16[256,256]{1,0:T(8,128)(2,1)S(1)}, bf16[256,256]{1,0:T(8,128)(2,1)S(1)}, u32[]{:S(2)}, u32[]{:S(2)}) collective-permute-start(bf16[256,256]{1,0:T(8,128)(2,1)S(1)} %get-tuple-element.61), channel_id=1, source_target_pairs={{0,3},{1,2},{2,1},{3,0},{4,7},{5,6},{6,5},{7,4},{8,11},{9,10},{10,... | collective-permute-start | bytes 393224 | tf_op jit(solution)/shard_map/ppermute | solution.py:26
  24.0 7.3 %collective-permute-start.7 = (bf16[256,256]{1,0:T(8,128)(2,1)S(1)}, bf16[256,256]{1,0:T(8,128)(2,1)S(1)}, u32[]{:S(2)}, u32[]{:S(2)}) collective-permute-start(bf16[256,256]{1,0:T(8,128)(2,1)S(1)} %get-tuple-element.62.refs_2_), channel_id=1, source_target_pairs={{0,4},{1,5},{2,6},{3,7},{4,0},{5,1},{6,2},{7,3},{8,12},{9,13},{10,... | collective-permute-start | bytes 393224 | tf_op jit(solution)/shard_map/ppermute | solution.py:26
  25.7 7.8 %collective-permute-start.11 = (bf16[128,256]{1,0:T(8,128)(2,1)S(1)}, bf16[128,256]{1,0:T(8,128)(2,1)S(1)}, u32[]{:S(2)}, u32[]{:S(2)}) collective-permute-start(bf16[128,256]{1,0:T(8,128)(2,1)S(1)} %get-tuple-element.66), channel_id=1, source_target_pairs={{0,1},{1,0},{2,3},{3,2},{4,5},{5,4},{6,7},{7,6},{8,9},{9,8},{10,11... | collective-permute-start | bytes 196616 | tf_op jit(solution)/shard_map/ppermute | solution.py:26
  27.2 6.9 %collective-permute-start.12 = (bf16[128,256]{1,0:T(8,128)(2,1)S(1)}, bf16[128,256]{1,0:T(8,128)(2,1)S(1)}, u32[]{:S(2)}, u32[]{:S(2)}) collective-permute-start(bf16[128,256]{1,0:T(8,128)(2,1)S(1)} %get-tuple-element.67), channel_id=1, source_target_pairs={{0,2},{1,3},{2,0},{3,1},{4,6},{5,7},{6,4},{7,5},{8,10},{9,11},{10,... | collective-permute-start | bytes 196616 | tf_op jit(solution)/shard_map/ppermute | solution.py:26
  29.3 11.1 %collective-permute-start.14 = (bf16[528,256]{1,0:T(8,128)(2,1)S(1)}, bf16[528,256]{1,0:T(8,128)(2,1)S(1)}, u32[]{:S(2)}, u32[]{:S(2)}) collective-permute-start(bf16[528,256]{1,0:T(8,128)(2,1)S(1)} %pack.1), channel_id=1, source_target_pairs={{0,8},{8,16},{16,24},{24,0},{1,9},{9,17},{17,25},{25,1},{2,10},{10... | collective-permute-start | bytes 811016 | tf_op jit(solution)/shard_map/ppermute | solution.py:39
  29.3 8.3 %collective-permute-start.13 = (bf16[128,256]{1,0:T(8,128)(2,1)}, bf16[128,256]{1,0:T(8,128)(2,1)}, u32[]{:S(2)}, u32[]{:S(2)}) collective-permute-start(bf16[128,256]{1,0:T(8,128)(2,1)} %get-tuple-element.68), channel_id=1, source_target_pairs={{0,3},{1,2},{2,1},{3,0},{4,7},{5,6},{6,5},{7,4},{8,11},{9,10},{10,... | collective-permute-start | bytes 196616 | tf_op jit(solution)/shard_map/ppermute | solution.py:26
  32.0 8.3 %collective-permute-start.8 = (bf16[128,256]{1,0:T(8,128)(2,1)}, bf16[128,256]{1,0:T(8,128)(2,1)}, u32[]{:S(2)}, u32[]{:S(2)}) collective-permute-start(bf16[128,256]{1,0:T(8,128)(2,1)} %get-tuple-element.63), channel_id=1, source_target_pairs={{0,1},{1,0},{2,3},{3,2},{4,5},{5,4},{6,7},{7,6},{8,9},{9,8},{10,11... | collective-permute-start | bytes 196616 | tf_op jit(solution)/shard_map/ppermute | solution.py:26
  33.5 6.8 %collective-permute-start.9 = (bf16[128,256]{1,0:T(8,128)(2,1)}, bf16[128,256]{1,0:T(8,128)(2,1)}, u32[]{:S(2)}, u32[]{:S(2)}) collective-permute-start(bf16[128,256]{1,0:T(8,128)(2,1)} %get-tuple-element.64), channel_id=1, source_target_pairs={{0,2},{1,3},{2,0},{3,1},{4,6},{5,7},{6,4},{7,5},{8,10},{9,11},{10,... | collective-permute-start | bytes 196616 | tf_op jit(solution)/shard_map/ppermute | solution.py:26
  34.1 6.2 %collective-permute-start.10 = (bf16[128,256]{1,0:T(8,128)(2,1)}, bf16[128,256]{1,0:T(8,128)(2,1)}, u32[]{:S(2)}, u32[]{:S(2)}) collective-permute-start(bf16[128,256]{1,0:T(8,128)(2,1)} %get-tuple-element.65), channel_id=1, source_target_pairs={{0,3},{1,2},{2,1},{3,0},{4,7},{5,6},{6,5},{7,4},{8,11},{9,10},{10,... | collective-permute-start | bytes 196616 | tf_op jit(solution)/shard_map/ppermute | solution.py:26
  41.8 11.7 %collective-permute-start.17 = (bf16[256,256]{1,0:T(8,128)(2,1)S(1)}, bf16[256,256]{1,0:T(8,128)(2,1)S(1)}, u32[]{:S(2)}, u32[]{:S(2)}) collective-permute-start(bf16[256,256]{1,0:T(8,128)(2,1)S(1)} %get-tuple-element.78), channel_id=1, source_target_pairs={{0,28},{1,29},{2,30},{3,31},{4,24},{5,25},{6,26},{7,27},{8,4},{9,5... | collective-permute-start | bytes 393224 | tf_op jit(solution)/shard_map/ppermute | solution.py:34
  46.5 7.0 %collective-permute-start.19 = (bf16[128,256]{1,0:T(8,128)(2,1)S(1)}, bf16[128,256]{1,0:T(8,128)(2,1)S(1)}, u32[]{:S(2)}, u32[]{:S(2)}) collective-permute-start(bf16[128,256]{1,0:T(8,128)(2,1)S(1)} %get-tuple-element.80), channel_id=1, source_target_pairs={{0,27},{1,26},{2,25},{3,24},{4,31},{5,30},{6,29},{7,28},{8,3},{9,2... | collective-permute-start | bytes 196616 | tf_op jit(solution)/shard_map/ppermute | solution.py:34
  48.3 9.1 %collective-permute-start.15 = (bf16[256,256]{1,0:T(8,128)(2,1)S(1)}, bf16[256,256]{1,0:T(8,128)(2,1)S(1)}, u32[]{:S(2)}, u32[]{:S(2)}) collective-permute-start(bf16[256,256]{1,0:T(8,128)(2,1)S(1)} %get-tuple-element.74.refs_10_), channel_id=1, source_target_pairs={{0,24},{1,25},{2,26},{3,27},{4,28},{5,29},{6,30},{7,31},{8,0},{9,1... | collective-permute-start | bytes 393224 | tf_op jit(solution)/shard_map/ppermute | solution.py:34
  48.6 8.7 %collective-permute-start.16 = (bf16[128,256]{1,0:T(8,128)(2,1)S(1)}, bf16[128,256]{1,0:T(8,128)(2,1)S(1)}, u32[]{:S(2)}, u32[]{:S(2)}) collective-permute-start(bf16[128,256]{1,0:T(8,128)(2,1)S(1)} %get-tuple-element.75), channel_id=1, source_target_pairs={{0,25},{1,24},{2,27},{3,26},{4,29},{5,28},{6,31},{7,30},{8,1},{9,0... | collective-permute-start | bytes 196616 | tf_op jit(solution)/shard_map/ppermute | solution.py:34
  54.7 6.6 %collective-permute-start.22 = (bf16[128,256]{1,0:T(8,128)(2,1)S(1)}, bf16[128,256]{1,0:T(8,128)(2,1)S(1)}, u32[]{:S(2)}, u32[]{:S(2)}) collective-permute-start(bf16[128,256]{1,0:T(8,128)(2,1)S(1)} %get-tuple-element.87), channel_id=1, source_target_pairs={{0,3},{1,2},{2,1},{3,0},{4,7},{5,6},{6,5},{7,4},{8,11},{9,10},{10,... | collective-permute-start | bytes 196616 | tf_op jit(solution)/shard_map/ppermute | solution.py:26
  62.0 7.9 %collective-permute-start.23 = (bf16[256,256]{1,0:T(8,128)(2,1)S(1)}, bf16[256,256]{1,0:T(8,128)(2,1)S(1)}, u32[]{:S(2)}, u32[]{:S(2)}) collective-permute-start(bf16[256,256]{1,0:T(8,128)(2,1)S(1)} %get-tuple-element.92.refs_2_), channel_id=1, source_target_pairs={{0,4},{1,5},{2,6},{3,7},{4,0},{5,1},{6,2},{7,3},{8,12},{9,13},{10,... | collective-permute-start | bytes 393224 | tf_op jit(solution)/shard_map/ppermute | solution.py:26
  63.2 8.2 %collective-permute-start.24 = (bf16[256,256]{1,0:T(8,128)(2,1)S(1)}, bf16[256,256]{1,0:T(8,128)(2,1)S(1)}, u32[]{:S(2)}, u32[]{:S(2)}) collective-permute-start(bf16[256,256]{1,0:T(8,128)(2,1)S(1)} %get-tuple-element.93), channel_id=1, source_target_pairs={{0,1},{1,0},{2,3},{3,2},{4,5},{5,4},{6,7},{7,6},{8,9},{9,8},{10,11... | collective-permute-start | bytes 393224 | tf_op jit(solution)/shard_map/ppermute | solution.py:26
  63.5 9.9 %collective-permute-start.25 = (bf16[256,256]{1,0:T(8,128)(2,1)S(1)}, bf16[256,256]{1,0:T(8,128)(2,1)S(1)}, u32[]{:S(2)}, u32[]{:S(2)}) collective-permute-start(bf16[256,256]{1,0:T(8,128)(2,1)S(1)} %get-tuple-element.94), channel_id=1, source_target_pairs={{0,2},{1,3},{2,0},{3,1},{4,6},{5,7},{6,4},{7,5},{8,10},{9,11},{10,... | collective-permute-start | bytes 393224 | tf_op jit(solution)/shard_map/ppermute | solution.py:26
  64.7 9.3 %collective-permute-start.26 = (bf16[256,256]{1,0:T(8,128)(2,1)S(1)}, bf16[256,256]{1,0:T(8,128)(2,1)S(1)}, u32[]{:S(2)}, u32[]{:S(2)}) collective-permute-start(bf16[256,256]{1,0:T(8,128)(2,1)S(1)} %get-tuple-element.95), channel_id=1, source_target_pairs={{0,3},{1,2},{2,1},{3,0},{4,7},{5,6},{6,5},{7,4},{8,11},{9,10},{10,... | collective-permute-start | bytes 393224 | tf_op jit(solution)/shard_map/ppermute | solution.py:26
  69.9 11.1 %collective-permute-start.27 = (bf16[128,256]{1,0:T(8,128)(2,1)S(1)}, bf16[128,256]{1,0:T(8,128)(2,1)S(1)}, u32[]{:S(2)}, u32[]{:S(2)}) collective-permute-start(bf16[128,256]{1,0:T(8,128)(2,1)S(1)} %get-tuple-element.96), channel_id=1, source_target_pairs={{0,1},{1,0},{2,3},{3,2},{4,5},{5,4},{6,7},{7,6},{8,9},{9,8},{10,11... | collective-permute-start | bytes 196616 | tf_op jit(solution)/shard_map/ppermute | solution.py:26
  71.4 12.1 %collective-permute-start.28 = (bf16[128,256]{1,0:T(8,128)(2,1)S(1)}, bf16[128,256]{1,0:T(8,128)(2,1)S(1)}, u32[]{:S(2)}, u32[]{:S(2)}) collective-permute-start(bf16[128,256]{1,0:T(8,128)(2,1)S(1)} %get-tuple-element.97), channel_id=1, source_target_pairs={{0,2},{1,3},{2,0},{3,1},{4,6},{5,7},{6,4},{7,5},{8,10},{9,11},{10,... | collective-permute-start | bytes 196616 | tf_op jit(solution)/shard_map/ppermute | solution.py:26
  71.4 12.1 %collective-permute-start.29 = (bf16[128,256]{1,0:T(8,128)(2,1)S(1)}, bf16[128,256]{1,0:T(8,128)(2,1)S(1)}, u32[]{:S(2)}, u32[]{:S(2)}) collective-permute-start(bf16[128,256]{1,0:T(8,128)(2,1)S(1)} %get-tuple-element.98), channel_id=1, source_target_pairs={{0,3},{1,2},{2,1},{3,0},{4,7},{5,6},{6,5},{7,4},{8,11},{9,10},{10,... | collective-permute-start | bytes 196616 | tf_op jit(solution)/shard_map/ppermute | solution.py:26
  (15 other events, 185.1 us)

commit v23 on v18

--- a/solution.py
+++ b/solution.py
@@ -542,7 +542,7 @@
     call.want(VMEM, (layers, chunk, width), BF16)
     (total,) = call.run(total_kernel, "total", small_cost)
     call = Call()
-    call.give(VMEM, total, *shared([total] * (h - 1)))
+    call.give(VMEM, total, *(swapped(total, k) for k in range(1, h)))
     call.want(HBM, (1, layers, width, width), F32)
     call.scratch = [pltpu.VMEM((layers, width, width), F32), pltpu.SemaphoreType.DMA((layers,))]
     (weight_grad,) = call.run(functools.partial(finish_kernel, h), "finish", small_cost)

time: 83.4 us -> 83.2 us (level)
  transfers between devices with their start and end apart: 34 -> 34, of which waited for: 14 -> 15; matrix products, arithmetic and copies ran while one was open for 5% -> 5% of each run, Pallas kernels for 9% -> 10%
where the time goes in v23:
time: 83.2 us; the launch traced here: 83 us
  starting transfers between devices  43.4 us (52%)
  waiting for transfers between devices  22.8 us (27%)
  Pallas kernels  10.3 us (12%)
  matrix products  2.6 us (3%)
  other arithmetic  1.67 us (2%)
  local copies, waits for them, and re-layouts  1.1 us (1%)
  between operations  1.07 us (1%)
    ppermute x28, starting transfers between devices, swapped(): return lax.ppermute(block, 'rows', [(i, i ^ k) for i in range(n)])  36 us
    ppermute x28, waiting for transfers between devices, swapped(): return lax.ppermute(block, 'rows', [(i, i ^ k) for i in range(n)])  21.4 us
    pallas_call x16, Pallas kernels, run(): pl.pallas_call(kernel, out_shape=self.outs, in_specs=self.specs, out_spec...  10.3 us
    ppermute x5, starting transfers between devices, lowered(): return lax.ppermute(block, ('section', 'rows'), route)  7.38 us
  transfers between devices with their start and end apart: 34, of which 15 were waited for; matrix products, arithmetic and copies ran while one was open for 5% of the time, Pallas kernels for 10%

profile of v23, /device:TPU:0, one launch (start us, length us, event | category | flops | bytes accessed | tf_op | source)
XLA Modules:
  0.0 83.0 jit_solution(8903328794247925523)
XLA Ops:
  2.2 4.1 %collective-permute-start.3 = (bf16[256,256]{1,0:T(8,128)(2,1)S(1)}, bf16[256,256]{1,0:T(8,128)(2,1)S(1)}, u32[]{:S(2)}, u32[]{:S(2)}) collective-permute-start(bf16[256,256]{1,0:T(8,128)(2,1)S(1)} %fusion.3.refs_1_.refs_7_), channel_id=1, source_target_pairs={{0,4},{1,5},{2,6},{3,7},{4,0},{5,1},{6,2},{7,3},{8,12},{9,13},{10,... | collective-permute-start | bytes 393224 | tf_op jit(solution)/shard_map/ppermute | solution.py:26
  7.2 1.6 %collective-permute-start = (f32[4,256]{1,0:T(4,128)S(1)}, f32[4,256]{1,0:T(4,128)S(1)}, u32[]{:S(2)}, u32[]{:S(2)}) collective-permute-start(f32[4,256]{1,0:T(4,128)S(1)} %get-tuple-element.54), channel_id=1, source_target_pairs={{0,1},{1,0},{2,3},{3,2},{4,5},{5,4},{6,7},{7,6},{8,9},{9,8},{10,11... | collective-permute-start | bytes 12296 | tf_op jit(solution)/shard_map/ppermute | solution.py:26
  8.7 1.6 %collective-permute-start.1 = (f32[4,256]{1,0:T(4,128)S(1)}, f32[4,256]{1,0:T(4,128)S(1)}, u32[]{:S(2)}, u32[]{:S(2)}) collective-permute-start(f32[4,256]{1,0:T(4,128)S(1)} %get-tuple-element.55), channel_id=1, source_target_pairs={{0,2},{1,3},{2,0},{3,1},{4,6},{5,7},{6,4},{7,5},{8,10},{9,11},{10,... | collective-permute-start | bytes 12296 | tf_op jit(solution)/shard_map/ppermute | solution.py:26
  10.7 3.1 %densify.2.refs_6_.refs_1_ = bf16[256,1152]{1,0:T(8,128)(2,1)S(1)} custom-call(s32[2,96]{1,0:T(2,128)S(1)} %fusion.15.words_ref, bf16[1,2,96,128,128]{4,3,2,1,0:T(8,128)(2,1)} %vals_ref.3), custom_call_target="tpu_custom_call" | custom-call | flops 31457280 | bytes 3145728 | tf_op jit(solution)/shard_map/densify/pallas_call | solution.py:71
  15.6 1.6 %collective-permute-start.5 = (bf16[256,256]{1,0:T(8,128)(2,1)S(1)}, bf16[256,256]{1,0:T(8,128)(2,1)S(1)}, u32[]{:S(2)}, u32[]{:S(2)}) collective-permute-start(bf16[256,256]{1,0:T(8,128)(2,1)S(1)} %get-tuple-element.60), channel_id=1, source_target_pairs={{0,2},{1,3},{2,0},{3,1},{4,6},{5,7},{6,4},{7,5},{8,10},{9,11},{10,... | collective-permute-start | bytes 393224 | tf_op jit(solution)/shard_map/ppermute | solution.py:26
  18.8 2.5 %collective-permute-done.4.refs_9_ = bf16[256,256]{1,0:T(8,128)(2,1)S(1)} collective-permute-done((bf16[256,256]{1,0:T(8,128)(2,1)S(1)}, bf16[256,256]{1,0:T(8,128)(2,1)S(1)}, u32[]{:S(2)}, u32[]{:S(2)}) %collective-permute-start.4) | collective-permute-done | bytes 131104 | tf_op jit(solution)/shard_map/ppermute | solution.py:26
  21.3 1.8 %collective-permute-done.6.refs_11_ = bf16[256,256]{1,0:T(8,128)(2,1)S(1)} collective-permute-done((bf16[256,256]{1,0:T(8,128)(2,1)S(1)}, bf16[256,256]{1,0:T(8,128)(2,1)S(1)}, u32[]{:S(2)}, u32[]{:S(2)}) %collective-permute-start.6) | collective-permute-done | bytes 131104 | tf_op jit(solution)/shard_map/ppermute | solution.py:26
  23.6 1.5 %collective-permute-start.7 = (bf16[256,256]{1,0:T(8,128)(2,1)S(1)}, bf16[256,256]{1,0:T(8,128)(2,1)S(1)}, u32[]{:S(2)}, u32[]{:S(2)}) collective-permute-start(bf16[256,256]{1,0:T(8,128)(2,1)S(1)} %get-tuple-element.62.refs_2_), channel_id=1, source_target_pairs={{0,4},{1,5},{2,6},{3,7},{4,0},{5,1},{6,2},{7,3},{8,12},{9,13},{10,... | collective-permute-start | bytes 393224 | tf_op jit(solution)/shard_map/ppermute | solution.py:26
  25.1 1.5 %collective-permute-start.11 = (bf16[128,256]{1,0:T(8,128)(2,1)S(1)}, bf16[128,256]{1,0:T(8,128)(2,1)S(1)}, u32[]{:S(2)}, u32[]{:S(2)}) collective-permute-start(bf16[128,256]{1,0:T(8,128)(2,1)S(1)} %get-tuple-element.66), channel_id=1, source_target_pairs={{0,1},{1,0},{2,3},{3,2},{4,5},{5,4},{6,7},{7,6},{8,9},{9,8},{10,11... | collective-permute-start | bytes 196616 | tf_op jit(solution)/shard_map/ppermute | solution.py:26
  26.6 1.7 %collective-permute-start.12 = (bf16[128,256]{1,0:T(8,128)(2,1)S(1)}, bf16[128,256]{1,0:T(8,128)(2,1)S(1)}, u32[]{:S(2)}, u32[]{:S(2)}) collective-permute-start(bf16[128,256]{1,0:T(8,128)(2,1)S(1)} %get-tuple-element.67), channel_id=1, source_target_pairs={{0,2},{1,3},{2,0},{3,1},{4,6},{5,7},{6,4},{7,5},{8,10},{9,11},{10,... | collective-permute-start | bytes 196616 | tf_op jit(solution)/shard_map/ppermute | solution.py:26
  28.6 2.4 %collective-permute-done.7.refs_0_.refs_3_ = bf16[256,256]{1,0:T(8,128)(2,1)S(1)} collective-permute-done((bf16[256,256]{1,0:T(8,128)(2,1)S(1)}, bf16[256,256]{1,0:T(8,128)(2,1)S(1)}, u32[]{:S(2)}, u32[]{:S(2)}) %collective-permute-start.7) | collective-permute-done | bytes 131104 | tf_op jit(solution)/shard_map/ppermute | solution.py:26
  32.9 1.7 %collective-permute-start.10 = (bf16[128,256]{1,0:T(8,128)(2,1)S(1)}, bf16[128,256]{1,0:T(8,128)(2,1)S(1)}, u32[]{:S(2)}, u32[]{:S(2)}) collective-permute-start(bf16[128,256]{1,0:T(8,128)(2,1)S(1)} %get-tuple-element.65), channel_id=1, source_target_pairs={{0,3},{1,2},{2,1},{3,0},{4,7},{5,6},{6,5},{7,4},{8,11},{9,10},{10,... | collective-permute-start | bytes 196616 | tf_op jit(solution)/shard_map/ppermute | solution.py:26
  34.6 2.8 %densify.3.refs_6_.refs_1_ = bf16[256,1152]{1,0:T(8,128)(2,1)S(1)} custom-call(s32[2,96]{1,0:T(2,128)S(1)} %fusion.15.words_ref, bf16[1,2,96,128,128]{4,3,2,1,0:T(8,128)(2,1)} %vals_ref.3), custom_call_target="tpu_custom_call" | custom-call | flops 31457280 | bytes 3145728 | tf_op jit(solution)/shard_map/densify/pallas_call | solution.py:71
  38.6 1.7 %collective-permute-start.17 = (bf16[256,256]{1,0:T(8,128)(2,1)S(1)}, bf16[256,256]{1,0:T(8,128)(2,1)S(1)}, u32[]{:S(2)}, u32[]{:S(2)}) collective-permute-start(bf16[256,256]{1,0:T(8,128)(2,1)S(1)} %get-tuple-element.78), channel_id=1, source_target_pairs={{0,28},{1,29},{2,30},{3,31},{4,24},{5,25},{6,26},{7,27},{8,4},{9,5... | collective-permute-start | bytes 393224 | tf_op jit(solution)/shard_map/ppermute | solution.py:34
  40.3 2.5 %collective-permute-start.18 = (bf16[128,256]{1,0:T(8,128)(2,1)S(1)}, bf16[128,256]{1,0:T(8,128)(2,1)S(1)}, u32[]{:S(2)}, u32[]{:S(2)}) collective-permute-start(bf16[128,256]{1,0:T(8,128)(2,1)S(1)} %get-tuple-element.79), channel_id=1, source_target_pairs={{0,26},{1,27},{2,24},{3,25},{4,30},{5,31},{6,28},{7,29},{8,2},{9,3... | collective-permute-start | bytes 196616 | tf_op jit(solution)/shard_map/ppermute | solution.py:34
  49.6 1.7 %collective-permute-start.20 = (bf16[128,256]{1,0:T(8,128)(2,1)S(1)}, bf16[128,256]{1,0:T(8,128)(2,1)S(1)}, u32[]{:S(2)}, u32[]{:S(2)}) collective-permute-start(bf16[128,256]{1,0:T(8,128)(2,1)S(1)} %get-tuple-element.85), channel_id=1, source_target_pairs={{0,1},{1,0},{2,3},{3,2},{4,5},{5,4},{6,7},{7,6},{8,9},{9,8},{10,11... | collective-permute-start | bytes 196616 | tf_op jit(solution)/shard_map/ppermute | solution.py:26
  51.2 1.9 %collective-permute-start.22 = (bf16[128,256]{1,0:T(8,128)(2,1)S(1)}, bf16[128,256]{1,0:T(8,128)(2,1)S(1)}, u32[]{:S(2)}, u32[]{:S(2)}) collective-permute-start(bf16[128,256]{1,0:T(8,128)(2,1)S(1)} %get-tuple-element.87), channel_id=1, source_target_pairs={{0,3},{1,2},{2,1},{3,0},{4,7},{5,6},{6,5},{7,4},{8,11},{9,10},{10,... | collective-permute-start | bytes 196616 | tf_op jit(solution)/shard_map/ppermute | solution.py:26
  54.2 1.9 %collective-permute-done.21.refs_13_ = bf16[128,256]{1,0:T(8,128)(2,1)S(1)} collective-permute-done((bf16[128,256]{1,0:T(8,128)(2,1)S(1)}, bf16[128,256]{1,0:T(8,128)(2,1)S(1)}, u32[]{:S(2)}, u32[]{:S(2)}) %collective-permute-start.21) | collective-permute-done | bytes 65568 | tf_op jit(solution)/shard_map/ppermute | solution.py:26
  60.4 1.5 %collective-permute-start.26 = (bf16[256,256]{1,0:T(8,128)(2,1)S(1)}, bf16[256,256]{1,0:T(8,128)(2,1)S(1)}, u32[]{:S(2)}, u32[]{:S(2)}) collective-permute-start(bf16[256,256]{1,0:T(8,128)(2,1)S(1)} %get-tuple-element.95), channel_id=1, source_target_pairs={{0,3},{1,2},{2,1},{3,0},{4,7},{5,6},{6,5},{7,4},{8,11},{9,10},{10,... | collective-permute-start | bytes 393224 | tf_op jit(solution)/shard_map/ppermute | solution.py:26
  61.9 4.6 %collective-permute-done.23.refs_0_.refs_3_ = bf16[256,256]{1,0:T(8,128)(2,1)S(1)} collective-permute-done((bf16[256,256]{1,0:T(8,128)(2,1)S(1)}, bf16[256,256]{1,0:T(8,128)(2,1)S(1)}, u32[]{:S(2)}, u32[]{:S(2)}) %collective-permute-start.23) | collective-permute-done | bytes 131104 | tf_op jit(solution)/shard_map/ppermute | solution.py:26
  68.0 1.7 %collective-permute-done.26.refs_6_.refs_4_ = bf16[256,256]{1,0:T(8,128)(2,1)S(1)} collective-permute-done((bf16[256,256]{1,0:T(8,128)(2,1)S(1)}, bf16[256,256]{1,0:T(8,128)(2,1)S(1)}, u32[]{:S(2)}, u32[]{:S(2)}) %collective-permute-start.26) | collective-permute-done | bytes 131104 | tf_op jit(solution)/shard_map/ppermute | solution.py:26
  70.7 1.8 %collective-permute-start.28 = (bf16[128,256]{1,0:T(8,128)(2,1)S(1)}, bf16[128,256]{1,0:T(8,128)(2,1)S(1)}, u32[]{:S(2)}, u32[]{:S(2)}) collective-permute-start(bf16[128,256]{1,0:T(8,128)(2,1)S(1)} %get-tuple-element.97), channel_id=1, source_target_pairs={{0,2},{1,3},{2,0},{3,1},{4,6},{5,7},{6,4},{7,5},{8,10},{9,11},{10,... | collective-permute-start | bytes 196616 | tf_op jit(solution)/shard_map/ppermute | solution.py:26
  75.3 1.6 %collective-permute-start.31 = (bf16[2,64,256]{2,1,0:T(8,128)(2,1)S(1)}, bf16[2,64,256]{2,1,0:T(8,128)(2,1)S(1)}, u32[]{:S(2)}, u32[]{:S(2)}) collective-permute-start(bf16[2,64,256]{2,1,0:T(8,128)(2,1)S(1)} %total.1.refs_0_), channel_id=1, source_target_pairs={{0,1},{1,0},{2,3},{3,2},{4,5},{5,4},{6,7},{7,6},{8,9},{9,8},{10,11... | collective-permute-start | bytes 196616 | tf_op jit(solution)/shard_map/ppermute | solution.py:26
  77.0 1.8 %collective-permute-start.33 = (bf16[2,64,256]{2,1,0:T(8,128)(2,1)S(1)}, bf16[2,64,256]{2,1,0:T(8,128)(2,1)S(1)}, u32[]{:S(2)}, u32[]{:S(2)}) collective-permute-start(bf16[2,64,256]{2,1,0:T(8,128)(2,1)S(1)} %total.1.refs_0_), channel_id=1, source_target_pairs={{0,3},{1,2},{2,1},{3,0},{4,7},{5,6},{6,5},{7,4},{8,11},{9,10},{10,... | collective-permute-start | bytes 196616 | tf_op jit(solution)/shard_map/ppermute | solution.py:26
  (78 shorter events, 31.6 us)
Async XLA Ops:
  2.2 12.6 %collective-permute-start.3 = (bf16[256,256]{1,0:T(8,128)(2,1)S(1)}, bf16[256,256]{1,0:T(8,128)(2,1)S(1)}, u32[]{:S(2)}, u32[]{:S(2)}) collective-permute-start(bf16[256,256]{1,0:T(8,128)(2,1)S(1)} %fusion.3.refs_1_.refs_7_), channel_id=1, source_target_pairs={{0,4},{1,5},{2,6},{3,7},{4,0},{5,1},{6,2},{7,3},{8,12},{9,13},{10,... | collective-permute-start | bytes 393224 | tf_op jit(solution)/shard_map/ppermute | solution.py:26
  7.2 6.7 %collective-permute-start = (f32[4,256]{1,0:T(4,128)S(1)}, f32[4,256]{1,0:T(4,128)S(1)}, u32[]{:S(2)}, u32[]{:S(2)}) collective-permute-start(f32[4,256]{1,0:T(4,128)S(1)} %get-tuple-element.54), channel_id=1, source_target_pairs={{0,1},{1,0},{2,3},{3,2},{4,5},{5,4},{6,7},{7,6},{8,9},{9,8},{10,11... | collective-permute-start | bytes 12296 | tf_op jit(solution)/shard_map/ppermute | solution.py:26
  14.9 6.4 %collective-permute-start.4 = (bf16[256,256]{1,0:T(8,128)(2,1)S(1)}, bf16[256,256]{1,0:T(8,128)(2,1)S(1)}, u32[]{:S(2)}, u32[]{:S(2)}) collective-permute-start(bf16[256,256]{1,0:T(8,128)(2,1)S(1)} %get-tuple-element.59), channel_id=1, source_target_pairs={{0,1},{1,0},{2,3},{3,2},{4,5},{5,4},{6,7},{7,6},{8,9},{9,8},{10,11... | collective-permute-start | bytes 393224 | tf_op jit(solution)/shard_map/ppermute | solution.py:26
  15.6 5.7 %collective-permute-start.5 = (bf16[256,256]{1,0:T(8,128)(2,1)S(1)}, bf16[256,256]{1,0:T(8,128)(2,1)S(1)}, u32[]{:S(2)}, u32[]{:S(2)}) collective-permute-start(bf16[256,256]{1,0:T(8,128)(2,1)S(1)} %get-tuple-element.60), channel_id=1, source_target_pairs={{0,2},{1,3},{2,0},{3,1},{4,6},{5,7},{6,4},{7,5},{8,10},{9,11},{10,... | collective-permute-start | bytes 393224 | tf_op jit(solution)/shard_map/ppermute | solution.py:26
  17.2 5.9 %collective-permute-start.6 = (bf16[256,256]{1,0:T(8,128)(2,1)S(1)}, bf16[256,256]{1,0:T(8,128)(2,1)S(1)}, u32[]{:S(2)}, u32[]{:S(2)}) collective-permute-start(bf16[256,256]{1,0:T(8,128)(2,1)S(1)} %get-tuple-element.61), channel_id=1, source_target_pairs={{0,3},{1,2},{2,1},{3,0},{4,7},{5,6},{6,5},{7,4},{8,11},{9,10},{10,... | collective-permute-start | bytes 393224 | tf_op jit(solution)/shard_map/ppermute | solution.py:26
  18.8 19.3 %collective-permute-start.14 = (bf16[528,256]{1,0:T(8,128)(2,1)S(1)}, bf16[528,256]{1,0:T(8,128)(2,1)S(1)}, u32[]{:S(2)}, u32[]{:S(2)}) collective-permute-start(bf16[528,256]{1,0:T(8,128)(2,1)S(1)} %pack.1), channel_id=1, source_target_pairs={{0,8},{8,16},{16,24},{24,0},{1,9},{9,17},{17,25},{25,1},{2,10},{10... | collective-permute-start | bytes 811016 | tf_op jit(solution)/shard_map/ppermute | solution.py:39
  23.6 7.4 %collective-permute-start.7 = (bf16[256,256]{1,0:T(8,128)(2,1)S(1)}, bf16[256,256]{1,0:T(8,128)(2,1)S(1)}, u32[]{:S(2)}, u32[]{:S(2)}) collective-permute-start(bf16[256,256]{1,0:T(8,128)(2,1)S(1)} %get-tuple-element.62.refs_2_), channel_id=1, source_target_pairs={{0,4},{1,5},{2,6},{3,7},{4,0},{5,1},{6,2},{7,3},{8,12},{9,13},{10,... | collective-permute-start | bytes 393224 | tf_op jit(solution)/shard_map/ppermute | solution.py:26
  25.1 7.2 %collective-permute-start.11 = (bf16[128,256]{1,0:T(8,128)(2,1)S(1)}, bf16[128,256]{1,0:T(8,128)(2,1)S(1)}, u32[]{:S(2)}, u32[]{:S(2)}) collective-permute-start(bf16[128,256]{1,0:T(8,128)(2,1)S(1)} %get-tuple-element.66), channel_id=1, source_target_pairs={{0,1},{1,0},{2,3},{3,2},{4,5},{5,4},{6,7},{7,6},{8,9},{9,8},{10,11... | collective-permute-start | bytes 196616 | tf_op jit(solution)/shard_map/ppermute | solution.py:26
  26.6 6.4 %collective-permute-start.12 = (bf16[128,256]{1,0:T(8,128)(2,1)S(1)}, bf16[128,256]{1,0:T(8,128)(2,1)S(1)}, u32[]{:S(2)}, u32[]{:S(2)}) collective-permute-start(bf16[128,256]{1,0:T(8,128)(2,1)S(1)} %get-tuple-element.67), channel_id=1, source_target_pairs={{0,2},{1,3},{2,0},{3,1},{4,6},{5,7},{6,4},{7,5},{8,10},{9,11},{10,... | collective-permute-start | bytes 196616 | tf_op jit(solution)/shard_map/ppermute | solution.py:26
  28.3 6.3 %collective-permute-start.13 = (bf16[128,256]{1,0:T(8,128)(2,1)S(1)}, bf16[128,256]{1,0:T(8,128)(2,1)S(1)}, u32[]{:S(2)}, u32[]{:S(2)}) collective-permute-start(bf16[128,256]{1,0:T(8,128)(2,1)S(1)} %get-tuple-element.68), channel_id=1, source_target_pairs={{0,3},{1,2},{2,1},{3,0},{4,7},{5,6},{6,5},{7,4},{8,11},{9,10},{10,... | collective-permute-start | bytes 196616 | tf_op jit(solution)/shard_map/ppermute | solution.py:26
  31.1 6.4 %collective-permute-start.8 = (bf16[128,256]{1,0:T(8,128)(2,1)S(1)}, bf16[128,256]{1,0:T(8,128)(2,1)S(1)}, u32[]{:S(2)}, u32[]{:S(2)}) collective-permute-start(bf16[128,256]{1,0:T(8,128)(2,1)S(1)} %get-tuple-element.63), channel_id=1, source_target_pairs={{0,1},{1,0},{2,3},{3,2},{4,5},{5,4},{6,7},{7,6},{8,9},{9,8},{10,11... | collective-permute-start | bytes 196616 | tf_op jit(solution)/shard_map/ppermute | solution.py:26
  38.6 10.9 %collective-permute-start.17 = (bf16[256,256]{1,0:T(8,128)(2,1)S(1)}, bf16[256,256]{1,0:T(8,128)(2,1)S(1)}, u32[]{:S(2)}, u32[]{:S(2)}) collective-permute-start(bf16[256,256]{1,0:T(8,128)(2,1)S(1)} %get-tuple-element.78), channel_id=1, source_target_pairs={{0,28},{1,29},{2,30},{3,31},{4,24},{5,25},{6,26},{7,27},{8,4},{9,5... | collective-permute-start | bytes 393224 | tf_op jit(solution)/shard_map/ppermute | solution.py:34
  40.3 7.8 %collective-permute-start.18 = (bf16[128,256]{1,0:T(8,128)(2,1)S(1)}, bf16[128,256]{1,0:T(8,128)(2,1)S(1)}, u32[]{:S(2)}, u32[]{:S(2)}) collective-permute-start(bf16[128,256]{1,0:T(8,128)(2,1)S(1)} %get-tuple-element.79), channel_id=1, source_target_pairs={{0,26},{1,27},{2,24},{3,25},{4,30},{5,31},{6,28},{7,29},{8,2},{9,3... | collective-permute-start | bytes 196616 | tf_op jit(solution)/shard_map/ppermute | solution.py:34
  42.8 6.7 %collective-permute-start.19 = (bf16[128,256]{1,0:T(8,128)(2,1)S(1)}, bf16[128,256]{1,0:T(8,128)(2,1)S(1)}, u32[]{:S(2)}, u32[]{:S(2)}) collective-permute-start(bf16[128,256]{1,0:T(8,128)(2,1)S(1)} %get-tuple-element.80), channel_id=1, source_target_pairs={{0,27},{1,26},{2,25},{3,24},{4,31},{5,30},{6,29},{7,28},{8,3},{9,2... | collective-permute-start | bytes 196616 | tf_op jit(solution)/shard_map/ppermute | solution.py:34
  46.0 7.4 %collective-permute-start.15 = (bf16[256,256]{1,0:T(8,128)(2,1)S(1)}, bf16[256,256]{1,0:T(8,128)(2,1)S(1)}, u32[]{:S(2)}, u32[]{:S(2)}) collective-permute-start(bf16[256,256]{1,0:T(8,128)(2,1)S(1)} %get-tuple-element.74.refs_10_), channel_id=1, source_target_pairs={{0,24},{1,25},{2,26},{3,27},{4,28},{5,29},{6,30},{7,31},{8,0},{9,1... | collective-permute-start | bytes 393224 | tf_op jit(solution)/shard_map/ppermute | solution.py:34
  47.1 6.3 %collective-permute-start.16 = (bf16[128,256]{1,0:T(8,128)(2,1)S(1)}, bf16[128,256]{1,0:T(8,128)(2,1)S(1)}, u32[]{:S(2)}, u32[]{:S(2)}) collective-permute-start(bf16[128,256]{1,0:T(8,128)(2,1)S(1)} %get-tuple-element.75), channel_id=1, source_target_pairs={{0,25},{1,24},{2,27},{3,26},{4,29},{5,28},{6,31},{7,30},{8,1},{9,0... | collective-permute-start | bytes 196616 | tf_op jit(solution)/shard_map/ppermute | solution.py:34
  51.2 5.7 %collective-permute-start.22 = (bf16[128,256]{1,0:T(8,128)(2,1)S(1)}, bf16[128,256]{1,0:T(8,128)(2,1)S(1)}, u32[]{:S(2)}, u32[]{:S(2)}) collective-permute-start(bf16[128,256]{1,0:T(8,128)(2,1)S(1)} %get-tuple-element.87), channel_id=1, source_target_pairs={{0,3},{1,2},{2,1},{3,0},{4,7},{5,6},{6,5},{7,4},{8,11},{9,10},{10,... | collective-permute-start | bytes 196616 | tf_op jit(solution)/shard_map/ppermute | solution.py:26
  57.6 8.9 %collective-permute-start.23 = (bf16[256,256]{1,0:T(8,128)(2,1)S(1)}, bf16[256,256]{1,0:T(8,128)(2,1)S(1)}, u32[]{:S(2)}, u32[]{:S(2)}) collective-permute-start(bf16[256,256]{1,0:T(8,128)(2,1)S(1)} %get-tuple-element.92.refs_2_), channel_id=1, source_target_pairs={{0,4},{1,5},{2,6},{3,7},{4,0},{5,1},{6,2},{7,3},{8,12},{9,13},{10,... | collective-permute-start | bytes 393224 | tf_op jit(solution)/shard_map/ppermute | solution.py:26
  58.4 9.0 %collective-permute-start.24 = (bf16[256,256]{1,0:T(8,128)(2,1)S(1)}, bf16[256,256]{1,0:T(8,128)(2,1)S(1)}, u32[]{:S(2)}, u32[]{:S(2)}) collective-permute-start(bf16[256,256]{1,0:T(8,128)(2,1)S(1)} %get-tuple-element.93), channel_id=1, source_target_pairs={{0,1},{1,0},{2,3},{3,2},{4,5},{5,4},{6,7},{7,6},{8,9},{9,8},{10,11... | collective-permute-start | bytes 393224 | tf_op jit(solution)/shard_map/ppermute | solution.py:26
  59.4 8.6 %collective-permute-start.25 = (bf16[256,256]{1,0:T(8,128)(2,1)S(1)}, bf16[256,256]{1,0:T(8,128)(2,1)S(1)}, u32[]{:S(2)}, u32[]{:S(2)}) collective-permute-start(bf16[256,256]{1,0:T(8,128)(2,1)S(1)} %get-tuple-element.94), channel_id=1, source_target_pairs={{0,2},{1,3},{2,0},{3,1},{4,6},{5,7},{6,4},{7,5},{8,10},{9,11},{10,... | collective-permute-start | bytes 393224 | tf_op jit(solution)/shard_map/ppermute | solution.py:26
  60.4 9.4 %collective-permute-start.26 = (bf16[256,256]{1,0:T(8,128)(2,1)S(1)}, bf16[256,256]{1,0:T(8,128)(2,1)S(1)}, u32[]{:S(2)}, u32[]{:S(2)}) collective-permute-start(bf16[256,256]{1,0:T(8,128)(2,1)S(1)} %get-tuple-element.95), channel_id=1, source_target_pairs={{0,3},{1,2},{2,1},{3,0},{4,7},{5,6},{6,5},{7,4},{8,11},{9,10},{10,... | collective-permute-start | bytes 393224 | tf_op jit(solution)/shard_map/ppermute | solution.py:26
  66.5 10.5 %collective-permute-start.27 = (bf16[128,256]{1,0:T(8,128)(2,1)S(1)}, bf16[128,256]{1,0:T(8,128)(2,1)S(1)}, u32[]{:S(2)}, u32[]{:S(2)}) collective-permute-start(bf16[128,256]{1,0:T(8,128)(2,1)S(1)} %get-tuple-element.96), channel_id=1, source_target_pairs={{0,1},{1,0},{2,3},{3,2},{4,5},{5,4},{6,7},{7,6},{8,9},{9,8},{10,11... | collective-permute-start | bytes 196616 | tf_op jit(solution)/shard_map/ppermute | solution.py:26
  70.7 8.9 %collective-permute-start.28 = (bf16[128,256]{1,0:T(8,128)(2,1)S(1)}, bf16[128,256]{1,0:T(8,128)(2,1)S(1)}, u32[]{:S(2)}, u32[]{:S(2)}) collective-permute-start(bf16[128,256]{1,0:T(8,128)(2,1)S(1)} %get-tuple-element.97), channel_id=1, source_target_pairs={{0,2},{1,3},{2,0},{3,1},{4,6},{5,7},{6,4},{7,5},{8,10},{9,11},{10,... | collective-permute-start | bytes 196616 | tf_op jit(solution)/shard_map/ppermute | solution.py:26
  72.6 7.1 %collective-permute-start.29 = (bf16[128,256]{1,0:T(8,128)(2,1)S(1)}, bf16[128,256]{1,0:T(8,128)(2,1)S(1)}, u32[]{:S(2)}, u32[]{:S(2)}) collective-permute-start(bf16[128,256]{1,0:T(8,128)(2,1)S(1)} %get-tuple-element.98), channel_id=1, source_target_pairs={{0,3},{1,2},{2,1},{3,0},{4,7},{5,6},{6,5},{7,4},{8,11},{9,10},{10,... | collective-permute-start | bytes 196616 | tf_op jit(solution)/shard_map/ppermute | solution.py:26
  (15 other events, 169.7 us)
